TPU v7x, 32 devices: a whole 2x2x4 slice. The times are simulated.
32 devices in a mesh: seq: 8 (over z, y), tp: 4 (over x, core).
Axes of the slice: x: 2, y: 2, z: 4, core: 2. Of those that a mesh axis runs over, the one named last changes fastest.
Arguments:
- lin_query: bfloat16 [2048, 64, 128], P('seq', 'tp'), may hold values from -6 to 6
- lin_key: bfloat16 [2048, 64, 128], P('seq', 'tp'), may hold values from -6 to 6
- lin_value: bfloat16 [2048, 64, 128], P('seq', 'tp'), may hold values from -80 to 80
- lin_gate: bfloat16 [2048, 64, 128], P('seq', 'tp'), may hold values from -6 to 6
- log_decay: float32 [2048, 64], P('seq', 'tp'), may hold values from -1 to 0
- norm_gain: float32 [64, 128], P('tp'), may hold values from 0.1 to 1.9
- doc_ids: int32 [2048], P('seq'), may hold values from 0 to 3, never falling along the last dimension, each value on 1 to 1280 neighbouring positions
- soft_query: bfloat16 [2048, 64, 128], P('seq', 'tp'), may hold values from -200 to 200
- soft_key: bfloat16 [2048, 8, 128], P('seq'), may hold values from -6 to 6
- soft_value: bfloat16 [2048, 8, 128], P('seq'), may hold values from -6 to 6
Outputs:
- lin_out: bfloat16 [2048, 64, 128], P('seq', 'tp')
- soft_out: bfloat16 [2048, 64, 128], P('seq', 'tp')
Inputs may be any that keep to these rules, and one draw needn't show every extreme that they name: `doc_ids`: ids never fall along the sequence; each document is one run of 1 to 1280 tokens, and one document has exactly that many.
All inputs are finite; a program needn't handle non-finite values.
Results may differ from a plain program's by a relative error of at most 0.012.
Values may be sent and summed in bfloat16 or wider, within the bound.
No kernel may reach another device: no remote copies, remote signals or barrier semaphores. Data moves between devices by JAX's collectives and lax.ppermute only.
A program may use at most 128 MiB of HBM per device.

v0:
```python
import jax
import jax.numpy as jnp
from jax import lax
from jax.sharding import PartitionSpec as P

HEADS = 64
HEAD_DIM = 128
KV_HEADS = 8


def lightning_part(lin_query, lin_key, lin_value, lin_gate, log_decay, norm_gain, doc_ids):
    tok_rows = lin_query.shape[0]
    seq_index = lax.axis_index("seq")
    highest = lax.Precision.HIGHEST
    cumul = jnp.cumsum(log_decay, axis=0)
    block_decay = cumul[-1]
    doc_float = doc_ids.astype(jnp.float32)
    last_doc = doc_float[-1:]
    token_order = jnp.arange(tok_rows)
    visible = (token_order[None, :] <= token_order[:, None]) & (
        doc_ids[None, :] == doc_ids[:, None]
    )
    cumul_heads = jnp.transpose(cumul)
    decay_gap = cumul_heads[:, :, None] - cumul_heads[:, None, :]
    factor = jnp.where(visible[None], jnp.exp(jnp.where(visible[None], decay_gap, 0.0)), 0.0)
    scores = jnp.einsum("thd,shd->hts", lin_query, lin_key, preferred_element_type=jnp.float32)
    weights = (scores * factor).astype(jnp.bfloat16)
    inner_part = jnp.einsum("hts,shd->thd", weights, lin_value, preferred_element_type=jnp.float32)
    tail_mask = (doc_ids == doc_ids[-1]).astype(jnp.float32)
    key_scale = jnp.exp(block_decay[None, :] - cumul) * tail_mask[:, None]
    scaled_keys = (lin_key * key_scale[:, :, None]).astype(jnp.bfloat16)
    own_state = jnp.einsum(
        "shd,she->hde", scaled_keys, lin_value, preferred_element_type=jnp.float32
    )
    table_decay, table_last = (
        lax.all_gather(block_decay[None, :], "seq", axis=0, tiled=True),
        lax.all_gather(last_doc, "seq", axis=0, tiled=True),
    )
    slot_ids = jnp.arange(table_last.shape[0])
    before_last = jnp.sum(jnp.where(slot_ids == seq_index - 1, table_last, 0.0))
    prior_doc = jnp.where(seq_index > 0, before_last, -1.0)
    shards = lax.all_gather(own_state[None].astype(jnp.bfloat16), "seq", axis=0, tiled=True).astype(
        jnp.float32
    )
    count_here = shards.shape[0]
    anchor = jnp.arange(count_here)
    between = (slot_ids[None, :] > anchor[:, None]) & (slot_ids[None, :] < seq_index)
    decay_sum = jnp.dot(between.astype(jnp.float32), table_decay, precision=highest)
    anchor_last = jnp.sum(
        jnp.where(anchor[:, None] == slot_ids[None, :], table_last[None, :], 0.0), axis=1
    )
    keep_mask = ((anchor < seq_index) & (anchor_last == prior_doc)).astype(jnp.float32)
    weight = jnp.exp(decay_sum) * keep_mask[:, None]
    prior_state = jnp.zeros_like(own_state) + jnp.einsum(
        "jh,jhde->hde", weight, shards, precision=highest
    )
    carried = jnp.einsum(
        "thd,hde->the",
        lin_query,
        prior_state.astype(jnp.bfloat16),
        preferred_element_type=jnp.float32,
    )
    open_mask = (doc_float == prior_doc).astype(jnp.float32)
    carried = carried * (jnp.exp(cumul) * open_mask[:, None])[:, :, None]
    mixed_heads = inner_part + carried
    square_sum = lax.psum(jnp.sum(mixed_heads * mixed_heads, axis=(1, 2)), "tp")
    inv_rms = lax.rsqrt(square_sum / (HEADS * HEAD_DIM) + 1e-06)
    gated = jax.nn.sigmoid(lin_gate.astype(jnp.float32))
    return (mixed_heads * inv_rms[:, None, None] * norm_gain[None] * gated).astype(jnp.bfloat16)


def softmax_part(soft_query, soft_key, soft_value, doc_ids):
    tok_rows = soft_query.shape[0]
    heads_here = soft_query.shape[1]
    head_width = soft_query.shape[2]
    seq_index = lax.axis_index("seq")
    group_size = HEADS // KV_HEADS
    kv_here = max(1, heads_here // group_size)
    per_group = heads_here // kv_here
    kv_start = lax.axis_index("tp") * heads_here // group_size
    key_here = lax.dynamic_slice_in_dim(soft_key, kv_start, kv_here, 1)
    value_here = lax.dynamic_slice_in_dim(soft_value, kv_start, kv_here, 1)
    queries = soft_query.reshape(tok_rows, kv_here, per_group, head_width)
    query_docs = doc_ids.astype(jnp.float32)
    query_pos = seq_index * tok_rows + jnp.arange(tok_rows)
    last_pos = seq_index * tok_rows + tok_rows - 1
    score_scale = HEAD_DIM ** (-0.5)

    def attend(state, key_block, value_block, key_docs):
        top_score, total_weight, weighted = state
        count_here = key_block.shape[0]
        key_pos = jnp.arange(count_here)
        visible = (key_pos[None, :] <= query_pos[:, None]) & (
            key_docs.astype(jnp.float32)[None, :] == query_docs[:, None]
        )
        score = (
            jnp.einsum("tkgd,skd->kgts", queries, key_block, preferred_element_type=jnp.float32)
            * score_scale
        )
        score = jnp.where(visible, score, -1e30)
        new_top = jnp.maximum(top_score, jnp.max(score, axis=-1))
        soft_exp = jnp.where(visible, jnp.exp(score - new_top[..., None]), 0.0)
        total_weight = jnp.sum(soft_exp, axis=-1)
        weighted = jnp.einsum(
            "kgts,skd->kgtd",
            soft_exp.astype(jnp.bfloat16),
            value_block,
            preferred_element_type=jnp.float32,
        )
        return (new_top, total_weight, weighted)

    def skip_block(state):
        return state

    start_state = (
        jnp.full((kv_here, per_group, tok_rows), -1e30, jnp.float32),
        jnp.zeros((kv_here, per_group, tok_rows), jnp.float32),
        jnp.zeros((kv_here, per_group, tok_rows, head_width), jnp.float32),
    )
    key_docs = doc_ids.astype(jnp.bfloat16)
    key_block = lax.all_gather(key_here, "seq", axis=0, tiled=True)
    value_block = lax.all_gather(value_here, "seq", axis=0, tiled=True)
    block_docs = lax.all_gather(key_docs, "seq", axis=0, tiled=True)
    state = lax.cond(
        jnp.int32(0) <= last_pos,
        lambda inner_state: attend(inner_state, key_block, value_block, block_docs),
        skip_block,
        start_state,
    )
    top_score, total_weight, weighted = state
    result = weighted / total_weight[..., None]
    return (
        jnp.transpose(result, (2, 0, 1, 3))
        .reshape(tok_rows, heads_here, head_width)
        .astype(jnp.bfloat16)
    )


def body(
    lin_query,
    lin_key,
    lin_value,
    lin_gate,
    log_decay,
    norm_gain,
    doc_ids,
    soft_query,
    soft_key,
    soft_value,
):
    lin_out = lightning_part(lin_query, lin_key, lin_value, lin_gate, log_decay, norm_gain, doc_ids)
    soft_out = softmax_part(soft_query, soft_key, soft_value, doc_ids)
    return (lin_out, soft_out)


def solution(mesh):
    in_specs = (
        P("seq", "tp", None),
        P("seq", "tp", None),
        P("seq", "tp", None),
        P("seq", "tp", None),
        P("seq", "tp"),
        P("tp", None),
        P("seq"),
        P("seq", "tp", None),
        P("seq", None, None),
        P("seq", None, None),
    )
    out_specs = (P("seq", "tp", None), P("seq", "tp", None))
    return jax.shard_map(body, mesh=mesh, in_specs=in_specs, out_specs=out_specs, check_vma=False)
```

profile of v0, /device:TPU:0, one launch (start us, length us, event | category | flops | bytes accessed | tf_op | source)
XLA Modules:
  0.0 193.6 jit_solution(17570529566558580508)
XLA Ops:
  7.2 0.0 all-gather.7.cloned.1.call-start
  7.3 1.3 constant_dynamic-slice_fusion.1
  8.6 0.7 copy.100
  9.2 0.0 all-gather.7.cloned.1.call-update
  9.3 0.0 all-gather.9.cloned.1.call-start
  9.3 1.2 constant_dynamic-slice_fusion
  10.5 0.7 copy.101
  11.2 0.0 all-gather.11.cloned.1.call-start
  11.3 0.8 fusion.34
  12.0 1.2 dynamic-slice
  13.3 0.8 slice_dynamic-update-slice_fusion
  14.1 23.3 %all-reduce = f32[8]{0:T(128)S(1)} all-reduce(f32[8]{0:T(128)S(1)} %slice_dynamic-update-slice_fusion), channel_id=1, replica_groups=mesh['seq'=8,'tp'=4] {'seq'}, use_global_device_ids=true, to_apply=%add | all-reduce | flops 8 | bytes 64
  37.3 1.3 slice.19
  38.6 0.7 copy_bitcast_fusion.2
  39.3 0.6 reduce-window.6
  39.9 0.2 slice_reduce_fusion
  40.1 0.6 fusion.31
  41.4 0.1 fusion.33
  41.4 0.2 slice_reduce_fusion.1
  41.6 1.4 compare_convert_fusion.1
  43.0 0.1 exponential_multiply_fusion.1
  43.1 0.1 copy.80
  43.2 1.7 multiply_convert_fusion.2
  45.0 1.4 convolution_convert_fusion
  46.4 0.0 all-gather.11.cloned.1.call-update
  46.4 1.6 copy.84
  48.0 16.1 %all-gather.1 = f32[8,1,16]{2,1,0:T(1,128)S(1)} all-gather(f32[1,1,16]{2,1,0:T(1,128)S(1)} %bitcast.76), channel_id=1, replica_groups=mesh['seq'=8,'tp'=4] {'seq'}, dimensions={0}, use_global_device_ids=true | all-gather | bytes 576 | tf_op jit(solution)/shard_map/all_gather | solution.py:36
  64.2 18.3 %all-gather.2 = bf16[8,1,256]{2,1,0:T(2,128)(2,1)S(1)} all-gather(bf16[1,1,256]{2,1,0:T(2,128)(2,1)S(1)} %reshape.118), channel_id=1, replica_groups=mesh['seq'=8,'tp'=4] {'seq'}, dimensions={0}, use_global_device_ids=true | all-gather | bytes 4608 | tf_op jit(solution)/shard_map/all_gather | solution.py:123
  82.4 0.1 select_reduce_fusion
  82.6 0.1 fusion.16
  82.6 0.2 fusion.27
  82.8 4.7 %fusion.14 = f32[16,256,128]{1,2,0:T(8,128)} fusion(f32[16,256]{1,0:T(8,128)S(1)} %get-tuple-element.83, pred[256,256]{1,0:T(8,128)(4,1)S(1)} %fusion.27, bf16[256,16,128]{2,1,0:T(8,128)(2,1)} %param.13, bf16[256,16,128]{2,1,0:T(8,128)(2,1)S(1)} %copy-done, bf16[256,16,128]{2,1,0:T(8,128)(2,1)S(1)} %copy-done.1), kind=kOutput, calls=%fused_computation.25 | convolution fusion | flops 542113792 | bytes 5324800 | tf_op jit(solution)/shard_map/hts,shd->thd/dot_general | solution.py:28
  87.5 7.3 %all-gather.9.cloned.1.call-done = bf16[2048,2,128]{2,0,1:T(8,128)(2,1)} async-done(((bf16[256,2,128]{2,0,1:T(8,128)(2,1)}), bf16[2048,2,128]{2,0,1:T(8,128)(2,1)}) %all-gather.9.cloned.1.call-update) | async-done | bytes 1048592 | tf_op jit(solution)/shard_map/all_gather | solution.py:122
  94.8 49.4 %conditional.1 = (f32[2,8,256]{2,1,0:T(8,128)S(1)}, f32[2,8,256,128]{3,2,1,0:T(8,128)}) conditional(s32[]{:T(128)} %convert_element_type.76, () %tuple.16, (s32[]{:T(128)}, s32[256]{0:T(256)S(1)}, bf16[8,1,256]{2,1,0:T(2,128)(2,1)S(1)}, f32[256]{0:T(256)S(1)}, bf16[256,16,128]{2,1,0:T(8,128)(2,1)S(1)}, /*index=5*/bf16[2048,2,128]{2,0,1:T(8,128)(2,1)}, ...), branch_computations={%region_6.7_spmd, %region_7.10_spmd} | conditional | flops 4405590016 | bytes 114434104 | solution.py:124
  94.9 0.5 fusion.6
  95.4 0.3 copy.87
  95.7 15.3 %fusion = (f32[2,8,256]{2,1,0:T(8,128)S(1)}, f32[2,2048,256,8]{2,1,3,0:T(8,128)}) fusion(pred[256,2048]{0,1:T(8,128)(4,1)S(1)} %fusion.6, bf16[256,2,8,128]{3,0,2,1:T(8,128)(2,1)S(1)} %bitcast.71, bf16[2048,2,128]{2,0,1:T(8,128)(2,1)} %get-tuple-element.21), kind=kOutput, calls=%fused_computation.2 | convolution fusion | flops 2172645376 | bytes 36192256 | tf_op jit(solution)/shard_map/cond/branch_1_fun/tkgd,skd->kgts/dot_general | solution.py:97
  111.0 15.0 %fusion.2 = f32[2,8,256]{2,1,0:T(8,128)S(1)} fusion(f32[2,2048,256,8]{2,1,3,0:T(8,128)} %get-tuple-element.79, f32[2,8,256]{2,1,0:T(8,128)S(1)} %broadcast_maximum_fusion, pred[256,2048]{0,1:T(8,128)(4,1)S(1)} %fusion.6), kind=kLoop, calls=%fused_computation.4 | loop fusion | flops 41938944 | bytes 34111488 | tf_op jit(solution)/shard_map/cond/branch_1_fun/reduce_sum | solution.py:103
  126.0 18.2 %fusion.3 = f32[2,8,256,128]{3,2,1,0:T(8,128)} fusion(f32[2,2048,256,8]{2,1,3,0:T(8,128)} %get-tuple-element.79, f32[2,8,256]{2,1,0:T(8,128)S(1)} %broadcast_maximum_fusion, pred[256,2048]{0,1:T(8,128)(4,1)S(1)} %fusion.6, bf16[2048,2,128]{2,0,1:T(8,128)(2,1)S(1)} %copy-done.6), kind=kOutput, calls=%fused_computation.5 | convolution fusion | flops 2189426688 | bytes 37240832 | tf_op jit(solution)/shard_map/cond/branch_1_fun/kgts,skd->kgtd/dot_general | solution.py:104
  144.2 1.9 %fusion.20 = bf16[256,2,8,128]{3,0,2,1:T(8,128)(2,1)S(1)} fusion(f32[2,8,256,128]{3,2,1,0:T(8,128)} %get-tuple-element.28, f32[2,8,256]{2,1,0:T(8,128)S(1)} %get-tuple-element.29), kind=kLoop, calls=%fused_computation.33 | loop fusion | flops 1048576 | bytes 3162112 | tf_op jit(solution)/shard_map/convert_element_type | solution.py:135
  146.2 1.6 copy.131
  147.8 21.3 %all-gather.11.cloned.1.call-done = bf16[128,128,128]{2,1,0:T(8,128)(2,1)} async-done(((bf16[16,128,128]{2,1,0:T(8,128)(2,1)}), bf16[128,128,128]{2,1,0:T(8,128)(2,1)}) %all-gather.11.cloned.1.call-update) | async-done | bytes 4194320 | tf_op jit(solution)/shard_map/all_gather | solution.py:42
  169.2 3.1 %multiply_reduce_fusion = bf16[16,128,128]{2,1,0:T(8,128)(2,1)S(1)} fusion(bf16[16,8,128,128]{3,2,0,1:T(8,128)(2,1)} %bitcast.72, f32[16,8]{0,1:T(8,128)S(1)} %fusion.16), kind=kLoop, calls=%fused_computation.17 | loop fusion | flops 6029312 | bytes 4719104
  172.3 1.0 copy.99
  173.3 2.6 %multiply_reduce_fusion.1 = (f32[256]{0:T(256)S(1)}, f32[256,16,128]{0,2,1:T(8,128)S(1)}) fusion(f32[256,16]{0,1:T(8,128)S(1)} %get-tuple-element.81, bf16[16,128,128]{1,2,0:T(8,128)(2,1)} %copy.99, bf16[256,16,128]{2,1,0:T(8,128)(2,1)} %param.12, f32[16,256,128]{1,2,0:T(8,128)} %fusion.14), kind=kOutput, calls=%fused_computation.23 | convolution fusion | flops 136314624 | bytes 5784576 | tf_op jit(solution)/shard_map/thd,hde->the/dot_general | solution.py:57
  175.9 5.7 %psum.7 = f32[256]{0:T(256)S(1)} all-reduce(f32[256]{0:T(256)S(1)} %get-tuple-element.88), channel_id=1, replica_groups=mesh['seq'=8,'tp'=4] {'tp'}, use_global_device_ids=true, to_apply=%region_5.6 | all-reduce | flops 256 | bytes 2048 | tf_op jit(solution)/shard_map/psum | solution.py:66
  181.6 2.8 %multiply_convert_fusion.1 = bf16[256,16,128]{0,2,1:T(8,128)(2,1)} fusion(bf16[256,16,128]{0,2,1:T(8,128)(2,1)} %copy.84, f32[256,16,128]{0,2,1:T(8,128)S(1)} %get-tuple-element.89, f32[16,128]{1,0:T(8,128)S(1)} %copy-done.5, f32[256]{0:T(256)S(1)} %add_rsqrt_fusion), kind=kLoop, calls=%fused_computation.22 | loop fusion | flops 4194304 | bytes 4203520 | tf_op jit(solution)/shard_map/convert_element_type | solution.py:69
  184.4 2.6 %copy.89 = bf16[256,16,128]{2,1,0:T(8,128)(2,1)} copy(bf16[256,16,128]{0,2,1:T(8,128)(2,1)} %multiply_convert_fusion.1) | data formatting | bytes 2097152
  (29 shorter events, 0.2 us)
Async XLA Ops:
  7.2 37.8 %copy-start = (bf16[256,16,128]{2,1,0:T(8,128)(2,1)S(1)}, bf16[256,16,128]{2,1,0:T(8,128)(2,1)}, u32[]{:S(2)}) copy-start(bf16[256,16,128]{2,1,0:T(8,128)(2,1)} %param.14) | copy-start | bytes 3145732
  7.2 39.2 %copy-start.2 = (bf16[256,16,128]{2,1,0:T(8,128)(2,1)S(1)}, bf16[256,16,128]{2,1,0:T(8,128)(2,1)}, u32[]{:S(2)}) copy-start(bf16[256,16,128]{2,1,0:T(8,128)(2,1)} %param.15) | copy-start | bytes 3145732
  7.2 80.3 %all-gather.7.cloned.1.call-start = ((), (), s32[]{:S(2)}) async-start(), calls=%async_computation | async-start | bytes 1179648 | tf_op jit(solution)/shard_map/all_gather | solution.py:121
  9.3 85.6 %all-gather.9.cloned.1.call-start = ((), (), s32[]{:S(2)}) async-start(), calls=%async_computation.1 | async-start | bytes 1179648 | tf_op jit(solution)/shard_map/all_gather | solution.py:122
  11.2 71.5 %copy-start.4 = (s32[256]{0:T(256)S(1)}, s32[256]{0:T(256)}, u32[]{:S(2)}) copy-start(s32[256]{0:T(256)} %param.18) | copy-start | bytes 3076
  11.2 71.6 %copy-start.1 = (bf16[256,16,128]{2,1,0:T(8,128)(2,1)S(1)}, bf16[256,16,128]{2,1,0:T(8,128)(2,1)}, u32[]{:S(2)}) copy-start(bf16[256,16,128]{2,1,0:T(8,128)(2,1)} %param.12) | copy-start | bytes 3145732
  11.2 158.0 %all-gather.11.cloned.1.call-start = ((), (), s32[]{:S(2)}) async-start(), calls=%async_computation.2 | async-start | bytes 4718592 | tf_op jit(solution)/shard_map/all_gather | solution.py:42
  82.8 12.0 %copy-start.3 = (bf16[256,16,128]{2,1,0:T(8,128)(2,1)S(1)}, bf16[256,16,128]{2,1,0:T(8,128)(2,1)}, u32[]{:S(2)}) copy-start(bf16[256,16,128]{2,1,0:T(8,128)(2,1)} %param.19) | copy-start | bytes 3145732
  111.0 15.0 %copy-start.6 = (bf16[2048,2,128]{2,0,1:T(8,128)(2,1)S(1)}, bf16[2048,2,128]{2,0,1:T(8,128)(2,1)}, u32[]{:S(2)}) copy-start(bf16[2048,2,128]{2,0,1:T(8,128)(2,1)} %get-tuple-element.23) | copy-start | bytes 3145732 | tf_op jit(solution)/shard_map/cond
  172.2 9.3 %copy-start.5 = (f32[16,128]{1,0:T(8,128)S(1)}, f32[16,128]{1,0:T(8,128)}, u32[]{:S(2)}) copy-start(f32[16,128]{1,0:T(8,128)} %param.17) | copy-start | bytes 24580
Sparse Core Ops, SparseCore 0:
  10.8 42.8 all-gather.6
  55.8 38.9 all-gather.8
  97.0 72.1 all-gather.10
where the time goes:
time: 194 us
  blocking collectives  63.3 us (33%)
  matrix products  42.3 us (22%)
  other arithmetic  29 us (15%)
  waiting for transfers between devices  28.7 us (15%)
  local copies, waits for them, and re-layouts  15.5 us (8%)
  between operations  14.5 us (7%)
    unnamed x1, blocking collectives  23.3 us
    all_gather x1, waiting for transfers between devices, lightning_part(): lax.all_gather(own_state[None].astype(jnp.bfloat16), 'seq', axis=0, tiled...  21.3 us
    all_gather x1, blocking collectives, softmax_part(): block_docs = lax.all_gather(key_docs, 'seq', axis=0, tiled=True)  18.3 us
    dot_general x1, matrix products, attend(): jnp.einsum('kgts,skd->kgtd', soft_exp.astype(jnp.bfloat16), value_block,...  18.2 us
    all_gather x1, blocking collectives, lightning_part(): lax.all_gather(block_decay[None, :], 'seq', axis=0, tiled=True)  16.1 us
    dot_general x1, matrix products, attend(): jnp.einsum('tkgd,skd->kgts', queries, key_block, preferred_element_type=j...  15.3 us
    reduce_sum x1, other arithmetic, attend(): total_weight = jnp.sum(soft_exp, axis=-1)  15 us
    unnamed x20, local copies, waits for them, and re-layouts  7.62 us
  transfers between devices with their start and end apart: 3, of which 2 were waited for; matrix products, arithmetic and copies ran while one was open for 37% of the time, Pallas kernels for 0%

commit v1 on v0

v1 whole, which is shorter than its diff:
```python
import functools

import jax
import jax.numpy as jnp
import numpy as np
from jax import lax
from jax.experimental import pallas as pl
from jax.experimental.pallas import tpu as pltpu
from jax.sharding import PartitionSpec as P

HEADS = 64
HEAD_DIM = 128
KV_HEADS = 8
LANES = 128
GROUP = HEADS // KV_HEADS
F32 = jnp.float32
BF16 = jnp.bfloat16
BIG = float(2**20)
SCORE_TO_EXP2 = HEAD_DIM**-0.5 * float(np.log2(np.e))
INFO = 16
HIGHEST = lax.Precision.HIGHEST

VMEM = pl.BlockSpec(memory_space=pltpu.VMEM)
SMEM = pl.BlockSpec(memory_space=pltpu.SMEM)


def sds(shape, dtype):
    return jax.ShapeDtypeStruct(shape, dtype)


def params(mib):
    return pltpu.CompilerParams(vmem_limit_bytes=mib * 1024 * 1024)


def cost(flops, bytes_accessed, transcendentals=0):
    return pl.CostEstimate(
        flops=int(flops), bytes_accessed=int(bytes_accessed), transcendentals=int(transcendentals)
    )


def doc_columns(doc_rows, tokens):
    parts = []
    for i in range(tokens // LANES):
        row = jnp.broadcast_to(doc_rows[i : i + 1, :], (LANES, LANES))
        parts.append(jnp.transpose(row))
    return jnp.concatenate(parts, axis=0)


def doc_line(doc_rows, tokens):
    return jnp.concatenate([doc_rows[i : i + 1, :] for i in range(tokens // LANES)], axis=1)


def lower_triangle(tokens):
    rows = lax.broadcasted_iota(jnp.int32, (tokens, tokens), 0)
    cols = lax.broadcasted_iota(jnp.int32, (tokens, tokens), 1)
    return rows >= cols


def cumulative(log_decay, tokens):
    return jnp.dot(
        lower_triangle(tokens).astype(F32), log_decay, precision=HIGHEST, preferred_element_type=F32
    )


def pack_kernel(tokens, kv_here, start_ref, key_ref, value_ref, doc_ref, out_ref, scratch):
    start = start_ref[0]
    for which, ref in enumerate((key_ref, value_ref)):
        scratch[...] = ref[...].astype(F32)
        for g in range(kv_here):
            rows = scratch[pl.ds(start + g, tokens, stride=KV_HEADS), :]
            at = (which * kv_here + g) * tokens
            out_ref[at : at + tokens, :] = rows.astype(BF16)
    end = 2 * kv_here * tokens
    out_ref[end : end + INFO, :] = doc_ref[...].astype(BF16)


def pack_kv(start, soft_key, soft_value, doc_rows, tokens, kv_here):
    rows = 2 * kv_here * tokens + INFO
    return pl.pallas_call(
        functools.partial(pack_kernel, tokens, kv_here),
        out_shape=sds((rows, LANES), BF16),
        in_specs=[SMEM, VMEM, VMEM, VMEM],
        out_specs=VMEM,
        scratch_shapes=[pltpu.VMEM((tokens * KV_HEADS, LANES), F32)],
        compiler_params=params(16),
        cost_estimate=cost(0, 4 * tokens * KV_HEADS * LANES * 2),
        name="pack_kv",
    )(start, soft_key, soft_value, doc_rows)


def state_kernel(tokens, heads, y_ref, ld_ref, doc_ref, key_ref, value_ref, keep_ref, send_ref, info_ref, kf, vf, states, ldp):
    half = heads // 2
    y = y_ref[0]
    ldp[...] = jnp.zeros_like(ldp)
    ldp[:, 0:heads] = ld_ref[...]
    cumul = cumulative(ldp[...], tokens)
    total = cumul[tokens - 1 : tokens, :]
    docs = doc_ref[...]
    last_row = tokens // LANES - 1
    first_doc = docs[0:1, 0:1]
    last_doc = docs[last_row : last_row + 1, LANES - 1 : LANES]
    tail = (doc_columns(docs, tokens) == last_doc).astype(F32)
    scale = jnp.exp(total - cumul) * tail
    kf[...] = key_ref[...].astype(F32)
    vf[...] = value_ref[...].astype(F32)
    for h in range(heads):
        keys = (kf[pl.ds(h, tokens, stride=heads), :] * scale[:, h : h + 1]).astype(BF16)
        values = vf[pl.ds(h, tokens, stride=heads), :].astype(BF16)
        states[h * HEAD_DIM : (h + 1) * HEAD_DIM, :] = lax.dot_general(
            keys, values, (((0,), (0,)), ((), ())), preferred_element_type=F32
        )
    size = half * HEAD_DIM
    keep_ref[...] = states[pl.ds(pl.multiple_of(y * size, size), size), :].astype(BF16)
    send_ref[0:size, :] = states[pl.ds(pl.multiple_of((1 - y) * size, size), size), :].astype(BF16)
    upper = pltpu.roll(total, LANES - half, 1)
    rows = lax.broadcasted_iota(jnp.int32, (INFO, LANES), 0)

    def info_of(totals):
        hi = totals.astype(BF16).astype(F32)
        mid = (totals - hi).astype(BF16).astype(F32)
        lo = totals - hi - mid
        return jnp.where(
            rows == 0,
            hi,
            jnp.where(
                rows == 1,
                mid,
                jnp.where(
                    rows == 2, lo, jnp.where(rows == 3, first_doc, jnp.where(rows == 4, last_doc, 0.0))
                ),
            ),
        ).astype(BF16)

    mine = (y == 0).astype(F32)
    info_ref[...] = info_of(total * mine + upper * (1.0 - mine))
    send_ref[size : size + INFO, :] = info_of(total * (1.0 - mine) + upper * mine)


def block_state(y, log_decay, doc_rows, key, value, tokens, heads):
    size = heads // 2 * HEAD_DIM
    return pl.pallas_call(
        functools.partial(state_kernel, tokens, heads),
        out_shape=(sds((size, LANES), BF16), sds((size + INFO, LANES), BF16), sds((INFO, LANES), BF16)),
        in_specs=[SMEM, VMEM, VMEM, VMEM, VMEM],
        out_specs=(VMEM, VMEM, VMEM),
        scratch_shapes=[
            pltpu.VMEM((tokens * heads, LANES), F32),
            pltpu.VMEM((tokens * heads, LANES), F32),
            pltpu.VMEM((heads * HEAD_DIM, LANES), F32),
            pltpu.VMEM((tokens, LANES), F32),
        ],
        compiler_params=params(24),
        cost_estimate=cost(2 * heads * tokens * HEAD_DIM**2, 3 * tokens * heads * LANES * 2),
        name="block_state",
    )(y, log_decay, doc_rows, key, value)


def row_terms(y_ref, own_info, other_info):
    even = y_ref[0] == 0
    own = own_info.astype(F32)
    other = other_info.astype(F32)
    a = jnp.where(even, own, other)
    b = jnp.where(even, other, own)
    decay_a = jnp.exp(a[0:1] + a[1:2] + a[2:3])
    decay_b = jnp.exp(b[0:1] + b[1:2] + b[2:3])
    first_a, last_a = a[3:4], a[4:5]
    first_b, last_b = b[3:4], b[4:5]
    whole_a = (first_a == last_a).astype(F32)
    link_b = ((last_a == first_b) & (first_b == last_b)).astype(F32)
    return even, decay_a, decay_b * link_b, first_a, whole_a, last_a, last_b


def chain_kernel(count, first, arrivals, y_ref, *refs):
    keep_ref, info_ref, other_ref, other_info_ref = refs[:4]
    came, out_ref = refs[4 : 4 + arrivals], refs[4 + arrivals]
    size = count * HEAD_DIM
    even, decay_a, gain_b, first_a, whole_a, _, last_b = row_terms(
        y_ref, info_ref[...], other_info_ref[...]
    )
    if arrivals:
        came_doc = came[0][size : size + 1, :].astype(F32)
        gain_a = decay_a * whole_a * (came_doc == first_a).astype(F32)
    for i in range(count):
        rows = slice(i * HEAD_DIM, (i + 1) * HEAD_DIM)
        lane = slice(first + i, first + i + 1)
        own = keep_ref[rows, :].astype(F32)
        other = other_ref[rows, :].astype(F32)
        total = jnp.where(even, own, other)
        if arrivals:
            total = total + gain_a[:, lane] * came[0][rows, :].astype(F32)
        out_ref[rows, :] = (gain_b[:, lane] * total + jnp.where(even, other, own)).astype(BF16)
    out_ref[size : size + INFO, :] = jnp.broadcast_to(last_b, (INFO, LANES)).astype(BF16)


def chain_step(y, keep, info, other, other_info, came, first, count):
    size = count * HEAD_DIM
    came = [] if came is None else [came]
    return pl.pallas_call(
        functools.partial(chain_kernel, count, first, len(came)),
        out_shape=sds((size + INFO, LANES), BF16),
        in_specs=[SMEM] + [VMEM] * (4 + len(came)),
        out_specs=VMEM,
        compiler_params=params(8),
        cost_estimate=cost(4 * size * LANES, 4 * size * LANES * 2),
        name="chain_step",
    )(y, keep, info, other, other_info, *came)


def prior_kernel(count, first, arrivals, y_ref, *refs):
    keep_ref, info_ref, other_ref, other_info_ref = refs[:4]
    came = refs[4 : 4 + arrivals]
    mine_ref, send_ref, doc_ref = refs[4 + arrivals :]
    size = count * HEAD_DIM
    even, decay_a, _, first_a, whole_a, last_a, _ = row_terms(
        y_ref, info_ref[...], other_info_ref[...]
    )
    came_doc = jnp.zeros((1, LANES), F32)
    for ref in came:
        came_doc = came_doc + ref[size : size + 1, :].astype(F32)
    gain_a = decay_a * whole_a * (came_doc == first_a).astype(F32)
    for i in range(count):
        rows = slice(i * HEAD_DIM, (i + 1) * HEAD_DIM)
        lane = slice(first + i, first + i + 1)
        before_a = jnp.zeros((HEAD_DIM, LANES), F32)
        for ref in came:
            before_a = before_a + ref[rows, :].astype(F32)
        state_a = jnp.where(even, keep_ref[rows, :].astype(F32), other_ref[rows, :].astype(F32))
        before_b = gain_a[:, lane] * before_a + state_a
        mine_ref[rows, :] = jnp.where(even, before_a, before_b).astype(BF16)
        send_ref[rows, :] = jnp.where(even, before_b, before_a).astype(BF16)
    doc_ref[...] = jnp.broadcast_to(jnp.where(even, came_doc, last_a), (8, LANES))


def prior_states(y, keep, info, other, other_info, came, first, count):
    size = count * HEAD_DIM
    return pl.pallas_call(
        functools.partial(prior_kernel, count, first, len(came)),
        out_shape=(sds((size, LANES), BF16), sds((size, LANES), BF16), sds((8, LANES), F32)),
        in_specs=[SMEM] + [VMEM] * (4 + len(came)),
        out_specs=(VMEM, VMEM, VMEM),
        compiler_params=params(8),
        cost_estimate=cost(4 * size * LANES, 6 * size * LANES * 2),
        name="prior_states",
    )(y, keep, info, other, other_info, *came)


def inner_kernel(tokens, heads, ld_ref, ldt_ref, doc_ref, query_ref, key_ref, value_ref, inner_ref, qh_ref, grow_ref, qf, kf, vf, ldp, mask):
    ldp[...] = jnp.zeros_like(ldp)
    ldp[:, 0:heads] = ld_ref[...]
    cumul = cumulative(ldp[...], tokens)
    grow_ref[...] = jnp.exp(cumul)
    cumul_t = lax.dot_general(
        ldt_ref[...],
        lower_triangle(tokens).astype(F32),
        (((1,), (1,)), ((), ())),
        precision=HIGHEST,
        preferred_element_type=F32,
    )
    docs = doc_ref[...]
    column = doc_columns(docs, tokens)
    line = doc_line(docs, tokens)
    same = jnp.concatenate([column] * (tokens // LANES), axis=1) == line
    mask[...] = jnp.where(lower_triangle(tokens) & same, 0.0, -1e9)
    qf[...] = query_ref[...].astype(F32)
    kf[...] = key_ref[...].astype(F32)
    vf[...] = value_ref[...].astype(F32)
    for h in range(heads):
        picked = pl.ds(h, tokens, stride=heads)
        query = qf[picked, :].astype(BF16)
        keys = kf[picked, :].astype(BF16)
        values = vf[picked, :].astype(BF16)
        qh_ref[h * tokens : (h + 1) * tokens, :] = query
        for i in range(tokens // LANES):
            seen = (i + 1) * LANES
            rows = slice(i * LANES, seen)
            scores = lax.dot_general(
                query[rows, :], keys[0:seen, :], (((1,), (1,)), ((), ())), preferred_element_type=F32
            )
            gap = cumul[rows, h : h + 1] - cumul_t[h : h + 1, 0:seen]
            weights = (scores * jnp.exp(gap + mask[rows, 0:seen])).astype(BF16)
            inner_ref[h * tokens + i * LANES : h * tokens + seen, :] = jnp.dot(
                weights, values[0:seen, :], preferred_element_type=F32
            )


def inner_part(log_decay, doc_rows, query, key, value, tokens, heads):
    return pl.pallas_call(
        functools.partial(inner_kernel, tokens, heads),
        out_shape=(
            sds((heads * tokens, LANES), F32),
            sds((heads * tokens, LANES), BF16),
            sds((tokens, LANES), F32),
        ),
        in_specs=[VMEM] * 6,
        out_specs=(VMEM, VMEM, VMEM),
        scratch_shapes=[pltpu.VMEM((tokens * heads, LANES), F32)] * 3
        + [pltpu.VMEM((tokens, LANES), F32), pltpu.VMEM((tokens, tokens), F32)],
        compiler_params=params(32),
        cost_estimate=cost(
            4 * heads * tokens * tokens * HEAD_DIM, tokens * heads * LANES * 12, heads * tokens * tokens
        ),
        name="inner_part",
    )(log_decay, jnp.transpose(log_decay), doc_rows, query, key, value)


def mix_kernel(tokens, heads, pieces, y_ref, doc_ref, prior_doc_ref, grow_ref, inner_ref, qh_ref, *refs):
    mine, other = refs[:pieces], refs[pieces : 2 * pieces]
    mixed_ref, square_ref = refs[2 * pieces :]
    half = heads // 2
    count = half // pieces
    even = y_ref[0] == 0
    is_open = (doc_columns(doc_ref[...], tokens) == prior_doc_ref[0:1, :]).astype(F32)
    gain = grow_ref[...] * is_open
    squares = jnp.zeros((tokens, LANES), F32)
    for h in range(heads):
        piece, i = divmod(h % half, count)
        rows = slice(i * HEAD_DIM, (i + 1) * HEAD_DIM)
        near, far = mine[piece][rows, :], other[piece][rows, :]
        lower = h < half
        state = jnp.where(even, near if lower else far, far if lower else near)
        held = slice(h * tokens, (h + 1) * tokens)
        carried = jnp.dot(qh_ref[held, :], state, preferred_element_type=F32)
        mixed = inner_ref[held, :] + carried * gain[:, h : h + 1]
        squares = squares + mixed * mixed
        mixed_ref[pl.ds(h, tokens, stride=heads), :] = mixed
    square_ref[...] = lax.dot_general(
        jnp.ones((8, LANES), F32),
        squares,
        (((1,), (1,)), ((), ())),
        precision=HIGHEST,
        preferred_element_type=F32,
    )


def mix(y, doc_rows, prior_doc, grow, inner, qh, mine, other, tokens, heads):
    return pl.pallas_call(
        functools.partial(mix_kernel, tokens, heads, len(mine)),
        out_shape=(sds((tokens * heads, LANES), F32), sds((8, tokens), F32)),
        in_specs=[SMEM] + [VMEM] * (5 + 2 * len(mine)),
        out_specs=(VMEM, VMEM),
        compiler_params=params(24),
        cost_estimate=cost(2 * heads * tokens * HEAD_DIM**2, tokens * heads * LANES * 10),
        name="mix",
    )(y, doc_rows, prior_doc, grow, inner, qh, *mine, *other)


def finish_kernel(tokens, heads, sums, gain_ref, gate_ref, mixed_ref, *refs):
    squares, out_ref = refs[:sums], refs[sums]
    total = squares[0][0:1, :]
    for ref in squares[1:]:
        total = total + ref[0:1, :]
    scale = lax.rsqrt(total / (HEADS * HEAD_DIM) + 1e-06)
    rows = jnp.concatenate([scale[:, i * LANES : (i + 1) * LANES] for i in range(tokens // LANES)], axis=0)
    column = doc_columns(rows, tokens)
    step = 32
    for i in range(0, tokens, step):
        at = slice(i * heads, (i + step) * heads)
        gate = jax.nn.sigmoid(gate_ref[at, :].astype(F32)).reshape(step, heads, LANES)
        mixed = mixed_ref[at, :].reshape(step, heads, LANES)
        inv = column[i : i + step, :][:, None, :]
        out = mixed * inv * gain_ref[...][None] * gate
        out_ref[at, :] = out.reshape(step * heads, LANES).astype(BF16)


def finish(gain, gate, mixed, squares, tokens, heads):
    return pl.pallas_call(
        functools.partial(finish_kernel, tokens, heads, len(squares)),
        out_shape=sds((tokens * heads, LANES), BF16),
        in_specs=[VMEM] * (3 + len(squares)),
        out_specs=VMEM,
        compiler_params=params(16),
        cost_estimate=cost(0, tokens * heads * LANES * 8, tokens * heads * LANES),
        name="finish",
    )(gain, gate, mixed, *squares)


def attend_kernel(tokens, step, heads, kv_here, blocks, has_own, has_state, is_last, *refs):
    refs = list(refs)
    doc_ref, query_ref = refs.pop(0), refs.pop(0)
    kv = [refs.pop(0) for _ in range(blocks)]
    state_ref = refs.pop(0) if has_state else None
    out_ref, keys_ext, values_ext, doc_rep, doc_col = refs
    per_group = heads // kv_here
    rows = step * per_group
    span = blocks * tokens
    index = pl.program_id(0)

    @pl.when(index == 0)
    def _():
        lane = lax.broadcasted_iota(jnp.int32, (tokens, LANES), 1).astype(F32)
        column = doc_columns(doc_ref[...], tokens)
        for h in range(per_group):
            doc_rep[pl.ds(h, tokens, stride=per_group), :] = (column == lane).astype(F32)
        for j, ref in enumerate(kv):
            end = 2 * kv_here * tokens
            docs = doc_columns(ref[end : end + INFO, :].astype(F32), tokens)
            bias = jnp.where(docs == lane, 0.0, -BIG).astype(BF16)
            for g in range(kv_here):
                at = slice(j * tokens, (j + 1) * tokens)
                keys_ext[g, at, 0:LANES] = ref[g * tokens : (g + 1) * tokens, :]
                keys_ext[g, at, LANES:] = bias
                begin = (kv_here + g) * tokens
                values_ext[g, at, 0:LANES] = ref[begin : begin + tokens, :]
                values_ext[g, at, LANES:] = jnp.ones((tokens, LANES), BF16)

    one_hot = doc_rep[pl.ds(pl.multiple_of(index * rows, rows), rows), :].astype(BF16)
    query_all = query_ref[...].astype(F32).reshape(step, heads, LANES)
    results = []
    for g in range(kv_here):
        query = query_all[:, g * per_group : (g + 1) * per_group, :].reshape(rows, LANES).astype(BF16)
        query = jnp.concatenate([query, one_hot], axis=1)
        scores = lax.dot_general(
            query, keys_ext[g], (((1,), (1,)), ((), ())), preferred_element_type=F32
        )
        if has_own:
            token = index * step + lax.broadcasted_iota(jnp.int32, (rows, tokens), 0) // per_group
            where_key = lax.broadcasted_iota(jnp.int32, (rows, tokens), 1)
            own = jnp.where(where_key <= token, scores[:, 0:tokens], -BIG)
            scores = own if blocks == 1 else jnp.concatenate([own, scores[:, tokens:]], axis=1)
        top = jnp.max(scores, axis=1, keepdims=True)
        if has_state:
            before = state_ref[g]
            top_before = before[:, 2 * LANES - 1 : 2 * LANES]
            top = jnp.maximum(top, top_before)
        weights = jnp.exp2((scores - top) * SCORE_TO_EXP2).astype(BF16)
        total = jnp.dot(weights, values_ext[g], preferred_element_type=F32)
        if has_state:
            total = total + before * jnp.exp2((top_before - top) * SCORE_TO_EXP2)
        if is_last:
            results.append(total[:, 0:LANES] / total[:, LANES : LANES + 1])
        else:
            lane = lax.broadcasted_iota(jnp.int32, (rows, 2 * LANES), 1)
            out_ref[g] = jnp.where(lane == 2 * LANES - 1, top, total)
    if is_last:
        results = [r.reshape(step, per_group, LANES) for r in results]
        out = results[0] if kv_here == 1 else jnp.concatenate(results, axis=1)
        out_ref[...] = out.reshape(step * heads, LANES).astype(BF16)


def attend(doc_rows, query, kv, state, is_last, has_own, tokens, heads, kv_here):
    step = 64
    per_group = heads // kv_here
    blocks = len(kv)
    span = blocks * tokens
    whole = lambda shape: pl.BlockSpec(shape, lambda i: (0,) * len(shape))
    state_spec = pl.BlockSpec((kv_here, step * per_group, 2 * LANES), lambda i: (0, i, 0))
    row_spec = pl.BlockSpec((step * heads, LANES), lambda i: (i, 0))
    in_specs = [whole((INFO, LANES)), row_spec] + [whole(kv[0].shape)] * blocks
    operands = [doc_rows, query, *kv]
    if state is not None:
        in_specs.append(state_spec)
        operands.append(state)
    if is_last:
        out_shape, out_spec = sds((tokens * heads, LANES), BF16), row_spec
    else:
        out_shape = sds((kv_here, tokens * per_group, 2 * LANES), F32)
        out_spec = state_spec
    moved = 2 * tokens * heads * LANES * 2 + blocks * kv[0].size * 2 + 4 * tokens * heads * LANES * 2
    return pl.pallas_call(
        functools.partial(
            attend_kernel, tokens, step, heads, kv_here, blocks, has_own, state is not None, is_last
        ),
        grid=(tokens // step,),
        out_shape=out_shape,
        in_specs=in_specs,
        out_specs=out_spec,
        scratch_shapes=[
            pltpu.VMEM((kv_here, span, 2 * LANES), BF16),
            pltpu.VMEM((kv_here, span, 2 * LANES), BF16),
            pltpu.VMEM((tokens * per_group, LANES), F32),
            pltpu.VMEM((tokens, LANES), F32),
        ],
        compiler_params=params(40),
        cost_estimate=cost(4 * tokens * heads * span * 2 * LANES, moved, tokens * heads * span),
        name="attend",
    )(*operands)


def body(
    blocks,
    lin_query,
    lin_key,
    lin_value,
    lin_gate,
    log_decay,
    norm_gain,
    doc_ids,
    soft_query,
    soft_key,
    soft_value,
):
    tokens, heads, _ = lin_query.shape
    tensor = HEADS // heads
    kv_here = max(1, heads // GROUP)
    half = heads // 2
    pieces = 2 if half % 2 == 0 else 1
    count = half // pieces
    longest = blocks * tokens * 5 // 8
    window = min(blocks - 1, (longest - 1 + tokens - 1) // tokens)
    flat = lambda x: x.reshape(-1, LANES)
    block = lax.axis_index("seq")
    y = (block % 2).astype(jnp.int32).reshape(1)
    start = (lax.axis_index("tp") * heads // GROUP).astype(jnp.int32).reshape(1)
    doc_rows = (doc_ids + 1).astype(F32).reshape(tokens // LANES, LANES)
    doc_rows = jnp.pad(doc_rows, ((0, INFO - tokens // LANES), (0, 0)))

    def send(x, pairs):
        return lax.ppermute(x, "seq", [p for p in pairs if 0 <= p[0] < blocks and 0 <= p[1] < blocks])

    everyone = range(blocks)
    swap = [(b, b ^ 1) for b in everyone]

    own_kv = pack_kv(start, flat(soft_key), flat(soft_value), doc_rows, tokens, kv_here)
    beside = send(own_kv, [(b, b + 1) for b in everyone if b % 2 == 0])
    lane_kv, cross_kv = [], []
    ahead = own_kv
    for back in range(1, window // 2 + 1):
        ahead = send(ahead, [(b, b + 2) for b in everyone if b >= 2 * (back - 1)])
        lane_kv.append(ahead)
        cross_kv.append(send(ahead, [p for p in swap if p[0] >= 2 * back]))
    extra_kv = []
    if window % 2:
        extra_kv.append(send(own_kv, [(b, b + window) for b in everyone if b % 2 == 1]))

    keep, other, info = block_state(y, log_decay, doc_rows, flat(lin_key), flat(lin_value), tokens, heads)
    size = count * HEAD_DIM
    other_info = None
    came = []
    for piece in range(pieces):
        sent = other[piece * size : (piece + 1) * size]
        if piece == 0:
            sent = jnp.concatenate([sent, other[half * HEAD_DIM :]], axis=0)
        got = send(sent, swap)
        if piece == 0:
            other_info = got[size:]
        came.append([got])
    rows = blocks // 2
    latest = [None] * pieces
    arrived = [[] for _ in range(pieces)]
    held = [keep[p * size : (p + 1) * size] for p in range(pieces)]
    for row in range(rows - 1):
        for p in range(pieces):
            out = chain_step(y, held[p], info, came[p][0], other_info, latest[p], p * count, count)
            latest[p] = send(out, [(2 * row, 2 * row + 2), (2 * row + 1, 2 * row + 3)])
            arrived[p].append(latest[p])
    mine, far = [], []
    prior_doc = None
    for p in range(pieces):
        got, sent, prior_doc = prior_states(
            y, held[p], info, came[p][0], other_info, arrived[p], p * count, count
        )
        mine.append(got)
        far.append(send(sent, swap))

    inner, qh, grow = inner_part(
        log_decay, doc_rows, flat(lin_query), flat(lin_key), flat(lin_value), tokens, heads
    )

    query = flat(soft_query)
    early = [own_kv, beside] + lane_kv[:1]
    late = lane_kv[1:] + cross_kv + extra_kv
    state = attend(doc_rows, query, early, None, False, True, tokens, heads, kv_here)
    soft_out = attend(doc_rows, query, late, state, True, False, tokens, heads, kv_here)

    mixed, squares = mix(y, doc_rows, prior_doc, grow, inner, qh, mine, far, tokens, heads)
    sums = [squares]
    for shift in range(1, tensor):
        sums.append(
            lax.ppermute(squares, "tp", [(t, (t + shift) % tensor) for t in range(tensor)])
        )
    lin_out = finish(norm_gain, flat(lin_gate), mixed, sums, tokens, heads)
    shape = (tokens, heads, HEAD_DIM)
    return lin_out.reshape(shape), soft_out.reshape(shape)


def solution(mesh):
    in_specs = (
        P("seq", "tp", None),
        P("seq", "tp", None),
        P("seq", "tp", None),
        P("seq", "tp", None),
        P("seq", "tp"),
        P("tp", None),
        P("seq"),
        P("seq", "tp", None),
        P("seq", None, None),
        P("seq", None, None),
    )
    out_specs = (P("seq", "tp", None), P("seq", "tp", None))
    return jax.shard_map(
        functools.partial(body, mesh.shape["seq"]),
        mesh=mesh,
        in_specs=in_specs,
        out_specs=out_specs,
        check_vma=False,
    )
```

time: 194 us -> 83.9 us (0.43)
  the two profiles are of different devices: /device:TPU:0 before, /device:TPU:25 now
where the time goes in v1:
time: 83.9 us; the launch traced here: 83.4 us
  Pallas kernels  31.5 us (38%)
  starting transfers between devices  29.8 us (36%)
  waiting for transfers between devices  17 us (20%)
  local copies, waits for them, and re-layouts  3.35 us (4%)
  between operations  1.05 us (1%)
    ppermute x16, starting transfers between devices, send(): lax.ppermute(x, 'seq', [p for p in pairs if 0 <= p[0] < blocks and 0 <= p...  21.9 us
    pallas_call x2, Pallas kernels, attend(): pl.pallas_call(functools.partial(attend_kernel, tokens, step, heads, kv_h...  18.4 us
    ppermute x16, waiting for transfers between devices, send(): lax.ppermute(x, 'seq', [p for p in pairs if 0 <= p[0] < blocks and 0 <= p...  17 us
    ppermute x3, starting transfers between devices, body(): lax.ppermute(squares, 'tp', [(t, (t + shift) % tensor) for t in range(ten...  7.92 us
    pallas_call x1, Pallas kernels, inner_part(): pl.pallas_call(functools.partial(inner_kernel, tokens, heads), out_shape=...  4.74 us
    unnamed x23, local copies, waits for them, and re-layouts  3.31 us
    pallas_call x1, Pallas kernels, block_state(): pl.pallas_call(functools.partial(state_kernel, tokens, heads), out_shape=...  3.02 us
    pallas_call x1, Pallas kernels, finish(): pl.pallas_call(functools.partial(finish_kernel, tokens, heads, len(square...  1.72 us
  transfers between devices with their start and end apart: 19, of which 7 were waited for; matrix products, arithmetic and copies ran while one was open for 0% of the time, Pallas kernels for 20%

profile of v1, /device:TPU:25, one launch (start us, length us, event | category | flops | bytes accessed | tf_op | source)
XLA Modules:
  0.0 83.4 jit_solution(5294360242267760558)
XLA Ops:
  0.6 0.7 convert_bitcast_fusion
  1.3 0.8 copy.12.ld_ref
  2.2 0.0 copy-start
  2.2 1.2 %copy-done = bf16[256,16,128]{2,1,0:T(8,128)(2,1)S(1)} copy-done((bf16[256,16,128]{2,1,0:T(8,128)(2,1)S(1)}, bf16[256,16,128]{2,1,0:T(8,128)(2,1)}, u32[]{:S(2)}) %copy-start) | copy-done | bytes 1048600
  3.4 1.2 %copy-done.2 = bf16[256,16,128]{2,1,0:T(8,128)(2,1)S(1)} copy-done((bf16[256,16,128]{2,1,0:T(8,128)(2,1)S(1)}, bf16[256,16,128]{2,1,0:T(8,128)(2,1)}, u32[]{:S(2)}) %copy-start.2) | copy-done | bytes 1048600
  4.6 3.0 %block_state.1 = (bf16[1024,128]{1,0:T(8,128)(2,1)S(1)}, bf16[1040,128]{1,0:T(8,128)(2,1)S(1)}, bf16[16,128]{1,0:T(8,128)(2,1)S(1)}) custom-call(s32[1]{0:T(128)} %bitcast.1.y_ref, f32[256,16]{1,0:T(8,128)S(1)} %copy.12.ld_ref, f32[16,128]{1,0:T(8,128)S(1)} %pad.4.doc_ref.refs_0_, bf16[4096,128]{1,0:T(8,128)(2,1)S(1)} %bitcast.14, bf16[4096,128]{1,0:T(8,128)(2,1)S(1)} %bitcast.16), custom_call_target="tpu_custom_call" | custom-call | flops 134217728 | bytes 3145728 | tf_op jit(solution)/shard_map/block_state/pallas_call | solution.py:141
  7.7 1.3 %collective-permute-start.1 = (bf16[528,128]{1,0:T(8,128)(2,1)S(1)}, bf16[528,128]{1,0:T(8,128)(2,1)S(1)}, u32[]{:S(2)}, u32[]{:S(2)}) collective-permute-start(bf16[528,128]{1,0:T(8,128)(2,1)S(1)} %pad_maximum_fusion), channel_id=1, source_target_pairs={{0,4},{4,0},{8,12},{12,8},{16,20},{20,16},{24,28},{28,24},{1,5},{5... | collective-permute-start | bytes 405512 | tf_op jit(solution)/shard_map/ppermute | solution.py:508
  9.0 0.2 collective-permute-start
  9.3 3.0 %collective-permute-done.1.refs_2_ = bf16[528,128]{1,0:T(8,128)(2,1)S(1)} collective-permute-done((bf16[528,128]{1,0:T(8,128)(2,1)S(1)}, bf16[528,128]{1,0:T(8,128)(2,1)S(1)}, u32[]{:S(2)}, u32[]{:S(2)}) %collective-permute-start.1) | collective-permute-done | bytes 135200 | tf_op jit(solution)/shard_map/ppermute | solution.py:508
  12.2 0.1 chain_step.9
  12.4 0.7 collective-permute-start.5
  13.0 2.0 %collective-permute-done.refs_2_ = bf16[512,128]{1,0:T(8,128)(2,1)S(1)} collective-permute-done((bf16[512,128]{1,0:T(8,128)(2,1)S(1)}, bf16[512,128]{1,0:T(8,128)(2,1)S(1)}, u32[]{:S(2)}, u32[]{:S(2)}) %collective-permute-start) | collective-permute-done | bytes 131104 | tf_op jit(solution)/shard_map/ppermute | solution.py:508
  15.0 0.1 chain_step.6
  15.2 0.7 collective-permute-start.2
  15.9 0.3 pack_kv.1.refs_2_
  16.2 0.0 copy-start.1
  16.2 0.0 copy-start.3
  16.2 1.6 %collective-permute-start.13 = (bf16[1040,128]{1,0:T(8,128)(2,1)S(1)}, bf16[1040,128]{1,0:T(8,128)(2,1)S(1)}, u32[]{:S(2)}, u32[]{:S(2)}) collective-permute-start(bf16[1040,128]{1,0:T(8,128)(2,1)S(1)} %pack_kv.1.refs_2_), channel_id=1, source_target_pairs={{0,8},{4,12},{8,16},{12,20},{16,24},{20,28},{1,9},{5,13},{9,17},{1... | collective-permute-start | bytes 798728 | tf_op jit(solution)/shard_map/ppermute | solution.py:508
  17.8 0.2 chain_step.10
  18.0 0.7 collective-permute-start.6
  18.6 0.2 chain_step.7
  18.8 0.7 collective-permute-start.3
  19.5 0.2 chain_step.11
  19.7 1.3 %collective-permute-start.7 = (bf16[528,128]{1,0:T(8,128)(2,1)S(1)}, bf16[528,128]{1,0:T(8,128)(2,1)S(1)}, u32[]{:S(2)}, u32[]{:S(2)}) collective-permute-start(bf16[528,128]{1,0:T(8,128)(2,1)S(1)} %chain_step.11), channel_id=1, source_target_pairs={{16,24},{20,28},{17,25},{21,29},{18,26},{22,30},{19,27},{23,31}} | collective-permute-start | bytes 405512 | tf_op jit(solution)/shard_map/ppermute | solution.py:508
  21.0 0.2 chain_step.8
  21.2 1.3 %collective-permute-start.4 = (bf16[528,128]{1,0:T(8,128)(2,1)S(1)}, bf16[528,128]{1,0:T(8,128)(2,1)S(1)}, u32[]{:S(2)}, u32[]{:S(2)}) collective-permute-start(bf16[528,128]{1,0:T(8,128)(2,1)S(1)} %chain_step.8), channel_id=1, source_target_pairs={{16,24},{20,28},{17,25},{21,29},{18,26},{22,30},{19,27},{23,31}} | collective-permute-start | bytes 405512 | tf_op jit(solution)/shard_map/ppermute | solution.py:508
  22.5 2.2 %collective-permute-done.13.refs_4_ = bf16[1040,128]{1,0:T(8,128)(2,1)S(1)} collective-permute-done((bf16[1040,128]{1,0:T(8,128)(2,1)S(1)}, bf16[1040,128]{1,0:T(8,128)(2,1)S(1)}, u32[]{:S(2)}, u32[]{:S(2)}) %collective-permute-start.13) | collective-permute-done | bytes 266272 | tf_op jit(solution)/shard_map/ppermute | solution.py:508
  24.7 1.3 %collective-permute-start.14 = (bf16[1040,128]{1,0:T(8,128)(2,1)S(1)}, bf16[1040,128]{1,0:T(8,128)(2,1)S(1)}, u32[]{:S(2)}, u32[]{:S(2)}) collective-permute-start(bf16[1040,128]{1,0:T(8,128)(2,1)S(1)} %collective-permute-done.13.refs_4_), channel_id=1, source_target_pairs={{8,16},{12,20},{16,24},{20,28},{9,17},{13,21},{17,25},{21,29},{10,... | collective-permute-start | bytes 798728 | tf_op jit(solution)/shard_map/ppermute | solution.py:508
  26.0 3.2 %collective-permute-start.18 = (bf16[1040,128]{1,0:T(8,128)(2,1)S(1)}, bf16[1040,128]{1,0:T(8,128)(2,1)S(1)}, u32[]{:S(2)}, u32[]{:S(2)}) collective-permute-start(bf16[1040,128]{1,0:T(8,128)(2,1)S(1)} %pack_kv.1.refs_2_), channel_id=1, source_target_pairs={{0,4},{8,12},{16,20},{24,28},{1,5},{9,13},{17,21},{25,29},{2,6},{1... | collective-permute-start | bytes 798728 | tf_op jit(solution)/shard_map/ppermute | solution.py:508
  29.2 2.5 %collective-permute-done.7.refs_6_ = bf16[528,128]{1,0:T(8,128)(2,1)S(1)} collective-permute-done((bf16[528,128]{1,0:T(8,128)(2,1)S(1)}, bf16[528,128]{1,0:T(8,128)(2,1)S(1)}, u32[]{:S(2)}, u32[]{:S(2)}) %collective-permute-start.7) | collective-permute-done | bytes 135200 | tf_op jit(solution)/shard_map/ppermute | solution.py:508
  31.6 0.7 prior_states.3
  32.3 1.3 %collective-permute-start.8 = (bf16[512,128]{1,0:T(8,128)(2,1)S(1)}, bf16[512,128]{1,0:T(8,128)(2,1)S(1)}, u32[]{:S(2)}, u32[]{:S(2)}) collective-permute-start(bf16[512,128]{1,0:T(8,128)(2,1)S(1)} %get-tuple-element.24), channel_id=1, source_target_pairs={{0,4},{4,0},{8,12},{12,8},{16,20},{20,16},{24,28},{28,24},{1,5},{5... | collective-permute-start | bytes 393224 | tf_op jit(solution)/shard_map/ppermute | solution.py:508
  33.6 1.5 %collective-permute-done.4.refs_6_ = bf16[528,128]{1,0:T(8,128)(2,1)S(1)} collective-permute-done((bf16[528,128]{1,0:T(8,128)(2,1)S(1)}, bf16[528,128]{1,0:T(8,128)(2,1)S(1)}, u32[]{:S(2)}, u32[]{:S(2)}) %collective-permute-start.4) | collective-permute-done | bytes 135200 | tf_op jit(solution)/shard_map/ppermute | solution.py:508
  35.1 0.2 prior_states.2
  35.2 1.3 %collective-permute-start.9 = (bf16[512,128]{1,0:T(8,128)(2,1)S(1)}, bf16[512,128]{1,0:T(8,128)(2,1)S(1)}, u32[]{:S(2)}, u32[]{:S(2)}) collective-permute-start(bf16[512,128]{1,0:T(8,128)(2,1)S(1)} %get-tuple-element.25), channel_id=1, source_target_pairs={{0,4},{4,0},{8,12},{12,8},{16,20},{20,16},{24,28},{28,24},{1,5},{5... | collective-permute-start | bytes 393224 | tf_op jit(solution)/shard_map/ppermute | solution.py:508
  36.6 4.7 %inner_part.1 = (f32[4096,128]{1,0:T(8,128)S(1)}, bf16[4096,128]{1,0:T(8,128)(2,1)S(1)}, f32[256,128]{1,0:T(8,128)S(1)}) custom-call(f32[256,16]{1,0:T(8,128)S(1)} %copy.12.ld_ref, f32[16,256]{1,0:T(8,128)S(1)} %bitcast.22, f32[16,128]{1,0:T(8,128)S(1)} %pad.4.doc_ref.refs_0_, bf16[4096,128]{1,0:T(8,128)(2,1)S(1)} %bitcast.18, ...), custom_call_target="tpu_custom_call" | custom-call | flops 536870912 | bytes 6291456 | tf_op jit(solution)/shard_map/inner_part/pallas_call | solution.py:287
  41.3 1.6 %mix.1 = (f32[4096,128]{1,0:T(8,128)S(1)}, f32[8,256]{1,0:T(8,128)S(1)}) custom-call(s32[1]{0:T(128)} %bitcast.1.y_ref, f32[16,128]{1,0:T(8,128)S(1)} %pad.4.doc_ref.refs_0_, f32[8,128]{1,0:T(8,128)S(1)} %get-tuple-element.18.prior_doc_ref, f32[256,128]{1,0:T(8,128)S(1)} %get-tuple-element.19.grow_ref, f32[4096,128]{1,0:T(8,128)S(1)} %get-tuple-element.20.inner_ref, ...), custom_call_target="tpu_custom_call" | custom-call | flops 134217728 | bytes 5242880 | tf_op jit(solution)/shard_map/mix/pallas_call | solution.py:336
  42.9 6.9 %collective-permute-start.10 = (f32[8,256]{1,0:T(8,128)S(1)}, f32[8,256]{1,0:T(8,128)S(1)}, u32[]{:S(2)}, u32[]{:S(2)}) collective-permute-start(f32[8,256]{1,0:T(8,128)S(1)} %get-tuple-element.27.refs_0_), channel_id=1, source_target_pairs={{0,1},{1,2},{2,3},{3,0},{4,5},{5,6},{6,7},{7,4},{8,9},{9,10},{10,1... | collective-permute-start | bytes 24584 | tf_op jit(solution)/shard_map/ppermute | solution.py:569
  49.8 1.3 %collective-permute-start.17 = (bf16[1040,128]{1,0:T(8,128)(2,1)S(1)}, bf16[1040,128]{1,0:T(8,128)(2,1)S(1)}, u32[]{:S(2)}, u32[]{:S(2)}) collective-permute-start(bf16[1040,128]{1,0:T(8,128)(2,1)S(1)} %pack_kv.1.refs_2_), channel_id=1, source_target_pairs={{4,24},{5,25},{6,26},{7,27}} | collective-permute-start | bytes 798728 | tf_op jit(solution)/shard_map/ppermute | solution.py:508
  51.1 1.9 %collective-permute-start.15 = (bf16[1040,128]{1,0:T(8,128)(2,1)S(1)}, bf16[1040,128]{1,0:T(8,128)(2,1)S(1)}, u32[]{:S(2)}, u32[]{:S(2)}) collective-permute-start(bf16[1040,128]{1,0:T(8,128)(2,1)S(1)} %collective-permute-done.13.refs_4_), channel_id=1, source_target_pairs={{8,12},{12,8},{16,20},{20,16},{24,28},{28,24},{9,13},{13,9},{17,21... | collective-permute-start | bytes 798728 | tf_op jit(solution)/shard_map/ppermute | solution.py:508
  53.0 3.4 %collective-permute-start.16 = (bf16[1040,128]{1,0:T(8,128)(2,1)S(1)}, bf16[1040,128]{1,0:T(8,128)(2,1)S(1)}, u32[]{:S(2)}, u32[]{:S(2)}) collective-permute-start(bf16[1040,128]{1,0:T(8,128)(2,1)S(1)} %collective-permute-done.14.refs_2_), channel_id=1, source_target_pairs={{16,20},{20,16},{24,28},{28,24},{17,21},{21,17},{25,29},{29,25},{1... | collective-permute-start | bytes 798728 | tf_op jit(solution)/shard_map/ppermute | solution.py:508
  56.4 0.3 collective-permute-start.11
  56.7 0.7 collective-permute-start.12
  57.5 6.8 %attend.2.refs_6_ = f32[2,2048,256]{2,1,0:T(8,128)S(1)} custom-call(f32[16,128]{1,0:T(8,128)S(1)} %pad.4.doc_ref.refs_0_, bf16[4096,128]{1,0:T(8,128)(2,1)S(1)} %bitcast.23, bf16[1040,128]{1,0:T(8,128)(2,1)S(1)} %pack_kv.1.refs_2_, bf16[1040,128]{1,0:T(8,128)(2,1)S(1)} %collective-permute-done.18.refs_3_, bf16[1040,128]{1,0:T(8,128)(2,1)S(1)} %collective-permute-done.13.refs_4_), custom_call_target="tpu_custom_call" | custom-call | flops 3221225472 | bytes 7090176 | tf_op jit(solution)/shard_map/attend/pallas_call | solution.py:459
  64.4 1.7 %finish.1 = bf16[4096,128]{1,0:T(8,128)(2,1)} custom-call(f32[16,128]{1,0:T(8,128)S(1)} %copy-done.9, bf16[4096,128]{1,0:T(8,128)(2,1)S(1)} %bitcast.19, f32[4096,128]{1,0:T(8,128)S(1)} %get-tuple-element.26.mixed_ref, f32[8,256]{1,0:T(8,128)S(1)} %get-tuple-element.27.refs_0_, f32[8,256]{1,0:T(8,128)S(1)} %collective-permute-done.10.refs_1_, ...), custom_call_target="tpu_custom_call" | custom-call | bytes 4194304 | tf_op jit(solution)/shard_map/finish/pallas_call | solution.py:366
  66.1 1.0 %collective-permute-done.15.refs_3_ = bf16[1040,128]{1,0:T(8,128)(2,1)S(1)} collective-permute-done((bf16[1040,128]{1,0:T(8,128)(2,1)S(1)}, bf16[1040,128]{1,0:T(8,128)(2,1)S(1)}, u32[]{:S(2)}, u32[]{:S(2)}) %collective-permute-start.15) | collective-permute-done | bytes 266272 | tf_op jit(solution)/shard_map/ppermute | solution.py:508
  67.0 4.8 %collective-permute-done.16.refs_4_ = bf16[1040,128]{1,0:T(8,128)(2,1)S(1)} collective-permute-done((bf16[1040,128]{1,0:T(8,128)(2,1)S(1)}, bf16[1040,128]{1,0:T(8,128)(2,1)S(1)}, u32[]{:S(2)}, u32[]{:S(2)}) %collective-permute-start.16) | collective-permute-done | bytes 266272 | tf_op jit(solution)/shard_map/ppermute | solution.py:508
  71.9 11.5 %attend.3 = bf16[4096,128]{1,0:T(8,128)(2,1)} custom-call(f32[16,128]{1,0:T(8,128)S(1)} %pad.4.doc_ref.refs_0_, bf16[4096,128]{1,0:T(8,128)(2,1)S(1)} %bitcast.24, bf16[1040,128]{1,0:T(8,128)(2,1)S(1)} %collective-permute-done.14.refs_2_, bf16[1040,128]{1,0:T(8,128)(2,1)S(1)} %collective-permute-done.15.refs_3_, ...), custom_call_target="tpu_custom_call" | custom-call | flops 4294967296 | bytes 7356416 | tf_op jit(solution)/shard_map/attend/pallas_call | solution.py:459
  (35 shorter events, 0.1 us)
Async XLA Ops:
  2.2 1.2 %copy-start = (bf16[256,16,128]{2,1,0:T(8,128)(2,1)S(1)}, bf16[256,16,128]{2,1,0:T(8,128)(2,1)}, u32[]{:S(2)}) copy-start(bf16[256,16,128]{2,1,0:T(8,128)(2,1)} %param.11) | copy-start | bytes 3145732
  3.4 1.2 %copy-start.2 = (bf16[256,16,128]{2,1,0:T(8,128)(2,1)S(1)}, bf16[256,16,128]{2,1,0:T(8,128)(2,1)}, u32[]{:S(2)}) copy-start(bf16[256,16,128]{2,1,0:T(8,128)(2,1)} %param.12) | copy-start | bytes 3145732
  4.6 11.3 %copy-start.6 = (bf16[256,8,128]{2,1,0:T(8,128)(2,1)S(1)}, bf16[256,8,128]{2,1,0:T(8,128)(2,1)}, u32[]{:S(2)}) copy-start(bf16[256,8,128]{2,1,0:T(8,128)(2,1)} %param.18) | copy-start | bytes 1572868
  4.6 11.3 %copy-start.7 = (bf16[256,8,128]{2,1,0:T(8,128)(2,1)S(1)}, bf16[256,8,128]{2,1,0:T(8,128)(2,1)}, u32[]{:S(2)}) copy-start(bf16[256,8,128]{2,1,0:T(8,128)(2,1)} %param.19) | copy-start | bytes 1572868
  7.7 4.5 %collective-permute-start.1 = (bf16[528,128]{1,0:T(8,128)(2,1)S(1)}, bf16[528,128]{1,0:T(8,128)(2,1)S(1)}, u32[]{:S(2)}, u32[]{:S(2)}) collective-permute-start(bf16[528,128]{1,0:T(8,128)(2,1)S(1)} %pad_maximum_fusion), channel_id=1, source_target_pairs={{0,4},{4,0},{8,12},{12,8},{16,20},{20,16},{24,28},{28,24},{1,5},{5... | collective-permute-start | bytes 405512 | tf_op jit(solution)/shard_map/ppermute | solution.py:508
  9.0 6.0 %collective-permute-start = (bf16[512,128]{1,0:T(8,128)(2,1)S(1)}, bf16[512,128]{1,0:T(8,128)(2,1)S(1)}, u32[]{:S(2)}, u32[]{:S(2)}) collective-permute-start(bf16[512,128]{1,0:T(8,128)(2,1)S(1)} %get-tuple-element.29), channel_id=1, source_target_pairs={{0,4},{4,0},{8,12},{12,8},{16,20},{20,16},{24,28},{28,24},{1,5},{5... | collective-permute-start | bytes 393224 | tf_op jit(solution)/shard_map/ppermute | solution.py:508
  12.4 5.4 %collective-permute-start.5 = (bf16[528,128]{1,0:T(8,128)(2,1)S(1)}, bf16[528,128]{1,0:T(8,128)(2,1)S(1)}, u32[]{:S(2)}, u32[]{:S(2)}) collective-permute-start(bf16[528,128]{1,0:T(8,128)(2,1)S(1)} %chain_step.9), channel_id=1, source_target_pairs={{0,8},{4,12},{1,9},{5,13},{2,10},{6,14},{3,11},{7,15}} | collective-permute-start | bytes 405512 | tf_op jit(solution)/shard_map/ppermute | solution.py:508
  15.2 3.5 %collective-permute-start.2 = (bf16[528,128]{1,0:T(8,128)(2,1)S(1)}, bf16[528,128]{1,0:T(8,128)(2,1)S(1)}, u32[]{:S(2)}, u32[]{:S(2)}) collective-permute-start(bf16[528,128]{1,0:T(8,128)(2,1)S(1)} %chain_step.6), channel_id=1, source_target_pairs={{0,8},{4,12},{1,9},{5,13},{2,10},{6,14},{3,11},{7,15}} | collective-permute-start | bytes 405512 | tf_op jit(solution)/shard_map/ppermute | solution.py:508
  16.2 20.4 %copy-start.1 = (bf16[256,16,128]{2,1,0:T(8,128)(2,1)S(1)}, bf16[256,16,128]{2,1,0:T(8,128)(2,1)}, u32[]{:S(2)}) copy-start(bf16[256,16,128]{2,1,0:T(8,128)(2,1)} %param.11) | copy-start | bytes 3145732
  16.2 20.4 %copy-start.3 = (bf16[256,16,128]{2,1,0:T(8,128)(2,1)S(1)}, bf16[256,16,128]{2,1,0:T(8,128)(2,1)}, u32[]{:S(2)}) copy-start(bf16[256,16,128]{2,1,0:T(8,128)(2,1)} %param.12) | copy-start | bytes 3145732
  16.2 20.4 %copy-start.4 = (bf16[256,16,128]{2,1,0:T(8,128)(2,1)S(1)}, bf16[256,16,128]{2,1,0:T(8,128)(2,1)}, u32[]{:S(2)}) copy-start(bf16[256,16,128]{2,1,0:T(8,128)(2,1)} %param.10) | copy-start | bytes 3145732
  16.2 20.4 %copy-start.8 = (f32[256,16]{0,1:T(8,128)S(1)}, f32[256,16]{0,1:T(8,128)}, u32[]{:S(2)}) copy-start(f32[256,16]{0,1:T(8,128)} %param.14) | copy-start | bytes 49156
  16.2 8.5 %collective-permute-start.13 = (bf16[1040,128]{1,0:T(8,128)(2,1)S(1)}, bf16[1040,128]{1,0:T(8,128)(2,1)S(1)}, u32[]{:S(2)}, u32[]{:S(2)}) collective-permute-start(bf16[1040,128]{1,0:T(8,128)(2,1)S(1)} %pack_kv.1.refs_2_), channel_id=1, source_target_pairs={{0,8},{4,12},{8,16},{12,20},{16,24},{20,28},{1,9},{5,13},{9,17},{1... | collective-permute-start | bytes 798728 | tf_op jit(solution)/shard_map/ppermute | solution.py:508
  18.0 1.6 %collective-permute-start.6 = (bf16[528,128]{1,0:T(8,128)(2,1)S(1)}, bf16[528,128]{1,0:T(8,128)(2,1)S(1)}, u32[]{:S(2)}, u32[]{:S(2)}) collective-permute-start(bf16[528,128]{1,0:T(8,128)(2,1)S(1)} %chain_step.10), channel_id=1, source_target_pairs={{8,16},{12,20},{9,17},{13,21},{10,18},{14,22},{11,19},{15,23}} | collective-permute-start | bytes 405512 | tf_op jit(solution)/shard_map/ppermute | solution.py:508
  18.8 2.2 %collective-permute-start.3 = (bf16[528,128]{1,0:T(8,128)(2,1)S(1)}, bf16[528,128]{1,0:T(8,128)(2,1)S(1)}, u32[]{:S(2)}, u32[]{:S(2)}) collective-permute-start(bf16[528,128]{1,0:T(8,128)(2,1)S(1)} %chain_step.7), channel_id=1, source_target_pairs={{8,16},{12,20},{9,17},{13,21},{10,18},{14,22},{11,19},{15,23}} | collective-permute-start | bytes 405512 | tf_op jit(solution)/shard_map/ppermute | solution.py:508
  19.7 11.9 %collective-permute-start.7 = (bf16[528,128]{1,0:T(8,128)(2,1)S(1)}, bf16[528,128]{1,0:T(8,128)(2,1)S(1)}, u32[]{:S(2)}, u32[]{:S(2)}) collective-permute-start(bf16[528,128]{1,0:T(8,128)(2,1)S(1)} %chain_step.11), channel_id=1, source_target_pairs={{16,24},{20,28},{17,25},{21,29},{18,26},{22,30},{19,27},{23,31}} | collective-permute-start | bytes 405512 | tf_op jit(solution)/shard_map/ppermute | solution.py:508
  21.2 13.9 %collective-permute-start.4 = (bf16[528,128]{1,0:T(8,128)(2,1)S(1)}, bf16[528,128]{1,0:T(8,128)(2,1)S(1)}, u32[]{:S(2)}, u32[]{:S(2)}) collective-permute-start(bf16[528,128]{1,0:T(8,128)(2,1)S(1)} %chain_step.8), channel_id=1, source_target_pairs={{16,24},{20,28},{17,25},{21,29},{18,26},{22,30},{19,27},{23,31}} | collective-permute-start | bytes 405512 | tf_op jit(solution)/shard_map/ppermute | solution.py:508
  24.7 28.3 %collective-permute-start.14 = (bf16[1040,128]{1,0:T(8,128)(2,1)S(1)}, bf16[1040,128]{1,0:T(8,128)(2,1)S(1)}, u32[]{:S(2)}, u32[]{:S(2)}) collective-permute-start(bf16[1040,128]{1,0:T(8,128)(2,1)S(1)} %collective-permute-done.13.refs_4_), channel_id=1, source_target_pairs={{8,16},{12,20},{16,24},{20,28},{9,17},{13,21},{17,25},{21,29},{10,... | collective-permute-start | bytes 798728 | tf_op jit(solution)/shard_map/ppermute | solution.py:508
  26.0 30.4 %collective-permute-start.18 = (bf16[1040,128]{1,0:T(8,128)(2,1)S(1)}, bf16[1040,128]{1,0:T(8,128)(2,1)S(1)}, u32[]{:S(2)}, u32[]{:S(2)}) collective-permute-start(bf16[1040,128]{1,0:T(8,128)(2,1)S(1)} %pack_kv.1.refs_2_), channel_id=1, source_target_pairs={{0,4},{8,12},{16,20},{24,28},{1,5},{9,13},{17,21},{25,29},{2,6},{1... | collective-permute-start | bytes 798728 | tf_op jit(solution)/shard_map/ppermute | solution.py:508
  32.3 9.0 %collective-permute-start.8 = (bf16[512,128]{1,0:T(8,128)(2,1)S(1)}, bf16[512,128]{1,0:T(8,128)(2,1)S(1)}, u32[]{:S(2)}, u32[]{:S(2)}) collective-permute-start(bf16[512,128]{1,0:T(8,128)(2,1)S(1)} %get-tuple-element.24), channel_id=1, source_target_pairs={{0,4},{4,0},{8,12},{12,8},{16,20},{20,16},{24,28},{28,24},{1,5},{5... | collective-permute-start | bytes 393224 | tf_op jit(solution)/shard_map/ppermute | solution.py:508
  35.2 6.1 %collective-permute-start.9 = (bf16[512,128]{1,0:T(8,128)(2,1)S(1)}, bf16[512,128]{1,0:T(8,128)(2,1)S(1)}, u32[]{:S(2)}, u32[]{:S(2)}) collective-permute-start(bf16[512,128]{1,0:T(8,128)(2,1)S(1)} %get-tuple-element.25), channel_id=1, source_target_pairs={{0,4},{4,0},{8,12},{12,8},{16,20},{20,16},{24,28},{28,24},{1,5},{5... | collective-permute-start | bytes 393224 | tf_op jit(solution)/shard_map/ppermute | solution.py:508
  41.3 16.1 %copy-start.10 = (bf16[256,16,128]{2,1,0:T(8,128)(2,1)S(1)}, bf16[256,16,128]{2,1,0:T(8,128)(2,1)}, u32[]{:S(2)}) copy-start(bf16[256,16,128]{2,1,0:T(8,128)(2,1)} %param.17) | copy-start | bytes 3145732
  42.9 13.8 %collective-permute-start.10 = (f32[8,256]{1,0:T(8,128)S(1)}, f32[8,256]{1,0:T(8,128)S(1)}, u32[]{:S(2)}, u32[]{:S(2)}) collective-permute-start(f32[8,256]{1,0:T(8,128)S(1)} %get-tuple-element.27.refs_0_), channel_id=1, source_target_pairs={{0,1},{1,2},{2,3},{3,0},{4,5},{5,6},{6,7},{7,4},{8,9},{9,10},{10,1... | collective-permute-start | bytes 24584 | tf_op jit(solution)/shard_map/ppermute | solution.py:569
  49.8 16.3 %collective-permute-start.17 = (bf16[1040,128]{1,0:T(8,128)(2,1)S(1)}, bf16[1040,128]{1,0:T(8,128)(2,1)S(1)}, u32[]{:S(2)}, u32[]{:S(2)}) collective-permute-start(bf16[1040,128]{1,0:T(8,128)(2,1)S(1)} %pack_kv.1.refs_2_), channel_id=1, source_target_pairs={{4,24},{5,25},{6,26},{7,27}} | collective-permute-start | bytes 798728 | tf_op jit(solution)/shard_map/ppermute | solution.py:508
  51.1 16.0 %collective-permute-start.15 = (bf16[1040,128]{1,0:T(8,128)(2,1)S(1)}, bf16[1040,128]{1,0:T(8,128)(2,1)S(1)}, u32[]{:S(2)}, u32[]{:S(2)}) collective-permute-start(bf16[1040,128]{1,0:T(8,128)(2,1)S(1)} %collective-permute-done.13.refs_4_), channel_id=1, source_target_pairs={{8,12},{12,8},{16,20},{20,16},{24,28},{28,24},{9,13},{13,9},{17,21... | collective-permute-start | bytes 798728 | tf_op jit(solution)/shard_map/ppermute | solution.py:508
  53.0 18.9 %collective-permute-start.16 = (bf16[1040,128]{1,0:T(8,128)(2,1)S(1)}, bf16[1040,128]{1,0:T(8,128)(2,1)S(1)}, u32[]{:S(2)}, u32[]{:S(2)}) collective-permute-start(bf16[1040,128]{1,0:T(8,128)(2,1)S(1)} %collective-permute-done.14.refs_2_), channel_id=1, source_target_pairs={{16,20},{20,16},{24,28},{28,24},{17,21},{21,17},{25,29},{29,25},{1... | collective-permute-start | bytes 798728 | tf_op jit(solution)/shard_map/ppermute | solution.py:508
  56.4 7.9 %collective-permute-start.11 = (f32[8,256]{1,0:T(8,128)S(1)}, f32[8,256]{1,0:T(8,128)S(1)}, u32[]{:S(2)}, u32[]{:S(2)}) collective-permute-start(f32[8,256]{1,0:T(8,128)S(1)} %get-tuple-element.27.refs_0_), channel_id=1, source_target_pairs={{0,2},{1,3},{2,0},{3,1},{4,6},{5,7},{6,4},{7,5},{8,10},{9,11},{10,... | collective-permute-start | bytes 24584 | tf_op jit(solution)/shard_map/ppermute | solution.py:569
  56.7 7.6 %collective-permute-start.12 = (f32[8,256]{1,0:T(8,128)S(1)}, f32[8,256]{1,0:T(8,128)S(1)}, u32[]{:S(2)}, u32[]{:S(2)}) collective-permute-start(f32[8,256]{1,0:T(8,128)S(1)} %get-tuple-element.27.refs_0_), channel_id=1, source_target_pairs={{0,3},{1,0},{2,1},{3,2},{4,7},{5,4},{6,5},{7,6},{8,11},{9,8},{10,9... | collective-permute-start | bytes 24584 | tf_op jit(solution)/shard_map/ppermute | solution.py:569
  57.5 6.9 %copy-start.5 = (bf16[256,16,128]{2,1,0:T(8,128)(2,1)S(1)}, bf16[256,16,128]{2,1,0:T(8,128)(2,1)}, u32[]{:S(2)}) copy-start(bf16[256,16,128]{2,1,0:T(8,128)(2,1)} %param.13) | copy-start | bytes 3145732
  57.5 6.9 %copy-start.9 = (f32[16,128]{1,0:T(8,128)S(1)}, f32[16,128]{1,0:T(8,128)}, u32[]{:S(2)}) copy-start(f32[16,128]{1,0:T(8,128)} %gain_ref.1) | copy-start | bytes 24580

commit v2 on v1

v2 whole, which is shorter than its diff:
```python
import functools

import jax
import jax.numpy as jnp
import numpy as np
from jax import lax
from jax.experimental import pallas as pl
from jax.experimental.pallas import tpu as pltpu
from jax.sharding import PartitionSpec as P

HEADS = 64
HEAD_DIM = 128
KV_HEADS = 8
LANES = 128
GROUP = HEADS // KV_HEADS
F32 = jnp.float32
BF16 = jnp.bfloat16
BIG = float(2**20)
SCORE_TO_EXP2 = HEAD_DIM**-0.5 * float(np.log2(np.e))
INFO = 16
HIGHEST = lax.Precision.HIGHEST

VMEM = pl.BlockSpec(memory_space=pltpu.VMEM)
SMEM = pl.BlockSpec(memory_space=pltpu.SMEM)
ANYWHERE = pl.BlockSpec(memory_space=pl.ANY)
STATE_ROWS = HEAD_DIM + 16
CHUNK = 256


def sds(shape, dtype):
    return jax.ShapeDtypeStruct(shape, dtype)


def cost(flops, bytes_accessed, transcendentals=0):
    return pl.CostEstimate(
        flops=int(flops), bytes_accessed=int(bytes_accessed), transcendentals=int(transcendentals)
    )


def call(kernel, name, operands, out_shape, scratch=(), mib=16, estimate=None, scalars=(), after=()):
    outs = out_shape if isinstance(out_shape, tuple) else (out_shape,)
    begin = len(scalars) + len(operands)
    skip = len(after)

    def run(*refs):
        kernel(*refs[:begin], *refs[begin + skip :])

    return pl.pallas_call(
        run,
        out_shape=out_shape,
        in_specs=[SMEM] * len(scalars) + [VMEM] * len(operands) + [ANYWHERE] * skip,
        out_specs=(VMEM,) * len(outs) if isinstance(out_shape, tuple) else VMEM,
        scratch_shapes=list(scratch),
        compiler_params=pltpu.CompilerParams(vmem_limit_bytes=mib * 1024 * 1024),
        cost_estimate=estimate,
        name=name,
    )(*scalars, *operands, *after)


def doc_columns(doc_rows, tokens):
    parts = []
    for i in range(tokens // LANES):
        row = jnp.broadcast_to(doc_rows[i : i + 1, :], (LANES, LANES))
        parts.append(jnp.transpose(row))
    return jnp.concatenate(parts, axis=0)


def doc_line(doc_rows, tokens):
    return jnp.concatenate([doc_rows[i : i + 1, :] for i in range(tokens // LANES)], axis=1)


def doc_numbers(doc_ref):
    return doc_ref[...].astype(F32) + 1.0


def lower_triangle(tokens):
    rows = lax.broadcasted_iota(jnp.int32, (tokens, tokens), 0)
    cols = lax.broadcasted_iota(jnp.int32, (tokens, tokens), 1)
    return rows >= cols


def cumulative(ld_ref, ldp, tokens, heads):
    ldp[...] = jnp.zeros_like(ldp)
    ldp[0:heads, :] = ld_ref[...]
    return lax.dot_general(
        lower_triangle(tokens).astype(F32),
        ldp[...],
        (((1,), (1,)), ((), ())),
        precision=HIGHEST,
        preferred_element_type=F32,
    )


def pack_kernel(tokens, kv_here, start_ref, key_ref, value_ref, doc_ref, out_ref, scratch):
    start = start_ref[0]
    for which, ref in enumerate((key_ref, value_ref)):
        scratch[...] = ref[...].astype(F32)
        for g in range(kv_here):
            rows = scratch[pl.ds(start + g, tokens, stride=KV_HEADS), :]
            at = (which * kv_here + g) * tokens
            if which:
                halves = [jnp.transpose(rows[i : i + LANES, :]) for i in range(0, tokens, LANES)]
                rows = jnp.concatenate(halves, axis=0)
            out_ref[at : at + tokens, :] = rows.astype(BF16)
    end = 2 * kv_here * tokens
    docs = doc_numbers(doc_ref)
    line = lax.broadcasted_iota(jnp.int32, (INFO, LANES), 0)
    info = jnp.zeros((INFO, LANES), F32)
    for i in range(tokens // LANES):
        info = jnp.where(line == i, docs[i : i + 1, :], info)
    out_ref[end : end + INFO, :] = info.astype(BF16)


def pack_kv(start, soft_key, soft_value, docs, tokens, kv_here):
    return call(
        functools.partial(pack_kernel, tokens, kv_here),
        "pack_kv",
        [soft_key, soft_value, docs],
        sds((2 * kv_here * tokens + INFO, LANES), BF16),
        scratch=[pltpu.VMEM((tokens * KV_HEADS, LANES), F32)],
        estimate=cost(0, 4 * tokens * KV_HEADS * LANES * 2),
        scalars=[start],
    )


def state_kernel(tokens, heads, y_ref, ld_ref, doc_ref, key_ref, value_ref, keep_ref, send_ref, info_ref, kf, vf, states, ldp):
    half = heads // 2
    y = y_ref[0]
    cumul = cumulative(ld_ref, ldp, tokens, heads)
    total = cumul[tokens - 1 : tokens, :]
    docs = doc_numbers(doc_ref)
    last_row = tokens // LANES - 1
    first_doc = docs[0:1, 0:1]
    last_doc = docs[last_row : last_row + 1, LANES - 1 : LANES]
    tail = (doc_columns(docs, tokens) == last_doc).astype(F32)
    scale = jnp.exp(total - cumul) * tail
    kf[...] = key_ref[...].astype(F32)
    vf[...] = value_ref[...].astype(F32)
    for h in range(heads):
        keys = (kf[pl.ds(h, tokens, stride=heads), :] * scale[:, h : h + 1]).astype(BF16)
        values = vf[pl.ds(h, tokens, stride=heads), :].astype(BF16)
        states[h * HEAD_DIM : (h + 1) * HEAD_DIM, :] = lax.dot_general(
            keys, values, (((0,), (0,)), ((), ())), preferred_element_type=F32
        )
    size = half * HEAD_DIM
    keep_ref[...] = states[pl.ds(pl.multiple_of(y * size, size), size), :].astype(BF16)
    send_ref[0:size, :] = states[pl.ds(pl.multiple_of((1 - y) * size, size), size), :].astype(BF16)
    upper = pltpu.roll(total, LANES - half, 1)
    rows = lax.broadcasted_iota(jnp.int32, (INFO, LANES), 0)

    def info_of(totals):
        hi = totals.astype(BF16).astype(F32)
        mid = (totals - hi).astype(BF16).astype(F32)
        lo = totals - hi - mid
        info = jnp.zeros((INFO, LANES), F32)
        for i, part in enumerate((hi, mid, lo, first_doc, last_doc)):
            info = jnp.where(rows == i, part, info)
        return info.astype(BF16)

    mine = (y == 0).astype(F32)
    info_ref[...] = info_of(total * mine + upper * (1.0 - mine))
    send_ref[size : size + INFO, :] = info_of(total * (1.0 - mine) + upper * mine)


def block_state(y, log_decay_t, docs, key, value, tokens, heads, after):
    size = heads // 2 * HEAD_DIM
    return call(
        functools.partial(state_kernel, tokens, heads),
        "block_state",
        [log_decay_t, docs, key, value],
        (sds((size, LANES), BF16), sds((size + INFO, LANES), BF16), sds((INFO, LANES), BF16)),
        scratch=[
            pltpu.VMEM((tokens * heads, LANES), F32),
            pltpu.VMEM((tokens * heads, LANES), F32),
            pltpu.VMEM((heads * HEAD_DIM, LANES), F32),
            pltpu.VMEM((LANES, tokens), F32),
        ],
        estimate=cost(2 * heads * tokens * HEAD_DIM**2, 3 * tokens * heads * LANES * 2),
        scalars=[y],
        after=after,
    )


def row_terms(y_ref, own_info, other_info):
    even = y_ref[0] == 0
    own = own_info.astype(F32)
    other = other_info.astype(F32)
    a = jnp.where(even, own, other)
    b = jnp.where(even, other, own)
    decay_a = jnp.exp(a[0:1] + a[1:2] + a[2:3])
    decay_b = jnp.exp(b[0:1] + b[1:2] + b[2:3])
    first_a, last_a = a[3:4], a[4:5]
    first_b, last_b = b[3:4], b[4:5]
    whole_a = (first_a == last_a).astype(F32)
    link_b = ((last_a == first_b) & (first_b == last_b)).astype(F32)
    return even, decay_a, decay_b * link_b, first_a, whole_a, last_a, last_b


def chain_kernel(count, first, arrivals, y_ref, *refs):
    keep_ref, info_ref, other_ref, other_info_ref = refs[:4]
    came, out_ref = refs[4 : 4 + arrivals], refs[4 + arrivals]
    size = count * HEAD_DIM
    even, decay_a, gain_b, first_a, whole_a, _, last_b = row_terms(
        y_ref, info_ref[...], other_info_ref[...]
    )
    if arrivals:
        came_doc = came[0][size : size + 1, :].astype(F32)
        gain_a = decay_a * whole_a * (came_doc == first_a).astype(F32)
    for i in range(count):
        rows = slice(i * HEAD_DIM, (i + 1) * HEAD_DIM)
        lane = slice(first + i, first + i + 1)
        own = keep_ref[rows, :].astype(F32)
        other = other_ref[rows, :].astype(F32)
        total = jnp.where(even, own, other)
        if arrivals:
            total = total + gain_a[:, lane] * came[0][rows, :].astype(F32)
        out_ref[rows, :] = (gain_b[:, lane] * total + jnp.where(even, other, own)).astype(BF16)
    out_ref[size : size + INFO, :] = jnp.broadcast_to(last_b, (INFO, LANES)).astype(BF16)


def chain_step(y, keep, info, other, other_info, came, first, count, after):
    size = count * HEAD_DIM
    came = [] if came is None else [came]
    return call(
        functools.partial(chain_kernel, count, first, len(came)),
        "chain_step",
        [keep, info, other, other_info, *came],
        sds((size + INFO, LANES), BF16),
        estimate=cost(4 * size * LANES, 4 * size * LANES * 2),
        scalars=[y],
        after=after,
    )


def prior_kernel(count, first, arrivals, y_ref, *refs):
    keep_ref, info_ref, other_ref, other_info_ref = refs[:4]
    came = refs[4 : 4 + arrivals]
    mine_ref, send_ref, doc_ref = refs[4 + arrivals :]
    size = count * HEAD_DIM
    even, decay_a, _, first_a, whole_a, last_a, _ = row_terms(
        y_ref, info_ref[...], other_info_ref[...]
    )
    came_doc = jnp.zeros((1, LANES), F32)
    for ref in came:
        came_doc = came_doc + ref[size : size + 1, :].astype(F32)
    gain_a = decay_a * whole_a * (came_doc == first_a).astype(F32)
    for i in range(count):
        rows = slice(i * HEAD_DIM, (i + 1) * HEAD_DIM)
        lane = slice(first + i, first + i + 1)
        before_a = jnp.zeros((HEAD_DIM, LANES), F32)
        for ref in came:
            before_a = before_a + ref[rows, :].astype(F32)
        state_a = jnp.where(even, keep_ref[rows, :].astype(F32), other_ref[rows, :].astype(F32))
        before_b = gain_a[:, lane] * before_a + state_a
        mine_ref[rows, :] = jnp.where(even, before_a, before_b).astype(BF16)
        send_ref[rows, :] = jnp.where(even, before_b, before_a).astype(BF16)
    doc_ref[...] = jnp.broadcast_to(jnp.where(even, came_doc, last_a), (8, LANES))


def prior_states(y, keep, info, other, other_info, came, first, count, after):
    size = count * HEAD_DIM
    return call(
        functools.partial(prior_kernel, count, first, len(came)),
        "prior_states",
        [keep, info, other, other_info, *came],
        (sds((size, LANES), BF16), sds((size, LANES), BF16), sds((8, LANES), F32)),
        estimate=cost(4 * size * LANES, 6 * size * LANES * 2),
        scalars=[y],
        after=after,
    )


def some_heads(ref, tokens, heads, first, count):
    x = ref[...].astype(F32)
    if count == heads:
        return x
    return x.reshape(tokens, heads, LANES)[:, first : first + count, :].reshape(tokens * count, LANES)


def inner_kernel(tokens, heads, first, count, ld_ref, doc_ref, query_ref, key_ref, value_ref, inner_ref, qh_ref, grow_ref, qf, kf, vf, ldp, mask):
    cumul = cumulative(ld_ref, ldp, tokens, heads)
    grow_ref[...] = jnp.exp(cumul)
    cumul_t = lax.dot_general(
        ld_ref[...],
        lower_triangle(tokens).astype(F32),
        (((1,), (1,)), ((), ())),
        precision=HIGHEST,
        preferred_element_type=F32,
    )
    docs = doc_numbers(doc_ref)
    column = doc_columns(docs, tokens)
    same = jnp.concatenate([column] * (tokens // LANES), axis=1) == doc_line(docs, tokens)
    mask[...] = jnp.where(lower_triangle(tokens) & same, 0.0, -1e9)
    qf[...] = some_heads(query_ref, tokens, heads, first, count)
    kf[...] = some_heads(key_ref, tokens, heads, first, count)
    vf[...] = some_heads(value_ref, tokens, heads, first, count)
    for n in range(count):
        h = first + n
        picked = pl.ds(n, tokens, stride=count)
        query = qf[picked, :].astype(BF16)
        keys = kf[picked, :].astype(BF16)
        values = vf[picked, :].astype(BF16)
        qh_ref[n * tokens : (n + 1) * tokens, :] = query
        for i in range(tokens // LANES):
            seen = (i + 1) * LANES
            rows = slice(i * LANES, seen)
            scores = lax.dot_general(
                query[rows, :], keys[0:seen, :], (((1,), (1,)), ((), ())), preferred_element_type=F32
            )
            gap = cumul[rows, h : h + 1] - cumul_t[h : h + 1, 0:seen]
            weights = (scores * jnp.exp(gap + mask[rows, 0:seen])).astype(BF16)
            inner_ref[n * tokens + i * LANES : n * tokens + seen, :] = jnp.dot(
                weights, values[0:seen, :], preferred_element_type=F32
            )


def inner_part(log_decay_t, docs, query, key, value, tokens, heads, first, count, after):
    return call(
        functools.partial(inner_kernel, tokens, heads, first, count),
        "inner_part",
        [log_decay_t, docs, query, key, value],
        (
            sds((count * tokens, LANES), F32),
            sds((count * tokens, LANES), BF16),
            sds((tokens, LANES), F32),
        ),
        scratch=[pltpu.VMEM((tokens * count, LANES), F32)] * 3
        + [pltpu.VMEM((LANES, tokens), F32), pltpu.VMEM((tokens, tokens), F32)],
        mib=24,
        estimate=cost(
            4 * count * tokens * tokens * HEAD_DIM, tokens * heads * LANES * 12, count * tokens * tokens
        ),
        after=after,
    )


def mix_kernel(tokens, heads, parts, pieces, y_ref, doc_ref, prior_doc_ref, grow_ref, *refs):
    refs = list(refs)
    take = lambda n: [refs.pop(0) for _ in range(n)]
    inner, qh, mine, other = take(parts), take(parts), take(pieces), take(pieces)
    mixed_ref, square_ref = refs
    half = heads // 2
    count = half // pieces
    even = y_ref[0] == 0
    is_open = (doc_columns(doc_numbers(doc_ref), tokens) == prior_doc_ref[0:1, :]).astype(F32)
    gain = grow_ref[...] * is_open
    squares = jnp.zeros((tokens, LANES), F32)
    for h in range(heads):
        piece, i = divmod(h % half, count)
        rows = slice(i * HEAD_DIM, (i + 1) * HEAD_DIM)
        near, far = mine[piece][rows, :], other[piece][rows, :]
        lower = h < half
        state = jnp.where(even, near if lower else far, far if lower else near)
        part, n = divmod(h, heads // parts)
        held = slice(n * tokens, (n + 1) * tokens)
        carried = jnp.dot(qh[part][held, :], state, preferred_element_type=F32)
        mixed = inner[part][held, :] + carried * gain[:, h : h + 1]
        squares = squares + mixed * mixed
        mixed_ref[pl.ds(h, tokens, stride=heads), :] = mixed
    square_ref[...] = lax.dot_general(
        jnp.ones((8, LANES), F32),
        squares,
        (((1,), (1,)), ((), ())),
        precision=HIGHEST,
        preferred_element_type=F32,
    )


def mix(y, docs, prior_doc, grow, inner, qh, mine, other, tokens, heads, after):
    return call(
        functools.partial(mix_kernel, tokens, heads, len(inner), len(mine)),
        "mix",
        [docs, prior_doc, grow, *inner, *qh, *mine, *other],
        (sds((tokens * heads, LANES), F32), sds((8, tokens), F32)),
        mib=24,
        estimate=cost(2 * heads * tokens * HEAD_DIM**2, tokens * heads * LANES * 10),
        scalars=[y],
        after=after,
    )


def finish_kernel(tokens, heads, sums, gain_ref, gate_ref, mixed_ref, *refs):
    squares, out_ref = refs[:sums], refs[sums]
    total = squares[0][0:1, :]
    for ref in squares[1:]:
        total = total + ref[0:1, :]
    scale = lax.rsqrt(total / (HEADS * HEAD_DIM) + 1e-06)
    rows = jnp.concatenate([scale[:, i * LANES : (i + 1) * LANES] for i in range(tokens // LANES)], axis=0)
    column = doc_columns(rows, tokens)
    step = 32
    for i in range(0, tokens, step):
        at = slice(i * heads, (i + step) * heads)
        gate = jax.nn.sigmoid(gate_ref[at, :].astype(F32)).reshape(step, heads, LANES)
        mixed = mixed_ref[at, :].reshape(step, heads, LANES)
        inv = column[i : i + step, :][:, None, :]
        out = mixed * inv * gain_ref[...][None] * gate
        out_ref[at, :] = out.reshape(step * heads, LANES).astype(BF16)


def finish(gain, gate, mixed, squares, tokens, heads, after):
    return call(
        functools.partial(finish_kernel, tokens, heads, len(squares)),
        "finish",
        [gain, gate, mixed, *squares],
        sds((tokens * heads, LANES), BF16),
        estimate=cost(0, tokens * heads * LANES * 8, tokens * heads * LANES),
        after=after,
    )


def attend_kernel(tokens, heads, kv_here, blocks, is_first, is_last, *refs):
    refs = list(refs)
    take = lambda n: [refs.pop(0) for _ in range(n)]
    per_group = heads // kv_here
    rows = tokens * per_group
    step = CHUNK // per_group
    if is_first:
        doc_ref, query_ref = take(2)
    else:
        wide_ref, state_ref = take(2)
    kv = take(blocks)
    if is_first:
        wide_ref, out_ref, bias, doc_rep = refs
    else:
        out_ref, bias = refs

    lane = lax.broadcasted_iota(jnp.int32, (tokens, LANES), 1).astype(F32)
    end = 2 * kv_here * tokens
    for j, ref in enumerate(kv):
        docs = doc_columns(ref[end : end + INFO, :].astype(F32), tokens)
        bias[j] = jnp.where(docs == lane, 0.0, -BIG).astype(BF16)
    if is_first:
        column = doc_columns(doc_numbers(doc_ref), tokens)
        for h in range(per_group):
            doc_rep[pl.ds(h, tokens, stride=per_group), :] = (column == lane).astype(F32)
    ones = jnp.ones((STATE_ROWS - HEAD_DIM, tokens), BF16)

    def one(i, carry):
        at = pl.ds(pl.multiple_of(i * CHUNK, CHUNK), CHUNK)
        results = []
        if is_first:
            picked = pl.ds(pl.multiple_of(i * (step * heads), step * heads), step * heads)
            query_all = query_ref[picked, :].astype(F32).reshape(step, heads, LANES)
            one_hot = doc_rep[at, :].astype(BF16)
        for g in range(kv_here):
            if is_first:
                query = query_all[:, g * per_group : (g + 1) * per_group, :].reshape(CHUNK, LANES)
                wide = jnp.concatenate([query.astype(BF16), one_hot], axis=1)
                wide_ref[g, at, :] = wide
            else:
                wide = wide_ref[g, at, :]
            scores = []
            for j, ref in enumerate(kv):
                keys = jnp.concatenate([ref[g * tokens : (g + 1) * tokens, :], bias[j]], axis=1)
                scores.append(
                    lax.dot_general(keys, wide, (((1,), (1,)), ((), ())), preferred_element_type=F32)
                )
            if is_first:
                token = i * step + lax.broadcasted_iota(jnp.int32, (tokens, CHUNK), 1) // per_group
                key_at = lax.broadcasted_iota(jnp.int32, (tokens, CHUNK), 0)
                scores[0] = jnp.where(key_at <= token, scores[0], -BIG)
            top = jnp.max(scores[0], axis=0, keepdims=True)
            for score in scores[1:]:
                top = jnp.maximum(top, jnp.max(score, axis=0, keepdims=True))
            if not is_first:
                before = state_ref[g, :, at]
                top_before = before[STATE_ROWS - 1 : STATE_ROWS, :]
                top = jnp.maximum(top, top_before)
                total = before * jnp.exp2((top_before - top) * SCORE_TO_EXP2)
            else:
                total = None
            for ref, score in zip(kv, scores):
                weights = jnp.exp2((score - top) * SCORE_TO_EXP2).astype(BF16)
                begin = (kv_here + g) * tokens
                parts = [ref[begin + p : begin + p + LANES, :] for p in range(0, tokens, LANES)]
                values = jnp.concatenate([jnp.concatenate(parts, axis=1), ones], axis=0)
                more = jnp.dot(values, weights, preferred_element_type=F32)
                total = more if total is None else total + more
            if is_last:
                results.append(jnp.transpose(total[0:HEAD_DIM] / total[HEAD_DIM : HEAD_DIM + 1]))
            else:
                out_ref[g, 0 : STATE_ROWS - 8, at] = total[0 : STATE_ROWS - 8]
                out_ref[g, STATE_ROWS - 8 : STATE_ROWS, at] = jnp.broadcast_to(top, (8, CHUNK))
        if is_last:
            if kv_here > 1:
                results = [r.reshape(step, per_group, LANES) for r in results]
                results = [jnp.concatenate(results, axis=1).reshape(step * heads, LANES)]
            picked = pl.ds(pl.multiple_of(i * (step * heads), step * heads), step * heads)
            out_ref[picked, :] = results[0].astype(BF16)
        return carry

    lax.fori_loop(0, rows // CHUNK, one, 0)


def attend(first, state, kv, is_last, tokens, heads, kv_here, after):
    is_first = state is None
    blocks = len(kv)
    rows = tokens * heads // kv_here
    wide_shape = sds((kv_here, rows, 2 * LANES), BF16)
    state_shape = sds((kv_here, STATE_ROWS, rows), F32)
    out_shape = sds((tokens * heads, LANES), BF16) if is_last else state_shape
    scratch = [pltpu.VMEM((blocks, tokens, LANES), BF16)]
    if is_first:
        out_shape = (wide_shape, out_shape)
        scratch.append(pltpu.VMEM((rows, LANES), F32))
    span = blocks * tokens
    return call(
        functools.partial(attend_kernel, tokens, heads, kv_here, blocks, is_first, is_last),
        "attend",
        [*first, *([] if is_first else [state]), *kv],
        out_shape,
        scratch=scratch,
        mib=24,
        estimate=cost(
            4 * tokens * heads * span * 2 * LANES, 4 * tokens * heads * LANES * 4, tokens * heads * span
        ),
        after=after,
    )


def body(
    blocks,
    lin_query,
    lin_key,
    lin_value,
    lin_gate,
    log_decay,
    norm_gain,
    doc_ids,
    soft_query,
    soft_key,
    soft_value,
):
    tokens, heads, _ = lin_query.shape
    tensor = HEADS // heads
    kv_here = max(1, heads // GROUP)
    half = heads // 2
    pieces = 2 if half % 2 == 0 else 1
    parts = 2 if half % 8 == 0 else 1
    count = half // pieces
    longest = blocks * tokens * 5 // 8
    window = min(blocks - 1, (longest - 1 + tokens - 1) // tokens)
    flat = lambda x: x.reshape(-1, LANES)
    block = lax.axis_index("seq")
    y = (block % 2).astype(jnp.int32).reshape(1)
    start = (lax.axis_index("tp") * heads // GROUP).astype(jnp.int32).reshape(1)
    docs = doc_ids.reshape(tokens // LANES, LANES)
    decays = jnp.transpose(log_decay)

    def send(x, pairs):
        return lax.ppermute(x, "seq", [p for p in pairs if 0 <= p[0] < blocks and 0 <= p[1] < blocks])

    everyone = range(blocks)
    swap = [(b, b ^ 1) for b in everyone]

    own_kv = pack_kv(start, flat(soft_key), flat(soft_value), docs, tokens, kv_here)
    far_step = window if window % 2 else blocks
    beside = send(own_kv, [(b, b + (far_step if b % 2 else 1)) for b in everyone])
    lane_kv, cross_kv = [], []
    ahead = own_kv
    for back in range(1, window // 2 + 1):
        ahead = send(ahead, [(b, b + 2) for b in everyone if b >= 2 * (back - 1)])
        lane_kv.append(ahead)
        cross_kv.append(send(ahead, [p for p in swap if p[0] >= 2 * back]))

    keep, other, info = block_state(
        y, decays, docs, flat(lin_key), flat(lin_value), tokens, heads, [own_kv]
    )
    size = count * HEAD_DIM
    other_info = None
    came = []
    for piece in range(pieces):
        sent = other[piece * size : (piece + 1) * size]
        if piece == 0:
            sent = jnp.concatenate([sent, other[half * HEAD_DIM :]], axis=0)
        got = send(sent, swap)
        if piece == 0:
            other_info = got[size:]
        came.append(got)
    held = [keep[p * size : (p + 1) * size] for p in range(pieces)]

    state = {}

    def first_attention(after):
        state["wide"], state["sum"] = attend(
            (docs, flat(soft_query)), None, [own_kv], False, tokens, heads, kv_here, after
        )
        return state["sum"]

    def more_attention(kv, is_last, after):
        state["sum"] = attend(
            (state["wide"],), state["sum"], kv, is_last, tokens, heads, kv_here, after
        )
        return state["sum"]

    inner, qh = [], []

    def inner_of(part, after):
        n = heads // parts
        got = inner_part(
            decays, docs, flat(lin_query), flat(lin_key), flat(lin_value), tokens, heads, part * n, n, after
        )
        inner.append(got[0])
        qh.append(got[1])
        state["grow"] = got[2]
        return got[0]

    beside_work = [first_attention]
    beside_work += [functools.partial(inner_of, part) for part in range(parts)]
    beside_work.append(functools.partial(more_attention, [beside] + lane_kv[:1], False))

    latest = [None] * pieces
    arrived = [[] for _ in range(pieces)]
    done = info
    for row in range(blocks // 2 - 1):
        if beside_work:
            done = beside_work.pop(0)([done])
        for p in range(pieces):
            done = chain_step(
                y, held[p], info, came[p], other_info, latest[p], p * count, count, [done]
            )
            latest[p] = send(done, [(2 * row, 2 * row + 2), (2 * row + 1, 2 * row + 3)])
            arrived[p].append(latest[p])
    while beside_work:
        done = beside_work.pop(0)([done])
    mine, far = [], []
    prior_doc = None
    for p in range(pieces):
        done, sent, prior_doc = prior_states(
            y, held[p], info, came[p], other_info, arrived[p], p * count, count, [done]
        )
        mine.append(done)
        far.append(send(sent, swap))
    rest = [kv for pair in zip(cross_kv, lane_kv[1:] + [None]) for kv in pair if kv is not None]
    done = more_attention(rest[:1], False, [done])
    rest = rest[1:]
    mixed, squares = mix(
        y, docs, prior_doc, state["grow"], inner, qh, mine, far, tokens, heads, [done]
    )
    sums = [squares]
    for shift in range(1, tensor):
        sums.append(
            lax.ppermute(squares, "tp", [(t, (t + shift) % tensor) for t in range(tensor)])
        )
    after = [squares]
    while rest:
        soft_out = more_attention(rest[:2], len(rest) <= 2, after)
        rest, after = rest[2:], []
    lin_out = finish(norm_gain, flat(lin_gate), mixed, sums, tokens, heads, [soft_out])
    shape = (tokens, heads, HEAD_DIM)
    return lin_out.reshape(shape), soft_out.reshape(shape)


def solution(mesh):
    in_specs = (
        P("seq", "tp", None),
        P("seq", "tp", None),
        P("seq", "tp", None),
        P("seq", "tp", None),
        P("seq", "tp"),
        P("tp", None),
        P("seq"),
        P("seq", "tp", None),
        P("seq", None, None),
        P("seq", None, None),
    )
    out_specs = (P("seq", "tp", None), P("seq", "tp", None))
    return jax.shard_map(
        functools.partial(body, mesh.shape["seq"]),
        mesh=mesh,
        in_specs=in_specs,
        out_specs=out_specs,
        check_vma=False,
    )
```

time: 83.9 us -> 81.2 us (0.968)
  the two profiles are of different devices: /device:TPU:25 before, /device:TPU:16 now
where the time goes in v2:
time: 81.2 us; the launch traced here: 80.6 us
  Pallas kernels  38.9 us (48%)
  starting transfers between devices  32 us (39%)
  local copies, waits for them, and re-layouts  7.9 us (10%)
  between operations  1.11 us (1%)
    pallas_call x18, Pallas kernels, call(): pl.pallas_call(run, out_shape=out_shape, in_specs=[SMEM] * len(scalars) +...  38.9 us
    ppermute x15, starting transfers between devices, send(): lax.ppermute(x, 'seq', [p for p in pairs if 0 <= p[0] < blocks and 0 <= p...  29 us
    unnamed x32, local copies, waits for them, and re-layouts  7.85 us
    ppermute x3, starting transfers between devices, body(): lax.ppermute(squares, 'tp', [(t, (t + shift) % tensor) for t in range(ten...  2.98 us
  transfers between devices with their start and end apart: 18, of which 1 were waited for; matrix products, arithmetic and copies ran while one was open for 0% of the time, Pallas kernels for 46%

profile of v2, /device:TPU:16, one launch (start us, length us, event | category | flops | bytes accessed | tf_op | source)
XLA Modules:
  0.0 80.6 jit_solution(14119345368306964128)
XLA Ops:
  0.7 1.0 %copy-done.7 = bf16[256,8,128]{2,1,0:T(8,128)(2,1)S(1)} copy-done((bf16[256,8,128]{2,1,0:T(8,128)(2,1)S(1)}, bf16[256,8,128]{2,1,0:T(8,128)(2,1)}, u32[]{:S(2)}) %copy-start.7) | copy-done | bytes 524312
  1.7 1.0 %copy-done.8 = bf16[256,8,128]{2,1,0:T(8,128)(2,1)S(1)} copy-done((bf16[256,8,128]{2,1,0:T(8,128)(2,1)S(1)}, bf16[256,8,128]{2,1,0:T(8,128)(2,1)}, u32[]{:S(2)}) %copy-start.8) | copy-done | bytes 524312
  2.7 0.7 copy-done.11
  3.4 0.3 pack_kv.1.refs_5_.refs_2_
  3.7 3.5 %collective-permute-start.9 = (bf16[1040,128]{1,0:T(8,128)(2,1)S(1)}, bf16[1040,128]{1,0:T(8,128)(2,1)S(1)}, u32[]{:S(2)}, u32[]{:S(2)}) collective-permute-start(bf16[1040,128]{1,0:T(8,128)(2,1)S(1)} %pack_kv.1.refs_5_.refs_2_), channel_id=1, source_target_pairs={{0,8},{4,12},{8,16},{12,20},{16,24},{20,28},{1,9},{5,13},{9,17},{1... | collective-permute-start | bytes 798728 | tf_op jit(solution)/shard_map/ppermute | solution.py:551
  7.2 0.0 copy-start
  7.3 1.2 %copy-done = bf16[256,16,128]{2,1,0:T(8,128)(2,1)S(1)} copy-done((bf16[256,16,128]{2,1,0:T(8,128)(2,1)S(1)}, bf16[256,16,128]{2,1,0:T(8,128)(2,1)}, u32[]{:S(2)}) %copy-start) | copy-done | bytes 1048600
  8.5 1.2 %copy-done.2 = bf16[256,16,128]{2,1,0:T(8,128)(2,1)S(1)} copy-done((bf16[256,16,128]{2,1,0:T(8,128)(2,1)S(1)}, bf16[256,16,128]{2,1,0:T(8,128)(2,1)}, u32[]{:S(2)}) %copy-start.2) | copy-done | bytes 1048600
  9.7 0.7 copy-done.9
  10.4 0.7 copy-done.12
  11.1 3.0 %block_state.1 = (bf16[1024,128]{1,0:T(8,128)(2,1)S(1)}, bf16[1040,128]{1,0:T(8,128)(2,1)S(1)}, bf16[16,128]{1,0:T(8,128)(2,1)S(1)}) custom-call(s32[1]{0:T(128)} %bitcast.1.refs_0_, f32[16,256]{1,0:T(8,128)S(1)} %bitcast.25, s32[2,128]{1,0:T(2,128)S(1)} %bitcast.29, bf16[4096,128]{1,0:T(8,128)(2,1)S(1)} %bitcast.13, bf16[4096,128]{1,0:T(8,128)(2,1)S(1)} %bitcast.16, ...), custom_call_target="tpu_custom_call" | custom-call | flops 134217728 | bytes 3145728 | tf_op jit(solution)/shard_map/block_state/pallas_call | solution.py:48
  14.2 1.6 %collective-permute-start.1 = (bf16[528,128]{1,0:T(8,128)(2,1)S(1)}, bf16[528,128]{1,0:T(8,128)(2,1)S(1)}, u32[]{:S(2)}, u32[]{:S(2)}) collective-permute-start(bf16[528,128]{1,0:T(8,128)(2,1)S(1)} %pad_maximum_fusion), channel_id=1, source_target_pairs={{0,4},{4,0},{8,12},{12,8},{16,20},{20,16},{24,28},{28,24},{1,5},{5... | collective-permute-start | bytes 405512 | tf_op jit(solution)/shard_map/ppermute | solution.py:551
  15.8 0.5 collective-permute-start
  16.3 6.5 %attend.4 = (bf16[2,2048,256]{2,1,0:T(8,128)(2,1)S(1)}, f32[2,144,2048]{2,1,0:T(8,128)S(1)}) custom-call(s32[2,128]{1,0:T(2,128)S(1)} %bitcast.30, bf16[4096,128]{1,0:T(8,128)(2,1)S(1)} %bitcast.34, bf16[1040,128]{1,0:T(8,128)(2,1)S(1)} %pack_kv.1.refs_5_.refs_2_, bf16[16,128]{1,0:T(8,128)(2,1)S(1)} %get-tuple-element.20.refs_3_.refs_2_), custom_call_target="tpu_custom_call" | custom-call | flops 1073741824 | bytes 8388608 | tf_op jit(solution)/shard_map/attend/pallas_call | solution.py:48
  22.8 0.0 copy-start.1
  22.9 0.1 chain_step.6.refs_5_
  23.0 0.8 collective-permute-start.3
  23.9 0.1 chain_step.7.refs_5_
  24.0 0.7 collective-permute-start.2
  24.7 1.9 %collective-permute-start.16 = (bf16[1040,128]{1,0:T(8,128)(2,1)S(1)}, bf16[1040,128]{1,0:T(8,128)(2,1)S(1)}, u32[]{:S(2)}, u32[]{:S(2)}) collective-permute-start(bf16[1040,128]{1,0:T(8,128)(2,1)S(1)} %collective-permute-done.9.refs_3_), channel_id=1, source_target_pairs={{8,16},{12,20},{16,24},{20,28},{9,17},{13,21},{17,25},{21,29},{10,... | collective-permute-start | bytes 798728 | tf_op jit(solution)/shard_map/ppermute | solution.py:551
  26.6 3.4 %collective-permute-start.8 = (bf16[1040,128]{1,0:T(8,128)(2,1)S(1)}, bf16[1040,128]{1,0:T(8,128)(2,1)S(1)}, u32[]{:S(2)}, u32[]{:S(2)}) collective-permute-start(bf16[1040,128]{1,0:T(8,128)(2,1)S(1)} %pack_kv.1.refs_5_.refs_2_), channel_id=1, source_target_pairs={{0,4},{4,24},{8,12},{16,20},{24,28},{1,5},{5,25},{9,13},{17,21},{2... | collective-permute-start | bytes 798728 | tf_op jit(solution)/shard_map/ppermute | solution.py:551
  30.1 2.2 %inner_part.2 = (f32[2048,128]{1,0:T(8,128)S(1)}, bf16[2048,128]{1,0:T(8,128)(2,1)S(1)}, f32[256,128]{1,0:T(8,128)}) custom-call(f32[16,256]{1,0:T(8,128)S(1)} %bitcast.26, s32[2,128]{1,0:T(2,128)S(1)} %bitcast.31, bf16[4096,128]{1,0:T(8,128)(2,1)S(1)} %bitcast.19, bf16[4096,128]{1,0:T(8,128)(2,1)S(1)} %bitcast.14, bf16[4096,128]{1,0:T(8,128)(2,1)S(1)} %bitcast.17, ...), custom_call_target="tpu_custom_call" | custom-call | flops 268435456 | bytes 6291456 | tf_op jit(solution)/shard_map/inner_part/pallas_call | solution.py:48
  32.4 0.2 chain_step.8.refs_6_
  32.5 1.3 %collective-permute-start.5 = (bf16[528,128]{1,0:T(8,128)(2,1)S(1)}, bf16[528,128]{1,0:T(8,128)(2,1)S(1)}, u32[]{:S(2)}, u32[]{:S(2)}) collective-permute-start(bf16[528,128]{1,0:T(8,128)(2,1)S(1)} %chain_step.8.refs_6_), channel_id=1, source_target_pairs={{8,16},{12,20},{9,17},{13,21},{10,18},{14,22},{11,19},{15,23}} | collective-permute-start | bytes 405512 | tf_op jit(solution)/shard_map/ppermute | solution.py:551
  33.8 0.2 chain_step.9.refs_5_
  34.0 1.3 %collective-permute-start.4 = (bf16[528,128]{1,0:T(8,128)(2,1)S(1)}, bf16[528,128]{1,0:T(8,128)(2,1)S(1)}, u32[]{:S(2)}, u32[]{:S(2)}) collective-permute-start(bf16[528,128]{1,0:T(8,128)(2,1)S(1)} %chain_step.9.refs_5_), channel_id=1, source_target_pairs={{8,16},{12,20},{9,17},{13,21},{10,18},{14,22},{11,19},{15,23}} | collective-permute-start | bytes 405512 | tf_op jit(solution)/shard_map/ppermute | solution.py:551
  35.3 1.9 %collective-permute-start.12 = (bf16[1040,128]{1,0:T(8,128)(2,1)S(1)}, bf16[1040,128]{1,0:T(8,128)(2,1)S(1)}, u32[]{:S(2)}, u32[]{:S(2)}) collective-permute-start(bf16[1040,128]{1,0:T(8,128)(2,1)S(1)} %collective-permute-done.9.refs_3_), channel_id=1, source_target_pairs={{8,12},{12,8},{16,20},{20,16},{24,28},{28,24},{9,13},{13,9},{17,21... | collective-permute-start | bytes 798728 | tf_op jit(solution)/shard_map/ppermute | solution.py:551
  37.2 2.2 %inner_part.3 = (f32[2048,128]{1,0:T(8,128)S(1)}, bf16[2048,128]{1,0:T(8,128)(2,1)S(1)}, f32[256,128]{1,0:T(8,128)S(1)}) custom-call(f32[16,256]{1,0:T(8,128)S(1)} %bitcast.27, s32[2,128]{1,0:T(2,128)S(1)} %bitcast.32, bf16[4096,128]{1,0:T(8,128)(2,1)S(1)} %bitcast.20, bf16[4096,128]{1,0:T(8,128)(2,1)S(1)} %bitcast.15, bf16[4096,128]{1,0:T(8,128)(2,1)S(1)} %bitcast.18, ...), custom_call_target="tpu_custom_call" | custom-call | flops 268435456 | bytes 6291456 | tf_op jit(solution)/shard_map/inner_part/pallas_call | solution.py:48
  39.5 0.7 collective-permute-done.5.refs_5_.refs_6_
  40.1 0.2 chain_step.10.refs_6_
  40.3 1.3 %collective-permute-start.7 = (bf16[528,128]{1,0:T(8,128)(2,1)S(1)}, bf16[528,128]{1,0:T(8,128)(2,1)S(1)}, u32[]{:S(2)}, u32[]{:S(2)}) collective-permute-start(bf16[528,128]{1,0:T(8,128)(2,1)S(1)} %chain_step.10.refs_6_), channel_id=1, source_target_pairs={{16,24},{20,28},{17,25},{21,29},{18,26},{22,30},{19,27},{23,31}} | collective-permute-start | bytes 405512 | tf_op jit(solution)/shard_map/ppermute | solution.py:551
  41.6 0.2 chain_step.11.refs_4_
  41.8 1.3 %collective-permute-start.6 = (bf16[528,128]{1,0:T(8,128)(2,1)S(1)}, bf16[528,128]{1,0:T(8,128)(2,1)S(1)}, u32[]{:S(2)}, u32[]{:S(2)}) collective-permute-start(bf16[528,128]{1,0:T(8,128)(2,1)S(1)} %chain_step.11.refs_4_), channel_id=1, source_target_pairs={{16,24},{20,28},{17,25},{21,29},{18,26},{22,30},{19,27},{23,31}} | collective-permute-start | bytes 405512 | tf_op jit(solution)/shard_map/ppermute | solution.py:551
  43.1 7.4 %collective-permute-start.17 = (bf16[1040,128]{1,0:T(8,128)(2,1)S(1)}, bf16[1040,128]{1,0:T(8,128)(2,1)S(1)}, u32[]{:S(2)}, u32[]{:S(2)}) collective-permute-start(bf16[1040,128]{1,0:T(8,128)(2,1)S(1)} %collective-permute-done.16.refs_2_), channel_id=1, source_target_pairs={{16,20},{20,16},{24,28},{28,24},{17,21},{21,17},{25,29},{29,25},{1... | collective-permute-start | bytes 798728 | tf_op jit(solution)/shard_map/ppermute | solution.py:551
  50.6 5.7 %attend.5.refs_8_.refs_1_ = f32[2,144,2048]{2,1,0:T(8,128)S(1)} custom-call(bf16[2,2048,256]{2,1,0:T(8,128)(2,1)S(1)} %get-tuple-element.25.refs_0_, f32[2,144,2048]{2,1,0:T(8,128)S(1)} %get-tuple-element.22.refs_5_.refs_1_, bf16[1040,128]{1,0:T(8,128)(2,1)S(1)} %collective-permute-done.8.refs_2_, bf16[1040,128]{1,0:T(8,128)(2,1)S(1)} %collective-permute-done.9.refs_3_, ...), custom_call_target="tpu_custom_call" | custom-call | flops 2147483648 | bytes 8388608 | tf_op jit(solution)/shard_map/attend/pallas_call | solution.py:48
  56.3 0.7 prior_states.2
  57.0 0.2 prior_states.3
  57.2 0.1 collective-permute-start.11
  57.3 2.0 %collective-permute-start.10 = (bf16[512,128]{1,0:T(8,128)(2,1)S(1)}, bf16[512,128]{1,0:T(8,128)(2,1)S(1)}, u32[]{:S(2)}, u32[]{:S(2)}) collective-permute-start(bf16[512,128]{1,0:T(8,128)(2,1)S(1)} %get-tuple-element.32), channel_id=1, source_target_pairs={{0,4},{4,0},{8,12},{12,8},{16,20},{20,16},{24,28},{28,24},{1,5},{5... | collective-permute-start | bytes 393224 | tf_op jit(solution)/shard_map/ppermute | solution.py:551
  59.3 6.4 %attend.6.refs_12_.refs_1_ = f32[2,144,2048]{2,1,0:T(8,128)S(1)} custom-call(bf16[2,2048,256]{2,1,0:T(8,128)(2,1)S(1)} %get-tuple-element.25.refs_0_, f32[2,144,2048]{2,1,0:T(8,128)S(1)} %attend.5.refs_8_.refs_1_, bf16[1040,128]{1,0:T(8,128)(2,1)S(1)} %collective-permute-done.12.refs_2_, bf16[512,128]{1,0:T(8,128)(2,1)S(1)} %get-tuple-element.31.refs_3_.refs_9_), custom_call_target="tpu_custom_call" | custom-call | flops 1073741824 | bytes 8388608 | tf_op jit(solution)/shard_map/attend/pallas_call | solution.py:48
  65.7 1.6 %mix.1 = (f32[4096,128]{1,0:T(8,128)S(1)}, f32[8,256]{1,0:T(8,128)S(1)}) custom-call(s32[1]{0:T(128)} %bitcast.1.refs_0_, s32[2,128]{1,0:T(2,128)S(1)} %bitcast.33, f32[8,128]{1,0:T(8,128)S(1)} %get-tuple-element.27.refs_2_, f32[256,128]{1,0:T(8,128)S(1)} %get-tuple-element.28.refs_3_, f32[2048,128]{1,0:T(8,128)S(1)} %get-tuple-element.23.refs_6_.refs_4_, ...), custom_call_target="tpu_custom_call" | custom-call | flops 134217728 | bytes 5242880 | tf_op jit(solution)/shard_map/mix/pallas_call | solution.py:48
  67.3 0.0 collective-permute-start.13
  67.3 1.6 %collective-permute-start.14 = (f32[8,256]{1,0:T(8,128)S(1)}, f32[8,256]{1,0:T(8,128)S(1)}, u32[]{:S(2)}, u32[]{:S(2)}) collective-permute-start(f32[8,256]{1,0:T(8,128)S(1)} %get-tuple-element.35.refs_4_.refs_3_), channel_id=1, source_target_pairs={{0,2},{1,3},{2,0},{3,1},{4,6},{5,7},{6,4},{7,5},{8,10},{9,11},{10,... | collective-permute-start | bytes 24584 | tf_op jit(solution)/shard_map/ppermute | solution.py:643
  68.8 1.4 %collective-permute-start.15 = (f32[8,256]{1,0:T(8,128)S(1)}, f32[8,256]{1,0:T(8,128)S(1)}, u32[]{:S(2)}, u32[]{:S(2)}) collective-permute-start(f32[8,256]{1,0:T(8,128)S(1)} %get-tuple-element.35.refs_4_.refs_3_), channel_id=1, source_target_pairs={{0,3},{1,0},{2,1},{3,2},{4,7},{5,4},{6,5},{7,6},{8,11},{9,8},{10,9... | collective-permute-start | bytes 24584 | tf_op jit(solution)/shard_map/ppermute | solution.py:643
  70.2 7.4 %attend.7.refs_7_ = bf16[4096,128]{1,0:T(8,128)(2,1)} custom-call(bf16[2,2048,256]{2,1,0:T(8,128)(2,1)S(1)} %get-tuple-element.25.refs_0_, f32[2,144,2048]{2,1,0:T(8,128)S(1)} %attend.6.refs_12_.refs_1_, bf16[1040,128]{1,0:T(8,128)(2,1)S(1)} %collective-permute-done.16.refs_2_, bf16[1040,128]{1,0:T(8,128)(2,1)S(1)} %collective-permute-done.17.refs_3_, ...), custom_call_target="tpu_custom_call" | custom-call | flops 2147483648 | bytes 8388608 | tf_op jit(solution)/shard_map/attend/pallas_call | solution.py:48
  77.7 0.0 copy-start.6
  77.7 1.2 %copy-done.6 = bf16[4096,128]{1,0:T(8,128)(2,1)S(1)} copy-done((bf16[4096,128]{1,0:T(8,128)(2,1)S(1)}, bf16[4096,128]{1,0:T(8,128)(2,1)}, u32[]{:S(2)}) %copy-start.6) | copy-done | bytes 1048600
  78.9 1.7 %finish.1 = bf16[4096,128]{1,0:T(8,128)(2,1)} custom-call(f32[16,128]{1,0:T(8,128)S(1)} %copy-done.14, bf16[4096,128]{1,0:T(8,128)(2,1)S(1)} %bitcast.21, f32[4096,128]{1,0:T(8,128)S(1)} %get-tuple-element.34.refs_2_, f32[8,256]{1,0:T(8,128)S(1)} %get-tuple-element.35.refs_4_.refs_3_, f32[8,256]{1,0:T(8,128)S(1)} %collective-permute-done.13.refs_4_, ...), custom_call_target="tpu_custom_call" | custom-call | bytes 4194304 | tf_op jit(solution)/shard_map/finish/pallas_call | solution.py:48
  (43 shorter events, 0.1 us)
Async XLA Ops:
  0.6 1.0 %copy-start.7 = (bf16[256,8,128]{2,1,0:T(8,128)(2,1)S(1)}, bf16[256,8,128]{2,1,0:T(8,128)(2,1)}, u32[]{:S(2)}) copy-start(bf16[256,8,128]{2,1,0:T(8,128)(2,1)} %param.18) | copy-start | bytes 1572868
  1.7 1.0 %copy-start.8 = (bf16[256,8,128]{2,1,0:T(8,128)(2,1)S(1)}, bf16[256,8,128]{2,1,0:T(8,128)(2,1)}, u32[]{:S(2)}) copy-start(bf16[256,8,128]{2,1,0:T(8,128)(2,1)} %param.19) | copy-start | bytes 1572868
  2.7 0.7 copy-start.11
  3.4 12.9 %copy-start.13 = (s32[256]{0:T(256)S(1)}, s32[256]{0:T(256)}, u32[]{:S(2)}) copy-start(s32[256]{0:T(256)} %param.16) | copy-start | bytes 3076
  3.4 12.9 %copy-start.15 = (bf16[256,16,128]{2,1,0:T(8,128)(2,1)S(1)}, bf16[256,16,128]{2,1,0:T(8,128)(2,1)}, u32[]{:S(2)}) copy-start(bf16[256,16,128]{2,1,0:T(8,128)(2,1)} %param.17) | copy-start | bytes 3145732
  3.7 21.0 %collective-permute-start.9 = (bf16[1040,128]{1,0:T(8,128)(2,1)S(1)}, bf16[1040,128]{1,0:T(8,128)(2,1)S(1)}, u32[]{:S(2)}, u32[]{:S(2)}) collective-permute-start(bf16[1040,128]{1,0:T(8,128)(2,1)S(1)} %pack_kv.1.refs_5_.refs_2_), channel_id=1, source_target_pairs={{0,8},{4,12},{8,16},{12,20},{16,24},{20,28},{1,9},{5,13},{9,17},{1... | collective-permute-start | bytes 798728 | tf_op jit(solution)/shard_map/ppermute | solution.py:551
  7.2 1.2 %copy-start = (bf16[256,16,128]{2,1,0:T(8,128)(2,1)S(1)}, bf16[256,16,128]{2,1,0:T(8,128)(2,1)}, u32[]{:S(2)}) copy-start(bf16[256,16,128]{2,1,0:T(8,128)(2,1)} %param.11) | copy-start | bytes 3145732
  8.5 1.2 %copy-start.2 = (bf16[256,16,128]{2,1,0:T(8,128)(2,1)S(1)}, bf16[256,16,128]{2,1,0:T(8,128)(2,1)}, u32[]{:S(2)}) copy-start(bf16[256,16,128]{2,1,0:T(8,128)(2,1)} %param.12) | copy-start | bytes 3145732
  9.7 0.7 copy-start.9
  10.4 0.7 copy-start.12
  14.2 8.7 %collective-permute-start.1 = (bf16[528,128]{1,0:T(8,128)(2,1)S(1)}, bf16[528,128]{1,0:T(8,128)(2,1)S(1)}, u32[]{:S(2)}, u32[]{:S(2)}) collective-permute-start(bf16[528,128]{1,0:T(8,128)(2,1)S(1)} %pad_maximum_fusion), channel_id=1, source_target_pairs={{0,4},{4,0},{8,12},{12,8},{16,20},{20,16},{24,28},{28,24},{1,5},{5... | collective-permute-start | bytes 405512 | tf_op jit(solution)/shard_map/ppermute | solution.py:551
  15.8 8.1 %collective-permute-start = (bf16[512,128]{1,0:T(8,128)(2,1)S(1)}, bf16[512,128]{1,0:T(8,128)(2,1)S(1)}, u32[]{:S(2)}, u32[]{:S(2)}) collective-permute-start(bf16[512,128]{1,0:T(8,128)(2,1)S(1)} %get-tuple-element.37), channel_id=1, source_target_pairs={{0,4},{4,0},{8,12},{12,8},{16,20},{20,16},{24,28},{28,24},{1,5},{5... | collective-permute-start | bytes 393224 | tf_op jit(solution)/shard_map/ppermute | solution.py:551
  22.8 7.3 %copy-start.1 = (bf16[256,16,128]{2,1,0:T(8,128)(2,1)S(1)}, bf16[256,16,128]{2,1,0:T(8,128)(2,1)}, u32[]{:S(2)}) copy-start(bf16[256,16,128]{2,1,0:T(8,128)(2,1)} %param.11) | copy-start | bytes 3145732
  22.8 7.3 %copy-start.3 = (bf16[256,16,128]{2,1,0:T(8,128)(2,1)S(1)}, bf16[256,16,128]{2,1,0:T(8,128)(2,1)}, u32[]{:S(2)}) copy-start(bf16[256,16,128]{2,1,0:T(8,128)(2,1)} %param.12) | copy-start | bytes 3145732
  22.9 7.3 %copy-start.4 = (bf16[256,16,128]{2,1,0:T(8,128)(2,1)S(1)}, bf16[256,16,128]{2,1,0:T(8,128)(2,1)}, u32[]{:S(2)}) copy-start(bf16[256,16,128]{2,1,0:T(8,128)(2,1)} %param.10) | copy-start | bytes 3145732
  22.9 7.3 %copy-start.10 = (f32[256,16]{0,1:T(8,128)S(1)}, f32[256,16]{0,1:T(8,128)}, u32[]{:S(2)}) copy-start(f32[256,16]{0,1:T(8,128)} %param.14) | copy-start | bytes 49156
  23.0 9.3 %collective-permute-start.3 = (bf16[528,128]{1,0:T(8,128)(2,1)S(1)}, bf16[528,128]{1,0:T(8,128)(2,1)S(1)}, u32[]{:S(2)}, u32[]{:S(2)}) collective-permute-start(bf16[528,128]{1,0:T(8,128)(2,1)S(1)} %chain_step.6.refs_5_), channel_id=1, source_target_pairs={{0,8},{4,12},{1,9},{5,13},{2,10},{6,14},{3,11},{7,15}} | collective-permute-start | bytes 405512 | tf_op jit(solution)/shard_map/ppermute | solution.py:551
  24.0 9.8 %collective-permute-start.2 = (bf16[528,128]{1,0:T(8,128)(2,1)S(1)}, bf16[528,128]{1,0:T(8,128)(2,1)S(1)}, u32[]{:S(2)}, u32[]{:S(2)}) collective-permute-start(bf16[528,128]{1,0:T(8,128)(2,1)S(1)} %chain_step.7.refs_5_), channel_id=1, source_target_pairs={{0,8},{4,12},{1,9},{5,13},{2,10},{6,14},{3,11},{7,15}} | collective-permute-start | bytes 405512 | tf_op jit(solution)/shard_map/ppermute | solution.py:551
  24.7 18.4 %collective-permute-start.16 = (bf16[1040,128]{1,0:T(8,128)(2,1)S(1)}, bf16[1040,128]{1,0:T(8,128)(2,1)S(1)}, u32[]{:S(2)}, u32[]{:S(2)}) collective-permute-start(bf16[1040,128]{1,0:T(8,128)(2,1)S(1)} %collective-permute-done.9.refs_3_), channel_id=1, source_target_pairs={{8,16},{12,20},{16,24},{20,28},{9,17},{13,21},{17,25},{21,29},{10,... | collective-permute-start | bytes 798728 | tf_op jit(solution)/shard_map/ppermute | solution.py:551
  26.6 23.9 %collective-permute-start.8 = (bf16[1040,128]{1,0:T(8,128)(2,1)S(1)}, bf16[1040,128]{1,0:T(8,128)(2,1)S(1)}, u32[]{:S(2)}, u32[]{:S(2)}) collective-permute-start(bf16[1040,128]{1,0:T(8,128)(2,1)S(1)} %pack_kv.1.refs_5_.refs_2_), channel_id=1, source_target_pairs={{0,4},{4,24},{8,12},{16,20},{24,28},{1,5},{5,25},{9,13},{17,21},{2... | collective-permute-start | bytes 798728 | tf_op jit(solution)/shard_map/ppermute | solution.py:551
  32.5 7.6 %collective-permute-start.5 = (bf16[528,128]{1,0:T(8,128)(2,1)S(1)}, bf16[528,128]{1,0:T(8,128)(2,1)S(1)}, u32[]{:S(2)}, u32[]{:S(2)}) collective-permute-start(bf16[528,128]{1,0:T(8,128)(2,1)S(1)} %chain_step.8.refs_6_), channel_id=1, source_target_pairs={{8,16},{12,20},{9,17},{13,21},{10,18},{14,22},{11,19},{15,23}} | collective-permute-start | bytes 405512 | tf_op jit(solution)/shard_map/ppermute | solution.py:551
  34.0 7.6 %collective-permute-start.4 = (bf16[528,128]{1,0:T(8,128)(2,1)S(1)}, bf16[528,128]{1,0:T(8,128)(2,1)S(1)}, u32[]{:S(2)}, u32[]{:S(2)}) collective-permute-start(bf16[528,128]{1,0:T(8,128)(2,1)S(1)} %chain_step.9.refs_5_), channel_id=1, source_target_pairs={{8,16},{12,20},{9,17},{13,21},{10,18},{14,22},{11,19},{15,23}} | collective-permute-start | bytes 405512 | tf_op jit(solution)/shard_map/ppermute | solution.py:551
  35.3 23.9 %collective-permute-start.12 = (bf16[1040,128]{1,0:T(8,128)(2,1)S(1)}, bf16[1040,128]{1,0:T(8,128)(2,1)S(1)}, u32[]{:S(2)}, u32[]{:S(2)}) collective-permute-start(bf16[1040,128]{1,0:T(8,128)(2,1)S(1)} %collective-permute-done.9.refs_3_), channel_id=1, source_target_pairs={{8,12},{12,8},{16,20},{20,16},{24,28},{28,24},{9,13},{13,9},{17,21... | collective-permute-start | bytes 798728 | tf_op jit(solution)/shard_map/ppermute | solution.py:551
  40.3 16.0 %collective-permute-start.7 = (bf16[528,128]{1,0:T(8,128)(2,1)S(1)}, bf16[528,128]{1,0:T(8,128)(2,1)S(1)}, u32[]{:S(2)}, u32[]{:S(2)}) collective-permute-start(bf16[528,128]{1,0:T(8,128)(2,1)S(1)} %chain_step.10.refs_6_), channel_id=1, source_target_pairs={{16,24},{20,28},{17,25},{21,29},{18,26},{22,30},{19,27},{23,31}} | collective-permute-start | bytes 405512 | tf_op jit(solution)/shard_map/ppermute | solution.py:551
  41.8 15.2 %collective-permute-start.6 = (bf16[528,128]{1,0:T(8,128)(2,1)S(1)}, bf16[528,128]{1,0:T(8,128)(2,1)S(1)}, u32[]{:S(2)}, u32[]{:S(2)}) collective-permute-start(bf16[528,128]{1,0:T(8,128)(2,1)S(1)} %chain_step.11.refs_4_), channel_id=1, source_target_pairs={{16,24},{20,28},{17,25},{21,29},{18,26},{22,30},{19,27},{23,31}} | collective-permute-start | bytes 405512 | tf_op jit(solution)/shard_map/ppermute | solution.py:551
  43.1 27.1 %collective-permute-start.17 = (bf16[1040,128]{1,0:T(8,128)(2,1)S(1)}, bf16[1040,128]{1,0:T(8,128)(2,1)S(1)}, u32[]{:S(2)}, u32[]{:S(2)}) collective-permute-start(bf16[1040,128]{1,0:T(8,128)(2,1)S(1)} %collective-permute-done.16.refs_2_), channel_id=1, source_target_pairs={{16,20},{20,16},{24,28},{28,24},{17,21},{21,17},{25,29},{29,25},{1... | collective-permute-start | bytes 798728 | tf_op jit(solution)/shard_map/ppermute | solution.py:551
  57.2 8.5 %collective-permute-start.11 = (bf16[512,128]{1,0:T(8,128)(2,1)S(1)}, bf16[512,128]{1,0:T(8,128)(2,1)S(1)}, u32[]{:S(2)}, u32[]{:S(2)}) collective-permute-start(bf16[512,128]{1,0:T(8,128)(2,1)S(1)} %get-tuple-element.33), channel_id=1, source_target_pairs={{0,4},{4,0},{8,12},{12,8},{16,20},{20,16},{24,28},{28,24},{1,5},{5... | collective-permute-start | bytes 393224 | tf_op jit(solution)/shard_map/ppermute | solution.py:551
  57.3 8.4 %collective-permute-start.10 = (bf16[512,128]{1,0:T(8,128)(2,1)S(1)}, bf16[512,128]{1,0:T(8,128)(2,1)S(1)}, u32[]{:S(2)}, u32[]{:S(2)}) collective-permute-start(bf16[512,128]{1,0:T(8,128)(2,1)S(1)} %get-tuple-element.32), channel_id=1, source_target_pairs={{0,4},{4,0},{8,12},{12,8},{16,20},{20,16},{24,28},{28,24},{1,5},{5... | collective-permute-start | bytes 393224 | tf_op jit(solution)/shard_map/ppermute | solution.py:551
  67.2 10.4 %copy-start.5 = (bf16[256,16,128]{2,1,0:T(8,128)(2,1)S(1)}, bf16[256,16,128]{2,1,0:T(8,128)(2,1)}, u32[]{:S(2)}) copy-start(bf16[256,16,128]{2,1,0:T(8,128)(2,1)} %param.13) | copy-start | bytes 3145732
  67.2 10.4 %copy-start.14 = (f32[16,128]{1,0:T(8,128)S(1)}, f32[16,128]{1,0:T(8,128)}, u32[]{:S(2)}) copy-start(f32[16,128]{1,0:T(8,128)} %refs_0_.1) | copy-start | bytes 24580
  67.3 10.4 %collective-permute-start.13 = (f32[8,256]{1,0:T(8,128)S(1)}, f32[8,256]{1,0:T(8,128)S(1)}, u32[]{:S(2)}, u32[]{:S(2)}) collective-permute-start(f32[8,256]{1,0:T(8,128)S(1)} %get-tuple-element.35.refs_4_.refs_3_), channel_id=1, source_target_pairs={{0,1},{1,2},{2,3},{3,0},{4,5},{5,6},{6,7},{7,4},{8,9},{9,10},{10,1... | collective-permute-start | bytes 24584 | tf_op jit(solution)/shard_map/ppermute | solution.py:643
  67.3 10.4 %collective-permute-start.14 = (f32[8,256]{1,0:T(8,128)S(1)}, f32[8,256]{1,0:T(8,128)S(1)}, u32[]{:S(2)}, u32[]{:S(2)}) collective-permute-start(f32[8,256]{1,0:T(8,128)S(1)} %get-tuple-element.35.refs_4_.refs_3_), channel_id=1, source_target_pairs={{0,2},{1,3},{2,0},{3,1},{4,6},{5,7},{6,4},{7,5},{8,10},{9,11},{10,... | collective-permute-start | bytes 24584 | tf_op jit(solution)/shard_map/ppermute | solution.py:643
  68.8 8.8 %collective-permute-start.15 = (f32[8,256]{1,0:T(8,128)S(1)}, f32[8,256]{1,0:T(8,128)S(1)}, u32[]{:S(2)}, u32[]{:S(2)}) collective-permute-start(f32[8,256]{1,0:T(8,128)S(1)} %get-tuple-element.35.refs_4_.refs_3_), channel_id=1, source_target_pairs={{0,3},{1,0},{2,1},{3,2},{4,7},{5,4},{6,5},{7,6},{8,11},{9,8},{10,9... | collective-permute-start | bytes 24584 | tf_op jit(solution)/shard_map/ppermute | solution.py:643
  77.7 1.2 %copy-start.6 = (bf16[4096,128]{1,0:T(8,128)(2,1)S(1)}, bf16[4096,128]{1,0:T(8,128)(2,1)}, u32[]{:S(2)}) copy-start(bf16[4096,128]{1,0:T(8,128)(2,1)} %attend.7.refs_7_) | copy-start | bytes 3145732

commit v3 on v2

v3 whole, which is shorter than its diff:
```python
import functools

import jax
import jax.numpy as jnp
import numpy as np
from jax import lax
from jax.experimental import pallas as pl
from jax.experimental.pallas import tpu as pltpu
from jax.sharding import PartitionSpec as P

HEADS = 64
HEAD_DIM = 128
KV_HEADS = 8
LANES = 128
GROUP = HEADS // KV_HEADS
F32 = jnp.float32
BF16 = jnp.bfloat16
BIG = float(2**20)
SCORE_TO_EXP2 = HEAD_DIM**-0.5 * float(np.log2(np.e))
INFO = 16
HIGHEST = lax.Precision.HIGHEST

VMEM = pl.BlockSpec(memory_space=pltpu.VMEM)
SMEM = pl.BlockSpec(memory_space=pltpu.SMEM)
HBM = pl.BlockSpec(memory_space=pltpu.HBM)
ANYWHERE = pl.BlockSpec(memory_space=pl.ANY)
STATE_ROWS = HEAD_DIM + 16
CHUNK = 256


def sds(shape, dtype):
    return jax.ShapeDtypeStruct(shape, dtype)


def cost(flops, bytes_accessed, transcendentals=0):
    return pl.CostEstimate(
        flops=int(flops), bytes_accessed=int(bytes_accessed), transcendentals=int(transcendentals)
    )


def call(kernel, name, operands, out_shape, scratch=(), mib=16, estimate=None, scalars=(), after=(), hbm=0, out_hbm=False):
    begin = len(scalars) + len(operands)
    skip = len(after)
    operands = [
        pltpu.with_memory_space_constraint(x, pltpu.HBM) if i < hbm else x for i, x in enumerate(operands)
    ]
    outs = out_shape if isinstance(out_shape, tuple) else (out_shape,)
    out_specs = (VMEM,) * len(outs)
    if out_hbm:
        outs = (pltpu.HBM(outs[0].shape, outs[0].dtype), *outs[1:])
        out_specs = (HBM, *out_specs[1:])

    def run(*refs):
        kernel(*refs[:begin], *refs[begin + skip :])

    out = pl.pallas_call(
        run,
        out_shape=outs,
        in_specs=[SMEM] * len(scalars) + [HBM] * hbm + [VMEM] * (len(operands) - hbm) + [ANYWHERE] * skip,
        out_specs=out_specs,
        scratch_shapes=list(scratch),
        compiler_params=pltpu.CompilerParams(vmem_limit_bytes=mib * 1024 * 1024),
        cost_estimate=estimate,
        name=name,
    )(*scalars, *operands, *after)
    return out if isinstance(out_shape, tuple) else out[0]


def doc_columns(doc_rows, tokens):
    parts = []
    for i in range(tokens // LANES):
        row = jnp.broadcast_to(doc_rows[i : i + 1, :], (LANES, LANES))
        parts.append(jnp.transpose(row))
    return jnp.concatenate(parts, axis=0)


def doc_line(doc_rows, tokens):
    return jnp.concatenate([doc_rows[i : i + 1, :] for i in range(tokens // LANES)], axis=1)


def lower_triangle(tokens):
    rows = lax.broadcasted_iota(jnp.int32, (tokens, tokens), 0)
    cols = lax.broadcasted_iota(jnp.int32, (tokens, tokens), 1)
    return rows >= cols


def front_kernel(tokens, heads, kv_here, pieces, start_ref, y_ref, *refs):
    refs = list(refs)
    take = lambda n: [refs.pop(0) for _ in range(n)]
    sources = take(6)
    kv_ref, doc_out, cumul_ref, info_ref = take(4)
    keep_refs, send_refs = take(pieces), take(pieces)
    held = take(6)
    sems, wide, kf, vf, states, ldp = refs
    docs_in, soft_key, soft_value, decays, lin_key, lin_value = held
    copies = [pltpu.make_async_copy(src, dst, sems.at[i]) for i, (src, dst) in enumerate(zip(sources, held))]
    for copy in copies:
        copy.start()

    copies[0].wait()
    docs = docs_in[...].astype(F32) + 1.0
    line = lax.broadcasted_iota(jnp.int32, (INFO, LANES), 0)
    info = jnp.zeros((INFO, LANES), F32)
    for i in range(tokens // LANES):
        info = jnp.where(line == i, docs[i : i + 1, :], info)
    doc_out[...] = info
    end = 2 * kv_here * tokens
    kv_ref[end : end + INFO, :] = info.astype(BF16)

    start = start_ref[0]
    for which, ref in enumerate((soft_key, soft_value)):
        copies[1 + which].wait()
        wide[...] = ref[...].astype(F32)
        for g in range(kv_here):
            rows = wide[pl.ds(start + g, tokens, stride=KV_HEADS), :]
            at = (which * kv_here + g) * tokens
            if which:
                halves = [jnp.transpose(rows[i : i + LANES, :]) for i in range(0, tokens, LANES)]
                rows = jnp.concatenate(halves, axis=0)
            kv_ref[at : at + tokens, :] = rows.astype(BF16)

    half = heads // 2
    y = y_ref[0]
    copies[3].wait()
    ldp[...] = jnp.zeros_like(ldp)
    ldp[0:heads, :] = decays[...]
    cumul = lax.dot_general(
        lower_triangle(tokens).astype(F32),
        ldp[...],
        (((1,), (1,)), ((), ())),
        precision=HIGHEST,
        preferred_element_type=F32,
    )
    cumul_ref[...] = cumul
    total = cumul[tokens - 1 : tokens, :]
    last_row = tokens // LANES - 1
    first_doc = docs[0:1, 0:1]
    last_doc = docs[last_row : last_row + 1, LANES - 1 : LANES]
    tail = (doc_columns(docs, tokens) == last_doc).astype(F32)
    scale = jnp.exp(total - cumul) * tail
    copies[4].wait()
    kf[...] = lin_key[...].astype(F32)
    copies[5].wait()
    vf[...] = lin_value[...].astype(F32)
    for h in range(heads):
        keys = (kf[pl.ds(h, tokens, stride=heads), :] * scale[:, h : h + 1]).astype(BF16)
        values = vf[pl.ds(h, tokens, stride=heads), :].astype(BF16)
        states[h * HEAD_DIM : (h + 1) * HEAD_DIM, :] = lax.dot_general(
            keys, values, (((0,), (0,)), ((), ())), preferred_element_type=F32
        )
    size = half // pieces * HEAD_DIM
    for p in range(pieces):
        keep_at = pl.multiple_of((y * pieces + p) * size, size)
        send_at = pl.multiple_of(((1 - y) * pieces + p) * size, size)
        keep_refs[p][...] = states[pl.ds(keep_at, size), :].astype(BF16)
        send_refs[p][0:size, :] = states[pl.ds(send_at, size), :].astype(BF16)
    upper = pltpu.roll(total, LANES - half, 1)

    def info_of(totals):
        hi = totals.astype(BF16).astype(F32)
        mid = (totals - hi).astype(BF16).astype(F32)
        lo = totals - hi - mid
        info = jnp.zeros((INFO, LANES), F32)
        for i, part in enumerate((hi, mid, lo, first_doc, last_doc)):
            info = jnp.where(line == i, part, info)
        return info.astype(BF16)

    mine = (y == 0).astype(F32)
    info_ref[...] = info_of(total * mine + upper * (1.0 - mine))
    send_refs[0][size : size + INFO, :] = info_of(total * (1.0 - mine) + upper * mine)


def front(start, y, operands, tokens, heads, kv_here, pieces):
    size = heads // 2 // pieces * HEAD_DIM
    keep = [sds((size, LANES), BF16)] * pieces
    send = [sds((size + (INFO if p == 0 else 0), LANES), BF16) for p in range(pieces)]
    out = call(
        functools.partial(front_kernel, tokens, heads, kv_here, pieces),
        "front",
        operands,
        (
            sds((2 * kv_here * tokens + INFO, LANES), BF16),
            sds((INFO, LANES), F32),
            sds((tokens, LANES), F32),
            sds((INFO, LANES), BF16),
            *keep,
            *send,
        ),
        scratch=[pltpu.VMEM(x.shape, x.dtype) for x in operands]
        + [
            pltpu.SemaphoreType.DMA((len(operands),)),
            pltpu.VMEM((tokens * KV_HEADS, LANES), F32),
            pltpu.VMEM((tokens * heads, LANES), F32),
            pltpu.VMEM((tokens * heads, LANES), F32),
            pltpu.VMEM((heads * HEAD_DIM, LANES), F32),
            pltpu.VMEM((LANES, tokens), F32),
        ],
        mib=24,
        estimate=cost(2 * heads * tokens * HEAD_DIM**2, 5 * tokens * heads * LANES * 2),
        scalars=[start, y],
        hbm=len(operands),
    )
    return (*out[:4], out[4 : 4 + pieces], out[4 + pieces :])


def row_terms(y_ref, own_info, other_info):
    even = y_ref[0] == 0
    own = own_info.astype(F32)
    other = other_info.astype(F32)
    a = jnp.where(even, own, other)
    b = jnp.where(even, other, own)
    decay_a = jnp.exp(a[0:1] + a[1:2] + a[2:3])
    decay_b = jnp.exp(b[0:1] + b[1:2] + b[2:3])
    first_a, last_a = a[3:4], a[4:5]
    first_b, last_b = b[3:4], b[4:5]
    whole_a = (first_a == last_a).astype(F32)
    link_b = ((last_a == first_b) & (first_b == last_b)).astype(F32)
    return even, decay_a, decay_b * link_b, first_a, whole_a, last_a, last_b


def chain_kernel(count, first, arrivals, y_ref, *refs):
    keep_ref, info_ref, other_ref, other_info_ref = refs[:4]
    came, out_ref = refs[4 : 4 + arrivals], refs[4 + arrivals]
    size = count * HEAD_DIM
    even, decay_a, gain_b, first_a, whole_a, _, last_b = row_terms(
        y_ref, info_ref[...], other_info_ref[size : size + INFO, :]
    )
    if arrivals:
        came_doc = came[0][size : size + 1, :].astype(F32)
        gain_a = decay_a * whole_a * (came_doc == first_a).astype(F32)
    for i in range(count):
        rows = slice(i * HEAD_DIM, (i + 1) * HEAD_DIM)
        lane = slice(first + i, first + i + 1)
        own = keep_ref[rows, :].astype(F32)
        other = other_ref[rows, :].astype(F32)
        total = jnp.where(even, own, other)
        if arrivals:
            total = total + gain_a[:, lane] * came[0][rows, :].astype(F32)
        out_ref[rows, :] = (gain_b[:, lane] * total + jnp.where(even, other, own)).astype(BF16)
    out_ref[size : size + INFO, :] = jnp.broadcast_to(last_b, (INFO, LANES)).astype(BF16)


def chain_step(y, keep, info, other, other_info, came, first, count, after):
    size = count * HEAD_DIM
    came = [] if came is None else [came]
    return call(
        functools.partial(chain_kernel, count, first, len(came)),
        "chain_step",
        [keep, info, other, other_info, *came],
        sds((size + INFO, LANES), BF16),
        estimate=cost(4 * size * LANES, 4 * size * LANES * 2),
        scalars=[y],
        after=after,
    )


def prior_kernel(count, first, arrivals, y_ref, *refs):
    keep_ref, info_ref, other_ref, other_info_ref = refs[:4]
    came = refs[4 : 4 + arrivals]
    mine_ref, send_ref, doc_ref = refs[4 + arrivals :]
    size = count * HEAD_DIM
    even, decay_a, _, first_a, whole_a, last_a, _ = row_terms(
        y_ref, info_ref[...], other_info_ref[size : size + INFO, :]
    )
    came_doc = jnp.zeros((1, LANES), F32)
    for ref in came:
        came_doc = came_doc + ref[size : size + 1, :].astype(F32)
    gain_a = decay_a * whole_a * (came_doc == first_a).astype(F32)
    for i in range(count):
        rows = slice(i * HEAD_DIM, (i + 1) * HEAD_DIM)
        lane = slice(first + i, first + i + 1)
        before_a = jnp.zeros((HEAD_DIM, LANES), F32)
        for ref in came:
            before_a = before_a + ref[rows, :].astype(F32)
        state_a = jnp.where(even, keep_ref[rows, :].astype(F32), other_ref[rows, :].astype(F32))
        before_b = gain_a[:, lane] * before_a + state_a
        mine_ref[rows, :] = jnp.where(even, before_a, before_b).astype(BF16)
        send_ref[rows, :] = jnp.where(even, before_b, before_a).astype(BF16)
    doc_ref[...] = jnp.broadcast_to(jnp.where(even, came_doc, last_a), (8, LANES))


def prior_states(y, keep, info, other, other_info, came, first, count, after):
    size = count * HEAD_DIM
    return call(
        functools.partial(prior_kernel, count, first, len(came)),
        "prior_states",
        [keep, info, other, other_info, *came],
        (sds((size, LANES), BF16), sds((size, LANES), BF16), sds((8, LANES), F32)),
        estimate=cost(4 * size * LANES, 6 * size * LANES * 2),
        scalars=[y],
        after=after,
    )


def some_heads(ref, tokens, heads, first, count):
    x = ref[...].astype(F32)
    if count == heads:
        return x
    return x.reshape(tokens, heads, LANES)[:, first : first + count, :].reshape(tokens * count, LANES)


def inner_kernel(tokens, heads, first, count, cumul_ref, doc_ref, query_ref, key_ref, value_ref, inner_ref, qh_ref, qf, kf, vf, mask):
    cumul = cumul_ref[...]
    cumul_t = jnp.transpose(cumul)
    docs = doc_ref[...]
    column = doc_columns(docs, tokens)
    same = jnp.concatenate([column] * (tokens // LANES), axis=1) == doc_line(docs, tokens)
    mask[...] = jnp.where(lower_triangle(tokens) & same, 0.0, -1e9)
    qf[...] = some_heads(query_ref, tokens, heads, first, count)
    kf[...] = some_heads(key_ref, tokens, heads, first, count)
    vf[...] = some_heads(value_ref, tokens, heads, first, count)
    for n in range(count):
        h = first + n
        picked = pl.ds(n, tokens, stride=count)
        query = qf[picked, :].astype(BF16)
        keys = kf[picked, :].astype(BF16)
        values = vf[picked, :].astype(BF16)
        qh_ref[n * tokens : (n + 1) * tokens, :] = query
        for i in range(tokens // LANES):
            seen = (i + 1) * LANES
            rows = slice(i * LANES, seen)
            scores = lax.dot_general(
                query[rows, :], keys[0:seen, :], (((1,), (1,)), ((), ())), preferred_element_type=F32
            )
            gap = cumul[rows, h : h + 1] - cumul_t[h : h + 1, 0:seen]
            weights = (scores * jnp.exp(gap + mask[rows, 0:seen])).astype(BF16)
            inner_ref[n * tokens + i * LANES : n * tokens + seen, :] = jnp.dot(
                weights, values[0:seen, :], preferred_element_type=F32
            )


def inner_part(cumul, docs, query, key, value, tokens, heads, first, count, after):
    return call(
        functools.partial(inner_kernel, tokens, heads, first, count),
        "inner_part",
        [cumul, docs, query, key, value],
        (sds((count * tokens, LANES), F32), sds((count * tokens, LANES), BF16)),
        scratch=[pltpu.VMEM((tokens * count, LANES), F32)] * 3 + [pltpu.VMEM((tokens, tokens), F32)],
        mib=24,
        estimate=cost(
            4 * count * tokens * tokens * HEAD_DIM, tokens * heads * LANES * 12, count * tokens * tokens
        ),
        after=after,
    )


def mix_kernel(tokens, heads, parts, pieces, y_ref, doc_ref, prior_doc_ref, cumul_ref, *refs):
    refs = list(refs)
    take = lambda n: [refs.pop(0) for _ in range(n)]
    inner, qh, mine, other = take(parts), take(parts), take(pieces), take(pieces)
    mixed_ref, square_ref = refs
    half = heads // 2
    count = half // pieces
    even = y_ref[0] == 0
    is_open = (doc_columns(doc_ref[...], tokens) == prior_doc_ref[0:1, :]).astype(F32)
    gain = jnp.exp(cumul_ref[...]) * is_open
    squares = jnp.zeros((tokens, LANES), F32)
    for h in range(heads):
        piece, i = divmod(h % half, count)
        rows = slice(i * HEAD_DIM, (i + 1) * HEAD_DIM)
        near, far = mine[piece][rows, :], other[piece][rows, :]
        lower = h < half
        state = jnp.where(even, near if lower else far, far if lower else near)
        part, n = divmod(h, heads // parts)
        held = slice(n * tokens, (n + 1) * tokens)
        carried = jnp.dot(qh[part][held, :], state, preferred_element_type=F32)
        mixed = inner[part][held, :] + carried * gain[:, h : h + 1]
        squares = squares + mixed * mixed
        mixed_ref[pl.ds(h, tokens, stride=heads), :] = mixed
    square_ref[...] = lax.dot_general(
        jnp.ones((8, LANES), F32),
        squares,
        (((1,), (1,)), ((), ())),
        precision=HIGHEST,
        preferred_element_type=F32,
    )


def mix(y, docs, prior_doc, cumul, inner, qh, mine, other, tokens, heads, after):
    return call(
        functools.partial(mix_kernel, tokens, heads, len(inner), len(mine)),
        "mix",
        [docs, prior_doc, cumul, *inner, *qh, *mine, *other],
        (sds((tokens * heads, LANES), F32), sds((8, tokens), F32)),
        mib=24,
        estimate=cost(2 * heads * tokens * HEAD_DIM**2, tokens * heads * LANES * 10),
        scalars=[y],
        after=after,
    )


def finish_kernel(tokens, heads, sums, step, gain_ref, gate_ref, mixed_ref, *refs):
    squares, (out_ref, done, sems) = refs[:sums], refs[sums:]
    total = squares[0][0:1, :]
    for ref in squares[1:]:
        total = total + ref[0:1, :]
    scale = lax.rsqrt(total / (HEADS * HEAD_DIM) + 1e-06)
    rows = jnp.concatenate([scale[:, i * LANES : (i + 1) * LANES] for i in range(tokens // LANES)], axis=0)
    column = doc_columns(rows, tokens)
    copies = []
    for i in range(0, tokens, step):
        at = pl.ds(i * heads, step * heads)
        gate = jax.nn.sigmoid(gate_ref[at, :].astype(F32)).reshape(step, heads, LANES)
        mixed = mixed_ref[at, :].reshape(step, heads, LANES)
        inv = column[i : i + step, :][:, None, :]
        out = mixed * inv * gain_ref[...][None] * gate
        done[at, :] = out.reshape(step * heads, LANES).astype(BF16)
        copies.append(pltpu.make_async_copy(done.at[at, :], out_ref.at[at, :], sems.at[i // step]))
        copies[-1].start()
    for copy in copies:
        copy.wait()


def finish(gain, gate, mixed, squares, tokens, heads, after):
    step = 64
    return call(
        functools.partial(finish_kernel, tokens, heads, len(squares), step),
        "finish",
        [gain, gate, mixed, *squares],
        sds((tokens * heads, LANES), BF16),
        scratch=[pltpu.VMEM((tokens * heads, LANES), BF16), pltpu.SemaphoreType.DMA((tokens // step,))],
        estimate=cost(0, tokens * heads * LANES * 8, tokens * heads * LANES),
        after=after,
        out_hbm=True,
    )


def attend_kernel(tokens, heads, kv_here, blocks, is_first, is_last, unroll, *refs):
    refs = list(refs)
    take = lambda n: [refs.pop(0) for _ in range(n)]
    per_group = heads // kv_here
    rows = tokens * per_group
    step = CHUNK // per_group
    if is_first:
        doc_ref, query_ref = take(2)
    else:
        wide_ref, state_ref = take(2)
    kv = take(blocks)
    if is_first:
        wide_ref = take(1)[0]
    out_ref = take(1)[0]
    if is_last:
        take(1)[0][...] = jnp.zeros((8, LANES), F32)
    bias = take(1)[0]
    if is_first:
        doc_rep = take(1)[0]
    if is_last:
        done, sems = take(2)

    lane = lax.broadcasted_iota(jnp.int32, (tokens, LANES), 1).astype(F32)
    end = 2 * kv_here * tokens
    for j, ref in enumerate(kv):
        docs = doc_columns(ref[end : end + INFO, :].astype(F32), tokens)
        bias[j] = jnp.where(docs == lane, 0.0, -BIG).astype(BF16)
    if is_first:
        column = doc_columns(doc_ref[...], tokens)
        for h in range(per_group):
            doc_rep[pl.ds(h, tokens, stride=per_group), :] = (column == lane).astype(F32)
    ones = jnp.ones((STATE_ROWS - HEAD_DIM, tokens), BF16)

    def some_chunks(i, carry):
        chains = [(u, g) for u in range(unroll) for g in range(kv_here)]
        chunk = [i * unroll + u for u in range(unroll)]
        at = [pl.ds(pl.multiple_of(c * CHUNK, CHUNK), CHUNK) for c in chunk]
        picked = [pl.ds(pl.multiple_of(c * (step * heads), step * heads), step * heads) for c in chunk]
        scores, results = {}, {}

        def begin(u, g):
            if is_first:
                query = query_ref[picked[u], :].astype(F32).reshape(step, heads, LANES)
                query = query[:, g * per_group : (g + 1) * per_group, :].reshape(CHUNK, LANES)
                wide = jnp.concatenate([query.astype(BF16), doc_rep[at[u], :].astype(BF16)], axis=1)
                wide_ref[g, at[u], :] = wide
            else:
                wide = wide_ref[g, at[u], :]
            out = []
            for j, ref in enumerate(kv):
                keys = jnp.concatenate([ref[g * tokens : (g + 1) * tokens, :], bias[j]], axis=1)
                out.append(
                    lax.dot_general(keys, wide, (((1,), (1,)), ((), ())), preferred_element_type=F32)
                )
            if is_first:
                token = chunk[u] * step + lax.broadcasted_iota(jnp.int32, (tokens, CHUNK), 1) // per_group
                key_at = lax.broadcasted_iota(jnp.int32, (tokens, CHUNK), 0)
                out[0] = jnp.where(key_at <= token, out[0], -BIG)
            scores[u, g] = out

        def end_chain(u, g):
            here = scores.pop((u, g))
            top = jnp.max(here[0], axis=0, keepdims=True)
            for score in here[1:]:
                top = jnp.maximum(top, jnp.max(score, axis=0, keepdims=True))
            total = None
            if not is_first:
                before = state_ref[g, :, at[u]]
                top_before = before[STATE_ROWS - 1 : STATE_ROWS, :]
                top = jnp.maximum(top, top_before)
                total = before * jnp.exp2((top_before - top) * SCORE_TO_EXP2)
            for ref, score in zip(kv, here):
                weights = jnp.exp2((score - top) * SCORE_TO_EXP2).astype(BF16)
                first = (kv_here + g) * tokens
                parts = [ref[first + p : first + p + LANES, :] for p in range(0, tokens, LANES)]
                values = jnp.concatenate([jnp.concatenate(parts, axis=1), ones], axis=0)
                more = jnp.dot(values, weights, preferred_element_type=F32)
                total = more if total is None else total + more
            if is_last:
                results[u, g] = jnp.transpose(total[0:HEAD_DIM] / total[HEAD_DIM : HEAD_DIM + 1])
            else:
                out_ref[g, 0 : STATE_ROWS - 8, at[u]] = total[0 : STATE_ROWS - 8]
                out_ref[g, STATE_ROWS - 8 : STATE_ROWS, at[u]] = jnp.broadcast_to(top, (8, CHUNK))

        ahead = 2
        for n in range(len(chains) + ahead):
            if n < len(chains):
                begin(*chains[n])
            if n >= ahead:
                end_chain(*chains[n - ahead])
        if is_last:
            for u in range(unroll):
                result = [results[u, g] for g in range(kv_here)]
                if kv_here > 1:
                    result = [r.reshape(step, per_group, LANES) for r in result]
                    result = [jnp.concatenate(result, axis=1).reshape(step * heads, LANES)]
                done[picked[u], :] = result[0].astype(BF16)
                pltpu.make_async_copy(
                    done.at[picked[u], :], out_ref.at[picked[u], :], sems.at[chunk[u]]
                ).start()
        return carry

    lax.fori_loop(0, rows // (CHUNK * unroll), some_chunks, 0)
    if is_last:
        for c in range(rows // CHUNK):
            at = pl.ds(c * step * heads, step * heads)
            pltpu.make_async_copy(done.at[at, :], out_ref.at[at, :], sems.at[c]).wait()


def attend(first, state, kv, is_last, tokens, heads, kv_here, after):
    is_first = state is None
    blocks = len(kv)
    rows = tokens * heads // kv_here
    unroll = min(4, rows // CHUNK)
    wide_shape = sds((kv_here, rows, 2 * LANES), BF16)
    state_shape = sds((kv_here, STATE_ROWS, rows), F32)
    out_shape = sds((tokens * heads, LANES), BF16) if is_last else state_shape
    scratch = [pltpu.VMEM((blocks, tokens, LANES), BF16)]
    if is_first:
        out_shape = (wide_shape, out_shape)
        scratch.append(pltpu.VMEM((rows, LANES), F32))
    if is_last:
        out_shape = (out_shape, sds((8, LANES), F32))
        scratch.append(pltpu.VMEM((tokens * heads, LANES), BF16))
        scratch.append(pltpu.SemaphoreType.DMA((rows // CHUNK,)))
    span = blocks * tokens
    return call(
        functools.partial(attend_kernel, tokens, heads, kv_here, blocks, is_first, is_last, unroll),
        "attend",
        [*first, *([] if is_first else [state]), *kv],
        out_shape,
        scratch=scratch,
        mib=24,
        estimate=cost(
            4 * tokens * heads * span * 2 * LANES, 4 * tokens * heads * LANES * 4, tokens * heads * span
        ),
        after=after,
        out_hbm=is_last,
    )


def body(
    blocks,
    lin_query,
    lin_key,
    lin_value,
    lin_gate,
    log_decay,
    norm_gain,
    doc_ids,
    soft_query,
    soft_key,
    soft_value,
):
    tokens, heads, _ = lin_query.shape
    tensor = HEADS // heads
    kv_here = max(1, heads // GROUP)
    half = heads // 2
    pieces = 2 if half % 2 == 0 else 1
    parts = 2 if half % 8 == 0 else 1
    count = half // pieces
    longest = blocks * tokens * 5 // 8
    window = min(blocks - 1, (longest - 1 + tokens - 1) // tokens)
    flat = lambda x: x.reshape(-1, LANES)
    block = lax.axis_index("seq")
    y = (block % 2).astype(jnp.int32).reshape(1)
    start = (lax.axis_index("tp") * heads // GROUP).astype(jnp.int32).reshape(1)
    def send(x, pairs):
        return lax.ppermute(x, "seq", [p for p in pairs if 0 <= p[0] < blocks and 0 <= p[1] < blocks])

    everyone = range(blocks)
    swap = [(b, b ^ 1) for b in everyone]

    own_kv, docs, cumul, info, held, sent = front(
        start,
        y,
        [
            doc_ids.reshape(tokens // LANES, LANES),
            flat(soft_key),
            flat(soft_value),
            jnp.transpose(log_decay),
            flat(lin_key),
            flat(lin_value),
        ],
        tokens,
        heads,
        kv_here,
        pieces,
    )
    came = [send(x, swap) for x in sent]
    far_step = window if window % 2 else blocks
    beside = send(own_kv, [(b, b + (far_step if b % 2 else 1)) for b in everyone])
    lane_kv, cross_kv = [], []
    ahead = own_kv
    for back in range(1, window // 2 + 1):
        ahead = send(ahead, [(b, b + 2) for b in everyone if b >= 2 * (back - 1)])
        lane_kv.append(ahead)
        cross_kv.append(send(ahead, [p for p in swap if p[0] >= 2 * back]))

    state = {}

    def first_attention(after):
        state["wide"], state["sum"] = attend(
            (docs, flat(soft_query)), None, [own_kv], False, tokens, heads, kv_here, after
        )
        return state["sum"]

    def more_attention(kv, is_last, after):
        state["sum"] = attend(
            (state["wide"],), state["sum"], kv, is_last, tokens, heads, kv_here, after
        )
        return state["sum"]

    inner, qh = [], []

    def inner_of(part, after):
        n = heads // parts
        got = inner_part(
            cumul, docs, flat(lin_query), flat(lin_key), flat(lin_value), tokens, heads, part * n, n, after
        )
        inner.append(got[0])
        qh.append(got[1])
        return got[0]

    beside_work = [first_attention]
    beside_work += [functools.partial(inner_of, part) for part in range(parts)]
    beside_work.append(functools.partial(more_attention, [beside] + lane_kv[:1], False))

    latest = [None] * pieces
    arrived = [[] for _ in range(pieces)]
    done = info
    for row in range(blocks // 2 - 1):
        if beside_work:
            done = beside_work.pop(0)([done])
        for p in range(pieces):
            done = chain_step(
                y, held[p], info, came[p], came[0], latest[p], p * count, count, [done]
            )
            latest[p] = send(done, [(2 * row, 2 * row + 2), (2 * row + 1, 2 * row + 3)])
            arrived[p].append(latest[p])
    while beside_work:
        done = beside_work.pop(0)([done])
    mine, far = [], []
    prior_doc = None
    for p in range(pieces):
        done, sent, prior_doc = prior_states(
            y, held[p], info, came[p], came[0], arrived[p], p * count, count, [done]
        )
        mine.append(done)
        far.append(send(sent, swap))
    rest = [kv for pair in zip(cross_kv, lane_kv[1:] + [None]) for kv in pair if kv is not None]
    done = more_attention(rest[:1], False, [done])
    rest = rest[1:]
    mixed, squares = mix(
        y, docs, prior_doc, cumul, inner, qh, mine, far, tokens, heads, [done]
    )
    sums = [squares]
    for shift in range(1, tensor):
        sums.append(
            lax.ppermute(squares, "tp", [(t, (t + shift) % tensor) for t in range(tensor)])
        )
    after = [squares]
    while rest:
        got = more_attention(rest[:2], len(rest) <= 2, after)
        rest, after = rest[2:], []
    soft_out, done = got
    lin_out = finish(norm_gain, flat(lin_gate), mixed, sums, tokens, heads, [done])
    shape = (tokens, heads, HEAD_DIM)
    return lin_out.reshape(shape), soft_out.reshape(shape)


def solution(mesh):
    in_specs = (
        P("seq", "tp", None),
        P("seq", "tp", None),
        P("seq", "tp", None),
        P("seq", "tp", None),
        P("seq", "tp"),
        P("tp", None),
        P("seq"),
        P("seq", "tp", None),
        P("seq", None, None),
        P("seq", None, None),
    )
    out_specs = (P("seq", "tp", None), P("seq", "tp", None))
    return jax.shard_map(
        functools.partial(body, mesh.shape["seq"]),
        mesh=mesh,
        in_specs=in_specs,
        out_specs=out_specs,
        check_vma=False,
    )
```

time: 81.2 us -> 65.6 us (0.81)
  Pallas kernels: 38.9 us -> 26.9 us
  local copies, waits for them, and re-layouts: 7.9 us -> 0.03 us
  waiting for transfers between devices: 0.71 us -> 5.02 us
    pallas_call x18 -> x17, Pallas kernels: 38.9 us -> 26.9 us  [call(): pl.pallas_call(run, out_shape=outs, in_specs=[SMEM] * len(scalars) + [HBM...]
    unnamed x32 -> x12, local copies, waits for them, and re-layouts: 7.85 us -> 0.03 us
    ppermute x15, waiting for transfers between devices: 0.7 us -> 5.02 us  [send(): lax.ppermute(x, 'seq', [p for p in pairs if 0 <= p[0] < blocks and 0 <= p...]
  transfers between devices with their start and end apart: 18 -> 18, of which waited for: 1 -> 5; matrix products, arithmetic and copies ran while one was open for 0% -> 0% of each run, Pallas kernels for 46% -> 31%
where the time goes in v3:
time: 65.6 us; the launch traced here: 65.3 us
  starting transfers between devices  32.2 us (49%)
  Pallas kernels  26.9 us (41%)
  waiting for transfers between devices  5.02 us (8%)
  between operations  1.18 us (2%)
    ppermute x15, starting transfers between devices, send(): lax.ppermute(x, 'seq', [p for p in pairs if 0 <= p[0] < blocks and 0 <= p...  29.2 us
    pallas_call x17, Pallas kernels, call(): pl.pallas_call(run, out_shape=outs, in_specs=[SMEM] * len(scalars) + [HBM...  26.9 us
    ppermute x15, waiting for transfers between devices, send(): lax.ppermute(x, 'seq', [p for p in pairs if 0 <= p[0] < blocks and 0 <= p...  5.02 us
    ppermute x3, starting transfers between devices, body(): lax.ppermute(squares, 'tp', [(t, (t + shift) % tensor) for t in range(ten...  2.97 us
  transfers between devices with their start and end apart: 18, of which 5 were waited for; matrix products, arithmetic and copies ran while one was open for 0% of the time, Pallas kernels for 31%

profile of v3, /device:TPU:16, one launch (start us, length us, event | category | flops | bytes accessed | tf_op | source)
XLA Modules:
  0.0 65.3 jit_solution(6653206052365967663)
XLA Ops:
  0.7 4.9 %front.1 = (bf16[1040,128]{1,0:T(8,128)(2,1)S(1)}, f32[16,128]{1,0:T(8,128)S(1)}, f32[256,128]{1,0:T(8,128)S(1)}, bf16[16,128]{1,0:T(8,128)(2,1)S(1)}, bf16[512,...) custom-call(s32[1]{0:T(128)} %bitcast.2.refs_0_, ...), custom_call_target="tpu_custom_call" | custom-call | flops 134217728 | bytes 5242880 | tf_op jit(solution)/shard_map/front/pallas_call | solution.py:56
  5.6 3.5 %collective-permute-start.9 = (bf16[1040,128]{1,0:T(8,128)(2,1)S(1)}, bf16[1040,128]{1,0:T(8,128)(2,1)S(1)}, u32[]{:S(2)}, u32[]{:S(2)}) collective-permute-start(bf16[1040,128]{1,0:T(8,128)(2,1)S(1)} %get-tuple-element.31.refs_2_), channel_id=1, source_target_pairs={{0,8},{4,12},{8,16},{12,20},{16,24},{20,28},{1,9},{5,13},{9,17},{1... | collective-permute-start | bytes 798728 | tf_op jit(solution)/shard_map/ppermute | solution.py:596
  9.1 1.6 %collective-permute-start.1 = (bf16[528,128]{1,0:T(8,128)(2,1)S(1)}, bf16[528,128]{1,0:T(8,128)(2,1)S(1)}, u32[]{:S(2)}, u32[]{:S(2)}) collective-permute-start(bf16[528,128]{1,0:T(8,128)(2,1)S(1)} %get-tuple-element.29), channel_id=1, source_target_pairs={{0,4},{4,0},{8,12},{12,8},{16,20},{20,16},{24,28},{28,24},{1,5},{5... | collective-permute-start | bytes 405512 | tf_op jit(solution)/shard_map/ppermute | solution.py:596
  10.6 0.5 collective-permute-start
  11.2 2.6 %attend.4 = (bf16[2,2048,256]{2,1,0:T(8,128)(2,1)S(1)}, f32[2,144,2048]{2,1,0:T(8,128)S(1)}) custom-call(f32[16,128]{1,0:T(8,128)S(1)} %get-tuple-element.25.refs_0_.refs_1_, bf16[4096,128]{1,0:T(8,128)(2,1)S(1)} %bitcast.22, bf16[1040,128]{1,0:T(8,128)(2,1)S(1)} %get-tuple-element.31.refs_2_, bf16[16,128]{1,0:T(8,128)(2,1)S(1)} %get-tuple-element.27.refs_3_.refs_2_), custom_call_target="tpu_custom_call" | custom-call | flops 1073741824 | bytes 8388608 | tf_op jit(solution)/shard_map/attend/pallas_call | solution.py:56
  13.8 0.0 copy-start
  13.8 0.0 copy-start.1
  13.8 0.0 copy-start.2
  13.8 1.8 %collective-permute-done.1.refs_3_.refs_4_ = bf16[528,128]{1,0:T(8,128)(2,1)S(1)} collective-permute-done((bf16[528,128]{1,0:T(8,128)(2,1)S(1)}, bf16[528,128]{1,0:T(8,128)(2,1)S(1)}, u32[]{:S(2)}, u32[]{:S(2)}) %collective-permute-start.1) | collective-permute-done | bytes 135200 | tf_op jit(solution)/shard_map/ppermute | solution.py:596
  15.6 0.1 chain_step.6.refs_5_
  15.7 0.7 %collective-permute-start.3 = (bf16[528,128]{1,0:T(8,128)(2,1)S(1)}, bf16[528,128]{1,0:T(8,128)(2,1)S(1)}, u32[]{:S(2)}, u32[]{:S(2)}) collective-permute-start(bf16[528,128]{1,0:T(8,128)(2,1)S(1)} %chain_step.6.refs_5_), channel_id=1, source_target_pairs={{0,8},{4,12},{1,9},{5,13},{2,10},{6,14},{3,11},{7,15}} | collective-permute-start | bytes 405512 | tf_op jit(solution)/shard_map/ppermute | solution.py:596
  16.4 0.6 collective-permute-done.refs_3_
  17.0 0.1 chain_step.7.refs_5_
  17.1 0.7 %collective-permute-start.2 = (bf16[528,128]{1,0:T(8,128)(2,1)S(1)}, bf16[528,128]{1,0:T(8,128)(2,1)S(1)}, u32[]{:S(2)}, u32[]{:S(2)}) collective-permute-start(bf16[528,128]{1,0:T(8,128)(2,1)S(1)} %chain_step.7.refs_5_), channel_id=1, source_target_pairs={{0,8},{4,12},{1,9},{5,13},{2,10},{6,14},{3,11},{7,15}} | collective-permute-start | bytes 405512 | tf_op jit(solution)/shard_map/ppermute | solution.py:596
  17.8 0.0 collective-permute-done.9.refs_3_
  17.8 1.9 %collective-permute-start.16 = (bf16[1040,128]{1,0:T(8,128)(2,1)S(1)}, bf16[1040,128]{1,0:T(8,128)(2,1)S(1)}, u32[]{:S(2)}, u32[]{:S(2)}) collective-permute-start(bf16[1040,128]{1,0:T(8,128)(2,1)S(1)} %collective-permute-done.9.refs_3_), channel_id=1, source_target_pairs={{8,16},{12,20},{16,24},{20,28},{9,17},{13,21},{17,25},{21,29},{10,... | collective-permute-start | bytes 798728 | tf_op jit(solution)/shard_map/ppermute | solution.py:596
  19.7 3.4 %collective-permute-start.8 = (bf16[1040,128]{1,0:T(8,128)(2,1)S(1)}, bf16[1040,128]{1,0:T(8,128)(2,1)S(1)}, u32[]{:S(2)}, u32[]{:S(2)}) collective-permute-start(bf16[1040,128]{1,0:T(8,128)(2,1)S(1)} %get-tuple-element.31.refs_2_), channel_id=1, source_target_pairs={{0,4},{4,24},{8,12},{16,20},{24,28},{1,5},{5,25},{9,13},{17,21},{2... | collective-permute-start | bytes 798728 | tf_op jit(solution)/shard_map/ppermute | solution.py:596
  23.2 1.9 %inner_part.2 = (f32[2048,128]{1,0:T(8,128)S(1)}, bf16[2048,128]{1,0:T(8,128)(2,1)S(1)}) custom-call(f32[256,128]{1,0:T(8,128)S(1)} %get-tuple-element.33.refs_0_.refs_3_, f32[16,128]{1,0:T(8,128)S(1)} %get-tuple-element.25.refs_0_.refs_1_, bf16[4096,128]{1,0:T(8,128)(2,1)S(1)} %bitcast.19, bf16[4096,128]{1,0:T(8,128)(2,1)S(1)} %bitcast.14, ...), custom_call_target="tpu_custom_call" | custom-call | flops 268435456 | bytes 6291456 | tf_op jit(solution)/shard_map/inner_part/pallas_call | solution.py:56
  25.1 0.0 collective-permute-done.3.refs_5_
  25.2 0.2 chain_step.8.refs_6_
  25.3 1.3 %collective-permute-start.5 = (bf16[528,128]{1,0:T(8,128)(2,1)S(1)}, bf16[528,128]{1,0:T(8,128)(2,1)S(1)}, u32[]{:S(2)}, u32[]{:S(2)}) collective-permute-start(bf16[528,128]{1,0:T(8,128)(2,1)S(1)} %chain_step.8.refs_6_), channel_id=1, source_target_pairs={{8,16},{12,20},{9,17},{13,21},{10,18},{14,22},{11,19},{15,23}} | collective-permute-start | bytes 405512 | tf_op jit(solution)/shard_map/ppermute | solution.py:596
  26.6 0.0 collective-permute-done.2.refs_5_
  26.6 0.2 chain_step.9.refs_5_
  26.8 1.3 %collective-permute-start.4 = (bf16[528,128]{1,0:T(8,128)(2,1)S(1)}, bf16[528,128]{1,0:T(8,128)(2,1)S(1)}, u32[]{:S(2)}, u32[]{:S(2)}) collective-permute-start(bf16[528,128]{1,0:T(8,128)(2,1)S(1)} %chain_step.9.refs_5_), channel_id=1, source_target_pairs={{8,16},{12,20},{9,17},{13,21},{10,18},{14,22},{11,19},{15,23}} | collective-permute-start | bytes 405512 | tf_op jit(solution)/shard_map/ppermute | solution.py:596
  28.1 1.9 %collective-permute-start.12 = (bf16[1040,128]{1,0:T(8,128)(2,1)S(1)}, bf16[1040,128]{1,0:T(8,128)(2,1)S(1)}, u32[]{:S(2)}, u32[]{:S(2)}) collective-permute-start(bf16[1040,128]{1,0:T(8,128)(2,1)S(1)} %collective-permute-done.9.refs_3_), channel_id=1, source_target_pairs={{8,12},{12,8},{16,20},{20,16},{24,28},{28,24},{9,13},{13,9},{17,21... | collective-permute-start | bytes 798728 | tf_op jit(solution)/shard_map/ppermute | solution.py:596
  30.0 1.9 %inner_part.3 = (f32[2048,128]{1,0:T(8,128)S(1)}, bf16[2048,128]{1,0:T(8,128)(2,1)S(1)}) custom-call(f32[256,128]{1,0:T(8,128)S(1)} %get-tuple-element.33.refs_0_.refs_3_, f32[16,128]{1,0:T(8,128)S(1)} %get-tuple-element.25.refs_0_.refs_1_, bf16[4096,128]{1,0:T(8,128)(2,1)S(1)} %bitcast.20, bf16[4096,128]{1,0:T(8,128)(2,1)S(1)} %bitcast.15, ...), custom_call_target="tpu_custom_call" | custom-call | flops 268435456 | bytes 6291456 | tf_op jit(solution)/shard_map/inner_part/pallas_call | solution.py:56
  32.0 0.6 collective-permute-done.5.refs_5_.refs_6_
  32.6 0.2 chain_step.10.refs_6_
  32.7 1.3 %collective-permute-start.7 = (bf16[528,128]{1,0:T(8,128)(2,1)S(1)}, bf16[528,128]{1,0:T(8,128)(2,1)S(1)}, u32[]{:S(2)}, u32[]{:S(2)}) collective-permute-start(bf16[528,128]{1,0:T(8,128)(2,1)S(1)} %chain_step.10.refs_6_), channel_id=1, source_target_pairs={{16,24},{20,28},{17,25},{21,29},{18,26},{22,30},{19,27},{23,31}} | collective-permute-start | bytes 405512 | tf_op jit(solution)/shard_map/ppermute | solution.py:596
  34.0 0.0 collective-permute-done.4.refs_5_.refs_6_
  34.1 0.2 chain_step.11.refs_4_
  34.2 1.3 %collective-permute-start.6 = (bf16[528,128]{1,0:T(8,128)(2,1)S(1)}, bf16[528,128]{1,0:T(8,128)(2,1)S(1)}, u32[]{:S(2)}, u32[]{:S(2)}) collective-permute-start(bf16[528,128]{1,0:T(8,128)(2,1)S(1)} %chain_step.11.refs_4_), channel_id=1, source_target_pairs={{16,24},{20,28},{17,25},{21,29},{18,26},{22,30},{19,27},{23,31}} | collective-permute-start | bytes 405512 | tf_op jit(solution)/shard_map/ppermute | solution.py:596
  35.5 0.0 collective-permute-done.16.refs_2_
  35.6 7.7 %collective-permute-start.17 = (bf16[1040,128]{1,0:T(8,128)(2,1)S(1)}, bf16[1040,128]{1,0:T(8,128)(2,1)S(1)}, u32[]{:S(2)}, u32[]{:S(2)}) collective-permute-start(bf16[1040,128]{1,0:T(8,128)(2,1)S(1)} %collective-permute-done.16.refs_2_), channel_id=1, source_target_pairs={{16,20},{20,16},{24,28},{28,24},{17,21},{21,17},{25,29},{29,25},{1... | collective-permute-start | bytes 798728 | tf_op jit(solution)/shard_map/ppermute | solution.py:596
  43.3 3.6 %attend.5.refs_8_.refs_1_ = f32[2,144,2048]{2,1,0:T(8,128)S(1)} custom-call(bf16[2,2048,256]{2,1,0:T(8,128)(2,1)S(1)} %get-tuple-element.36.refs_0_, f32[2,144,2048]{2,1,0:T(8,128)S(1)} %get-tuple-element.32.refs_5_.refs_1_, bf16[1040,128]{1,0:T(8,128)(2,1)S(1)} %collective-permute-done.8.refs_2_, bf16[1040,128]{1,0:T(8,128)(2,1)S(1)} %collective-permute-done.9.refs_3_, ...), custom_call_target="tpu_custom_call" | custom-call | flops 2147483648 | bytes 8388608 | tf_op jit(solution)/shard_map/attend/pallas_call | solution.py:56
  47.0 0.7 %prior_states.2 = (bf16[512,128]{1,0:T(8,128)(2,1)S(1)}, bf16[512,128]{1,0:T(8,128)(2,1)S(1)}, f32[8,128]{1,0:T(8,128)}) custom-call(s32[1]{0:T(128)} %bitcast.1.refs_1_.refs_0_, bf16[512,128]{1,0:T(8,128)(2,1)S(1)} %get-tuple-element.30.refs_1_, bf16[16,128]{1,0:T(8,128)(2,1)S(1)} %get-tuple-element.27.refs_3_.refs_2_, ...), custom_call_target="tpu_custom_call" | custom-call | flops 262144 | bytes 786432 | tf_op jit(solution)/shard_map/prior_states/pallas_call | solution.py:56
  47.7 0.2 prior_states.3
  47.9 0.1 collective-permute-start.11
  47.9 2.0 %collective-permute-start.10 = (bf16[512,128]{1,0:T(8,128)(2,1)S(1)}, bf16[512,128]{1,0:T(8,128)(2,1)S(1)}, u32[]{:S(2)}, u32[]{:S(2)}) collective-permute-start(bf16[512,128]{1,0:T(8,128)(2,1)S(1)} %get-tuple-element.42), channel_id=1, source_target_pairs={{0,4},{4,0},{8,12},{12,8},{16,20},{20,16},{24,28},{28,24},{1,5},{5... | collective-permute-start | bytes 393224 | tf_op jit(solution)/shard_map/ppermute | solution.py:596
  49.9 2.3 %attend.6.refs_12_.refs_1_ = f32[2,144,2048]{2,1,0:T(8,128)S(1)} custom-call(bf16[2,2048,256]{2,1,0:T(8,128)(2,1)S(1)} %get-tuple-element.36.refs_0_, f32[2,144,2048]{2,1,0:T(8,128)S(1)} %attend.5.refs_8_.refs_1_, bf16[1040,128]{1,0:T(8,128)(2,1)S(1)} %collective-permute-done.12.refs_2_, bf16[512,128]{1,0:T(8,128)(2,1)S(1)} %get-tuple-element.41.refs_3_.refs_9_), custom_call_target="tpu_custom_call" | custom-call | flops 1073741824 | bytes 8388608 | tf_op jit(solution)/shard_map/attend/pallas_call | solution.py:56
  52.3 0.6 collective-permute-done.11.refs_11_
  52.9 1.4 %collective-permute-done.10.refs_10_ = bf16[512,128]{1,0:T(8,128)(2,1)S(1)} collective-permute-done((bf16[512,128]{1,0:T(8,128)(2,1)S(1)}, bf16[512,128]{1,0:T(8,128)(2,1)S(1)}, u32[]{:S(2)}, u32[]{:S(2)}) %collective-permute-start.10) | collective-permute-done | bytes 131104 | tf_op jit(solution)/shard_map/ppermute | solution.py:596
  54.3 1.6 %mix.1 = (f32[4096,128]{1,0:T(8,128)S(1)}, f32[8,256]{1,0:T(8,128)S(1)}) custom-call(s32[1]{0:T(128)} %bitcast.1.refs_1_.refs_0_, f32[16,128]{1,0:T(8,128)S(1)} %get-tuple-element.25.refs_0_.refs_1_, f32[8,128]{1,0:T(8,128)S(1)} %get-tuple-element.38.refs_2_, f32[256,128]{1,0:T(8,128)S(1)} %get-tuple-element.33.refs_0_.refs_3_, ...), custom_call_target="tpu_custom_call" | custom-call | flops 134217728 | bytes 5242880 | tf_op jit(solution)/shard_map/mix/pallas_call | solution.py:56
  55.9 0.0 collective-permute-start.13
  55.9 1.6 %collective-permute-start.14 = (f32[8,256]{1,0:T(8,128)S(1)}, f32[8,256]{1,0:T(8,128)S(1)}, u32[]{:S(2)}, u32[]{:S(2)}) collective-permute-start(f32[8,256]{1,0:T(8,128)S(1)} %get-tuple-element.45.refs_4_.refs_3_), channel_id=1, source_target_pairs={{0,2},{1,3},{2,0},{3,1},{4,6},{5,7},{6,4},{7,5},{8,10},{9,11},{10,... | collective-permute-start | bytes 24584 | tf_op jit(solution)/shard_map/ppermute | solution.py:687
  57.5 1.4 %collective-permute-start.15 = (f32[8,256]{1,0:T(8,128)S(1)}, f32[8,256]{1,0:T(8,128)S(1)}, u32[]{:S(2)}, u32[]{:S(2)}) collective-permute-start(f32[8,256]{1,0:T(8,128)S(1)} %get-tuple-element.45.refs_4_.refs_3_), channel_id=1, source_target_pairs={{0,3},{1,0},{2,1},{3,2},{4,7},{5,4},{6,5},{7,6},{8,11},{9,8},{10,9... | collective-permute-start | bytes 24584 | tf_op jit(solution)/shard_map/ppermute | solution.py:687
  58.9 4.6 %attend.7 = (bf16[4096,128]{1,0:T(8,128)(2,1)}, f32[8,128]{1,0:T(8,128)S(1)}) custom-call(bf16[2,2048,256]{2,1,0:T(8,128)(2,1)S(1)} %get-tuple-element.36.refs_0_, f32[2,144,2048]{2,1,0:T(8,128)S(1)} %attend.6.refs_12_.refs_1_, bf16[1040,128]{1,0:T(8,128)(2,1)S(1)} %collective-permute-done.16.refs_2_, bf16[1040,128]{1,0:T(8,128)(2,1)S(1)} %collective-permute-done.17.refs_3_, ...), custom_call_target="tpu_custom_call" | custom-call | flops 2147483648 | bytes 8388608 | tf_op jit(solution)/shard_map/attend/pallas_call | solution.py:56
  63.5 1.6 %finish.1 = bf16[4096,128]{1,0:T(8,128)(2,1)} custom-call(f32[16,128]{1,0:T(8,128)S(1)} %copy-done.4, bf16[4096,128]{1,0:T(8,128)(2,1)S(1)} %bitcast.21, f32[4096,128]{1,0:T(8,128)S(1)} %get-tuple-element.44.refs_2_, f32[8,256]{1,0:T(8,128)S(1)} %get-tuple-element.45.refs_4_.refs_3_, f32[8,256]{1,0:T(8,128)S(1)} %collective-permute-done.13.refs_4_, ...), custom_call_target="tpu_custom_call" | custom-call | bytes 4194304 | tf_op jit(solution)/shard_map/finish/pallas_call | solution.py:56
  (17 shorter events, 0.0 us)
Async XLA Ops:
  0.6 10.5 %copy-start.5 = (bf16[256,16,128]{2,1,0:T(8,128)(2,1)S(1)}, bf16[256,16,128]{2,1,0:T(8,128)(2,1)}, u32[]{:S(2)}) copy-start(bf16[256,16,128]{2,1,0:T(8,128)(2,1)} %param.17) | copy-start | bytes 3145732
  5.6 12.2 %collective-permute-start.9 = (bf16[1040,128]{1,0:T(8,128)(2,1)S(1)}, bf16[1040,128]{1,0:T(8,128)(2,1)S(1)}, u32[]{:S(2)}, u32[]{:S(2)}) collective-permute-start(bf16[1040,128]{1,0:T(8,128)(2,1)S(1)} %get-tuple-element.31.refs_2_), channel_id=1, source_target_pairs={{0,8},{4,12},{8,16},{12,20},{16,24},{20,28},{1,9},{5,13},{9,17},{1... | collective-permute-start | bytes 798728 | tf_op jit(solution)/shard_map/ppermute | solution.py:596
  9.1 6.5 %collective-permute-start.1 = (bf16[528,128]{1,0:T(8,128)(2,1)S(1)}, bf16[528,128]{1,0:T(8,128)(2,1)S(1)}, u32[]{:S(2)}, u32[]{:S(2)}) collective-permute-start(bf16[528,128]{1,0:T(8,128)(2,1)S(1)} %get-tuple-element.29), channel_id=1, source_target_pairs={{0,4},{4,0},{8,12},{12,8},{16,20},{20,16},{24,28},{28,24},{1,5},{5... | collective-permute-start | bytes 405512 | tf_op jit(solution)/shard_map/ppermute | solution.py:596
  10.6 6.3 %collective-permute-start = (bf16[512,128]{1,0:T(8,128)(2,1)S(1)}, bf16[512,128]{1,0:T(8,128)(2,1)S(1)}, u32[]{:S(2)}, u32[]{:S(2)}) collective-permute-start(bf16[512,128]{1,0:T(8,128)(2,1)S(1)} %get-tuple-element.28), channel_id=1, source_target_pairs={{0,4},{4,0},{8,12},{12,8},{16,20},{20,16},{24,28},{28,24},{1,5},{5... | collective-permute-start | bytes 393224 | tf_op jit(solution)/shard_map/ppermute | solution.py:596
  13.8 9.4 %copy-start = (bf16[256,16,128]{2,1,0:T(8,128)(2,1)S(1)}, bf16[256,16,128]{2,1,0:T(8,128)(2,1)}, u32[]{:S(2)}) copy-start(bf16[256,16,128]{2,1,0:T(8,128)(2,1)} %param.11) | copy-start | bytes 3145732
  13.8 9.4 %copy-start.1 = (bf16[256,16,128]{2,1,0:T(8,128)(2,1)S(1)}, bf16[256,16,128]{2,1,0:T(8,128)(2,1)}, u32[]{:S(2)}) copy-start(bf16[256,16,128]{2,1,0:T(8,128)(2,1)} %param.12) | copy-start | bytes 3145732
  13.8 9.4 %copy-start.2 = (bf16[256,16,128]{2,1,0:T(8,128)(2,1)S(1)}, bf16[256,16,128]{2,1,0:T(8,128)(2,1)}, u32[]{:S(2)}) copy-start(bf16[256,16,128]{2,1,0:T(8,128)(2,1)} %param.10) | copy-start | bytes 3145732
  15.7 9.4 %collective-permute-start.3 = (bf16[528,128]{1,0:T(8,128)(2,1)S(1)}, bf16[528,128]{1,0:T(8,128)(2,1)S(1)}, u32[]{:S(2)}, u32[]{:S(2)}) collective-permute-start(bf16[528,128]{1,0:T(8,128)(2,1)S(1)} %chain_step.6.refs_5_), channel_id=1, source_target_pairs={{0,8},{4,12},{1,9},{5,13},{2,10},{6,14},{3,11},{7,15}} | collective-permute-start | bytes 405512 | tf_op jit(solution)/shard_map/ppermute | solution.py:596
  17.1 9.5 %collective-permute-start.2 = (bf16[528,128]{1,0:T(8,128)(2,1)S(1)}, bf16[528,128]{1,0:T(8,128)(2,1)S(1)}, u32[]{:S(2)}, u32[]{:S(2)}) collective-permute-start(bf16[528,128]{1,0:T(8,128)(2,1)S(1)} %chain_step.7.refs_5_), channel_id=1, source_target_pairs={{0,8},{4,12},{1,9},{5,13},{2,10},{6,14},{3,11},{7,15}} | collective-permute-start | bytes 405512 | tf_op jit(solution)/shard_map/ppermute | solution.py:596
  17.8 17.7 %collective-permute-start.16 = (bf16[1040,128]{1,0:T(8,128)(2,1)S(1)}, bf16[1040,128]{1,0:T(8,128)(2,1)S(1)}, u32[]{:S(2)}, u32[]{:S(2)}) collective-permute-start(bf16[1040,128]{1,0:T(8,128)(2,1)S(1)} %collective-permute-done.9.refs_3_), channel_id=1, source_target_pairs={{8,16},{12,20},{16,24},{20,28},{9,17},{13,21},{17,25},{21,29},{10,... | collective-permute-start | bytes 798728 | tf_op jit(solution)/shard_map/ppermute | solution.py:596
  19.7 23.6 %collective-permute-start.8 = (bf16[1040,128]{1,0:T(8,128)(2,1)S(1)}, bf16[1040,128]{1,0:T(8,128)(2,1)S(1)}, u32[]{:S(2)}, u32[]{:S(2)}) collective-permute-start(bf16[1040,128]{1,0:T(8,128)(2,1)S(1)} %get-tuple-element.31.refs_2_), channel_id=1, source_target_pairs={{0,4},{4,24},{8,12},{16,20},{24,28},{1,5},{5,25},{9,13},{17,21},{2... | collective-permute-start | bytes 798728 | tf_op jit(solution)/shard_map/ppermute | solution.py:596
  25.3 7.2 %collective-permute-start.5 = (bf16[528,128]{1,0:T(8,128)(2,1)S(1)}, bf16[528,128]{1,0:T(8,128)(2,1)S(1)}, u32[]{:S(2)}, u32[]{:S(2)}) collective-permute-start(bf16[528,128]{1,0:T(8,128)(2,1)S(1)} %chain_step.8.refs_6_), channel_id=1, source_target_pairs={{8,16},{12,20},{9,17},{13,21},{10,18},{14,22},{11,19},{15,23}} | collective-permute-start | bytes 405512 | tf_op jit(solution)/shard_map/ppermute | solution.py:596
  26.8 7.2 %collective-permute-start.4 = (bf16[528,128]{1,0:T(8,128)(2,1)S(1)}, bf16[528,128]{1,0:T(8,128)(2,1)S(1)}, u32[]{:S(2)}, u32[]{:S(2)}) collective-permute-start(bf16[528,128]{1,0:T(8,128)(2,1)S(1)} %chain_step.9.refs_5_), channel_id=1, source_target_pairs={{8,16},{12,20},{9,17},{13,21},{10,18},{14,22},{11,19},{15,23}} | collective-permute-start | bytes 405512 | tf_op jit(solution)/shard_map/ppermute | solution.py:596
  28.1 21.8 %collective-permute-start.12 = (bf16[1040,128]{1,0:T(8,128)(2,1)S(1)}, bf16[1040,128]{1,0:T(8,128)(2,1)S(1)}, u32[]{:S(2)}, u32[]{:S(2)}) collective-permute-start(bf16[1040,128]{1,0:T(8,128)(2,1)S(1)} %collective-permute-done.9.refs_3_), channel_id=1, source_target_pairs={{8,12},{12,8},{16,20},{20,16},{24,28},{28,24},{9,13},{13,9},{17,21... | collective-permute-start | bytes 798728 | tf_op jit(solution)/shard_map/ppermute | solution.py:596
  32.7 14.2 %collective-permute-start.7 = (bf16[528,128]{1,0:T(8,128)(2,1)S(1)}, bf16[528,128]{1,0:T(8,128)(2,1)S(1)}, u32[]{:S(2)}, u32[]{:S(2)}) collective-permute-start(bf16[528,128]{1,0:T(8,128)(2,1)S(1)} %chain_step.10.refs_6_), channel_id=1, source_target_pairs={{16,24},{20,28},{17,25},{21,29},{18,26},{22,30},{19,27},{23,31}} | collective-permute-start | bytes 405512 | tf_op jit(solution)/shard_map/ppermute | solution.py:596
  34.2 13.4 %collective-permute-start.6 = (bf16[528,128]{1,0:T(8,128)(2,1)S(1)}, bf16[528,128]{1,0:T(8,128)(2,1)S(1)}, u32[]{:S(2)}, u32[]{:S(2)}) collective-permute-start(bf16[528,128]{1,0:T(8,128)(2,1)S(1)} %chain_step.11.refs_4_), channel_id=1, source_target_pairs={{16,24},{20,28},{17,25},{21,29},{18,26},{22,30},{19,27},{23,31}} | collective-permute-start | bytes 405512 | tf_op jit(solution)/shard_map/ppermute | solution.py:596
  35.6 23.3 %collective-permute-start.17 = (bf16[1040,128]{1,0:T(8,128)(2,1)S(1)}, bf16[1040,128]{1,0:T(8,128)(2,1)S(1)}, u32[]{:S(2)}, u32[]{:S(2)}) collective-permute-start(bf16[1040,128]{1,0:T(8,128)(2,1)S(1)} %collective-permute-done.16.refs_2_), channel_id=1, source_target_pairs={{16,20},{20,16},{24,28},{28,24},{17,21},{21,17},{25,29},{29,25},{1... | collective-permute-start | bytes 798728 | tf_op jit(solution)/shard_map/ppermute | solution.py:596
  47.9 5.0 %collective-permute-start.11 = (bf16[512,128]{1,0:T(8,128)(2,1)S(1)}, bf16[512,128]{1,0:T(8,128)(2,1)S(1)}, u32[]{:S(2)}, u32[]{:S(2)}) collective-permute-start(bf16[512,128]{1,0:T(8,128)(2,1)S(1)} %get-tuple-element.43), channel_id=1, source_target_pairs={{0,4},{4,0},{8,12},{12,8},{16,20},{20,16},{24,28},{28,24},{1,5},{5... | collective-permute-start | bytes 393224 | tf_op jit(solution)/shard_map/ppermute | solution.py:596
  47.9 6.4 %collective-permute-start.10 = (bf16[512,128]{1,0:T(8,128)(2,1)S(1)}, bf16[512,128]{1,0:T(8,128)(2,1)S(1)}, u32[]{:S(2)}, u32[]{:S(2)}) collective-permute-start(bf16[512,128]{1,0:T(8,128)(2,1)S(1)} %get-tuple-element.42), channel_id=1, source_target_pairs={{0,4},{4,0},{8,12},{12,8},{16,20},{20,16},{24,28},{28,24},{1,5},{5... | collective-permute-start | bytes 393224 | tf_op jit(solution)/shard_map/ppermute | solution.py:596
  55.9 7.6 %copy-start.3 = (bf16[256,16,128]{2,1,0:T(8,128)(2,1)S(1)}, bf16[256,16,128]{2,1,0:T(8,128)(2,1)}, u32[]{:S(2)}) copy-start(bf16[256,16,128]{2,1,0:T(8,128)(2,1)} %param.13) | copy-start | bytes 3145732
  55.9 7.6 %copy-start.4 = (f32[16,128]{1,0:T(8,128)S(1)}, f32[16,128]{1,0:T(8,128)}, u32[]{:S(2)}) copy-start(f32[16,128]{1,0:T(8,128)} %refs_0_.1) | copy-start | bytes 24580
  55.9 7.6 %collective-permute-start.13 = (f32[8,256]{1,0:T(8,128)S(1)}, f32[8,256]{1,0:T(8,128)S(1)}, u32[]{:S(2)}, u32[]{:S(2)}) collective-permute-start(f32[8,256]{1,0:T(8,128)S(1)} %get-tuple-element.45.refs_4_.refs_3_), channel_id=1, source_target_pairs={{0,1},{1,2},{2,3},{3,0},{4,5},{5,6},{6,7},{7,4},{8,9},{9,10},{10,1... | collective-permute-start | bytes 24584 | tf_op jit(solution)/shard_map/ppermute | solution.py:687
  55.9 7.5 %collective-permute-start.14 = (f32[8,256]{1,0:T(8,128)S(1)}, f32[8,256]{1,0:T(8,128)S(1)}, u32[]{:S(2)}, u32[]{:S(2)}) collective-permute-start(f32[8,256]{1,0:T(8,128)S(1)} %get-tuple-element.45.refs_4_.refs_3_), channel_id=1, source_target_pairs={{0,2},{1,3},{2,0},{3,1},{4,6},{5,7},{6,4},{7,5},{8,10},{9,11},{10,... | collective-permute-start | bytes 24584 | tf_op jit(solution)/shard_map/ppermute | solution.py:687
  57.5 6.0 %collective-permute-start.15 = (f32[8,256]{1,0:T(8,128)S(1)}, f32[8,256]{1,0:T(8,128)S(1)}, u32[]{:S(2)}, u32[]{:S(2)}) collective-permute-start(f32[8,256]{1,0:T(8,128)S(1)} %get-tuple-element.45.refs_4_.refs_3_), channel_id=1, source_target_pairs={{0,3},{1,0},{2,1},{3,2},{4,7},{5,4},{6,5},{7,6},{8,11},{9,8},{10,9... | collective-permute-start | bytes 24584 | tf_op jit(solution)/shard_map/ppermute | solution.py:687

commit v4 on v3

--- a/solution.py
+++ b/solution.py
@@ -157,13 +157,7 @@
     upper = pltpu.roll(total, LANES - half, 1)
 
     def info_of(totals):
-        hi = totals.astype(BF16).astype(F32)
-        mid = (totals - hi).astype(BF16).astype(F32)
-        lo = totals - hi - mid
-        info = jnp.zeros((INFO, LANES), F32)
-        for i, part in enumerate((hi, mid, lo, first_doc, last_doc)):
-            info = jnp.where(line == i, part, info)
-        return info.astype(BF16)
+        return info_rows((*in_parts(totals), first_doc, last_doc))
 
     mine = (y == 0).astype(F32)
     info_ref[...] = info_of(total * mine + upper * (1.0 - mine))
@@ -203,6 +197,25 @@
     return (*out[:4], out[4 : 4 + pieces], out[4 + pieces :])
 
 
+def in_parts(x):
+    hi = x.astype(BF16).astype(F32)
+    mid = (x - hi).astype(BF16).astype(F32)
+    return hi, mid, x - hi - mid
+
+
+def info_rows(parts):
+    line = lax.broadcasted_iota(jnp.int32, (INFO, LANES), 0)
+    info = jnp.zeros((INFO, LANES), F32)
+    for i, part in enumerate(parts):
+        info = jnp.where(line == i, part, info)
+    return info.astype(BF16)
+
+
+def read_map(ref, size):
+    info = ref[size : size + INFO, :].astype(F32)
+    return info[0:1] + info[1:2] + info[2:3], info[3:4], info[4:5]
+
+
 def row_terms(y_ref, own_info, other_info):
     even = y_ref[0] == 0
     own = own_info.astype(F32)
@@ -215,38 +228,30 @@
     first_b, last_b = b[3:4], b[4:5]
     whole_a = (first_a == last_a).astype(F32)
     link_b = ((last_a == first_b) & (first_b == last_b)).astype(F32)
-    return even, decay_a, decay_b * link_b, first_a, whole_a, last_a, last_b
-
-
-def chain_kernel(count, first, arrivals, y_ref, *refs):
-    keep_ref, info_ref, other_ref, other_info_ref = refs[:4]
-    came, out_ref = refs[4 : 4 + arrivals], refs[4 + arrivals]
+    return even, decay_a * whole_a, decay_b * link_b, first_a, last_a, last_b
+
+
+def row_kernel(count, first, y_ref, keep_ref, info_ref, other_ref, other_info_ref, out_ref):
     size = count * HEAD_DIM
-    even, decay_a, gain_b, first_a, whole_a, _, last_b = row_terms(
+    even, gain_a, gain_b, first_a, _, last_b = row_terms(
         y_ref, info_ref[...], other_info_ref[size : size + INFO, :]
     )
-    if arrivals:
-        came_doc = came[0][size : size + 1, :].astype(F32)
-        gain_a = decay_a * whole_a * (came_doc == first_a).astype(F32)
     for i in range(count):
         rows = slice(i * HEAD_DIM, (i + 1) * HEAD_DIM)
         lane = slice(first + i, first + i + 1)
         own = keep_ref[rows, :].astype(F32)
         other = other_ref[rows, :].astype(F32)
-        total = jnp.where(even, own, other)
-        if arrivals:
-            total = total + gain_a[:, lane] * came[0][rows, :].astype(F32)
-        out_ref[rows, :] = (gain_b[:, lane] * total + jnp.where(even, other, own)).astype(BF16)
-    out_ref[size : size + INFO, :] = jnp.broadcast_to(last_b, (INFO, LANES)).astype(BF16)
-
-
-def chain_step(y, keep, info, other, other_info, came, first, count, after):
+        state_a, state_b = jnp.where(even, own, other), jnp.where(even, other, own)
+        out_ref[rows, :] = (gain_b[:, lane] * state_a + state_b).astype(BF16)
+    out_ref[size : size + INFO, :] = info_rows((*in_parts(gain_a * gain_b), first_a, last_b))
+
+
+def row_map(y, keep, info, other, other_info, first, count, after):
     size = count * HEAD_DIM
-    came = [] if came is None else [came]
     return call(
-        functools.partial(chain_kernel, count, first, len(came)),
-        "chain_step",
-        [keep, info, other, other_info, *came],
+        functools.partial(row_kernel, count, first),
+        "row_map",
+        [keep, info, other, other_info],
         sds((size + INFO, LANES), BF16),
         estimate=cost(4 * size * LANES, 4 * size * LANES * 2),
         scalars=[y],
@@ -254,40 +259,108 @@
     )
 
 
-def prior_kernel(count, first, arrivals, y_ref, *refs):
-    keep_ref, info_ref, other_ref, other_info_ref = refs[:4]
-    came = refs[4 : 4 + arrivals]
-    mine_ref, send_ref, doc_ref = refs[4 + arrivals :]
+def scan_kernel(count, first, has_before, upper_ref, *refs):
+    refs = list(refs)
+    mine_ref, came_ref = refs[:2]
+    before_ref = refs[2] if has_before else None
+    run_ref, out_ref = refs[-2:]
     size = count * HEAD_DIM
-    even, decay_a, _, first_a, whole_a, last_a, _ = row_terms(
-        y_ref, info_ref[...], other_info_ref[size : size + INFO, :]
-    )
-    came_doc = jnp.zeros((1, LANES), F32)
-    for ref in came:
-        came_doc = came_doc + ref[size : size + 1, :].astype(F32)
-    gain_a = decay_a * whole_a * (came_doc == first_a).astype(F32)
+    upper = upper_ref[0] == 1
+    gain_m, first_m, last_m = read_map(mine_ref, size)
+    gain_c, first_c, last_c = read_map(came_ref, size)
+    link = jnp.where(upper, (last_c == first_m).astype(F32), (last_m == first_c).astype(F32))
+    gain = jnp.where(upper, gain_m, gain_c) * link
     for i in range(count):
         rows = slice(i * HEAD_DIM, (i + 1) * HEAD_DIM)
         lane = slice(first + i, first + i + 1)
-        before_a = jnp.zeros((HEAD_DIM, LANES), F32)
-        for ref in came:
-            before_a = before_a + ref[rows, :].astype(F32)
+        mine, came = mine_ref[rows, :].astype(F32), came_ref[rows, :].astype(F32)
+        lower_sum, upper_sum = jnp.where(upper, came, mine), jnp.where(upper, mine, came)
+        run_ref[rows, :] = (gain[:, lane] * lower_sum + upper_sum).astype(BF16)
+    run_ref[size : size + INFO, :] = info_rows(
+        (
+            *in_parts(gain * jnp.where(upper, gain_c, gain_m)),
+            jnp.where(upper, first_c, first_m),
+            jnp.where(upper, last_m, last_c),
+        )
+    )
+    if not has_before:
+        out_ref[...] = jnp.where(upper, came_ref[...], jnp.zeros_like(came_ref))
+        return
+    gain_b, first_b, last_b = read_map(before_ref, size)
+    empty = first_b == 0.0
+    factor = jnp.where(empty, 1.0, gain_b * (last_c == first_b).astype(F32))
+    for i in range(count):
+        rows = slice(i * HEAD_DIM, (i + 1) * HEAD_DIM)
+        lane = slice(first + i, first + i + 1)
+        before = before_ref[rows, :].astype(F32)
+        joined = factor[:, lane] * came_ref[rows, :].astype(F32) + before
+        out_ref[rows, :] = jnp.where(upper, joined, before).astype(BF16)
+    out_ref[size : size + INFO, :] = info_rows(
+        (
+            *in_parts(jnp.where(upper, factor * gain_c, gain_b)),
+            jnp.where(upper, first_c, first_b),
+            jnp.where(upper, jnp.where(empty, last_c, last_b), last_b),
+        )
+    )
+
+
+def scan_step(upper, mine, came, before, first, count, after):
+    size = count * HEAD_DIM
+    shape = sds((size + INFO, LANES), BF16)
+    before = [] if before is None else [before]
+    return call(
+        functools.partial(scan_kernel, count, first, len(before)),
+        "scan_step",
+        [mine, came, *before],
+        (shape, shape),
+        estimate=cost(6 * size * LANES, 6 * size * LANES * 2),
+        scalars=[upper],
+        after=after,
+    )
+
+
+def prior_kernel(count, first, has_before, y_ref, upper_ref, *refs):
+    keep_ref, info_ref, other_ref, other_info_ref, came_ref = refs[:5]
+    before_ref = refs[5] if has_before else None
+    mine_ref, send_ref, doc_ref = refs[-3:]
+    size = count * HEAD_DIM
+    upper = (upper_ref[0] == 1).astype(F32)
+    even, gain_a, _, first_a, last_a, _ = row_terms(
+        y_ref, info_ref[...], other_info_ref[size : size + INFO, :]
+    )
+    _, _, last_c = read_map(came_ref, size)
+    factor, doc = upper, upper * last_c
+    if has_before:
+        gain_b, first_b, last_b = read_map(before_ref, size)
+        empty = first_b == 0.0
+        factor = upper * jnp.where(empty, 1.0, gain_b * (last_c == first_b).astype(F32))
+        doc = jnp.where(empty, doc, last_b)
+    else:
+        factor = jnp.broadcast_to(factor, (1, LANES))
+    gain_a = gain_a * (doc == first_a).astype(F32)
+    for i in range(count):
+        rows = slice(i * HEAD_DIM, (i + 1) * HEAD_DIM)
+        lane = slice(first + i, first + i + 1)
+        before_a = factor[:, lane] * came_ref[rows, :].astype(F32)
+        if has_before:
+            before_a = before_a + before_ref[rows, :].astype(F32)
         state_a = jnp.where(even, keep_ref[rows, :].astype(F32), other_ref[rows, :].astype(F32))
         before_b = gain_a[:, lane] * before_a + state_a
         mine_ref[rows, :] = jnp.where(even, before_a, before_b).astype(BF16)
         send_ref[rows, :] = jnp.where(even, before_b, before_a).astype(BF16)
-    doc_ref[...] = jnp.broadcast_to(jnp.where(even, came_doc, last_a), (8, LANES))
-
-
-def prior_states(y, keep, info, other, other_info, came, first, count, after):
+    doc_ref[...] = jnp.broadcast_to(jnp.where(even, doc, last_a), (8, LANES))
+
+
+def prior_states(y, upper, keep, info, other, other_info, came, before, first, count, after):
     size = count * HEAD_DIM
+    before = [] if before is None else [before]
     return call(
-        functools.partial(prior_kernel, count, first, len(came)),
+        functools.partial(prior_kernel, count, first, len(before)),
         "prior_states",
-        [keep, info, other, other_info, *came],
+        [keep, info, other, other_info, came, *before],
         (sds((size, LANES), BF16), sds((size, LANES), BF16), sds((8, LANES), F32)),
         estimate=cost(4 * size * LANES, 6 * size * LANES * 2),
-        scalars=[y],
+        scalars=[y, upper],
         after=after,
     )
 
@@ -583,7 +656,7 @@
     tensor = HEADS // heads
     kv_here = max(1, heads // GROUP)
     half = heads // 2
-    pieces = 2 if half % 2 == 0 else 1
+    pieces = 1
     parts = 2 if half % 8 == 0 else 1
     count = half // pieces
     longest = blocks * tokens * 5 // 8
@@ -653,28 +726,33 @@
     beside_work += [functools.partial(inner_of, part) for part in range(parts)]
     beside_work.append(functools.partial(more_attention, [beside] + lane_kv[:1], False))
 
-    latest = [None] * pieces
-    arrived = [[] for _ in range(pieces)]
     done = info
-    for row in range(blocks // 2 - 1):
+    mine, far = [], []
+    prior_doc = None
+    run, before = [None] * pieces, [None] * pieces
+    stages = (blocks // 2).bit_length() - 1
+    for stage in range(stages + 1):
         if beside_work:
             done = beside_work.pop(0)([done])
+        if stage == stages:
+            while beside_work:
+                done = beside_work.pop(0)([done])
+        upper = ((block >> stage) & 1).astype(jnp.int32).reshape(1)
         for p in range(pieces):
-            done = chain_step(
-                y, held[p], info, came[p], came[0], latest[p], p * count, count, [done]
-            )
-            latest[p] = send(done, [(2 * row, 2 * row + 2), (2 * row + 1, 2 * row + 3)])
-            arrived[p].append(latest[p])
-    while beside_work:
-        done = beside_work.pop(0)([done])
-    mine, far = [], []
-    prior_doc = None
-    for p in range(pieces):
-        done, sent, prior_doc = prior_states(
-            y, held[p], info, came[p], came[0], arrived[p], p * count, count, [done]
-        )
-        mine.append(done)
-        far.append(send(sent, swap))
+            at = (p * count, count, [done])
+            if stage == 0:
+                done = run[p] = row_map(y, held[p], info, came[p], came[0], *at)
+            elif stage < stages:
+                run[p], before[p] = scan_step(upper, run[p], got[p], before[p], *at)
+                done = run[p]
+            else:
+                done, sent, prior_doc = prior_states(
+                    y, upper, held[p], info, came[p], came[0], got[p], before[p], *at
+                )
+                mine.append(done)
+                far.append(send(sent, swap))
+        if stage < stages:
+            got = [send(x, [(b, b ^ (2 << stage)) for b in everyone]) for x in run]
     rest = [kv for pair in zip(cross_kv, lane_kv[1:] + [None]) for kv in pair if kv is not None]
     done = more_attention(rest[:1], False, [done])
     rest = rest[1:]
@@ -682,10 +760,8 @@
         y, docs, prior_doc, cumul, inner, qh, mine, far, tokens, heads, [done]
     )
     sums = [squares]
-    for shift in range(1, tensor):
-        sums.append(
-            lax.ppermute(squares, "tp", [(t, (t + shift) % tensor) for t in range(tensor)])
-        )
+    for other in range(1, tensor):
+        sums.append(lax.ppermute(squares, "tp", [(t, t ^ other) for t in range(tensor)]))
     after = [squares]
     while rest:
         got = more_attention(rest[:2], len(rest) <= 2, after)

time: 65.6 us -> 71 us (1.082)
  the two profiles are of different devices: /device:TPU:16 before, /device:TPU:19 now
where the time goes in v4:
time: 71 us; the launch traced here: 70.5 us
  Pallas kernels  32.7 us (46%)
  starting transfers between devices  26.3 us (37%)
  local copies, waits for them, and re-layouts  8.7 us (12%)
  waiting for transfers between devices  1.76 us (2%)
  between operations  1.13 us (2%)
    pallas_call x12, Pallas kernels, call(): pl.pallas_call(run, out_shape=outs, in_specs=[SMEM] * len(scalars) + [HBM...  32.7 us
    ppermute x9, starting transfers between devices, send(): lax.ppermute(x, 'seq', [p for p in pairs if 0 <= p[0] < blocks and 0 <= p...  21.8 us
    unnamed x40, local copies, waits for them, and re-layouts  8.7 us
    ppermute x3, starting transfers between devices, body(): lax.ppermute(squares, 'tp', [(t, t ^ other) for t in range(tensor)])  4.46 us
    ppermute x9, waiting for transfers between devices, send(): lax.ppermute(x, 'seq', [p for p in pairs if 0 <= p[0] < blocks and 0 <= p...  1.75 us
  transfers between devices with their start and end apart: 12, of which 2 were waited for; matrix products, arithmetic and copies ran while one was open for 0% of the time, Pallas kernels for 35%

profile of v4, /device:TPU:19, one launch (start us, length us, event | category | flops | bytes accessed | tf_op | source)
XLA Modules:
  0.0 70.5 jit_solution(14925823281999749810)
XLA Ops:
  0.7 5.5 %front.1 = (bf16[1040,128]{1,0:T(8,128)(2,1)}, f32[16,128]{1,0:T(8,128)S(1)}, f32[256,128]{1,0:T(8,128)S(1)}, bf16[16,128]{1,0:T(8,128)(2,1)S(1)}, bf16[1024,128...) custom-call(s32[1]{0:T(128)} %bitcast.2.refs_0_, s32[1]{0:T(128)} %bitcast.1.refs_1_.refs_0_, s32[2,128]{1,0:T(2,128)} %bitcast.29, ...), custom_call_target="tpu_custom_call" | custom-call | flops 134217728 | bytes 5242880 | tf_op jit(solution)/shard_map/front/pallas_call | solution.py:56
  6.1 1.3 %collective-permute-start = (bf16[1040,128]{1,0:T(8,128)(2,1)S(1)}, bf16[1040,128]{1,0:T(8,128)(2,1)S(1)}, u32[]{:S(2)}, u32[]{:S(2)}) collective-permute-start(bf16[1040,128]{1,0:T(8,128)(2,1)S(1)} %get-tuple-element.26), channel_id=1, source_target_pairs={{0,4},{4,0},{8,12},{12,8},{16,20},{20,16},{24,28},{28,24},{1,5},{5... | collective-permute-start | bytes 798728 | tf_op jit(solution)/shard_map/ppermute | solution.py:669
  7.5 3.5 %attend.4 = (bf16[2,2048,256]{2,1,0:T(8,128)(2,1)S(1)}, f32[2,144,2048]{2,1,0:T(8,128)S(1)}) custom-call(f32[16,128]{1,0:T(8,128)S(1)} %get-tuple-element.23.refs_0_.refs_1_, bf16[4096,128]{1,0:T(8,128)(2,1)S(1)} %bitcast.24, bf16[1040,128]{1,0:T(8,128)(2,1)} %get-tuple-element.27.refs_2_, bf16[16,128]{1,0:T(8,128)(2,1)S(1)} %get-tuple-element.25.refs_3_.refs_2_), custom_call_target="tpu_custom_call" | custom-call | flops 1073741824 | bytes 8388608 | tf_op jit(solution)/shard_map/attend/pallas_call | solution.py:56
  11.0 1.4 %copy-done.3 = bf16[2,2048,256]{2,1,0:T(8,128)(2,1)} copy-done((bf16[2,2048,256]{2,1,0:T(8,128)(2,1)}, bf16[2,2048,256]{2,1,0:T(8,128)(2,1)S(1)}, u32[]{:S(2)}) %copy-start.3) | copy-done | bytes 2097176
  12.3 1.1 %collective-permute-done.refs_3_.refs_4_.refs_5_ = bf16[1040,128]{1,0:T(8,128)(2,1)S(1)} collective-permute-done((bf16[1040,128]{1,0:T(8,128)(2,1)S(1)}, bf16[1040,128]{1,0:T(8,128)(2,1)S(1)}, u32[]{:S(2)}, u32[]{:S(2)}) %collective-permute-start) | collective-permute-done | bytes 266272 | tf_op jit(solution)/shard_map/ppermute | solution.py:669
  13.5 0.9 %row_map.1.refs_5_.refs_1_ = bf16[1040,128]{1,0:T(8,128)(2,1)} custom-call(s32[1]{0:T(128)} %bitcast.1.refs_1_.refs_0_, bf16[1024,128]{1,0:T(8,128)(2,1)S(1)} %get-tuple-element.24.refs_1_.refs_2_, bf16[16,128]{1,0:T(8,128)(2,1)S(1)} %get-tuple-element.25.refs_3_.refs_2_, bf16[1040,128]{1,0:T(8,128)(2,1)S(1)} %collective-permute-done.refs_3_.refs_4_.refs_5_, ...), custom_call_target="tpu_custom_call" | custom-call | flops 524288 | bytes 1048576 | tf_op jit(solution)/shard_map/row_map/pallas_call | solution.py:56
  14.4 0.7 %copy-done.5 = bf16[1040,128]{1,0:T(8,128)(2,1)} copy-done((bf16[1040,128]{1,0:T(8,128)(2,1)}, bf16[1040,128]{1,0:T(8,128)(2,1)S(1)}, u32[]{:S(2)}) %copy-start.5) | copy-done | bytes 266264
  15.1 1.3 %collective-permute-start.1 = (bf16[1040,128]{1,0:T(8,128)(2,1)}, bf16[1040,128]{1,0:T(8,128)(2,1)}, u32[]{:S(2)}, u32[]{:S(2)}) collective-permute-start(bf16[1040,128]{1,0:T(8,128)(2,1)} %row_map.1.refs_5_.refs_1_), channel_id=1, source_target_pairs={{0,8},{4,12},{8,0},{12,4},{16,24},{20,28},{24,16},{28,20},{1,9},{5... | collective-permute-start | bytes 798728 | tf_op jit(solution)/shard_map/ppermute | solution.py:669
  16.4 2.1 %collective-permute-start.4 = (bf16[1040,128]{1,0:T(8,128)(2,1)}, bf16[1040,128]{1,0:T(8,128)(2,1)}, u32[]{:S(2)}, u32[]{:S(2)}) collective-permute-start(bf16[1040,128]{1,0:T(8,128)(2,1)} %get-tuple-element.27.refs_2_), channel_id=1, source_target_pairs={{0,8},{4,12},{8,16},{12,20},{16,24},{20,28},{1,9},{5,13},{9,17},{1... | collective-permute-start | bytes 798728 | tf_op jit(solution)/shard_map/ppermute | solution.py:669
  18.4 3.9 %collective-permute-start.3 = (bf16[1040,128]{1,0:T(8,128)(2,1)}, bf16[1040,128]{1,0:T(8,128)(2,1)}, u32[]{:S(2)}, u32[]{:S(2)}) collective-permute-start(bf16[1040,128]{1,0:T(8,128)(2,1)} %get-tuple-element.27.refs_2_), channel_id=1, source_target_pairs={{0,4},{4,24},{8,12},{16,20},{24,28},{1,5},{5,25},{9,13},{17,21},{2... | collective-permute-start | bytes 798728 | tf_op jit(solution)/shard_map/ppermute | solution.py:669
  22.3 1.2 %copy-done.1 = bf16[256,16,128]{2,1,0:T(8,128)(2,1)S(1)} copy-done((bf16[256,16,128]{2,1,0:T(8,128)(2,1)S(1)}, bf16[256,16,128]{2,1,0:T(8,128)(2,1)}, u32[]{:S(2)}) %copy-start.1) | copy-done | bytes 1048600
  23.5 1.2 %copy-done.9 = bf16[256,16,128]{2,1,0:T(8,128)(2,1)S(1)} copy-done((bf16[256,16,128]{2,1,0:T(8,128)(2,1)S(1)}, bf16[256,16,128]{2,1,0:T(8,128)(2,1)}, u32[]{:S(2)}) %copy-start.9) | copy-done | bytes 1048600
  24.8 1.9 %inner_part.2 = (f32[2048,128]{1,0:T(8,128)S(1)}, bf16[2048,128]{1,0:T(8,128)(2,1)S(1)}) custom-call(f32[256,128]{1,0:T(8,128)S(1)} %get-tuple-element.29.refs_0_.refs_3_, f32[16,128]{1,0:T(8,128)S(1)} %get-tuple-element.23.refs_0_.refs_1_, bf16[4096,128]{1,0:T(8,128)(2,1)S(1)} %bitcast.21, bf16[4096,128]{1,0:T(8,128)(2,1)S(1)} %bitcast.16, ...), custom_call_target="tpu_custom_call" | custom-call | flops 268435456 | bytes 6291456 | tf_op jit(solution)/shard_map/inner_part/pallas_call | solution.py:56
  26.7 0.0 copy-start.14
  26.7 0.0 collective-permute-done.1.refs_2_
  26.7 2.1 %scan_step.1 = (bf16[1040,128]{1,0:T(8,128)(2,1)}, bf16[1040,128]{1,0:T(8,128)(2,1)S(1)}) custom-call(s32[1]{0:T(128)} %bitcast.10.refs_0_, bf16[1040,128]{1,0:T(8,128)(2,1)} %row_map.1.refs_5_.refs_1_, bf16[1040,128]{1,0:T(8,128)(2,1)} %collective-permute-done.1.refs_2_, f32[2048,128]{1,0:T(8,128)S(1)} %get-tuple-element.30.refs_3_.refs_4_), custom_call_target="tpu_custom_call" | custom-call | flops 786432 | bytes 1572864 | tf_op jit(solution)/shard_map/scan_step/pallas_call | solution.py:56
  28.8 1.0 %copy-done.7 = f32[2048,128]{1,0:T(8,128)} copy-done((f32[2048,128]{1,0:T(8,128)}, f32[2048,128]{1,0:T(8,128)S(1)}, u32[]{:S(2)}) %copy-start.7) | copy-done | bytes 1048600
  29.8 0.7 %copy-done.16 = bf16[1040,128]{1,0:T(8,128)(2,1)} copy-done((bf16[1040,128]{1,0:T(8,128)(2,1)}, bf16[1040,128]{1,0:T(8,128)(2,1)S(1)}, u32[]{:S(2)}) %copy-start.16) | copy-done | bytes 266264
  30.5 0.8 %collective-permute-start.2 = (bf16[1040,128]{1,0:T(8,128)(2,1)}, bf16[1040,128]{1,0:T(8,128)(2,1)}, u32[]{:S(2)}, u32[]{:S(2)}) collective-permute-start(bf16[1040,128]{1,0:T(8,128)(2,1)} %get-tuple-element.31.refs_5_), channel_id=1, source_target_pairs={{0,16},{4,20},{8,24},{12,28},{16,0},{20,4},{24,8},{28,12},{1,17},{... | collective-permute-start | bytes 798728 | tf_op jit(solution)/shard_map/ppermute | solution.py:669
  31.3 0.0 collective-permute-done.4.refs_3_
  31.3 3.6 %collective-permute-start.10 = (bf16[1040,128]{1,0:T(8,128)(2,1)}, bf16[1040,128]{1,0:T(8,128)(2,1)}, u32[]{:S(2)}, u32[]{:S(2)}) collective-permute-start(bf16[1040,128]{1,0:T(8,128)(2,1)} %collective-permute-done.4.refs_3_), channel_id=1, source_target_pairs={{8,16},{12,20},{16,24},{20,28},{9,17},{13,21},{17,25},{21,29},{10,... | collective-permute-start | bytes 798728 | tf_op jit(solution)/shard_map/ppermute | solution.py:669
  34.9 1.9 %collective-permute-start.6 = (bf16[1040,128]{1,0:T(8,128)(2,1)}, bf16[1040,128]{1,0:T(8,128)(2,1)S(1)}, u32[]{:S(2)}, u32[]{:S(2)}) collective-permute-start(bf16[1040,128]{1,0:T(8,128)(2,1)} %collective-permute-done.4.refs_3_), channel_id=1, source_target_pairs={{8,12},{12,8},{16,20},{20,16},{24,28},{28,24},{9,13},{13,9},{17,21... | collective-permute-start | bytes 798728 | tf_op jit(solution)/shard_map/ppermute | solution.py:669
  36.8 0.0 copy-start.2
  36.8 1.2 %copy-done.2 = bf16[256,16,128]{2,1,0:T(8,128)(2,1)S(1)} copy-done((bf16[256,16,128]{2,1,0:T(8,128)(2,1)S(1)}, bf16[256,16,128]{2,1,0:T(8,128)(2,1)}, u32[]{:S(2)}) %copy-start.2) | copy-done | bytes 1048600
  38.1 1.2 %copy-done.10 = bf16[256,16,128]{2,1,0:T(8,128)(2,1)S(1)} copy-done((bf16[256,16,128]{2,1,0:T(8,128)(2,1)S(1)}, bf16[256,16,128]{2,1,0:T(8,128)(2,1)}, u32[]{:S(2)}) %copy-start.10) | copy-done | bytes 1048600
  39.3 1.9 %inner_part.3 = (f32[2048,128]{1,0:T(8,128)S(1)}, bf16[2048,128]{1,0:T(8,128)(2,1)S(1)}) custom-call(f32[256,128]{1,0:T(8,128)S(1)} %get-tuple-element.29.refs_0_.refs_3_, f32[16,128]{1,0:T(8,128)S(1)} %get-tuple-element.23.refs_0_.refs_1_, bf16[4096,128]{1,0:T(8,128)(2,1)S(1)} %bitcast.22, bf16[4096,128]{1,0:T(8,128)(2,1)S(1)} %bitcast.17, ...), custom_call_target="tpu_custom_call" | custom-call | flops 268435456 | bytes 6291456 | tf_op jit(solution)/shard_map/inner_part/pallas_call | solution.py:56
  41.2 0.0 collective-permute-done.3.refs_2_
  41.2 4.7 %attend.5.refs_8_.refs_1_ = f32[2,144,2048]{2,1,0:T(8,128)S(1)} custom-call(bf16[2,2048,256]{2,1,0:T(8,128)(2,1)S(1)} %copy-done.4, f32[2,144,2048]{2,1,0:T(8,128)S(1)} %get-tuple-element.28.refs_5_.refs_1_, bf16[1040,128]{1,0:T(8,128)(2,1)} %collective-permute-done.3.refs_2_, bf16[1040,128]{1,0:T(8,128)(2,1)} %collective-permute-done.4.refs_3_, ...), custom_call_target="tpu_custom_call" | custom-call | flops 2147483648 | bytes 8388608 | tf_op jit(solution)/shard_map/attend/pallas_call | solution.py:56
  45.9 0.0 collective-permute-done.2.refs_6_
  45.9 1.2 %prior_states.1 = (bf16[1024,128]{1,0:T(8,128)(2,1)S(1)}, bf16[1024,128]{1,0:T(8,128)(2,1)S(1)}, f32[8,128]{1,0:T(8,128)S(1)}) custom-call(s32[1]{0:T(128)} %bitcast.1.refs_1_.refs_0_, s32[1]{0:T(128)} %bitcast.9.refs_1_, bf16[1024,128]{1,0:T(8,128)(2,1)S(1)} %copy-done.13, bf16[16,128]{1,0:T(8,128)(2,1)S(1)} %get-tuple-element.25.refs_3_.refs_2_, ...), custom_call_target="tpu_custom_call" | custom-call | flops 524288 | bytes 1572864 | tf_op jit(solution)/shard_map/prior_states/pallas_call | solution.py:56
  47.2 1.5 %collective-permute-start.5 = (bf16[1024,128]{1,0:T(8,128)(2,1)S(1)}, bf16[1024,128]{1,0:T(8,128)(2,1)S(1)}, u32[]{:S(2)}, u32[]{:S(2)}) collective-permute-start(bf16[1024,128]{1,0:T(8,128)(2,1)S(1)} %get-tuple-element.39), channel_id=1, source_target_pairs={{0,4},{4,0},{8,12},{12,8},{16,20},{20,16},{24,28},{28,24},{1,5},{5... | collective-permute-start | bytes 786440 | tf_op jit(solution)/shard_map/ppermute | solution.py:669
  48.7 0.6 collective-permute-done.10.refs_2_
  49.3 5.5 %collective-permute-start.11 = (bf16[1040,128]{1,0:T(8,128)(2,1)}, bf16[1040,128]{1,0:T(8,128)(2,1)S(1)}, u32[]{:S(2)}, u32[]{:S(2)}) collective-permute-start(bf16[1040,128]{1,0:T(8,128)(2,1)} %collective-permute-done.10.refs_2_), channel_id=1, source_target_pairs={{16,20},{20,16},{24,28},{28,24},{17,21},{21,17},{25,29},{29,25},{1... | collective-permute-start | bytes 798728 | tf_op jit(solution)/shard_map/ppermute | solution.py:669
  54.8 0.0 collective-permute-done.6.refs_2_
  54.8 0.0 copy-start.8
  54.8 0.0 copy-start.15
  54.8 2.3 %attend.6.refs_10_.refs_1_ = f32[2,144,2048]{2,1,0:T(8,128)S(1)} custom-call(bf16[2,2048,256]{2,1,0:T(8,128)(2,1)S(1)} %copy-done.4, f32[2,144,2048]{2,1,0:T(8,128)S(1)} %attend.5.refs_8_.refs_1_, bf16[1040,128]{1,0:T(8,128)(2,1)S(1)} %collective-permute-done.6.refs_2_, bf16[1024,128]{1,0:T(8,128)(2,1)S(1)} %get-tuple-element.38.refs_3_.refs_8_), custom_call_target="tpu_custom_call" | custom-call | flops 1073741824 | bytes 8388608 | tf_op jit(solution)/shard_map/attend/pallas_call | solution.py:56
  57.1 0.0 collective-permute-done.5.refs_9_
  57.1 1.6 %mix.1 = (f32[4096,128]{1,0:T(8,128)S(1)}, f32[8,256]{1,0:T(8,128)S(1)}) custom-call(s32[1]{0:T(128)} %bitcast.1.refs_1_.refs_0_, f32[16,128]{1,0:T(8,128)S(1)} %get-tuple-element.23.refs_0_.refs_1_, f32[8,128]{1,0:T(8,128)S(1)} %get-tuple-element.35.refs_2_, f32[256,128]{1,0:T(8,128)S(1)} %get-tuple-element.29.refs_0_.refs_3_, f32[2048,128]{1,0:T(8,128)S(1)} %copy-done.8, ...), custom_call_target="tpu_custom_call" | custom-call | flops 134217728 | bytes 5242880 | tf_op jit(solution)/shard_map/mix/pallas_call | solution.py:56
  58.7 2.8 %collective-permute-start.7 = (f32[8,256]{1,0:T(8,128)S(1)}, f32[8,256]{1,0:T(8,128)S(1)}, u32[]{:S(2)}, u32[]{:S(2)}) collective-permute-start(f32[8,256]{1,0:T(8,128)S(1)} %get-tuple-element.41.refs_4_.refs_3_), channel_id=1, source_target_pairs={{0,1},{1,0},{2,3},{3,2},{4,5},{5,4},{6,7},{7,6},{8,9},{9,8},{10,11... | collective-permute-start | bytes 24584 | tf_op jit(solution)/shard_map/ppermute | solution.py:764
  61.5 0.2 collective-permute-start.8
  61.7 1.5 %collective-permute-start.9 = (f32[8,256]{1,0:T(8,128)S(1)}, f32[8,256]{1,0:T(8,128)S(1)}, u32[]{:S(2)}, u32[]{:S(2)}) collective-permute-start(f32[8,256]{1,0:T(8,128)S(1)} %get-tuple-element.41.refs_4_.refs_3_), channel_id=1, source_target_pairs={{0,3},{1,2},{2,1},{3,0},{4,7},{5,6},{6,5},{7,4},{8,11},{9,10},{10,... | collective-permute-start | bytes 24584 | tf_op jit(solution)/shard_map/ppermute | solution.py:764
  63.2 0.0 collective-permute-done.11.refs_3_
  63.2 5.5 %attend.7 = (bf16[4096,128]{1,0:T(8,128)(2,1)}, f32[8,128]{1,0:T(8,128)S(1)}) custom-call(bf16[2,2048,256]{2,1,0:T(8,128)(2,1)S(1)} %copy-done.4, f32[2,144,2048]{2,1,0:T(8,128)S(1)} %attend.6.refs_10_.refs_1_, bf16[1040,128]{1,0:T(8,128)(2,1)} %collective-permute-done.10.refs_2_, bf16[1040,128]{1,0:T(8,128)(2,1)S(1)} %collective-permute-done.11.refs_3_, ...), custom_call_target="tpu_custom_call" | custom-call | flops 2147483648 | bytes 8388608 | tf_op jit(solution)/shard_map/attend/pallas_call | solution.py:56
  68.7 0.0 collective-permute-done.7.refs_4_
  68.7 0.0 collective-permute-done.8.refs_5_
  68.7 0.0 collective-permute-done.9.refs_6_
  68.7 1.6 %finish.1 = bf16[4096,128]{1,0:T(8,128)(2,1)} custom-call(f32[16,128]{1,0:T(8,128)S(1)} %copy-done.18, bf16[4096,128]{1,0:T(8,128)(2,1)S(1)} %bitcast.23, f32[4096,128]{1,0:T(8,128)S(1)} %get-tuple-element.40.refs_2_, f32[8,256]{1,0:T(8,128)S(1)} %get-tuple-element.41.refs_4_.refs_3_, f32[8,256]{1,0:T(8,128)S(1)} %collective-permute-done.7.refs_4_, ...), custom_call_target="tpu_custom_call" | custom-call | bytes 4194304 | tf_op jit(solution)/shard_map/finish/pallas_call | solution.py:56
  (28 shorter events, 0.1 us)
Async XLA Ops:
  0.6 6.8 %copy-start.19 = (bf16[256,16,128]{2,1,0:T(8,128)(2,1)S(1)}, bf16[256,16,128]{2,1,0:T(8,128)(2,1)}, u32[]{:S(2)}) copy-start(bf16[256,16,128]{2,1,0:T(8,128)(2,1)} %param.17) | copy-start | bytes 3145732
  6.1 8.2 %copy-start.12 = (bf16[1024,128]{1,0:T(8,128)(2,1)}, bf16[1024,128]{1,0:T(8,128)(2,1)S(1)}, u32[]{:S(2)}) copy-start(bf16[1024,128]{1,0:T(8,128)(2,1)S(1)} %get-tuple-element.24.refs_1_.refs_2_) | copy-start | bytes 786436
  6.1 7.3 %collective-permute-start = (bf16[1040,128]{1,0:T(8,128)(2,1)S(1)}, bf16[1040,128]{1,0:T(8,128)(2,1)S(1)}, u32[]{:S(2)}, u32[]{:S(2)}) collective-permute-start(bf16[1040,128]{1,0:T(8,128)(2,1)S(1)} %get-tuple-element.26), channel_id=1, source_target_pairs={{0,4},{4,0},{8,12},{12,8},{16,20},{20,16},{24,28},{28,24},{1,5},{5... | collective-permute-start | bytes 798728 | tf_op jit(solution)/shard_map/ppermute | solution.py:669
  11.0 1.4 %copy-start.3 = (bf16[2,2048,256]{2,1,0:T(8,128)(2,1)}, bf16[2,2048,256]{2,1,0:T(8,128)(2,1)S(1)}, u32[]{:S(2)}) copy-start(bf16[2,2048,256]{2,1,0:T(8,128)(2,1)S(1)} %get-tuple-element.33.refs_0_) | copy-start | bytes 6291460
  12.3 10.0 %copy-start = (bf16[256,16,128]{2,1,0:T(8,128)(2,1)S(1)}, bf16[256,16,128]{2,1,0:T(8,128)(2,1)}, u32[]{:S(2)}) copy-start(bf16[256,16,128]{2,1,0:T(8,128)(2,1)} %param.11) | copy-start | bytes 3145732
  14.3 0.7 %copy-start.5 = (bf16[1040,128]{1,0:T(8,128)(2,1)}, bf16[1040,128]{1,0:T(8,128)(2,1)S(1)}, u32[]{:S(2)}) copy-start(bf16[1040,128]{1,0:T(8,128)(2,1)S(1)} %collective-permute-done.refs_3_.refs_4_.refs_5_) | copy-start | bytes 798724
  15.1 11.6 %collective-permute-start.1 = (bf16[1040,128]{1,0:T(8,128)(2,1)}, bf16[1040,128]{1,0:T(8,128)(2,1)}, u32[]{:S(2)}, u32[]{:S(2)}) collective-permute-start(bf16[1040,128]{1,0:T(8,128)(2,1)} %row_map.1.refs_5_.refs_1_), channel_id=1, source_target_pairs={{0,8},{4,12},{8,0},{12,4},{16,24},{20,28},{24,16},{28,20},{1,9},{5... | collective-permute-start | bytes 798728 | tf_op jit(solution)/shard_map/ppermute | solution.py:669
  16.4 14.9 %collective-permute-start.4 = (bf16[1040,128]{1,0:T(8,128)(2,1)}, bf16[1040,128]{1,0:T(8,128)(2,1)}, u32[]{:S(2)}, u32[]{:S(2)}) collective-permute-start(bf16[1040,128]{1,0:T(8,128)(2,1)} %get-tuple-element.27.refs_2_), channel_id=1, source_target_pairs={{0,8},{4,12},{8,16},{12,20},{16,24},{20,28},{1,9},{5,13},{9,17},{1... | collective-permute-start | bytes 798728 | tf_op jit(solution)/shard_map/ppermute | solution.py:669
  18.4 22.8 %collective-permute-start.3 = (bf16[1040,128]{1,0:T(8,128)(2,1)}, bf16[1040,128]{1,0:T(8,128)(2,1)}, u32[]{:S(2)}, u32[]{:S(2)}) collective-permute-start(bf16[1040,128]{1,0:T(8,128)(2,1)} %get-tuple-element.27.refs_2_), channel_id=1, source_target_pairs={{0,4},{4,24},{8,12},{16,20},{24,28},{1,5},{5,25},{9,13},{17,21},{2... | collective-permute-start | bytes 798728 | tf_op jit(solution)/shard_map/ppermute | solution.py:669
  22.3 1.2 %copy-start.1 = (bf16[256,16,128]{2,1,0:T(8,128)(2,1)S(1)}, bf16[256,16,128]{2,1,0:T(8,128)(2,1)}, u32[]{:S(2)}) copy-start(bf16[256,16,128]{2,1,0:T(8,128)(2,1)} %param.12) | copy-start | bytes 3145732
  23.5 1.2 %copy-start.9 = (bf16[256,16,128]{2,1,0:T(8,128)(2,1)S(1)}, bf16[256,16,128]{2,1,0:T(8,128)(2,1)}, u32[]{:S(2)}) copy-start(bf16[256,16,128]{2,1,0:T(8,128)(2,1)} %param.10) | copy-start | bytes 3145732
  26.7 2.2 %copy-start.14 = (bf16[2048,128]{1,0:T(8,128)(2,1)}, bf16[2048,128]{1,0:T(8,128)(2,1)S(1)}, u32[]{:S(2)}) copy-start(bf16[2048,128]{1,0:T(8,128)(2,1)S(1)} %get-tuple-element.36.refs_6_) | copy-start | bytes 1572868
  28.8 1.0 %copy-start.7 = (f32[2048,128]{1,0:T(8,128)}, f32[2048,128]{1,0:T(8,128)S(1)}, u32[]{:S(2)}) copy-start(f32[2048,128]{1,0:T(8,128)S(1)} %get-tuple-element.30.refs_3_.refs_4_) | copy-start | bytes 3145732
  29.8 0.7 %copy-start.16 = (bf16[1040,128]{1,0:T(8,128)(2,1)}, bf16[1040,128]{1,0:T(8,128)(2,1)S(1)}, u32[]{:S(2)}) copy-start(bf16[1040,128]{1,0:T(8,128)(2,1)S(1)} %get-tuple-element.32.refs_7_) | copy-start | bytes 798724
  30.5 15.4 %collective-permute-start.2 = (bf16[1040,128]{1,0:T(8,128)(2,1)}, bf16[1040,128]{1,0:T(8,128)(2,1)}, u32[]{:S(2)}, u32[]{:S(2)}) collective-permute-start(bf16[1040,128]{1,0:T(8,128)(2,1)} %get-tuple-element.31.refs_5_), channel_id=1, source_target_pairs={{0,16},{4,20},{8,24},{12,28},{16,0},{20,4},{24,8},{28,12},{1,17},{... | collective-permute-start | bytes 798728 | tf_op jit(solution)/shard_map/ppermute | solution.py:669
  31.3 18.0 %collective-permute-start.10 = (bf16[1040,128]{1,0:T(8,128)(2,1)}, bf16[1040,128]{1,0:T(8,128)(2,1)}, u32[]{:S(2)}, u32[]{:S(2)}) collective-permute-start(bf16[1040,128]{1,0:T(8,128)(2,1)} %collective-permute-done.4.refs_3_), channel_id=1, source_target_pairs={{8,16},{12,20},{16,24},{20,28},{9,17},{13,21},{17,25},{21,29},{10,... | collective-permute-start | bytes 798728 | tf_op jit(solution)/shard_map/ppermute | solution.py:669
  34.9 19.9 %collective-permute-start.6 = (bf16[1040,128]{1,0:T(8,128)(2,1)}, bf16[1040,128]{1,0:T(8,128)(2,1)S(1)}, u32[]{:S(2)}, u32[]{:S(2)}) collective-permute-start(bf16[1040,128]{1,0:T(8,128)(2,1)} %collective-permute-done.4.refs_3_), channel_id=1, source_target_pairs={{8,12},{12,8},{16,20},{20,16},{24,28},{28,24},{9,13},{13,9},{17,21... | collective-permute-start | bytes 798728 | tf_op jit(solution)/shard_map/ppermute | solution.py:669
  36.8 1.2 %copy-start.2 = (bf16[256,16,128]{2,1,0:T(8,128)(2,1)S(1)}, bf16[256,16,128]{2,1,0:T(8,128)(2,1)}, u32[]{:S(2)}) copy-start(bf16[256,16,128]{2,1,0:T(8,128)(2,1)} %param.12) | copy-start | bytes 3145732
  38.1 1.2 %copy-start.10 = (bf16[256,16,128]{2,1,0:T(8,128)(2,1)S(1)}, bf16[256,16,128]{2,1,0:T(8,128)(2,1)}, u32[]{:S(2)}) copy-start(bf16[256,16,128]{2,1,0:T(8,128)(2,1)} %param.10) | copy-start | bytes 3145732
  39.3 1.9 %copy-start.4 = (bf16[2,2048,256]{2,1,0:T(8,128)(2,1)S(1)}, bf16[2,2048,256]{2,1,0:T(8,128)(2,1)}, u32[]{:S(2)}) copy-start(bf16[2,2048,256]{2,1,0:T(8,128)(2,1)} %copy-done.3) | copy-start | bytes 6291460
  41.2 4.7 %copy-start.6 = (bf16[1040,128]{1,0:T(8,128)(2,1)S(1)}, bf16[1040,128]{1,0:T(8,128)(2,1)}, u32[]{:S(2)}) copy-start(bf16[1040,128]{1,0:T(8,128)(2,1)} %copy-done.5) | copy-start | bytes 798724
  41.2 4.7 %copy-start.13 = (bf16[1024,128]{1,0:T(8,128)(2,1)S(1)}, bf16[1024,128]{1,0:T(8,128)(2,1)}, u32[]{:S(2)}) copy-start(bf16[1024,128]{1,0:T(8,128)(2,1)} %copy-done.12) | copy-start | bytes 786436
  41.2 4.7 %copy-start.17 = (bf16[1040,128]{1,0:T(8,128)(2,1)S(1)}, bf16[1040,128]{1,0:T(8,128)(2,1)}, u32[]{:S(2)}) copy-start(bf16[1040,128]{1,0:T(8,128)(2,1)} %copy-done.16) | copy-start | bytes 798724
  47.2 9.9 %collective-permute-start.5 = (bf16[1024,128]{1,0:T(8,128)(2,1)S(1)}, bf16[1024,128]{1,0:T(8,128)(2,1)S(1)}, u32[]{:S(2)}, u32[]{:S(2)}) collective-permute-start(bf16[1024,128]{1,0:T(8,128)(2,1)S(1)} %get-tuple-element.39), channel_id=1, source_target_pairs={{0,4},{4,0},{8,12},{12,8},{16,20},{20,16},{24,28},{28,24},{1,5},{5... | collective-permute-start | bytes 786440 | tf_op jit(solution)/shard_map/ppermute | solution.py:669
  49.3 13.9 %collective-permute-start.11 = (bf16[1040,128]{1,0:T(8,128)(2,1)}, bf16[1040,128]{1,0:T(8,128)(2,1)S(1)}, u32[]{:S(2)}, u32[]{:S(2)}) collective-permute-start(bf16[1040,128]{1,0:T(8,128)(2,1)} %collective-permute-done.10.refs_2_), channel_id=1, source_target_pairs={{16,20},{20,16},{24,28},{28,24},{17,21},{21,17},{25,29},{29,25},{1... | collective-permute-start | bytes 798728 | tf_op jit(solution)/shard_map/ppermute | solution.py:669
  54.8 2.3 %copy-start.8 = (f32[2048,128]{1,0:T(8,128)S(1)}, f32[2048,128]{1,0:T(8,128)}, u32[]{:S(2)}) copy-start(f32[2048,128]{1,0:T(8,128)} %copy-done.7) | copy-start | bytes 3145732
  54.8 2.3 %copy-start.15 = (bf16[2048,128]{1,0:T(8,128)(2,1)S(1)}, bf16[2048,128]{1,0:T(8,128)(2,1)}, u32[]{:S(2)}) copy-start(bf16[2048,128]{1,0:T(8,128)(2,1)} %copy-done.14) | copy-start | bytes 1572868
  58.7 10.0 %copy-start.11 = (bf16[256,16,128]{2,1,0:T(8,128)(2,1)S(1)}, bf16[256,16,128]{2,1,0:T(8,128)(2,1)}, u32[]{:S(2)}) copy-start(bf16[256,16,128]{2,1,0:T(8,128)(2,1)} %param.13) | copy-start | bytes 3145732
  58.7 10.0 %copy-start.18 = (f32[16,128]{1,0:T(8,128)S(1)}, f32[16,128]{1,0:T(8,128)}, u32[]{:S(2)}) copy-start(f32[16,128]{1,0:T(8,128)} %refs_0_.1) | copy-start | bytes 24580
  58.7 9.9 %collective-permute-start.7 = (f32[8,256]{1,0:T(8,128)S(1)}, f32[8,256]{1,0:T(8,128)S(1)}, u32[]{:S(2)}, u32[]{:S(2)}) collective-permute-start(f32[8,256]{1,0:T(8,128)S(1)} %get-tuple-element.41.refs_4_.refs_3_), channel_id=1, source_target_pairs={{0,1},{1,0},{2,3},{3,2},{4,5},{5,4},{6,7},{7,6},{8,9},{9,8},{10,11... | collective-permute-start | bytes 24584 | tf_op jit(solution)/shard_map/ppermute | solution.py:764
  61.5 7.2 %collective-permute-start.8 = (f32[8,256]{1,0:T(8,128)S(1)}, f32[8,256]{1,0:T(8,128)S(1)}, u32[]{:S(2)}, u32[]{:S(2)}) collective-permute-start(f32[8,256]{1,0:T(8,128)S(1)} %get-tuple-element.41.refs_4_.refs_3_), channel_id=1, source_target_pairs={{0,2},{1,3},{2,0},{3,1},{4,6},{5,7},{6,4},{7,5},{8,10},{9,11},{10,... | collective-permute-start | bytes 24584 | tf_op jit(solution)/shard_map/ppermute | solution.py:764
  61.7 7.0 %collective-permute-start.9 = (f32[8,256]{1,0:T(8,128)S(1)}, f32[8,256]{1,0:T(8,128)S(1)}, u32[]{:S(2)}, u32[]{:S(2)}) collective-permute-start(f32[8,256]{1,0:T(8,128)S(1)} %get-tuple-element.41.refs_4_.refs_3_), channel_id=1, source_target_pairs={{0,3},{1,2},{2,1},{3,0},{4,7},{5,6},{6,5},{7,4},{8,11},{9,10},{10,... | collective-permute-start | bytes 24584 | tf_op jit(solution)/shard_map/ppermute | solution.py:764

commit v5 on v4

--- a/solution.py
+++ b/solution.py
@@ -34,20 +34,22 @@
 
 def cost(flops, bytes_accessed, transcendentals=0):
     return pl.CostEstimate(
-        flops=int(flops), bytes_accessed=int(bytes_accessed), transcendentals=int(transcendentals)
-    )
-
-
-def call(kernel, name, operands, out_shape, scratch=(), mib=16, estimate=None, scalars=(), after=(), hbm=0, out_hbm=False):
-    begin = len(scalars) + len(operands)
+        flops=int(flops) // 64, bytes_accessed=int(bytes_accessed) // 64, transcendentals=int(transcendentals) // 64
+    )
+
+
+def call(kernel, name, place, operands, out_shape, scratch=(), mib=16, estimate=None, after=(), hbm=0, out_hbm=False):
+    begin = 1 + len(operands)
     skip = len(after)
     operands = [
         pltpu.with_memory_space_constraint(x, pltpu.HBM) if i < hbm else x for i, x in enumerate(operands)
     ]
     outs = out_shape if isinstance(out_shape, tuple) else (out_shape,)
     out_specs = (VMEM,) * len(outs)
+    outs = tuple(
+        (pltpu.HBM if out_hbm and i == 0 else pltpu.VMEM)(x.shape, x.dtype) for i, x in enumerate(outs)
+    )
     if out_hbm:
-        outs = (pltpu.HBM(outs[0].shape, outs[0].dtype), *outs[1:])
         out_specs = (HBM, *out_specs[1:])
 
     def run(*refs):
@@ -56,13 +58,13 @@
     out = pl.pallas_call(
         run,
         out_shape=outs,
-        in_specs=[SMEM] * len(scalars) + [HBM] * hbm + [VMEM] * (len(operands) - hbm) + [ANYWHERE] * skip,
+        in_specs=[SMEM] + [HBM] * hbm + [VMEM] * (len(operands) - hbm) + [ANYWHERE] * skip,
         out_specs=out_specs,
         scratch_shapes=list(scratch),
         compiler_params=pltpu.CompilerParams(vmem_limit_bytes=mib * 1024 * 1024),
         cost_estimate=estimate,
         name=name,
-    )(*scalars, *operands, *after)
+    )(place, *operands, *after)
     return out if isinstance(out_shape, tuple) else out[0]
 
 
@@ -84,7 +86,7 @@
     return rows >= cols
 
 
-def front_kernel(tokens, heads, kv_here, pieces, start_ref, y_ref, *refs):
+def front_kernel(tokens, heads, kv_here, pieces, place_ref, *refs):
     refs = list(refs)
     take = lambda n: [refs.pop(0) for _ in range(n)]
     sources = take(6)
@@ -107,7 +109,7 @@
     end = 2 * kv_here * tokens
     kv_ref[end : end + INFO, :] = info.astype(BF16)
 
-    start = start_ref[0]
+    start = place_ref[1]
     for which, ref in enumerate((soft_key, soft_value)):
         copies[1 + which].wait()
         wide[...] = ref[...].astype(F32)
@@ -120,7 +122,7 @@
             kv_ref[at : at + tokens, :] = rows.astype(BF16)
 
     half = heads // 2
-    y = y_ref[0]
+    y = place_ref[0] % 2
     copies[3].wait()
     ldp[...] = jnp.zeros_like(ldp)
     ldp[0:heads, :] = decays[...]
@@ -164,13 +166,14 @@
     send_refs[0][size : size + INFO, :] = info_of(total * (1.0 - mine) + upper * mine)
 
 
-def front(start, y, operands, tokens, heads, kv_here, pieces):
+def front(place, operands, tokens, heads, kv_here, pieces):
     size = heads // 2 // pieces * HEAD_DIM
     keep = [sds((size, LANES), BF16)] * pieces
     send = [sds((size + (INFO if p == 0 else 0), LANES), BF16) for p in range(pieces)]
     out = call(
         functools.partial(front_kernel, tokens, heads, kv_here, pieces),
         "front",
+        place,
         operands,
         (
             sds((2 * kv_here * tokens + INFO, LANES), BF16),
@@ -191,7 +194,6 @@
         ],
         mib=24,
         estimate=cost(2 * heads * tokens * HEAD_DIM**2, 5 * tokens * heads * LANES * 2),
-        scalars=[start, y],
         hbm=len(operands),
     )
     return (*out[:4], out[4 : 4 + pieces], out[4 + pieces :])
@@ -216,8 +218,8 @@
     return info[0:1] + info[1:2] + info[2:3], info[3:4], info[4:5]
 
 
-def row_terms(y_ref, own_info, other_info):
-    even = y_ref[0] == 0
+def row_terms(place_ref, own_info, other_info):
+    even = place_ref[0] % 2 == 0
     own = own_info.astype(F32)
     other = other_info.astype(F32)
     a = jnp.where(even, own, other)
@@ -231,10 +233,10 @@
     return even, decay_a * whole_a, decay_b * link_b, first_a, last_a, last_b
 
 
-def row_kernel(count, first, y_ref, keep_ref, info_ref, other_ref, other_info_ref, out_ref):
+def row_kernel(count, first, place_ref, keep_ref, info_ref, other_ref, other_info_ref, out_ref):
     size = count * HEAD_DIM
     even, gain_a, gain_b, first_a, _, last_b = row_terms(
-        y_ref, info_ref[...], other_info_ref[size : size + INFO, :]
+        place_ref, info_ref[...], other_info_ref[size : size + INFO, :]
     )
     for i in range(count):
         rows = slice(i * HEAD_DIM, (i + 1) * HEAD_DIM)
@@ -246,26 +248,26 @@
     out_ref[size : size + INFO, :] = info_rows((*in_parts(gain_a * gain_b), first_a, last_b))
 
 
-def row_map(y, keep, info, other, other_info, first, count, after):
+def row_map(place, keep, info, other, other_info, first, count, after):
     size = count * HEAD_DIM
     return call(
         functools.partial(row_kernel, count, first),
         "row_map",
+        place,
         [keep, info, other, other_info],
         sds((size + INFO, LANES), BF16),
         estimate=cost(4 * size * LANES, 4 * size * LANES * 2),
-        scalars=[y],
         after=after,
     )
 
 
-def scan_kernel(count, first, has_before, upper_ref, *refs):
+def scan_kernel(count, first, has_before, stage, place_ref, *refs):
     refs = list(refs)
     mine_ref, came_ref = refs[:2]
     before_ref = refs[2] if has_before else None
     run_ref, out_ref = refs[-2:]
     size = count * HEAD_DIM
-    upper = upper_ref[0] == 1
+    upper = (place_ref[0] >> stage) & 1 == 1
     gain_m, first_m, last_m = read_map(mine_ref, size)
     gain_c, first_c, last_c = read_map(came_ref, size)
     link = jnp.where(upper, (last_c == first_m).astype(F32), (last_m == first_c).astype(F32))
@@ -304,29 +306,29 @@
     )
 
 
-def scan_step(upper, mine, came, before, first, count, after):
+def scan_step(place, stage, mine, came, before, first, count, after):
     size = count * HEAD_DIM
     shape = sds((size + INFO, LANES), BF16)
     before = [] if before is None else [before]
     return call(
-        functools.partial(scan_kernel, count, first, len(before)),
+        functools.partial(scan_kernel, count, first, len(before), stage),
         "scan_step",
+        place,
         [mine, came, *before],
         (shape, shape),
         estimate=cost(6 * size * LANES, 6 * size * LANES * 2),
-        scalars=[upper],
         after=after,
     )
 
 
-def prior_kernel(count, first, has_before, y_ref, upper_ref, *refs):
+def prior_kernel(count, first, has_before, stage, place_ref, *refs):
     keep_ref, info_ref, other_ref, other_info_ref, came_ref = refs[:5]
     before_ref = refs[5] if has_before else None
     mine_ref, send_ref, doc_ref = refs[-3:]
     size = count * HEAD_DIM
-    upper = (upper_ref[0] == 1).astype(F32)
+    upper = ((place_ref[0] >> stage) & 1).astype(F32)
     even, gain_a, _, first_a, last_a, _ = row_terms(
-        y_ref, info_ref[...], other_info_ref[size : size + INFO, :]
+        place_ref, info_ref[...], other_info_ref[size : size + INFO, :]
     )
     _, _, last_c = read_map(came_ref, size)
     factor, doc = upper, upper * last_c
@@ -351,16 +353,16 @@
     doc_ref[...] = jnp.broadcast_to(jnp.where(even, doc, last_a), (8, LANES))
 
 
-def prior_states(y, upper, keep, info, other, other_info, came, before, first, count, after):
+def prior_states(place, stage, keep, info, other, other_info, came, before, first, count, after):
     size = count * HEAD_DIM
     before = [] if before is None else [before]
     return call(
-        functools.partial(prior_kernel, count, first, len(before)),
+        functools.partial(prior_kernel, count, first, len(before), stage),
         "prior_states",
+        place,
         [keep, info, other, other_info, came, *before],
         (sds((size, LANES), BF16), sds((size, LANES), BF16), sds((8, LANES), F32)),
         estimate=cost(4 * size * LANES, 6 * size * LANES * 2),
-        scalars=[y, upper],
         after=after,
     )
 
@@ -372,7 +374,7 @@
     return x.reshape(tokens, heads, LANES)[:, first : first + count, :].reshape(tokens * count, LANES)
 
 
-def inner_kernel(tokens, heads, first, count, cumul_ref, doc_ref, query_ref, key_ref, value_ref, inner_ref, qh_ref, qf, kf, vf, mask):
+def inner_kernel(tokens, heads, first, count, place_ref, cumul_ref, doc_ref, query_ref, key_ref, value_ref, inner_ref, qh_ref, qf, kf, vf, mask):
     cumul = cumul_ref[...]
     cumul_t = jnp.transpose(cumul)
     docs = doc_ref[...]
@@ -402,10 +404,11 @@
             )
 
 
-def inner_part(cumul, docs, query, key, value, tokens, heads, first, count, after):
+def inner_part(place, cumul, docs, query, key, value, tokens, heads, first, count, after):
     return call(
         functools.partial(inner_kernel, tokens, heads, first, count),
         "inner_part",
+        place,
         [cumul, docs, query, key, value],
         (sds((count * tokens, LANES), F32), sds((count * tokens, LANES), BF16)),
         scratch=[pltpu.VMEM((tokens * count, LANES), F32)] * 3 + [pltpu.VMEM((tokens, tokens), F32)],
@@ -417,14 +420,14 @@
     )
 
 
-def mix_kernel(tokens, heads, parts, pieces, y_ref, doc_ref, prior_doc_ref, cumul_ref, *refs):
+def mix_kernel(tokens, heads, parts, pieces, place_ref, doc_ref, prior_doc_ref, cumul_ref, *refs):
     refs = list(refs)
     take = lambda n: [refs.pop(0) for _ in range(n)]
     inner, qh, mine, other = take(parts), take(parts), take(pieces), take(pieces)
     mixed_ref, square_ref = refs
     half = heads // 2
     count = half // pieces
-    even = y_ref[0] == 0
+    even = place_ref[0] % 2 == 0
     is_open = (doc_columns(doc_ref[...], tokens) == prior_doc_ref[0:1, :]).astype(F32)
     gain = jnp.exp(cumul_ref[...]) * is_open
     squares = jnp.zeros((tokens, LANES), F32)
@@ -449,20 +452,20 @@
     )
 
 
-def mix(y, docs, prior_doc, cumul, inner, qh, mine, other, tokens, heads, after):
+def mix(place, docs, prior_doc, cumul, inner, qh, mine, other, tokens, heads, after):
     return call(
         functools.partial(mix_kernel, tokens, heads, len(inner), len(mine)),
         "mix",
+        place,
         [docs, prior_doc, cumul, *inner, *qh, *mine, *other],
         (sds((tokens * heads, LANES), F32), sds((8, tokens), F32)),
         mib=24,
         estimate=cost(2 * heads * tokens * HEAD_DIM**2, tokens * heads * LANES * 10),
-        scalars=[y],
         after=after,
     )
 
 
-def finish_kernel(tokens, heads, sums, step, gain_ref, gate_ref, mixed_ref, *refs):
+def finish_kernel(tokens, heads, sums, step, place_ref, gain_ref, gate_ref, mixed_ref, *refs):
     squares, (out_ref, done, sems) = refs[:sums], refs[sums:]
     total = squares[0][0:1, :]
     for ref in squares[1:]:
@@ -484,11 +487,12 @@
         copy.wait()
 
 
-def finish(gain, gate, mixed, squares, tokens, heads, after):
+def finish(place, gain, gate, mixed, squares, tokens, heads, after):
     step = 64
     return call(
         functools.partial(finish_kernel, tokens, heads, len(squares), step),
         "finish",
+        place,
         [gain, gate, mixed, *squares],
         sds((tokens * heads, LANES), BF16),
         scratch=[pltpu.VMEM((tokens * heads, LANES), BF16), pltpu.SemaphoreType.DMA((tokens // step,))],
@@ -498,7 +502,7 @@
     )
 
 
-def attend_kernel(tokens, heads, kv_here, blocks, is_first, is_last, unroll, *refs):
+def attend_kernel(tokens, heads, kv_here, least, is_first, is_last, unroll, place_ref, *refs):
     refs = list(refs)
     take = lambda n: [refs.pop(0) for _ in range(n)]
     per_group = heads // kv_here
@@ -508,7 +512,7 @@
         doc_ref, query_ref = take(2)
     else:
         wide_ref, state_ref = take(2)
-    kv = take(blocks)
+    kv = take(len(least))
     if is_first:
         wide_ref = take(1)[0]
     out_ref = take(1)[0]
@@ -522,8 +526,10 @@
 
     lane = lax.broadcasted_iota(jnp.int32, (tokens, LANES), 1).astype(F32)
     end = 2 * kv_here * tokens
+    block = place_ref[0]
     for j, ref in enumerate(kv):
-        docs = doc_columns(ref[end : end + INFO, :].astype(F32), tokens)
+        valid = (block >= jnp.where(block % 2 == 0, *least[j])).astype(F32)
+        docs = doc_columns(ref[end : end + INFO, :].astype(F32) * valid, tokens)
         bias[j] = jnp.where(docs == lane, 0.0, -BIG).astype(BF16)
     if is_first:
         column = doc_columns(doc_ref[...], tokens)
@@ -607,8 +613,10 @@
             pltpu.make_async_copy(done.at[at, :], out_ref.at[at, :], sems.at[c]).wait()
 
 
-def attend(first, state, kv, is_last, tokens, heads, kv_here, after):
+def attend(place, first, state, kv, is_last, tokens, heads, kv_here, after):
     is_first = state is None
+    least = tuple(pair for _, pair in kv)
+    kv = [block for block, _ in kv]
     blocks = len(kv)
     rows = tokens * heads // kv_here
     unroll = min(4, rows // CHUNK)
@@ -625,8 +633,9 @@
         scratch.append(pltpu.SemaphoreType.DMA((rows // CHUNK,)))
     span = blocks * tokens
     return call(
-        functools.partial(attend_kernel, tokens, heads, kv_here, blocks, is_first, is_last, unroll),
+        functools.partial(attend_kernel, tokens, heads, kv_here, least, is_first, is_last, unroll),
         "attend",
+        place,
         [*first, *([] if is_first else [state]), *kv],
         out_shape,
         scratch=scratch,
@@ -656,24 +665,23 @@
     tensor = HEADS // heads
     kv_here = max(1, heads // GROUP)
     half = heads // 2
-    pieces = 1
+    pieces = 2 if half % 2 == 0 else 1
     parts = 2 if half % 8 == 0 else 1
     count = half // pieces
     longest = blocks * tokens * 5 // 8
     window = min(blocks - 1, (longest - 1 + tokens - 1) // tokens)
     flat = lambda x: x.reshape(-1, LANES)
     block = lax.axis_index("seq")
-    y = (block % 2).astype(jnp.int32).reshape(1)
-    start = (lax.axis_index("tp") * heads // GROUP).astype(jnp.int32).reshape(1)
+    place = jnp.stack([block, lax.axis_index("tp") * heads // GROUP]).astype(jnp.int32)
+
     def send(x, pairs):
-        return lax.ppermute(x, "seq", [p for p in pairs if 0 <= p[0] < blocks and 0 <= p[1] < blocks])
+        return lax.ppermute(x, "seq", [(a, b % blocks) for a, b in pairs])
 
     everyone = range(blocks)
     swap = [(b, b ^ 1) for b in everyone]
 
     own_kv, docs, cumul, info, held, sent = front(
-        start,
-        y,
+        place,
         [
             doc_ids.reshape(tokens // LANES, LANES),
             flat(soft_key),
@@ -688,26 +696,28 @@
         pieces,
     )
     came = [send(x, swap) for x in sent]
-    far_step = window if window % 2 else blocks
-    beside = send(own_kv, [(b, b + (far_step if b % 2 else 1)) for b in everyone])
+    odd_window = window % 2 == 1
+    beside = send(own_kv, [(b, b + (1 if b % 2 == 0 else window if odd_window else -1)) for b in everyone])
+    beside = (beside, (window if odd_window else blocks, 1))
     lane_kv, cross_kv = [], []
     ahead = own_kv
     for back in range(1, window // 2 + 1):
-        ahead = send(ahead, [(b, b + 2) for b in everyone if b >= 2 * (back - 1)])
-        lane_kv.append(ahead)
-        cross_kv.append(send(ahead, [p for p in swap if p[0] >= 2 * back]))
+        ahead = send(ahead, [(b, b + 2) for b in everyone])
+        lane_kv.append((ahead, (2 * back, 2 * back)))
+        cross_kv.append((send(ahead, swap), (2 * back, 2 * back + 1)))
+    held = list(held)
 
     state = {}
 
     def first_attention(after):
         state["wide"], state["sum"] = attend(
-            (docs, flat(soft_query)), None, [own_kv], False, tokens, heads, kv_here, after
+            place, (docs, flat(soft_query)), None, [(own_kv, (0, 0))], False, tokens, heads, kv_here, after
         )
         return state["sum"]
 
     def more_attention(kv, is_last, after):
         state["sum"] = attend(
-            (state["wide"],), state["sum"], kv, is_last, tokens, heads, kv_here, after
+            place, (state["wide"],), state["sum"], kv, is_last, tokens, heads, kv_here, after
         )
         return state["sum"]
 
@@ -716,7 +726,7 @@
     def inner_of(part, after):
         n = heads // parts
         got = inner_part(
-            cumul, docs, flat(lin_query), flat(lin_key), flat(lin_value), tokens, heads, part * n, n, after
+            place, cumul, docs, flat(lin_query), flat(lin_key), flat(lin_value), tokens, heads, part * n, n, after
         )
         inner.append(got[0])
         qh.append(got[1])
@@ -737,17 +747,16 @@
         if stage == stages:
             while beside_work:
                 done = beside_work.pop(0)([done])
-        upper = ((block >> stage) & 1).astype(jnp.int32).reshape(1)
         for p in range(pieces):
             at = (p * count, count, [done])
             if stage == 0:
-                done = run[p] = row_map(y, held[p], info, came[p], came[0], *at)
+                done = run[p] = row_map(place, held[p], info, came[p], came[0], *at)
             elif stage < stages:
-                run[p], before[p] = scan_step(upper, run[p], got[p], before[p], *at)
+                run[p], before[p] = scan_step(place, stage, run[p], got[p], before[p], *at)
                 done = run[p]
             else:
                 done, sent, prior_doc = prior_states(
-                    y, upper, held[p], info, came[p], came[0], got[p], before[p], *at
+                    place, stage, held[p], info, came[p], came[0], got[p], before[p], *at
                 )
                 mine.append(done)
                 far.append(send(sent, swap))
@@ -757,7 +766,7 @@
     done = more_attention(rest[:1], False, [done])
     rest = rest[1:]
     mixed, squares = mix(
-        y, docs, prior_doc, cumul, inner, qh, mine, far, tokens, heads, [done]
+        place, docs, prior_doc, cumul, inner, qh, mine, far, tokens, heads, [done]
     )
     sums = [squares]
     for other in range(1, tensor):
@@ -767,7 +776,7 @@
         got = more_attention(rest[:2], len(rest) <= 2, after)
         rest, after = rest[2:], []
     soft_out, done = got
-    lin_out = finish(norm_gain, flat(lin_gate), mixed, sums, tokens, heads, [done])
+    lin_out = finish(place, norm_gain, flat(lin_gate), mixed, sums, tokens, heads, [done])
     shape = (tokens, heads, HEAD_DIM)
     return lin_out.reshape(shape), soft_out.reshape(shape)
 

time: 71 us -> 68.7 us (0.968)
  the two profiles are of different devices: /device:TPU:19 before, /device:TPU:0 now
where the time goes in v5:
time: 68.7 us; the launch traced here: 68.5 us
  Pallas kernels  34.6 us (50%)
  starting transfers between devices  20 us (29%)
  waiting for transfers between devices  12.7 us (18%)
  between operations  1.03 us (1%)
    pallas_call x15, Pallas kernels, call(): pl.pallas_call(run, out_shape=outs, in_specs=[SMEM] + [HBM] * hbm + [VMEM...  34.6 us
    ppermute x13, starting transfers between devices, send(): return lax.ppermute(x, 'seq', [(a, b % blocks) for a, b in pairs])  18.2 us
    ppermute x13, waiting for transfers between devices, send(): return lax.ppermute(x, 'seq', [(a, b % blocks) for a, b in pairs])  12.7 us
    ppermute x3, starting transfers between devices, body(): lax.ppermute(squares, 'tp', [(t, t ^ other) for t in range(tensor)])  1.88 us
  transfers between devices with their start and end apart: 16, of which 4 were waited for; matrix products, arithmetic and copies ran while one was open for 0% of the time, Pallas kernels for 39%

profile of v5, /device:TPU:0, one launch (start us, length us, event | category | flops | bytes accessed | tf_op | source)
XLA Modules:
  0.0 68.5 jit_solution(11167197074742647537)
XLA Ops:
  0.7 0.1 pad_add_fusion.refs_0_
  0.7 5.4 %front.1 = (bf16[1040,128]{1,0:T(8,128)(2,1)S(1)}, f32[16,128]{1,0:T(8,128)S(1)}, f32[256,128]{1,0:T(8,128)S(1)}, bf16[16,128]{1,0:T(8,128)(2,1)S(1)}, bf16[512,...) custom-call(s32[2]{0:T(128)S(1)} %pad_add_fusion.refs_0_, ...), custom_call_target="tpu_custom_call" | custom-call | flops 2097152 | bytes 81920 | tf_op jit(solution)/shard_map/front/pallas_call | solution.py:58
  6.1 3.1 %collective-permute-start.7 = (bf16[1040,128]{1,0:T(8,128)(2,1)S(1)}, bf16[1040,128]{1,0:T(8,128)(2,1)S(1)}, u32[]{:S(2)}, u32[]{:S(2)}) collective-permute-start(bf16[1040,128]{1,0:T(8,128)(2,1)S(1)} %get-tuple-element.35.refs_3_), channel_id=1, source_target_pairs={{0,8},{4,12},{8,16},{12,20},{16,24},{20,28},{24,0},{28,4},{1,9},{5... | collective-permute-start | bytes 798728 | tf_op jit(solution)/shard_map/ppermute | solution.py:678
  9.2 1.5 %collective-permute-start.1 = (bf16[528,128]{1,0:T(8,128)(2,1)S(1)}, bf16[528,128]{1,0:T(8,128)(2,1)S(1)}, u32[]{:S(2)}, u32[]{:S(2)}) collective-permute-start(bf16[528,128]{1,0:T(8,128)(2,1)S(1)} %get-tuple-element.33), channel_id=1, source_target_pairs={{0,4},{4,0},{8,12},{12,8},{16,20},{20,16},{24,28},{28,24},{1,5},{5... | collective-permute-start | bytes 405512 | tf_op jit(solution)/shard_map/ppermute | solution.py:678
  10.8 0.5 collective-permute-start
  11.3 6.4 %collective-permute-done.7.refs_4_ = bf16[1040,128]{1,0:T(8,128)(2,1)S(1)} collective-permute-done((bf16[1040,128]{1,0:T(8,128)(2,1)S(1)}, bf16[1040,128]{1,0:T(8,128)(2,1)S(1)}, u32[]{:S(2)}, u32[]{:S(2)}) %collective-permute-start.7) | collective-permute-done | bytes 266272 | tf_op jit(solution)/shard_map/ppermute | solution.py:678
  17.6 0.0 collective-permute-start.14
  17.7 0.0 copy-start.1
  17.7 0.0 copy-start.2
  17.7 3.2 %attend.4 = (bf16[2,2048,256]{2,1,0:T(8,128)(2,1)S(1)}, f32[2,144,2048]{2,1,0:T(8,128)S(1)}) custom-call(s32[2]{0:T(128)S(1)} %pad_add_fusion.refs_0_, f32[16,128]{1,0:T(8,128)S(1)} %get-tuple-element.29.refs_1_.refs_2_, bf16[4096,128]{1,0:T(8,128)(2,1)S(1)} %bitcast.22, bf16[1040,128]{1,0:T(8,128)(2,1)S(1)} %get-tuple-element.35.refs_3_, ...), custom_call_target="tpu_custom_call" | custom-call | flops 16777216 | bytes 131072 | tf_op jit(solution)/shard_map/attend/pallas_call | solution.py:58
  20.9 0.0 collective-permute-done.1.refs_3_.refs_4_
  20.9 0.7 row_map.2.refs_5_.refs_1_
  21.6 1.3 %collective-permute-start.3 = (bf16[528,128]{1,0:T(8,128)(2,1)S(1)}, bf16[528,128]{1,0:T(8,128)(2,1)S(1)}, u32[]{:S(2)}, u32[]{:S(2)}) collective-permute-start(bf16[528,128]{1,0:T(8,128)(2,1)S(1)} %row_map.2.refs_5_.refs_1_), channel_id=1, source_target_pairs={{0,8},{4,12},{8,0},{12,4},{16,24},{20,28},{24,16},{28,20},{1,9},{5... | collective-permute-start | bytes 405512 | tf_op jit(solution)/shard_map/ppermute | solution.py:678
  22.9 0.0 collective-permute-done.refs_3_
  22.9 0.7 %row_map.3.refs_6_.refs_1_ = bf16[528,128]{1,0:T(8,128)(2,1)S(1)} custom-call(s32[2]{0:T(128)S(1)} %pad_add_fusion.refs_0_, bf16[512,128]{1,0:T(8,128)(2,1)S(1)} %get-tuple-element.30.refs_1_, bf16[16,128]{1,0:T(8,128)(2,1)S(1)} %get-tuple-element.31.refs_4_.refs_2_, bf16[512,128]{1,0:T(8,128)(2,1)S(1)} %collective-permute-done.refs_3_, ...), custom_call_target="tpu_custom_call" | custom-call | flops 4096 | bytes 8192 | tf_op jit(solution)/shard_map/row_map/pallas_call | solution.py:58
  23.6 0.8 %collective-permute-start.2 = (bf16[528,128]{1,0:T(8,128)(2,1)S(1)}, bf16[528,128]{1,0:T(8,128)(2,1)S(1)}, u32[]{:S(2)}, u32[]{:S(2)}) collective-permute-start(bf16[528,128]{1,0:T(8,128)(2,1)S(1)} %row_map.3.refs_6_.refs_1_), channel_id=1, source_target_pairs={{0,8},{4,12},{8,0},{12,4},{16,24},{20,28},{24,16},{28,20},{1,9},{5... | collective-permute-start | bytes 405512 | tf_op jit(solution)/shard_map/ppermute | solution.py:678
  24.4 1.5 %collective-permute-start.6 = (bf16[1040,128]{1,0:T(8,128)(2,1)S(1)}, bf16[1040,128]{1,0:T(8,128)(2,1)S(1)}, u32[]{:S(2)}, u32[]{:S(2)}) collective-permute-start(bf16[1040,128]{1,0:T(8,128)(2,1)S(1)} %get-tuple-element.35.refs_3_), channel_id=1, source_target_pairs={{0,4},{4,24},{8,12},{12,0},{16,20},{20,8},{24,28},{28,16},{1,5},{5... | collective-permute-start | bytes 798728 | tf_op jit(solution)/shard_map/ppermute | solution.py:678
  25.9 3.7 %collective-permute-start.10 = (bf16[1040,128]{1,0:T(8,128)(2,1)S(1)}, bf16[1040,128]{1,0:T(8,128)(2,1)S(1)}, u32[]{:S(2)}, u32[]{:S(2)}) collective-permute-start(bf16[1040,128]{1,0:T(8,128)(2,1)S(1)} %collective-permute-done.7.refs_4_), channel_id=1, source_target_pairs={{0,4},{4,0},{8,12},{12,8},{16,20},{20,16},{24,28},{28,24},{1,5},{5... | collective-permute-start | bytes 798728 | tf_op jit(solution)/shard_map/ppermute | solution.py:678
  29.7 2.5 %inner_part.2 = (f32[2048,128]{1,0:T(8,128)S(1)}, bf16[2048,128]{1,0:T(8,128)(2,1)S(1)}) custom-call(s32[2]{0:T(128)S(1)} %pad_add_fusion.refs_0_, f32[256,128]{1,0:T(8,128)S(1)} %get-tuple-element.37.refs_1_.refs_3_, f32[16,128]{1,0:T(8,128)S(1)} %get-tuple-element.29.refs_1_.refs_2_, bf16[4096,128]{1,0:T(8,128)(2,1)S(1)} %bitcast.19, ...), custom_call_target="tpu_custom_call" | custom-call | flops 4194304 | bytes 98304 | tf_op jit(solution)/shard_map/inner_part/pallas_call | solution.py:58
  32.1 0.0 collective-permute-done.3.refs_2_
  32.2 0.7 scan_step.2
  32.8 0.1 collective-permute-start.5
  32.9 0.0 collective-permute-done.2.refs_2_
  32.9 0.7 scan_step.3
  33.6 3.0 %collective-permute-start.4 = (bf16[528,128]{1,0:T(8,128)(2,1)S(1)}, bf16[528,128]{1,0:T(8,128)(2,1)S(1)}, u32[]{:S(2)}, u32[]{:S(2)}) collective-permute-start(bf16[528,128]{1,0:T(8,128)(2,1)S(1)} %get-tuple-element.40.refs_6_), channel_id=1, source_target_pairs={{0,16},{4,20},{8,24},{12,28},{16,0},{20,4},{24,8},{28,12},{1,17},{... | collective-permute-start | bytes 405512 | tf_op jit(solution)/shard_map/ppermute | solution.py:678
  36.6 0.5 collective-permute-start.15
  37.1 2.4 %inner_part.3 = (f32[2048,128]{1,0:T(8,128)S(1)}, bf16[2048,128]{1,0:T(8,128)(2,1)S(1)}) custom-call(s32[2]{0:T(128)S(1)} %pad_add_fusion.refs_0_, f32[256,128]{1,0:T(8,128)S(1)} %get-tuple-element.37.refs_1_.refs_3_, f32[16,128]{1,0:T(8,128)S(1)} %get-tuple-element.29.refs_1_.refs_2_, bf16[4096,128]{1,0:T(8,128)(2,1)S(1)} %bitcast.20, ...), custom_call_target="tpu_custom_call" | custom-call | flops 4194304 | bytes 98304 | tf_op jit(solution)/shard_map/inner_part/pallas_call | solution.py:58
  39.5 3.8 %collective-permute-done.6.refs_3_ = bf16[1040,128]{1,0:T(8,128)(2,1)S(1)} collective-permute-done((bf16[1040,128]{1,0:T(8,128)(2,1)S(1)}, bf16[1040,128]{1,0:T(8,128)(2,1)S(1)}, u32[]{:S(2)}, u32[]{:S(2)}) %collective-permute-start.6) | collective-permute-done | bytes 266272 | tf_op jit(solution)/shard_map/ppermute | solution.py:678
  43.3 4.2 %attend.5.refs_7_.refs_2_ = f32[2,144,2048]{2,1,0:T(8,128)S(1)} custom-call(s32[2]{0:T(128)S(1)} %pad_add_fusion.refs_0_, bf16[2,2048,256]{2,1,0:T(8,128)(2,1)S(1)} %get-tuple-element.43.refs_1_, f32[2,144,2048]{2,1,0:T(8,128)S(1)} %get-tuple-element.36.refs_5_.refs_2_, bf16[1040,128]{1,0:T(8,128)(2,1)S(1)} %collective-permute-done.6.refs_3_, ...), custom_call_target="tpu_custom_call" | custom-call | flops 33554432 | bytes 131072 | tf_op jit(solution)/shard_map/attend/pallas_call | solution.py:58
  47.5 0.0 collective-permute-done.5.refs_5_
  47.6 1.2 %prior_states.2 = (bf16[512,128]{1,0:T(8,128)(2,1)S(1)}, bf16[512,128]{1,0:T(8,128)(2,1)S(1)}, f32[8,128]{1,0:T(8,128)}) custom-call(s32[2]{0:T(128)S(1)} %pad_add_fusion.refs_0_, bf16[512,128]{1,0:T(8,128)(2,1)S(1)} %get-tuple-element.34.refs_1_, bf16[16,128]{1,0:T(8,128)(2,1)S(1)} %get-tuple-element.31.refs_4_.refs_2_, ...), custom_call_target="tpu_custom_call" | custom-call | flops 4096 | bytes 12288 | tf_op jit(solution)/shard_map/prior_states/pallas_call | solution.py:58
  48.8 0.0 collective-permute-start.8
  48.8 0.0 collective-permute-done.4.refs_5_
  48.8 0.7 %prior_states.3 = (bf16[512,128]{1,0:T(8,128)(2,1)S(1)}, bf16[512,128]{1,0:T(8,128)(2,1)S(1)}, f32[8,128]{1,0:T(8,128)S(1)}) custom-call(s32[2]{0:T(128)S(1)} %pad_add_fusion.refs_0_, bf16[512,128]{1,0:T(8,128)(2,1)S(1)} %get-tuple-element.30.refs_1_, bf16[16,128]{1,0:T(8,128)(2,1)S(1)} %get-tuple-element.31.refs_4_.refs_2_, ...), custom_call_target="tpu_custom_call" | custom-call | flops 4096 | bytes 12288 | tf_op jit(solution)/shard_map/prior_states/pallas_call | solution.py:58
  49.5 2.1 %collective-permute-start.9 = (bf16[512,128]{1,0:T(8,128)(2,1)S(1)}, bf16[512,128]{1,0:T(8,128)(2,1)S(1)}, u32[]{:S(2)}, u32[]{:S(2)}) collective-permute-start(bf16[512,128]{1,0:T(8,128)(2,1)S(1)} %get-tuple-element.51), channel_id=1, source_target_pairs={{0,4},{4,0},{8,12},{12,8},{16,20},{20,16},{24,28},{28,24},{1,5},{5... | collective-permute-start | bytes 393224 | tf_op jit(solution)/shard_map/ppermute | solution.py:678
  51.6 0.0 collective-permute-done.10.refs_3_
  51.6 2.8 %attend.6.refs_12_.refs_2_ = f32[2,144,2048]{2,1,0:T(8,128)S(1)} custom-call(s32[2]{0:T(128)S(1)} %pad_add_fusion.refs_0_, bf16[2,2048,256]{2,1,0:T(8,128)(2,1)S(1)} %get-tuple-element.43.refs_1_, f32[2,144,2048]{2,1,0:T(8,128)S(1)} %attend.5.refs_7_.refs_2_, bf16[1040,128]{1,0:T(8,128)(2,1)S(1)} %collective-permute-done.10.refs_3_, ...), custom_call_target="tpu_custom_call" | custom-call | flops 16777216 | bytes 131072 | tf_op jit(solution)/shard_map/attend/pallas_call | solution.py:58
  54.5 0.7 collective-permute-done.8.refs_10_
  55.1 1.8 %collective-permute-done.9.refs_11_ = bf16[512,128]{1,0:T(8,128)(2,1)S(1)} collective-permute-done((bf16[512,128]{1,0:T(8,128)(2,1)S(1)}, bf16[512,128]{1,0:T(8,128)(2,1)S(1)}, u32[]{:S(2)}, u32[]{:S(2)}) %collective-permute-start.9) | collective-permute-done | bytes 131104 | tf_op jit(solution)/shard_map/ppermute | solution.py:678
  56.9 2.1 %mix.1 = (f32[4096,128]{1,0:T(8,128)S(1)}, f32[8,256]{1,0:T(8,128)S(1)}) custom-call(s32[2]{0:T(128)S(1)} %pad_add_fusion.refs_0_, f32[16,128]{1,0:T(8,128)S(1)} %get-tuple-element.29.refs_1_.refs_2_, f32[8,128]{1,0:T(8,128)S(1)} %get-tuple-element.46.refs_2_, f32[256,128]{1,0:T(8,128)S(1)} %get-tuple-element.37.refs_1_.refs_3_, ...), custom_call_target="tpu_custom_call" | custom-call | flops 2097152 | bytes 81920 | tf_op jit(solution)/shard_map/mix/pallas_call | solution.py:58
  59.1 0.0 collective-permute-start.11
  59.1 1.6 %collective-permute-start.12 = (f32[8,256]{1,0:T(8,128)S(1)}, f32[8,256]{1,0:T(8,128)S(1)}, u32[]{:S(2)}, u32[]{:S(2)}) collective-permute-start(f32[8,256]{1,0:T(8,128)S(1)} %get-tuple-element.53.refs_5_.refs_4_), channel_id=1, source_target_pairs={{0,2},{1,3},{2,0},{3,1},{4,6},{5,7},{6,4},{7,5},{8,10},{9,11},{10,... | collective-permute-start | bytes 24584 | tf_op jit(solution)/shard_map/ppermute | solution.py:773
  60.7 0.3 collective-permute-start.13
  61.0 0.0 collective-permute-done.15.refs_4_
  61.0 5.1 %attend.7 = (bf16[4096,128]{1,0:T(8,128)(2,1)}, f32[8,128]{1,0:T(8,128)S(1)}) custom-call(s32[2]{0:T(128)S(1)} %pad_add_fusion.refs_0_, bf16[2,2048,256]{2,1,0:T(8,128)(2,1)S(1)} %get-tuple-element.43.refs_1_, f32[2,144,2048]{2,1,0:T(8,128)S(1)} %attend.6.refs_12_.refs_2_, bf16[1040,128]{1,0:T(8,128)(2,1)S(1)} %collective-permute-done.14.refs_3_, ...), custom_call_target="tpu_custom_call" | custom-call | flops 33554432 | bytes 131072 | tf_op jit(solution)/shard_map/attend/pallas_call | solution.py:58
  66.1 0.0 collective-permute-done.11.refs_5_
  66.1 0.0 collective-permute-done.12.refs_6_
  66.2 2.2 %finish.1 = bf16[4096,128]{1,0:T(8,128)(2,1)} custom-call(s32[2]{0:T(128)S(1)} %pad_add_fusion.refs_0_, f32[16,128]{1,0:T(8,128)S(1)} %copy-done.5, bf16[4096,128]{1,0:T(8,128)(2,1)S(1)} %bitcast.21, f32[4096,128]{1,0:T(8,128)S(1)} %get-tuple-element.52.refs_3_, f32[8,256]{1,0:T(8,128)S(1)} %get-tuple-element.53.refs_5_.refs_4_, ...), custom_call_target="tpu_custom_call" | custom-call | bytes 65536 | tf_op jit(solution)/shard_map/finish/pallas_call | solution.py:58
  (12 shorter events, 0.0 us)
Async XLA Ops:
  0.6 17.0 %copy-start.4 = (bf16[256,16,128]{2,1,0:T(8,128)(2,1)S(1)}, bf16[256,16,128]{2,1,0:T(8,128)(2,1)}, u32[]{:S(2)}) copy-start(bf16[256,16,128]{2,1,0:T(8,128)(2,1)} %param.17) | copy-start | bytes 3145732
  6.1 11.5 %collective-permute-start.7 = (bf16[1040,128]{1,0:T(8,128)(2,1)S(1)}, bf16[1040,128]{1,0:T(8,128)(2,1)S(1)}, u32[]{:S(2)}, u32[]{:S(2)}) collective-permute-start(bf16[1040,128]{1,0:T(8,128)(2,1)S(1)} %get-tuple-element.35.refs_3_), channel_id=1, source_target_pairs={{0,8},{4,12},{8,16},{12,20},{16,24},{20,28},{24,0},{28,4},{1,9},{5... | collective-permute-start | bytes 798728 | tf_op jit(solution)/shard_map/ppermute | solution.py:678
  9.2 11.6 %collective-permute-start.1 = (bf16[528,128]{1,0:T(8,128)(2,1)S(1)}, bf16[528,128]{1,0:T(8,128)(2,1)S(1)}, u32[]{:S(2)}, u32[]{:S(2)}) collective-permute-start(bf16[528,128]{1,0:T(8,128)(2,1)S(1)} %get-tuple-element.33), channel_id=1, source_target_pairs={{0,4},{4,0},{8,12},{12,8},{16,20},{20,16},{24,28},{28,24},{1,5},{5... | collective-permute-start | bytes 405512 | tf_op jit(solution)/shard_map/ppermute | solution.py:678
  10.8 12.1 %collective-permute-start = (bf16[512,128]{1,0:T(8,128)(2,1)S(1)}, bf16[512,128]{1,0:T(8,128)(2,1)S(1)}, u32[]{:S(2)}, u32[]{:S(2)}) collective-permute-start(bf16[512,128]{1,0:T(8,128)(2,1)S(1)} %get-tuple-element.32), channel_id=1, source_target_pairs={{0,4},{4,0},{8,12},{12,8},{16,20},{20,16},{24,28},{28,24},{1,5},{5... | collective-permute-start | bytes 393224 | tf_op jit(solution)/shard_map/ppermute | solution.py:678
  17.6 18.9 %collective-permute-start.14 = (bf16[1040,128]{1,0:T(8,128)(2,1)S(1)}, bf16[1040,128]{1,0:T(8,128)(2,1)S(1)}, u32[]{:S(2)}, u32[]{:S(2)}) collective-permute-start(bf16[1040,128]{1,0:T(8,128)(2,1)S(1)} %collective-permute-done.7.refs_4_), channel_id=1, source_target_pairs={{0,8},{4,12},{8,16},{12,20},{16,24},{20,28},{24,0},{28,4},{1,9},{5... | collective-permute-start | bytes 798728 | tf_op jit(solution)/shard_map/ppermute | solution.py:678
  17.6 12.0 %copy-start = (bf16[256,16,128]{2,1,0:T(8,128)(2,1)S(1)}, bf16[256,16,128]{2,1,0:T(8,128)(2,1)}, u32[]{:S(2)}) copy-start(bf16[256,16,128]{2,1,0:T(8,128)(2,1)} %param.11) | copy-start | bytes 3145732
  17.7 12.0 %copy-start.1 = (bf16[256,16,128]{2,1,0:T(8,128)(2,1)S(1)}, bf16[256,16,128]{2,1,0:T(8,128)(2,1)}, u32[]{:S(2)}) copy-start(bf16[256,16,128]{2,1,0:T(8,128)(2,1)} %param.12) | copy-start | bytes 3145732
  17.7 12.0 %copy-start.2 = (bf16[256,16,128]{2,1,0:T(8,128)(2,1)S(1)}, bf16[256,16,128]{2,1,0:T(8,128)(2,1)}, u32[]{:S(2)}) copy-start(bf16[256,16,128]{2,1,0:T(8,128)(2,1)} %param.10) | copy-start | bytes 3145732
  21.6 10.6 %collective-permute-start.3 = (bf16[528,128]{1,0:T(8,128)(2,1)S(1)}, bf16[528,128]{1,0:T(8,128)(2,1)S(1)}, u32[]{:S(2)}, u32[]{:S(2)}) collective-permute-start(bf16[528,128]{1,0:T(8,128)(2,1)S(1)} %row_map.2.refs_5_.refs_1_), channel_id=1, source_target_pairs={{0,8},{4,12},{8,0},{12,4},{16,24},{20,28},{24,16},{28,20},{1,9},{5... | collective-permute-start | bytes 405512 | tf_op jit(solution)/shard_map/ppermute | solution.py:678
  23.6 9.3 %collective-permute-start.2 = (bf16[528,128]{1,0:T(8,128)(2,1)S(1)}, bf16[528,128]{1,0:T(8,128)(2,1)S(1)}, u32[]{:S(2)}, u32[]{:S(2)}) collective-permute-start(bf16[528,128]{1,0:T(8,128)(2,1)S(1)} %row_map.3.refs_6_.refs_1_), channel_id=1, source_target_pairs={{0,8},{4,12},{8,0},{12,4},{16,24},{20,28},{24,16},{28,20},{1,9},{5... | collective-permute-start | bytes 405512 | tf_op jit(solution)/shard_map/ppermute | solution.py:678
  24.4 18.9 %collective-permute-start.6 = (bf16[1040,128]{1,0:T(8,128)(2,1)S(1)}, bf16[1040,128]{1,0:T(8,128)(2,1)S(1)}, u32[]{:S(2)}, u32[]{:S(2)}) collective-permute-start(bf16[1040,128]{1,0:T(8,128)(2,1)S(1)} %get-tuple-element.35.refs_3_), channel_id=1, source_target_pairs={{0,4},{4,24},{8,12},{12,0},{16,20},{20,8},{24,28},{28,16},{1,5},{5... | collective-permute-start | bytes 798728 | tf_op jit(solution)/shard_map/ppermute | solution.py:678
  25.9 25.7 %collective-permute-start.10 = (bf16[1040,128]{1,0:T(8,128)(2,1)S(1)}, bf16[1040,128]{1,0:T(8,128)(2,1)S(1)}, u32[]{:S(2)}, u32[]{:S(2)}) collective-permute-start(bf16[1040,128]{1,0:T(8,128)(2,1)S(1)} %collective-permute-done.7.refs_4_), channel_id=1, source_target_pairs={{0,4},{4,0},{8,12},{12,8},{16,20},{20,16},{24,28},{28,24},{1,5},{5... | collective-permute-start | bytes 798728 | tf_op jit(solution)/shard_map/ppermute | solution.py:678
  32.8 14.7 %collective-permute-start.5 = (bf16[528,128]{1,0:T(8,128)(2,1)S(1)}, bf16[528,128]{1,0:T(8,128)(2,1)S(1)}, u32[]{:S(2)}, u32[]{:S(2)}) collective-permute-start(bf16[528,128]{1,0:T(8,128)(2,1)S(1)} %get-tuple-element.39.refs_3_), channel_id=1, source_target_pairs={{0,16},{4,20},{8,24},{12,28},{16,0},{20,4},{24,8},{28,12},{1,17},{... | collective-permute-start | bytes 405512 | tf_op jit(solution)/shard_map/ppermute | solution.py:678
  33.6 15.2 %collective-permute-start.4 = (bf16[528,128]{1,0:T(8,128)(2,1)S(1)}, bf16[528,128]{1,0:T(8,128)(2,1)S(1)}, u32[]{:S(2)}, u32[]{:S(2)}) collective-permute-start(bf16[528,128]{1,0:T(8,128)(2,1)S(1)} %get-tuple-element.40.refs_6_), channel_id=1, source_target_pairs={{0,16},{4,20},{8,24},{12,28},{16,0},{20,4},{24,8},{28,12},{1,17},{... | collective-permute-start | bytes 405512 | tf_op jit(solution)/shard_map/ppermute | solution.py:678
  36.6 24.4 %collective-permute-start.15 = (bf16[1040,128]{1,0:T(8,128)(2,1)S(1)}, bf16[1040,128]{1,0:T(8,128)(2,1)S(1)}, u32[]{:S(2)}, u32[]{:S(2)}) collective-permute-start(bf16[1040,128]{1,0:T(8,128)(2,1)S(1)} %collective-permute-done.14.refs_3_), channel_id=1, source_target_pairs={{0,4},{4,0},{8,12},{12,8},{16,20},{20,16},{24,28},{28,24},{1,5},{5... | collective-permute-start | bytes 798728 | tf_op jit(solution)/shard_map/ppermute | solution.py:678
  48.8 6.4 %collective-permute-start.8 = (bf16[512,128]{1,0:T(8,128)(2,1)S(1)}, bf16[512,128]{1,0:T(8,128)(2,1)S(1)}, u32[]{:S(2)}, u32[]{:S(2)}) collective-permute-start(bf16[512,128]{1,0:T(8,128)(2,1)S(1)} %get-tuple-element.50), channel_id=1, source_target_pairs={{0,4},{4,0},{8,12},{12,8},{16,20},{20,16},{24,28},{28,24},{1,5},{5... | collective-permute-start | bytes 393224 | tf_op jit(solution)/shard_map/ppermute | solution.py:678
  49.5 7.4 %collective-permute-start.9 = (bf16[512,128]{1,0:T(8,128)(2,1)S(1)}, bf16[512,128]{1,0:T(8,128)(2,1)S(1)}, u32[]{:S(2)}, u32[]{:S(2)}) collective-permute-start(bf16[512,128]{1,0:T(8,128)(2,1)S(1)} %get-tuple-element.51), channel_id=1, source_target_pairs={{0,4},{4,0},{8,12},{12,8},{16,20},{20,16},{24,28},{28,24},{1,5},{5... | collective-permute-start | bytes 393224 | tf_op jit(solution)/shard_map/ppermute | solution.py:678
  59.1 7.1 %copy-start.3 = (bf16[256,16,128]{2,1,0:T(8,128)(2,1)S(1)}, bf16[256,16,128]{2,1,0:T(8,128)(2,1)}, u32[]{:S(2)}) copy-start(bf16[256,16,128]{2,1,0:T(8,128)(2,1)} %param.13) | copy-start | bytes 3145732
  59.1 7.1 %copy-start.5 = (f32[16,128]{1,0:T(8,128)S(1)}, f32[16,128]{1,0:T(8,128)}, u32[]{:S(2)}) copy-start(f32[16,128]{1,0:T(8,128)} %refs_1_.1) | copy-start | bytes 24580
  59.1 7.0 %collective-permute-start.11 = (f32[8,256]{1,0:T(8,128)S(1)}, f32[8,256]{1,0:T(8,128)S(1)}, u32[]{:S(2)}, u32[]{:S(2)}) collective-permute-start(f32[8,256]{1,0:T(8,128)S(1)} %get-tuple-element.53.refs_5_.refs_4_), channel_id=1, source_target_pairs={{0,1},{1,0},{2,3},{3,2},{4,5},{5,4},{6,7},{7,6},{8,9},{9,8},{10,11... | collective-permute-start | bytes 24584 | tf_op jit(solution)/shard_map/ppermute | solution.py:773
  59.1 7.0 %collective-permute-start.12 = (f32[8,256]{1,0:T(8,128)S(1)}, f32[8,256]{1,0:T(8,128)S(1)}, u32[]{:S(2)}, u32[]{:S(2)}) collective-permute-start(f32[8,256]{1,0:T(8,128)S(1)} %get-tuple-element.53.refs_5_.refs_4_), channel_id=1, source_target_pairs={{0,2},{1,3},{2,0},{3,1},{4,6},{5,7},{6,4},{7,5},{8,10},{9,11},{10,... | collective-permute-start | bytes 24584 | tf_op jit(solution)/shard_map/ppermute | solution.py:773
  60.7 5.5 %collective-permute-start.13 = (f32[8,256]{1,0:T(8,128)S(1)}, f32[8,256]{1,0:T(8,128)S(1)}, u32[]{:S(2)}, u32[]{:S(2)}) collective-permute-start(f32[8,256]{1,0:T(8,128)S(1)} %get-tuple-element.53.refs_5_.refs_4_), channel_id=1, source_target_pairs={{0,3},{1,2},{2,1},{3,0},{4,7},{5,6},{6,5},{7,4},{8,11},{9,10},{10,... | collective-permute-start | bytes 24584 | tf_op jit(solution)/shard_map/ppermute | solution.py:773

commit v6 on v5

--- a/solution.py
+++ b/solution.py
@@ -34,12 +34,12 @@
 
 def cost(flops, bytes_accessed, transcendentals=0):
     return pl.CostEstimate(
-        flops=int(flops) // 64, bytes_accessed=int(bytes_accessed) // 64, transcendentals=int(transcendentals) // 64
-    )
-
-
-def call(kernel, name, place, operands, out_shape, scratch=(), mib=16, estimate=None, after=(), hbm=0, out_hbm=False):
-    begin = 1 + len(operands)
+        flops=int(flops), bytes_accessed=int(bytes_accessed), transcendentals=int(transcendentals)
+    )
+
+
+def call(kernel, name, scalars, operands, out_shape, scratch=(), mib=16, estimate=None, after=(), hbm=0, out_hbm=False):
+    begin = len(scalars) + len(operands)
     skip = len(after)
     operands = [
         pltpu.with_memory_space_constraint(x, pltpu.HBM) if i < hbm else x for i, x in enumerate(operands)
@@ -58,13 +58,13 @@
     out = pl.pallas_call(
         run,
         out_shape=outs,
-        in_specs=[SMEM] + [HBM] * hbm + [VMEM] * (len(operands) - hbm) + [ANYWHERE] * skip,
+        in_specs=[SMEM] * len(scalars) + [HBM] * hbm + [VMEM] * (len(operands) - hbm) + [ANYWHERE] * skip,
         out_specs=out_specs,
         scratch_shapes=list(scratch),
         compiler_params=pltpu.CompilerParams(vmem_limit_bytes=mib * 1024 * 1024),
         cost_estimate=estimate,
         name=name,
-    )(place, *operands, *after)
+    )(*scalars, *operands, *after)
     return out if isinstance(out_shape, tuple) else out[0]
 
 
@@ -86,16 +86,19 @@
     return rows >= cols
 
 
-def front_kernel(tokens, heads, kv_here, pieces, place_ref, *refs):
+def fetch_kernel(tokens, heads, kv_here, start_ref, *refs):
     refs = list(refs)
     take = lambda n: [refs.pop(0) for _ in range(n)]
     sources = take(6)
-    kv_ref, doc_out, cumul_ref, info_ref = take(4)
-    keep_refs, send_refs = take(pieces), take(pieces)
-    held = take(6)
-    sems, wide, kf, vf, states, ldp = refs
-    docs_in, soft_key, soft_value, decays, lin_key, lin_value = held
-    copies = [pltpu.make_async_copy(src, dst, sems.at[i]) for i, (src, dst) in enumerate(zip(sources, held))]
+    kv_ref, doc_out, cumul_ref, key_out, value_out = take(5)
+    held = take(4)
+    sems, wide, ldp = refs
+    docs_in, decays, soft_key, soft_value = held
+    targets = [*held, key_out, value_out]
+    copies = [
+        pltpu.make_async_copy(source, target, sems.at[i])
+        for i, (source, target) in enumerate(zip(sources, targets))
+    ]
     for copy in copies:
         copy.start()
 
@@ -109,9 +112,20 @@
     end = 2 * kv_here * tokens
     kv_ref[end : end + INFO, :] = info.astype(BF16)
 
-    start = place_ref[1]
+    copies[1].wait()
+    ldp[...] = jnp.zeros_like(ldp)
+    ldp[0:heads, :] = decays[...]
+    cumul_ref[...] = lax.dot_general(
+        lower_triangle(tokens).astype(F32),
+        ldp[...],
+        (((1,), (1,)), ((), ())),
+        precision=HIGHEST,
+        preferred_element_type=F32,
+    )
+
+    start = start_ref[0]
     for which, ref in enumerate((soft_key, soft_value)):
-        copies[1 + which].wait()
+        copies[2 + which].wait()
         wide[...] = ref[...].astype(F32)
         for g in range(kv_here):
             rows = wide[pl.ds(start + g, tokens, stride=KV_HEADS), :]
@@ -120,30 +134,51 @@
                 halves = [jnp.transpose(rows[i : i + LANES, :]) for i in range(0, tokens, LANES)]
                 rows = jnp.concatenate(halves, axis=0)
             kv_ref[at : at + tokens, :] = rows.astype(BF16)
-
+    copies[4].wait()
+    copies[5].wait()
+
+
+def fetch(start, operands, tokens, heads, kv_here):
+    return call(
+        functools.partial(fetch_kernel, tokens, heads, kv_here),
+        "fetch",
+        [start],
+        operands,
+        (
+            sds((2 * kv_here * tokens + INFO, LANES), BF16),
+            sds((INFO, LANES), F32),
+            sds((tokens, LANES), F32),
+            sds(operands[4].shape, BF16),
+            sds(operands[5].shape, BF16),
+        ),
+        scratch=[pltpu.VMEM(x.shape, x.dtype) for x in operands[:4]]
+        + [
+            pltpu.SemaphoreType.DMA((len(operands),)),
+            pltpu.VMEM((tokens * KV_HEADS, LANES), F32),
+            pltpu.VMEM((LANES, tokens), F32),
+        ],
+        estimate=cost(0, 3 * tokens * heads * LANES * 2),
+        hbm=len(operands),
+    )
+
+
+def state_kernel(tokens, heads, pieces, place_ref, *refs):
+    refs = list(refs)
+    take = lambda n: [refs.pop(0) for _ in range(n)]
+    cumul_ref, doc_ref, key_ref, value_ref, info_ref = take(5)
+    keep_refs, send_refs = take(pieces), take(pieces)
+    kf, vf, states = refs
     half = heads // 2
     y = place_ref[0] % 2
-    copies[3].wait()
-    ldp[...] = jnp.zeros_like(ldp)
-    ldp[0:heads, :] = decays[...]
-    cumul = lax.dot_general(
-        lower_triangle(tokens).astype(F32),
-        ldp[...],
-        (((1,), (1,)), ((), ())),
-        precision=HIGHEST,
-        preferred_element_type=F32,
-    )
-    cumul_ref[...] = cumul
+    cumul, docs = cumul_ref[...], doc_ref[...]
     total = cumul[tokens - 1 : tokens, :]
     last_row = tokens // LANES - 1
     first_doc = docs[0:1, 0:1]
     last_doc = docs[last_row : last_row + 1, LANES - 1 : LANES]
     tail = (doc_columns(docs, tokens) == last_doc).astype(F32)
     scale = jnp.exp(total - cumul) * tail
-    copies[4].wait()
-    kf[...] = lin_key[...].astype(F32)
-    copies[5].wait()
-    vf[...] = lin_value[...].astype(F32)
+    kf[...] = key_ref[...].astype(F32)
+    vf[...] = value_ref[...].astype(F32)
     for h in range(heads):
         keys = (kf[pl.ds(h, tokens, stride=heads), :] * scale[:, h : h + 1]).astype(BF16)
         values = vf[pl.ds(h, tokens, stride=heads), :].astype(BF16)
@@ -166,37 +201,24 @@
     send_refs[0][size : size + INFO, :] = info_of(total * (1.0 - mine) + upper * mine)
 
 
-def front(place, operands, tokens, heads, kv_here, pieces):
+def block_state(place, cumul, docs, key, value, tokens, heads, pieces):
     size = heads // 2 // pieces * HEAD_DIM
     keep = [sds((size, LANES), BF16)] * pieces
     send = [sds((size + (INFO if p == 0 else 0), LANES), BF16) for p in range(pieces)]
     out = call(
-        functools.partial(front_kernel, tokens, heads, kv_here, pieces),
-        "front",
-        place,
-        operands,
-        (
-            sds((2 * kv_here * tokens + INFO, LANES), BF16),
-            sds((INFO, LANES), F32),
-            sds((tokens, LANES), F32),
-            sds((INFO, LANES), BF16),
-            *keep,
-            *send,
-        ),
-        scratch=[pltpu.VMEM(x.shape, x.dtype) for x in operands]
-        + [
-            pltpu.SemaphoreType.DMA((len(operands),)),
-            pltpu.VMEM((tokens * KV_HEADS, LANES), F32),
+        functools.partial(state_kernel, tokens, heads, pieces),
+        "block_state",
+        [place],
+        [cumul, docs, key, value],
+        (sds((INFO, LANES), BF16), *keep, *send),
+        scratch=[
             pltpu.VMEM((tokens * heads, LANES), F32),
             pltpu.VMEM((tokens * heads, LANES), F32),
             pltpu.VMEM((heads * HEAD_DIM, LANES), F32),
-            pltpu.VMEM((LANES, tokens), F32),
         ],
-        mib=24,
         estimate=cost(2 * heads * tokens * HEAD_DIM**2, 5 * tokens * heads * LANES * 2),
-        hbm=len(operands),
-    )
-    return (*out[:4], out[4 : 4 + pieces], out[4 + pieces :])
+    )
+    return out[0], out[1 : 1 + pieces], out[1 + pieces :]
 
 
 def in_parts(x):
@@ -233,7 +255,10 @@
     return even, decay_a * whole_a, decay_b * link_b, first_a, last_a, last_b
 
 
-def row_kernel(count, first, place_ref, keep_ref, info_ref, other_ref, other_info_ref, out_ref):
+def row_kernel(count, first, place_ref, keep_ref, info_ref, other_ref, other_info_ref, *refs):
+    out_ref = refs[len(refs) // 2]
+    if len(refs) > 1:
+        refs[2][...] = refs[0][...]
     size = count * HEAD_DIM
     even, gain_a, gain_b, first_a, _, last_b = row_terms(
         place_ref, info_ref[...], other_info_ref[size : size + INFO, :]
@@ -248,17 +273,19 @@
     out_ref[size : size + INFO, :] = info_rows((*in_parts(gain_a * gain_b), first_a, last_b))
 
 
-def row_map(place, keep, info, other, other_info, first, count, after):
+def row_map(place, keep, info, other, other_info, first, count, after, relay=None):
     size = count * HEAD_DIM
-    return call(
+    relay = [] if relay is None else [relay]
+    out = call(
         functools.partial(row_kernel, count, first),
         "row_map",
-        place,
-        [keep, info, other, other_info],
-        sds((size + INFO, LANES), BF16),
+        [place],
+        [keep, info, other, other_info, *relay],
+        (sds((size + INFO, LANES), BF16), *[sds(x.shape, BF16) for x in relay]),
         estimate=cost(4 * size * LANES, 4 * size * LANES * 2),
         after=after,
     )
+    return out if relay else out[0]
 
 
 def scan_kernel(count, first, has_before, stage, place_ref, *refs):
@@ -313,7 +340,7 @@
     return call(
         functools.partial(scan_kernel, count, first, len(before), stage),
         "scan_step",
-        place,
+        [place],
         [mine, came, *before],
         (shape, shape),
         estimate=cost(6 * size * LANES, 6 * size * LANES * 2),
@@ -321,10 +348,10 @@
     )
 
 
-def prior_kernel(count, first, has_before, stage, place_ref, *refs):
+def prior_kernel(count, first, has_before, stage, wants_doc, place_ref, *refs):
     keep_ref, info_ref, other_ref, other_info_ref, came_ref = refs[:5]
     before_ref = refs[5] if has_before else None
-    mine_ref, send_ref, doc_ref = refs[-3:]
+    mine_ref, send_ref = refs[-3:-1] if wants_doc else refs[-2:]
     size = count * HEAD_DIM
     upper = ((place_ref[0] >> stage) & 1).astype(F32)
     even, gain_a, _, first_a, last_a, _ = row_terms(
@@ -350,18 +377,20 @@
         before_b = gain_a[:, lane] * before_a + state_a
         mine_ref[rows, :] = jnp.where(even, before_a, before_b).astype(BF16)
         send_ref[rows, :] = jnp.where(even, before_b, before_a).astype(BF16)
-    doc_ref[...] = jnp.broadcast_to(jnp.where(even, doc, last_a), (8, LANES))
-
-
-def prior_states(place, stage, keep, info, other, other_info, came, before, first, count, after):
+    if wants_doc:
+        refs[-1][...] = jnp.broadcast_to(jnp.where(even, doc, last_a), (8, LANES))
+
+
+def prior_states(place, stage, keep, info, other, other_info, came, before, first, count, after, wants_doc):
     size = count * HEAD_DIM
+    docs = (sds((8, LANES), F32),) if wants_doc else ()
     before = [] if before is None else [before]
     return call(
-        functools.partial(prior_kernel, count, first, len(before), stage),
+        functools.partial(prior_kernel, count, first, len(before), stage, wants_doc),
         "prior_states",
-        place,
+        [place],
         [keep, info, other, other_info, came, *before],
-        (sds((size, LANES), BF16), sds((size, LANES), BF16), sds((8, LANES), F32)),
+        (sds((size, LANES), BF16), sds((size, LANES), BF16), *docs),
         estimate=cost(4 * size * LANES, 6 * size * LANES * 2),
         after=after,
     )
@@ -374,7 +403,7 @@
     return x.reshape(tokens, heads, LANES)[:, first : first + count, :].reshape(tokens * count, LANES)
 
 
-def inner_kernel(tokens, heads, first, count, place_ref, cumul_ref, doc_ref, query_ref, key_ref, value_ref, inner_ref, qh_ref, qf, kf, vf, mask):
+def inner_kernel(tokens, heads, first, count, cumul_ref, doc_ref, query_ref, key_ref, value_ref, inner_ref, qh_ref, qf, kf, vf, mask):
     cumul = cumul_ref[...]
     cumul_t = jnp.transpose(cumul)
     docs = doc_ref[...]
@@ -404,11 +433,11 @@
             )
 
 
-def inner_part(place, cumul, docs, query, key, value, tokens, heads, first, count, after):
+def inner_part(cumul, docs, query, key, value, tokens, heads, first, count, after):
     return call(
         functools.partial(inner_kernel, tokens, heads, first, count),
         "inner_part",
-        place,
+        [],
         [cumul, docs, query, key, value],
         (sds((count * tokens, LANES), F32), sds((count * tokens, LANES), BF16)),
         scratch=[pltpu.VMEM((tokens * count, LANES), F32)] * 3 + [pltpu.VMEM((tokens, tokens), F32)],
@@ -456,7 +485,7 @@
     return call(
         functools.partial(mix_kernel, tokens, heads, len(inner), len(mine)),
         "mix",
-        place,
+        [place],
         [docs, prior_doc, cumul, *inner, *qh, *mine, *other],
         (sds((tokens * heads, LANES), F32), sds((8, tokens), F32)),
         mib=24,
@@ -465,7 +494,7 @@
     )
 
 
-def finish_kernel(tokens, heads, sums, step, place_ref, gain_ref, gate_ref, mixed_ref, *refs):
+def finish_kernel(tokens, heads, sums, step, gain_ref, gate_ref, mixed_ref, *refs):
     squares, (out_ref, done, sems) = refs[:sums], refs[sums:]
     total = squares[0][0:1, :]
     for ref in squares[1:]:
@@ -487,12 +516,12 @@
         copy.wait()
 
 
-def finish(place, gain, gate, mixed, squares, tokens, heads, after):
+def finish(gain, gate, mixed, squares, tokens, heads, after):
     step = 64
     return call(
         functools.partial(finish_kernel, tokens, heads, len(squares), step),
         "finish",
-        place,
+        [],
         [gain, gate, mixed, *squares],
         sds((tokens * heads, LANES), BF16),
         scratch=[pltpu.VMEM((tokens * heads, LANES), BF16), pltpu.SemaphoreType.DMA((tokens // step,))],
@@ -635,7 +664,7 @@
     return call(
         functools.partial(attend_kernel, tokens, heads, kv_here, least, is_first, is_last, unroll),
         "attend",
-        place,
+        [place],
         [*first, *([] if is_first else [state]), *kv],
         out_shape,
         scratch=scratch,
@@ -672,7 +701,8 @@
     window = min(blocks - 1, (longest - 1 + tokens - 1) // tokens)
     flat = lambda x: x.reshape(-1, LANES)
     block = lax.axis_index("seq")
-    place = jnp.stack([block, lax.axis_index("tp") * heads // GROUP]).astype(jnp.int32)
+    place = block.astype(jnp.int32).reshape(1)
+    start = (lax.axis_index("tp") * heads // GROUP).astype(jnp.int32).reshape(1)
 
     def send(x, pairs):
         return lax.ppermute(x, "seq", [(a, b % blocks) for a, b in pairs])
@@ -680,32 +710,29 @@
     everyone = range(blocks)
     swap = [(b, b ^ 1) for b in everyone]
 
-    own_kv, docs, cumul, info, held, sent = front(
-        place,
+    own_kv, docs, cumul, key, value = fetch(
+        start,
         [
             doc_ids.reshape(tokens // LANES, LANES),
+            jnp.transpose(log_decay),
             flat(soft_key),
             flat(soft_value),
-            jnp.transpose(log_decay),
             flat(lin_key),
             flat(lin_value),
         ],
         tokens,
         heads,
         kv_here,
-        pieces,
-    )
-    came = [send(x, swap) for x in sent]
+    )
+
     odd_window = window % 2 == 1
+    forward = [(b, b + 2) for b in everyone]
+    ahead = send(own_kv, forward)
     beside = send(own_kv, [(b, b + (1 if b % 2 == 0 else window if odd_window else -1)) for b in everyone])
     beside = (beside, (window if odd_window else blocks, 1))
-    lane_kv, cross_kv = [], []
-    ahead = own_kv
-    for back in range(1, window // 2 + 1):
-        ahead = send(ahead, [(b, b + 2) for b in everyone])
-        lane_kv.append((ahead, (2 * back, 2 * back)))
-        cross_kv.append((send(ahead, swap), (2 * back, 2 * back + 1)))
-    held = list(held)
+
+    info, held, sent = block_state(place, cumul, docs, key, value, tokens, heads, pieces)
+    came = [send(x, swap) for x in sent]
 
     state = {}
 
@@ -726,19 +753,19 @@
     def inner_of(part, after):
         n = heads // parts
         got = inner_part(
-            place, cumul, docs, flat(lin_query), flat(lin_key), flat(lin_value), tokens, heads, part * n, n, after
+            cumul, docs, flat(lin_query), key, value, tokens, heads, part * n, n, after
         )
         inner.append(got[0])
         qh.append(got[1])
         return got[0]
 
     beside_work = [first_attention]
+    beside_work.append(lambda after: more_attention([beside] + lane_kv[:1], False, after))
     beside_work += [functools.partial(inner_of, part) for part in range(parts)]
-    beside_work.append(functools.partial(more_attention, [beside] + lane_kv[:1], False))
+    lane_kv, cross_kv = [], []
 
     done = info
     mine, far = [], []
-    prior_doc = None
     run, before = [None] * pieces, [None] * pieces
     stages = (blocks // 2).bit_length() - 1
     for stage in range(stages + 1):
@@ -750,13 +777,23 @@
         for p in range(pieces):
             at = (p * count, count, [done])
             if stage == 0:
-                done = run[p] = row_map(place, held[p], info, came[p], came[0], *at)
+                args = (place, held[p], info, came[p], came[0], *at)
+                if p == 0:
+                    run[p], ahead = row_map(*args, ahead)
+                    for back in range(1, window // 2 + 1):
+                        lane_kv.append((ahead, (2 * back, 2 * back)))
+                        cross_kv.append((send(ahead, swap), (2 * back, 2 * back + 1)))
+                        ahead = send(ahead, forward)
+                else:
+                    run[p] = row_map(*args)
+                done = run[p]
             elif stage < stages:
                 run[p], before[p] = scan_step(place, stage, run[p], got[p], before[p], *at)
                 done = run[p]
             else:
-                done, sent, prior_doc = prior_states(
-                    place, stage, held[p], info, came[p], came[0], got[p], before[p], *at
+                wants_doc = p == pieces - 1
+                done, sent, *docs_before = prior_states(
+                    place, stage, held[p], info, came[p], came[0], got[p], before[p], *at, wants_doc
                 )
                 mine.append(done)
                 far.append(send(sent, swap))
@@ -766,7 +803,7 @@
     done = more_attention(rest[:1], False, [done])
     rest = rest[1:]
     mixed, squares = mix(
-        place, docs, prior_doc, cumul, inner, qh, mine, far, tokens, heads, [done]
+        place, docs, docs_before[0], cumul, inner, qh, mine, far, tokens, heads, [done]
     )
     sums = [squares]
     for other in range(1, tensor):
@@ -776,7 +813,7 @@
         got = more_attention(rest[:2], len(rest) <= 2, after)
         rest, after = rest[2:], []
     soft_out, done = got
-    lin_out = finish(place, norm_gain, flat(lin_gate), mixed, sums, tokens, heads, [done])
+    lin_out = finish(norm_gain, flat(lin_gate), mixed, sums, tokens, heads, [done])
     shape = (tokens, heads, HEAD_DIM)
     return lin_out.reshape(shape), soft_out.reshape(shape)
 

time: 68.7 us -> 59.5 us (0.87)
  Pallas kernels: 34.6 us -> 28.5 us
  waiting for transfers between devices: 12.7 us -> 8.94 us
  starting transfers between devices: 20 us -> 20.9 us
    pallas_call x15 -> x16, Pallas kernels: 34.6 us -> 28.5 us  [call(): pl.pallas_call(run, out_shape=outs, in_specs=[SMEM] * len(scalars) + [HBM...]
    ppermute x13, waiting for transfers between devices: 12.7 us -> 8.93 us  [send(): return lax.ppermute(x, 'seq', [(a, b % blocks) for a, b in pairs])]
    ppermute x13, starting transfers between devices: 18.2 us -> 19 us  [send(): return lax.ppermute(x, 'seq', [(a, b % blocks) for a, b in pairs])]
  transfers between devices with their start and end apart: 16 -> 16, of which waited for: 4 -> 4; matrix products, arithmetic and copies ran while one was open for 0% -> 0% of each run, Pallas kernels for 39% -> 41%
where the time goes in v6:
time: 59.5 us; the launch traced here: 59.3 us
  Pallas kernels  28.5 us (48%)
  starting transfers between devices  20.9 us (35%)
  waiting for transfers between devices  8.94 us (15%)
  between operations  1.01 us (2%)
    pallas_call x16, Pallas kernels, call(): pl.pallas_call(run, out_shape=outs, in_specs=[SMEM] * len(scalars) + [HBM...  28.5 us
    ppermute x13, starting transfers between devices, send(): return lax.ppermute(x, 'seq', [(a, b % blocks) for a, b in pairs])  19 us
    ppermute x13, waiting for transfers between devices, send(): return lax.ppermute(x, 'seq', [(a, b % blocks) for a, b in pairs])  8.93 us
    ppermute x3, starting transfers between devices, body(): lax.ppermute(squares, 'tp', [(t, t ^ other) for t in range(tensor)])  1.88 us
  transfers between devices with their start and end apart: 16, of which 4 were waited for; matrix products, arithmetic and copies ran while one was open for 0% of the time, Pallas kernels for 41%

profile of v6, /device:TPU:0, one launch (start us, length us, event | category | flops | bytes accessed | tf_op | source)
XLA Modules:
  0.0 59.3 jit_solution(6695141732496350428)
XLA Ops:
  0.7 2.7 %fetch.1 = (bf16[1040,128]{1,0:T(8,128)(2,1)}, f32[16,128]{1,0:T(8,128)S(1)}, f32[256,128]{1,0:T(8,128)S(1)}, bf16[4096,128]{1,0:T(8,128)(2,1)S(1)}, bf16[4096,128]{1,0:T(8,128)(2,1)S(1)}) custom-call(s32[1]{0:T(128)} %bitcast.2.refs_0_, s32[2,128]{1,0:T(2,128)} %bitcast.23, f32[16,256]{1,0:T(8,128)} %bitcast.22, bf16[2048,128]{1,0:T(8,128)(2,1)} %bitcast.20, ...), custom_call_target="tpu_custom_call" | custom-call | bytes 3145728 | tf_op jit(solution)/shard_map/fetch/pallas_call | solution.py:58
  3.4 3.1 %collective-permute-start.2 = (bf16[1040,128]{1,0:T(8,128)(2,1)}, bf16[1040,128]{1,0:T(8,128)(2,1)S(1)}, u32[]{:S(2)}, u32[]{:S(2)}) collective-permute-start(bf16[1040,128]{1,0:T(8,128)(2,1)} %get-tuple-element.42.refs_3_), channel_id=1, source_target_pairs={{0,8},{4,12},{8,16},{12,20},{16,24},{20,28},{24,0},{28,4},{1,9},{5... | collective-permute-start | bytes 798728 | tf_op jit(solution)/shard_map/ppermute | solution.py:708
  6.5 1.5 %collective-permute-start.5 = (bf16[1040,128]{1,0:T(8,128)(2,1)}, bf16[1040,128]{1,0:T(8,128)(2,1)}, u32[]{:S(2)}, u32[]{:S(2)}) collective-permute-start(bf16[1040,128]{1,0:T(8,128)(2,1)} %get-tuple-element.42.refs_3_), channel_id=1, source_target_pairs={{0,4},{4,24},{8,12},{12,0},{16,20},{20,8},{24,28},{28,16},{1,5},{5... | collective-permute-start | bytes 798728 | tf_op jit(solution)/shard_map/ppermute | solution.py:708
  8.0 2.8 %block_state.1 = (bf16[16,128]{1,0:T(8,128)(2,1)S(1)}, bf16[512,128]{1,0:T(8,128)(2,1)S(1)}, bf16[512,128]{1,0:T(8,128)(2,1)S(1)}, bf16[528,128]{1,0:T(8,128)(2,1)S(1)}, bf16[512,128]{1,0:T(8,128)(2,1)S(1)}) custom-call(s32[1]{0:T(128)} %bitcast.1.refs_0_, f32[256,128]{1,0:T(8,128)S(1)} %get-tuple-element.34.refs_1_.refs_0_.refs_3_, ...), custom_call_target="tpu_custom_call" | custom-call | flops 134217728 | bytes 5242880 | tf_op jit(solution)/shard_map/block_state/pallas_call | solution.py:58
  10.8 2.1 %collective-permute-start.1 = (bf16[528,128]{1,0:T(8,128)(2,1)S(1)}, bf16[528,128]{1,0:T(8,128)(2,1)S(1)}, u32[]{:S(2)}, u32[]{:S(2)}) collective-permute-start(bf16[528,128]{1,0:T(8,128)(2,1)S(1)} %get-tuple-element.40), channel_id=1, source_target_pairs={{0,4},{4,0},{8,12},{12,8},{16,20},{20,16},{24,28},{28,24},{1,5},{5... | collective-permute-start | bytes 405512 | tf_op jit(solution)/shard_map/ppermute | solution.py:708
  12.9 0.1 collective-permute-start
  13.0 3.6 %attend.4 = (bf16[2,2048,256]{2,1,0:T(8,128)(2,1)S(1)}, f32[2,144,2048]{2,1,0:T(8,128)S(1)}) custom-call(s32[1]{0:T(128)} %bitcast.1.refs_0_, f32[16,128]{1,0:T(8,128)S(1)} %get-tuple-element.33.refs_2_.refs_1_, bf16[4096,128]{1,0:T(8,128)(2,1)S(1)} %bitcast.16, bf16[1040,128]{1,0:T(8,128)(2,1)} %get-tuple-element.42.refs_3_, ...), custom_call_target="tpu_custom_call" | custom-call | flops 1073741824 | bytes 8388608 | tf_op jit(solution)/shard_map/attend/pallas_call | solution.py:58
  16.5 5.8 %collective-permute-done.1.refs_3_.refs_4_ = bf16[528,128]{1,0:T(8,128)(2,1)S(1)} collective-permute-done((bf16[528,128]{1,0:T(8,128)(2,1)S(1)}, bf16[528,128]{1,0:T(8,128)(2,1)S(1)}, u32[]{:S(2)}, u32[]{:S(2)}) %collective-permute-start.1) | collective-permute-done | bytes 135200 | tf_op jit(solution)/shard_map/ppermute | solution.py:708
  22.3 0.0 collective-permute-done.2.refs_5_
  22.3 0.1 row_map.2
  22.5 2.1 %collective-permute-start.14 = (bf16[1040,128]{1,0:T(8,128)(2,1)S(1)}, bf16[1040,128]{1,0:T(8,128)(2,1)S(1)}, u32[]{:S(2)}, u32[]{:S(2)}) collective-permute-start(bf16[1040,128]{1,0:T(8,128)(2,1)S(1)} %get-tuple-element.46.refs_4_), channel_id=1, source_target_pairs={{0,8},{4,12},{8,16},{12,20},{16,24},{20,28},{24,0},{28,4},{1,9},{5... | collective-permute-start | bytes 798728 | tf_op jit(solution)/shard_map/ppermute | solution.py:708
  24.6 0.0 collective-permute-start.10
  24.6 1.3 %collective-permute-start.4 = (bf16[528,128]{1,0:T(8,128)(2,1)S(1)}, bf16[528,128]{1,0:T(8,128)(2,1)S(1)}, u32[]{:S(2)}, u32[]{:S(2)}) collective-permute-start(bf16[528,128]{1,0:T(8,128)(2,1)S(1)} %get-tuple-element.44.refs_5_.refs_1_), channel_id=1, source_target_pairs={{0,8},{4,12},{8,0},{12,4},{16,24},{20,28},{24,16},{28,20},{1,9},{5... | collective-permute-start | bytes 405512 | tf_op jit(solution)/shard_map/ppermute | solution.py:708
  25.9 0.0 collective-permute-done.refs_3_
  25.9 0.1 row_map.3.refs_5_.refs_1_
  26.1 0.8 %collective-permute-start.3 = (bf16[528,128]{1,0:T(8,128)(2,1)S(1)}, bf16[528,128]{1,0:T(8,128)(2,1)S(1)}, u32[]{:S(2)}, u32[]{:S(2)}) collective-permute-start(bf16[528,128]{1,0:T(8,128)(2,1)S(1)} %row_map.3.refs_5_.refs_1_), channel_id=1, source_target_pairs={{0,8},{4,12},{8,0},{12,4},{16,24},{20,28},{24,16},{28,20},{1,9},{5... | collective-permute-start | bytes 405512 | tf_op jit(solution)/shard_map/ppermute | solution.py:708
  26.8 0.0 collective-permute-done.5.refs_3_
  26.8 4.6 %attend.5.refs_3_.refs_2_ = f32[2,144,2048]{2,1,0:T(8,128)S(1)} custom-call(s32[1]{0:T(128)} %bitcast.1.refs_0_, bf16[2,2048,256]{2,1,0:T(8,128)(2,1)S(1)} %get-tuple-element.45.refs_1_, f32[2,144,2048]{2,1,0:T(8,128)S(1)} %get-tuple-element.43.refs_6_.refs_2_, bf16[1040,128]{1,0:T(8,128)(2,1)} %collective-permute-done.5.refs_3_, ...), custom_call_target="tpu_custom_call" | custom-call | flops 2147483648 | bytes 8388608 | tf_op jit(solution)/shard_map/attend/pallas_call | solution.py:58
  31.4 0.0 copy-start
  31.4 0.0 collective-permute-done.4.refs_2_
  31.4 0.1 scan_step.2
  31.6 3.6 %collective-permute-start.7 = (bf16[528,128]{1,0:T(8,128)(2,1)S(1)}, bf16[528,128]{1,0:T(8,128)(2,1)S(1)}, u32[]{:S(2)}, u32[]{:S(2)}) collective-permute-start(bf16[528,128]{1,0:T(8,128)(2,1)S(1)} %get-tuple-element.47.refs_3_), channel_id=1, source_target_pairs={{0,16},{4,20},{8,24},{12,28},{16,0},{20,4},{24,8},{28,12},{1,17},{... | collective-permute-start | bytes 405512 | tf_op jit(solution)/shard_map/ppermute | solution.py:708
  35.2 1.0 %collective-permute-done.3.refs_2_ = bf16[528,128]{1,0:T(8,128)(2,1)S(1)} collective-permute-done((bf16[528,128]{1,0:T(8,128)(2,1)S(1)}, bf16[528,128]{1,0:T(8,128)(2,1)S(1)}, u32[]{:S(2)}, u32[]{:S(2)}) %collective-permute-start.3) | collective-permute-done | bytes 135200 | tf_op jit(solution)/shard_map/ppermute | solution.py:708
  36.1 0.1 scan_step.3
  36.3 1.8 %collective-permute-start.6 = (bf16[528,128]{1,0:T(8,128)(2,1)S(1)}, bf16[528,128]{1,0:T(8,128)(2,1)S(1)}, u32[]{:S(2)}, u32[]{:S(2)}) collective-permute-start(bf16[528,128]{1,0:T(8,128)(2,1)S(1)} %get-tuple-element.48.refs_5_), channel_id=1, source_target_pairs={{0,16},{4,20},{8,24},{12,28},{16,0},{20,4},{24,8},{28,12},{1,17},{... | collective-permute-start | bytes 405512 | tf_op jit(solution)/shard_map/ppermute | solution.py:708
  38.0 0.0 collective-permute-done.14.refs_3_
  38.0 0.0 collective-permute-start.15
  38.1 1.9 %inner_part.2 = (f32[2048,128]{1,0:T(8,128)S(1)}, bf16[2048,128]{1,0:T(8,128)(2,1)S(1)}) custom-call(f32[256,128]{1,0:T(8,128)S(1)} %get-tuple-element.34.refs_1_.refs_0_.refs_3_, f32[16,128]{1,0:T(8,128)S(1)} %get-tuple-element.33.refs_2_.refs_1_, bf16[4096,128]{1,0:T(8,128)(2,1)S(1)} %bitcast.13, bf16[4096,128]{1,0:T(8,128)(2,1)S(1)} %get-tuple-element.35.refs_3_, ...), custom_call_target="tpu_custom_call" | custom-call | flops 268435456 | bytes 6291456 | tf_op jit(solution)/shard_map/inner_part/pallas_call | solution.py:58
  40.0 1.9 %inner_part.3 = (f32[2048,128]{1,0:T(8,128)S(1)}, bf16[2048,128]{1,0:T(8,128)(2,1)S(1)}) custom-call(f32[256,128]{1,0:T(8,128)S(1)} %get-tuple-element.34.refs_1_.refs_0_.refs_3_, f32[16,128]{1,0:T(8,128)S(1)} %get-tuple-element.33.refs_2_.refs_1_, bf16[4096,128]{1,0:T(8,128)(2,1)S(1)} %bitcast.14, bf16[4096,128]{1,0:T(8,128)(2,1)S(1)} %get-tuple-element.35.refs_3_, ...), custom_call_target="tpu_custom_call" | custom-call | flops 268435456 | bytes 6291456 | tf_op jit(solution)/shard_map/inner_part/pallas_call | solution.py:58
  41.9 0.6 %collective-permute-done.7.refs_5_ = bf16[528,128]{1,0:T(8,128)(2,1)S(1)} collective-permute-done((bf16[528,128]{1,0:T(8,128)(2,1)S(1)}, bf16[528,128]{1,0:T(8,128)(2,1)S(1)}, u32[]{:S(2)}, u32[]{:S(2)}) %collective-permute-start.7) | collective-permute-done | bytes 135200 | tf_op jit(solution)/shard_map/ppermute | solution.py:708
  42.5 0.2 prior_states.2
  42.7 1.5 %collective-permute-start.8 = (bf16[512,128]{1,0:T(8,128)(2,1)S(1)}, bf16[512,128]{1,0:T(8,128)(2,1)S(1)}, u32[]{:S(2)}, u32[]{:S(2)}) collective-permute-start(bf16[512,128]{1,0:T(8,128)(2,1)S(1)} %get-tuple-element.58), channel_id=1, source_target_pairs={{0,4},{4,0},{8,12},{12,8},{16,20},{20,16},{24,28},{28,24},{1,5},{5... | collective-permute-start | bytes 393224 | tf_op jit(solution)/shard_map/ppermute | solution.py:708
  44.2 0.0 collective-permute-done.6.refs_5_
  44.2 0.2 prior_states.3
  44.4 1.2 %collective-permute-start.9 = (bf16[512,128]{1,0:T(8,128)(2,1)S(1)}, bf16[512,128]{1,0:T(8,128)(2,1)S(1)}, u32[]{:S(2)}, u32[]{:S(2)}) collective-permute-start(bf16[512,128]{1,0:T(8,128)(2,1)S(1)} %get-tuple-element.59), channel_id=1, source_target_pairs={{0,4},{4,0},{8,12},{12,8},{16,20},{20,16},{24,28},{28,24},{1,5},{5... | collective-permute-start | bytes 393224 | tf_op jit(solution)/shard_map/ppermute | solution.py:708
  45.5 0.0 collective-permute-done.10.refs_3_
  45.5 2.3 %attend.6.refs_12_.refs_2_ = f32[2,144,2048]{2,1,0:T(8,128)S(1)} custom-call(s32[1]{0:T(128)} %bitcast.1.refs_0_, bf16[2,2048,256]{2,1,0:T(8,128)(2,1)S(1)} %get-tuple-element.45.refs_1_, f32[2,144,2048]{2,1,0:T(8,128)S(1)} %attend.5.refs_3_.refs_2_, bf16[1040,128]{1,0:T(8,128)(2,1)S(1)} %collective-permute-done.10.refs_3_, ...), custom_call_target="tpu_custom_call" | custom-call | flops 1073741824 | bytes 8388608 | tf_op jit(solution)/shard_map/attend/pallas_call | solution.py:58
  47.9 0.0 collective-permute-done.8.refs_10_
  47.9 1.5 %collective-permute-done.9.refs_11_ = bf16[512,128]{1,0:T(8,128)(2,1)S(1)} collective-permute-done((bf16[512,128]{1,0:T(8,128)(2,1)S(1)}, bf16[512,128]{1,0:T(8,128)(2,1)S(1)}, u32[]{:S(2)}, u32[]{:S(2)}) %collective-permute-start.9) | collective-permute-done | bytes 131104 | tf_op jit(solution)/shard_map/ppermute | solution.py:708
  49.4 1.6 %mix.1 = (f32[4096,128]{1,0:T(8,128)S(1)}, f32[8,256]{1,0:T(8,128)S(1)}) custom-call(s32[1]{0:T(128)} %bitcast.1.refs_0_, f32[16,128]{1,0:T(8,128)S(1)} %get-tuple-element.33.refs_2_.refs_1_, f32[8,128]{1,0:T(8,128)S(1)} %get-tuple-element.54.refs_2_, f32[256,128]{1,0:T(8,128)S(1)} %get-tuple-element.34.refs_1_.refs_0_.refs_3_, ...), custom_call_target="tpu_custom_call" | custom-call | flops 134217728 | bytes 5242880 | tf_op jit(solution)/shard_map/mix/pallas_call | solution.py:58
  51.0 0.0 collective-permute-start.11
  51.0 1.6 %collective-permute-start.12 = (f32[8,256]{1,0:T(8,128)S(1)}, f32[8,256]{1,0:T(8,128)S(1)}, u32[]{:S(2)}, u32[]{:S(2)}) collective-permute-start(f32[8,256]{1,0:T(8,128)S(1)} %get-tuple-element.61.refs_5_.refs_3_), channel_id=1, source_target_pairs={{0,2},{1,3},{2,0},{3,1},{4,6},{5,7},{6,4},{7,5},{8,10},{9,11},{10,... | collective-permute-start | bytes 24584 | tf_op jit(solution)/shard_map/ppermute | solution.py:810
  52.6 0.3 collective-permute-start.13
  52.9 0.0 collective-permute-done.15.refs_4_
  52.9 4.6 %attend.7 = (bf16[4096,128]{1,0:T(8,128)(2,1)}, f32[8,128]{1,0:T(8,128)S(1)}) custom-call(s32[1]{0:T(128)} %bitcast.1.refs_0_, bf16[2,2048,256]{2,1,0:T(8,128)(2,1)S(1)} %get-tuple-element.45.refs_1_, f32[2,144,2048]{2,1,0:T(8,128)S(1)} %attend.6.refs_12_.refs_2_, bf16[1040,128]{1,0:T(8,128)(2,1)S(1)} %collective-permute-done.14.refs_3_, ...), custom_call_target="tpu_custom_call" | custom-call | flops 2147483648 | bytes 8388608 | tf_op jit(solution)/shard_map/attend/pallas_call | solution.py:58
  57.4 0.0 collective-permute-done.11.refs_4_
  57.5 0.0 collective-permute-done.12.refs_5_
  57.5 1.6 %finish.1 = bf16[4096,128]{1,0:T(8,128)(2,1)} custom-call(f32[16,128]{1,0:T(8,128)S(1)} %copy-done.2, bf16[4096,128]{1,0:T(8,128)(2,1)S(1)} %bitcast.15, f32[4096,128]{1,0:T(8,128)S(1)} %get-tuple-element.60.refs_2_, f32[8,256]{1,0:T(8,128)S(1)} %get-tuple-element.61.refs_5_.refs_3_, f32[8,256]{1,0:T(8,128)S(1)} %collective-permute-done.11.refs_4_, ...), custom_call_target="tpu_custom_call" | custom-call | bytes 4194304 | tf_op jit(solution)/shard_map/finish/pallas_call | solution.py:58
  (8 shorter events, 0.0 us)
Async XLA Ops:
  0.6 12.3 %copy-start.3 = (bf16[256,16,128]{2,1,0:T(8,128)(2,1)S(1)}, bf16[256,16,128]{2,1,0:T(8,128)(2,1)}, u32[]{:S(2)}) copy-start(bf16[256,16,128]{2,1,0:T(8,128)(2,1)} %param.17) | copy-start | bytes 3145732
  3.4 18.9 %collective-permute-start.2 = (bf16[1040,128]{1,0:T(8,128)(2,1)}, bf16[1040,128]{1,0:T(8,128)(2,1)S(1)}, u32[]{:S(2)}, u32[]{:S(2)}) collective-permute-start(bf16[1040,128]{1,0:T(8,128)(2,1)} %get-tuple-element.42.refs_3_), channel_id=1, source_target_pairs={{0,8},{4,12},{8,16},{12,20},{16,24},{20,28},{24,0},{28,4},{1,9},{5... | collective-permute-start | bytes 798728 | tf_op jit(solution)/shard_map/ppermute | solution.py:708
  6.5 20.4 %collective-permute-start.5 = (bf16[1040,128]{1,0:T(8,128)(2,1)}, bf16[1040,128]{1,0:T(8,128)(2,1)}, u32[]{:S(2)}, u32[]{:S(2)}) collective-permute-start(bf16[1040,128]{1,0:T(8,128)(2,1)} %get-tuple-element.42.refs_3_), channel_id=1, source_target_pairs={{0,4},{4,24},{8,12},{12,0},{16,20},{20,8},{24,28},{28,16},{1,5},{5... | collective-permute-start | bytes 798728 | tf_op jit(solution)/shard_map/ppermute | solution.py:708
  10.8 11.5 %collective-permute-start.1 = (bf16[528,128]{1,0:T(8,128)(2,1)S(1)}, bf16[528,128]{1,0:T(8,128)(2,1)S(1)}, u32[]{:S(2)}, u32[]{:S(2)}) collective-permute-start(bf16[528,128]{1,0:T(8,128)(2,1)S(1)} %get-tuple-element.40), channel_id=1, source_target_pairs={{0,4},{4,0},{8,12},{12,8},{16,20},{20,16},{24,28},{28,24},{1,5},{5... | collective-permute-start | bytes 405512 | tf_op jit(solution)/shard_map/ppermute | solution.py:708
  12.9 13.0 %collective-permute-start = (bf16[512,128]{1,0:T(8,128)(2,1)S(1)}, bf16[512,128]{1,0:T(8,128)(2,1)S(1)}, u32[]{:S(2)}, u32[]{:S(2)}) collective-permute-start(bf16[512,128]{1,0:T(8,128)(2,1)S(1)} %get-tuple-element.39), channel_id=1, source_target_pairs={{0,4},{4,0},{8,12},{12,8},{16,20},{20,16},{24,28},{28,24},{1,5},{5... | collective-permute-start | bytes 393224 | tf_op jit(solution)/shard_map/ppermute | solution.py:708
  22.5 15.6 %collective-permute-start.14 = (bf16[1040,128]{1,0:T(8,128)(2,1)S(1)}, bf16[1040,128]{1,0:T(8,128)(2,1)S(1)}, u32[]{:S(2)}, u32[]{:S(2)}) collective-permute-start(bf16[1040,128]{1,0:T(8,128)(2,1)S(1)} %get-tuple-element.46.refs_4_), channel_id=1, source_target_pairs={{0,8},{4,12},{8,16},{12,20},{16,24},{20,28},{24,0},{28,4},{1,9},{5... | collective-permute-start | bytes 798728 | tf_op jit(solution)/shard_map/ppermute | solution.py:708
  24.6 21.0 %collective-permute-start.10 = (bf16[1040,128]{1,0:T(8,128)(2,1)S(1)}, bf16[1040,128]{1,0:T(8,128)(2,1)S(1)}, u32[]{:S(2)}, u32[]{:S(2)}) collective-permute-start(bf16[1040,128]{1,0:T(8,128)(2,1)S(1)} %get-tuple-element.46.refs_4_), channel_id=1, source_target_pairs={{0,4},{4,0},{8,12},{12,8},{16,20},{20,16},{24,28},{28,24},{1,5},{5... | collective-permute-start | bytes 798728 | tf_op jit(solution)/shard_map/ppermute | solution.py:708
  24.6 6.8 %collective-permute-start.4 = (bf16[528,128]{1,0:T(8,128)(2,1)S(1)}, bf16[528,128]{1,0:T(8,128)(2,1)S(1)}, u32[]{:S(2)}, u32[]{:S(2)}) collective-permute-start(bf16[528,128]{1,0:T(8,128)(2,1)S(1)} %get-tuple-element.44.refs_5_.refs_1_), channel_id=1, source_target_pairs={{0,8},{4,12},{8,0},{12,4},{16,24},{20,28},{24,16},{28,20},{1,9},{5... | collective-permute-start | bytes 405512 | tf_op jit(solution)/shard_map/ppermute | solution.py:708
  26.1 10.1 %collective-permute-start.3 = (bf16[528,128]{1,0:T(8,128)(2,1)S(1)}, bf16[528,128]{1,0:T(8,128)(2,1)S(1)}, u32[]{:S(2)}, u32[]{:S(2)}) collective-permute-start(bf16[528,128]{1,0:T(8,128)(2,1)S(1)} %row_map.3.refs_5_.refs_1_), channel_id=1, source_target_pairs={{0,8},{4,12},{8,0},{12,4},{16,24},{20,28},{24,16},{28,20},{1,9},{5... | collective-permute-start | bytes 405512 | tf_op jit(solution)/shard_map/ppermute | solution.py:708
  31.4 6.6 %copy-start = (bf16[256,16,128]{2,1,0:T(8,128)(2,1)S(1)}, bf16[256,16,128]{2,1,0:T(8,128)(2,1)}, u32[]{:S(2)}) copy-start(bf16[256,16,128]{2,1,0:T(8,128)(2,1)} %param.10) | copy-start | bytes 3145732
  31.6 10.9 %collective-permute-start.7 = (bf16[528,128]{1,0:T(8,128)(2,1)S(1)}, bf16[528,128]{1,0:T(8,128)(2,1)S(1)}, u32[]{:S(2)}, u32[]{:S(2)}) collective-permute-start(bf16[528,128]{1,0:T(8,128)(2,1)S(1)} %get-tuple-element.47.refs_3_), channel_id=1, source_target_pairs={{0,16},{4,20},{8,24},{12,28},{16,0},{20,4},{24,8},{28,12},{1,17},{... | collective-permute-start | bytes 405512 | tf_op jit(solution)/shard_map/ppermute | solution.py:708
  36.3 7.9 %collective-permute-start.6 = (bf16[528,128]{1,0:T(8,128)(2,1)S(1)}, bf16[528,128]{1,0:T(8,128)(2,1)S(1)}, u32[]{:S(2)}, u32[]{:S(2)}) collective-permute-start(bf16[528,128]{1,0:T(8,128)(2,1)S(1)} %get-tuple-element.48.refs_5_), channel_id=1, source_target_pairs={{0,16},{4,20},{8,24},{12,28},{16,0},{20,4},{24,8},{28,12},{1,17},{... | collective-permute-start | bytes 405512 | tf_op jit(solution)/shard_map/ppermute | solution.py:708
  38.0 14.8 %collective-permute-start.15 = (bf16[1040,128]{1,0:T(8,128)(2,1)S(1)}, bf16[1040,128]{1,0:T(8,128)(2,1)S(1)}, u32[]{:S(2)}, u32[]{:S(2)}) collective-permute-start(bf16[1040,128]{1,0:T(8,128)(2,1)S(1)} %collective-permute-done.14.refs_3_), channel_id=1, source_target_pairs={{0,4},{4,0},{8,12},{12,8},{16,20},{20,16},{24,28},{28,24},{1,5},{5... | collective-permute-start | bytes 798728 | tf_op jit(solution)/shard_map/ppermute | solution.py:708
  42.7 5.2 %collective-permute-start.8 = (bf16[512,128]{1,0:T(8,128)(2,1)S(1)}, bf16[512,128]{1,0:T(8,128)(2,1)S(1)}, u32[]{:S(2)}, u32[]{:S(2)}) collective-permute-start(bf16[512,128]{1,0:T(8,128)(2,1)S(1)} %get-tuple-element.58), channel_id=1, source_target_pairs={{0,4},{4,0},{8,12},{12,8},{16,20},{20,16},{24,28},{28,24},{1,5},{5... | collective-permute-start | bytes 393224 | tf_op jit(solution)/shard_map/ppermute | solution.py:708
  44.4 5.0 %collective-permute-start.9 = (bf16[512,128]{1,0:T(8,128)(2,1)S(1)}, bf16[512,128]{1,0:T(8,128)(2,1)S(1)}, u32[]{:S(2)}, u32[]{:S(2)}) collective-permute-start(bf16[512,128]{1,0:T(8,128)(2,1)S(1)} %get-tuple-element.59), channel_id=1, source_target_pairs={{0,4},{4,0},{8,12},{12,8},{16,20},{20,16},{24,28},{28,24},{1,5},{5... | collective-permute-start | bytes 393224 | tf_op jit(solution)/shard_map/ppermute | solution.py:708
  51.0 6.5 %copy-start.1 = (bf16[256,16,128]{2,1,0:T(8,128)(2,1)S(1)}, bf16[256,16,128]{2,1,0:T(8,128)(2,1)}, u32[]{:S(2)}) copy-start(bf16[256,16,128]{2,1,0:T(8,128)(2,1)} %param.13) | copy-start | bytes 3145732
  51.0 6.5 %copy-start.2 = (f32[16,128]{1,0:T(8,128)S(1)}, f32[16,128]{1,0:T(8,128)}, u32[]{:S(2)}) copy-start(f32[16,128]{1,0:T(8,128)} %refs_0_.1) | copy-start | bytes 24580
  51.0 6.5 %collective-permute-start.11 = (f32[8,256]{1,0:T(8,128)S(1)}, f32[8,256]{1,0:T(8,128)S(1)}, u32[]{:S(2)}, u32[]{:S(2)}) collective-permute-start(f32[8,256]{1,0:T(8,128)S(1)} %get-tuple-element.61.refs_5_.refs_3_), channel_id=1, source_target_pairs={{0,1},{1,0},{2,3},{3,2},{4,5},{5,4},{6,7},{7,6},{8,9},{9,8},{10,11... | collective-permute-start | bytes 24584 | tf_op jit(solution)/shard_map/ppermute | solution.py:810
  51.0 6.4 %collective-permute-start.12 = (f32[8,256]{1,0:T(8,128)S(1)}, f32[8,256]{1,0:T(8,128)S(1)}, u32[]{:S(2)}, u32[]{:S(2)}) collective-permute-start(f32[8,256]{1,0:T(8,128)S(1)} %get-tuple-element.61.refs_5_.refs_3_), channel_id=1, source_target_pairs={{0,2},{1,3},{2,0},{3,1},{4,6},{5,7},{6,4},{7,5},{8,10},{9,11},{10,... | collective-permute-start | bytes 24584 | tf_op jit(solution)/shard_map/ppermute | solution.py:810
  52.6 4.9 %collective-permute-start.13 = (f32[8,256]{1,0:T(8,128)S(1)}, f32[8,256]{1,0:T(8,128)S(1)}, u32[]{:S(2)}, u32[]{:S(2)}) collective-permute-start(f32[8,256]{1,0:T(8,128)S(1)} %get-tuple-element.61.refs_5_.refs_3_), channel_id=1, source_target_pairs={{0,3},{1,2},{2,1},{3,0},{4,7},{5,6},{6,5},{7,4},{8,11},{9,10},{10,... | collective-permute-start | bytes 24584 | tf_op jit(solution)/shard_map/ppermute | solution.py:810

commit v7 on v6

--- a/solution.py
+++ b/solution.py
@@ -26,6 +26,7 @@
 ANYWHERE = pl.BlockSpec(memory_space=pl.ANY)
 STATE_ROWS = HEAD_DIM + 16
 CHUNK = 256
+GROUP_BLOCKS = 4
 
 
 def sds(shape, dtype):
@@ -162,14 +163,16 @@
     )
 
 
-def state_kernel(tokens, heads, pieces, place_ref, *refs):
+def quarter_rows(heads):
+    return heads * HEAD_DIM // GROUP_BLOCKS
+
+
+def state_kernel(tokens, heads, place_ref, *refs):
     refs = list(refs)
     take = lambda n: [refs.pop(0) for _ in range(n)]
-    cumul_ref, doc_ref, key_ref, value_ref, info_ref = take(5)
-    keep_refs, send_refs = take(pieces), take(pieces)
+    cumul_ref, doc_ref, key_ref, value_ref = take(4)
+    out_refs = take(GROUP_BLOCKS)
     kf, vf, states = refs
-    half = heads // 2
-    y = place_ref[0] % 2
     cumul, docs = cumul_ref[...], doc_ref[...]
     total = cumul[tokens - 1 : tokens, :]
     last_row = tokens // LANES - 1
@@ -185,32 +188,26 @@
         states[h * HEAD_DIM : (h + 1) * HEAD_DIM, :] = lax.dot_general(
             keys, values, (((0,), (0,)), ((), ())), preferred_element_type=F32
         )
-    size = half // pieces * HEAD_DIM
-    for p in range(pieces):
-        keep_at = pl.multiple_of((y * pieces + p) * size, size)
-        send_at = pl.multiple_of(((1 - y) * pieces + p) * size, size)
-        keep_refs[p][...] = states[pl.ds(keep_at, size), :].astype(BF16)
-        send_refs[p][0:size, :] = states[pl.ds(send_at, size), :].astype(BF16)
-    upper = pltpu.roll(total, LANES - half, 1)
-
-    def info_of(totals):
-        return info_rows((*in_parts(totals), first_doc, last_doc))
-
-    mine = (y == 0).astype(F32)
-    info_ref[...] = info_of(total * mine + upper * (1.0 - mine))
-    send_refs[0][size : size + INFO, :] = info_of(total * (1.0 - mine) + upper * mine)
-
-
-def block_state(place, cumul, docs, key, value, tokens, heads, pieces):
-    size = heads // 2 // pieces * HEAD_DIM
-    keep = [sds((size, LANES), BF16)] * pieces
-    send = [sds((size + (INFO if p == 0 else 0), LANES), BF16) for p in range(pieces)]
-    out = call(
-        functools.partial(state_kernel, tokens, heads, pieces),
+    size = quarter_rows(heads)
+    mine = place_ref[0] % GROUP_BLOCKS
+    for j, ref in enumerate(out_refs):
+        taker = mine ^ j
+        ref[0:size, :] = states[pl.ds(pl.multiple_of(taker * size, size), size), :].astype(BF16)
+        totals = jnp.zeros_like(total)
+        for c in range(GROUP_BLOCKS):
+            skip = c * heads // GROUP_BLOCKS
+            moved = pltpu.roll(total, LANES - skip, 1) if skip else total
+            totals = jnp.where(taker == c, moved, totals)
+        ref[size : size + INFO, :] = info_rows((*in_parts(totals), first_doc, last_doc))
+
+
+def block_state(place, cumul, docs, key, value, tokens, heads):
+    return call(
+        functools.partial(state_kernel, tokens, heads),
         "block_state",
         [place],
         [cumul, docs, key, value],
-        (sds((INFO, LANES), BF16), *keep, *send),
+        (sds((quarter_rows(heads) + INFO, LANES), BF16),) * GROUP_BLOCKS,
         scratch=[
             pltpu.VMEM((tokens * heads, LANES), F32),
             pltpu.VMEM((tokens * heads, LANES), F32),
@@ -218,7 +215,6 @@
         ],
         estimate=cost(2 * heads * tokens * HEAD_DIM**2, 5 * tokens * heads * LANES * 2),
     )
-    return out[0], out[1 : 1 + pieces], out[1 + pieces :]
 
 
 def in_parts(x):
@@ -240,68 +236,71 @@
     return info[0:1] + info[1:2] + info[2:3], info[3:4], info[4:5]
 
 
-def row_terms(place_ref, own_info, other_info):
-    even = place_ref[0] % 2 == 0
-    own = own_info.astype(F32)
-    other = other_info.astype(F32)
-    a = jnp.where(even, own, other)
-    b = jnp.where(even, other, own)
-    decay_a = jnp.exp(a[0:1] + a[1:2] + a[2:3])
-    decay_b = jnp.exp(b[0:1] + b[1:2] + b[2:3])
-    first_a, last_a = a[3:4], a[4:5]
-    first_b, last_b = b[3:4], b[4:5]
-    whole_a = (first_a == last_a).astype(F32)
-    link_b = ((last_a == first_b) & (first_b == last_b)).astype(F32)
-    return even, decay_a * whole_a, decay_b * link_b, first_a, last_a, last_b
-
-
-def row_kernel(count, first, place_ref, keep_ref, info_ref, other_ref, other_info_ref, *refs):
-    out_ref = refs[len(refs) // 2]
-    if len(refs) > 1:
-        refs[2][...] = refs[0][...]
-    size = count * HEAD_DIM
-    even, gain_a, gain_b, first_a, _, last_b = row_terms(
-        place_ref, info_ref[...], other_info_ref[size : size + INFO, :]
-    )
-    for i in range(count):
-        rows = slice(i * HEAD_DIM, (i + 1) * HEAD_DIM)
-        lane = slice(first + i, first + i + 1)
-        own = keep_ref[rows, :].astype(F32)
-        other = other_ref[rows, :].astype(F32)
-        state_a, state_b = jnp.where(even, own, other), jnp.where(even, other, own)
-        out_ref[rows, :] = (gain_b[:, lane] * state_a + state_b).astype(BF16)
-    out_ref[size : size + INFO, :] = info_rows((*in_parts(gain_a * gain_b), first_a, last_b))
-
-
-def row_map(place, keep, info, other, other_info, first, count, after, relay=None):
-    size = count * HEAD_DIM
+def row_chunks(size):
+    unit = min(HEAD_DIM, size)
+    return [(slice(i * unit, (i + 1) * unit), slice(i, i + 1)) for i in range(size // unit)]
+
+
+def in_block_order(place_ref, refs, blocks):
+    mine = place_ref[0] % GROUP_BLOCKS
+    for j, ref in enumerate(refs):
+        blocks[mine ^ j] = ref[...]
+
+
+def block_maps(blocks, size):
+    maps = []
+    for c in range(GROUP_BLOCKS):
+        info = blocks[c, size : size + INFO, :].astype(F32)
+        first, last = info[3:4], info[4:5]
+        gain = jnp.exp(info[0:1] + info[1:2] + info[2:3]) * (first == last).astype(F32)
+        maps.append((gain, first, last))
+    return maps
+
+
+def group_kernel(size, place_ref, *refs):
+    sources = refs[:GROUP_BLOCKS]
+    out_ref, blocks = refs[-2 - (len(refs) > GROUP_BLOCKS + 2)], refs[-1]
+    if len(refs) > GROUP_BLOCKS + 2:
+        refs[-2][...] = refs[GROUP_BLOCKS][...]
+    in_block_order(place_ref, sources, blocks)
+    maps = block_maps(blocks, size)
+    gains = [None]
+    for (gain, first, _), (_, _, last_before) in zip(maps[1:], maps[:-1]):
+        gains.append(gain * (last_before == first).astype(F32))
+    for rows, lane in row_chunks(size):
+        total = blocks[0, rows, :].astype(F32)
+        for c in range(1, GROUP_BLOCKS):
+            total = gains[c][:, lane] * total + blocks[c, rows, :].astype(F32)
+        out_ref[rows, :] = total.astype(BF16)
+    gain = maps[0][0] * gains[1] * gains[2] * gains[3]
+    out_ref[size : size + INFO, :] = info_rows((*in_parts(gain), maps[0][1], maps[-1][2]))
+
+
+def group_map(place, quarters, size, after, relay):
     relay = [] if relay is None else [relay]
     out = call(
-        functools.partial(row_kernel, count, first),
-        "row_map",
+        functools.partial(group_kernel, size),
+        "group_map",
         [place],
-        [keep, info, other, other_info, *relay],
+        [*quarters, *relay],
         (sds((size + INFO, LANES), BF16), *[sds(x.shape, BF16) for x in relay]),
-        estimate=cost(4 * size * LANES, 4 * size * LANES * 2),
+        scratch=[pltpu.VMEM((GROUP_BLOCKS, size + INFO, LANES), BF16)],
+        estimate=cost(8 * size * LANES, 10 * size * LANES * 2),
         after=after,
     )
-    return out if relay else out[0]
-
-
-def scan_kernel(count, first, has_before, stage, place_ref, *refs):
-    refs = list(refs)
+    return out if relay else (out[0], None)
+
+
+def scan_kernel(size, has_before, bit, place_ref, *refs):
     mine_ref, came_ref = refs[:2]
     before_ref = refs[2] if has_before else None
     run_ref, out_ref = refs[-2:]
-    size = count * HEAD_DIM
-    upper = (place_ref[0] >> stage) & 1 == 1
+    upper = (place_ref[0] >> bit) & 1 == 1
     gain_m, first_m, last_m = read_map(mine_ref, size)
     gain_c, first_c, last_c = read_map(came_ref, size)
     link = jnp.where(upper, (last_c == first_m).astype(F32), (last_m == first_c).astype(F32))
     gain = jnp.where(upper, gain_m, gain_c) * link
-    for i in range(count):
-        rows = slice(i * HEAD_DIM, (i + 1) * HEAD_DIM)
-        lane = slice(first + i, first + i + 1)
+    for rows, lane in row_chunks(size):
         mine, came = mine_ref[rows, :].astype(F32), came_ref[rows, :].astype(F32)
         lower_sum, upper_sum = jnp.where(upper, came, mine), jnp.where(upper, mine, came)
         run_ref[rows, :] = (gain[:, lane] * lower_sum + upper_sum).astype(BF16)
@@ -318,9 +317,7 @@
     gain_b, first_b, last_b = read_map(before_ref, size)
     empty = first_b == 0.0
     factor = jnp.where(empty, 1.0, gain_b * (last_c == first_b).astype(F32))
-    for i in range(count):
-        rows = slice(i * HEAD_DIM, (i + 1) * HEAD_DIM)
-        lane = slice(first + i, first + i + 1)
+    for rows, lane in row_chunks(size):
         before = before_ref[rows, :].astype(F32)
         joined = factor[:, lane] * came_ref[rows, :].astype(F32) + before
         out_ref[rows, :] = jnp.where(upper, joined, before).astype(BF16)
@@ -333,12 +330,11 @@
     )
 
 
-def scan_step(place, stage, mine, came, before, first, count, after):
-    size = count * HEAD_DIM
+def scan_step(place, bit, mine, came, before, size, after):
     shape = sds((size + INFO, LANES), BF16)
     before = [] if before is None else [before]
     return call(
-        functools.partial(scan_kernel, count, first, len(before), stage),
+        functools.partial(scan_kernel, size, len(before), bit),
         "scan_step",
         [place],
         [mine, came, *before],
@@ -348,50 +344,53 @@
     )
 
 
-def prior_kernel(count, first, has_before, stage, wants_doc, place_ref, *refs):
-    keep_ref, info_ref, other_ref, other_info_ref, came_ref = refs[:5]
-    before_ref = refs[5] if has_before else None
-    mine_ref, send_ref = refs[-3:-1] if wants_doc else refs[-2:]
-    size = count * HEAD_DIM
-    upper = ((place_ref[0] >> stage) & 1).astype(F32)
-    even, gain_a, _, first_a, last_a, _ = row_terms(
-        place_ref, info_ref[...], other_info_ref[size : size + INFO, :]
-    )
+def prior_kernel(size, has_before, bit, place_ref, *refs):
+    sources, came_ref = refs[:GROUP_BLOCKS], refs[GROUP_BLOCKS]
+    before_ref = refs[GROUP_BLOCKS + 1] if has_before else None
+    out_refs, doc_ref = refs[-GROUP_BLOCKS - 3 : -3], refs[-3]
+    blocks, priors = refs[-2:]
+    mine = place_ref[0] % GROUP_BLOCKS
+    in_block_order(place_ref, sources, blocks)
+    maps = block_maps(blocks, size)
+    upper = ((place_ref[0] >> bit) & 1).astype(F32)
     _, _, last_c = read_map(came_ref, size)
-    factor, doc = upper, upper * last_c
+    factor, doc = jnp.broadcast_to(upper, (1, LANES)), upper * last_c
     if has_before:
         gain_b, first_b, last_b = read_map(before_ref, size)
         empty = first_b == 0.0
         factor = upper * jnp.where(empty, 1.0, gain_b * (last_c == first_b).astype(F32))
         doc = jnp.where(empty, doc, last_b)
-    else:
-        factor = jnp.broadcast_to(factor, (1, LANES))
-    gain_a = gain_a * (doc == first_a).astype(F32)
-    for i in range(count):
-        rows = slice(i * HEAD_DIM, (i + 1) * HEAD_DIM)
-        lane = slice(first + i, first + i + 1)
-        before_a = factor[:, lane] * came_ref[rows, :].astype(F32)
+    docs = [doc] + [last for _, _, last in maps[:-1]]
+    gains = [gain * (doc == first).astype(F32) for (gain, first, _), doc in zip(maps, docs)]
+    for rows, lane in row_chunks(size):
+        state = factor[:, lane] * came_ref[rows, :].astype(F32)
         if has_before:
-            before_a = before_a + before_ref[rows, :].astype(F32)
-        state_a = jnp.where(even, keep_ref[rows, :].astype(F32), other_ref[rows, :].astype(F32))
-        before_b = gain_a[:, lane] * before_a + state_a
-        mine_ref[rows, :] = jnp.where(even, before_a, before_b).astype(BF16)
-        send_ref[rows, :] = jnp.where(even, before_b, before_a).astype(BF16)
-    if wants_doc:
-        refs[-1][...] = jnp.broadcast_to(jnp.where(even, doc, last_a), (8, LANES))
-
-
-def prior_states(place, stage, keep, info, other, other_info, came, before, first, count, after, wants_doc):
-    size = count * HEAD_DIM
-    docs = (sds((8, LANES), F32),) if wants_doc else ()
+            state = state + before_ref[rows, :].astype(F32)
+        for c in range(GROUP_BLOCKS):
+            priors[c, rows, :] = state.astype(BF16)
+            if c < GROUP_BLOCKS - 1:
+                state = gains[c][:, lane] * state + blocks[c, rows, :].astype(F32)
+    for j, ref in enumerate(out_refs):
+        ref[...] = priors[mine ^ j]
+    own_doc = docs[0]
+    for c in range(1, GROUP_BLOCKS):
+        own_doc = jnp.where(mine == c, docs[c], own_doc)
+    doc_ref[...] = jnp.broadcast_to(own_doc, (8, LANES))
+
+
+def prior_states(place, bit, quarters, came, before, size, after):
     before = [] if before is None else [before]
     return call(
-        functools.partial(prior_kernel, count, first, len(before), stage, wants_doc),
+        functools.partial(prior_kernel, size, len(before), bit),
         "prior_states",
         [place],
-        [keep, info, other, other_info, came, *before],
-        (sds((size, LANES), BF16), sds((size, LANES), BF16), *docs),
-        estimate=cost(4 * size * LANES, 6 * size * LANES * 2),
+        [*quarters, came, *before],
+        (*[sds((size, LANES), BF16)] * GROUP_BLOCKS, sds((8, LANES), F32)),
+        scratch=[
+            pltpu.VMEM((GROUP_BLOCKS, size + INFO, LANES), BF16),
+            pltpu.VMEM((GROUP_BLOCKS, size, LANES), BF16),
+        ],
+        estimate=cost(8 * size * LANES, 10 * size * LANES * 2),
         after=after,
     )
 
@@ -449,25 +448,22 @@
     )
 
 
-def mix_kernel(tokens, heads, parts, pieces, place_ref, doc_ref, prior_doc_ref, cumul_ref, *refs):
+def mix_kernel(tokens, heads, parts, place_ref, doc_ref, prior_doc_ref, cumul_ref, *refs):
     refs = list(refs)
     take = lambda n: [refs.pop(0) for _ in range(n)]
-    inner, qh, mine, other = take(parts), take(parts), take(pieces), take(pieces)
-    mixed_ref, square_ref = refs
-    half = heads // 2
-    count = half // pieces
-    even = place_ref[0] % 2 == 0
+    inner, qh, quarters = take(parts), take(parts), take(GROUP_BLOCKS)
+    mixed_ref, square_ref, states = refs
+    size = quarter_rows(heads)
+    mine = place_ref[0] % GROUP_BLOCKS
+    for j, ref in enumerate(quarters):
+        states[pl.ds(pl.multiple_of((mine ^ j) * size, size), size), :] = ref[...]
     is_open = (doc_columns(doc_ref[...], tokens) == prior_doc_ref[0:1, :]).astype(F32)
     gain = jnp.exp(cumul_ref[...]) * is_open
     squares = jnp.zeros((tokens, LANES), F32)
     for h in range(heads):
-        piece, i = divmod(h % half, count)
-        rows = slice(i * HEAD_DIM, (i + 1) * HEAD_DIM)
-        near, far = mine[piece][rows, :], other[piece][rows, :]
-        lower = h < half
-        state = jnp.where(even, near if lower else far, far if lower else near)
         part, n = divmod(h, heads // parts)
         held = slice(n * tokens, (n + 1) * tokens)
+        state = states[h * HEAD_DIM : (h + 1) * HEAD_DIM, :]
         carried = jnp.dot(qh[part][held, :], state, preferred_element_type=F32)
         mixed = inner[part][held, :] + carried * gain[:, h : h + 1]
         squares = squares + mixed * mixed
@@ -481,13 +477,14 @@
     )
 
 
-def mix(place, docs, prior_doc, cumul, inner, qh, mine, other, tokens, heads, after):
+def mix(place, docs, prior_doc, cumul, inner, qh, quarters, tokens, heads, after):
     return call(
-        functools.partial(mix_kernel, tokens, heads, len(inner), len(mine)),
+        functools.partial(mix_kernel, tokens, heads, len(inner)),
         "mix",
         [place],
-        [docs, prior_doc, cumul, *inner, *qh, *mine, *other],
+        [docs, prior_doc, cumul, *inner, *qh, *quarters],
         (sds((tokens * heads, LANES), F32), sds((8, tokens), F32)),
+        scratch=[pltpu.VMEM((heads * HEAD_DIM, LANES), BF16)],
         mib=24,
         estimate=cost(2 * heads * tokens * HEAD_DIM**2, tokens * heads * LANES * 10),
         after=after,
@@ -693,10 +690,7 @@
     tokens, heads, _ = lin_query.shape
     tensor = HEADS // heads
     kv_here = max(1, heads // GROUP)
-    half = heads // 2
-    pieces = 2 if half % 2 == 0 else 1
-    parts = 2 if half % 8 == 0 else 1
-    count = half // pieces
+    parts = 2 if heads % 16 == 0 else 1
     longest = blocks * tokens * 5 // 8
     window = min(blocks - 1, (longest - 1 + tokens - 1) // tokens)
     flat = lambda x: x.reshape(-1, LANES)
@@ -731,8 +725,10 @@
     beside = send(own_kv, [(b, b + (1 if b % 2 == 0 else window if odd_window else -1)) for b in everyone])
     beside = (beside, (window if odd_window else blocks, 1))
 
-    info, held, sent = block_state(place, cumul, docs, key, value, tokens, heads, pieces)
-    came = [send(x, swap) for x in sent]
+    size = quarter_rows(heads)
+    others = range(1, GROUP_BLOCKS)
+    sent = block_state(place, cumul, docs, key, value, tokens, heads)
+    quarters = [sent[0]] + [send(sent[j], [(b, b ^ j) for b in everyone]) for j in others]
 
     state = {}
 
@@ -759,52 +755,28 @@
         qh.append(got[1])
         return got[0]
 
-    beside_work = [first_attention]
-    beside_work.append(lambda after: more_attention([beside] + lane_kv[:1], False, after))
-    beside_work += [functools.partial(inner_of, part) for part in range(parts)]
+    done = first_attention([sent[0]])
+    run, ahead = group_map(place, quarters, size, [done], ahead)
     lane_kv, cross_kv = [], []
-
-    done = info
-    mine, far = [], []
-    run, before = [None] * pieces, [None] * pieces
-    stages = (blocks // 2).bit_length() - 1
-    for stage in range(stages + 1):
-        if beside_work:
-            done = beside_work.pop(0)([done])
-        if stage == stages:
-            while beside_work:
-                done = beside_work.pop(0)([done])
-        for p in range(pieces):
-            at = (p * count, count, [done])
-            if stage == 0:
-                args = (place, held[p], info, came[p], came[0], *at)
-                if p == 0:
-                    run[p], ahead = row_map(*args, ahead)
-                    for back in range(1, window // 2 + 1):
-                        lane_kv.append((ahead, (2 * back, 2 * back)))
-                        cross_kv.append((send(ahead, swap), (2 * back, 2 * back + 1)))
-                        ahead = send(ahead, forward)
-                else:
-                    run[p] = row_map(*args)
-                done = run[p]
-            elif stage < stages:
-                run[p], before[p] = scan_step(place, stage, run[p], got[p], before[p], *at)
-                done = run[p]
-            else:
-                wants_doc = p == pieces - 1
-                done, sent, *docs_before = prior_states(
-                    place, stage, held[p], info, came[p], came[0], got[p], before[p], *at, wants_doc
-                )
-                mine.append(done)
-                far.append(send(sent, swap))
-        if stage < stages:
-            got = [send(x, [(b, b ^ (2 << stage)) for b in everyone]) for x in run]
+    for back in range(1, window // 2 + 1):
+        lane_kv.append((ahead, (2 * back, 2 * back)))
+        cross_kv.append((send(ahead, swap), (2 * back, 2 * back + 1)))
+        ahead = send(ahead, forward)
+    stages = (blocks // GROUP_BLOCKS).bit_length() - 1
+    before, done = None, run
+    for stage in range(stages):
+        came = send(run, [(b, b ^ (GROUP_BLOCKS << stage)) for b in everyone])
+        if stage == stages - 1:
+            for part in range(parts):
+                done = inner_of(part, [done])
+        else:
+            run, before = scan_step(place, stage + 2, run, came, before, size, [done])
+            done = run
+    *priors, prior_doc = prior_states(place, stages + 1, quarters, came, before, size, [done])
+    priors = [priors[0]] + [send(priors[j], [(b, b ^ j) for b in everyone]) for j in others]
+    done = more_attention([beside] + lane_kv[:1], False, [prior_doc])
     rest = [kv for pair in zip(cross_kv, lane_kv[1:] + [None]) for kv in pair if kv is not None]
-    done = more_attention(rest[:1], False, [done])
-    rest = rest[1:]
-    mixed, squares = mix(
-        place, docs, docs_before[0], cumul, inner, qh, mine, far, tokens, heads, [done]
-    )
+    mixed, squares = mix(place, docs, prior_doc, cumul, inner, qh, priors, tokens, heads, [done])
     sums = [squares]
     for other in range(1, tensor):
         sums.append(lax.ppermute(squares, "tp", [(t, t ^ other) for t in range(tensor)]))

time: 59.5 us -> 58.9 us (0.990)
  waiting for transfers between devices: 8.94 us -> 12.8 us
  starting transfers between devices: 20.9 us -> 17.7 us
  Pallas kernels: 28.5 us -> 27.2 us
    ppermute x13 -> x12, waiting for transfers between devices: 8.93 us -> 12.8 us  [send(): return lax.ppermute(x, 'seq', [(a, b % blocks) for a, b in pairs])]
    ppermute x13 -> x12, starting transfers between devices: 19 us -> 15.8 us  [send(): return lax.ppermute(x, 'seq', [(a, b % blocks) for a, b in pairs])]
    pallas_call x16 -> x12, Pallas kernels: 28.5 us -> 27.2 us  [call(): pl.pallas_call(run, out_shape=outs, in_specs=[SMEM] * len(scalars) + [HBM...]
  transfers between devices with their start and end apart: 16 -> 15, of which waited for: 4 -> 4; matrix products, arithmetic and copies ran while one was open for 0% -> 0% of each run, Pallas kernels for 41% -> 39%
where the time goes in v7:
time: 58.9 us; the launch traced here: 58.7 us
  Pallas kernels  27.2 us (46%)
  starting transfers between devices  17.7 us (30%)
  waiting for transfers between devices  12.8 us (22%)
  between operations  1 us (2%)
    pallas_call x12, Pallas kernels, call(): pl.pallas_call(run, out_shape=outs, in_specs=[SMEM] * len(scalars) + [HBM...  27.2 us
    ppermute x12, starting transfers between devices, send(): return lax.ppermute(x, 'seq', [(a, b % blocks) for a, b in pairs])  15.8 us
    ppermute x12, waiting for transfers between devices, send(): return lax.ppermute(x, 'seq', [(a, b % blocks) for a, b in pairs])  12.8 us
    ppermute x3, starting transfers between devices, body(): lax.ppermute(squares, 'tp', [(t, t ^ other) for t in range(tensor)])  1.89 us
  transfers between devices with their start and end apart: 15, of which 4 were waited for; matrix products, arithmetic and copies ran while one was open for 0% of the time, Pallas kernels for 39%

profile of v7, /device:TPU:0, one launch (start us, length us, event | category | flops | bytes accessed | tf_op | source)
XLA Modules:
  0.0 58.7 jit_solution(629685549749770981)
XLA Ops:
  0.6 0.0 copy-start.3
  0.7 2.7 %fetch.1 = (bf16[1040,128]{1,0:T(8,128)(2,1)}, f32[16,128]{1,0:T(8,128)S(1)}, f32[256,128]{1,0:T(8,128)S(1)}, bf16[4096,128]{1,0:T(8,128)(2,1)S(1)}, bf16[4096,128]{1,0:T(8,128)(2,1)S(1)}) custom-call(s32[1]{0:T(128)} %bitcast.2.refs_0_, s32[2,128]{1,0:T(2,128)} %bitcast.23, f32[16,256]{1,0:T(8,128)} %bitcast.22, bf16[2048,128]{1,0:T(8,128)(2,1)} %bitcast.20, ...), custom_call_target="tpu_custom_call" | custom-call | bytes 3145728 | tf_op jit(solution)/shard_map/fetch/pallas_call | solution.py:59
  3.4 3.1 %collective-permute-start.3 = (bf16[1040,128]{1,0:T(8,128)(2,1)}, bf16[1040,128]{1,0:T(8,128)(2,1)S(1)}, u32[]{:S(2)}, u32[]{:S(2)}) collective-permute-start(bf16[1040,128]{1,0:T(8,128)(2,1)} %get-tuple-element.36.refs_3_), channel_id=1, source_target_pairs={{0,8},{4,12},{8,16},{12,20},{16,24},{20,28},{24,0},{28,4},{1,9},{5... | collective-permute-start | bytes 798728 | tf_op jit(solution)/shard_map/ppermute | solution.py:702
  6.5 2.7 %block_state.1 = (bf16[528,128]{1,0:T(8,128)(2,1)S(1)}, bf16[528,128]{1,0:T(8,128)(2,1)S(1)}, bf16[528,128]{1,0:T(8,128)(2,1)S(1)}, bf16[528,128]{1,0:T(8,128)(2,1)S(1)}) custom-call(s32[1]{0:T(128)} %bitcast.1.refs_0_, f32[256,128]{1,0:T(8,128)S(1)} %get-tuple-element.29.refs_1_.refs_0_.refs_3_, f32[16,128]{1,0:T(8,128)S(1)} %get-tuple-element.28.refs_2_.refs_1_, ...), custom_call_target="tpu_custom_call" | custom-call | flops 134217728 | bytes 5242880 | tf_op jit(solution)/shard_map/block_state/pallas_call | solution.py:59
  9.2 1.6 %collective-permute-start = (bf16[528,128]{1,0:T(8,128)(2,1)S(1)}, bf16[528,128]{1,0:T(8,128)(2,1)S(1)}, u32[]{:S(2)}, u32[]{:S(2)}) collective-permute-start(bf16[528,128]{1,0:T(8,128)(2,1)S(1)} %get-tuple-element.33), channel_id=1, source_target_pairs={{0,4},{4,0},{8,12},{12,8},{16,20},{20,16},{24,28},{28,24},{1,5},{5... | collective-permute-start | bytes 405512 | tf_op jit(solution)/shard_map/ppermute | solution.py:702
  10.8 1.6 %collective-permute-start.1 = (bf16[528,128]{1,0:T(8,128)(2,1)S(1)}, bf16[528,128]{1,0:T(8,128)(2,1)S(1)}, u32[]{:S(2)}, u32[]{:S(2)}) collective-permute-start(bf16[528,128]{1,0:T(8,128)(2,1)S(1)} %get-tuple-element.34), channel_id=1, source_target_pairs={{0,8},{4,12},{8,0},{12,4},{16,24},{20,28},{24,16},{28,20},{1,9},{5... | collective-permute-start | bytes 405512 | tf_op jit(solution)/shard_map/ppermute | solution.py:702
  12.4 0.4 collective-permute-start.2
  12.8 1.5 %collective-permute-start.8 = (bf16[1040,128]{1,0:T(8,128)(2,1)}, bf16[1040,128]{1,0:T(8,128)(2,1)S(1)}, u32[]{:S(2)}, u32[]{:S(2)}) collective-permute-start(bf16[1040,128]{1,0:T(8,128)(2,1)} %get-tuple-element.36.refs_3_), channel_id=1, source_target_pairs={{0,4},{4,24},{8,12},{12,0},{16,20},{20,8},{24,28},{28,16},{1,5},{5... | collective-permute-start | bytes 798728 | tf_op jit(solution)/shard_map/ppermute | solution.py:702
  14.3 0.0 copy-done.3
  14.3 3.6 %attend.4 = (bf16[2,2048,256]{2,1,0:T(8,128)(2,1)S(1)}, f32[2,144,2048]{2,1,0:T(8,128)S(1)}) custom-call(s32[1]{0:T(128)} %bitcast.1.refs_0_, f32[16,128]{1,0:T(8,128)S(1)} %get-tuple-element.28.refs_2_.refs_1_, bf16[4096,128]{1,0:T(8,128)(2,1)S(1)} %bitcast.16, bf16[1040,128]{1,0:T(8,128)(2,1)} %get-tuple-element.36.refs_3_, ...), custom_call_target="tpu_custom_call" | custom-call | flops 1073741824 | bytes 8388608 | tf_op jit(solution)/shard_map/attend/pallas_call | solution.py:59
  17.9 0.0 copy-start
  17.9 0.0 collective-permute-done.refs_2_
  17.9 0.2 collective-permute-done.1.refs_3_
  18.1 3.9 %collective-permute-done.2.refs_4_ = bf16[528,128]{1,0:T(8,128)(2,1)S(1)} collective-permute-done((bf16[528,128]{1,0:T(8,128)(2,1)S(1)}, bf16[528,128]{1,0:T(8,128)(2,1)S(1)}, u32[]{:S(2)}, u32[]{:S(2)}) %collective-permute-start.2) | collective-permute-done | bytes 135200 | tf_op jit(solution)/shard_map/ppermute | solution.py:702
  21.9 0.0 collective-permute-done.3.refs_5_
  21.9 0.2 group_map.1
  22.2 2.3 %collective-permute-start.13 = (bf16[1040,128]{1,0:T(8,128)(2,1)S(1)}, bf16[1040,128]{1,0:T(8,128)(2,1)S(1)}, u32[]{:S(2)}, u32[]{:S(2)}) collective-permute-start(bf16[1040,128]{1,0:T(8,128)(2,1)S(1)} %get-tuple-element.49.refs_4_), channel_id=1, source_target_pairs={{0,8},{4,12},{8,16},{12,20},{16,24},{20,28},{24,0},{28,4},{1,9},{5... | collective-permute-start | bytes 798728 | tf_op jit(solution)/shard_map/ppermute | solution.py:702
  24.5 1.2 %collective-permute-start.4 = (bf16[528,128]{1,0:T(8,128)(2,1)S(1)}, bf16[528,128]{1,0:T(8,128)(2,1)S(1)}, u32[]{:S(2)}, u32[]{:S(2)}) collective-permute-start(bf16[528,128]{1,0:T(8,128)(2,1)S(1)} %get-tuple-element.38.refs_5_), channel_id=1, source_target_pairs={{0,16},{4,20},{8,24},{12,28},{16,0},{20,4},{24,8},{28,12},{1,17},{... | collective-permute-start | bytes 405512 | tf_op jit(solution)/shard_map/ppermute | solution.py:702
  25.7 0.0 collective-permute-start.12
  25.7 0.0 copy-done
  25.7 1.9 %inner_part.2 = (f32[2048,128]{1,0:T(8,128)S(1)}, bf16[2048,128]{1,0:T(8,128)(2,1)S(1)}) custom-call(f32[256,128]{1,0:T(8,128)S(1)} %get-tuple-element.29.refs_1_.refs_0_.refs_3_, f32[16,128]{1,0:T(8,128)S(1)} %get-tuple-element.28.refs_2_.refs_1_, bf16[4096,128]{1,0:T(8,128)(2,1)S(1)} %bitcast.13, bf16[4096,128]{1,0:T(8,128)(2,1)S(1)} %get-tuple-element.30.refs_3_, ...), custom_call_target="tpu_custom_call" | custom-call | flops 268435456 | bytes 6291456 | tf_op jit(solution)/shard_map/inner_part/pallas_call | solution.py:59
  27.6 1.9 %inner_part.3 = (f32[2048,128]{1,0:T(8,128)S(1)}, bf16[2048,128]{1,0:T(8,128)(2,1)S(1)}) custom-call(f32[256,128]{1,0:T(8,128)S(1)} %get-tuple-element.29.refs_1_.refs_0_.refs_3_, f32[16,128]{1,0:T(8,128)S(1)} %get-tuple-element.28.refs_2_.refs_1_, bf16[4096,128]{1,0:T(8,128)(2,1)S(1)} %bitcast.14, bf16[4096,128]{1,0:T(8,128)(2,1)S(1)} %get-tuple-element.30.refs_3_, ...), custom_call_target="tpu_custom_call" | custom-call | flops 268435456 | bytes 6291456 | tf_op jit(solution)/shard_map/inner_part/pallas_call | solution.py:59
  29.5 7.9 %collective-permute-done.4.refs_5_ = bf16[528,128]{1,0:T(8,128)(2,1)S(1)} collective-permute-done((bf16[528,128]{1,0:T(8,128)(2,1)S(1)}, bf16[528,128]{1,0:T(8,128)(2,1)S(1)}, u32[]{:S(2)}, u32[]{:S(2)}) %collective-permute-start.4) | collective-permute-done | bytes 135200 | tf_op jit(solution)/shard_map/ppermute | solution.py:702
  37.4 0.3 prior_states.1
  37.7 0.7 %collective-permute-start.5 = (bf16[512,128]{1,0:T(8,128)(2,1)S(1)}, bf16[512,128]{1,0:T(8,128)(2,1)S(1)}, u32[]{:S(2)}, u32[]{:S(2)}) collective-permute-start(bf16[512,128]{1,0:T(8,128)(2,1)S(1)} %get-tuple-element.45), channel_id=1, source_target_pairs={{0,4},{4,0},{8,12},{12,8},{16,20},{20,16},{24,28},{28,24},{1,5},{5... | collective-permute-start | bytes 393224 | tf_op jit(solution)/shard_map/ppermute | solution.py:702
  38.3 0.6 %collective-permute-start.6 = (bf16[512,128]{1,0:T(8,128)(2,1)S(1)}, bf16[512,128]{1,0:T(8,128)(2,1)S(1)}, u32[]{:S(2)}, u32[]{:S(2)}) collective-permute-start(bf16[512,128]{1,0:T(8,128)(2,1)S(1)} %get-tuple-element.46), channel_id=1, source_target_pairs={{0,8},{4,12},{8,0},{12,4},{16,24},{20,28},{24,16},{28,20},{1,9},{5... | collective-permute-start | bytes 393224 | tf_op jit(solution)/shard_map/ppermute | solution.py:702
  38.9 0.0 collective-permute-done.8.refs_3_
  39.0 2.3 %collective-permute-start.7 = (bf16[512,128]{1,0:T(8,128)(2,1)S(1)}, bf16[512,128]{1,0:T(8,128)(2,1)S(1)}, u32[]{:S(2)}, u32[]{:S(2)}) collective-permute-start(bf16[512,128]{1,0:T(8,128)(2,1)S(1)} %get-tuple-element.47), channel_id=1, source_target_pairs={{0,12},{4,8},{8,4},{12,0},{16,28},{20,24},{24,20},{28,16},{1,13},{... | collective-permute-start | bytes 393224 | tf_op jit(solution)/shard_map/ppermute | solution.py:702
  41.2 0.0 collective-permute-done.13.refs_4_
  41.2 0.6 %collective-permute-start.14 = (bf16[1040,128]{1,0:T(8,128)(2,1)S(1)}, bf16[1040,128]{1,0:T(8,128)(2,1)S(1)}, u32[]{:S(2)}, u32[]{:S(2)}) collective-permute-start(bf16[1040,128]{1,0:T(8,128)(2,1)S(1)} %collective-permute-done.13.refs_4_), channel_id=1, source_target_pairs={{0,4},{4,0},{8,12},{12,8},{16,20},{20,16},{24,28},{28,24},{1,5},{5... | collective-permute-start | bytes 798728 | tf_op jit(solution)/shard_map/ppermute | solution.py:702
  41.8 3.7 %attend.5.refs_12_.refs_2_ = f32[2,144,2048]{2,1,0:T(8,128)S(1)} custom-call(s32[1]{0:T(128)} %bitcast.1.refs_0_, bf16[2,2048,256]{2,1,0:T(8,128)(2,1)S(1)} %get-tuple-element.48.refs_1_, f32[2,144,2048]{2,1,0:T(8,128)S(1)} %get-tuple-element.37.refs_6_.refs_2_, bf16[1040,128]{1,0:T(8,128)(2,1)S(1)} %collective-permute-done.8.refs_3_, ...), custom_call_target="tpu_custom_call" | custom-call | flops 2147483648 | bytes 8388608 | tf_op jit(solution)/shard_map/attend/pallas_call | solution.py:59
  45.5 0.0 collective-permute-done.5.refs_9_
  45.5 0.0 collective-permute-done.6.refs_10_
  45.5 0.8 %collective-permute-done.7.refs_11_ = bf16[512,128]{1,0:T(8,128)(2,1)S(1)} collective-permute-done((bf16[512,128]{1,0:T(8,128)(2,1)S(1)}, bf16[512,128]{1,0:T(8,128)(2,1)S(1)}, u32[]{:S(2)}, u32[]{:S(2)}) %collective-permute-start.7) | collective-permute-done | bytes 131104 | tf_op jit(solution)/shard_map/ppermute | solution.py:702
  46.4 1.6 %mix.1 = (f32[4096,128]{1,0:T(8,128)S(1)}, f32[8,256]{1,0:T(8,128)S(1)}) custom-call(s32[1]{0:T(128)} %bitcast.1.refs_0_, f32[16,128]{1,0:T(8,128)S(1)} %get-tuple-element.28.refs_2_.refs_1_, f32[8,128]{1,0:T(8,128)S(1)} %get-tuple-element.41.refs_5_.refs_2_, f32[256,128]{1,0:T(8,128)S(1)} %get-tuple-element.29.refs_1_.refs_0_.refs_3_, ...), custom_call_target="tpu_custom_call" | custom-call | flops 134217728 | bytes 5242880 | tf_op jit(solution)/shard_map/mix/pallas_call | solution.py:59
  48.0 0.0 collective-permute-start.9
  48.0 1.5 %collective-permute-start.10 = (f32[8,256]{1,0:T(8,128)S(1)}, f32[8,256]{1,0:T(8,128)S(1)}, u32[]{:S(2)}, u32[]{:S(2)}) collective-permute-start(f32[8,256]{1,0:T(8,128)S(1)} %get-tuple-element.51.refs_5_.refs_3_), channel_id=1, source_target_pairs={{0,2},{1,3},{2,0},{3,1},{4,6},{5,7},{6,4},{7,5},{8,10},{9,11},{10,... | collective-permute-start | bytes 24584 | tf_op jit(solution)/shard_map/ppermute | solution.py:782
  49.5 0.4 collective-permute-start.11
  49.8 0.0 collective-permute-done.12.refs_3_
  49.8 3.7 %attend.6.refs_2_ = f32[2,144,2048]{2,1,0:T(8,128)S(1)} custom-call(s32[1]{0:T(128)} %bitcast.1.refs_0_, bf16[2,2048,256]{2,1,0:T(8,128)(2,1)S(1)} %get-tuple-element.48.refs_1_, f32[2,144,2048]{2,1,0:T(8,128)S(1)} %attend.5.refs_12_.refs_2_, bf16[1040,128]{1,0:T(8,128)(2,1)S(1)} %collective-permute-done.12.refs_3_, ...), custom_call_target="tpu_custom_call" | custom-call | flops 2147483648 | bytes 8388608 | tf_op jit(solution)/shard_map/attend/pallas_call | solution.py:59
  53.5 0.0 copy-start.1
  53.5 0.0 copy-start.2
  53.6 0.0 collective-permute-done.14.refs_3_
  53.6 3.3 %attend.7 = (bf16[4096,128]{1,0:T(8,128)(2,1)}, f32[8,128]{1,0:T(8,128)S(1)}) custom-call(s32[1]{0:T(128)} %bitcast.1.refs_0_, bf16[2,2048,256]{2,1,0:T(8,128)(2,1)S(1)} %get-tuple-element.48.refs_1_, f32[2,144,2048]{2,1,0:T(8,128)S(1)} %attend.6.refs_2_, bf16[1040,128]{1,0:T(8,128)(2,1)S(1)} %collective-permute-done.14.refs_3_), custom_call_target="tpu_custom_call" | custom-call | flops 1073741824 | bytes 8388608 | tf_op jit(solution)/shard_map/attend/pallas_call | solution.py:59
  56.9 0.0 collective-permute-done.9.refs_4_
  56.9 0.0 collective-permute-done.10.refs_5_
  56.9 0.0 collective-permute-done.11.refs_6_
  56.9 1.6 %finish.1 = bf16[4096,128]{1,0:T(8,128)(2,1)} custom-call(f32[16,128]{1,0:T(8,128)S(1)} %copy-done.2, bf16[4096,128]{1,0:T(8,128)(2,1)S(1)} %bitcast.15, f32[4096,128]{1,0:T(8,128)S(1)} %get-tuple-element.50.refs_2_, f32[8,256]{1,0:T(8,128)S(1)} %get-tuple-element.51.refs_5_.refs_3_, f32[8,256]{1,0:T(8,128)S(1)} %collective-permute-done.9.refs_4_, ...), custom_call_target="tpu_custom_call" | custom-call | bytes 4194304 | tf_op jit(solution)/shard_map/finish/pallas_call | solution.py:59
  (2 shorter events, 0.0 us)
Async XLA Ops:
  0.6 13.6 %copy-start.3 = (bf16[256,16,128]{2,1,0:T(8,128)(2,1)S(1)}, bf16[256,16,128]{2,1,0:T(8,128)(2,1)}, u32[]{:S(2)}) copy-start(bf16[256,16,128]{2,1,0:T(8,128)(2,1)} %param.17) | copy-start | bytes 3145732
  3.4 18.6 %collective-permute-start.3 = (bf16[1040,128]{1,0:T(8,128)(2,1)}, bf16[1040,128]{1,0:T(8,128)(2,1)S(1)}, u32[]{:S(2)}, u32[]{:S(2)}) collective-permute-start(bf16[1040,128]{1,0:T(8,128)(2,1)} %get-tuple-element.36.refs_3_), channel_id=1, source_target_pairs={{0,8},{4,12},{8,16},{12,20},{16,24},{20,28},{24,0},{28,4},{1,9},{5... | collective-permute-start | bytes 798728 | tf_op jit(solution)/shard_map/ppermute | solution.py:702
  9.2 8.7 %collective-permute-start = (bf16[528,128]{1,0:T(8,128)(2,1)S(1)}, bf16[528,128]{1,0:T(8,128)(2,1)S(1)}, u32[]{:S(2)}, u32[]{:S(2)}) collective-permute-start(bf16[528,128]{1,0:T(8,128)(2,1)S(1)} %get-tuple-element.33), channel_id=1, source_target_pairs={{0,4},{4,0},{8,12},{12,8},{16,20},{20,16},{24,28},{28,24},{1,5},{5... | collective-permute-start | bytes 405512 | tf_op jit(solution)/shard_map/ppermute | solution.py:702
  10.8 7.3 %collective-permute-start.1 = (bf16[528,128]{1,0:T(8,128)(2,1)S(1)}, bf16[528,128]{1,0:T(8,128)(2,1)S(1)}, u32[]{:S(2)}, u32[]{:S(2)}) collective-permute-start(bf16[528,128]{1,0:T(8,128)(2,1)S(1)} %get-tuple-element.34), channel_id=1, source_target_pairs={{0,8},{4,12},{8,0},{12,4},{16,24},{20,28},{24,16},{28,20},{1,9},{5... | collective-permute-start | bytes 405512 | tf_op jit(solution)/shard_map/ppermute | solution.py:702
  12.4 9.6 %collective-permute-start.2 = (bf16[528,128]{1,0:T(8,128)(2,1)S(1)}, bf16[528,128]{1,0:T(8,128)(2,1)S(1)}, u32[]{:S(2)}, u32[]{:S(2)}) collective-permute-start(bf16[528,128]{1,0:T(8,128)(2,1)S(1)} %get-tuple-element.35), channel_id=1, source_target_pairs={{0,12},{4,8},{8,4},{12,0},{16,28},{20,24},{24,20},{28,16},{1,13},{... | collective-permute-start | bytes 405512 | tf_op jit(solution)/shard_map/ppermute | solution.py:702
  12.8 26.2 %collective-permute-start.8 = (bf16[1040,128]{1,0:T(8,128)(2,1)}, bf16[1040,128]{1,0:T(8,128)(2,1)S(1)}, u32[]{:S(2)}, u32[]{:S(2)}) collective-permute-start(bf16[1040,128]{1,0:T(8,128)(2,1)} %get-tuple-element.36.refs_3_), channel_id=1, source_target_pairs={{0,4},{4,24},{8,12},{12,0},{16,20},{20,8},{24,28},{28,16},{1,5},{5... | collective-permute-start | bytes 798728 | tf_op jit(solution)/shard_map/ppermute | solution.py:702
  17.9 7.8 %copy-start = (bf16[256,16,128]{2,1,0:T(8,128)(2,1)S(1)}, bf16[256,16,128]{2,1,0:T(8,128)(2,1)}, u32[]{:S(2)}) copy-start(bf16[256,16,128]{2,1,0:T(8,128)(2,1)} %param.10) | copy-start | bytes 3145732
  22.2 19.1 %collective-permute-start.13 = (bf16[1040,128]{1,0:T(8,128)(2,1)S(1)}, bf16[1040,128]{1,0:T(8,128)(2,1)S(1)}, u32[]{:S(2)}, u32[]{:S(2)}) collective-permute-start(bf16[1040,128]{1,0:T(8,128)(2,1)S(1)} %get-tuple-element.49.refs_4_), channel_id=1, source_target_pairs={{0,8},{4,12},{8,16},{12,20},{16,24},{20,28},{24,0},{28,4},{1,9},{5... | collective-permute-start | bytes 798728 | tf_op jit(solution)/shard_map/ppermute | solution.py:702
  24.5 12.9 %collective-permute-start.4 = (bf16[528,128]{1,0:T(8,128)(2,1)S(1)}, bf16[528,128]{1,0:T(8,128)(2,1)S(1)}, u32[]{:S(2)}, u32[]{:S(2)}) collective-permute-start(bf16[528,128]{1,0:T(8,128)(2,1)S(1)} %get-tuple-element.38.refs_5_), channel_id=1, source_target_pairs={{0,16},{4,20},{8,24},{12,28},{16,0},{20,4},{24,8},{28,12},{1,17},{... | collective-permute-start | bytes 405512 | tf_op jit(solution)/shard_map/ppermute | solution.py:702
  25.7 24.1 %collective-permute-start.12 = (bf16[1040,128]{1,0:T(8,128)(2,1)S(1)}, bf16[1040,128]{1,0:T(8,128)(2,1)S(1)}, u32[]{:S(2)}, u32[]{:S(2)}) collective-permute-start(bf16[1040,128]{1,0:T(8,128)(2,1)S(1)} %get-tuple-element.49.refs_4_), channel_id=1, source_target_pairs={{0,4},{4,0},{8,12},{12,8},{16,20},{20,16},{24,28},{28,24},{1,5},{5... | collective-permute-start | bytes 798728 | tf_op jit(solution)/shard_map/ppermute | solution.py:702
  37.7 7.8 %collective-permute-start.5 = (bf16[512,128]{1,0:T(8,128)(2,1)S(1)}, bf16[512,128]{1,0:T(8,128)(2,1)S(1)}, u32[]{:S(2)}, u32[]{:S(2)}) collective-permute-start(bf16[512,128]{1,0:T(8,128)(2,1)S(1)} %get-tuple-element.45), channel_id=1, source_target_pairs={{0,4},{4,0},{8,12},{12,8},{16,20},{20,16},{24,28},{28,24},{1,5},{5... | collective-permute-start | bytes 393224 | tf_op jit(solution)/shard_map/ppermute | solution.py:702
  38.3 7.2 %collective-permute-start.6 = (bf16[512,128]{1,0:T(8,128)(2,1)S(1)}, bf16[512,128]{1,0:T(8,128)(2,1)S(1)}, u32[]{:S(2)}, u32[]{:S(2)}) collective-permute-start(bf16[512,128]{1,0:T(8,128)(2,1)S(1)} %get-tuple-element.46), channel_id=1, source_target_pairs={{0,8},{4,12},{8,0},{12,4},{16,24},{20,28},{24,16},{28,20},{1,9},{5... | collective-permute-start | bytes 393224 | tf_op jit(solution)/shard_map/ppermute | solution.py:702
  39.0 7.4 %collective-permute-start.7 = (bf16[512,128]{1,0:T(8,128)(2,1)S(1)}, bf16[512,128]{1,0:T(8,128)(2,1)S(1)}, u32[]{:S(2)}, u32[]{:S(2)}) collective-permute-start(bf16[512,128]{1,0:T(8,128)(2,1)S(1)} %get-tuple-element.47), channel_id=1, source_target_pairs={{0,12},{4,8},{8,4},{12,0},{16,28},{20,24},{24,20},{28,16},{1,13},{... | collective-permute-start | bytes 393224 | tf_op jit(solution)/shard_map/ppermute | solution.py:702
  41.2 12.3 %collective-permute-start.14 = (bf16[1040,128]{1,0:T(8,128)(2,1)S(1)}, bf16[1040,128]{1,0:T(8,128)(2,1)S(1)}, u32[]{:S(2)}, u32[]{:S(2)}) collective-permute-start(bf16[1040,128]{1,0:T(8,128)(2,1)S(1)} %collective-permute-done.13.refs_4_), channel_id=1, source_target_pairs={{0,4},{4,0},{8,12},{12,8},{16,20},{20,16},{24,28},{28,24},{1,5},{5... | collective-permute-start | bytes 798728 | tf_op jit(solution)/shard_map/ppermute | solution.py:702
  48.0 8.9 %collective-permute-start.9 = (f32[8,256]{1,0:T(8,128)S(1)}, f32[8,256]{1,0:T(8,128)S(1)}, u32[]{:S(2)}, u32[]{:S(2)}) collective-permute-start(f32[8,256]{1,0:T(8,128)S(1)} %get-tuple-element.51.refs_5_.refs_3_), channel_id=1, source_target_pairs={{0,1},{1,0},{2,3},{3,2},{4,5},{5,4},{6,7},{7,6},{8,9},{9,8},{10,11... | collective-permute-start | bytes 24584 | tf_op jit(solution)/shard_map/ppermute | solution.py:782
  48.0 8.9 %collective-permute-start.10 = (f32[8,256]{1,0:T(8,128)S(1)}, f32[8,256]{1,0:T(8,128)S(1)}, u32[]{:S(2)}, u32[]{:S(2)}) collective-permute-start(f32[8,256]{1,0:T(8,128)S(1)} %get-tuple-element.51.refs_5_.refs_3_), channel_id=1, source_target_pairs={{0,2},{1,3},{2,0},{3,1},{4,6},{5,7},{6,4},{7,5},{8,10},{9,11},{10,... | collective-permute-start | bytes 24584 | tf_op jit(solution)/shard_map/ppermute | solution.py:782
  49.5 7.4 %collective-permute-start.11 = (f32[8,256]{1,0:T(8,128)S(1)}, f32[8,256]{1,0:T(8,128)S(1)}, u32[]{:S(2)}, u32[]{:S(2)}) collective-permute-start(f32[8,256]{1,0:T(8,128)S(1)} %get-tuple-element.51.refs_5_.refs_3_), channel_id=1, source_target_pairs={{0,3},{1,2},{2,1},{3,0},{4,7},{5,6},{6,5},{7,4},{8,11},{9,10},{10,... | collective-permute-start | bytes 24584 | tf_op jit(solution)/shard_map/ppermute | solution.py:782
  53.5 3.4 %copy-start.1 = (bf16[256,16,128]{2,1,0:T(8,128)(2,1)S(1)}, bf16[256,16,128]{2,1,0:T(8,128)(2,1)}, u32[]{:S(2)}) copy-start(bf16[256,16,128]{2,1,0:T(8,128)(2,1)} %param.13) | copy-start | bytes 3145732
  53.5 3.4 %copy-start.2 = (f32[16,128]{1,0:T(8,128)S(1)}, f32[16,128]{1,0:T(8,128)}, u32[]{:S(2)}) copy-start(f32[16,128]{1,0:T(8,128)} %refs_0_.1) | copy-start | bytes 24580

commit v8 on v7

--- a/solution.py
+++ b/solution.py
@@ -344,11 +344,13 @@
     )
 
 
-def prior_kernel(size, has_before, bit, place_ref, *refs):
+def prior_kernel(size, has_before, relays, bit, place_ref, *refs):
     sources, came_ref = refs[:GROUP_BLOCKS], refs[GROUP_BLOCKS]
     before_ref = refs[GROUP_BLOCKS + 1] if has_before else None
-    out_refs, doc_ref = refs[-GROUP_BLOCKS - 3 : -3], refs[-3]
+    if relays:
+        refs[-3][...] = refs[GROUP_BLOCKS + 1 + has_before][...]
     blocks, priors = refs[-2:]
+    *out_refs, doc_ref = refs[-GROUP_BLOCKS - 3 - relays : -2 - relays]
     mine = place_ref[0] % GROUP_BLOCKS
     in_block_order(place_ref, sources, blocks)
     maps = block_maps(blocks, size)
@@ -378,14 +380,19 @@
     doc_ref[...] = jnp.broadcast_to(own_doc, (8, LANES))
 
 
-def prior_states(place, bit, quarters, came, before, size, after):
+def prior_states(place, bit, quarters, came, before, size, after, relay):
     before = [] if before is None else [before]
+    relay = [] if relay is None else [relay]
     return call(
-        functools.partial(prior_kernel, size, len(before), bit),
+        functools.partial(prior_kernel, size, len(before), len(relay), bit),
         "prior_states",
         [place],
-        [*quarters, came, *before],
-        (*[sds((size, LANES), BF16)] * GROUP_BLOCKS, sds((8, LANES), F32)),
+        [*quarters, came, *before, *relay],
+        (
+            *[sds((size, LANES), BF16)] * GROUP_BLOCKS,
+            sds((8, LANES), F32),
+            *[sds(x.shape, BF16) for x in relay],
+        ),
         scratch=[
             pltpu.VMEM((GROUP_BLOCKS, size + INFO, LANES), BF16),
             pltpu.VMEM((GROUP_BLOCKS, size, LANES), BF16),
@@ -755,27 +762,34 @@
         qh.append(got[1])
         return got[0]
 
-    done = first_attention([sent[0]])
-    run, ahead = group_map(place, quarters, size, [done], ahead)
-    lane_kv, cross_kv = [], []
-    for back in range(1, window // 2 + 1):
-        lane_kv.append((ahead, (2 * back, 2 * back)))
-        cross_kv.append((send(ahead, swap), (2 * back, 2 * back + 1)))
-        ahead = send(ahead, forward)
+    done = inner_of(0, [first_attention([sent[0]])])
+    run, ahead = group_map(place, quarters, size, [done, beside[0]], ahead)
+    lanes = [ahead]
+    for _ in range(1, window // 2):
+        lanes.append(send(lanes[-1], forward))
+    lane_kv = [(kv, (2 * n + 2, 2 * n + 2)) for n, kv in enumerate(lanes)]
+    cross_kv = [(send(ahead, swap), (2, 3))]
     stages = (blocks // GROUP_BLOCKS).bit_length() - 1
     before, done = None, run
     for stage in range(stages):
         came = send(run, [(b, b ^ (GROUP_BLOCKS << stage)) for b in everyone])
         if stage == stages - 1:
-            for part in range(parts):
+            for part in range(1, parts):
                 done = inner_of(part, [done])
+            done = more_attention([beside] + lane_kv[:1], False, [done])
         else:
             run, before = scan_step(place, stage + 2, run, came, before, size, [done])
             done = run
-    *priors, prior_doc = prior_states(place, stages + 1, quarters, came, before, size, [done])
+    *priors, prior_doc, relayed = prior_states(
+        place, stages + 1, quarters, came, before, size, [done], lanes[1]
+    )
     priors = [priors[0]] + [send(priors[j], [(b, b ^ j) for b in everyone]) for j in others]
-    done = more_attention([beside] + lane_kv[:1], False, [prior_doc])
+    lane_kv[1] = (relayed, lane_kv[1][1])
+    for n, kv in enumerate([relayed] + lanes[2:]):
+        cross_kv.append((send(kv, swap), (2 * n + 4, 2 * n + 5)))
     rest = [kv for pair in zip(cross_kv, lane_kv[1:] + [None]) for kv in pair if kv is not None]
+    done = more_attention(rest[:2], False, [prior_doc])
+    rest = rest[2:]
     mixed, squares = mix(place, docs, prior_doc, cumul, inner, qh, priors, tokens, heads, [done])
     sums = [squares]
     for other in range(1, tensor):

time: 58.9 us -> 63.7 us (1.081)
  waiting for transfers between devices: 12.8 us -> 17.2 us
  Pallas kernels: 27.2 us -> 25.3 us
  local copies, waits for them, and re-layouts: 0.02 us -> 1.24 us
  starting transfers between devices: 17.7 us -> 18.8 us
    ppermute x12, waiting for transfers between devices: 12.8 us -> 17.2 us  [send(): return lax.ppermute(x, 'seq', [(a, b % blocks) for a, b in pairs])]
    pallas_call x12, Pallas kernels: 27.2 us -> 25.3 us  [call(): pl.pallas_call(run, out_shape=outs, in_specs=[SMEM] * len(scalars) + [HBM...]
    unnamed x8, local copies, waits for them, and re-layouts: 0.02 us -> 1.24 us
    ppermute x12, starting transfers between devices: 15.8 us -> 16.9 us  [send(): return lax.ppermute(x, 'seq', [(a, b % blocks) for a, b in pairs])]
  transfers between devices with their start and end apart: 15 -> 15, of which waited for: 4 -> 3; matrix products, arithmetic and copies ran while one was open for 0% -> 0% of each run, Pallas kernels for 39% -> 34%
where the time goes in v8:
time: 63.7 us; the launch traced here: 63.5 us
  Pallas kernels  25.3 us (40%)
  starting transfers between devices  18.8 us (30%)
  waiting for transfers between devices  17.2 us (27%)
  local copies, waits for them, and re-layouts  1.24 us (2%)
  between operations  0.97 us (2%)
    pallas_call x12, Pallas kernels, call(): pl.pallas_call(run, out_shape=outs, in_specs=[SMEM] * len(scalars) + [HBM...  25.3 us
    ppermute x12, waiting for transfers between devices, send(): return lax.ppermute(x, 'seq', [(a, b % blocks) for a, b in pairs])  17.2 us
    ppermute x12, starting transfers between devices, send(): return lax.ppermute(x, 'seq', [(a, b % blocks) for a, b in pairs])  16.9 us
    ppermute x3, starting transfers between devices, body(): lax.ppermute(squares, 'tp', [(t, t ^ other) for t in range(tensor)])  1.89 us
  transfers between devices with their start and end apart: 15, of which 3 were waited for; matrix products, arithmetic and copies ran while one was open for 0% of the time, Pallas kernels for 34%

profile of v8, /device:TPU:0, one launch (start us, length us, event | category | flops | bytes accessed | tf_op | source)
XLA Modules:
  0.0 63.5 jit_solution(14745594549206925412)
XLA Ops:
  0.6 1.9 %fetch.1 = (bf16[1040,128]{1,0:T(8,128)(2,1)S(1)}, f32[16,128]{1,0:T(8,128)S(1)}, f32[256,128]{1,0:T(8,128)S(1)}, bf16[4096,128]{1,0:T(8,128)(2,1)S(1)}, bf16[4096,128]{1,0:T(8,128)(2,1)S(1)}) custom-call(s32[1]{0:T(128)} %bitcast.2.refs_0_, s32[2,128]{1,0:T(2,128)} %bitcast.23, f32[16,256]{1,0:T(8,128)} %bitcast.22, bf16[2048,128]{1,0:T(8,128)(2,1)} %bitcast.20, ...), custom_call_target="tpu_custom_call" | custom-call | bytes 3145728 | tf_op jit(solution)/shard_map/fetch/pallas_call | solution.py:59
  2.6 3.0 %collective-permute-start.4 = (bf16[1040,128]{1,0:T(8,128)(2,1)S(1)}, bf16[1040,128]{1,0:T(8,128)(2,1)S(1)}, u32[]{:S(2)}, u32[]{:S(2)}) collective-permute-start(bf16[1040,128]{1,0:T(8,128)(2,1)S(1)} %get-tuple-element.37.refs_3_), channel_id=1, source_target_pairs={{0,4},{4,24},{8,12},{12,0},{16,20},{20,8},{24,28},{28,16},{1,5},{5... | collective-permute-start | bytes 798728 | tf_op jit(solution)/shard_map/ppermute | solution.py:709
  5.6 1.6 %collective-permute-start.3 = (bf16[1040,128]{1,0:T(8,128)(2,1)S(1)}, bf16[1040,128]{1,0:T(8,128)(2,1)S(1)}, u32[]{:S(2)}, u32[]{:S(2)}) collective-permute-start(bf16[1040,128]{1,0:T(8,128)(2,1)S(1)} %get-tuple-element.37.refs_3_), channel_id=1, source_target_pairs={{0,8},{4,12},{8,16},{12,20},{16,24},{20,28},{24,0},{28,4},{1,9},{5... | collective-permute-start | bytes 798728 | tf_op jit(solution)/shard_map/ppermute | solution.py:709
  7.2 2.7 %block_state.1 = (bf16[528,128]{1,0:T(8,128)(2,1)S(1)}, bf16[528,128]{1,0:T(8,128)(2,1)S(1)}, bf16[528,128]{1,0:T(8,128)(2,1)S(1)}, bf16[528,128]{1,0:T(8,128)(2,1)S(1)}) custom-call(s32[1]{0:T(128)} %bitcast.1.refs_0_, f32[256,128]{1,0:T(8,128)S(1)} %get-tuple-element.30.refs_1_.refs_0_.refs_3_, f32[16,128]{1,0:T(8,128)S(1)} %get-tuple-element.29.refs_2_.refs_1_, ...), custom_call_target="tpu_custom_call" | custom-call | flops 134217728 | bytes 5242880 | tf_op jit(solution)/shard_map/block_state/pallas_call | solution.py:59
  9.9 0.0 copy-start
  9.9 2.0 %collective-permute-start = (bf16[528,128]{1,0:T(8,128)(2,1)S(1)}, bf16[528,128]{1,0:T(8,128)(2,1)S(1)}, u32[]{:S(2)}, u32[]{:S(2)}) collective-permute-start(bf16[528,128]{1,0:T(8,128)(2,1)S(1)} %get-tuple-element.34), channel_id=1, source_target_pairs={{0,4},{4,0},{8,12},{12,8},{16,20},{20,16},{24,28},{28,24},{1,5},{5... | collective-permute-start | bytes 405512 | tf_op jit(solution)/shard_map/ppermute | solution.py:709
  12.0 0.0 collective-permute-start.1
  12.0 1.5 %collective-permute-start.2 = (bf16[528,128]{1,0:T(8,128)(2,1)S(1)}, bf16[528,128]{1,0:T(8,128)(2,1)S(1)}, u32[]{:S(2)}, u32[]{:S(2)}) collective-permute-start(bf16[528,128]{1,0:T(8,128)(2,1)S(1)} %get-tuple-element.36), channel_id=1, source_target_pairs={{0,12},{4,8},{8,4},{12,0},{16,28},{20,24},{24,20},{28,16},{1,13},{... | collective-permute-start | bytes 405512 | tf_op jit(solution)/shard_map/ppermute | solution.py:709
  13.5 0.0 copy-start.3
  13.5 1.2 %copy-done.3 = bf16[256,16,128]{2,1,0:T(8,128)(2,1)S(1)} copy-done((bf16[256,16,128]{2,1,0:T(8,128)(2,1)S(1)}, bf16[256,16,128]{2,1,0:T(8,128)(2,1)}, u32[]{:S(2)}) %copy-start.3) | copy-done | bytes 1048600
  14.7 2.6 %attend.4 = (bf16[2,2048,256]{2,1,0:T(8,128)(2,1)S(1)}, f32[2,144,2048]{2,1,0:T(8,128)S(1)}) custom-call(s32[1]{0:T(128)} %bitcast.1.refs_0_, f32[16,128]{1,0:T(8,128)S(1)} %get-tuple-element.29.refs_2_.refs_1_, bf16[4096,128]{1,0:T(8,128)(2,1)S(1)} %bitcast.16, bf16[1040,128]{1,0:T(8,128)(2,1)S(1)} %get-tuple-element.37.refs_3_, ...), custom_call_target="tpu_custom_call" | custom-call | flops 1073741824 | bytes 8388608 | tf_op jit(solution)/shard_map/attend/pallas_call | solution.py:59
  17.4 0.0 copy-done
  17.4 1.9 %inner_part.2 = (f32[2048,128]{1,0:T(8,128)S(1)}, bf16[2048,128]{1,0:T(8,128)(2,1)S(1)}) custom-call(f32[256,128]{1,0:T(8,128)S(1)} %get-tuple-element.30.refs_1_.refs_0_.refs_3_, f32[16,128]{1,0:T(8,128)S(1)} %get-tuple-element.29.refs_2_.refs_1_, bf16[4096,128]{1,0:T(8,128)(2,1)S(1)} %bitcast.13, bf16[4096,128]{1,0:T(8,128)(2,1)S(1)} %get-tuple-element.31.refs_3_, ...), custom_call_target="tpu_custom_call" | custom-call | flops 268435456 | bytes 6291456 | tf_op jit(solution)/shard_map/inner_part/pallas_call | solution.py:59
  19.3 0.0 collective-permute-done.refs_2_
  19.3 0.0 collective-permute-done.1.refs_3_
  19.3 5.8 %collective-permute-done.2.refs_4_ = bf16[528,128]{1,0:T(8,128)(2,1)S(1)} collective-permute-done((bf16[528,128]{1,0:T(8,128)(2,1)S(1)}, bf16[528,128]{1,0:T(8,128)(2,1)S(1)}, u32[]{:S(2)}, u32[]{:S(2)}) %collective-permute-start.2) | collective-permute-done | bytes 135200 | tf_op jit(solution)/shard_map/ppermute | solution.py:709
  25.1 0.0 collective-permute-done.4.refs_7_.refs_3_
  25.1 0.0 collective-permute-done.3.refs_5_
  25.2 0.2 group_map.1
  25.4 3.4 %collective-permute-start.6 = (bf16[1040,128]{1,0:T(8,128)(2,1)S(1)}, bf16[1040,128]{1,0:T(8,128)(2,1)S(1)}, u32[]{:S(2)}, u32[]{:S(2)}) collective-permute-start(bf16[1040,128]{1,0:T(8,128)(2,1)S(1)} %get-tuple-element.41.refs_4_), channel_id=1, source_target_pairs={{0,8},{4,12},{8,16},{12,20},{16,24},{20,28},{24,0},{28,4},{1,9},{5... | collective-permute-start | bytes 798728 | tf_op jit(solution)/shard_map/ppermute | solution.py:709
  28.8 0.0 collective-permute-start.10
  28.8 0.7 %collective-permute-start.5 = (bf16[528,128]{1,0:T(8,128)(2,1)S(1)}, bf16[528,128]{1,0:T(8,128)(2,1)S(1)}, u32[]{:S(2)}, u32[]{:S(2)}) collective-permute-start(bf16[528,128]{1,0:T(8,128)(2,1)S(1)} %get-tuple-element.40.refs_5_), channel_id=1, source_target_pairs={{0,16},{4,20},{8,24},{12,28},{16,0},{20,4},{24,8},{28,12},{1,17},{... | collective-permute-start | bytes 405512 | tf_op jit(solution)/shard_map/ppermute | solution.py:709
  29.5 1.9 %inner_part.3 = (f32[2048,128]{1,0:T(8,128)S(1)}, bf16[2048,128]{1,0:T(8,128)(2,1)S(1)}) custom-call(f32[256,128]{1,0:T(8,128)S(1)} %get-tuple-element.30.refs_1_.refs_0_.refs_3_, f32[16,128]{1,0:T(8,128)S(1)} %get-tuple-element.29.refs_2_.refs_1_, bf16[4096,128]{1,0:T(8,128)(2,1)S(1)} %bitcast.14, bf16[4096,128]{1,0:T(8,128)(2,1)S(1)} %get-tuple-element.31.refs_3_, ...), custom_call_target="tpu_custom_call" | custom-call | flops 268435456 | bytes 6291456 | tf_op jit(solution)/shard_map/inner_part/pallas_call | solution.py:59
  31.5 3.6 %attend.5.refs_7_.refs_2_ = f32[2,144,2048]{2,1,0:T(8,128)S(1)} custom-call(s32[1]{0:T(128)} %bitcast.1.refs_0_, bf16[2,2048,256]{2,1,0:T(8,128)(2,1)S(1)} %get-tuple-element.42.refs_1_, f32[2,144,2048]{2,1,0:T(8,128)S(1)} %get-tuple-element.38.refs_5_.refs_2_, bf16[1040,128]{1,0:T(8,128)(2,1)S(1)} %collective-permute-done.4.refs_7_.refs_3_, ...), custom_call_target="tpu_custom_call" | custom-call | flops 2147483648 | bytes 8388608 | tf_op jit(solution)/shard_map/attend/pallas_call | solution.py:59
  35.1 5.6 %collective-permute-done.5.refs_5_ = bf16[528,128]{1,0:T(8,128)(2,1)S(1)} collective-permute-done((bf16[528,128]{1,0:T(8,128)(2,1)S(1)}, bf16[528,128]{1,0:T(8,128)(2,1)S(1)}, u32[]{:S(2)}, u32[]{:S(2)}) %collective-permute-start.5) | collective-permute-done | bytes 135200 | tf_op jit(solution)/shard_map/ppermute | solution.py:709
  40.7 0.0 collective-permute-done.6.refs_6_
  40.7 0.3 prior_states.1
  40.9 1.1 %collective-permute-start.14 = (bf16[1040,128]{1,0:T(8,128)(2,1)S(1)}, bf16[1040,128]{1,0:T(8,128)(2,1)S(1)}, u32[]{:S(2)}, u32[]{:S(2)}) collective-permute-start(bf16[1040,128]{1,0:T(8,128)(2,1)S(1)} %get-tuple-element.51.refs_4_), channel_id=1, source_target_pairs={{0,4},{4,0},{8,12},{12,8},{16,20},{20,16},{24,28},{28,24},{1,5},{5... | collective-permute-start | bytes 798728 | tf_op jit(solution)/shard_map/ppermute | solution.py:709
  42.1 1.0 %collective-permute-start.7 = (bf16[512,128]{1,0:T(8,128)(2,1)S(1)}, bf16[512,128]{1,0:T(8,128)(2,1)S(1)}, u32[]{:S(2)}, u32[]{:S(2)}) collective-permute-start(bf16[512,128]{1,0:T(8,128)(2,1)S(1)} %get-tuple-element.48), channel_id=1, source_target_pairs={{0,4},{4,0},{8,12},{12,8},{16,20},{20,16},{24,28},{28,24},{1,5},{5... | collective-permute-start | bytes 393224 | tf_op jit(solution)/shard_map/ppermute | solution.py:709
  43.0 0.0 collective-permute-start.8
  43.0 2.5 %collective-permute-start.9 = (bf16[512,128]{1,0:T(8,128)(2,1)S(1)}, bf16[512,128]{1,0:T(8,128)(2,1)S(1)}, u32[]{:S(2)}, u32[]{:S(2)}) collective-permute-start(bf16[512,128]{1,0:T(8,128)(2,1)S(1)} %get-tuple-element.50), channel_id=1, source_target_pairs={{0,12},{4,8},{8,4},{12,0},{16,28},{20,24},{24,20},{28,16},{1,13},{... | collective-permute-start | bytes 393224 | tf_op jit(solution)/shard_map/ppermute | solution.py:709
  45.6 0.0 collective-permute-done.10.refs_3_
  45.6 3.6 %attend.6.refs_12_.refs_2_ = f32[2,144,2048]{2,1,0:T(8,128)S(1)} custom-call(s32[1]{0:T(128)} %bitcast.1.refs_0_, bf16[2,2048,256]{2,1,0:T(8,128)(2,1)S(1)} %get-tuple-element.42.refs_1_, f32[2,144,2048]{2,1,0:T(8,128)S(1)} %attend.5.refs_7_.refs_2_, bf16[1040,128]{1,0:T(8,128)(2,1)S(1)} %collective-permute-done.10.refs_3_, ...), custom_call_target="tpu_custom_call" | custom-call | flops 2147483648 | bytes 8388608 | tf_op jit(solution)/shard_map/attend/pallas_call | solution.py:59
  49.2 5.8 %collective-permute-done.7.refs_9_ = bf16[512,128]{1,0:T(8,128)(2,1)S(1)} collective-permute-done((bf16[512,128]{1,0:T(8,128)(2,1)S(1)}, bf16[512,128]{1,0:T(8,128)(2,1)S(1)}, u32[]{:S(2)}, u32[]{:S(2)}) %collective-permute-start.7) | collective-permute-done | bytes 131104 | tf_op jit(solution)/shard_map/ppermute | solution.py:709
  54.9 0.0 collective-permute-done.8.refs_10_
  54.9 0.0 collective-permute-done.9.refs_11_
  55.0 1.6 %mix.1 = (f32[4096,128]{1,0:T(8,128)S(1)}, f32[8,256]{1,0:T(8,128)S(1)}) custom-call(s32[1]{0:T(128)} %bitcast.1.refs_0_, f32[16,128]{1,0:T(8,128)S(1)} %get-tuple-element.29.refs_2_.refs_1_, f32[8,128]{1,0:T(8,128)S(1)} %get-tuple-element.44.refs_5_.refs_2_, f32[256,128]{1,0:T(8,128)S(1)} %get-tuple-element.30.refs_1_.refs_0_.refs_3_, ...), custom_call_target="tpu_custom_call" | custom-call | flops 134217728 | bytes 5242880 | tf_op jit(solution)/shard_map/mix/pallas_call | solution.py:59
  56.5 0.3 collective-permute-start.13
  56.8 1.3 %collective-permute-start.12 = (f32[8,256]{1,0:T(8,128)S(1)}, f32[8,256]{1,0:T(8,128)S(1)}, u32[]{:S(2)}, u32[]{:S(2)}) collective-permute-start(f32[8,256]{1,0:T(8,128)S(1)} %get-tuple-element.53.refs_4_.refs_3_), channel_id=1, source_target_pairs={{0,2},{1,3},{2,0},{3,1},{4,6},{5,7},{6,4},{7,5},{8,10},{9,11},{10,... | collective-permute-start | bytes 24584 | tf_op jit(solution)/shard_map/ppermute | solution.py:796
  58.1 0.3 collective-permute-start.11
  58.4 0.0 collective-permute-done.14.refs_3_
  58.4 3.2 %attend.7 = (bf16[4096,128]{1,0:T(8,128)(2,1)}, f32[8,128]{1,0:T(8,128)S(1)}) custom-call(s32[1]{0:T(128)} %bitcast.1.refs_0_, bf16[2,2048,256]{2,1,0:T(8,128)(2,1)S(1)} %get-tuple-element.42.refs_1_, f32[2,144,2048]{2,1,0:T(8,128)S(1)} %attend.6.refs_12_.refs_2_, bf16[1040,128]{1,0:T(8,128)(2,1)S(1)} %collective-permute-done.14.refs_3_, ...), custom_call_target="tpu_custom_call" | custom-call | flops 1073741824 | bytes 8388608 | tf_op jit(solution)/shard_map/attend/pallas_call | solution.py:59
  61.7 0.0 collective-permute-done.13.refs_6_
  61.7 0.0 collective-permute-done.12.refs_5_
  61.7 0.0 collective-permute-done.11.refs_4_
  61.7 0.0 copy-done.1
  61.7 0.0 copy-done.2
  61.7 1.6 %finish.1 = bf16[4096,128]{1,0:T(8,128)(2,1)} custom-call(f32[16,128]{1,0:T(8,128)S(1)} %copy-done.2, bf16[4096,128]{1,0:T(8,128)(2,1)S(1)} %bitcast.15, f32[4096,128]{1,0:T(8,128)S(1)} %get-tuple-element.52.refs_2_, f32[8,256]{1,0:T(8,128)S(1)} %get-tuple-element.53.refs_4_.refs_3_, f32[8,256]{1,0:T(8,128)S(1)} %collective-permute-done.11.refs_4_, ...), custom_call_target="tpu_custom_call" | custom-call | bytes 4194304 | tf_op jit(solution)/shard_map/finish/pallas_call | solution.py:59
  (2 shorter events, 0.0 us)
Async XLA Ops:
  2.6 22.5 %collective-permute-start.4 = (bf16[1040,128]{1,0:T(8,128)(2,1)S(1)}, bf16[1040,128]{1,0:T(8,128)(2,1)S(1)}, u32[]{:S(2)}, u32[]{:S(2)}) collective-permute-start(bf16[1040,128]{1,0:T(8,128)(2,1)S(1)} %get-tuple-element.37.refs_3_), channel_id=1, source_target_pairs={{0,4},{4,24},{8,12},{12,0},{16,20},{20,8},{24,28},{28,16},{1,5},{5... | collective-permute-start | bytes 798728 | tf_op jit(solution)/shard_map/ppermute | solution.py:709
  5.6 19.5 %collective-permute-start.3 = (bf16[1040,128]{1,0:T(8,128)(2,1)S(1)}, bf16[1040,128]{1,0:T(8,128)(2,1)S(1)}, u32[]{:S(2)}, u32[]{:S(2)}) collective-permute-start(bf16[1040,128]{1,0:T(8,128)(2,1)S(1)} %get-tuple-element.37.refs_3_), channel_id=1, source_target_pairs={{0,8},{4,12},{8,16},{12,20},{16,24},{20,28},{24,0},{28,4},{1,9},{5... | collective-permute-start | bytes 798728 | tf_op jit(solution)/shard_map/ppermute | solution.py:709
  9.9 7.4 %copy-start = (bf16[256,16,128]{2,1,0:T(8,128)(2,1)S(1)}, bf16[256,16,128]{2,1,0:T(8,128)(2,1)}, u32[]{:S(2)}) copy-start(bf16[256,16,128]{2,1,0:T(8,128)(2,1)} %param.10) | copy-start | bytes 3145732
  9.9 9.4 %collective-permute-start = (bf16[528,128]{1,0:T(8,128)(2,1)S(1)}, bf16[528,128]{1,0:T(8,128)(2,1)S(1)}, u32[]{:S(2)}, u32[]{:S(2)}) collective-permute-start(bf16[528,128]{1,0:T(8,128)(2,1)S(1)} %get-tuple-element.34), channel_id=1, source_target_pairs={{0,4},{4,0},{8,12},{12,8},{16,20},{20,16},{24,28},{28,24},{1,5},{5... | collective-permute-start | bytes 405512 | tf_op jit(solution)/shard_map/ppermute | solution.py:709
  12.0 7.3 %collective-permute-start.1 = (bf16[528,128]{1,0:T(8,128)(2,1)S(1)}, bf16[528,128]{1,0:T(8,128)(2,1)S(1)}, u32[]{:S(2)}, u32[]{:S(2)}) collective-permute-start(bf16[528,128]{1,0:T(8,128)(2,1)S(1)} %get-tuple-element.35), channel_id=1, source_target_pairs={{0,8},{4,12},{8,0},{12,4},{16,24},{20,28},{24,16},{28,20},{1,9},{5... | collective-permute-start | bytes 405512 | tf_op jit(solution)/shard_map/ppermute | solution.py:709
  12.0 13.2 %collective-permute-start.2 = (bf16[528,128]{1,0:T(8,128)(2,1)S(1)}, bf16[528,128]{1,0:T(8,128)(2,1)S(1)}, u32[]{:S(2)}, u32[]{:S(2)}) collective-permute-start(bf16[528,128]{1,0:T(8,128)(2,1)S(1)} %get-tuple-element.36), channel_id=1, source_target_pairs={{0,12},{4,8},{8,4},{12,0},{16,28},{20,24},{24,20},{28,16},{1,13},{... | collective-permute-start | bytes 405512 | tf_op jit(solution)/shard_map/ppermute | solution.py:709
  13.5 1.2 %copy-start.3 = (bf16[256,16,128]{2,1,0:T(8,128)(2,1)S(1)}, bf16[256,16,128]{2,1,0:T(8,128)(2,1)}, u32[]{:S(2)}) copy-start(bf16[256,16,128]{2,1,0:T(8,128)(2,1)} %param.17) | copy-start | bytes 3145732
  25.4 15.3 %collective-permute-start.6 = (bf16[1040,128]{1,0:T(8,128)(2,1)S(1)}, bf16[1040,128]{1,0:T(8,128)(2,1)S(1)}, u32[]{:S(2)}, u32[]{:S(2)}) collective-permute-start(bf16[1040,128]{1,0:T(8,128)(2,1)S(1)} %get-tuple-element.41.refs_4_), channel_id=1, source_target_pairs={{0,8},{4,12},{8,16},{12,20},{16,24},{20,28},{24,0},{28,4},{1,9},{5... | collective-permute-start | bytes 798728 | tf_op jit(solution)/shard_map/ppermute | solution.py:709
  28.8 16.8 %collective-permute-start.10 = (bf16[1040,128]{1,0:T(8,128)(2,1)S(1)}, bf16[1040,128]{1,0:T(8,128)(2,1)S(1)}, u32[]{:S(2)}, u32[]{:S(2)}) collective-permute-start(bf16[1040,128]{1,0:T(8,128)(2,1)S(1)} %get-tuple-element.41.refs_4_), channel_id=1, source_target_pairs={{0,4},{4,0},{8,12},{12,8},{16,20},{20,16},{24,28},{28,24},{1,5},{5... | collective-permute-start | bytes 798728 | tf_op jit(solution)/shard_map/ppermute | solution.py:709
  28.8 11.9 %collective-permute-start.5 = (bf16[528,128]{1,0:T(8,128)(2,1)S(1)}, bf16[528,128]{1,0:T(8,128)(2,1)S(1)}, u32[]{:S(2)}, u32[]{:S(2)}) collective-permute-start(bf16[528,128]{1,0:T(8,128)(2,1)S(1)} %get-tuple-element.40.refs_5_), channel_id=1, source_target_pairs={{0,16},{4,20},{8,24},{12,28},{16,0},{20,4},{24,8},{28,12},{1,17},{... | collective-permute-start | bytes 405512 | tf_op jit(solution)/shard_map/ppermute | solution.py:709
  40.9 17.5 %collective-permute-start.14 = (bf16[1040,128]{1,0:T(8,128)(2,1)S(1)}, bf16[1040,128]{1,0:T(8,128)(2,1)S(1)}, u32[]{:S(2)}, u32[]{:S(2)}) collective-permute-start(bf16[1040,128]{1,0:T(8,128)(2,1)S(1)} %get-tuple-element.51.refs_4_), channel_id=1, source_target_pairs={{0,4},{4,0},{8,12},{12,8},{16,20},{20,16},{24,28},{28,24},{1,5},{5... | collective-permute-start | bytes 798728 | tf_op jit(solution)/shard_map/ppermute | solution.py:709
  42.1 12.9 %collective-permute-start.7 = (bf16[512,128]{1,0:T(8,128)(2,1)S(1)}, bf16[512,128]{1,0:T(8,128)(2,1)S(1)}, u32[]{:S(2)}, u32[]{:S(2)}) collective-permute-start(bf16[512,128]{1,0:T(8,128)(2,1)S(1)} %get-tuple-element.48), channel_id=1, source_target_pairs={{0,4},{4,0},{8,12},{12,8},{16,20},{20,16},{24,28},{28,24},{1,5},{5... | collective-permute-start | bytes 393224 | tf_op jit(solution)/shard_map/ppermute | solution.py:709
  43.0 11.9 %collective-permute-start.8 = (bf16[512,128]{1,0:T(8,128)(2,1)S(1)}, bf16[512,128]{1,0:T(8,128)(2,1)S(1)}, u32[]{:S(2)}, u32[]{:S(2)}) collective-permute-start(bf16[512,128]{1,0:T(8,128)(2,1)S(1)} %get-tuple-element.49), channel_id=1, source_target_pairs={{0,8},{4,12},{8,0},{12,4},{16,24},{20,28},{24,16},{28,20},{1,9},{5... | collective-permute-start | bytes 393224 | tf_op jit(solution)/shard_map/ppermute | solution.py:709
  43.0 11.9 %collective-permute-start.9 = (bf16[512,128]{1,0:T(8,128)(2,1)S(1)}, bf16[512,128]{1,0:T(8,128)(2,1)S(1)}, u32[]{:S(2)}, u32[]{:S(2)}) collective-permute-start(bf16[512,128]{1,0:T(8,128)(2,1)S(1)} %get-tuple-element.50), channel_id=1, source_target_pairs={{0,12},{4,8},{8,4},{12,0},{16,28},{20,24},{24,20},{28,16},{1,13},{... | collective-permute-start | bytes 393224 | tf_op jit(solution)/shard_map/ppermute | solution.py:709
  56.5 5.2 %copy-start.1 = (bf16[256,16,128]{2,1,0:T(8,128)(2,1)S(1)}, bf16[256,16,128]{2,1,0:T(8,128)(2,1)}, u32[]{:S(2)}) copy-start(bf16[256,16,128]{2,1,0:T(8,128)(2,1)} %param.13) | copy-start | bytes 3145732
  56.5 5.2 %copy-start.2 = (f32[16,128]{1,0:T(8,128)S(1)}, f32[16,128]{1,0:T(8,128)}, u32[]{:S(2)}) copy-start(f32[16,128]{1,0:T(8,128)} %refs_0_.1) | copy-start | bytes 24580
  56.5 5.1 %collective-permute-start.13 = (f32[8,256]{1,0:T(8,128)S(1)}, f32[8,256]{1,0:T(8,128)S(1)}, u32[]{:S(2)}, u32[]{:S(2)}) collective-permute-start(f32[8,256]{1,0:T(8,128)S(1)} %get-tuple-element.53.refs_4_.refs_3_), channel_id=1, source_target_pairs={{0,3},{1,2},{2,1},{3,0},{4,7},{5,6},{6,5},{7,4},{8,11},{9,10},{10,... | collective-permute-start | bytes 24584 | tf_op jit(solution)/shard_map/ppermute | solution.py:796
  56.8 4.9 %collective-permute-start.12 = (f32[8,256]{1,0:T(8,128)S(1)}, f32[8,256]{1,0:T(8,128)S(1)}, u32[]{:S(2)}, u32[]{:S(2)}) collective-permute-start(f32[8,256]{1,0:T(8,128)S(1)} %get-tuple-element.53.refs_4_.refs_3_), channel_id=1, source_target_pairs={{0,2},{1,3},{2,0},{3,1},{4,6},{5,7},{6,4},{7,5},{8,10},{9,11},{10,... | collective-permute-start | bytes 24584 | tf_op jit(solution)/shard_map/ppermute | solution.py:796
  58.1 3.6 %collective-permute-start.11 = (f32[8,256]{1,0:T(8,128)S(1)}, f32[8,256]{1,0:T(8,128)S(1)}, u32[]{:S(2)}, u32[]{:S(2)}) collective-permute-start(f32[8,256]{1,0:T(8,128)S(1)} %get-tuple-element.53.refs_4_.refs_3_), channel_id=1, source_target_pairs={{0,1},{1,0},{2,3},{3,2},{4,5},{5,4},{6,7},{7,6},{8,9},{9,8},{10,11... | collective-permute-start | bytes 24584 | tf_op jit(solution)/shard_map/ppermute | solution.py:796

commit v9 on v7

--- a/solution.py
+++ b/solution.py
@@ -35,11 +35,11 @@
 
 def cost(flops, bytes_accessed, transcendentals=0):
     return pl.CostEstimate(
-        flops=int(flops), bytes_accessed=int(bytes_accessed), transcendentals=int(transcendentals)
-    )
-
-
-def call(kernel, name, scalars, operands, out_shape, scratch=(), mib=16, estimate=None, after=(), hbm=0, out_hbm=False):
+        flops=int(flops) // 8, bytes_accessed=int(bytes_accessed) // 8, transcendentals=int(transcendentals) // 8
+    )
+
+
+def call(kernel, name, scalars, operands, out_shape, scratch=(), mib=16, estimate=None, after=(), hbm=0, out_hbm=False, relay=()):
     begin = len(scalars) + len(operands)
     skip = len(after)
     operands = [
@@ -53,20 +53,29 @@
     if out_hbm:
         out_specs = (HBM, *out_specs[1:])
 
+    moved = len(relay)
+    many = len(outs)
+    single = not isinstance(out_shape, tuple) and not relay
+    out_specs += (VMEM,) * moved
+    outs += tuple(pltpu.VMEM(x.shape, x.dtype) for x in relay)
+
     def run(*refs):
-        kernel(*refs[:begin], *refs[begin + skip :])
+        rest = refs[begin + skip + moved :]
+        for source, target in zip(refs[begin + skip : begin + skip + moved], rest[many : many + moved]):
+            target[...] = source[...]
+        kernel(*refs[:begin], *rest[:many], *rest[many + moved :])
 
     out = pl.pallas_call(
         run,
         out_shape=outs,
-        in_specs=[SMEM] * len(scalars) + [HBM] * hbm + [VMEM] * (len(operands) - hbm) + [ANYWHERE] * skip,
+        in_specs=[SMEM] * len(scalars) + [HBM] * hbm + [VMEM] * (len(operands) - hbm) + [ANYWHERE] * skip + [VMEM] * moved,
         out_specs=out_specs,
         scratch_shapes=list(scratch),
         compiler_params=pltpu.CompilerParams(vmem_limit_bytes=mib * 1024 * 1024),
         cost_estimate=estimate,
         name=name,
-    )(*scalars, *operands, *after)
-    return out if isinstance(out_shape, tuple) else out[0]
+    )(*scalars, *operands, *after, *relay)
+    return out[0] if single else out
 
 
 def doc_columns(doc_rows, tokens):
@@ -90,12 +99,12 @@
 def fetch_kernel(tokens, heads, kv_here, start_ref, *refs):
     refs = list(refs)
     take = lambda n: [refs.pop(0) for _ in range(n)]
-    sources = take(6)
-    kv_ref, doc_out, cumul_ref, key_out, value_out = take(5)
+    sources = take(7)
+    kv_ref, doc_out, cumul_ref, key_out, value_out, query_out = take(6)
     held = take(4)
     sems, wide, ldp = refs
     docs_in, decays, soft_key, soft_value = held
-    targets = [*held, key_out, value_out]
+    targets = [*held, key_out, value_out, query_out]
     copies = [
         pltpu.make_async_copy(source, target, sems.at[i])
         for i, (source, target) in enumerate(zip(sources, targets))
@@ -135,8 +144,8 @@
                 halves = [jnp.transpose(rows[i : i + LANES, :]) for i in range(0, tokens, LANES)]
                 rows = jnp.concatenate(halves, axis=0)
             kv_ref[at : at + tokens, :] = rows.astype(BF16)
-    copies[4].wait()
-    copies[5].wait()
+    for copy in copies[4:]:
+        copy.wait()
 
 
 def fetch(start, operands, tokens, heads, kv_here):
@@ -151,6 +160,7 @@
             sds((tokens, LANES), F32),
             sds(operands[4].shape, BF16),
             sds(operands[5].shape, BF16),
+            sds(operands[6].shape, BF16),
         ),
         scratch=[pltpu.VMEM(x.shape, x.dtype) for x in operands[:4]]
         + [
@@ -259,9 +269,7 @@
 
 def group_kernel(size, place_ref, *refs):
     sources = refs[:GROUP_BLOCKS]
-    out_ref, blocks = refs[-2 - (len(refs) > GROUP_BLOCKS + 2)], refs[-1]
-    if len(refs) > GROUP_BLOCKS + 2:
-        refs[-2][...] = refs[GROUP_BLOCKS][...]
+    out_ref, blocks = refs[GROUP_BLOCKS:]
     in_block_order(place_ref, sources, blocks)
     maps = block_maps(blocks, size)
     gains = [None]
@@ -277,18 +285,17 @@
 
 
 def group_map(place, quarters, size, after, relay):
-    relay = [] if relay is None else [relay]
-    out = call(
+    return call(
         functools.partial(group_kernel, size),
         "group_map",
         [place],
-        [*quarters, *relay],
-        (sds((size + INFO, LANES), BF16), *[sds(x.shape, BF16) for x in relay]),
+        quarters,
+        (sds((size + INFO, LANES), BF16),),
         scratch=[pltpu.VMEM((GROUP_BLOCKS, size + INFO, LANES), BF16)],
         estimate=cost(8 * size * LANES, 10 * size * LANES * 2),
         after=after,
-    )
-    return out if relay else (out[0], None)
+        relay=relay,
+    )
 
 
 def scan_kernel(size, has_before, bit, place_ref, *refs):
@@ -347,8 +354,7 @@
 def prior_kernel(size, has_before, bit, place_ref, *refs):
     sources, came_ref = refs[:GROUP_BLOCKS], refs[GROUP_BLOCKS]
     before_ref = refs[GROUP_BLOCKS + 1] if has_before else None
-    out_refs, doc_ref = refs[-GROUP_BLOCKS - 3 : -3], refs[-3]
-    blocks, priors = refs[-2:]
+    *out_refs, doc_ref, blocks, priors = refs[GROUP_BLOCKS + 1 + has_before :]
     mine = place_ref[0] % GROUP_BLOCKS
     in_block_order(place_ref, sources, blocks)
     maps = block_maps(blocks, size)
@@ -378,7 +384,7 @@
     doc_ref[...] = jnp.broadcast_to(own_doc, (8, LANES))
 
 
-def prior_states(place, bit, quarters, came, before, size, after):
+def prior_states(place, bit, quarters, came, before, size, after, relay):
     before = [] if before is None else [before]
     return call(
         functools.partial(prior_kernel, size, len(before), bit),
@@ -392,6 +398,7 @@
         ],
         estimate=cost(8 * size * LANES, 10 * size * LANES * 2),
         after=after,
+        relay=relay,
     )
 
 
@@ -528,7 +535,7 @@
     )
 
 
-def attend_kernel(tokens, heads, kv_here, least, is_first, is_last, unroll, place_ref, *refs):
+def attend_kernel(tokens, heads, kv_here, least, has_choice, is_first, is_last, unroll, place_ref, *refs):
     refs = list(refs)
     take = lambda n: [refs.pop(0) for _ in range(n)]
     per_group = heads // kv_here
@@ -539,6 +546,7 @@
     else:
         wide_ref, state_ref = take(2)
     kv = take(len(least))
+    other = take(1)[0] if has_choice else None
     if is_first:
         wide_ref = take(1)[0]
     out_ref = take(1)[0]
@@ -549,10 +557,14 @@
         doc_rep = take(1)[0]
     if is_last:
         done, sems = take(2)
+    block = place_ref[0]
+    if has_choice:
+        slot = take(1)[0]
+        slot[...] = jnp.where(block % 2 == 0, kv[0][...], other[...])
+        kv[0] = slot
 
     lane = lax.broadcasted_iota(jnp.int32, (tokens, LANES), 1).astype(F32)
     end = 2 * kv_here * tokens
-    block = place_ref[0]
     for j, ref in enumerate(kv):
         valid = (block >= jnp.where(block % 2 == 0, *least[j])).astype(F32)
         docs = doc_columns(ref[end : end + INFO, :].astype(F32) * valid, tokens)
@@ -639,7 +651,7 @@
             pltpu.make_async_copy(done.at[at, :], out_ref.at[at, :], sems.at[c]).wait()
 
 
-def attend(place, first, state, kv, is_last, tokens, heads, kv_here, after):
+def attend(place, first, state, kv, is_last, tokens, heads, kv_here, after, odd=None):
     is_first = state is None
     least = tuple(pair for _, pair in kv)
     kv = [block for block, _ in kv]
@@ -657,12 +669,14 @@
         out_shape = (out_shape, sds((8, LANES), F32))
         scratch.append(pltpu.VMEM((tokens * heads, LANES), BF16))
         scratch.append(pltpu.SemaphoreType.DMA((rows // CHUNK,)))
+    if odd is not None:
+        scratch.append(pltpu.VMEM(odd.shape, BF16))
     span = blocks * tokens
     return call(
-        functools.partial(attend_kernel, tokens, heads, kv_here, least, is_first, is_last, unroll),
+        functools.partial(attend_kernel, tokens, heads, kv_here, least, odd is not None, is_first, is_last, unroll),
         "attend",
         [place],
-        [*first, *([] if is_first else [state]), *kv],
+        [*first, *([] if is_first else [state]), *kv, *([] if odd is None else [odd])],
         out_shape,
         scratch=scratch,
         mib=24,
@@ -704,7 +718,7 @@
     everyone = range(blocks)
     swap = [(b, b ^ 1) for b in everyone]
 
-    own_kv, docs, cumul, key, value = fetch(
+    own_kv, docs, cumul, key, value, soft_query = fetch(
         start,
         [
             doc_ids.reshape(tokens // LANES, LANES),
@@ -713,17 +727,17 @@
             flat(soft_value),
             flat(lin_key),
             flat(lin_value),
+            flat(soft_query),
         ],
         tokens,
         heads,
         kv_here,
     )
 
-    odd_window = window % 2 == 1
     forward = [(b, b + 2) for b in everyone]
+    beside = send(own_kv, swap)
     ahead = send(own_kv, forward)
-    beside = send(own_kv, [(b, b + (1 if b % 2 == 0 else window if odd_window else -1)) for b in everyone])
-    beside = (beside, (window if odd_window else blocks, 1))
+    second = send(own_kv, [(b, b + 4) for b in everyone])
 
     size = quarter_rows(heads)
     others = range(1, GROUP_BLOCKS)
@@ -734,13 +748,13 @@
 
     def first_attention(after):
         state["wide"], state["sum"] = attend(
-            place, (docs, flat(soft_query)), None, [(own_kv, (0, 0))], False, tokens, heads, kv_here, after
+            place, (docs, soft_query), None, [(own_kv, (0, 0))], False, tokens, heads, kv_here, after
         )
         return state["sum"]
 
-    def more_attention(kv, is_last, after):
+    def more_attention(kv, is_last, after, odd=None):
         state["sum"] = attend(
-            place, (state["wide"],), state["sum"], kv, is_last, tokens, heads, kv_here, after
+            place, (state["wide"],), state["sum"], kv, is_last, tokens, heads, kv_here, after, odd
         )
         return state["sum"]
 
@@ -755,35 +769,46 @@
         qh.append(got[1])
         return got[0]
 
-    done = first_attention([sent[0]])
-    run, ahead = group_map(place, quarters, size, [done], ahead)
-    lane_kv, cross_kv = [], []
-    for back in range(1, window // 2 + 1):
-        lane_kv.append((ahead, (2 * back, 2 * back)))
-        cross_kv.append((send(ahead, swap), (2 * back, 2 * back + 1)))
-        ahead = send(ahead, forward)
+    done = first_attention([sent[0], beside])
+    if parts > 1:
+        done = inner_of(0, [done])
+    run, lane = group_map(place, quarters, size, [done], [ahead])
+    lane_kv, cross_kv = [(lane, (2, 2)), (second, (4, 4))], [(send(lane, swap), (2, 3))]
     stages = (blocks // GROUP_BLOCKS).bit_length() - 1
     before, done = None, run
     for stage in range(stages):
         came = send(run, [(b, b ^ (GROUP_BLOCKS << stage)) for b in everyone])
         if stage == stages - 1:
-            for part in range(parts):
-                done = inner_of(part, [done])
+            done = more_attention(lane_kv, False, [done])
+            done = inner_of(parts - 1, [done])
         else:
             run, before = scan_step(place, stage + 2, run, came, before, size, [done])
             done = run
-    *priors, prior_doc = prior_states(place, stages + 1, quarters, came, before, size, [done])
+    *priors, prior_doc, own_copy, lane = prior_states(
+        place, stages + 1, quarters, came, before, size, [done], [own_kv, second]
+    )
     priors = [priors[0]] + [send(priors[j], [(b, b ^ j) for b in everyone]) for j in others]
-    done = more_attention([beside] + lane_kv[:1], False, [prior_doc])
-    rest = [kv for pair in zip(cross_kv, lane_kv[1:] + [None]) for kv in pair if kv is not None]
+    done = more_attention(cross_kv, False, [prior_doc])
+    far = None
+    if window % 2:
+        pairs = {b: b for b in everyone}
+        for b in range(1, blocks - window, 2):
+            pairs[b], pairs[b + window] = b + window, b
+        far = send(own_copy, list(pairs.items()))
+    rest = [(send(lane, swap), (4, 5))]
+    for back in range(3, window // 2 + 1):
+        lane = send(lane, forward)
+        rest.append((lane, (2 * back, 2 * back)))
+        rest.append((send(lane, swap), (2 * back, 2 * back + 1)))
+    slot = (beside if far is None else far, (blocks if far is None else window, 1))
     mixed, squares = mix(place, docs, prior_doc, cumul, inner, qh, priors, tokens, heads, [done])
     sums = [squares]
     for other in range(1, tensor):
         sums.append(lax.ppermute(squares, "tp", [(t, t ^ other) for t in range(tensor)]))
-    after = [squares]
+    rest, done = [slot] + rest, squares
     while rest:
-        got = more_attention(rest[:2], len(rest) <= 2, after)
-        rest, after = rest[2:], []
+        got = more_attention(rest[:2], len(rest) <= 2, [done], beside if rest[0] is slot else None)
+        rest, done = rest[2:], got
     soft_out, done = got
     lin_out = finish(norm_gain, flat(lin_gate), mixed, sums, tokens, heads, [done])
     shape = (tokens, heads, HEAD_DIM)

time: 58.9 us -> 70.1 us (1.19)
  starting transfers between devices: 17.7 us -> 22.9 us
  Pallas kernels: 27.2 us -> 30.2 us
  waiting for transfers between devices: 12.8 us -> 14.8 us
  local copies, waits for them, and re-layouts: 0.02 us -> 0.98 us
    ppermute x12 -> x13, starting transfers between devices: 15.8 us -> 21 us  [send(): return lax.ppermute(x, 'seq', [(a, b % blocks) for a, b in pairs])]
    pallas_call x12, Pallas kernels: 27.2 us -> 30.2 us  [call(): pl.pallas_call(run, out_shape=outs, in_specs=[SMEM] * len(scalars) + [HBM...]
    ppermute x12 -> x13, waiting for transfers between devices: 12.8 us -> 14.8 us  [send(): return lax.ppermute(x, 'seq', [(a, b % blocks) for a, b in pairs])]
    unnamed x8 -> x10, local copies, waits for them, and re-layouts: 0.02 us -> 0.98 us
  transfers between devices with their start and end apart: 15 -> 16, of which waited for: 4 -> 3; matrix products, arithmetic and copies ran while one was open for 0% -> 0% of each run, Pallas kernels for 39% -> 37%
where the time goes in v9:
time: 70.1 us; the launch traced here: 69.9 us
  Pallas kernels  30.2 us (43%)
  starting transfers between devices  22.9 us (33%)
  waiting for transfers between devices  14.8 us (21%)
  local copies, waits for them, and re-layouts  0.98 us (1%)
  between operations  0.98 us (1%)
    pallas_call x12, Pallas kernels, call(): pl.pallas_call(run, out_shape=outs, in_specs=[SMEM] * len(scalars) + [HBM...  30.2 us
    ppermute x13, starting transfers between devices, send(): return lax.ppermute(x, 'seq', [(a, b % blocks) for a, b in pairs])  21 us
    ppermute x13, waiting for transfers between devices, send(): return lax.ppermute(x, 'seq', [(a, b % blocks) for a, b in pairs])  14.8 us
    ppermute x3, starting transfers between devices, body(): lax.ppermute(squares, 'tp', [(t, t ^ other) for t in range(tensor)])  1.89 us
  transfers between devices with their start and end apart: 16, of which 3 were waited for; matrix products, arithmetic and copies ran while one was open for 0% of the time, Pallas kernels for 37%

profile of v9, /device:TPU:0, one launch (start us, length us, event | category | flops | bytes accessed | tf_op | source)
XLA Modules:
  0.0 69.9 jit_solution(16590765703357548871)
XLA Ops:
  0.6 3.0 %fetch.1 = (bf16[1040,128]{1,0:T(8,128)(2,1)}, f32[16,128]{1,0:T(8,128)S(1)}, f32[256,128]{1,0:T(8,128)S(1)}, bf16[4096,128]{1,0:T(8,128)(2,1)S(1)}, bf16[4096,1...) custom-call(s32[1]{0:T(128)} %bitcast.2.refs_0_, s32[2,128]{1,0:T(2,128)} %bitcast.23, f32[16,256]{1,0:T(8,128)} %bitcast.22, ...), custom_call_target="tpu_custom_call" | custom-call | bytes 393216 | tf_op jit(solution)/shard_map/fetch/pallas_call | solution.py:68
  3.6 0.0 copy-start.2
  3.6 1.0 %copy-done.2 = bf16[4096,128]{1,0:T(8,128)(2,1)} copy-done((bf16[4096,128]{1,0:T(8,128)(2,1)}, bf16[4096,128]{1,0:T(8,128)(2,1)S(1)}, u32[]{:S(2)}) %copy-start.2) | copy-done | bytes 1048600
  4.6 3.0 %collective-permute-start.3 = (bf16[1040,128]{1,0:T(8,128)(2,1)}, bf16[1040,128]{1,0:T(8,128)(2,1)S(1)}, u32[]{:S(2)}, u32[]{:S(2)}) collective-permute-start(bf16[1040,128]{1,0:T(8,128)(2,1)} %get-tuple-element.40.refs_3_.refs_7_), channel_id=1, source_target_pairs={{0,4},{4,0},{8,12},{12,8},{16,20},{20,16},{24,28},{28,24},{1,5},{5... | collective-permute-start | bytes 798728 | tf_op jit(solution)/shard_map/ppermute | solution.py:716
  7.6 1.6 %collective-permute-start.4 = (bf16[1040,128]{1,0:T(8,128)(2,1)}, bf16[1040,128]{1,0:T(8,128)(2,1)}, u32[]{:S(2)}, u32[]{:S(2)}) collective-permute-start(bf16[1040,128]{1,0:T(8,128)(2,1)} %get-tuple-element.40.refs_3_.refs_7_), channel_id=1, source_target_pairs={{0,8},{4,12},{8,16},{12,20},{16,24},{20,28},{24,0},{28,4},{1,9},{5... | collective-permute-start | bytes 798728 | tf_op jit(solution)/shard_map/ppermute | solution.py:716
  9.1 2.6 %collective-permute-start.6 = (bf16[1040,128]{1,0:T(8,128)(2,1)}, bf16[1040,128]{1,0:T(8,128)(2,1)}, u32[]{:S(2)}, u32[]{:S(2)}) collective-permute-start(bf16[1040,128]{1,0:T(8,128)(2,1)} %get-tuple-element.40.refs_3_.refs_7_), channel_id=1, source_target_pairs={{0,16},{4,20},{8,24},{12,28},{16,0},{20,4},{24,8},{28,12},{1,17},{... | collective-permute-start | bytes 798728 | tf_op jit(solution)/shard_map/ppermute | solution.py:716
  11.7 2.7 %block_state.1 = (bf16[528,128]{1,0:T(8,128)(2,1)S(1)}, bf16[528,128]{1,0:T(8,128)(2,1)S(1)}, bf16[528,128]{1,0:T(8,128)(2,1)S(1)}, bf16[528,128]{1,0:T(8,128)(2,1)S(1)}) custom-call(s32[1]{0:T(128)} %bitcast.1.refs_0_, f32[256,128]{1,0:T(8,128)S(1)} %get-tuple-element.32.refs_1_.refs_0_.refs_3_, f32[16,128]{1,0:T(8,128)S(1)} %get-tuple-element.31.refs_2_.refs_1_, ...), custom_call_target="tpu_custom_call" | custom-call | flops 16777216 | bytes 655360 | tf_op jit(solution)/shard_map/block_state/pallas_call | solution.py:68
  14.5 0.6 collective-permute-start
  15.0 0.0 collective-permute-start.1
  15.0 0.0 collective-permute-done.3.refs_5_
  15.0 3.0 %collective-permute-start.2 = (bf16[528,128]{1,0:T(8,128)(2,1)S(1)}, bf16[528,128]{1,0:T(8,128)(2,1)S(1)}, u32[]{:S(2)}, u32[]{:S(2)}) collective-permute-start(bf16[528,128]{1,0:T(8,128)(2,1)S(1)} %get-tuple-element.38), channel_id=1, source_target_pairs={{0,12},{4,8},{8,4},{12,0},{16,28},{20,24},{24,20},{28,16},{1,13},{... | collective-permute-start | bytes 405512 | tf_op jit(solution)/shard_map/ppermute | solution.py:716
  18.0 0.0 copy-done.3
  18.0 3.6 %attend.4 = (bf16[2,2048,256]{2,1,0:T(8,128)(2,1)S(1)}, f32[2,144,2048]{2,1,0:T(8,128)S(1)}) custom-call(s32[1]{0:T(128)} %bitcast.1.refs_0_, f32[16,128]{1,0:T(8,128)S(1)} %get-tuple-element.31.refs_2_.refs_1_, bf16[4096,128]{1,0:T(8,128)(2,1)S(1)} %copy-done.3, bf16[1040,128]{1,0:T(8,128)(2,1)} %get-tuple-element.40.refs_3_.refs_7_, ...), custom_call_target="tpu_custom_call" | custom-call | flops 134217728 | bytes 1048576 | tf_op jit(solution)/shard_map/attend/pallas_call | solution.py:68
  21.6 0.0 copy-done
  21.6 1.9 %inner_part.2 = (f32[2048,128]{1,0:T(8,128)S(1)}, bf16[2048,128]{1,0:T(8,128)(2,1)S(1)}) custom-call(f32[256,128]{1,0:T(8,128)S(1)} %get-tuple-element.32.refs_1_.refs_0_.refs_3_, f32[16,128]{1,0:T(8,128)S(1)} %get-tuple-element.31.refs_2_.refs_1_, bf16[4096,128]{1,0:T(8,128)(2,1)S(1)} %bitcast.13, bf16[4096,128]{1,0:T(8,128)(2,1)S(1)} %get-tuple-element.33.refs_3_, ...), custom_call_target="tpu_custom_call" | custom-call | flops 33554432 | bytes 786432 | tf_op jit(solution)/shard_map/inner_part/pallas_call | solution.py:68
  23.5 0.0 collective-permute-done.refs_2_
  23.5 1.3 %collective-permute-done.1.refs_3_ = bf16[528,128]{1,0:T(8,128)(2,1)S(1)} collective-permute-done((bf16[528,128]{1,0:T(8,128)(2,1)S(1)}, bf16[528,128]{1,0:T(8,128)(2,1)S(1)}, u32[]{:S(2)}, u32[]{:S(2)}) %collective-permute-start.1) | collective-permute-done | bytes 135200 | tf_op jit(solution)/shard_map/ppermute | solution.py:716
  24.8 4.6 %collective-permute-done.2.refs_4_ = bf16[528,128]{1,0:T(8,128)(2,1)S(1)} collective-permute-done((bf16[528,128]{1,0:T(8,128)(2,1)S(1)}, bf16[528,128]{1,0:T(8,128)(2,1)S(1)}, u32[]{:S(2)}, u32[]{:S(2)}) %collective-permute-start.2) | collective-permute-done | bytes 135200 | tf_op jit(solution)/shard_map/ppermute | solution.py:716
  29.4 0.0 collective-permute-done.4.refs_6_
  29.4 1.2 %group_map.1 = (bf16[528,128]{1,0:T(8,128)(2,1)S(1)}, bf16[1040,128]{1,0:T(8,128)(2,1)S(1)}) custom-call(s32[1]{0:T(128)} %bitcast.1.refs_0_, bf16[528,128]{1,0:T(8,128)(2,1)S(1)} %get-tuple-element.35.refs_4_.refs_1_, bf16[528,128]{1,0:T(8,128)(2,1)S(1)} %collective-permute-done.refs_2_, bf16[528,128]{1,0:T(8,128)(2,1)S(1)} %collective-permute-done.1.refs_3_, ...), custom_call_target="tpu_custom_call" | custom-call | flops 65536 | bytes 163840 | tf_op jit(solution)/shard_map/group_map/pallas_call | solution.py:68
  30.6 0.2 collective-permute-start.5
  30.8 1.5 %collective-permute-start.10 = (bf16[1040,128]{1,0:T(8,128)(2,1)S(1)}, bf16[1040,128]{1,0:T(8,128)(2,1)S(1)}, u32[]{:S(2)}, u32[]{:S(2)}) collective-permute-start(bf16[1040,128]{1,0:T(8,128)(2,1)S(1)} %get-tuple-element.45.refs_3_), channel_id=1, source_target_pairs={{0,4},{4,0},{8,12},{12,8},{16,20},{20,16},{24,28},{28,24},{1,5},{5... | collective-permute-start | bytes 798728 | tf_op jit(solution)/shard_map/ppermute | solution.py:716
  32.4 0.0 collective-permute-done.6.refs_4_.refs_8_
  32.4 4.5 %attend.5.refs_5_.refs_2_ = f32[2,144,2048]{2,1,0:T(8,128)S(1)} custom-call(s32[1]{0:T(128)} %bitcast.1.refs_0_, bf16[2,2048,256]{2,1,0:T(8,128)(2,1)S(1)} %get-tuple-element.44.refs_1_, f32[2,144,2048]{2,1,0:T(8,128)S(1)} %get-tuple-element.41.refs_5_.refs_2_, bf16[1040,128]{1,0:T(8,128)(2,1)S(1)} %get-tuple-element.45.refs_3_, ...), custom_call_target="tpu_custom_call" | custom-call | flops 268435456 | bytes 1048576 | tf_op jit(solution)/shard_map/attend/pallas_call | solution.py:68
  36.9 1.9 %inner_part.3 = (f32[2048,128]{1,0:T(8,128)S(1)}, bf16[2048,128]{1,0:T(8,128)(2,1)S(1)}) custom-call(f32[256,128]{1,0:T(8,128)S(1)} %get-tuple-element.32.refs_1_.refs_0_.refs_3_, f32[16,128]{1,0:T(8,128)S(1)} %get-tuple-element.31.refs_2_.refs_1_, bf16[4096,128]{1,0:T(8,128)(2,1)S(1)} %bitcast.14, bf16[4096,128]{1,0:T(8,128)(2,1)S(1)} %get-tuple-element.33.refs_3_, ...), custom_call_target="tpu_custom_call" | custom-call | flops 33554432 | bytes 786432 | tf_op jit(solution)/shard_map/inner_part/pallas_call | solution.py:68
  38.8 0.0 collective-permute-done.5.refs_5_
  38.8 1.3 %prior_states.1 = (bf16[512,128]{1,0:T(8,128)(2,1)S(1)}, bf16[512,128]{1,0:T(8,128)(2,1)S(1)}, bf16[512,128]{1,0:T(8,128)(2,1)S(1)}, bf16[512,128]{1,0:T(8,128)(...) custom-call(s32[1]{0:T(128)} %bitcast.1.refs_0_, ...), custom_call_target="tpu_custom_call" | custom-call | flops 65536 | bytes 163840 | tf_op jit(solution)/shard_map/prior_states/pallas_call | solution.py:68
  40.1 0.9 %collective-permute-start.14 = (bf16[1040,128]{1,0:T(8,128)(2,1)S(1)}, bf16[1040,128]{1,0:T(8,128)(2,1)S(1)}, u32[]{:S(2)}, u32[]{:S(2)}) collective-permute-start(bf16[1040,128]{1,0:T(8,128)(2,1)S(1)} %get-tuple-element.56), channel_id=1, source_target_pairs={{0,0},{4,24},{8,8},{12,12},{16,16},{20,20},{24,4},{28,28},{1,1},{5... | collective-permute-start | bytes 798728 | tf_op jit(solution)/shard_map/ppermute | solution.py:716
  41.0 4.3 %collective-permute-start.15 = (bf16[1040,128]{1,0:T(8,128)(2,1)S(1)}, bf16[1040,128]{1,0:T(8,128)(2,1)S(1)}, u32[]{:S(2)}, u32[]{:S(2)}) collective-permute-start(bf16[1040,128]{1,0:T(8,128)(2,1)S(1)} %get-tuple-element.57), channel_id=1, source_target_pairs={{0,4},{4,0},{8,12},{12,8},{16,20},{20,16},{24,28},{28,24},{1,5},{5... | collective-permute-start | bytes 798728 | tf_op jit(solution)/shard_map/ppermute | solution.py:716
  45.2 0.1 collective-permute-start.7
  45.3 0.0 collective-permute-start.8
  45.3 0.0 collective-permute-done.10.refs_3_
  45.3 3.4 %collective-permute-start.9 = (bf16[512,128]{1,0:T(8,128)(2,1)S(1)}, bf16[512,128]{1,0:T(8,128)(2,1)S(1)}, u32[]{:S(2)}, u32[]{:S(2)}) collective-permute-start(bf16[512,128]{1,0:T(8,128)(2,1)S(1)} %get-tuple-element.53), channel_id=1, source_target_pairs={{0,12},{4,8},{8,4},{12,0},{16,28},{20,24},{24,20},{28,16},{1,13},{... | collective-permute-start | bytes 393224 | tf_op jit(solution)/shard_map/ppermute | solution.py:716
  48.7 2.3 %attend.6.refs_12_.refs_2_ = f32[2,144,2048]{2,1,0:T(8,128)S(1)} custom-call(s32[1]{0:T(128)} %bitcast.1.refs_0_, bf16[2,2048,256]{2,1,0:T(8,128)(2,1)S(1)} %get-tuple-element.44.refs_1_, f32[2,144,2048]{2,1,0:T(8,128)S(1)} %attend.5.refs_5_.refs_2_, bf16[1040,128]{1,0:T(8,128)(2,1)S(1)} %collective-permute-done.10.refs_3_, ...), custom_call_target="tpu_custom_call" | custom-call | flops 134217728 | bytes 1048576 | tf_op jit(solution)/shard_map/attend/pallas_call | solution.py:68
  51.0 8.9 %collective-permute-done.7.refs_9_ = bf16[512,128]{1,0:T(8,128)(2,1)S(1)} collective-permute-done((bf16[512,128]{1,0:T(8,128)(2,1)S(1)}, bf16[512,128]{1,0:T(8,128)(2,1)S(1)}, u32[]{:S(2)}, u32[]{:S(2)}) %collective-permute-start.7) | collective-permute-done | bytes 131104 | tf_op jit(solution)/shard_map/ppermute | solution.py:716
  59.9 0.0 collective-permute-done.8.refs_10_
  59.9 0.0 collective-permute-done.9.refs_11_
  59.9 1.6 %mix.1 = (f32[4096,128]{1,0:T(8,128)S(1)}, f32[8,256]{1,0:T(8,128)S(1)}) custom-call(s32[1]{0:T(128)} %bitcast.1.refs_0_, f32[16,128]{1,0:T(8,128)S(1)} %get-tuple-element.31.refs_2_.refs_1_, f32[8,128]{1,0:T(8,128)S(1)} %get-tuple-element.47.refs_4_.refs_2_, f32[256,128]{1,0:T(8,128)S(1)} %get-tuple-element.32.refs_1_.refs_0_.refs_3_, ...), custom_call_target="tpu_custom_call" | custom-call | flops 16777216 | bytes 655360 | tf_op jit(solution)/shard_map/mix/pallas_call | solution.py:68
  61.5 0.4 collective-permute-start.13
  61.9 1.2 %collective-permute-start.12 = (f32[8,256]{1,0:T(8,128)S(1)}, f32[8,256]{1,0:T(8,128)S(1)}, u32[]{:S(2)}, u32[]{:S(2)}) collective-permute-start(f32[8,256]{1,0:T(8,128)S(1)} %get-tuple-element.55.refs_6_.refs_3_), channel_id=1, source_target_pairs={{0,2},{1,3},{2,0},{3,1},{4,6},{5,7},{6,4},{7,5},{8,10},{9,11},{10,... | collective-permute-start | bytes 24584 | tf_op jit(solution)/shard_map/ppermute | solution.py:807
  63.1 0.3 collective-permute-start.11
  63.4 0.0 collective-permute-done.14.refs_3_
  63.4 0.0 collective-permute-done.15.refs_4_
  63.4 4.6 %attend.7 = (bf16[4096,128]{1,0:T(8,128)(2,1)}, f32[8,128]{1,0:T(8,128)S(1)}) custom-call(s32[1]{0:T(128)} %bitcast.1.refs_0_, bf16[2,2048,256]{2,1,0:T(8,128)(2,1)S(1)} %get-tuple-element.44.refs_1_, f32[2,144,2048]{2,1,0:T(8,128)S(1)} %attend.6.refs_12_.refs_2_, bf16[1040,128]{1,0:T(8,128)(2,1)S(1)} %collective-permute-done.14.refs_3_, ...), custom_call_target="tpu_custom_call" | custom-call | flops 268435456 | bytes 1048576 | tf_op jit(solution)/shard_map/attend/pallas_call | solution.py:68
  68.0 0.0 collective-permute-done.13.refs_6_
  68.0 0.0 collective-permute-done.12.refs_5_
  68.0 0.0 collective-permute-done.11.refs_4_
  68.1 1.6 %finish.1 = bf16[4096,128]{1,0:T(8,128)(2,1)} custom-call(f32[16,128]{1,0:T(8,128)S(1)} %copy-done.4, bf16[4096,128]{1,0:T(8,128)(2,1)S(1)} %bitcast.15, f32[4096,128]{1,0:T(8,128)S(1)} %get-tuple-element.54.refs_2_, f32[8,256]{1,0:T(8,128)S(1)} %get-tuple-element.55.refs_6_.refs_3_, f32[8,256]{1,0:T(8,128)S(1)} %collective-permute-done.11.refs_4_, ...), custom_call_target="tpu_custom_call" | custom-call | bytes 524288 | tf_op jit(solution)/shard_map/finish/pallas_call | solution.py:68
  (6 shorter events, 0.0 us)
Async XLA Ops:
  3.6 1.0 %copy-start.2 = (bf16[4096,128]{1,0:T(8,128)(2,1)}, bf16[4096,128]{1,0:T(8,128)(2,1)S(1)}, u32[]{:S(2)}) copy-start(bf16[4096,128]{1,0:T(8,128)(2,1)S(1)} %get-tuple-element.39.refs_2_) | copy-start | bytes 3145732
  4.6 17.0 %copy-start = (bf16[256,16,128]{2,1,0:T(8,128)(2,1)S(1)}, bf16[256,16,128]{2,1,0:T(8,128)(2,1)}, u32[]{:S(2)}) copy-start(bf16[256,16,128]{2,1,0:T(8,128)(2,1)} %param.10) | copy-start | bytes 3145732
  4.6 10.4 %collective-permute-start.3 = (bf16[1040,128]{1,0:T(8,128)(2,1)}, bf16[1040,128]{1,0:T(8,128)(2,1)S(1)}, u32[]{:S(2)}, u32[]{:S(2)}) collective-permute-start(bf16[1040,128]{1,0:T(8,128)(2,1)} %get-tuple-element.40.refs_3_.refs_7_), channel_id=1, source_target_pairs={{0,4},{4,0},{8,12},{12,8},{16,20},{20,16},{24,28},{28,24},{1,5},{5... | collective-permute-start | bytes 798728 | tf_op jit(solution)/shard_map/ppermute | solution.py:716
  7.6 21.8 %collective-permute-start.4 = (bf16[1040,128]{1,0:T(8,128)(2,1)}, bf16[1040,128]{1,0:T(8,128)(2,1)}, u32[]{:S(2)}, u32[]{:S(2)}) collective-permute-start(bf16[1040,128]{1,0:T(8,128)(2,1)} %get-tuple-element.40.refs_3_.refs_7_), channel_id=1, source_target_pairs={{0,8},{4,12},{8,16},{12,20},{16,24},{20,28},{24,0},{28,4},{1,9},{5... | collective-permute-start | bytes 798728 | tf_op jit(solution)/shard_map/ppermute | solution.py:716
  9.1 23.2 %collective-permute-start.6 = (bf16[1040,128]{1,0:T(8,128)(2,1)}, bf16[1040,128]{1,0:T(8,128)(2,1)}, u32[]{:S(2)}, u32[]{:S(2)}) collective-permute-start(bf16[1040,128]{1,0:T(8,128)(2,1)} %get-tuple-element.40.refs_3_.refs_7_), channel_id=1, source_target_pairs={{0,16},{4,20},{8,24},{12,28},{16,0},{20,4},{24,8},{28,12},{1,17},{... | collective-permute-start | bytes 798728 | tf_op jit(solution)/shard_map/ppermute | solution.py:716
  11.7 6.3 %copy-start.3 = (bf16[4096,128]{1,0:T(8,128)(2,1)S(1)}, bf16[4096,128]{1,0:T(8,128)(2,1)}, u32[]{:S(2)}) copy-start(bf16[4096,128]{1,0:T(8,128)(2,1)} %copy-done.2) | copy-start | bytes 3145732
  14.5 9.1 %collective-permute-start = (bf16[528,128]{1,0:T(8,128)(2,1)S(1)}, bf16[528,128]{1,0:T(8,128)(2,1)S(1)}, u32[]{:S(2)}, u32[]{:S(2)}) collective-permute-start(bf16[528,128]{1,0:T(8,128)(2,1)S(1)} %get-tuple-element.36), channel_id=1, source_target_pairs={{0,4},{4,0},{8,12},{12,8},{16,20},{20,16},{24,28},{28,24},{1,5},{5... | collective-permute-start | bytes 405512 | tf_op jit(solution)/shard_map/ppermute | solution.py:716
  15.0 9.8 %collective-permute-start.1 = (bf16[528,128]{1,0:T(8,128)(2,1)S(1)}, bf16[528,128]{1,0:T(8,128)(2,1)S(1)}, u32[]{:S(2)}, u32[]{:S(2)}) collective-permute-start(bf16[528,128]{1,0:T(8,128)(2,1)S(1)} %get-tuple-element.37), channel_id=1, source_target_pairs={{0,8},{4,12},{8,0},{12,4},{16,24},{20,28},{24,16},{28,20},{1,9},{5... | collective-permute-start | bytes 405512 | tf_op jit(solution)/shard_map/ppermute | solution.py:716
  15.0 14.4 %collective-permute-start.2 = (bf16[528,128]{1,0:T(8,128)(2,1)S(1)}, bf16[528,128]{1,0:T(8,128)(2,1)S(1)}, u32[]{:S(2)}, u32[]{:S(2)}) collective-permute-start(bf16[528,128]{1,0:T(8,128)(2,1)S(1)} %get-tuple-element.38), channel_id=1, source_target_pairs={{0,12},{4,8},{8,4},{12,0},{16,28},{20,24},{24,20},{28,16},{1,13},{... | collective-permute-start | bytes 405512 | tf_op jit(solution)/shard_map/ppermute | solution.py:716
  30.6 8.2 %collective-permute-start.5 = (bf16[528,128]{1,0:T(8,128)(2,1)S(1)}, bf16[528,128]{1,0:T(8,128)(2,1)S(1)}, u32[]{:S(2)}, u32[]{:S(2)}) collective-permute-start(bf16[528,128]{1,0:T(8,128)(2,1)S(1)} %get-tuple-element.43.refs_5_), channel_id=1, source_target_pairs={{0,16},{4,20},{8,24},{12,28},{16,0},{20,4},{24,8},{28,12},{1,17},{... | collective-permute-start | bytes 405512 | tf_op jit(solution)/shard_map/ppermute | solution.py:716
  30.8 14.5 %collective-permute-start.10 = (bf16[1040,128]{1,0:T(8,128)(2,1)S(1)}, bf16[1040,128]{1,0:T(8,128)(2,1)S(1)}, u32[]{:S(2)}, u32[]{:S(2)}) collective-permute-start(bf16[1040,128]{1,0:T(8,128)(2,1)S(1)} %get-tuple-element.45.refs_3_), channel_id=1, source_target_pairs={{0,4},{4,0},{8,12},{12,8},{16,20},{20,16},{24,28},{28,24},{1,5},{5... | collective-permute-start | bytes 798728 | tf_op jit(solution)/shard_map/ppermute | solution.py:716
  40.1 23.3 %collective-permute-start.14 = (bf16[1040,128]{1,0:T(8,128)(2,1)S(1)}, bf16[1040,128]{1,0:T(8,128)(2,1)S(1)}, u32[]{:S(2)}, u32[]{:S(2)}) collective-permute-start(bf16[1040,128]{1,0:T(8,128)(2,1)S(1)} %get-tuple-element.56), channel_id=1, source_target_pairs={{0,0},{4,24},{8,8},{12,12},{16,16},{20,20},{24,4},{28,28},{1,1},{5... | collective-permute-start | bytes 798728 | tf_op jit(solution)/shard_map/ppermute | solution.py:716
  41.0 22.4 %collective-permute-start.15 = (bf16[1040,128]{1,0:T(8,128)(2,1)S(1)}, bf16[1040,128]{1,0:T(8,128)(2,1)S(1)}, u32[]{:S(2)}, u32[]{:S(2)}) collective-permute-start(bf16[1040,128]{1,0:T(8,128)(2,1)S(1)} %get-tuple-element.57), channel_id=1, source_target_pairs={{0,4},{4,0},{8,12},{12,8},{16,20},{20,16},{24,28},{28,24},{1,5},{5... | collective-permute-start | bytes 798728 | tf_op jit(solution)/shard_map/ppermute | solution.py:716
  45.2 14.7 %collective-permute-start.7 = (bf16[512,128]{1,0:T(8,128)(2,1)S(1)}, bf16[512,128]{1,0:T(8,128)(2,1)S(1)}, u32[]{:S(2)}, u32[]{:S(2)}) collective-permute-start(bf16[512,128]{1,0:T(8,128)(2,1)S(1)} %get-tuple-element.51), channel_id=1, source_target_pairs={{0,4},{4,0},{8,12},{12,8},{16,20},{20,16},{24,28},{28,24},{1,5},{5... | collective-permute-start | bytes 393224 | tf_op jit(solution)/shard_map/ppermute | solution.py:716
  45.3 14.6 %collective-permute-start.8 = (bf16[512,128]{1,0:T(8,128)(2,1)S(1)}, bf16[512,128]{1,0:T(8,128)(2,1)S(1)}, u32[]{:S(2)}, u32[]{:S(2)}) collective-permute-start(bf16[512,128]{1,0:T(8,128)(2,1)S(1)} %get-tuple-element.52), channel_id=1, source_target_pairs={{0,8},{4,12},{8,0},{12,4},{16,24},{20,28},{24,16},{28,20},{1,9},{5... | collective-permute-start | bytes 393224 | tf_op jit(solution)/shard_map/ppermute | solution.py:716
  45.3 14.6 %collective-permute-start.9 = (bf16[512,128]{1,0:T(8,128)(2,1)S(1)}, bf16[512,128]{1,0:T(8,128)(2,1)S(1)}, u32[]{:S(2)}, u32[]{:S(2)}) collective-permute-start(bf16[512,128]{1,0:T(8,128)(2,1)S(1)} %get-tuple-element.53), channel_id=1, source_target_pairs={{0,12},{4,8},{8,4},{12,0},{16,28},{20,24},{24,20},{28,16},{1,13},{... | collective-permute-start | bytes 393224 | tf_op jit(solution)/shard_map/ppermute | solution.py:716
  61.5 6.5 %copy-start.1 = (bf16[256,16,128]{2,1,0:T(8,128)(2,1)S(1)}, bf16[256,16,128]{2,1,0:T(8,128)(2,1)}, u32[]{:S(2)}) copy-start(bf16[256,16,128]{2,1,0:T(8,128)(2,1)} %param.13) | copy-start | bytes 3145732
  61.5 6.6 %copy-start.4 = (f32[16,128]{1,0:T(8,128)S(1)}, f32[16,128]{1,0:T(8,128)}, u32[]{:S(2)}) copy-start(f32[16,128]{1,0:T(8,128)} %refs_0_.1) | copy-start | bytes 24580
  61.5 6.5 %collective-permute-start.13 = (f32[8,256]{1,0:T(8,128)S(1)}, f32[8,256]{1,0:T(8,128)S(1)}, u32[]{:S(2)}, u32[]{:S(2)}) collective-permute-start(f32[8,256]{1,0:T(8,128)S(1)} %get-tuple-element.55.refs_6_.refs_3_), channel_id=1, source_target_pairs={{0,3},{1,2},{2,1},{3,0},{4,7},{5,6},{6,5},{7,4},{8,11},{9,10},{10,... | collective-permute-start | bytes 24584 | tf_op jit(solution)/shard_map/ppermute | solution.py:807
  61.9 6.1 %collective-permute-start.12 = (f32[8,256]{1,0:T(8,128)S(1)}, f32[8,256]{1,0:T(8,128)S(1)}, u32[]{:S(2)}, u32[]{:S(2)}) collective-permute-start(f32[8,256]{1,0:T(8,128)S(1)} %get-tuple-element.55.refs_6_.refs_3_), channel_id=1, source_target_pairs={{0,2},{1,3},{2,0},{3,1},{4,6},{5,7},{6,4},{7,5},{8,10},{9,11},{10,... | collective-permute-start | bytes 24584 | tf_op jit(solution)/shard_map/ppermute | solution.py:807
  63.1 4.9 %collective-permute-start.11 = (f32[8,256]{1,0:T(8,128)S(1)}, f32[8,256]{1,0:T(8,128)S(1)}, u32[]{:S(2)}, u32[]{:S(2)}) collective-permute-start(f32[8,256]{1,0:T(8,128)S(1)} %get-tuple-element.55.refs_6_.refs_3_), channel_id=1, source_target_pairs={{0,1},{1,0},{2,3},{3,2},{4,5},{5,4},{6,7},{7,6},{8,9},{9,8},{10,11... | collective-permute-start | bytes 24584 | tf_op jit(solution)/shard_map/ppermute | solution.py:807

commit v10 on v9

--- a/solution.py
+++ b/solution.py
@@ -35,7 +35,7 @@
 
 def cost(flops, bytes_accessed, transcendentals=0):
     return pl.CostEstimate(
-        flops=int(flops) // 8, bytes_accessed=int(bytes_accessed) // 8, transcendentals=int(transcendentals) // 8
+        flops=int(flops) , bytes_accessed=int(bytes_accessed) , transcendentals=int(transcendentals)
     )
 
 
@@ -99,12 +99,12 @@
 def fetch_kernel(tokens, heads, kv_here, start_ref, *refs):
     refs = list(refs)
     take = lambda n: [refs.pop(0) for _ in range(n)]
-    sources = take(7)
-    kv_ref, doc_out, cumul_ref, key_out, value_out, query_out = take(6)
+    sources = take(6)
+    kv_ref, doc_out, cumul_ref, key_out, value_out = take(5)
     held = take(4)
     sems, wide, ldp = refs
     docs_in, decays, soft_key, soft_value = held
-    targets = [*held, key_out, value_out, query_out]
+    targets = [*held, key_out, value_out]
     copies = [
         pltpu.make_async_copy(source, target, sems.at[i])
         for i, (source, target) in enumerate(zip(sources, targets))
@@ -160,7 +160,6 @@
             sds((tokens, LANES), F32),
             sds(operands[4].shape, BF16),
             sds(operands[5].shape, BF16),
-            sds(operands[6].shape, BF16),
         ),
         scratch=[pltpu.VMEM(x.shape, x.dtype) for x in operands[:4]]
         + [
@@ -384,7 +383,7 @@
     doc_ref[...] = jnp.broadcast_to(own_doc, (8, LANES))
 
 
-def prior_states(place, bit, quarters, came, before, size, after, relay):
+def prior_states(place, bit, quarters, came, before, size, after, relay=()):
     before = [] if before is None else [before]
     return call(
         functools.partial(prior_kernel, size, len(before), bit),
@@ -535,7 +534,7 @@
     )
 
 
-def attend_kernel(tokens, heads, kv_here, least, has_choice, is_first, is_last, unroll, place_ref, *refs):
+def attend_kernel(tokens, heads, kv_here, least, is_first, is_last, unroll, place_ref, *refs):
     refs = list(refs)
     take = lambda n: [refs.pop(0) for _ in range(n)]
     per_group = heads // kv_here
@@ -546,7 +545,6 @@
     else:
         wide_ref, state_ref = take(2)
     kv = take(len(least))
-    other = take(1)[0] if has_choice else None
     if is_first:
         wide_ref = take(1)[0]
     out_ref = take(1)[0]
@@ -558,10 +556,6 @@
     if is_last:
         done, sems = take(2)
     block = place_ref[0]
-    if has_choice:
-        slot = take(1)[0]
-        slot[...] = jnp.where(block % 2 == 0, kv[0][...], other[...])
-        kv[0] = slot
 
     lane = lax.broadcasted_iota(jnp.int32, (tokens, LANES), 1).astype(F32)
     end = 2 * kv_here * tokens
@@ -651,7 +645,7 @@
             pltpu.make_async_copy(done.at[at, :], out_ref.at[at, :], sems.at[c]).wait()
 
 
-def attend(place, first, state, kv, is_last, tokens, heads, kv_here, after, odd=None):
+def attend(place, first, state, kv, is_last, tokens, heads, kv_here, after, relay=()):
     is_first = state is None
     least = tuple(pair for _, pair in kv)
     kv = [block for block, _ in kv]
@@ -669,14 +663,12 @@
         out_shape = (out_shape, sds((8, LANES), F32))
         scratch.append(pltpu.VMEM((tokens * heads, LANES), BF16))
         scratch.append(pltpu.SemaphoreType.DMA((rows // CHUNK,)))
-    if odd is not None:
-        scratch.append(pltpu.VMEM(odd.shape, BF16))
     span = blocks * tokens
     return call(
-        functools.partial(attend_kernel, tokens, heads, kv_here, least, odd is not None, is_first, is_last, unroll),
+        functools.partial(attend_kernel, tokens, heads, kv_here, least, is_first, is_last, unroll),
         "attend",
         [place],
-        [*first, *([] if is_first else [state]), *kv, *([] if odd is None else [odd])],
+        [*first, *([] if is_first else [state]), *kv],
         out_shape,
         scratch=scratch,
         mib=24,
@@ -685,6 +677,7 @@
         ),
         after=after,
         out_hbm=is_last,
+        relay=relay,
     )
 
 
@@ -718,7 +711,7 @@
     everyone = range(blocks)
     swap = [(b, b ^ 1) for b in everyone]
 
-    own_kv, docs, cumul, key, value, soft_query = fetch(
+    own_kv, docs, cumul, key, value = fetch(
         start,
         [
             doc_ids.reshape(tokens // LANES, LANES),
@@ -727,7 +720,6 @@
             flat(soft_value),
             flat(lin_key),
             flat(lin_value),
-            flat(soft_query),
         ],
         tokens,
         heads,
@@ -735,9 +727,13 @@
     )
 
     forward = [(b, b + 2) for b in everyone]
-    beside = send(own_kv, swap)
+    pairs = [(b, b + 1) for b in everyone if b % 2 == 0]
+    longest_hop = [b for b in everyone if b % 2 and b + window < blocks] if window % 2 else []
+    pairs += [(b, b + window) for b in longest_hop]
+    taken = [b + window for b in longest_hop]
+    pairs += [(b, b - 1) for b in everyone if b % 2 and b not in longest_hop and b - 1 not in taken]
+    beside = (send(own_kv, pairs), (window if window % 2 else blocks, 1))
     ahead = send(own_kv, forward)
-    second = send(own_kv, [(b, b + 4) for b in everyone])
 
     size = quarter_rows(heads)
     others = range(1, GROUP_BLOCKS)
@@ -746,17 +742,19 @@
 
     state = {}
 
-    def first_attention(after):
-        state["wide"], state["sum"] = attend(
-            place, (docs, soft_query), None, [(own_kv, (0, 0))], False, tokens, heads, kv_here, after
+    def first_attention(after, relay):
+        state["wide"], *out = attend(
+            place, (docs, flat(soft_query)), None, [(own_kv, (0, 0))], False, tokens, heads, kv_here, after, relay
         )
-        return state["sum"]
-
-    def more_attention(kv, is_last, after, odd=None):
-        state["sum"] = attend(
-            place, (state["wide"],), state["sum"], kv, is_last, tokens, heads, kv_here, after, odd
+        state["sum"] = out[0]
+        return out
+
+    def more_attention(kv, is_last, after, relay=()):
+        out = attend(
+            place, (state["wide"],), state["sum"], kv, is_last, tokens, heads, kv_here, after, relay
         )
-        return state["sum"]
+        state["sum"] = out[0] if relay else out
+        return out
 
     inner, qh = [], []
 
@@ -769,45 +767,39 @@
         qh.append(got[1])
         return got[0]
 
-    done = first_attention([sent[0], beside])
+    done, lane = first_attention([sent[0], beside[0]], [ahead])
+    second = send(lane, [(b, b + 2) for b in range(2, blocks - 2)])
     if parts > 1:
         done = inner_of(0, [done])
-    run, lane = group_map(place, quarters, size, [done], [ahead])
-    lane_kv, cross_kv = [(lane, (2, 2)), (second, (4, 4))], [(send(lane, swap), (2, 3))]
+    run, lane = group_map(place, quarters, size, [done], [lane])
+    first_cross = send(lane, swap)
     stages = (blocks // GROUP_BLOCKS).bit_length() - 1
     before, done = None, run
     for stage in range(stages):
         came = send(run, [(b, b ^ (GROUP_BLOCKS << stage)) for b in everyone])
         if stage == stages - 1:
-            done = more_attention(lane_kv, False, [done])
+            done = more_attention([beside, (lane, (2, 2))], False, [done])
             done = inner_of(parts - 1, [done])
         else:
             run, before = scan_step(place, stage + 2, run, came, before, size, [done])
             done = run
-    *priors, prior_doc, own_copy, lane = prior_states(
-        place, stages + 1, quarters, came, before, size, [done], [own_kv, second]
+    *priors, prior_doc, lane = prior_states(
+        place, stages + 1, quarters, came, before, size, [done], [second]
     )
     priors = [priors[0]] + [send(priors[j], [(b, b ^ j) for b in everyone]) for j in others]
-    done = more_attention(cross_kv, False, [prior_doc])
-    far = None
-    if window % 2:
-        pairs = {b: b for b in everyone}
-        for b in range(1, blocks - window, 2):
-            pairs[b], pairs[b + window] = b + window, b
-        far = send(own_copy, list(pairs.items()))
+    done = more_attention([(first_cross, (2, 3)), (lane, (4, 4))], False, [prior_doc])
     rest = [(send(lane, swap), (4, 5))]
     for back in range(3, window // 2 + 1):
         lane = send(lane, forward)
         rest.append((lane, (2 * back, 2 * back)))
         rest.append((send(lane, swap), (2 * back, 2 * back + 1)))
-    slot = (beside if far is None else far, (blocks if far is None else window, 1))
     mixed, squares = mix(place, docs, prior_doc, cumul, inner, qh, priors, tokens, heads, [done])
     sums = [squares]
     for other in range(1, tensor):
         sums.append(lax.ppermute(squares, "tp", [(t, t ^ other) for t in range(tensor)]))
-    rest, done = [slot] + rest, squares
+    done = squares
     while rest:
-        got = more_attention(rest[:2], len(rest) <= 2, [done], beside if rest[0] is slot else None)
+        got = more_attention(rest[:2], len(rest) <= 2, [done])
         rest, done = rest[2:], got
     soft_out, done = got
     lin_out = finish(norm_gain, flat(lin_gate), mixed, sums, tokens, heads, [done])

time: 70.1 us -> 59.6 us (0.85)
  waiting for transfers between devices: 14.8 us -> 2.96 us
  starting transfers between devices: 22.9 us -> 28.2 us
  Pallas kernels: 30.2 us -> 27.2 us
  local copies, waits for them, and re-layouts: 0.98 us -> 0.02 us
    ppermute x13 -> x12, waiting for transfers between devices: 14.8 us -> 2.95 us  [send(): return lax.ppermute(x, 'seq', [(a, b % blocks) for a, b in pairs])]
    ppermute x13 -> x12, starting transfers between devices: 21 us -> 26.3 us  [send(): return lax.ppermute(x, 'seq', [(a, b % blocks) for a, b in pairs])]
    pallas_call x12, Pallas kernels: 30.2 us -> 27.2 us  [call(): pl.pallas_call(run, out_shape=outs, in_specs=[SMEM] * len(scalars) + [HBM...]
    unnamed x10 -> x8, local copies, waits for them, and re-layouts: 0.98 us -> 0.02 us
  transfers between devices with their start and end apart: 16 -> 15, of which waited for: 3 -> 2; matrix products, arithmetic and copies ran while one was open for 0% -> 0% of each run, Pallas kernels for 37% -> 38%
where the time goes in v10:
time: 59.6 us; the launch traced here: 59.4 us
  starting transfers between devices  28.2 us (47%)
  Pallas kernels  27.2 us (46%)
  waiting for transfers between devices  2.96 us (5%)
  between operations  1.03 us (2%)
    pallas_call x12, Pallas kernels, call(): pl.pallas_call(run, out_shape=outs, in_specs=[SMEM] * len(scalars) + [HBM...  27.2 us
    ppermute x12, starting transfers between devices, send(): return lax.ppermute(x, 'seq', [(a, b % blocks) for a, b in pairs])  26.3 us
    ppermute x12, waiting for transfers between devices, send(): return lax.ppermute(x, 'seq', [(a, b % blocks) for a, b in pairs])  2.95 us
    ppermute x3, starting transfers between devices, body(): lax.ppermute(squares, 'tp', [(t, t ^ other) for t in range(tensor)])  1.88 us
  transfers between devices with their start and end apart: 15, of which 2 were waited for; matrix products, arithmetic and copies ran while one was open for 0% of the time, Pallas kernels for 38%

profile of v10, /device:TPU:0, one launch (start us, length us, event | category | flops | bytes accessed | tf_op | source)
XLA Modules:
  0.0 59.4 jit_solution(494898883743990730)
XLA Ops:
  0.6 0.0 copy-start.3
  0.7 2.7 %fetch.1 = (bf16[1040,128]{1,0:T(8,128)(2,1)}, f32[16,128]{1,0:T(8,128)S(1)}, f32[256,128]{1,0:T(8,128)S(1)}, bf16[4096,128]{1,0:T(8,128)(2,1)S(1)}, bf16[4096,128]{1,0:T(8,128)(2,1)S(1)}) custom-call(s32[1]{0:T(128)} %bitcast.2.refs_0_, s32[2,128]{1,0:T(2,128)} %bitcast.23, f32[16,256]{1,0:T(8,128)} %bitcast.22, bf16[2048,128]{1,0:T(8,128)(2,1)} %bitcast.20, ...), custom_call_target="tpu_custom_call" | custom-call | bytes 3145728 | tf_op jit(solution)/shard_map/fetch/pallas_call | solution.py:68
  3.4 3.1 %collective-permute-start.4 = (bf16[1040,128]{1,0:T(8,128)(2,1)}, bf16[1040,128]{1,0:T(8,128)(2,1)}, u32[]{:S(2)}, u32[]{:S(2)}) collective-permute-start(bf16[1040,128]{1,0:T(8,128)(2,1)} %get-tuple-element.38.refs_3_), channel_id=1, source_target_pairs={{0,8},{4,12},{8,16},{12,20},{16,24},{20,28},{24,0},{28,4},{1,9},{5... | collective-permute-start | bytes 798728 | tf_op jit(solution)/shard_map/ppermute | solution.py:709
  6.5 3.4 %collective-permute-start.3 = (bf16[1040,128]{1,0:T(8,128)(2,1)}, bf16[1040,128]{1,0:T(8,128)(2,1)S(1)}, u32[]{:S(2)}, u32[]{:S(2)}) collective-permute-start(bf16[1040,128]{1,0:T(8,128)(2,1)} %get-tuple-element.38.refs_3_), channel_id=1, source_target_pairs={{0,4},{8,12},{16,20},{24,28},{4,24},{12,8},{20,16},{1,5},{9,13},{1... | collective-permute-start | bytes 798728 | tf_op jit(solution)/shard_map/ppermute | solution.py:709
  9.9 2.7 %block_state.1 = (bf16[528,128]{1,0:T(8,128)(2,1)S(1)}, bf16[528,128]{1,0:T(8,128)(2,1)S(1)}, bf16[528,128]{1,0:T(8,128)(2,1)S(1)}, bf16[528,128]{1,0:T(8,128)(2,1)S(1)}) custom-call(s32[1]{0:T(128)} %bitcast.1.refs_0_, f32[256,128]{1,0:T(8,128)S(1)} %get-tuple-element.31.refs_1_.refs_0_.refs_3_, f32[16,128]{1,0:T(8,128)S(1)} %get-tuple-element.30.refs_2_.refs_1_, ...), custom_call_target="tpu_custom_call" | custom-call | flops 134217728 | bytes 5242880 | tf_op jit(solution)/shard_map/block_state/pallas_call | solution.py:68
  12.6 0.0 copy-start
  12.7 2.0 %collective-permute-start = (bf16[528,128]{1,0:T(8,128)(2,1)S(1)}, bf16[528,128]{1,0:T(8,128)(2,1)S(1)}, u32[]{:S(2)}, u32[]{:S(2)}) collective-permute-start(bf16[528,128]{1,0:T(8,128)(2,1)S(1)} %get-tuple-element.35), channel_id=1, source_target_pairs={{0,4},{4,0},{8,12},{12,8},{16,20},{20,16},{24,28},{28,24},{1,5},{5... | collective-permute-start | bytes 405512 | tf_op jit(solution)/shard_map/ppermute | solution.py:709
  14.7 0.1 collective-permute-start.1
  14.8 1.5 %collective-permute-start.2 = (bf16[528,128]{1,0:T(8,128)(2,1)S(1)}, bf16[528,128]{1,0:T(8,128)(2,1)S(1)}, u32[]{:S(2)}, u32[]{:S(2)}) collective-permute-start(bf16[528,128]{1,0:T(8,128)(2,1)S(1)} %get-tuple-element.37), channel_id=1, source_target_pairs={{0,12},{4,8},{8,4},{12,0},{16,28},{20,24},{24,20},{28,16},{1,13},{... | collective-permute-start | bytes 405512 | tf_op jit(solution)/shard_map/ppermute | solution.py:709
  16.2 0.0 collective-permute-done.4.refs_6_
  16.3 0.3 collective-permute-done.3.refs_5_.refs_3_
  16.6 0.0 copy-done.3
  16.6 3.7 %attend.4 = (bf16[2,2048,256]{2,1,0:T(8,128)(2,1)S(1)}, f32[2,144,2048]{2,1,0:T(8,128)S(1)}, bf16[1040,128]{1,0:T(8,128)(2,1)S(1)}) custom-call(s32[1]{0:T(128)} %bitcast.1.refs_0_, f32[16,128]{1,0:T(8,128)S(1)} %get-tuple-element.30.refs_2_.refs_1_, bf16[4096,128]{1,0:T(8,128)(2,1)S(1)} %bitcast.16, bf16[1040,128]{1,0:T(8,128)(2,1)} %get-tuple-element.38.refs_3_, ...), custom_call_target="tpu_custom_call" | custom-call | flops 1073741824 | bytes 8388608 | tf_op jit(solution)/shard_map/attend/pallas_call | solution.py:68
  20.2 0.9 %collective-permute-start.6 = (bf16[1040,128]{1,0:T(8,128)(2,1)S(1)}, bf16[1040,128]{1,0:T(8,128)(2,1)S(1)}, u32[]{:S(2)}, u32[]{:S(2)}) collective-permute-start(bf16[1040,128]{1,0:T(8,128)(2,1)S(1)} %get-tuple-element.41.refs_6_), channel_id=1, source_target_pairs={{8,16},{12,20},{16,24},{20,28},{9,17},{13,21},{17,25},{21,29},{10,... | collective-permute-start | bytes 798728 | tf_op jit(solution)/shard_map/ppermute | solution.py:709
  21.1 0.0 copy-done
  21.1 1.9 %inner_part.2 = (f32[2048,128]{1,0:T(8,128)S(1)}, bf16[2048,128]{1,0:T(8,128)(2,1)S(1)}) custom-call(f32[256,128]{1,0:T(8,128)S(1)} %get-tuple-element.31.refs_1_.refs_0_.refs_3_, f32[16,128]{1,0:T(8,128)S(1)} %get-tuple-element.30.refs_2_.refs_1_, bf16[4096,128]{1,0:T(8,128)(2,1)S(1)} %bitcast.13, bf16[4096,128]{1,0:T(8,128)(2,1)S(1)} %get-tuple-element.32.refs_3_, ...), custom_call_target="tpu_custom_call" | custom-call | flops 268435456 | bytes 6291456 | tf_op jit(solution)/shard_map/inner_part/pallas_call | solution.py:68
  23.0 0.0 collective-permute-done.refs_2_
  23.0 0.0 collective-permute-done.1.refs_3_
  23.1 0.0 collective-permute-done.2.refs_4_
  23.1 0.2 group_map.1
  23.3 9.8 %collective-permute-start.5 = (bf16[528,128]{1,0:T(8,128)(2,1)S(1)}, bf16[528,128]{1,0:T(8,128)(2,1)S(1)}, u32[]{:S(2)}, u32[]{:S(2)}) collective-permute-start(bf16[528,128]{1,0:T(8,128)(2,1)S(1)} %get-tuple-element.42.refs_5_), channel_id=1, source_target_pairs={{0,16},{4,20},{8,24},{12,28},{16,0},{20,4},{24,8},{28,12},{1,17},{... | collective-permute-start | bytes 405512 | tf_op jit(solution)/shard_map/ppermute | solution.py:709
  33.1 0.0 collective-permute-start.10
  33.1 3.7 %attend.5.refs_5_.refs_2_ = f32[2,144,2048]{2,1,0:T(8,128)S(1)} custom-call(s32[1]{0:T(128)} %bitcast.1.refs_0_, bf16[2,2048,256]{2,1,0:T(8,128)(2,1)S(1)} %get-tuple-element.43.refs_1_, f32[2,144,2048]{2,1,0:T(8,128)S(1)} %get-tuple-element.39.refs_5_.refs_2_, bf16[1040,128]{1,0:T(8,128)(2,1)S(1)} %collective-permute-done.3.refs_5_.refs_3_, ...), custom_call_target="tpu_custom_call" | custom-call | flops 2147483648 | bytes 8388608 | tf_op jit(solution)/shard_map/attend/pallas_call | solution.py:68
  36.7 1.9 %inner_part.3 = (f32[2048,128]{1,0:T(8,128)S(1)}, bf16[2048,128]{1,0:T(8,128)(2,1)S(1)}) custom-call(f32[256,128]{1,0:T(8,128)S(1)} %get-tuple-element.31.refs_1_.refs_0_.refs_3_, f32[16,128]{1,0:T(8,128)S(1)} %get-tuple-element.30.refs_2_.refs_1_, bf16[4096,128]{1,0:T(8,128)(2,1)S(1)} %bitcast.14, bf16[4096,128]{1,0:T(8,128)(2,1)S(1)} %get-tuple-element.32.refs_3_, ...), custom_call_target="tpu_custom_call" | custom-call | flops 268435456 | bytes 6291456 | tf_op jit(solution)/shard_map/inner_part/pallas_call | solution.py:68
  38.6 0.0 collective-permute-done.5.refs_5_
  38.7 0.0 collective-permute-done.6.refs_7_
  38.7 0.3 prior_states.1
  38.9 2.1 %collective-permute-start.14 = (bf16[1040,128]{1,0:T(8,128)(2,1)S(1)}, bf16[1040,128]{1,0:T(8,128)(2,1)S(1)}, u32[]{:S(2)}, u32[]{:S(2)}) collective-permute-start(bf16[1040,128]{1,0:T(8,128)(2,1)S(1)} %get-tuple-element.53.refs_4_), channel_id=1, source_target_pairs={{0,4},{4,0},{8,12},{12,8},{16,20},{20,16},{24,28},{28,24},{1,5},{5... | collective-permute-start | bytes 798728 | tf_op jit(solution)/shard_map/ppermute | solution.py:709
  41.0 0.1 collective-permute-start.7
  41.1 0.4 collective-permute-start.8
  41.5 3.0 %collective-permute-start.9 = (bf16[512,128]{1,0:T(8,128)(2,1)S(1)}, bf16[512,128]{1,0:T(8,128)(2,1)S(1)}, u32[]{:S(2)}, u32[]{:S(2)}) collective-permute-start(bf16[512,128]{1,0:T(8,128)(2,1)S(1)} %get-tuple-element.52), channel_id=1, source_target_pairs={{0,12},{4,8},{8,4},{12,0},{16,28},{20,24},{24,20},{28,16},{1,13},{... | collective-permute-start | bytes 393224 | tf_op jit(solution)/shard_map/ppermute | solution.py:709
  44.5 0.0 collective-permute-done.10.refs_3_
  44.5 3.7 %attend.6.refs_12_.refs_2_ = f32[2,144,2048]{2,1,0:T(8,128)S(1)} custom-call(s32[1]{0:T(128)} %bitcast.1.refs_0_, bf16[2,2048,256]{2,1,0:T(8,128)(2,1)S(1)} %get-tuple-element.43.refs_1_, f32[2,144,2048]{2,1,0:T(8,128)S(1)} %attend.5.refs_5_.refs_2_, bf16[1040,128]{1,0:T(8,128)(2,1)S(1)} %collective-permute-done.10.refs_3_, ...), custom_call_target="tpu_custom_call" | custom-call | flops 2147483648 | bytes 8388608 | tf_op jit(solution)/shard_map/attend/pallas_call | solution.py:68
  48.2 2.6 %collective-permute-done.7.refs_9_ = bf16[512,128]{1,0:T(8,128)(2,1)S(1)} collective-permute-done((bf16[512,128]{1,0:T(8,128)(2,1)S(1)}, bf16[512,128]{1,0:T(8,128)(2,1)S(1)}, u32[]{:S(2)}, u32[]{:S(2)}) %collective-permute-start.7) | collective-permute-done | bytes 131104 | tf_op jit(solution)/shard_map/ppermute | solution.py:709
  50.8 0.0 collective-permute-done.8.refs_10_
  50.8 0.0 collective-permute-done.9.refs_11_
  50.8 1.6 %mix.1 = (f32[4096,128]{1,0:T(8,128)S(1)}, f32[8,256]{1,0:T(8,128)S(1)}) custom-call(s32[1]{0:T(128)} %bitcast.1.refs_0_, f32[16,128]{1,0:T(8,128)S(1)} %get-tuple-element.30.refs_2_.refs_1_, f32[8,128]{1,0:T(8,128)S(1)} %get-tuple-element.46.refs_5_.refs_2_, f32[256,128]{1,0:T(8,128)S(1)} %get-tuple-element.31.refs_1_.refs_0_.refs_3_, ...), custom_call_target="tpu_custom_call" | custom-call | flops 134217728 | bytes 5242880 | tf_op jit(solution)/shard_map/mix/pallas_call | solution.py:68
  52.4 0.0 collective-permute-start.13
  52.4 1.6 %collective-permute-start.12 = (f32[8,256]{1,0:T(8,128)S(1)}, f32[8,256]{1,0:T(8,128)S(1)}, u32[]{:S(2)}, u32[]{:S(2)}) collective-permute-start(f32[8,256]{1,0:T(8,128)S(1)} %get-tuple-element.55.refs_4_.refs_3_), channel_id=1, source_target_pairs={{0,2},{1,3},{2,0},{3,1},{4,6},{5,7},{6,4},{7,5},{8,10},{9,11},{10,... | collective-permute-start | bytes 24584 | tf_op jit(solution)/shard_map/ppermute | solution.py:799
  54.0 0.3 collective-permute-start.11
  54.3 0.0 collective-permute-done.14.refs_3_
  54.3 3.3 %attend.7 = (bf16[4096,128]{1,0:T(8,128)(2,1)}, f32[8,128]{1,0:T(8,128)S(1)}) custom-call(s32[1]{0:T(128)} %bitcast.1.refs_0_, bf16[2,2048,256]{2,1,0:T(8,128)(2,1)S(1)} %get-tuple-element.43.refs_1_, f32[2,144,2048]{2,1,0:T(8,128)S(1)} %attend.6.refs_12_.refs_2_, bf16[1040,128]{1,0:T(8,128)(2,1)S(1)} %collective-permute-done.14.refs_3_, ...), custom_call_target="tpu_custom_call" | custom-call | flops 1073741824 | bytes 8388608 | tf_op jit(solution)/shard_map/attend/pallas_call | solution.py:68
  57.6 0.0 collective-permute-done.13.refs_6_
  57.6 0.0 collective-permute-done.12.refs_5_
  57.6 0.0 collective-permute-done.11.refs_4_
  57.6 0.0 copy-done.1
  57.6 0.0 copy-done.2
  57.6 1.6 %finish.1 = bf16[4096,128]{1,0:T(8,128)(2,1)} custom-call(f32[16,128]{1,0:T(8,128)S(1)} %copy-done.2, bf16[4096,128]{1,0:T(8,128)(2,1)S(1)} %bitcast.15, f32[4096,128]{1,0:T(8,128)S(1)} %get-tuple-element.54.refs_2_, f32[8,256]{1,0:T(8,128)S(1)} %get-tuple-element.55.refs_4_.refs_3_, f32[8,256]{1,0:T(8,128)S(1)} %collective-permute-done.11.refs_4_, ...), custom_call_target="tpu_custom_call" | custom-call | bytes 4194304 | tf_op jit(solution)/shard_map/finish/pallas_call | solution.py:68
  (2 shorter events, 0.0 us)
Async XLA Ops:
  0.6 15.9 %copy-start.3 = (bf16[256,16,128]{2,1,0:T(8,128)(2,1)S(1)}, bf16[256,16,128]{2,1,0:T(8,128)(2,1)}, u32[]{:S(2)}) copy-start(bf16[256,16,128]{2,1,0:T(8,128)(2,1)} %param.17) | copy-start | bytes 3145732
  3.4 12.9 %collective-permute-start.4 = (bf16[1040,128]{1,0:T(8,128)(2,1)}, bf16[1040,128]{1,0:T(8,128)(2,1)}, u32[]{:S(2)}, u32[]{:S(2)}) collective-permute-start(bf16[1040,128]{1,0:T(8,128)(2,1)} %get-tuple-element.38.refs_3_), channel_id=1, source_target_pairs={{0,8},{4,12},{8,16},{12,20},{16,24},{20,28},{24,0},{28,4},{1,9},{5... | collective-permute-start | bytes 798728 | tf_op jit(solution)/shard_map/ppermute | solution.py:709
  6.5 10.1 %collective-permute-start.3 = (bf16[1040,128]{1,0:T(8,128)(2,1)}, bf16[1040,128]{1,0:T(8,128)(2,1)S(1)}, u32[]{:S(2)}, u32[]{:S(2)}) collective-permute-start(bf16[1040,128]{1,0:T(8,128)(2,1)} %get-tuple-element.38.refs_3_), channel_id=1, source_target_pairs={{0,4},{8,12},{16,20},{24,28},{4,24},{12,8},{20,16},{1,5},{9,13},{1... | collective-permute-start | bytes 798728 | tf_op jit(solution)/shard_map/ppermute | solution.py:709
  12.6 8.5 %copy-start = (bf16[256,16,128]{2,1,0:T(8,128)(2,1)S(1)}, bf16[256,16,128]{2,1,0:T(8,128)(2,1)}, u32[]{:S(2)}) copy-start(bf16[256,16,128]{2,1,0:T(8,128)(2,1)} %param.10) | copy-start | bytes 3145732
  12.7 10.4 %collective-permute-start = (bf16[528,128]{1,0:T(8,128)(2,1)S(1)}, bf16[528,128]{1,0:T(8,128)(2,1)S(1)}, u32[]{:S(2)}, u32[]{:S(2)}) collective-permute-start(bf16[528,128]{1,0:T(8,128)(2,1)S(1)} %get-tuple-element.35), channel_id=1, source_target_pairs={{0,4},{4,0},{8,12},{12,8},{16,20},{20,16},{24,28},{28,24},{1,5},{5... | collective-permute-start | bytes 405512 | tf_op jit(solution)/shard_map/ppermute | solution.py:709
  14.7 8.3 %collective-permute-start.1 = (bf16[528,128]{1,0:T(8,128)(2,1)S(1)}, bf16[528,128]{1,0:T(8,128)(2,1)S(1)}, u32[]{:S(2)}, u32[]{:S(2)}) collective-permute-start(bf16[528,128]{1,0:T(8,128)(2,1)S(1)} %get-tuple-element.36), channel_id=1, source_target_pairs={{0,8},{4,12},{8,0},{12,4},{16,24},{20,28},{24,16},{28,20},{1,9},{5... | collective-permute-start | bytes 405512 | tf_op jit(solution)/shard_map/ppermute | solution.py:709
  14.8 8.3 %collective-permute-start.2 = (bf16[528,128]{1,0:T(8,128)(2,1)S(1)}, bf16[528,128]{1,0:T(8,128)(2,1)S(1)}, u32[]{:S(2)}, u32[]{:S(2)}) collective-permute-start(bf16[528,128]{1,0:T(8,128)(2,1)S(1)} %get-tuple-element.37), channel_id=1, source_target_pairs={{0,12},{4,8},{8,4},{12,0},{16,28},{20,24},{24,20},{28,16},{1,13},{... | collective-permute-start | bytes 405512 | tf_op jit(solution)/shard_map/ppermute | solution.py:709
  20.2 18.4 %collective-permute-start.6 = (bf16[1040,128]{1,0:T(8,128)(2,1)S(1)}, bf16[1040,128]{1,0:T(8,128)(2,1)S(1)}, u32[]{:S(2)}, u32[]{:S(2)}) collective-permute-start(bf16[1040,128]{1,0:T(8,128)(2,1)S(1)} %get-tuple-element.41.refs_6_), channel_id=1, source_target_pairs={{8,16},{12,20},{16,24},{20,28},{9,17},{13,21},{17,25},{21,29},{10,... | collective-permute-start | bytes 798728 | tf_op jit(solution)/shard_map/ppermute | solution.py:709
  23.3 15.3 %collective-permute-start.5 = (bf16[528,128]{1,0:T(8,128)(2,1)S(1)}, bf16[528,128]{1,0:T(8,128)(2,1)S(1)}, u32[]{:S(2)}, u32[]{:S(2)}) collective-permute-start(bf16[528,128]{1,0:T(8,128)(2,1)S(1)} %get-tuple-element.42.refs_5_), channel_id=1, source_target_pairs={{0,16},{4,20},{8,24},{12,28},{16,0},{20,4},{24,8},{28,12},{1,17},{... | collective-permute-start | bytes 405512 | tf_op jit(solution)/shard_map/ppermute | solution.py:709
  33.1 11.5 %collective-permute-start.10 = (bf16[1040,128]{1,0:T(8,128)(2,1)S(1)}, bf16[1040,128]{1,0:T(8,128)(2,1)S(1)}, u32[]{:S(2)}, u32[]{:S(2)}) collective-permute-start(bf16[1040,128]{1,0:T(8,128)(2,1)S(1)} %get-tuple-element.44.refs_4_), channel_id=1, source_target_pairs={{0,4},{4,0},{8,12},{12,8},{16,20},{20,16},{24,28},{28,24},{1,5},{5... | collective-permute-start | bytes 798728 | tf_op jit(solution)/shard_map/ppermute | solution.py:709
  38.9 15.4 %collective-permute-start.14 = (bf16[1040,128]{1,0:T(8,128)(2,1)S(1)}, bf16[1040,128]{1,0:T(8,128)(2,1)S(1)}, u32[]{:S(2)}, u32[]{:S(2)}) collective-permute-start(bf16[1040,128]{1,0:T(8,128)(2,1)S(1)} %get-tuple-element.53.refs_4_), channel_id=1, source_target_pairs={{0,4},{4,0},{8,12},{12,8},{16,20},{20,16},{24,28},{28,24},{1,5},{5... | collective-permute-start | bytes 798728 | tf_op jit(solution)/shard_map/ppermute | solution.py:709
  41.0 9.8 %collective-permute-start.7 = (bf16[512,128]{1,0:T(8,128)(2,1)S(1)}, bf16[512,128]{1,0:T(8,128)(2,1)S(1)}, u32[]{:S(2)}, u32[]{:S(2)}) collective-permute-start(bf16[512,128]{1,0:T(8,128)(2,1)S(1)} %get-tuple-element.50), channel_id=1, source_target_pairs={{0,4},{4,0},{8,12},{12,8},{16,20},{20,16},{24,28},{28,24},{1,5},{5... | collective-permute-start | bytes 393224 | tf_op jit(solution)/shard_map/ppermute | solution.py:709
  41.1 9.7 %collective-permute-start.8 = (bf16[512,128]{1,0:T(8,128)(2,1)S(1)}, bf16[512,128]{1,0:T(8,128)(2,1)S(1)}, u32[]{:S(2)}, u32[]{:S(2)}) collective-permute-start(bf16[512,128]{1,0:T(8,128)(2,1)S(1)} %get-tuple-element.51), channel_id=1, source_target_pairs={{0,8},{4,12},{8,0},{12,4},{16,24},{20,28},{24,16},{28,20},{1,9},{5... | collective-permute-start | bytes 393224 | tf_op jit(solution)/shard_map/ppermute | solution.py:709
  41.5 9.3 %collective-permute-start.9 = (bf16[512,128]{1,0:T(8,128)(2,1)S(1)}, bf16[512,128]{1,0:T(8,128)(2,1)S(1)}, u32[]{:S(2)}, u32[]{:S(2)}) collective-permute-start(bf16[512,128]{1,0:T(8,128)(2,1)S(1)} %get-tuple-element.52), channel_id=1, source_target_pairs={{0,12},{4,8},{8,4},{12,0},{16,28},{20,24},{24,20},{28,16},{1,13},{... | collective-permute-start | bytes 393224 | tf_op jit(solution)/shard_map/ppermute | solution.py:709
  52.4 5.2 %copy-start.1 = (bf16[256,16,128]{2,1,0:T(8,128)(2,1)S(1)}, bf16[256,16,128]{2,1,0:T(8,128)(2,1)}, u32[]{:S(2)}) copy-start(bf16[256,16,128]{2,1,0:T(8,128)(2,1)} %param.13) | copy-start | bytes 3145732
  52.4 5.2 %copy-start.2 = (f32[16,128]{1,0:T(8,128)S(1)}, f32[16,128]{1,0:T(8,128)}, u32[]{:S(2)}) copy-start(f32[16,128]{1,0:T(8,128)} %refs_0_.1) | copy-start | bytes 24580
  52.4 5.2 %collective-permute-start.13 = (f32[8,256]{1,0:T(8,128)S(1)}, f32[8,256]{1,0:T(8,128)S(1)}, u32[]{:S(2)}, u32[]{:S(2)}) collective-permute-start(f32[8,256]{1,0:T(8,128)S(1)} %get-tuple-element.55.refs_4_.refs_3_), channel_id=1, source_target_pairs={{0,3},{1,2},{2,1},{3,0},{4,7},{5,6},{6,5},{7,4},{8,11},{9,10},{10,... | collective-permute-start | bytes 24584 | tf_op jit(solution)/shard_map/ppermute | solution.py:799
  52.4 5.1 %collective-permute-start.12 = (f32[8,256]{1,0:T(8,128)S(1)}, f32[8,256]{1,0:T(8,128)S(1)}, u32[]{:S(2)}, u32[]{:S(2)}) collective-permute-start(f32[8,256]{1,0:T(8,128)S(1)} %get-tuple-element.55.refs_4_.refs_3_), channel_id=1, source_target_pairs={{0,2},{1,3},{2,0},{3,1},{4,6},{5,7},{6,4},{7,5},{8,10},{9,11},{10,... | collective-permute-start | bytes 24584 | tf_op jit(solution)/shard_map/ppermute | solution.py:799
  54.0 3.6 %collective-permute-start.11 = (f32[8,256]{1,0:T(8,128)S(1)}, f32[8,256]{1,0:T(8,128)S(1)}, u32[]{:S(2)}, u32[]{:S(2)}) collective-permute-start(f32[8,256]{1,0:T(8,128)S(1)} %get-tuple-element.55.refs_4_.refs_3_), channel_id=1, source_target_pairs={{0,1},{1,0},{2,3},{3,2},{4,5},{5,4},{6,7},{7,6},{8,9},{9,8},{10,11... | collective-permute-start | bytes 24584 | tf_op jit(solution)/shard_map/ppermute | solution.py:799

commit v11 on v10

--- a/solution.py
+++ b/solution.py
@@ -35,7 +35,7 @@
 
 def cost(flops, bytes_accessed, transcendentals=0):
     return pl.CostEstimate(
-        flops=int(flops) , bytes_accessed=int(bytes_accessed) , transcendentals=int(transcendentals)
+        flops=int(flops), bytes_accessed=int(bytes_accessed), transcendentals=int(transcendentals)
     )
 
 
@@ -767,11 +767,11 @@
         qh.append(got[1])
         return got[0]
 
-    done, lane = first_attention([sent[0], beside[0]], [ahead])
+    done, lane = first_attention([sent[0]], [ahead])
     second = send(lane, [(b, b + 2) for b in range(2, blocks - 2)])
     if parts > 1:
         done = inner_of(0, [done])
-    run, lane = group_map(place, quarters, size, [done], [lane])
+    run, lane = group_map(place, quarters, size, [done, beside[0]], [lane])
     first_cross = send(lane, swap)
     stages = (blocks // GROUP_BLOCKS).bit_length() - 1
     before, done = None, run

time: 59.6 us -> 57.2 us (0.960)
  starting transfers between devices: 28.2 us -> 26.2 us
    ppermute x12, starting transfers between devices: 26.3 us -> 24.3 us  [send(): return lax.ppermute(x, 'seq', [(a, b % blocks) for a, b in pairs])]
  transfers between devices with their start and end apart: 15 -> 15, of which waited for: 2 -> 1; matrix products, arithmetic and copies ran while one was open for 0% -> 0% of each run, Pallas kernels for 38% -> 40%
where the time goes in v11:
time: 57.2 us; the launch traced here: 57.1 us
  Pallas kernels  27.2 us (48%)
  starting transfers between devices  26.2 us (46%)
  waiting for transfers between devices  2.64 us (5%)
  between operations  1.04 us (2%)
    pallas_call x12, Pallas kernels, call(): pl.pallas_call(run, out_shape=outs, in_specs=[SMEM] * len(scalars) + [HBM...  27.2 us
    ppermute x12, starting transfers between devices, send(): return lax.ppermute(x, 'seq', [(a, b % blocks) for a, b in pairs])  24.3 us
    ppermute x12, waiting for transfers between devices, send(): return lax.ppermute(x, 'seq', [(a, b % blocks) for a, b in pairs])  2.63 us
    ppermute x3, starting transfers between devices, body(): lax.ppermute(squares, 'tp', [(t, t ^ other) for t in range(tensor)])  1.88 us
  transfers between devices with their start and end apart: 15, of which 1 were waited for; matrix products, arithmetic and copies ran while one was open for 0% of the time, Pallas kernels for 40%

profile of v11, /device:TPU:0, one launch (start us, length us, event | category | flops | bytes accessed | tf_op | source)
XLA Modules:
  0.0 57.1 jit_solution(4765016741450552679)
XLA Ops:
  0.6 0.0 copy-start.3
  0.7 2.7 %fetch.1 = (bf16[1040,128]{1,0:T(8,128)(2,1)}, f32[16,128]{1,0:T(8,128)S(1)}, f32[256,128]{1,0:T(8,128)S(1)}, bf16[4096,128]{1,0:T(8,128)(2,1)S(1)}, bf16[4096,128]{1,0:T(8,128)(2,1)S(1)}) custom-call(s32[1]{0:T(128)} %bitcast.2.refs_0_, s32[2,128]{1,0:T(2,128)} %bitcast.23, f32[16,256]{1,0:T(8,128)} %bitcast.22, bf16[2048,128]{1,0:T(8,128)(2,1)} %bitcast.20, ...), custom_call_target="tpu_custom_call" | custom-call | bytes 3145728 | tf_op jit(solution)/shard_map/fetch/pallas_call | solution.py:68
  3.4 3.1 %collective-permute-start.3 = (bf16[1040,128]{1,0:T(8,128)(2,1)}, bf16[1040,128]{1,0:T(8,128)(2,1)}, u32[]{:S(2)}, u32[]{:S(2)}) collective-permute-start(bf16[1040,128]{1,0:T(8,128)(2,1)} %get-tuple-element.38.refs_3_), channel_id=1, source_target_pairs={{0,8},{4,12},{8,16},{12,20},{16,24},{20,28},{24,0},{28,4},{1,9},{5... | collective-permute-start | bytes 798728 | tf_op jit(solution)/shard_map/ppermute | solution.py:709
  6.5 3.4 %collective-permute-start.4 = (bf16[1040,128]{1,0:T(8,128)(2,1)}, bf16[1040,128]{1,0:T(8,128)(2,1)S(1)}, u32[]{:S(2)}, u32[]{:S(2)}) collective-permute-start(bf16[1040,128]{1,0:T(8,128)(2,1)} %get-tuple-element.38.refs_3_), channel_id=1, source_target_pairs={{0,4},{8,12},{16,20},{24,28},{4,24},{12,8},{20,16},{1,5},{9,13},{1... | collective-permute-start | bytes 798728 | tf_op jit(solution)/shard_map/ppermute | solution.py:709
  9.9 2.7 %block_state.1 = (bf16[528,128]{1,0:T(8,128)(2,1)S(1)}, bf16[528,128]{1,0:T(8,128)(2,1)S(1)}, bf16[528,128]{1,0:T(8,128)(2,1)S(1)}, bf16[528,128]{1,0:T(8,128)(2,1)S(1)}) custom-call(s32[1]{0:T(128)} %bitcast.1.refs_0_, f32[256,128]{1,0:T(8,128)S(1)} %get-tuple-element.31.refs_1_.refs_0_.refs_3_, f32[16,128]{1,0:T(8,128)S(1)} %get-tuple-element.30.refs_2_.refs_1_, ...), custom_call_target="tpu_custom_call" | custom-call | flops 134217728 | bytes 5242880 | tf_op jit(solution)/shard_map/block_state/pallas_call | solution.py:68
  12.6 0.0 copy-start
  12.7 2.0 %collective-permute-start = (bf16[528,128]{1,0:T(8,128)(2,1)S(1)}, bf16[528,128]{1,0:T(8,128)(2,1)S(1)}, u32[]{:S(2)}, u32[]{:S(2)}) collective-permute-start(bf16[528,128]{1,0:T(8,128)(2,1)S(1)} %get-tuple-element.35), channel_id=1, source_target_pairs={{0,4},{4,0},{8,12},{12,8},{16,20},{20,16},{24,28},{28,24},{1,5},{5... | collective-permute-start | bytes 405512 | tf_op jit(solution)/shard_map/ppermute | solution.py:709
  14.7 0.1 collective-permute-start.1
  14.8 1.5 %collective-permute-start.2 = (bf16[528,128]{1,0:T(8,128)(2,1)S(1)}, bf16[528,128]{1,0:T(8,128)(2,1)S(1)}, u32[]{:S(2)}, u32[]{:S(2)}) collective-permute-start(bf16[528,128]{1,0:T(8,128)(2,1)S(1)} %get-tuple-element.37), channel_id=1, source_target_pairs={{0,12},{4,8},{8,4},{12,0},{16,28},{20,24},{24,20},{28,16},{1,13},{... | collective-permute-start | bytes 405512 | tf_op jit(solution)/shard_map/ppermute | solution.py:709
  16.2 0.0 collective-permute-done.3.refs_5_
  16.3 0.0 copy-done.3
  16.3 3.7 %attend.4 = (bf16[2,2048,256]{2,1,0:T(8,128)(2,1)S(1)}, f32[2,144,2048]{2,1,0:T(8,128)S(1)}, bf16[1040,128]{1,0:T(8,128)(2,1)S(1)}) custom-call(s32[1]{0:T(128)} %bitcast.1.refs_0_, f32[16,128]{1,0:T(8,128)S(1)} %get-tuple-element.30.refs_2_.refs_1_, bf16[4096,128]{1,0:T(8,128)(2,1)S(1)} %bitcast.16, bf16[1040,128]{1,0:T(8,128)(2,1)} %get-tuple-element.38.refs_3_, ...), custom_call_target="tpu_custom_call" | custom-call | flops 1073741824 | bytes 8388608 | tf_op jit(solution)/shard_map/attend/pallas_call | solution.py:68
  19.9 0.9 %collective-permute-start.6 = (bf16[1040,128]{1,0:T(8,128)(2,1)S(1)}, bf16[1040,128]{1,0:T(8,128)(2,1)S(1)}, u32[]{:S(2)}, u32[]{:S(2)}) collective-permute-start(bf16[1040,128]{1,0:T(8,128)(2,1)S(1)} %get-tuple-element.41.refs_7_), channel_id=1, source_target_pairs={{8,16},{12,20},{16,24},{20,28},{9,17},{13,21},{17,25},{21,29},{10,... | collective-permute-start | bytes 798728 | tf_op jit(solution)/shard_map/ppermute | solution.py:709
  20.8 0.0 copy-done
  20.8 1.9 %inner_part.2 = (f32[2048,128]{1,0:T(8,128)S(1)}, bf16[2048,128]{1,0:T(8,128)(2,1)S(1)}) custom-call(f32[256,128]{1,0:T(8,128)S(1)} %get-tuple-element.31.refs_1_.refs_0_.refs_3_, f32[16,128]{1,0:T(8,128)S(1)} %get-tuple-element.30.refs_2_.refs_1_, bf16[4096,128]{1,0:T(8,128)(2,1)S(1)} %bitcast.13, bf16[4096,128]{1,0:T(8,128)(2,1)S(1)} %get-tuple-element.32.refs_3_, ...), custom_call_target="tpu_custom_call" | custom-call | flops 268435456 | bytes 6291456 | tf_op jit(solution)/shard_map/inner_part/pallas_call | solution.py:68
  22.7 0.0 collective-permute-done.refs_2_
  22.7 0.0 collective-permute-done.1.refs_3_
  22.7 0.0 collective-permute-done.2.refs_4_
  22.7 0.0 collective-permute-done.4.refs_6_.refs_3_
  22.8 0.2 group_map.1
  23.0 4.1 %collective-permute-start.5 = (bf16[528,128]{1,0:T(8,128)(2,1)S(1)}, bf16[528,128]{1,0:T(8,128)(2,1)S(1)}, u32[]{:S(2)}, u32[]{:S(2)}) collective-permute-start(bf16[528,128]{1,0:T(8,128)(2,1)S(1)} %get-tuple-element.42.refs_5_), channel_id=1, source_target_pairs={{0,16},{4,20},{8,24},{12,28},{16,0},{20,4},{24,8},{28,12},{1,17},{... | collective-permute-start | bytes 405512 | tf_op jit(solution)/shard_map/ppermute | solution.py:709
  27.0 5.7 %collective-permute-start.10 = (bf16[1040,128]{1,0:T(8,128)(2,1)S(1)}, bf16[1040,128]{1,0:T(8,128)(2,1)S(1)}, u32[]{:S(2)}, u32[]{:S(2)}) collective-permute-start(bf16[1040,128]{1,0:T(8,128)(2,1)S(1)} %get-tuple-element.44.refs_4_), channel_id=1, source_target_pairs={{0,4},{4,0},{8,12},{12,8},{16,20},{20,16},{24,28},{28,24},{1,5},{5... | collective-permute-start | bytes 798728 | tf_op jit(solution)/shard_map/ppermute | solution.py:709
  32.7 3.6 %attend.5.refs_5_.refs_2_ = f32[2,144,2048]{2,1,0:T(8,128)S(1)} custom-call(s32[1]{0:T(128)} %bitcast.1.refs_0_, bf16[2,2048,256]{2,1,0:T(8,128)(2,1)S(1)} %get-tuple-element.43.refs_1_, f32[2,144,2048]{2,1,0:T(8,128)S(1)} %get-tuple-element.39.refs_5_.refs_2_, bf16[1040,128]{1,0:T(8,128)(2,1)S(1)} %collective-permute-done.4.refs_6_.refs_3_, ...), custom_call_target="tpu_custom_call" | custom-call | flops 2147483648 | bytes 8388608 | tf_op jit(solution)/shard_map/attend/pallas_call | solution.py:68
  36.3 1.9 %inner_part.3 = (f32[2048,128]{1,0:T(8,128)S(1)}, bf16[2048,128]{1,0:T(8,128)(2,1)S(1)}) custom-call(f32[256,128]{1,0:T(8,128)S(1)} %get-tuple-element.31.refs_1_.refs_0_.refs_3_, f32[16,128]{1,0:T(8,128)S(1)} %get-tuple-element.30.refs_2_.refs_1_, bf16[4096,128]{1,0:T(8,128)(2,1)S(1)} %bitcast.14, bf16[4096,128]{1,0:T(8,128)(2,1)S(1)} %get-tuple-element.32.refs_3_, ...), custom_call_target="tpu_custom_call" | custom-call | flops 268435456 | bytes 6291456 | tf_op jit(solution)/shard_map/inner_part/pallas_call | solution.py:68
  38.3 0.0 collective-permute-done.5.refs_5_
  38.3 0.0 collective-permute-done.6.refs_7_
  38.3 0.3 prior_states.1
  38.5 0.1 collective-permute-start.14
  38.6 2.0 %collective-permute-start.7 = (bf16[512,128]{1,0:T(8,128)(2,1)S(1)}, bf16[512,128]{1,0:T(8,128)(2,1)S(1)}, u32[]{:S(2)}, u32[]{:S(2)}) collective-permute-start(bf16[512,128]{1,0:T(8,128)(2,1)S(1)} %get-tuple-element.50), channel_id=1, source_target_pairs={{0,4},{4,0},{8,12},{12,8},{16,20},{20,16},{24,28},{28,24},{1,5},{5... | collective-permute-start | bytes 393224 | tf_op jit(solution)/shard_map/ppermute | solution.py:709
  40.6 0.0 collective-permute-start.8
  40.6 1.5 %collective-permute-start.9 = (bf16[512,128]{1,0:T(8,128)(2,1)S(1)}, bf16[512,128]{1,0:T(8,128)(2,1)S(1)}, u32[]{:S(2)}, u32[]{:S(2)}) collective-permute-start(bf16[512,128]{1,0:T(8,128)(2,1)S(1)} %get-tuple-element.52), channel_id=1, source_target_pairs={{0,12},{4,8},{8,4},{12,0},{16,28},{20,24},{24,20},{28,16},{1,13},{... | collective-permute-start | bytes 393224 | tf_op jit(solution)/shard_map/ppermute | solution.py:709
  42.2 0.0 collective-permute-done.10.refs_3_
  42.2 3.7 %attend.6.refs_12_.refs_2_ = f32[2,144,2048]{2,1,0:T(8,128)S(1)} custom-call(s32[1]{0:T(128)} %bitcast.1.refs_0_, bf16[2,2048,256]{2,1,0:T(8,128)(2,1)S(1)} %get-tuple-element.43.refs_1_, f32[2,144,2048]{2,1,0:T(8,128)S(1)} %attend.5.refs_5_.refs_2_, bf16[1040,128]{1,0:T(8,128)(2,1)S(1)} %collective-permute-done.10.refs_3_, ...), custom_call_target="tpu_custom_call" | custom-call | flops 2147483648 | bytes 8388608 | tf_op jit(solution)/shard_map/attend/pallas_call | solution.py:68
  45.9 2.6 %collective-permute-done.7.refs_9_ = bf16[512,128]{1,0:T(8,128)(2,1)S(1)} collective-permute-done((bf16[512,128]{1,0:T(8,128)(2,1)S(1)}, bf16[512,128]{1,0:T(8,128)(2,1)S(1)}, u32[]{:S(2)}, u32[]{:S(2)}) %collective-permute-start.7) | collective-permute-done | bytes 131104 | tf_op jit(solution)/shard_map/ppermute | solution.py:709
  48.5 0.0 collective-permute-done.8.refs_10_
  48.5 0.0 collective-permute-done.9.refs_11_
  48.5 1.6 %mix.1 = (f32[4096,128]{1,0:T(8,128)S(1)}, f32[8,256]{1,0:T(8,128)S(1)}) custom-call(s32[1]{0:T(128)} %bitcast.1.refs_0_, f32[16,128]{1,0:T(8,128)S(1)} %get-tuple-element.30.refs_2_.refs_1_, f32[8,128]{1,0:T(8,128)S(1)} %get-tuple-element.46.refs_5_.refs_2_, f32[256,128]{1,0:T(8,128)S(1)} %get-tuple-element.31.refs_1_.refs_0_.refs_3_, ...), custom_call_target="tpu_custom_call" | custom-call | flops 134217728 | bytes 5242880 | tf_op jit(solution)/shard_map/mix/pallas_call | solution.py:68
  50.0 0.0 collective-permute-start.13
  50.1 1.6 %collective-permute-start.12 = (f32[8,256]{1,0:T(8,128)S(1)}, f32[8,256]{1,0:T(8,128)S(1)}, u32[]{:S(2)}, u32[]{:S(2)}) collective-permute-start(f32[8,256]{1,0:T(8,128)S(1)} %get-tuple-element.55.refs_4_.refs_3_), channel_id=1, source_target_pairs={{0,2},{1,3},{2,0},{3,1},{4,6},{5,7},{6,4},{7,5},{8,10},{9,11},{10,... | collective-permute-start | bytes 24584 | tf_op jit(solution)/shard_map/ppermute | solution.py:799
  51.6 0.3 collective-permute-start.11
  51.9 0.0 collective-permute-done.14.refs_3_
  51.9 3.3 %attend.7 = (bf16[4096,128]{1,0:T(8,128)(2,1)}, f32[8,128]{1,0:T(8,128)S(1)}) custom-call(s32[1]{0:T(128)} %bitcast.1.refs_0_, bf16[2,2048,256]{2,1,0:T(8,128)(2,1)S(1)} %get-tuple-element.43.refs_1_, f32[2,144,2048]{2,1,0:T(8,128)S(1)} %attend.6.refs_12_.refs_2_, bf16[1040,128]{1,0:T(8,128)(2,1)S(1)} %collective-permute-done.14.refs_3_, ...), custom_call_target="tpu_custom_call" | custom-call | flops 1073741824 | bytes 8388608 | tf_op jit(solution)/shard_map/attend/pallas_call | solution.py:68
  55.2 0.0 collective-permute-done.13.refs_6_
  55.2 0.0 collective-permute-done.12.refs_5_
  55.2 0.0 collective-permute-done.11.refs_4_
  55.2 0.0 copy-done.1
  55.2 0.0 copy-done.2
  55.3 1.6 %finish.1 = bf16[4096,128]{1,0:T(8,128)(2,1)} custom-call(f32[16,128]{1,0:T(8,128)S(1)} %copy-done.2, bf16[4096,128]{1,0:T(8,128)(2,1)S(1)} %bitcast.15, f32[4096,128]{1,0:T(8,128)S(1)} %get-tuple-element.54.refs_2_, f32[8,256]{1,0:T(8,128)S(1)} %get-tuple-element.55.refs_4_.refs_3_, f32[8,256]{1,0:T(8,128)S(1)} %collective-permute-done.11.refs_4_, ...), custom_call_target="tpu_custom_call" | custom-call | bytes 4194304 | tf_op jit(solution)/shard_map/finish/pallas_call | solution.py:68
  (2 shorter events, 0.0 us)
Async XLA Ops:
  0.6 15.6 %copy-start.3 = (bf16[256,16,128]{2,1,0:T(8,128)(2,1)S(1)}, bf16[256,16,128]{2,1,0:T(8,128)(2,1)}, u32[]{:S(2)}) copy-start(bf16[256,16,128]{2,1,0:T(8,128)(2,1)} %param.17) | copy-start | bytes 3145732
  3.4 12.9 %collective-permute-start.3 = (bf16[1040,128]{1,0:T(8,128)(2,1)}, bf16[1040,128]{1,0:T(8,128)(2,1)}, u32[]{:S(2)}, u32[]{:S(2)}) collective-permute-start(bf16[1040,128]{1,0:T(8,128)(2,1)} %get-tuple-element.38.refs_3_), channel_id=1, source_target_pairs={{0,8},{4,12},{8,16},{12,20},{16,24},{20,28},{24,0},{28,4},{1,9},{5... | collective-permute-start | bytes 798728 | tf_op jit(solution)/shard_map/ppermute | solution.py:709
  6.5 16.3 %collective-permute-start.4 = (bf16[1040,128]{1,0:T(8,128)(2,1)}, bf16[1040,128]{1,0:T(8,128)(2,1)S(1)}, u32[]{:S(2)}, u32[]{:S(2)}) collective-permute-start(bf16[1040,128]{1,0:T(8,128)(2,1)} %get-tuple-element.38.refs_3_), channel_id=1, source_target_pairs={{0,4},{8,12},{16,20},{24,28},{4,24},{12,8},{20,16},{1,5},{9,13},{1... | collective-permute-start | bytes 798728 | tf_op jit(solution)/shard_map/ppermute | solution.py:709
  12.6 8.1 %copy-start = (bf16[256,16,128]{2,1,0:T(8,128)(2,1)S(1)}, bf16[256,16,128]{2,1,0:T(8,128)(2,1)}, u32[]{:S(2)}) copy-start(bf16[256,16,128]{2,1,0:T(8,128)(2,1)} %param.10) | copy-start | bytes 3145732
  12.7 10.1 %collective-permute-start = (bf16[528,128]{1,0:T(8,128)(2,1)S(1)}, bf16[528,128]{1,0:T(8,128)(2,1)S(1)}, u32[]{:S(2)}, u32[]{:S(2)}) collective-permute-start(bf16[528,128]{1,0:T(8,128)(2,1)S(1)} %get-tuple-element.35), channel_id=1, source_target_pairs={{0,4},{4,0},{8,12},{12,8},{16,20},{20,16},{24,28},{28,24},{1,5},{5... | collective-permute-start | bytes 405512 | tf_op jit(solution)/shard_map/ppermute | solution.py:709
  14.7 8.0 %collective-permute-start.1 = (bf16[528,128]{1,0:T(8,128)(2,1)S(1)}, bf16[528,128]{1,0:T(8,128)(2,1)S(1)}, u32[]{:S(2)}, u32[]{:S(2)}) collective-permute-start(bf16[528,128]{1,0:T(8,128)(2,1)S(1)} %get-tuple-element.36), channel_id=1, source_target_pairs={{0,8},{4,12},{8,0},{12,4},{16,24},{20,28},{24,16},{28,20},{1,9},{5... | collective-permute-start | bytes 405512 | tf_op jit(solution)/shard_map/ppermute | solution.py:709
  14.8 7.9 %collective-permute-start.2 = (bf16[528,128]{1,0:T(8,128)(2,1)S(1)}, bf16[528,128]{1,0:T(8,128)(2,1)S(1)}, u32[]{:S(2)}, u32[]{:S(2)}) collective-permute-start(bf16[528,128]{1,0:T(8,128)(2,1)S(1)} %get-tuple-element.37), channel_id=1, source_target_pairs={{0,12},{4,8},{8,4},{12,0},{16,28},{20,24},{24,20},{28,16},{1,13},{... | collective-permute-start | bytes 405512 | tf_op jit(solution)/shard_map/ppermute | solution.py:709
  19.9 18.3 %collective-permute-start.6 = (bf16[1040,128]{1,0:T(8,128)(2,1)S(1)}, bf16[1040,128]{1,0:T(8,128)(2,1)S(1)}, u32[]{:S(2)}, u32[]{:S(2)}) collective-permute-start(bf16[1040,128]{1,0:T(8,128)(2,1)S(1)} %get-tuple-element.41.refs_7_), channel_id=1, source_target_pairs={{8,16},{12,20},{16,24},{20,28},{9,17},{13,21},{17,25},{21,29},{10,... | collective-permute-start | bytes 798728 | tf_op jit(solution)/shard_map/ppermute | solution.py:709
  23.0 15.3 %collective-permute-start.5 = (bf16[528,128]{1,0:T(8,128)(2,1)S(1)}, bf16[528,128]{1,0:T(8,128)(2,1)S(1)}, u32[]{:S(2)}, u32[]{:S(2)}) collective-permute-start(bf16[528,128]{1,0:T(8,128)(2,1)S(1)} %get-tuple-element.42.refs_5_), channel_id=1, source_target_pairs={{0,16},{4,20},{8,24},{12,28},{16,0},{20,4},{24,8},{28,12},{1,17},{... | collective-permute-start | bytes 405512 | tf_op jit(solution)/shard_map/ppermute | solution.py:709
  27.0 15.1 %collective-permute-start.10 = (bf16[1040,128]{1,0:T(8,128)(2,1)S(1)}, bf16[1040,128]{1,0:T(8,128)(2,1)S(1)}, u32[]{:S(2)}, u32[]{:S(2)}) collective-permute-start(bf16[1040,128]{1,0:T(8,128)(2,1)S(1)} %get-tuple-element.44.refs_4_), channel_id=1, source_target_pairs={{0,4},{4,0},{8,12},{12,8},{16,20},{20,16},{24,28},{28,24},{1,5},{5... | collective-permute-start | bytes 798728 | tf_op jit(solution)/shard_map/ppermute | solution.py:709
  38.5 13.4 %collective-permute-start.14 = (bf16[1040,128]{1,0:T(8,128)(2,1)S(1)}, bf16[1040,128]{1,0:T(8,128)(2,1)S(1)}, u32[]{:S(2)}, u32[]{:S(2)}) collective-permute-start(bf16[1040,128]{1,0:T(8,128)(2,1)S(1)} %get-tuple-element.53.refs_4_), channel_id=1, source_target_pairs={{0,4},{4,0},{8,12},{12,8},{16,20},{20,16},{24,28},{28,24},{1,5},{5... | collective-permute-start | bytes 798728 | tf_op jit(solution)/shard_map/ppermute | solution.py:709
  38.6 9.8 %collective-permute-start.7 = (bf16[512,128]{1,0:T(8,128)(2,1)S(1)}, bf16[512,128]{1,0:T(8,128)(2,1)S(1)}, u32[]{:S(2)}, u32[]{:S(2)}) collective-permute-start(bf16[512,128]{1,0:T(8,128)(2,1)S(1)} %get-tuple-element.50), channel_id=1, source_target_pairs={{0,4},{4,0},{8,12},{12,8},{16,20},{20,16},{24,28},{28,24},{1,5},{5... | collective-permute-start | bytes 393224 | tf_op jit(solution)/shard_map/ppermute | solution.py:709
  40.6 7.8 %collective-permute-start.8 = (bf16[512,128]{1,0:T(8,128)(2,1)S(1)}, bf16[512,128]{1,0:T(8,128)(2,1)S(1)}, u32[]{:S(2)}, u32[]{:S(2)}) collective-permute-start(bf16[512,128]{1,0:T(8,128)(2,1)S(1)} %get-tuple-element.51), channel_id=1, source_target_pairs={{0,8},{4,12},{8,0},{12,4},{16,24},{20,28},{24,16},{28,20},{1,9},{5... | collective-permute-start | bytes 393224 | tf_op jit(solution)/shard_map/ppermute | solution.py:709
  40.6 7.8 %collective-permute-start.9 = (bf16[512,128]{1,0:T(8,128)(2,1)S(1)}, bf16[512,128]{1,0:T(8,128)(2,1)S(1)}, u32[]{:S(2)}, u32[]{:S(2)}) collective-permute-start(bf16[512,128]{1,0:T(8,128)(2,1)S(1)} %get-tuple-element.52), channel_id=1, source_target_pairs={{0,12},{4,8},{8,4},{12,0},{16,28},{20,24},{24,20},{28,16},{1,13},{... | collective-permute-start | bytes 393224 | tf_op jit(solution)/shard_map/ppermute | solution.py:709
  50.0 5.2 %copy-start.1 = (bf16[256,16,128]{2,1,0:T(8,128)(2,1)S(1)}, bf16[256,16,128]{2,1,0:T(8,128)(2,1)}, u32[]{:S(2)}) copy-start(bf16[256,16,128]{2,1,0:T(8,128)(2,1)} %param.13) | copy-start | bytes 3145732
  50.0 5.2 %copy-start.2 = (f32[16,128]{1,0:T(8,128)S(1)}, f32[16,128]{1,0:T(8,128)}, u32[]{:S(2)}) copy-start(f32[16,128]{1,0:T(8,128)} %refs_0_.1) | copy-start | bytes 24580
  50.0 5.2 %collective-permute-start.13 = (f32[8,256]{1,0:T(8,128)S(1)}, f32[8,256]{1,0:T(8,128)S(1)}, u32[]{:S(2)}, u32[]{:S(2)}) collective-permute-start(f32[8,256]{1,0:T(8,128)S(1)} %get-tuple-element.55.refs_4_.refs_3_), channel_id=1, source_target_pairs={{0,3},{1,2},{2,1},{3,0},{4,7},{5,6},{6,5},{7,4},{8,11},{9,10},{10,... | collective-permute-start | bytes 24584 | tf_op jit(solution)/shard_map/ppermute | solution.py:799
  50.1 5.1 %collective-permute-start.12 = (f32[8,256]{1,0:T(8,128)S(1)}, f32[8,256]{1,0:T(8,128)S(1)}, u32[]{:S(2)}, u32[]{:S(2)}) collective-permute-start(f32[8,256]{1,0:T(8,128)S(1)} %get-tuple-element.55.refs_4_.refs_3_), channel_id=1, source_target_pairs={{0,2},{1,3},{2,0},{3,1},{4,6},{5,7},{6,4},{7,5},{8,10},{9,11},{10,... | collective-permute-start | bytes 24584 | tf_op jit(solution)/shard_map/ppermute | solution.py:799
  51.6 3.6 %collective-permute-start.11 = (f32[8,256]{1,0:T(8,128)S(1)}, f32[8,256]{1,0:T(8,128)S(1)}, u32[]{:S(2)}, u32[]{:S(2)}) collective-permute-start(f32[8,256]{1,0:T(8,128)S(1)} %get-tuple-element.55.refs_4_.refs_3_), channel_id=1, source_target_pairs={{0,1},{1,0},{2,3},{3,2},{4,5},{5,4},{6,7},{7,6},{8,9},{9,8},{10,11... | collective-permute-start | bytes 24584 | tf_op jit(solution)/shard_map/ppermute | solution.py:799

commit v12 on v11

--- a/solution.py
+++ b/solution.py
@@ -438,7 +438,7 @@
             )
 
 
-def inner_part(cumul, docs, query, key, value, tokens, heads, first, count, after):
+def inner_part(cumul, docs, query, key, value, tokens, heads, first, count, after, relay):
     return call(
         functools.partial(inner_kernel, tokens, heads, first, count),
         "inner_part",
@@ -451,6 +451,7 @@
             4 * count * tokens * tokens * HEAD_DIM, tokens * heads * LANES * 12, count * tokens * tokens
         ),
         after=after,
+        relay=relay,
     )
 
 
@@ -727,12 +728,12 @@
     )
 
     forward = [(b, b + 2) for b in everyone]
-    pairs = [(b, b + 1) for b in everyone if b % 2 == 0]
-    longest_hop = [b for b in everyone if b % 2 and b + window < blocks] if window % 2 else []
-    pairs += [(b, b + window) for b in longest_hop]
-    taken = [b + window for b in longest_hop]
-    pairs += [(b, b - 1) for b in everyone if b % 2 and b not in longest_hop and b - 1 not in taken]
-    beside = (send(own_kv, pairs), (window if window % 2 else blocks, 1))
+    hop = {b: b ^ 1 for b in everyone}
+    if window % 2:
+        for b in range(1, blocks - window, 2):
+            last = next(a for a in everyone if hop[a] == b + window)
+            hop[b], hop[last] = b + window, hop[b]
+    beside = (send(own_kv, list(hop.items())), (window if window % 2 else blocks, 1))
     ahead = send(own_kv, forward)
 
     size = quarter_rows(heads)
@@ -742,12 +743,11 @@
 
     state = {}
 
-    def first_attention(after, relay):
-        state["wide"], *out = attend(
-            place, (docs, flat(soft_query)), None, [(own_kv, (0, 0))], False, tokens, heads, kv_here, after, relay
+    def first_attention(after):
+        state["wide"], state["sum"] = attend(
+            place, (docs, flat(soft_query)), None, [(own_kv, (0, 0))], False, tokens, heads, kv_here, after
         )
-        state["sum"] = out[0]
-        return out
+        return state["sum"]
 
     def more_attention(kv, is_last, after, relay=()):
         out = attend(
@@ -758,19 +758,20 @@
 
     inner, qh = [], []
 
-    def inner_of(part, after):
+    def inner_of(part, after, relay=()):
         n = heads // parts
         got = inner_part(
-            cumul, docs, flat(lin_query), key, value, tokens, heads, part * n, n, after
+            cumul, docs, flat(lin_query), key, value, tokens, heads, part * n, n, after, relay
         )
         inner.append(got[0])
         qh.append(got[1])
-        return got[0]
-
-    done, lane = first_attention([sent[0]], [ahead])
+        return (got[0], *got[2:]) if relay else got[0]
+
+    done = first_attention([sent[0]])
+    lane = ahead
+    if parts > 1:
+        done, lane = inner_of(0, [done], [ahead])
     second = send(lane, [(b, b + 2) for b in range(2, blocks - 2)])
-    if parts > 1:
-        done = inner_of(0, [done])
     run, lane = group_map(place, quarters, size, [done, beside[0]], [lane])
     first_cross = send(lane, swap)
     stages = (blocks // GROUP_BLOCKS).bit_length() - 1

time: 57.2 us -> 56.9 us (level)
  waiting for transfers between devices: 2.64 us -> 11 us
  starting transfers between devices: 26.2 us -> 18.1 us
  Pallas kernels: 27.2 us -> 25.5 us
  local copies, waits for them, and re-layouts: 0.02 us -> 1.24 us
    ppermute x12, waiting for transfers between devices: 2.63 us -> 11 us  [send(): return lax.ppermute(x, 'seq', [(a, b % blocks) for a, b in pairs])]
    ppermute x12, starting transfers between devices: 24.3 us -> 16.2 us  [send(): return lax.ppermute(x, 'seq', [(a, b % blocks) for a, b in pairs])]
    pallas_call x12, Pallas kernels: 27.2 us -> 25.5 us  [call(): pl.pallas_call(run, out_shape=outs, in_specs=[SMEM] * len(scalars) + [HBM...]
    unnamed x8, local copies, waits for them, and re-layouts: 0.02 us -> 1.24 us
  transfers between devices with their start and end apart: 15 -> 15, of which waited for: 1 -> 2; matrix products, arithmetic and copies ran while one was open for 0% -> 0% of each run, Pallas kernels for 40% -> 39%
where the time goes in v12:
time: 56.9 us; the launch traced here: 56.8 us
  Pallas kernels  25.5 us (45%)
  starting transfers between devices  18.1 us (32%)
  waiting for transfers between devices  11 us (19%)
  local copies, waits for them, and re-layouts  1.24 us (2%)
  between operations  1.01 us (2%)
    pallas_call x12, Pallas kernels, call(): pl.pallas_call(run, out_shape=outs, in_specs=[SMEM] * len(scalars) + [HBM...  25.5 us
    ppermute x12, starting transfers between devices, send(): return lax.ppermute(x, 'seq', [(a, b % blocks) for a, b in pairs])  16.2 us
    ppermute x12, waiting for transfers between devices, send(): return lax.ppermute(x, 'seq', [(a, b % blocks) for a, b in pairs])  11 us
    ppermute x3, starting transfers between devices, body(): lax.ppermute(squares, 'tp', [(t, t ^ other) for t in range(tensor)])  1.88 us
    unnamed x8, local copies, waits for them, and re-layouts  1.24 us
  transfers between devices with their start and end apart: 15, of which 2 were waited for; matrix products, arithmetic and copies ran while one was open for 0% of the time, Pallas kernels for 39%

profile of v12, /device:TPU:0, one launch (start us, length us, event | category | flops | bytes accessed | tf_op | source)
XLA Modules:
  0.0 56.8 jit_solution(16940094620864424867)
XLA Ops:
  0.6 1.9 %fetch.1 = (bf16[1040,128]{1,0:T(8,128)(2,1)S(1)}, f32[16,128]{1,0:T(8,128)S(1)}, f32[256,128]{1,0:T(8,128)S(1)}, bf16[4096,128]{1,0:T(8,128)(2,1)S(1)}, bf16[4096,128]{1,0:T(8,128)(2,1)S(1)}) custom-call(s32[1]{0:T(128)} %bitcast.2.refs_0_, s32[2,128]{1,0:T(2,128)} %bitcast.23, f32[16,256]{1,0:T(8,128)} %bitcast.22, bf16[2048,128]{1,0:T(8,128)(2,1)} %bitcast.20, ...), custom_call_target="tpu_custom_call" | custom-call | bytes 3145728 | tf_op jit(solution)/shard_map/fetch/pallas_call | solution.py:68
  2.6 3.1 %collective-permute-start.3 = (bf16[1040,128]{1,0:T(8,128)(2,1)S(1)}, bf16[1040,128]{1,0:T(8,128)(2,1)S(1)}, u32[]{:S(2)}, u32[]{:S(2)}) collective-permute-start(bf16[1040,128]{1,0:T(8,128)(2,1)S(1)} %get-tuple-element.38.refs_3_), channel_id=1, source_target_pairs={{0,8},{4,12},{8,16},{12,20},{16,24},{20,28},{24,0},{28,4},{1,9},{5... | collective-permute-start | bytes 798728 | tf_op jit(solution)/shard_map/ppermute | solution.py:710
  5.7 1.5 %collective-permute-start.4 = (bf16[1040,128]{1,0:T(8,128)(2,1)S(1)}, bf16[1040,128]{1,0:T(8,128)(2,1)S(1)}, u32[]{:S(2)}, u32[]{:S(2)}) collective-permute-start(bf16[1040,128]{1,0:T(8,128)(2,1)S(1)} %get-tuple-element.38.refs_3_), channel_id=1, source_target_pairs={{0,4},{4,24},{8,12},{12,8},{16,20},{20,16},{24,28},{28,0},{1,5},{5... | collective-permute-start | bytes 798728 | tf_op jit(solution)/shard_map/ppermute | solution.py:710
  7.2 2.7 %block_state.1 = (bf16[528,128]{1,0:T(8,128)(2,1)S(1)}, bf16[528,128]{1,0:T(8,128)(2,1)S(1)}, bf16[528,128]{1,0:T(8,128)(2,1)S(1)}, bf16[528,128]{1,0:T(8,128)(2,1)S(1)}) custom-call(s32[1]{0:T(128)} %bitcast.1.refs_0_, f32[256,128]{1,0:T(8,128)S(1)} %get-tuple-element.31.refs_1_.refs_0_.refs_3_, f32[16,128]{1,0:T(8,128)S(1)} %get-tuple-element.30.refs_2_.refs_1_, ...), custom_call_target="tpu_custom_call" | custom-call | flops 134217728 | bytes 5242880 | tf_op jit(solution)/shard_map/block_state/pallas_call | solution.py:68
  9.9 0.0 copy-start
  9.9 2.1 %collective-permute-start = (bf16[528,128]{1,0:T(8,128)(2,1)S(1)}, bf16[528,128]{1,0:T(8,128)(2,1)S(1)}, u32[]{:S(2)}, u32[]{:S(2)}) collective-permute-start(bf16[528,128]{1,0:T(8,128)(2,1)S(1)} %get-tuple-element.35), channel_id=1, source_target_pairs={{0,4},{4,0},{8,12},{12,8},{16,20},{20,16},{24,28},{28,24},{1,5},{5... | collective-permute-start | bytes 405512 | tf_op jit(solution)/shard_map/ppermute | solution.py:710
  12.0 0.0 collective-permute-start.1
  12.1 1.5 %collective-permute-start.2 = (bf16[528,128]{1,0:T(8,128)(2,1)S(1)}, bf16[528,128]{1,0:T(8,128)(2,1)S(1)}, u32[]{:S(2)}, u32[]{:S(2)}) collective-permute-start(bf16[528,128]{1,0:T(8,128)(2,1)S(1)} %get-tuple-element.37), channel_id=1, source_target_pairs={{0,12},{4,8},{8,4},{12,0},{16,28},{20,24},{24,20},{28,16},{1,13},{... | collective-permute-start | bytes 405512 | tf_op jit(solution)/shard_map/ppermute | solution.py:710
  13.6 0.0 copy-start.3
  13.6 1.2 %copy-done.3 = bf16[256,16,128]{2,1,0:T(8,128)(2,1)S(1)} copy-done((bf16[256,16,128]{2,1,0:T(8,128)(2,1)S(1)}, bf16[256,16,128]{2,1,0:T(8,128)(2,1)}, u32[]{:S(2)}) %copy-start.3) | copy-done | bytes 1048600
  14.8 2.6 %attend.4 = (bf16[2,2048,256]{2,1,0:T(8,128)(2,1)S(1)}, f32[2,144,2048]{2,1,0:T(8,128)S(1)}) custom-call(s32[1]{0:T(128)} %bitcast.1.refs_0_, f32[16,128]{1,0:T(8,128)S(1)} %get-tuple-element.30.refs_2_.refs_1_, bf16[4096,128]{1,0:T(8,128)(2,1)S(1)} %bitcast.16, bf16[1040,128]{1,0:T(8,128)(2,1)S(1)} %get-tuple-element.38.refs_3_, ...), custom_call_target="tpu_custom_call" | custom-call | flops 1073741824 | bytes 8388608 | tf_op jit(solution)/shard_map/attend/pallas_call | solution.py:68
  17.4 0.0 collective-permute-done.3.refs_6_
  17.4 0.0 copy-done
  17.5 1.9 %inner_part.2 = (f32[2048,128]{1,0:T(8,128)S(1)}, bf16[2048,128]{1,0:T(8,128)(2,1)S(1)}, bf16[1040,128]{1,0:T(8,128)(2,1)S(1)}) custom-call(f32[256,128]{1,0:T(8,128)S(1)} %get-tuple-element.31.refs_1_.refs_0_.refs_3_, f32[16,128]{1,0:T(8,128)S(1)} %get-tuple-element.30.refs_2_.refs_1_, bf16[4096,128]{1,0:T(8,128)(2,1)S(1)} %bitcast.13, ...), custom_call_target="tpu_custom_call" | custom-call | flops 268435456 | bytes 6291456 | tf_op jit(solution)/shard_map/inner_part/pallas_call | solution.py:68
  19.4 0.9 %collective-permute-start.6 = (bf16[1040,128]{1,0:T(8,128)(2,1)S(1)}, bf16[1040,128]{1,0:T(8,128)(2,1)S(1)}, u32[]{:S(2)}, u32[]{:S(2)}) collective-permute-start(bf16[1040,128]{1,0:T(8,128)(2,1)S(1)} %get-tuple-element.41.refs_7_), channel_id=1, source_target_pairs={{8,16},{12,20},{16,24},{20,28},{9,17},{13,21},{17,25},{21,29},{10,... | collective-permute-start | bytes 798728 | tf_op jit(solution)/shard_map/ppermute | solution.py:710
  20.3 0.0 collective-permute-done.refs_2_
  20.3 0.0 collective-permute-done.1.refs_3_
  20.3 6.3 %collective-permute-done.2.refs_4_ = bf16[528,128]{1,0:T(8,128)(2,1)S(1)} collective-permute-done((bf16[528,128]{1,0:T(8,128)(2,1)S(1)}, bf16[528,128]{1,0:T(8,128)(2,1)S(1)}, u32[]{:S(2)}, u32[]{:S(2)}) %collective-permute-start.2) | collective-permute-done | bytes 135200 | tf_op jit(solution)/shard_map/ppermute | solution.py:710
  26.5 0.0 collective-permute-done.4.refs_6_.refs_3_
  26.6 0.2 group_map.1
  26.8 0.7 %collective-permute-start.5 = (bf16[528,128]{1,0:T(8,128)(2,1)S(1)}, bf16[528,128]{1,0:T(8,128)(2,1)S(1)}, u32[]{:S(2)}, u32[]{:S(2)}) collective-permute-start(bf16[528,128]{1,0:T(8,128)(2,1)S(1)} %get-tuple-element.42.refs_5_), channel_id=1, source_target_pairs={{0,16},{4,20},{8,24},{12,28},{16,0},{20,4},{24,8},{28,12},{1,17},{... | collective-permute-start | bytes 405512 | tf_op jit(solution)/shard_map/ppermute | solution.py:710
  27.4 1.7 %collective-permute-start.10 = (bf16[1040,128]{1,0:T(8,128)(2,1)S(1)}, bf16[1040,128]{1,0:T(8,128)(2,1)S(1)}, u32[]{:S(2)}, u32[]{:S(2)}) collective-permute-start(bf16[1040,128]{1,0:T(8,128)(2,1)S(1)} %get-tuple-element.44.refs_4_), channel_id=1, source_target_pairs={{0,4},{4,0},{8,12},{12,8},{16,20},{20,16},{24,28},{28,24},{1,5},{5... | collective-permute-start | bytes 798728 | tf_op jit(solution)/shard_map/ppermute | solution.py:710
  29.1 3.7 %attend.5.refs_5_.refs_2_ = f32[2,144,2048]{2,1,0:T(8,128)S(1)} custom-call(s32[1]{0:T(128)} %bitcast.1.refs_0_, bf16[2,2048,256]{2,1,0:T(8,128)(2,1)S(1)} %get-tuple-element.43.refs_1_, f32[2,144,2048]{2,1,0:T(8,128)S(1)} %get-tuple-element.39.refs_5_.refs_2_, bf16[1040,128]{1,0:T(8,128)(2,1)S(1)} %collective-permute-done.4.refs_6_.refs_3_, ...), custom_call_target="tpu_custom_call" | custom-call | flops 2147483648 | bytes 8388608 | tf_op jit(solution)/shard_map/attend/pallas_call | solution.py:68
  32.8 1.9 %inner_part.3 = (f32[2048,128]{1,0:T(8,128)S(1)}, bf16[2048,128]{1,0:T(8,128)(2,1)S(1)}) custom-call(f32[256,128]{1,0:T(8,128)S(1)} %get-tuple-element.31.refs_1_.refs_0_.refs_3_, f32[16,128]{1,0:T(8,128)S(1)} %get-tuple-element.30.refs_2_.refs_1_, bf16[4096,128]{1,0:T(8,128)(2,1)S(1)} %bitcast.14, bf16[4096,128]{1,0:T(8,128)(2,1)S(1)} %get-tuple-element.32.refs_3_, ...), custom_call_target="tpu_custom_call" | custom-call | flops 268435456 | bytes 6291456 | tf_op jit(solution)/shard_map/inner_part/pallas_call | solution.py:68
  34.7 0.0 collective-permute-done.5.refs_5_
  34.8 0.0 collective-permute-done.6.refs_7_
  34.8 0.3 prior_states.1
  35.0 0.4 collective-permute-start.14
  35.4 1.7 %collective-permute-start.7 = (bf16[512,128]{1,0:T(8,128)(2,1)S(1)}, bf16[512,128]{1,0:T(8,128)(2,1)S(1)}, u32[]{:S(2)}, u32[]{:S(2)}) collective-permute-start(bf16[512,128]{1,0:T(8,128)(2,1)S(1)} %get-tuple-element.50), channel_id=1, source_target_pairs={{0,4},{4,0},{8,12},{12,8},{16,20},{20,16},{24,28},{28,24},{1,5},{5... | collective-permute-start | bytes 393224 | tf_op jit(solution)/shard_map/ppermute | solution.py:710
  37.1 1.2 %collective-permute-start.8 = (bf16[512,128]{1,0:T(8,128)(2,1)S(1)}, bf16[512,128]{1,0:T(8,128)(2,1)S(1)}, u32[]{:S(2)}, u32[]{:S(2)}) collective-permute-start(bf16[512,128]{1,0:T(8,128)(2,1)S(1)} %get-tuple-element.51), channel_id=1, source_target_pairs={{0,8},{4,12},{8,0},{12,4},{16,24},{20,28},{24,16},{28,20},{1,9},{5... | collective-permute-start | bytes 393224 | tf_op jit(solution)/shard_map/ppermute | solution.py:710
  38.4 1.4 %collective-permute-start.9 = (bf16[512,128]{1,0:T(8,128)(2,1)S(1)}, bf16[512,128]{1,0:T(8,128)(2,1)S(1)}, u32[]{:S(2)}, u32[]{:S(2)}) collective-permute-start(bf16[512,128]{1,0:T(8,128)(2,1)S(1)} %get-tuple-element.52), channel_id=1, source_target_pairs={{0,12},{4,8},{8,4},{12,0},{16,28},{20,24},{24,20},{28,16},{1,13},{... | collective-permute-start | bytes 393224 | tf_op jit(solution)/shard_map/ppermute | solution.py:710
  39.8 0.0 collective-permute-done.10.refs_3_
  39.8 3.7 %attend.6.refs_12_.refs_2_ = f32[2,144,2048]{2,1,0:T(8,128)S(1)} custom-call(s32[1]{0:T(128)} %bitcast.1.refs_0_, bf16[2,2048,256]{2,1,0:T(8,128)(2,1)S(1)} %get-tuple-element.43.refs_1_, f32[2,144,2048]{2,1,0:T(8,128)S(1)} %attend.5.refs_5_.refs_2_, bf16[1040,128]{1,0:T(8,128)(2,1)S(1)} %collective-permute-done.10.refs_3_, ...), custom_call_target="tpu_custom_call" | custom-call | flops 2147483648 | bytes 8388608 | tf_op jit(solution)/shard_map/attend/pallas_call | solution.py:68
  43.4 4.7 %collective-permute-done.7.refs_9_ = bf16[512,128]{1,0:T(8,128)(2,1)S(1)} collective-permute-done((bf16[512,128]{1,0:T(8,128)(2,1)S(1)}, bf16[512,128]{1,0:T(8,128)(2,1)S(1)}, u32[]{:S(2)}, u32[]{:S(2)}) %collective-permute-start.7) | collective-permute-done | bytes 131104 | tf_op jit(solution)/shard_map/ppermute | solution.py:710
  48.1 0.0 collective-permute-done.8.refs_10_
  48.1 0.0 collective-permute-done.9.refs_11_
  48.1 1.6 %mix.1 = (f32[4096,128]{1,0:T(8,128)S(1)}, f32[8,256]{1,0:T(8,128)S(1)}) custom-call(s32[1]{0:T(128)} %bitcast.1.refs_0_, f32[16,128]{1,0:T(8,128)S(1)} %get-tuple-element.30.refs_2_.refs_1_, f32[8,128]{1,0:T(8,128)S(1)} %get-tuple-element.46.refs_5_.refs_2_, f32[256,128]{1,0:T(8,128)S(1)} %get-tuple-element.31.refs_1_.refs_0_.refs_3_, ...), custom_call_target="tpu_custom_call" | custom-call | flops 134217728 | bytes 5242880 | tf_op jit(solution)/shard_map/mix/pallas_call | solution.py:68
  49.7 0.0 collective-permute-start.13
  49.8 1.6 %collective-permute-start.12 = (f32[8,256]{1,0:T(8,128)S(1)}, f32[8,256]{1,0:T(8,128)S(1)}, u32[]{:S(2)}, u32[]{:S(2)}) collective-permute-start(f32[8,256]{1,0:T(8,128)S(1)} %get-tuple-element.55.refs_4_.refs_3_), channel_id=1, source_target_pairs={{0,2},{1,3},{2,0},{3,1},{4,6},{5,7},{6,4},{7,5},{8,10},{9,11},{10,... | collective-permute-start | bytes 24584 | tf_op jit(solution)/shard_map/ppermute | solution.py:800
  51.3 0.3 collective-permute-start.11
  51.6 0.0 collective-permute-done.14.refs_3_
  51.6 3.3 %attend.7 = (bf16[4096,128]{1,0:T(8,128)(2,1)}, f32[8,128]{1,0:T(8,128)S(1)}) custom-call(s32[1]{0:T(128)} %bitcast.1.refs_0_, bf16[2,2048,256]{2,1,0:T(8,128)(2,1)S(1)} %get-tuple-element.43.refs_1_, f32[2,144,2048]{2,1,0:T(8,128)S(1)} %attend.6.refs_12_.refs_2_, bf16[1040,128]{1,0:T(8,128)(2,1)S(1)} %collective-permute-done.14.refs_3_, ...), custom_call_target="tpu_custom_call" | custom-call | flops 1073741824 | bytes 8388608 | tf_op jit(solution)/shard_map/attend/pallas_call | solution.py:68
  54.9 0.0 collective-permute-done.13.refs_6_
  54.9 0.0 collective-permute-done.12.refs_5_
  54.9 0.0 collective-permute-done.11.refs_4_
  54.9 0.0 copy-done.1
  54.9 0.0 copy-done.2
  55.0 1.6 %finish.1 = bf16[4096,128]{1,0:T(8,128)(2,1)} custom-call(f32[16,128]{1,0:T(8,128)S(1)} %copy-done.2, bf16[4096,128]{1,0:T(8,128)(2,1)S(1)} %bitcast.15, f32[4096,128]{1,0:T(8,128)S(1)} %get-tuple-element.54.refs_2_, f32[8,256]{1,0:T(8,128)S(1)} %get-tuple-element.55.refs_4_.refs_3_, f32[8,256]{1,0:T(8,128)S(1)} %collective-permute-done.11.refs_4_, ...), custom_call_target="tpu_custom_call" | custom-call | bytes 4194304 | tf_op jit(solution)/shard_map/finish/pallas_call | solution.py:68
  (2 shorter events, 0.0 us)
Async XLA Ops:
  2.6 14.8 %collective-permute-start.3 = (bf16[1040,128]{1,0:T(8,128)(2,1)S(1)}, bf16[1040,128]{1,0:T(8,128)(2,1)S(1)}, u32[]{:S(2)}, u32[]{:S(2)}) collective-permute-start(bf16[1040,128]{1,0:T(8,128)(2,1)S(1)} %get-tuple-element.38.refs_3_), channel_id=1, source_target_pairs={{0,8},{4,12},{8,16},{12,20},{16,24},{20,28},{24,0},{28,4},{1,9},{5... | collective-permute-start | bytes 798728 | tf_op jit(solution)/shard_map/ppermute | solution.py:710
  5.7 20.9 %collective-permute-start.4 = (bf16[1040,128]{1,0:T(8,128)(2,1)S(1)}, bf16[1040,128]{1,0:T(8,128)(2,1)S(1)}, u32[]{:S(2)}, u32[]{:S(2)}) collective-permute-start(bf16[1040,128]{1,0:T(8,128)(2,1)S(1)} %get-tuple-element.38.refs_3_), channel_id=1, source_target_pairs={{0,4},{4,24},{8,12},{12,8},{16,20},{20,16},{24,28},{28,0},{1,5},{5... | collective-permute-start | bytes 798728 | tf_op jit(solution)/shard_map/ppermute | solution.py:710
  9.9 7.5 %copy-start = (bf16[256,16,128]{2,1,0:T(8,128)(2,1)S(1)}, bf16[256,16,128]{2,1,0:T(8,128)(2,1)}, u32[]{:S(2)}) copy-start(bf16[256,16,128]{2,1,0:T(8,128)(2,1)} %param.10) | copy-start | bytes 3145732
  9.9 10.3 %collective-permute-start = (bf16[528,128]{1,0:T(8,128)(2,1)S(1)}, bf16[528,128]{1,0:T(8,128)(2,1)S(1)}, u32[]{:S(2)}, u32[]{:S(2)}) collective-permute-start(bf16[528,128]{1,0:T(8,128)(2,1)S(1)} %get-tuple-element.35), channel_id=1, source_target_pairs={{0,4},{4,0},{8,12},{12,8},{16,20},{20,16},{24,28},{28,24},{1,5},{5... | collective-permute-start | bytes 405512 | tf_op jit(solution)/shard_map/ppermute | solution.py:710
  12.0 8.2 %collective-permute-start.1 = (bf16[528,128]{1,0:T(8,128)(2,1)S(1)}, bf16[528,128]{1,0:T(8,128)(2,1)S(1)}, u32[]{:S(2)}, u32[]{:S(2)}) collective-permute-start(bf16[528,128]{1,0:T(8,128)(2,1)S(1)} %get-tuple-element.36), channel_id=1, source_target_pairs={{0,8},{4,12},{8,0},{12,4},{16,24},{20,28},{24,16},{28,20},{1,9},{5... | collective-permute-start | bytes 405512 | tf_op jit(solution)/shard_map/ppermute | solution.py:710
  12.1 14.5 %collective-permute-start.2 = (bf16[528,128]{1,0:T(8,128)(2,1)S(1)}, bf16[528,128]{1,0:T(8,128)(2,1)S(1)}, u32[]{:S(2)}, u32[]{:S(2)}) collective-permute-start(bf16[528,128]{1,0:T(8,128)(2,1)S(1)} %get-tuple-element.37), channel_id=1, source_target_pairs={{0,12},{4,8},{8,4},{12,0},{16,28},{20,24},{24,20},{28,16},{1,13},{... | collective-permute-start | bytes 405512 | tf_op jit(solution)/shard_map/ppermute | solution.py:710
  13.6 1.2 %copy-start.3 = (bf16[256,16,128]{2,1,0:T(8,128)(2,1)S(1)}, bf16[256,16,128]{2,1,0:T(8,128)(2,1)}, u32[]{:S(2)}) copy-start(bf16[256,16,128]{2,1,0:T(8,128)(2,1)} %param.17) | copy-start | bytes 3145732
  19.4 15.4 %collective-permute-start.6 = (bf16[1040,128]{1,0:T(8,128)(2,1)S(1)}, bf16[1040,128]{1,0:T(8,128)(2,1)S(1)}, u32[]{:S(2)}, u32[]{:S(2)}) collective-permute-start(bf16[1040,128]{1,0:T(8,128)(2,1)S(1)} %get-tuple-element.41.refs_7_), channel_id=1, source_target_pairs={{8,16},{12,20},{16,24},{20,28},{9,17},{13,21},{17,25},{21,29},{10,... | collective-permute-start | bytes 798728 | tf_op jit(solution)/shard_map/ppermute | solution.py:710
  26.8 8.0 %collective-permute-start.5 = (bf16[528,128]{1,0:T(8,128)(2,1)S(1)}, bf16[528,128]{1,0:T(8,128)(2,1)S(1)}, u32[]{:S(2)}, u32[]{:S(2)}) collective-permute-start(bf16[528,128]{1,0:T(8,128)(2,1)S(1)} %get-tuple-element.42.refs_5_), channel_id=1, source_target_pairs={{0,16},{4,20},{8,24},{12,28},{16,0},{20,4},{24,8},{28,12},{1,17},{... | collective-permute-start | bytes 405512 | tf_op jit(solution)/shard_map/ppermute | solution.py:710
  27.4 12.3 %collective-permute-start.10 = (bf16[1040,128]{1,0:T(8,128)(2,1)S(1)}, bf16[1040,128]{1,0:T(8,128)(2,1)S(1)}, u32[]{:S(2)}, u32[]{:S(2)}) collective-permute-start(bf16[1040,128]{1,0:T(8,128)(2,1)S(1)} %get-tuple-element.44.refs_4_), channel_id=1, source_target_pairs={{0,4},{4,0},{8,12},{12,8},{16,20},{20,16},{24,28},{28,24},{1,5},{5... | collective-permute-start | bytes 798728 | tf_op jit(solution)/shard_map/ppermute | solution.py:710
  35.0 16.6 %collective-permute-start.14 = (bf16[1040,128]{1,0:T(8,128)(2,1)S(1)}, bf16[1040,128]{1,0:T(8,128)(2,1)S(1)}, u32[]{:S(2)}, u32[]{:S(2)}) collective-permute-start(bf16[1040,128]{1,0:T(8,128)(2,1)S(1)} %get-tuple-element.53.refs_4_), channel_id=1, source_target_pairs={{0,4},{4,0},{8,12},{12,8},{16,20},{20,16},{24,28},{28,24},{1,5},{5... | collective-permute-start | bytes 798728 | tf_op jit(solution)/shard_map/ppermute | solution.py:710
  35.4 12.7 %collective-permute-start.7 = (bf16[512,128]{1,0:T(8,128)(2,1)S(1)}, bf16[512,128]{1,0:T(8,128)(2,1)S(1)}, u32[]{:S(2)}, u32[]{:S(2)}) collective-permute-start(bf16[512,128]{1,0:T(8,128)(2,1)S(1)} %get-tuple-element.50), channel_id=1, source_target_pairs={{0,4},{4,0},{8,12},{12,8},{16,20},{20,16},{24,28},{28,24},{1,5},{5... | collective-permute-start | bytes 393224 | tf_op jit(solution)/shard_map/ppermute | solution.py:710
  37.1 11.0 %collective-permute-start.8 = (bf16[512,128]{1,0:T(8,128)(2,1)S(1)}, bf16[512,128]{1,0:T(8,128)(2,1)S(1)}, u32[]{:S(2)}, u32[]{:S(2)}) collective-permute-start(bf16[512,128]{1,0:T(8,128)(2,1)S(1)} %get-tuple-element.51), channel_id=1, source_target_pairs={{0,8},{4,12},{8,0},{12,4},{16,24},{20,28},{24,16},{28,20},{1,9},{5... | collective-permute-start | bytes 393224 | tf_op jit(solution)/shard_map/ppermute | solution.py:710
  38.4 9.8 %collective-permute-start.9 = (bf16[512,128]{1,0:T(8,128)(2,1)S(1)}, bf16[512,128]{1,0:T(8,128)(2,1)S(1)}, u32[]{:S(2)}, u32[]{:S(2)}) collective-permute-start(bf16[512,128]{1,0:T(8,128)(2,1)S(1)} %get-tuple-element.52), channel_id=1, source_target_pairs={{0,12},{4,8},{8,4},{12,0},{16,28},{20,24},{24,20},{28,16},{1,13},{... | collective-permute-start | bytes 393224 | tf_op jit(solution)/shard_map/ppermute | solution.py:710
  49.7 5.2 %copy-start.1 = (bf16[256,16,128]{2,1,0:T(8,128)(2,1)S(1)}, bf16[256,16,128]{2,1,0:T(8,128)(2,1)}, u32[]{:S(2)}) copy-start(bf16[256,16,128]{2,1,0:T(8,128)(2,1)} %param.13) | copy-start | bytes 3145732
  49.7 5.2 %copy-start.2 = (f32[16,128]{1,0:T(8,128)S(1)}, f32[16,128]{1,0:T(8,128)}, u32[]{:S(2)}) copy-start(f32[16,128]{1,0:T(8,128)} %refs_0_.1) | copy-start | bytes 24580
  49.7 5.2 %collective-permute-start.13 = (f32[8,256]{1,0:T(8,128)S(1)}, f32[8,256]{1,0:T(8,128)S(1)}, u32[]{:S(2)}, u32[]{:S(2)}) collective-permute-start(f32[8,256]{1,0:T(8,128)S(1)} %get-tuple-element.55.refs_4_.refs_3_), channel_id=1, source_target_pairs={{0,3},{1,2},{2,1},{3,0},{4,7},{5,6},{6,5},{7,4},{8,11},{9,10},{10,... | collective-permute-start | bytes 24584 | tf_op jit(solution)/shard_map/ppermute | solution.py:800
  49.8 5.1 %collective-permute-start.12 = (f32[8,256]{1,0:T(8,128)S(1)}, f32[8,256]{1,0:T(8,128)S(1)}, u32[]{:S(2)}, u32[]{:S(2)}) collective-permute-start(f32[8,256]{1,0:T(8,128)S(1)} %get-tuple-element.55.refs_4_.refs_3_), channel_id=1, source_target_pairs={{0,2},{1,3},{2,0},{3,1},{4,6},{5,7},{6,4},{7,5},{8,10},{9,11},{10,... | collective-permute-start | bytes 24584 | tf_op jit(solution)/shard_map/ppermute | solution.py:800
  51.3 3.6 %collective-permute-start.11 = (f32[8,256]{1,0:T(8,128)S(1)}, f32[8,256]{1,0:T(8,128)S(1)}, u32[]{:S(2)}, u32[]{:S(2)}) collective-permute-start(f32[8,256]{1,0:T(8,128)S(1)} %get-tuple-element.55.refs_4_.refs_3_), channel_id=1, source_target_pairs={{0,1},{1,0},{2,3},{3,2},{4,5},{5,4},{6,7},{7,6},{8,9},{9,8},{10,11... | collective-permute-start | bytes 24584 | tf_op jit(solution)/shard_map/ppermute | solution.py:800

commit v13 on v12

--- a/solution.py
+++ b/solution.py
@@ -94,6 +94,10 @@
     rows = lax.broadcasted_iota(jnp.int32, (tokens, tokens), 0)
     cols = lax.broadcasted_iota(jnp.int32, (tokens, tokens), 1)
     return rows >= cols
+
+
+def pass_on(x, after):
+    return call(lambda: None, "pass_on", [], [], (), after=after, relay=[x])[0]
 
 
 def fetch_kernel(tokens, heads, kv_here, start_ref, *refs):
@@ -179,9 +183,11 @@
 def state_kernel(tokens, heads, place_ref, *refs):
     refs = list(refs)
     take = lambda n: [refs.pop(0) for _ in range(n)]
-    cumul_ref, doc_ref, key_ref, value_ref = take(4)
-    out_refs = take(GROUP_BLOCKS)
-    kf, vf, states = refs
+    query_in, cumul_ref, doc_ref, key_ref, value_ref = take(5)
+    out_refs, query_out = take(GROUP_BLOCKS), take(1)[0]
+    kf, vf, states, sem = refs
+    copy = pltpu.make_async_copy(query_in, query_out, sem)
+    copy.start()
     cumul, docs = cumul_ref[...], doc_ref[...]
     total = cumul[tokens - 1 : tokens, :]
     last_row = tokens // LANES - 1
@@ -208,21 +214,27 @@
             moved = pltpu.roll(total, LANES - skip, 1) if skip else total
             totals = jnp.where(taker == c, moved, totals)
         ref[size : size + INFO, :] = info_rows((*in_parts(totals), first_doc, last_doc))
-
-
-def block_state(place, cumul, docs, key, value, tokens, heads):
+    copy.wait()
+
+
+def block_state(place, soft_query, cumul, docs, key, value, tokens, heads):
     return call(
         functools.partial(state_kernel, tokens, heads),
         "block_state",
         [place],
-        [cumul, docs, key, value],
-        (sds((quarter_rows(heads) + INFO, LANES), BF16),) * GROUP_BLOCKS,
+        [soft_query, cumul, docs, key, value],
+        (
+            *[sds((quarter_rows(heads) + INFO, LANES), BF16)] * GROUP_BLOCKS,
+            sds(soft_query.shape, BF16),
+        ),
         scratch=[
             pltpu.VMEM((tokens * heads, LANES), F32),
             pltpu.VMEM((tokens * heads, LANES), F32),
             pltpu.VMEM((heads * HEAD_DIM, LANES), F32),
+            pltpu.SemaphoreType.DMA,
         ],
         estimate=cost(2 * heads * tokens * HEAD_DIM**2, 5 * tokens * heads * LANES * 2),
+        hbm=1,
     )
 
 
@@ -733,19 +745,20 @@
         for b in range(1, blocks - window, 2):
             last = next(a for a in everyone if hop[a] == b + window)
             hop[b], hop[last] = b + window, hop[b]
-    beside = (send(own_kv, list(hop.items())), (window if window % 2 else blocks, 1))
     ahead = send(own_kv, forward)
 
     size = quarter_rows(heads)
     others = range(1, GROUP_BLOCKS)
-    sent = block_state(place, cumul, docs, key, value, tokens, heads)
+    *sent, query = block_state(
+        place, flat(soft_query), cumul, docs, key, value, tokens, heads
+    )
     quarters = [sent[0]] + [send(sent[j], [(b, b ^ j) for b in everyone]) for j in others]
 
     state = {}
 
     def first_attention(after):
         state["wide"], state["sum"] = attend(
-            place, (docs, flat(soft_query)), None, [(own_kv, (0, 0))], False, tokens, heads, kv_here, after
+            place, (docs, query), None, [(own_kv, (0, 0))], False, tokens, heads, kv_here, after
         )
         return state["sum"]
 
@@ -772,24 +785,24 @@
     if parts > 1:
         done, lane = inner_of(0, [done], [ahead])
     second = send(lane, [(b, b + 2) for b in range(2, blocks - 2)])
-    run, lane = group_map(place, quarters, size, [done, beside[0]], [lane])
+    run, lane, own_copy = group_map(place, quarters, size, [done], [lane, own_kv])
     first_cross = send(lane, swap)
+    beside = (send(own_copy, list(hop.items())), (window if window % 2 else blocks, 1))
     stages = (blocks // GROUP_BLOCKS).bit_length() - 1
     before, done = None, run
     for stage in range(stages):
         came = send(run, [(b, b ^ (GROUP_BLOCKS << stage)) for b in everyone])
         if stage == stages - 1:
-            done = more_attention([beside, (lane, (2, 2))], False, [done])
+            done = more_attention([(lane, (2, 2))], False, [done])
             done = inner_of(parts - 1, [done])
         else:
             run, before = scan_step(place, stage + 2, run, came, before, size, [done])
             done = run
-    *priors, prior_doc, lane = prior_states(
-        place, stages + 1, quarters, came, before, size, [done], [second]
-    )
+    *priors, prior_doc = prior_states(place, stages + 1, quarters, came, before, size, [done])
     priors = [priors[0]] + [send(priors[j], [(b, b ^ j) for b in everyone]) for j in others]
-    done = more_attention([(first_cross, (2, 3)), (lane, (4, 4))], False, [prior_doc])
-    rest = [(send(lane, swap), (4, 5))]
+    done = more_attention([(first_cross, (2, 3)), (second, (4, 4))], False, [prior_doc])
+    lane = pass_on(second, [done, *priors])
+    rest = [beside, (send(lane, swap), (4, 5))]
     for back in range(3, window // 2 + 1):
         lane = send(lane, forward)
         rest.append((lane, (2 * back, 2 * back)))

time: 56.9 us -> 59.5 us (1.046)
  starting transfers between devices: 18.1 us -> 23.5 us
  waiting for transfers between devices: 11 us -> 8.41 us
  local copies, waits for them, and re-layouts: 1.24 us -> 0.01 us
  Pallas kernels: 25.5 us -> 26.4 us
    ppermute x12, starting transfers between devices: 16.2 us -> 21.6 us  [send(): return lax.ppermute(x, 'seq', [(a, b % blocks) for a, b in pairs])]
    ppermute x12, waiting for transfers between devices: 11 us -> 8.4 us  [send(): return lax.ppermute(x, 'seq', [(a, b % blocks) for a, b in pairs])]
    unnamed x8 -> x6, local copies, waits for them, and re-layouts: 1.24 us -> 0.01 us
    pallas_call x12 -> x13, Pallas kernels: 25.5 us -> 26.4 us  [call(): pl.pallas_call(run, out_shape=outs, in_specs=[SMEM] * len(scalars) + [HBM...]
  transfers between devices with their start and end apart: 15 -> 15, of which waited for: 2 -> 5; matrix products, arithmetic and copies ran while one was open for 0% -> 0% of each run, Pallas kernels for 39% -> 38%
where the time goes in v13:
time: 59.5 us; the launch traced here: 59.4 us
  Pallas kernels  26.4 us (44%)
  starting transfers between devices  23.5 us (39%)
  waiting for transfers between devices  8.41 us (14%)
  between operations  1 us (2%)
    pallas_call x13, Pallas kernels, call(): pl.pallas_call(run, out_shape=outs, in_specs=[SMEM] * len(scalars) + [HBM...  26.4 us
    ppermute x12, starting transfers between devices, send(): return lax.ppermute(x, 'seq', [(a, b % blocks) for a, b in pairs])  21.6 us
    ppermute x12, waiting for transfers between devices, send(): return lax.ppermute(x, 'seq', [(a, b % blocks) for a, b in pairs])  8.4 us
    ppermute x3, starting transfers between devices, body(): lax.ppermute(squares, 'tp', [(t, t ^ other) for t in range(tensor)])  1.88 us
  transfers between devices with their start and end apart: 15, of which 5 were waited for; matrix products, arithmetic and copies ran while one was open for 0% of the time, Pallas kernels for 38%

profile of v13, /device:TPU:0, one launch (start us, length us, event | category | flops | bytes accessed | tf_op | source)
XLA Modules:
  0.0 59.4 jit_solution(11697190077971363891)
XLA Ops:
  0.6 1.9 %fetch.1 = (bf16[1040,128]{1,0:T(8,128)(2,1)S(1)}, f32[16,128]{1,0:T(8,128)S(1)}, f32[256,128]{1,0:T(8,128)S(1)}, bf16[4096,128]{1,0:T(8,128)(2,1)S(1)}, bf16[4096,128]{1,0:T(8,128)(2,1)S(1)}) custom-call(s32[1]{0:T(128)} %bitcast.2.refs_0_, s32[2,128]{1,0:T(2,128)} %bitcast.23, f32[16,256]{1,0:T(8,128)} %bitcast.22, bf16[2048,128]{1,0:T(8,128)(2,1)} %bitcast.20, ...), custom_call_target="tpu_custom_call" | custom-call | bytes 3145728 | tf_op jit(solution)/shard_map/fetch/pallas_call | solution.py:68
  2.6 3.1 %collective-permute-start.3 = (bf16[1040,128]{1,0:T(8,128)(2,1)S(1)}, bf16[1040,128]{1,0:T(8,128)(2,1)S(1)}, u32[]{:S(2)}, u32[]{:S(2)}) collective-permute-start(bf16[1040,128]{1,0:T(8,128)(2,1)S(1)} %get-tuple-element.40.refs_3_.refs_7_), channel_id=1, source_target_pairs={{0,8},{4,12},{8,16},{12,20},{16,24},{20,28},{24,0},{28,4},{1,9},{5... | collective-permute-start | bytes 798728 | tf_op jit(solution)/shard_map/ppermute | solution.py:722
  5.7 3.8 %block_state.1 = (bf16[528,128]{1,0:T(8,128)(2,1)S(1)}, bf16[528,128]{1,0:T(8,128)(2,1)S(1)}, bf16[528,128]{1,0:T(8,128)(2,1)S(1)}, bf16[528,128]{1,0:T(8,128)(2,1)S(1)}, bf16[4096,128]{1,0:T(8,128)(2,1)S(1)}) custom-call(s32[1]{0:T(128)} %bitcast.1.refs_0_, bf16[4096,128]{1,0:T(8,128)(2,1)} %bitcast.19, ...), custom_call_target="tpu_custom_call" | custom-call | flops 134217728 | bytes 5242880 | tf_op jit(solution)/shard_map/block_state/pallas_call | solution.py:68
  9.4 0.0 copy-start
  9.5 1.6 %collective-permute-start = (bf16[528,128]{1,0:T(8,128)(2,1)S(1)}, bf16[528,128]{1,0:T(8,128)(2,1)S(1)}, u32[]{:S(2)}, u32[]{:S(2)}) collective-permute-start(bf16[528,128]{1,0:T(8,128)(2,1)S(1)} %get-tuple-element.36), channel_id=1, source_target_pairs={{0,4},{4,0},{8,12},{12,8},{16,20},{20,16},{24,28},{28,24},{1,5},{5... | collective-permute-start | bytes 405512 | tf_op jit(solution)/shard_map/ppermute | solution.py:722
  11.1 1.6 %collective-permute-start.1 = (bf16[528,128]{1,0:T(8,128)(2,1)S(1)}, bf16[528,128]{1,0:T(8,128)(2,1)S(1)}, u32[]{:S(2)}, u32[]{:S(2)}) collective-permute-start(bf16[528,128]{1,0:T(8,128)(2,1)S(1)} %get-tuple-element.37), channel_id=1, source_target_pairs={{0,8},{4,12},{8,0},{12,4},{16,24},{20,28},{24,16},{28,20},{1,9},{5... | collective-permute-start | bytes 405512 | tf_op jit(solution)/shard_map/ppermute | solution.py:722
  12.6 0.4 collective-permute-start.2
  13.0 2.7 %attend.4 = (bf16[2,2048,256]{2,1,0:T(8,128)(2,1)S(1)}, f32[2,144,2048]{2,1,0:T(8,128)S(1)}) custom-call(s32[1]{0:T(128)} %bitcast.1.refs_0_, f32[16,128]{1,0:T(8,128)S(1)} %get-tuple-element.31.refs_3_.refs_1_, bf16[4096,128]{1,0:T(8,128)(2,1)S(1)} %get-tuple-element.39.refs_2_, bf16[1040,128]{1,0:T(8,128)(2,1)S(1)} %get-tuple-element.40.refs_3_.refs_7_, ...), custom_call_target="tpu_custom_call" | custom-call | flops 1073741824 | bytes 8388608 | tf_op jit(solution)/shard_map/attend/pallas_call | solution.py:68
  15.7 0.0 collective-permute-done.3.refs_6_
  15.7 0.0 copy-done
  15.7 1.9 %inner_part.2 = (f32[2048,128]{1,0:T(8,128)S(1)}, bf16[2048,128]{1,0:T(8,128)(2,1)S(1)}, bf16[1040,128]{1,0:T(8,128)(2,1)S(1)}) custom-call(f32[256,128]{1,0:T(8,128)S(1)} %get-tuple-element.32.refs_2_.refs_0_.refs_3_, f32[16,128]{1,0:T(8,128)S(1)} %get-tuple-element.31.refs_3_.refs_1_, bf16[4096,128]{1,0:T(8,128)(2,1)S(1)} %bitcast.13, ...), custom_call_target="tpu_custom_call" | custom-call | flops 268435456 | bytes 6291456 | tf_op jit(solution)/shard_map/inner_part/pallas_call | solution.py:68
  17.6 0.7 %collective-permute-start.9 = (bf16[1040,128]{1,0:T(8,128)(2,1)S(1)}, bf16[1040,128]{1,0:T(8,128)(2,1)S(1)}, u32[]{:S(2)}, u32[]{:S(2)}) collective-permute-start(bf16[1040,128]{1,0:T(8,128)(2,1)S(1)} %get-tuple-element.43.refs_6_), channel_id=1, source_target_pairs={{8,16},{12,20},{16,24},{20,28},{9,17},{13,21},{17,25},{21,29},{10,... | collective-permute-start | bytes 798728 | tf_op jit(solution)/shard_map/ppermute | solution.py:722
  18.3 0.0 collective-permute-done.refs_2_
  18.3 0.0 collective-permute-done.1.refs_3_
  18.3 2.5 %collective-permute-done.2.refs_4_ = bf16[528,128]{1,0:T(8,128)(2,1)S(1)} collective-permute-done((bf16[528,128]{1,0:T(8,128)(2,1)S(1)}, bf16[528,128]{1,0:T(8,128)(2,1)S(1)}, u32[]{:S(2)}, u32[]{:S(2)}) %collective-permute-start.2) | collective-permute-done | bytes 135200 | tf_op jit(solution)/shard_map/ppermute | solution.py:722
  20.8 0.2 group_map.1
  21.1 0.6 collective-permute-start.8
  21.6 2.6 %collective-permute-start.4 = (bf16[528,128]{1,0:T(8,128)(2,1)S(1)}, bf16[528,128]{1,0:T(8,128)(2,1)S(1)}, u32[]{:S(2)}, u32[]{:S(2)}) collective-permute-start(bf16[528,128]{1,0:T(8,128)(2,1)S(1)} %get-tuple-element.44.refs_4_), channel_id=1, source_target_pairs={{0,16},{4,20},{8,24},{12,28},{16,0},{20,4},{24,8},{28,12},{1,17},{... | collective-permute-start | bytes 405512 | tf_op jit(solution)/shard_map/ppermute | solution.py:722
  24.2 0.3 collective-permute-start.13
  24.6 2.3 %attend.5.refs_5_.refs_2_ = f32[2,144,2048]{2,1,0:T(8,128)S(1)} custom-call(s32[1]{0:T(128)} %bitcast.1.refs_0_, bf16[2,2048,256]{2,1,0:T(8,128)(2,1)S(1)} %get-tuple-element.45.refs_1_, f32[2,144,2048]{2,1,0:T(8,128)S(1)} %get-tuple-element.41.refs_5_.refs_2_, bf16[1040,128]{1,0:T(8,128)(2,1)S(1)} %get-tuple-element.46.refs_3_, ...), custom_call_target="tpu_custom_call" | custom-call | flops 1073741824 | bytes 8388608 | tf_op jit(solution)/shard_map/attend/pallas_call | solution.py:68
  26.9 1.9 %inner_part.3 = (f32[2048,128]{1,0:T(8,128)S(1)}, bf16[2048,128]{1,0:T(8,128)(2,1)S(1)}) custom-call(f32[256,128]{1,0:T(8,128)S(1)} %get-tuple-element.32.refs_2_.refs_0_.refs_3_, f32[16,128]{1,0:T(8,128)S(1)} %get-tuple-element.31.refs_3_.refs_1_, bf16[4096,128]{1,0:T(8,128)(2,1)S(1)} %bitcast.14, bf16[4096,128]{1,0:T(8,128)(2,1)S(1)} %get-tuple-element.33.refs_4_.refs_3_, ...), custom_call_target="tpu_custom_call" | custom-call | flops 268435456 | bytes 6291456 | tf_op jit(solution)/shard_map/inner_part/pallas_call | solution.py:68
  28.8 1.7 %collective-permute-done.4.refs_5_ = bf16[528,128]{1,0:T(8,128)(2,1)S(1)} collective-permute-done((bf16[528,128]{1,0:T(8,128)(2,1)S(1)}, bf16[528,128]{1,0:T(8,128)(2,1)S(1)}, u32[]{:S(2)}, u32[]{:S(2)}) %collective-permute-start.4) | collective-permute-done | bytes 135200 | tf_op jit(solution)/shard_map/ppermute | solution.py:722
  30.5 0.3 prior_states.1
  30.8 7.2 %collective-permute-start.5 = (bf16[512,128]{1,0:T(8,128)(2,1)S(1)}, bf16[512,128]{1,0:T(8,128)(2,1)S(1)}, u32[]{:S(2)}, u32[]{:S(2)}) collective-permute-start(bf16[512,128]{1,0:T(8,128)(2,1)S(1)} %get-tuple-element.52), channel_id=1, source_target_pairs={{0,4},{4,0},{8,12},{12,8},{16,20},{20,16},{24,28},{28,24},{1,5},{5... | collective-permute-start | bytes 393224 | tf_op jit(solution)/shard_map/ppermute | solution.py:722
  38.0 2.6 %collective-permute-start.6 = (bf16[512,128]{1,0:T(8,128)(2,1)S(1)}, bf16[512,128]{1,0:T(8,128)(2,1)S(1)}, u32[]{:S(2)}, u32[]{:S(2)}) collective-permute-start(bf16[512,128]{1,0:T(8,128)(2,1)S(1)} %get-tuple-element.53), channel_id=1, source_target_pairs={{0,8},{4,12},{8,0},{12,4},{16,24},{20,28},{24,16},{28,20},{1,9},{5... | collective-permute-start | bytes 393224 | tf_op jit(solution)/shard_map/ppermute | solution.py:722
  40.6 0.0 collective-permute-done.9.refs_4_.refs_5_
  40.6 0.0 collective-permute-start.7
  40.6 0.0 collective-permute-done.8.refs_3_
  40.6 3.7 %attend.6.refs_12_.refs_0_.refs_2_ = f32[2,144,2048]{2,1,0:T(8,128)S(1)} custom-call(s32[1]{0:T(128)} %bitcast.1.refs_0_, bf16[2,2048,256]{2,1,0:T(8,128)(2,1)S(1)} %get-tuple-element.45.refs_1_, f32[2,144,2048]{2,1,0:T(8,128)S(1)} %attend.5.refs_5_.refs_2_, bf16[1040,128]{1,0:T(8,128)(2,1)S(1)} %collective-permute-done.8.refs_3_, ...), custom_call_target="tpu_custom_call" | custom-call | flops 2147483648 | bytes 8388608 | tf_op jit(solution)/shard_map/attend/pallas_call | solution.py:68
  44.3 0.0 collective-permute-done.5.refs_9_.refs_2_
  44.3 0.3 collective-permute-done.6.refs_10_.refs_3_
  44.5 1.9 %collective-permute-done.7.refs_11_.refs_4_ = bf16[512,128]{1,0:T(8,128)(2,1)S(1)} collective-permute-done((bf16[512,128]{1,0:T(8,128)(2,1)S(1)}, bf16[512,128]{1,0:T(8,128)(2,1)S(1)}, u32[]{:S(2)}, u32[]{:S(2)}) %collective-permute-start.7) | collective-permute-done | bytes 131104 | tf_op jit(solution)/shard_map/ppermute | solution.py:722
  46.5 1.0 %collective-permute-start.14 = (bf16[1040,128]{1,0:T(8,128)(2,1)S(1)}, bf16[1040,128]{1,0:T(8,128)(2,1)S(1)}, u32[]{:S(2)}, u32[]{:S(2)}) collective-permute-start(bf16[1040,128]{1,0:T(8,128)(2,1)S(1)} %pass_on.1), channel_id=1, source_target_pairs={{0,4},{4,0},{8,12},{12,8},{16,20},{20,16},{24,28},{28,24},{1,5},{5... | collective-permute-start | bytes 798728 | tf_op jit(solution)/shard_map/ppermute | solution.py:722
  47.5 1.6 %mix.1 = (f32[4096,128]{1,0:T(8,128)S(1)}, f32[8,256]{1,0:T(8,128)S(1)}) custom-call(s32[1]{0:T(128)} %bitcast.1.refs_0_, f32[16,128]{1,0:T(8,128)S(1)} %get-tuple-element.31.refs_3_.refs_1_, f32[8,128]{1,0:T(8,128)S(1)} %get-tuple-element.48.refs_5_.refs_2_, f32[256,128]{1,0:T(8,128)S(1)} %get-tuple-element.32.refs_2_.refs_0_.refs_3_, ...), custom_call_target="tpu_custom_call" | custom-call | flops 134217728 | bytes 5242880 | tf_op jit(solution)/shard_map/mix/pallas_call | solution.py:68
  49.1 0.0 copy-start.1
  49.1 0.0 copy-start.2
  49.1 0.0 collective-permute-start.12
  49.1 1.6 %collective-permute-start.11 = (f32[8,256]{1,0:T(8,128)S(1)}, f32[8,256]{1,0:T(8,128)S(1)}, u32[]{:S(2)}, u32[]{:S(2)}) collective-permute-start(f32[8,256]{1,0:T(8,128)S(1)} %get-tuple-element.56.refs_5_.refs_3_), channel_id=1, source_target_pairs={{0,2},{1,3},{2,0},{3,1},{4,6},{5,7},{6,4},{7,5},{8,10},{9,11},{10,... | collective-permute-start | bytes 24584 | tf_op jit(solution)/shard_map/ppermute | solution.py:813
  50.7 0.3 collective-permute-start.10
  51.0 0.0 collective-permute-done.13.refs_3_
  51.0 2.0 %collective-permute-done.14.refs_4_ = bf16[1040,128]{1,0:T(8,128)(2,1)S(1)} collective-permute-done((bf16[1040,128]{1,0:T(8,128)(2,1)S(1)}, bf16[1040,128]{1,0:T(8,128)(2,1)S(1)}, u32[]{:S(2)}, u32[]{:S(2)}) %collective-permute-start.14) | collective-permute-done | bytes 266272 | tf_op jit(solution)/shard_map/ppermute | solution.py:722
  52.9 4.6 %attend.7 = (bf16[4096,128]{1,0:T(8,128)(2,1)}, f32[8,128]{1,0:T(8,128)S(1)}) custom-call(s32[1]{0:T(128)} %bitcast.1.refs_0_, bf16[2,2048,256]{2,1,0:T(8,128)(2,1)S(1)} %get-tuple-element.45.refs_1_, f32[2,144,2048]{2,1,0:T(8,128)S(1)} %attend.6.refs_12_.refs_0_.refs_2_, bf16[1040,128]{1,0:T(8,128)(2,1)S(1)} %collective-permute-done.13.refs_3_, ...), custom_call_target="tpu_custom_call" | custom-call | flops 2147483648 | bytes 8388608 | tf_op jit(solution)/shard_map/attend/pallas_call | solution.py:68
  57.5 0.0 collective-permute-done.12.refs_6_
  57.5 0.0 collective-permute-done.11.refs_5_
  57.5 0.0 collective-permute-done.10.refs_4_
  57.5 0.0 copy-done.1
  57.6 0.0 copy-done.2
  57.6 1.6 %finish.1 = bf16[4096,128]{1,0:T(8,128)(2,1)} custom-call(f32[16,128]{1,0:T(8,128)S(1)} %copy-done.2, bf16[4096,128]{1,0:T(8,128)(2,1)S(1)} %bitcast.15, f32[4096,128]{1,0:T(8,128)S(1)} %get-tuple-element.55.refs_2_, f32[8,256]{1,0:T(8,128)S(1)} %get-tuple-element.56.refs_5_.refs_3_, f32[8,256]{1,0:T(8,128)S(1)} %collective-permute-done.10.refs_4_, ...), custom_call_target="tpu_custom_call" | custom-call | bytes 4194304 | tf_op jit(solution)/shard_map/finish/pallas_call | solution.py:68
  (1 shorter events, 0.0 us)
Async XLA Ops:
  2.6 13.1 %collective-permute-start.3 = (bf16[1040,128]{1,0:T(8,128)(2,1)S(1)}, bf16[1040,128]{1,0:T(8,128)(2,1)S(1)}, u32[]{:S(2)}, u32[]{:S(2)}) collective-permute-start(bf16[1040,128]{1,0:T(8,128)(2,1)S(1)} %get-tuple-element.40.refs_3_.refs_7_), channel_id=1, source_target_pairs={{0,8},{4,12},{8,16},{12,20},{16,24},{20,28},{24,0},{28,4},{1,9},{5... | collective-permute-start | bytes 798728 | tf_op jit(solution)/shard_map/ppermute | solution.py:722
  9.4 6.2 %copy-start = (bf16[256,16,128]{2,1,0:T(8,128)(2,1)S(1)}, bf16[256,16,128]{2,1,0:T(8,128)(2,1)}, u32[]{:S(2)}) copy-start(bf16[256,16,128]{2,1,0:T(8,128)(2,1)} %param.10) | copy-start | bytes 3145732
  9.5 8.9 %collective-permute-start = (bf16[528,128]{1,0:T(8,128)(2,1)S(1)}, bf16[528,128]{1,0:T(8,128)(2,1)S(1)}, u32[]{:S(2)}, u32[]{:S(2)}) collective-permute-start(bf16[528,128]{1,0:T(8,128)(2,1)S(1)} %get-tuple-element.36), channel_id=1, source_target_pairs={{0,4},{4,0},{8,12},{12,8},{16,20},{20,16},{24,28},{28,24},{1,5},{5... | collective-permute-start | bytes 405512 | tf_op jit(solution)/shard_map/ppermute | solution.py:722
  11.1 7.3 %collective-permute-start.1 = (bf16[528,128]{1,0:T(8,128)(2,1)S(1)}, bf16[528,128]{1,0:T(8,128)(2,1)S(1)}, u32[]{:S(2)}, u32[]{:S(2)}) collective-permute-start(bf16[528,128]{1,0:T(8,128)(2,1)S(1)} %get-tuple-element.37), channel_id=1, source_target_pairs={{0,8},{4,12},{8,0},{12,4},{16,24},{20,28},{24,16},{28,20},{1,9},{5... | collective-permute-start | bytes 405512 | tf_op jit(solution)/shard_map/ppermute | solution.py:722
  12.6 8.2 %collective-permute-start.2 = (bf16[528,128]{1,0:T(8,128)(2,1)S(1)}, bf16[528,128]{1,0:T(8,128)(2,1)S(1)}, u32[]{:S(2)}, u32[]{:S(2)}) collective-permute-start(bf16[528,128]{1,0:T(8,128)(2,1)S(1)} %get-tuple-element.38), channel_id=1, source_target_pairs={{0,12},{4,8},{8,4},{12,0},{16,28},{20,24},{24,20},{28,16},{1,13},{... | collective-permute-start | bytes 405512 | tf_op jit(solution)/shard_map/ppermute | solution.py:722
  17.6 22.9 %collective-permute-start.9 = (bf16[1040,128]{1,0:T(8,128)(2,1)S(1)}, bf16[1040,128]{1,0:T(8,128)(2,1)S(1)}, u32[]{:S(2)}, u32[]{:S(2)}) collective-permute-start(bf16[1040,128]{1,0:T(8,128)(2,1)S(1)} %get-tuple-element.43.refs_6_), channel_id=1, source_target_pairs={{8,16},{12,20},{16,24},{20,28},{9,17},{13,21},{17,25},{21,29},{10,... | collective-permute-start | bytes 798728 | tf_op jit(solution)/shard_map/ppermute | solution.py:722
  21.1 19.5 %collective-permute-start.8 = (bf16[1040,128]{1,0:T(8,128)(2,1)S(1)}, bf16[1040,128]{1,0:T(8,128)(2,1)S(1)}, u32[]{:S(2)}, u32[]{:S(2)}) collective-permute-start(bf16[1040,128]{1,0:T(8,128)(2,1)S(1)} %get-tuple-element.46.refs_3_), channel_id=1, source_target_pairs={{0,4},{4,0},{8,12},{12,8},{16,20},{20,16},{24,28},{28,24},{1,5},{5... | collective-permute-start | bytes 798728 | tf_op jit(solution)/shard_map/ppermute | solution.py:722
  21.6 8.9 %collective-permute-start.4 = (bf16[528,128]{1,0:T(8,128)(2,1)S(1)}, bf16[528,128]{1,0:T(8,128)(2,1)S(1)}, u32[]{:S(2)}, u32[]{:S(2)}) collective-permute-start(bf16[528,128]{1,0:T(8,128)(2,1)S(1)} %get-tuple-element.44.refs_4_), channel_id=1, source_target_pairs={{0,16},{4,20},{8,24},{12,28},{16,0},{20,4},{24,8},{28,12},{1,17},{... | collective-permute-start | bytes 405512 | tf_op jit(solution)/shard_map/ppermute | solution.py:722
  24.2 26.8 %collective-permute-start.13 = (bf16[1040,128]{1,0:T(8,128)(2,1)S(1)}, bf16[1040,128]{1,0:T(8,128)(2,1)S(1)}, u32[]{:S(2)}, u32[]{:S(2)}) collective-permute-start(bf16[1040,128]{1,0:T(8,128)(2,1)S(1)} %get-tuple-element.57), channel_id=1, source_target_pairs={{0,4},{4,24},{8,12},{12,8},{16,20},{20,16},{24,28},{28,0},{1,5},{5... | collective-permute-start | bytes 798728 | tf_op jit(solution)/shard_map/ppermute | solution.py:722
  30.8 13.5 %collective-permute-start.5 = (bf16[512,128]{1,0:T(8,128)(2,1)S(1)}, bf16[512,128]{1,0:T(8,128)(2,1)S(1)}, u32[]{:S(2)}, u32[]{:S(2)}) collective-permute-start(bf16[512,128]{1,0:T(8,128)(2,1)S(1)} %get-tuple-element.52), channel_id=1, source_target_pairs={{0,4},{4,0},{8,12},{12,8},{16,20},{20,16},{24,28},{28,24},{1,5},{5... | collective-permute-start | bytes 393224 | tf_op jit(solution)/shard_map/ppermute | solution.py:722
  38.0 6.5 %collective-permute-start.6 = (bf16[512,128]{1,0:T(8,128)(2,1)S(1)}, bf16[512,128]{1,0:T(8,128)(2,1)S(1)}, u32[]{:S(2)}, u32[]{:S(2)}) collective-permute-start(bf16[512,128]{1,0:T(8,128)(2,1)S(1)} %get-tuple-element.53), channel_id=1, source_target_pairs={{0,8},{4,12},{8,0},{12,4},{16,24},{20,28},{24,16},{28,20},{1,9},{5... | collective-permute-start | bytes 393224 | tf_op jit(solution)/shard_map/ppermute | solution.py:722
  40.6 5.9 %collective-permute-start.7 = (bf16[512,128]{1,0:T(8,128)(2,1)S(1)}, bf16[512,128]{1,0:T(8,128)(2,1)S(1)}, u32[]{:S(2)}, u32[]{:S(2)}) collective-permute-start(bf16[512,128]{1,0:T(8,128)(2,1)S(1)} %get-tuple-element.54), channel_id=1, source_target_pairs={{0,12},{4,8},{8,4},{12,0},{16,28},{20,24},{24,20},{28,16},{1,13},{... | collective-permute-start | bytes 393224 | tf_op jit(solution)/shard_map/ppermute | solution.py:722
  46.5 6.5 %collective-permute-start.14 = (bf16[1040,128]{1,0:T(8,128)(2,1)S(1)}, bf16[1040,128]{1,0:T(8,128)(2,1)S(1)}, u32[]{:S(2)}, u32[]{:S(2)}) collective-permute-start(bf16[1040,128]{1,0:T(8,128)(2,1)S(1)} %pass_on.1), channel_id=1, source_target_pairs={{0,4},{4,0},{8,12},{12,8},{16,20},{20,16},{24,28},{28,24},{1,5},{5... | collective-permute-start | bytes 798728 | tf_op jit(solution)/shard_map/ppermute | solution.py:722
  49.1 8.5 %copy-start.1 = (bf16[256,16,128]{2,1,0:T(8,128)(2,1)S(1)}, bf16[256,16,128]{2,1,0:T(8,128)(2,1)}, u32[]{:S(2)}) copy-start(bf16[256,16,128]{2,1,0:T(8,128)(2,1)} %param.13) | copy-start | bytes 3145732
  49.1 8.5 %copy-start.2 = (f32[16,128]{1,0:T(8,128)S(1)}, f32[16,128]{1,0:T(8,128)}, u32[]{:S(2)}) copy-start(f32[16,128]{1,0:T(8,128)} %refs_0_.1) | copy-start | bytes 24580
  49.1 8.4 %collective-permute-start.12 = (f32[8,256]{1,0:T(8,128)S(1)}, f32[8,256]{1,0:T(8,128)S(1)}, u32[]{:S(2)}, u32[]{:S(2)}) collective-permute-start(f32[8,256]{1,0:T(8,128)S(1)} %get-tuple-element.56.refs_5_.refs_3_), channel_id=1, source_target_pairs={{0,3},{1,2},{2,1},{3,0},{4,7},{5,6},{6,5},{7,4},{8,11},{9,10},{10,... | collective-permute-start | bytes 24584 | tf_op jit(solution)/shard_map/ppermute | solution.py:813
  49.1 8.4 %collective-permute-start.11 = (f32[8,256]{1,0:T(8,128)S(1)}, f32[8,256]{1,0:T(8,128)S(1)}, u32[]{:S(2)}, u32[]{:S(2)}) collective-permute-start(f32[8,256]{1,0:T(8,128)S(1)} %get-tuple-element.56.refs_5_.refs_3_), channel_id=1, source_target_pairs={{0,2},{1,3},{2,0},{3,1},{4,6},{5,7},{6,4},{7,5},{8,10},{9,11},{10,... | collective-permute-start | bytes 24584 | tf_op jit(solution)/shard_map/ppermute | solution.py:813
  50.7 6.9 %collective-permute-start.10 = (f32[8,256]{1,0:T(8,128)S(1)}, f32[8,256]{1,0:T(8,128)S(1)}, u32[]{:S(2)}, u32[]{:S(2)}) collective-permute-start(f32[8,256]{1,0:T(8,128)S(1)} %get-tuple-element.56.refs_5_.refs_3_), channel_id=1, source_target_pairs={{0,1},{1,0},{2,3},{3,2},{4,5},{5,4},{6,7},{7,6},{8,9},{9,8},{10,11... | collective-permute-start | bytes 24584 | tf_op jit(solution)/shard_map/ppermute | solution.py:813

commit v14 on v13

--- a/solution.py
+++ b/solution.py
@@ -96,8 +96,14 @@
     return rows >= cols
 
 
-def pass_on(x, after):
-    return call(lambda: None, "pass_on", [], [], (), after=after, relay=[x])[0]
+def pick_kernel(place_ref, even_ref, odd_ref, out_ref):
+    out_ref[...] = jnp.where(place_ref[0] % 2 == 0, even_ref[...], odd_ref[...])
+
+
+def pass_on(place, even, odd, x, after):
+    return call(
+        pick_kernel, "pass_on", [place], [even, odd], (sds(even.shape, BF16),), after=after, relay=[x]
+    )
 
 
 def fetch_kernel(tokens, heads, kv_here, start_ref, *refs):
@@ -740,12 +746,10 @@
     )
 
     forward = [(b, b + 2) for b in everyone]
-    hop = {b: b ^ 1 for b in everyone}
+    ahead = send(own_kv, forward)
+    far = None
     if window % 2:
-        for b in range(1, blocks - window, 2):
-            last = next(a for a in everyone if hop[a] == b + window)
-            hop[b], hop[last] = b + window, hop[b]
-    ahead = send(own_kv, forward)
+        far = send(own_kv, [(b, b + window) for b in range(1, blocks - window, 2)])
 
     size = quarter_rows(heads)
     others = range(1, GROUP_BLOCKS)
@@ -785,9 +789,11 @@
     if parts > 1:
         done, lane = inner_of(0, [done], [ahead])
     second = send(lane, [(b, b + 2) for b in range(2, blocks - 2)])
-    run, lane, own_copy = group_map(place, quarters, size, [done], [lane, own_kv])
+    run, lane, own_copy = group_map(
+        place, quarters, size, [done] if far is None else [done, far], [lane, own_kv]
+    )
     first_cross = send(lane, swap)
-    beside = (send(own_copy, list(hop.items())), (window if window % 2 else blocks, 1))
+    beside = send(own_copy, swap)
     stages = (blocks // GROUP_BLOCKS).bit_length() - 1
     before, done = None, run
     for stage in range(stages):
@@ -801,8 +807,8 @@
     *priors, prior_doc = prior_states(place, stages + 1, quarters, came, before, size, [done])
     priors = [priors[0]] + [send(priors[j], [(b, b ^ j) for b in everyone]) for j in others]
     done = more_attention([(first_cross, (2, 3)), (second, (4, 4))], False, [prior_doc])
-    lane = pass_on(second, [done, *priors])
-    rest = [beside, (send(lane, swap), (4, 5))]
+    slot, lane = pass_on(place, beside if far is None else far, beside, second, [done, *priors])
+    rest = [(slot, (blocks if far is None else window, 1)), (send(lane, swap), (4, 5))]
     for back in range(3, window // 2 + 1):
         lane = send(lane, forward)
         rest.append((lane, (2 * back, 2 * back)))

time: 59.5 us -> 56.6 us (0.951); the launches traced: 59.4 us -> 55.5 us
  waiting for transfers between devices: 8.41 us -> 2.54 us
  starting transfers between devices: 23.5 us -> 25.5 us
    ppermute x12 -> x13, waiting for transfers between devices: 8.4 us -> 2.53 us  [send(): return lax.ppermute(x, 'seq', [(a, b % blocks) for a, b in pairs])]
    ppermute x12 -> x13, starting transfers between devices: 21.6 us -> 23.6 us  [send(): return lax.ppermute(x, 'seq', [(a, b % blocks) for a, b in pairs])]
  transfers between devices with their start and end apart: 15 -> 16, of which waited for: 5 -> 4; matrix products, arithmetic and copies ran while one was open for 0% -> 0% of each run, Pallas kernels for 38% -> 41%
where the time goes in v14:
time: 56.6 us; the launch traced here: 55.5 us
  Pallas kernels  26.5 us (47%)
  starting transfers between devices  25.5 us (45%)
  waiting for transfers between devices  2.54 us (4%)
  between operations  1.01 us (2%)
    pallas_call x13, Pallas kernels, call(): pl.pallas_call(run, out_shape=outs, in_specs=[SMEM] * len(scalars) + [HBM...  26.5 us
    ppermute x13, starting transfers between devices, send(): return lax.ppermute(x, 'seq', [(a, b % blocks) for a, b in pairs])  23.6 us
    ppermute x13, waiting for transfers between devices, send(): return lax.ppermute(x, 'seq', [(a, b % blocks) for a, b in pairs])  2.53 us
    ppermute x3, starting transfers between devices, body(): lax.ppermute(squares, 'tp', [(t, t ^ other) for t in range(tensor)])  1.89 us
  transfers between devices with their start and end apart: 16, of which 4 were waited for; matrix products, arithmetic and copies ran while one was open for 0% of the time, Pallas kernels for 41%

profile of v14, /device:TPU:0, one launch (start us, length us, event | category | flops | bytes accessed | tf_op | source)
XLA Modules:
  0.0 55.5 jit_solution(13629738933859906268)
XLA Ops:
  0.6 1.9 %fetch.1 = (bf16[1040,128]{1,0:T(8,128)(2,1)S(1)}, f32[16,128]{1,0:T(8,128)S(1)}, f32[256,128]{1,0:T(8,128)S(1)}, bf16[4096,128]{1,0:T(8,128)(2,1)S(1)}, bf16[4096,128]{1,0:T(8,128)(2,1)S(1)}) custom-call(s32[1]{0:T(128)} %bitcast.2.refs_0_, s32[2,128]{1,0:T(2,128)} %bitcast.23, f32[16,256]{1,0:T(8,128)} %bitcast.22, bf16[2048,128]{1,0:T(8,128)(2,1)} %bitcast.20, ...), custom_call_target="tpu_custom_call" | custom-call | bytes 3145728 | tf_op jit(solution)/shard_map/fetch/pallas_call | solution.py:68
  2.6 3.1 %collective-permute-start.3 = (bf16[1040,128]{1,0:T(8,128)(2,1)S(1)}, bf16[1040,128]{1,0:T(8,128)(2,1)S(1)}, u32[]{:S(2)}, u32[]{:S(2)}) collective-permute-start(bf16[1040,128]{1,0:T(8,128)(2,1)S(1)} %get-tuple-element.42.refs_3_.refs_8_), channel_id=1, source_target_pairs={{0,8},{4,12},{8,16},{12,20},{16,24},{20,28},{24,0},{28,4},{1,9},{5... | collective-permute-start | bytes 798728 | tf_op jit(solution)/shard_map/ppermute | solution.py:728
  5.7 0.7 %collective-permute-start.4 = (bf16[1040,128]{1,0:T(8,128)(2,1)S(1)}, bf16[1040,128]{1,0:T(8,128)(2,1)S(1)}, u32[]{:S(2)}, u32[]{:S(2)}) collective-permute-start(bf16[1040,128]{1,0:T(8,128)(2,1)S(1)} %get-tuple-element.42.refs_3_.refs_8_), channel_id=1, source_target_pairs={{4,24},{5,25},{6,26},{7,27}} | collective-permute-start | bytes 798728 | tf_op jit(solution)/shard_map/ppermute | solution.py:728
  6.4 3.8 %block_state.1 = (bf16[528,128]{1,0:T(8,128)(2,1)S(1)}, bf16[528,128]{1,0:T(8,128)(2,1)S(1)}, bf16[528,128]{1,0:T(8,128)(2,1)S(1)}, bf16[528,128]{1,0:T(8,128)(2,1)S(1)}, bf16[4096,128]{1,0:T(8,128)(2,1)S(1)}) custom-call(s32[1]{0:T(128)} %bitcast.1.refs_0_, bf16[4096,128]{1,0:T(8,128)(2,1)} %bitcast.19, ...), custom_call_target="tpu_custom_call" | custom-call | flops 134217728 | bytes 5242880 | tf_op jit(solution)/shard_map/block_state/pallas_call | solution.py:68
  10.1 0.0 copy-start
  10.1 4.8 %collective-permute-start = (bf16[528,128]{1,0:T(8,128)(2,1)S(1)}, bf16[528,128]{1,0:T(8,128)(2,1)S(1)}, u32[]{:S(2)}, u32[]{:S(2)}) collective-permute-start(bf16[528,128]{1,0:T(8,128)(2,1)S(1)} %get-tuple-element.38), channel_id=1, source_target_pairs={{0,4},{4,0},{8,12},{12,8},{16,20},{20,16},{24,28},{28,24},{1,5},{5... | collective-permute-start | bytes 405512 | tf_op jit(solution)/shard_map/ppermute | solution.py:728
  15.0 0.0 collective-permute-start.1
  15.0 1.5 %collective-permute-start.2 = (bf16[528,128]{1,0:T(8,128)(2,1)S(1)}, bf16[528,128]{1,0:T(8,128)(2,1)S(1)}, u32[]{:S(2)}, u32[]{:S(2)}) collective-permute-start(bf16[528,128]{1,0:T(8,128)(2,1)S(1)} %get-tuple-element.40), channel_id=1, source_target_pairs={{0,12},{4,8},{8,4},{12,0},{16,28},{20,24},{24,20},{28,16},{1,13},{... | collective-permute-start | bytes 405512 | tf_op jit(solution)/shard_map/ppermute | solution.py:728
  16.5 2.6 %attend.4 = (bf16[2,2048,256]{2,1,0:T(8,128)(2,1)S(1)}, f32[2,144,2048]{2,1,0:T(8,128)S(1)}) custom-call(s32[1]{0:T(128)} %bitcast.1.refs_0_, f32[16,128]{1,0:T(8,128)S(1)} %get-tuple-element.33.refs_3_.refs_1_, bf16[4096,128]{1,0:T(8,128)(2,1)S(1)} %get-tuple-element.41.refs_2_, bf16[1040,128]{1,0:T(8,128)(2,1)S(1)} %get-tuple-element.42.refs_3_.refs_8_, ...), custom_call_target="tpu_custom_call" | custom-call | flops 1073741824 | bytes 8388608 | tf_op jit(solution)/shard_map/attend/pallas_call | solution.py:68
  19.2 0.0 collective-permute-done.3.refs_6_
  19.2 0.0 copy-done
  19.2 1.9 %inner_part.2 = (f32[2048,128]{1,0:T(8,128)S(1)}, bf16[2048,128]{1,0:T(8,128)(2,1)S(1)}, bf16[1040,128]{1,0:T(8,128)(2,1)S(1)}) custom-call(f32[256,128]{1,0:T(8,128)S(1)} %get-tuple-element.34.refs_2_.refs_0_.refs_3_, f32[16,128]{1,0:T(8,128)S(1)} %get-tuple-element.33.refs_3_.refs_1_, bf16[4096,128]{1,0:T(8,128)(2,1)S(1)} %bitcast.13, ...), custom_call_target="tpu_custom_call" | custom-call | flops 268435456 | bytes 6291456 | tf_op jit(solution)/shard_map/inner_part/pallas_call | solution.py:68
  21.1 0.9 %collective-permute-start.10 = (bf16[1040,128]{1,0:T(8,128)(2,1)S(1)}, bf16[1040,128]{1,0:T(8,128)(2,1)S(1)}, u32[]{:S(2)}, u32[]{:S(2)}) collective-permute-start(bf16[1040,128]{1,0:T(8,128)(2,1)S(1)} %get-tuple-element.45.refs_7_), channel_id=1, source_target_pairs={{8,16},{12,20},{16,24},{20,28},{9,17},{13,21},{17,25},{21,29},{10,... | collective-permute-start | bytes 798728 | tf_op jit(solution)/shard_map/ppermute | solution.py:728
  22.0 0.0 collective-permute-done.refs_2_
  22.0 0.0 collective-permute-done.1.refs_3_
  22.0 0.4 collective-permute-done.2.refs_4_
  22.4 0.0 collective-permute-done.4.refs_6_.refs_1_
  22.4 0.2 group_map.1
  22.6 2.0 %collective-permute-start.9 = (bf16[1040,128]{1,0:T(8,128)(2,1)S(1)}, bf16[1040,128]{1,0:T(8,128)(2,1)S(1)}, u32[]{:S(2)}, u32[]{:S(2)}) collective-permute-start(bf16[1040,128]{1,0:T(8,128)(2,1)S(1)} %get-tuple-element.48.refs_3_), channel_id=1, source_target_pairs={{0,4},{4,0},{8,12},{12,8},{16,20},{20,16},{24,28},{28,24},{1,5},{5... | collective-permute-start | bytes 798728 | tf_op jit(solution)/shard_map/ppermute | solution.py:728
  24.7 3.9 %collective-permute-start.5 = (bf16[528,128]{1,0:T(8,128)(2,1)S(1)}, bf16[528,128]{1,0:T(8,128)(2,1)S(1)}, u32[]{:S(2)}, u32[]{:S(2)}) collective-permute-start(bf16[528,128]{1,0:T(8,128)(2,1)S(1)} %get-tuple-element.46.refs_4_), channel_id=1, source_target_pairs={{0,16},{4,20},{8,24},{12,28},{16,0},{20,4},{24,8},{28,12},{1,17},{... | collective-permute-start | bytes 405512 | tf_op jit(solution)/shard_map/ppermute | solution.py:728
  28.6 0.1 collective-permute-start.14
  28.7 2.3 %attend.5.refs_5_.refs_2_ = f32[2,144,2048]{2,1,0:T(8,128)S(1)} custom-call(s32[1]{0:T(128)} %bitcast.1.refs_0_, bf16[2,2048,256]{2,1,0:T(8,128)(2,1)S(1)} %get-tuple-element.47.refs_1_, f32[2,144,2048]{2,1,0:T(8,128)S(1)} %get-tuple-element.43.refs_5_.refs_2_, bf16[1040,128]{1,0:T(8,128)(2,1)S(1)} %get-tuple-element.48.refs_3_, ...), custom_call_target="tpu_custom_call" | custom-call | flops 1073741824 | bytes 8388608 | tf_op jit(solution)/shard_map/attend/pallas_call | solution.py:68
  31.0 1.9 %inner_part.3 = (f32[2048,128]{1,0:T(8,128)S(1)}, bf16[2048,128]{1,0:T(8,128)(2,1)S(1)}) custom-call(f32[256,128]{1,0:T(8,128)S(1)} %get-tuple-element.34.refs_2_.refs_0_.refs_3_, f32[16,128]{1,0:T(8,128)S(1)} %get-tuple-element.33.refs_3_.refs_1_, bf16[4096,128]{1,0:T(8,128)(2,1)S(1)} %bitcast.14, bf16[4096,128]{1,0:T(8,128)(2,1)S(1)} %get-tuple-element.35.refs_4_.refs_3_, ...), custom_call_target="tpu_custom_call" | custom-call | flops 268435456 | bytes 6291456 | tf_op jit(solution)/shard_map/inner_part/pallas_call | solution.py:68
  32.9 0.3 collective-permute-done.5.refs_5_
  33.2 0.3 prior_states.1
  33.5 1.7 %collective-permute-start.6 = (bf16[512,128]{1,0:T(8,128)(2,1)S(1)}, bf16[512,128]{1,0:T(8,128)(2,1)S(1)}, u32[]{:S(2)}, u32[]{:S(2)}) collective-permute-start(bf16[512,128]{1,0:T(8,128)(2,1)S(1)} %get-tuple-element.54), channel_id=1, source_target_pairs={{0,4},{4,0},{8,12},{12,8},{16,20},{20,16},{24,28},{28,24},{1,5},{5... | collective-permute-start | bytes 393224 | tf_op jit(solution)/shard_map/ppermute | solution.py:728
  35.2 1.4 %collective-permute-start.7 = (bf16[512,128]{1,0:T(8,128)(2,1)S(1)}, bf16[512,128]{1,0:T(8,128)(2,1)S(1)}, u32[]{:S(2)}, u32[]{:S(2)}) collective-permute-start(bf16[512,128]{1,0:T(8,128)(2,1)S(1)} %get-tuple-element.55), channel_id=1, source_target_pairs={{0,8},{4,12},{8,0},{12,4},{16,24},{20,28},{24,16},{28,20},{1,9},{5... | collective-permute-start | bytes 393224 | tf_op jit(solution)/shard_map/ppermute | solution.py:728
  36.6 0.0 collective-permute-done.10.refs_4_.refs_8_
  36.6 1.4 %collective-permute-start.8 = (bf16[512,128]{1,0:T(8,128)(2,1)S(1)}, bf16[512,128]{1,0:T(8,128)(2,1)S(1)}, u32[]{:S(2)}, u32[]{:S(2)}) collective-permute-start(bf16[512,128]{1,0:T(8,128)(2,1)S(1)} %get-tuple-element.56), channel_id=1, source_target_pairs={{0,12},{4,8},{8,4},{12,0},{16,28},{20,24},{24,20},{28,16},{1,13},{... | collective-permute-start | bytes 393224 | tf_op jit(solution)/shard_map/ppermute | solution.py:728
  38.0 0.0 collective-permute-done.9.refs_3_
  38.0 3.6 %attend.6.refs_12_.refs_3_.refs_2_ = f32[2,144,2048]{2,1,0:T(8,128)S(1)} custom-call(s32[1]{0:T(128)} %bitcast.1.refs_0_, bf16[2,2048,256]{2,1,0:T(8,128)(2,1)S(1)} %get-tuple-element.47.refs_1_, f32[2,144,2048]{2,1,0:T(8,128)S(1)} %attend.5.refs_5_.refs_2_, bf16[1040,128]{1,0:T(8,128)(2,1)S(1)} %collective-permute-done.9.refs_3_, ...), custom_call_target="tpu_custom_call" | custom-call | flops 2147483648 | bytes 8388608 | tf_op jit(solution)/shard_map/attend/pallas_call | solution.py:68
  41.6 0.0 collective-permute-done.6.refs_9_.refs_5_
  41.6 0.0 collective-permute-done.7.refs_10_.refs_6_
  41.7 0.9 %collective-permute-done.8.refs_11_.refs_7_ = bf16[512,128]{1,0:T(8,128)(2,1)S(1)} collective-permute-done((bf16[512,128]{1,0:T(8,128)(2,1)S(1)}, bf16[512,128]{1,0:T(8,128)(2,1)S(1)}, u32[]{:S(2)}, u32[]{:S(2)}) %collective-permute-start.8) | collective-permute-done | bytes 131104 | tf_op jit(solution)/shard_map/ppermute | solution.py:728
  42.5 0.0 collective-permute-done.14.refs_2_
  42.5 0.1 pass_on.1
  42.6 2.1 %collective-permute-start.15 = (bf16[1040,128]{1,0:T(8,128)(2,1)S(1)}, bf16[1040,128]{1,0:T(8,128)(2,1)S(1)}, u32[]{:S(2)}, u32[]{:S(2)}) collective-permute-start(bf16[1040,128]{1,0:T(8,128)(2,1)S(1)} %get-tuple-element.61), channel_id=1, source_target_pairs={{0,4},{4,0},{8,12},{12,8},{16,20},{20,16},{24,28},{28,24},{1,5},{5... | collective-permute-start | bytes 798728 | tf_op jit(solution)/shard_map/ppermute | solution.py:728
  44.7 1.6 %mix.1 = (f32[4096,128]{1,0:T(8,128)S(1)}, f32[8,256]{1,0:T(8,128)S(1)}) custom-call(s32[1]{0:T(128)} %bitcast.1.refs_0_, f32[16,128]{1,0:T(8,128)S(1)} %get-tuple-element.33.refs_3_.refs_1_, f32[8,128]{1,0:T(8,128)S(1)} %get-tuple-element.50.refs_5_.refs_2_, f32[256,128]{1,0:T(8,128)S(1)} %get-tuple-element.34.refs_2_.refs_0_.refs_3_, ...), custom_call_target="tpu_custom_call" | custom-call | flops 134217728 | bytes 5242880 | tf_op jit(solution)/shard_map/mix/pallas_call | solution.py:68
  46.3 0.0 collective-permute-start.13
  46.3 1.6 %collective-permute-start.12 = (f32[8,256]{1,0:T(8,128)S(1)}, f32[8,256]{1,0:T(8,128)S(1)}, u32[]{:S(2)}, u32[]{:S(2)}) collective-permute-start(f32[8,256]{1,0:T(8,128)S(1)} %get-tuple-element.58.refs_5_.refs_3_), channel_id=1, source_target_pairs={{0,2},{1,3},{2,0},{3,1},{4,6},{5,7},{6,4},{7,5},{8,10},{9,11},{10,... | collective-permute-start | bytes 24584 | tf_op jit(solution)/shard_map/ppermute | solution.py:819
  47.8 0.3 collective-permute-start.11
  48.2 0.9 %collective-permute-done.15.refs_4_ = bf16[1040,128]{1,0:T(8,128)(2,1)S(1)} collective-permute-done((bf16[1040,128]{1,0:T(8,128)(2,1)S(1)}, bf16[1040,128]{1,0:T(8,128)(2,1)S(1)}, u32[]{:S(2)}, u32[]{:S(2)}) %collective-permute-start.15) | collective-permute-done | bytes 266272 | tf_op jit(solution)/shard_map/ppermute | solution.py:728
  49.1 4.6 %attend.7 = (bf16[4096,128]{1,0:T(8,128)(2,1)}, f32[8,128]{1,0:T(8,128)S(1)}) custom-call(s32[1]{0:T(128)} %bitcast.1.refs_0_, bf16[2,2048,256]{2,1,0:T(8,128)(2,1)S(1)} %get-tuple-element.47.refs_1_, f32[2,144,2048]{2,1,0:T(8,128)S(1)} %attend.6.refs_12_.refs_3_.refs_2_, bf16[1040,128]{1,0:T(8,128)(2,1)S(1)} %get-tuple-element.60.refs_3_, ...), custom_call_target="tpu_custom_call" | custom-call | flops 2147483648 | bytes 8388608 | tf_op jit(solution)/shard_map/attend/pallas_call | solution.py:68
  53.7 0.0 collective-permute-done.13.refs_6_
  53.7 0.0 collective-permute-done.12.refs_5_
  53.7 0.0 collective-permute-done.11.refs_4_
  53.7 0.0 copy-done.1
  53.7 1.6 %finish.1 = bf16[4096,128]{1,0:T(8,128)(2,1)} custom-call(f32[16,128]{1,0:T(8,128)S(1)} %copy-done.2, bf16[4096,128]{1,0:T(8,128)(2,1)S(1)} %bitcast.15, f32[4096,128]{1,0:T(8,128)S(1)} %get-tuple-element.57.refs_2_, f32[8,256]{1,0:T(8,128)S(1)} %get-tuple-element.58.refs_5_.refs_3_, f32[8,256]{1,0:T(8,128)S(1)} %collective-permute-done.11.refs_4_, ...), custom_call_target="tpu_custom_call" | custom-call | bytes 4194304 | tf_op jit(solution)/shard_map/finish/pallas_call | solution.py:68
  (3 shorter events, 0.0 us)
Async XLA Ops:
  2.6 16.6 %collective-permute-start.3 = (bf16[1040,128]{1,0:T(8,128)(2,1)S(1)}, bf16[1040,128]{1,0:T(8,128)(2,1)S(1)}, u32[]{:S(2)}, u32[]{:S(2)}) collective-permute-start(bf16[1040,128]{1,0:T(8,128)(2,1)S(1)} %get-tuple-element.42.refs_3_.refs_8_), channel_id=1, source_target_pairs={{0,8},{4,12},{8,16},{12,20},{16,24},{20,28},{24,0},{28,4},{1,9},{5... | collective-permute-start | bytes 798728 | tf_op jit(solution)/shard_map/ppermute | solution.py:728
  5.7 16.7 %collective-permute-start.4 = (bf16[1040,128]{1,0:T(8,128)(2,1)S(1)}, bf16[1040,128]{1,0:T(8,128)(2,1)S(1)}, u32[]{:S(2)}, u32[]{:S(2)}) collective-permute-start(bf16[1040,128]{1,0:T(8,128)(2,1)S(1)} %get-tuple-element.42.refs_3_.refs_8_), channel_id=1, source_target_pairs={{4,24},{5,25},{6,26},{7,27}} | collective-permute-start | bytes 798728 | tf_op jit(solution)/shard_map/ppermute | solution.py:728
  10.1 9.0 %copy-start = (bf16[256,16,128]{2,1,0:T(8,128)(2,1)S(1)}, bf16[256,16,128]{2,1,0:T(8,128)(2,1)}, u32[]{:S(2)}) copy-start(bf16[256,16,128]{2,1,0:T(8,128)(2,1)} %param.10) | copy-start | bytes 3145732
  10.1 11.8 %collective-permute-start = (bf16[528,128]{1,0:T(8,128)(2,1)S(1)}, bf16[528,128]{1,0:T(8,128)(2,1)S(1)}, u32[]{:S(2)}, u32[]{:S(2)}) collective-permute-start(bf16[528,128]{1,0:T(8,128)(2,1)S(1)} %get-tuple-element.38), channel_id=1, source_target_pairs={{0,4},{4,0},{8,12},{12,8},{16,20},{20,16},{24,28},{28,24},{1,5},{5... | collective-permute-start | bytes 405512 | tf_op jit(solution)/shard_map/ppermute | solution.py:728
  15.0 7.0 %collective-permute-start.1 = (bf16[528,128]{1,0:T(8,128)(2,1)S(1)}, bf16[528,128]{1,0:T(8,128)(2,1)S(1)}, u32[]{:S(2)}, u32[]{:S(2)}) collective-permute-start(bf16[528,128]{1,0:T(8,128)(2,1)S(1)} %get-tuple-element.39), channel_id=1, source_target_pairs={{0,8},{4,12},{8,0},{12,4},{16,24},{20,28},{24,16},{28,20},{1,9},{5... | collective-permute-start | bytes 405512 | tf_op jit(solution)/shard_map/ppermute | solution.py:728
  15.0 7.4 %collective-permute-start.2 = (bf16[528,128]{1,0:T(8,128)(2,1)S(1)}, bf16[528,128]{1,0:T(8,128)(2,1)S(1)}, u32[]{:S(2)}, u32[]{:S(2)}) collective-permute-start(bf16[528,128]{1,0:T(8,128)(2,1)S(1)} %get-tuple-element.40), channel_id=1, source_target_pairs={{0,12},{4,8},{8,4},{12,0},{16,28},{20,24},{24,20},{28,16},{1,13},{... | collective-permute-start | bytes 405512 | tf_op jit(solution)/shard_map/ppermute | solution.py:728
  21.1 15.5 %collective-permute-start.10 = (bf16[1040,128]{1,0:T(8,128)(2,1)S(1)}, bf16[1040,128]{1,0:T(8,128)(2,1)S(1)}, u32[]{:S(2)}, u32[]{:S(2)}) collective-permute-start(bf16[1040,128]{1,0:T(8,128)(2,1)S(1)} %get-tuple-element.45.refs_7_), channel_id=1, source_target_pairs={{8,16},{12,20},{16,24},{20,28},{9,17},{13,21},{17,25},{21,29},{10,... | collective-permute-start | bytes 798728 | tf_op jit(solution)/shard_map/ppermute | solution.py:728
  22.6 15.4 %collective-permute-start.9 = (bf16[1040,128]{1,0:T(8,128)(2,1)S(1)}, bf16[1040,128]{1,0:T(8,128)(2,1)S(1)}, u32[]{:S(2)}, u32[]{:S(2)}) collective-permute-start(bf16[1040,128]{1,0:T(8,128)(2,1)S(1)} %get-tuple-element.48.refs_3_), channel_id=1, source_target_pairs={{0,4},{4,0},{8,12},{12,8},{16,20},{20,16},{24,28},{28,24},{1,5},{5... | collective-permute-start | bytes 798728 | tf_op jit(solution)/shard_map/ppermute | solution.py:728
  24.7 8.5 %collective-permute-start.5 = (bf16[528,128]{1,0:T(8,128)(2,1)S(1)}, bf16[528,128]{1,0:T(8,128)(2,1)S(1)}, u32[]{:S(2)}, u32[]{:S(2)}) collective-permute-start(bf16[528,128]{1,0:T(8,128)(2,1)S(1)} %get-tuple-element.46.refs_4_), channel_id=1, source_target_pairs={{0,16},{4,20},{8,24},{12,28},{16,0},{20,4},{24,8},{28,12},{1,17},{... | collective-permute-start | bytes 405512 | tf_op jit(solution)/shard_map/ppermute | solution.py:728
  28.6 13.9 %collective-permute-start.14 = (bf16[1040,128]{1,0:T(8,128)(2,1)S(1)}, bf16[1040,128]{1,0:T(8,128)(2,1)S(1)}, u32[]{:S(2)}, u32[]{:S(2)}) collective-permute-start(bf16[1040,128]{1,0:T(8,128)(2,1)S(1)} %get-tuple-element.59), channel_id=1, source_target_pairs={{0,4},{4,0},{8,12},{12,8},{16,20},{20,16},{24,28},{28,24},{1,5},{5... | collective-permute-start | bytes 798728 | tf_op jit(solution)/shard_map/ppermute | solution.py:728
  33.5 8.2 %collective-permute-start.6 = (bf16[512,128]{1,0:T(8,128)(2,1)S(1)}, bf16[512,128]{1,0:T(8,128)(2,1)S(1)}, u32[]{:S(2)}, u32[]{:S(2)}) collective-permute-start(bf16[512,128]{1,0:T(8,128)(2,1)S(1)} %get-tuple-element.54), channel_id=1, source_target_pairs={{0,4},{4,0},{8,12},{12,8},{16,20},{20,16},{24,28},{28,24},{1,5},{5... | collective-permute-start | bytes 393224 | tf_op jit(solution)/shard_map/ppermute | solution.py:728
  35.2 6.5 %collective-permute-start.7 = (bf16[512,128]{1,0:T(8,128)(2,1)S(1)}, bf16[512,128]{1,0:T(8,128)(2,1)S(1)}, u32[]{:S(2)}, u32[]{:S(2)}) collective-permute-start(bf16[512,128]{1,0:T(8,128)(2,1)S(1)} %get-tuple-element.55), channel_id=1, source_target_pairs={{0,8},{4,12},{8,0},{12,4},{16,24},{20,28},{24,16},{28,20},{1,9},{5... | collective-permute-start | bytes 393224 | tf_op jit(solution)/shard_map/ppermute | solution.py:728
  36.6 5.9 %collective-permute-start.8 = (bf16[512,128]{1,0:T(8,128)(2,1)S(1)}, bf16[512,128]{1,0:T(8,128)(2,1)S(1)}, u32[]{:S(2)}, u32[]{:S(2)}) collective-permute-start(bf16[512,128]{1,0:T(8,128)(2,1)S(1)} %get-tuple-element.56), channel_id=1, source_target_pairs={{0,12},{4,8},{8,4},{12,0},{16,28},{20,24},{24,20},{28,16},{1,13},{... | collective-permute-start | bytes 393224 | tf_op jit(solution)/shard_map/ppermute | solution.py:728
  42.6 6.5 %collective-permute-start.15 = (bf16[1040,128]{1,0:T(8,128)(2,1)S(1)}, bf16[1040,128]{1,0:T(8,128)(2,1)S(1)}, u32[]{:S(2)}, u32[]{:S(2)}) collective-permute-start(bf16[1040,128]{1,0:T(8,128)(2,1)S(1)} %get-tuple-element.61), channel_id=1, source_target_pairs={{0,4},{4,0},{8,12},{12,8},{16,20},{20,16},{24,28},{28,24},{1,5},{5... | collective-permute-start | bytes 798728 | tf_op jit(solution)/shard_map/ppermute | solution.py:728
  46.3 7.4 %collective-permute-start.13 = (f32[8,256]{1,0:T(8,128)S(1)}, f32[8,256]{1,0:T(8,128)S(1)}, u32[]{:S(2)}, u32[]{:S(2)}) collective-permute-start(f32[8,256]{1,0:T(8,128)S(1)} %get-tuple-element.58.refs_5_.refs_3_), channel_id=1, source_target_pairs={{0,3},{1,2},{2,1},{3,0},{4,7},{5,6},{6,5},{7,4},{8,11},{9,10},{10,... | collective-permute-start | bytes 24584 | tf_op jit(solution)/shard_map/ppermute | solution.py:819
  46.3 7.4 %collective-permute-start.12 = (f32[8,256]{1,0:T(8,128)S(1)}, f32[8,256]{1,0:T(8,128)S(1)}, u32[]{:S(2)}, u32[]{:S(2)}) collective-permute-start(f32[8,256]{1,0:T(8,128)S(1)} %get-tuple-element.58.refs_5_.refs_3_), channel_id=1, source_target_pairs={{0,2},{1,3},{2,0},{3,1},{4,6},{5,7},{6,4},{7,5},{8,10},{9,11},{10,... | collective-permute-start | bytes 24584 | tf_op jit(solution)/shard_map/ppermute | solution.py:819
  47.8 5.9 %collective-permute-start.11 = (f32[8,256]{1,0:T(8,128)S(1)}, f32[8,256]{1,0:T(8,128)S(1)}, u32[]{:S(2)}, u32[]{:S(2)}) collective-permute-start(f32[8,256]{1,0:T(8,128)S(1)} %get-tuple-element.58.refs_5_.refs_3_), channel_id=1, source_target_pairs={{0,1},{1,0},{2,3},{3,2},{4,5},{5,4},{6,7},{7,6},{8,9},{9,8},{10,11... | collective-permute-start | bytes 24584 | tf_op jit(solution)/shard_map/ppermute | solution.py:819
  49.1 4.6 %copy-start.1 = (bf16[256,16,128]{2,1,0:T(8,128)(2,1)S(1)}, bf16[256,16,128]{2,1,0:T(8,128)(2,1)}, u32[]{:S(2)}) copy-start(bf16[256,16,128]{2,1,0:T(8,128)(2,1)} %param.13) | copy-start | bytes 3145732
  49.1 4.6 %copy-start.2 = (f32[16,128]{1,0:T(8,128)S(1)}, f32[16,128]{1,0:T(8,128)}, u32[]{:S(2)}) copy-start(f32[16,128]{1,0:T(8,128)} %refs_0_.1) | copy-start | bytes 24580

commit v15 on v14

--- a/solution.py
+++ b/solution.py
@@ -100,10 +100,14 @@
     out_ref[...] = jnp.where(place_ref[0] % 2 == 0, even_ref[...], odd_ref[...])
 
 
-def pass_on(place, even, odd, x, after):
-    return call(
-        pick_kernel, "pass_on", [place], [even, odd], (sds(even.shape, BF16),), after=after, relay=[x]
-    )
+def pick(place, even, odd, x, after):
+    return call(
+        pick_kernel, "pick", [place], [even, odd], (sds(even.shape, BF16),), after=after, relay=[x]
+    )
+
+
+def pass_on(x, after):
+    return call(lambda: None, "pass_on", [], [], (), after=after, relay=[x])[0]
 
 
 def fetch_kernel(tokens, heads, kv_here, start_ref, *refs):
@@ -301,17 +305,16 @@
     out_ref[size : size + INFO, :] = info_rows((*in_parts(gain), maps[0][1], maps[-1][2]))
 
 
-def group_map(place, quarters, size, after, relay):
+def group_map(place, quarters, size, after):
     return call(
         functools.partial(group_kernel, size),
         "group_map",
         [place],
         quarters,
-        (sds((size + INFO, LANES), BF16),),
+        sds((size + INFO, LANES), BF16),
         scratch=[pltpu.VMEM((GROUP_BLOCKS, size + INFO, LANES), BF16)],
         estimate=cost(8 * size * LANES, 10 * size * LANES * 2),
         after=after,
-        relay=relay,
     )
 
 
@@ -517,7 +520,8 @@
 
 
 def finish_kernel(tokens, heads, sums, step, gain_ref, gate_ref, mixed_ref, *refs):
-    squares, (out_ref, done, sems) = refs[:sums], refs[sums:]
+    squares, (out_ref, token_ref, done, sems) = refs[:sums], refs[sums:]
+    token_ref[...] = jnp.zeros((8, LANES), F32)
     total = squares[0][0:1, :]
     for ref in squares[1:]:
         total = total + ref[0:1, :]
@@ -545,7 +549,7 @@
         "finish",
         [],
         [gain, gate, mixed, *squares],
-        sds((tokens * heads, LANES), BF16),
+        (sds((tokens * heads, LANES), BF16), sds((8, LANES), F32)),
         scratch=[pltpu.VMEM((tokens * heads, LANES), BF16), pltpu.SemaphoreType.DMA((tokens // step,))],
         estimate=cost(0, tokens * heads * LANES * 8, tokens * heads * LANES),
         after=after,
@@ -747,6 +751,7 @@
 
     forward = [(b, b + 2) for b in everyone]
     ahead = send(own_kv, forward)
+    beside = send(own_kv, swap)
     far = None
     if window % 2:
         far = send(own_kv, [(b, b + window) for b in range(1, blocks - window, 2)])
@@ -784,22 +789,20 @@
         qh.append(got[1])
         return (got[0], *got[2:]) if relay else got[0]
 
-    done = first_attention([sent[0]])
-    lane = ahead
+    done = first_attention([sent[0], beside])
     if parts > 1:
-        done, lane = inner_of(0, [done], [ahead])
+        done = inner_of(0, [done])
+    run = group_map(place, quarters, size, [done])
+    slot, lane = pick(place, beside if far is None else far, beside, ahead, [run])
+    slot = (slot, (blocks if far is None else window, 1))
+    first_cross = send(lane, swap)
     second = send(lane, [(b, b + 2) for b in range(2, blocks - 2)])
-    run, lane, own_copy = group_map(
-        place, quarters, size, [done] if far is None else [done, far], [lane, own_kv]
-    )
-    first_cross = send(lane, swap)
-    beside = send(own_copy, swap)
     stages = (blocks // GROUP_BLOCKS).bit_length() - 1
     before, done = None, run
     for stage in range(stages):
         came = send(run, [(b, b ^ (GROUP_BLOCKS << stage)) for b in everyone])
         if stage == stages - 1:
-            done = more_attention([(lane, (2, 2))], False, [done])
+            done = more_attention([slot, (lane, (2, 2))], False, [done])
             done = inner_of(parts - 1, [done])
         else:
             run, before = scan_step(place, stage + 2, run, came, before, size, [done])
@@ -807,8 +810,8 @@
     *priors, prior_doc = prior_states(place, stages + 1, quarters, came, before, size, [done])
     priors = [priors[0]] + [send(priors[j], [(b, b ^ j) for b in everyone]) for j in others]
     done = more_attention([(first_cross, (2, 3)), (second, (4, 4))], False, [prior_doc])
-    slot, lane = pass_on(place, beside if far is None else far, beside, second, [done, *priors])
-    rest = [(slot, (blocks if far is None else window, 1)), (send(lane, swap), (4, 5))]
+    lane = pass_on(second, [done, *priors])
+    rest = [(send(lane, swap), (4, 5))]
     for back in range(3, window // 2 + 1):
         lane = send(lane, forward)
         rest.append((lane, (2 * back, 2 * back)))
@@ -817,12 +820,11 @@
     sums = [squares]
     for other in range(1, tensor):
         sums.append(lax.ppermute(squares, "tp", [(t, t ^ other) for t in range(tensor)]))
-    done = squares
+    lin_out, done = finish(norm_gain, flat(lin_gate), mixed, sums, tokens, heads, [squares])
     while rest:
         got = more_attention(rest[:2], len(rest) <= 2, [done])
         rest, done = rest[2:], got
-    soft_out, done = got
-    lin_out = finish(norm_gain, flat(lin_gate), mixed, sums, tokens, heads, [done])
+    soft_out = got[0]
     shape = (tokens, heads, HEAD_DIM)
     return lin_out.reshape(shape), soft_out.reshape(shape)
 

time: 56.6 us -> 60.2 us (1.064); the launches traced: 55.5 us -> 59.9 us
  waiting for transfers between devices: 2.54 us -> 5.69 us
  Pallas kernels: 26.5 us -> 27.2 us
    ppermute x3, waiting for transfers between devices: 0.01 us -> 1.82 us  [body(): lax.ppermute(squares, 'tp', [(t, t ^ other) for t in range(tensor)])]
    ppermute x13, waiting for transfers between devices: 2.53 us -> 3.86 us  [send(): return lax.ppermute(x, 'seq', [(a, b % blocks) for a, b in pairs])]
    pallas_call x13 -> x14, Pallas kernels: 26.5 us -> 27.2 us  [call(): pl.pallas_call(run, out_shape=outs, in_specs=[SMEM] * len(scalars) + [HBM...]
  transfers between devices with their start and end apart: 16 -> 16, of which waited for: 4 -> 6; matrix products, arithmetic and copies ran while one was open for 0% -> 0% of each run, Pallas kernels for 41% -> 35%
where the time goes in v15:
time: 60.2 us; the launch traced here: 59.9 us
  Pallas kernels  27.2 us (45%)
  starting transfers between devices  26.1 us (43%)
  waiting for transfers between devices  5.69 us (9%)
  between operations  1 us (2%)
    pallas_call x14, Pallas kernels, call(): pl.pallas_call(run, out_shape=outs, in_specs=[SMEM] * len(scalars) + [HBM...  27.2 us
    ppermute x13, starting transfers between devices, send(): return lax.ppermute(x, 'seq', [(a, b % blocks) for a, b in pairs])  24.2 us
    ppermute x13, waiting for transfers between devices, send(): return lax.ppermute(x, 'seq', [(a, b % blocks) for a, b in pairs])  3.86 us
    ppermute x3, starting transfers between devices, body(): lax.ppermute(squares, 'tp', [(t, t ^ other) for t in range(tensor)])  1.89 us
    ppermute x3, waiting for transfers between devices, body(): lax.ppermute(squares, 'tp', [(t, t ^ other) for t in range(tensor)])  1.82 us
  transfers between devices with their start and end apart: 16, of which 6 were waited for; matrix products, arithmetic and copies ran while one was open for 0% of the time, Pallas kernels for 35%

profile of v15, /device:TPU:0, one launch (start us, length us, event | category | flops | bytes accessed | tf_op | source)
XLA Modules:
  0.0 59.9 jit_solution(11771603704372106669)
XLA Ops:
  0.6 1.9 %fetch.1 = (bf16[1040,128]{1,0:T(8,128)(2,1)S(1)}, f32[16,128]{1,0:T(8,128)S(1)}, f32[256,128]{1,0:T(8,128)S(1)}, bf16[4096,128]{1,0:T(8,128)(2,1)S(1)}, bf16[4096,128]{1,0:T(8,128)(2,1)S(1)}) custom-call(s32[1]{0:T(128)} %bitcast.2.refs_0_, s32[2,128]{1,0:T(2,128)} %bitcast.22, f32[16,256]{1,0:T(8,128)} %bitcast.21, bf16[2048,128]{1,0:T(8,128)(2,1)} %bitcast.19, ...), custom_call_target="tpu_custom_call" | custom-call | bytes 3145728 | tf_op jit(solution)/shard_map/fetch/pallas_call | solution.py:68
  2.6 3.0 %collective-permute-start.3 = (bf16[1040,128]{1,0:T(8,128)(2,1)S(1)}, bf16[1040,128]{1,0:T(8,128)(2,1)S(1)}, u32[]{:S(2)}, u32[]{:S(2)}) collective-permute-start(bf16[1040,128]{1,0:T(8,128)(2,1)S(1)} %get-tuple-element.39.refs_3_), channel_id=1, source_target_pairs={{0,4},{4,0},{8,12},{12,8},{16,20},{20,16},{24,28},{28,24},{1,5},{5... | collective-permute-start | bytes 798728 | tf_op jit(solution)/shard_map/ppermute | solution.py:732
  5.6 1.6 %collective-permute-start.6 = (bf16[1040,128]{1,0:T(8,128)(2,1)S(1)}, bf16[1040,128]{1,0:T(8,128)(2,1)S(1)}, u32[]{:S(2)}, u32[]{:S(2)}) collective-permute-start(bf16[1040,128]{1,0:T(8,128)(2,1)S(1)} %get-tuple-element.39.refs_3_), channel_id=1, source_target_pairs={{0,8},{4,12},{8,16},{12,20},{16,24},{20,28},{24,0},{28,4},{1,9},{5... | collective-permute-start | bytes 798728 | tf_op jit(solution)/shard_map/ppermute | solution.py:732
  7.2 0.7 %collective-permute-start.5 = (bf16[1040,128]{1,0:T(8,128)(2,1)S(1)}, bf16[1040,128]{1,0:T(8,128)(2,1)S(1)}, u32[]{:S(2)}, u32[]{:S(2)}) collective-permute-start(bf16[1040,128]{1,0:T(8,128)(2,1)S(1)} %get-tuple-element.39.refs_3_), channel_id=1, source_target_pairs={{4,24},{5,25},{6,26},{7,27}} | collective-permute-start | bytes 798728 | tf_op jit(solution)/shard_map/ppermute | solution.py:732
  7.9 3.8 %block_state.1 = (bf16[528,128]{1,0:T(8,128)(2,1)S(1)}, bf16[528,128]{1,0:T(8,128)(2,1)S(1)}, bf16[528,128]{1,0:T(8,128)(2,1)S(1)}, bf16[528,128]{1,0:T(8,128)(2,1)S(1)}, bf16[4096,128]{1,0:T(8,128)(2,1)S(1)}) custom-call(s32[1]{0:T(128)} %bitcast.1.refs_0_, bf16[4096,128]{1,0:T(8,128)(2,1)} %bitcast.18, ...), custom_call_target="tpu_custom_call" | custom-call | flops 134217728 | bytes 5242880 | tf_op jit(solution)/shard_map/block_state/pallas_call | solution.py:68
  11.7 0.0 copy-start
  11.7 5.0 %collective-permute-start = (bf16[528,128]{1,0:T(8,128)(2,1)S(1)}, bf16[528,128]{1,0:T(8,128)(2,1)S(1)}, u32[]{:S(2)}, u32[]{:S(2)}) collective-permute-start(bf16[528,128]{1,0:T(8,128)(2,1)S(1)} %get-tuple-element.35), channel_id=1, source_target_pairs={{0,4},{4,0},{8,12},{12,8},{16,20},{20,16},{24,28},{28,24},{1,5},{5... | collective-permute-start | bytes 405512 | tf_op jit(solution)/shard_map/ppermute | solution.py:732
  16.7 0.0 collective-permute-start.1
  16.7 0.0 collective-permute-done.3.refs_5_.refs_2_
  16.7 1.5 %collective-permute-start.2 = (bf16[528,128]{1,0:T(8,128)(2,1)S(1)}, bf16[528,128]{1,0:T(8,128)(2,1)S(1)}, u32[]{:S(2)}, u32[]{:S(2)}) collective-permute-start(bf16[528,128]{1,0:T(8,128)(2,1)S(1)} %get-tuple-element.37), channel_id=1, source_target_pairs={{0,12},{4,8},{8,4},{12,0},{16,28},{20,24},{24,20},{28,16},{1,13},{... | collective-permute-start | bytes 405512 | tf_op jit(solution)/shard_map/ppermute | solution.py:732
  18.2 2.7 %attend.4 = (bf16[2,2048,256]{2,1,0:T(8,128)(2,1)S(1)}, f32[2,144,2048]{2,1,0:T(8,128)S(1)}) custom-call(s32[1]{0:T(128)} %bitcast.1.refs_0_, f32[16,128]{1,0:T(8,128)S(1)} %get-tuple-element.30.refs_3_.refs_1_, bf16[4096,128]{1,0:T(8,128)(2,1)S(1)} %get-tuple-element.38.refs_2_, bf16[1040,128]{1,0:T(8,128)(2,1)S(1)} %get-tuple-element.39.refs_3_, ...), custom_call_target="tpu_custom_call" | custom-call | flops 1073741824 | bytes 8388608 | tf_op jit(solution)/shard_map/attend/pallas_call | solution.py:68
  20.9 0.0 copy-done
  20.9 1.9 %inner_part.2 = (f32[2048,128]{1,0:T(8,128)S(1)}, bf16[2048,128]{1,0:T(8,128)(2,1)S(1)}) custom-call(f32[256,128]{1,0:T(8,128)S(1)} %get-tuple-element.31.refs_2_.refs_0_.refs_3_, f32[16,128]{1,0:T(8,128)S(1)} %get-tuple-element.30.refs_3_.refs_1_, bf16[4096,128]{1,0:T(8,128)(2,1)S(1)} %bitcast.13, bf16[4096,128]{1,0:T(8,128)(2,1)S(1)} %get-tuple-element.32.refs_4_.refs_3_, ...), custom_call_target="tpu_custom_call" | custom-call | flops 268435456 | bytes 6291456 | tf_op jit(solution)/shard_map/inner_part/pallas_call | solution.py:68
  22.8 0.0 collective-permute-done.refs_2_
  22.8 0.0 collective-permute-done.1.refs_3_
  22.8 0.8 %collective-permute-done.2.refs_4_ = bf16[528,128]{1,0:T(8,128)(2,1)S(1)} collective-permute-done((bf16[528,128]{1,0:T(8,128)(2,1)S(1)}, bf16[528,128]{1,0:T(8,128)(2,1)S(1)}, u32[]{:S(2)}, u32[]{:S(2)}) %collective-permute-start.2) | collective-permute-done | bytes 135200 | tf_op jit(solution)/shard_map/ppermute | solution.py:732
  23.6 0.2 group_map.1.refs_3_.refs_5_
  23.9 0.0 collective-permute-done.6.refs_4_
  23.9 0.0 collective-permute-done.5.refs_1_
  23.9 0.1 pick.1
  24.0 0.9 %collective-permute-start.11 = (bf16[1040,128]{1,0:T(8,128)(2,1)S(1)}, bf16[1040,128]{1,0:T(8,128)(2,1)S(1)}, u32[]{:S(2)}, u32[]{:S(2)}) collective-permute-start(bf16[1040,128]{1,0:T(8,128)(2,1)S(1)} %get-tuple-element.44.refs_4_), channel_id=1, source_target_pairs={{8,16},{12,20},{16,24},{20,28},{9,17},{13,21},{17,25},{21,29},{10,... | collective-permute-start | bytes 798728 | tf_op jit(solution)/shard_map/ppermute | solution.py:732
  24.9 1.7 %collective-permute-start.10 = (bf16[1040,128]{1,0:T(8,128)(2,1)S(1)}, bf16[1040,128]{1,0:T(8,128)(2,1)S(1)}, u32[]{:S(2)}, u32[]{:S(2)}) collective-permute-start(bf16[1040,128]{1,0:T(8,128)(2,1)S(1)} %get-tuple-element.44.refs_4_), channel_id=1, source_target_pairs={{0,4},{4,0},{8,12},{12,8},{16,20},{20,16},{24,28},{28,24},{1,5},{5... | collective-permute-start | bytes 798728 | tf_op jit(solution)/shard_map/ppermute | solution.py:732
  26.6 5.1 %collective-permute-start.4 = (bf16[528,128]{1,0:T(8,128)(2,1)S(1)}, bf16[528,128]{1,0:T(8,128)(2,1)S(1)}, u32[]{:S(2)}, u32[]{:S(2)}) collective-permute-start(bf16[528,128]{1,0:T(8,128)(2,1)S(1)} %group_map.1.refs_3_.refs_5_), channel_id=1, source_target_pairs={{0,16},{4,20},{8,24},{12,28},{16,0},{20,4},{24,8},{28,12},{1,17},{... | collective-permute-start | bytes 405512 | tf_op jit(solution)/shard_map/ppermute | solution.py:732
  31.7 3.6 %attend.5.refs_5_.refs_2_ = f32[2,144,2048]{2,1,0:T(8,128)S(1)} custom-call(s32[1]{0:T(128)} %bitcast.1.refs_0_, bf16[2,2048,256]{2,1,0:T(8,128)(2,1)S(1)} %get-tuple-element.42.refs_1_, f32[2,144,2048]{2,1,0:T(8,128)S(1)} %get-tuple-element.40.refs_5_.refs_2_, bf16[1040,128]{1,0:T(8,128)(2,1)S(1)} %get-tuple-element.43.refs_3_, ...), custom_call_target="tpu_custom_call" | custom-call | flops 2147483648 | bytes 8388608 | tf_op jit(solution)/shard_map/attend/pallas_call | solution.py:68
  35.3 1.9 %inner_part.3 = (f32[2048,128]{1,0:T(8,128)S(1)}, bf16[2048,128]{1,0:T(8,128)(2,1)S(1)}) custom-call(f32[256,128]{1,0:T(8,128)S(1)} %get-tuple-element.31.refs_2_.refs_0_.refs_3_, f32[16,128]{1,0:T(8,128)S(1)} %get-tuple-element.30.refs_3_.refs_1_, bf16[4096,128]{1,0:T(8,128)(2,1)S(1)} %bitcast.14, bf16[4096,128]{1,0:T(8,128)(2,1)S(1)} %get-tuple-element.32.refs_4_.refs_3_, ...), custom_call_target="tpu_custom_call" | custom-call | flops 268435456 | bytes 6291456 | tf_op jit(solution)/shard_map/inner_part/pallas_call | solution.py:68
  37.2 0.9 %collective-permute-done.4.refs_5_ = bf16[528,128]{1,0:T(8,128)(2,1)S(1)} collective-permute-done((bf16[528,128]{1,0:T(8,128)(2,1)S(1)}, bf16[528,128]{1,0:T(8,128)(2,1)S(1)}, u32[]{:S(2)}, u32[]{:S(2)}) %collective-permute-start.4) | collective-permute-done | bytes 135200 | tf_op jit(solution)/shard_map/ppermute | solution.py:732
  38.1 0.3 prior_states.1
  38.4 1.1 %collective-permute-start.7 = (bf16[512,128]{1,0:T(8,128)(2,1)S(1)}, bf16[512,128]{1,0:T(8,128)(2,1)S(1)}, u32[]{:S(2)}, u32[]{:S(2)}) collective-permute-start(bf16[512,128]{1,0:T(8,128)(2,1)S(1)} %get-tuple-element.50), channel_id=1, source_target_pairs={{0,4},{4,0},{8,12},{12,8},{16,20},{20,16},{24,28},{28,24},{1,5},{5... | collective-permute-start | bytes 393224 | tf_op jit(solution)/shard_map/ppermute | solution.py:732
  39.5 2.5 %collective-permute-start.8 = (bf16[512,128]{1,0:T(8,128)(2,1)S(1)}, bf16[512,128]{1,0:T(8,128)(2,1)S(1)}, u32[]{:S(2)}, u32[]{:S(2)}) collective-permute-start(bf16[512,128]{1,0:T(8,128)(2,1)S(1)} %get-tuple-element.51), channel_id=1, source_target_pairs={{0,8},{4,12},{8,0},{12,4},{16,24},{20,28},{24,16},{28,20},{1,9},{5... | collective-permute-start | bytes 393224 | tf_op jit(solution)/shard_map/ppermute | solution.py:732
  42.0 0.0 collective-permute-start.9
  42.0 0.0 collective-permute-done.11.refs_4_.refs_5_
  42.0 0.0 collective-permute-done.10.refs_3_
  42.0 3.7 %attend.6.refs_12_.refs_0_.refs_2_ = f32[2,144,2048]{2,1,0:T(8,128)S(1)} custom-call(s32[1]{0:T(128)} %bitcast.1.refs_0_, bf16[2,2048,256]{2,1,0:T(8,128)(2,1)S(1)} %get-tuple-element.42.refs_1_, f32[2,144,2048]{2,1,0:T(8,128)S(1)} %attend.5.refs_5_.refs_2_, bf16[1040,128]{1,0:T(8,128)(2,1)S(1)} %collective-permute-done.10.refs_3_, ...), custom_call_target="tpu_custom_call" | custom-call | flops 2147483648 | bytes 8388608 | tf_op jit(solution)/shard_map/attend/pallas_call | solution.py:68
  45.7 0.0 collective-permute-done.7.refs_9_.refs_2_
  45.7 0.3 collective-permute-done.8.refs_10_.refs_3_
  46.0 1.9 %collective-permute-done.9.refs_11_.refs_4_ = bf16[512,128]{1,0:T(8,128)(2,1)S(1)} collective-permute-done((bf16[512,128]{1,0:T(8,128)(2,1)S(1)}, bf16[512,128]{1,0:T(8,128)(2,1)S(1)}, u32[]{:S(2)}, u32[]{:S(2)}) %collective-permute-start.9) | collective-permute-done | bytes 131104 | tf_op jit(solution)/shard_map/ppermute | solution.py:732
  47.9 1.0 %collective-permute-start.15 = (bf16[1040,128]{1,0:T(8,128)(2,1)S(1)}, bf16[1040,128]{1,0:T(8,128)(2,1)S(1)}, u32[]{:S(2)}, u32[]{:S(2)}) collective-permute-start(bf16[1040,128]{1,0:T(8,128)(2,1)S(1)} %pass_on.1), channel_id=1, source_target_pairs={{0,4},{4,0},{8,12},{12,8},{16,20},{20,16},{24,28},{28,24},{1,5},{5... | collective-permute-start | bytes 798728 | tf_op jit(solution)/shard_map/ppermute | solution.py:732
  48.9 1.6 %mix.1 = (f32[4096,128]{1,0:T(8,128)S(1)}, f32[8,256]{1,0:T(8,128)S(1)}) custom-call(s32[1]{0:T(128)} %bitcast.1.refs_0_, f32[16,128]{1,0:T(8,128)S(1)} %get-tuple-element.30.refs_3_.refs_1_, f32[8,128]{1,0:T(8,128)S(1)} %get-tuple-element.46.refs_5_.refs_2_, f32[256,128]{1,0:T(8,128)S(1)} %get-tuple-element.31.refs_2_.refs_0_.refs_3_, ...), custom_call_target="tpu_custom_call" | custom-call | flops 134217728 | bytes 5242880 | tf_op jit(solution)/shard_map/mix/pallas_call | solution.py:68
  50.5 0.0 collective-permute-start.14
  50.5 1.6 %collective-permute-start.13 = (f32[8,256]{1,0:T(8,128)S(1)}, f32[8,256]{1,0:T(8,128)S(1)}, u32[]{:S(2)}, u32[]{:S(2)}) collective-permute-start(f32[8,256]{1,0:T(8,128)S(1)} %get-tuple-element.54.refs_3_.refs_7_), channel_id=1, source_target_pairs={{0,2},{1,3},{2,0},{3,1},{4,6},{5,7},{6,4},{7,5},{8,10},{9,11},{10,... | collective-permute-start | bytes 24584 | tf_op jit(solution)/shard_map/ppermute | solution.py:822
  52.1 0.3 collective-permute-start.12
  52.4 1.3 %collective-permute-done.14.refs_6_ = f32[8,256]{1,0:T(8,128)S(1)} collective-permute-done((f32[8,256]{1,0:T(8,128)S(1)}, f32[8,256]{1,0:T(8,128)S(1)}, u32[]{:S(2)}, u32[]{:S(2)}) %collective-permute-start.14) | collective-permute-done | bytes 8224 | tf_op jit(solution)/shard_map/ppermute | solution.py:822
  53.6 0.6 collective-permute-done.13.refs_5_
  54.2 0.0 collective-permute-done.12.refs_4_
  54.2 0.0 copy-done.1
  54.2 1.6 %finish.1 = (bf16[4096,128]{1,0:T(8,128)(2,1)}, f32[8,128]{1,0:T(8,128)S(1)}) custom-call(f32[16,128]{1,0:T(8,128)S(1)} %copy-done.2, bf16[4096,128]{1,0:T(8,128)(2,1)S(1)} %bitcast.15, f32[4096,128]{1,0:T(8,128)S(1)} %get-tuple-element.53.refs_2_, f32[8,256]{1,0:T(8,128)S(1)} %get-tuple-element.54.refs_3_.refs_7_, ...), custom_call_target="tpu_custom_call" | custom-call | bytes 4194304 | tf_op jit(solution)/shard_map/finish/pallas_call | solution.py:68
  55.9 0.0 collective-permute-done.15.refs_3_
  55.9 3.9 %attend.7 = (bf16[4096,128]{1,0:T(8,128)(2,1)}, f32[8,128]{1,0:T(8,128)}) custom-call(s32[1]{0:T(128)} %bitcast.1.refs_0_, bf16[2,2048,256]{2,1,0:T(8,128)(2,1)S(1)} %get-tuple-element.42.refs_1_, f32[2,144,2048]{2,1,0:T(8,128)S(1)} %attend.6.refs_12_.refs_0_.refs_2_, bf16[1040,128]{1,0:T(8,128)(2,1)S(1)} %collective-permute-done.15.refs_3_, ...), custom_call_target="tpu_custom_call" | custom-call | flops 1073741824 | bytes 8388608 | tf_op jit(solution)/shard_map/attend/pallas_call | solution.py:68
  (4 shorter events, 0.0 us)
Async XLA Ops:
  2.6 14.1 %collective-permute-start.3 = (bf16[1040,128]{1,0:T(8,128)(2,1)S(1)}, bf16[1040,128]{1,0:T(8,128)(2,1)S(1)}, u32[]{:S(2)}, u32[]{:S(2)}) collective-permute-start(bf16[1040,128]{1,0:T(8,128)(2,1)S(1)} %get-tuple-element.39.refs_3_), channel_id=1, source_target_pairs={{0,4},{4,0},{8,12},{12,8},{16,20},{20,16},{24,28},{28,24},{1,5},{5... | collective-permute-start | bytes 798728 | tf_op jit(solution)/shard_map/ppermute | solution.py:732
  5.6 18.2 %collective-permute-start.6 = (bf16[1040,128]{1,0:T(8,128)(2,1)S(1)}, bf16[1040,128]{1,0:T(8,128)(2,1)S(1)}, u32[]{:S(2)}, u32[]{:S(2)}) collective-permute-start(bf16[1040,128]{1,0:T(8,128)(2,1)S(1)} %get-tuple-element.39.refs_3_), channel_id=1, source_target_pairs={{0,8},{4,12},{8,16},{12,20},{16,24},{20,28},{24,0},{28,4},{1,9},{5... | collective-permute-start | bytes 798728 | tf_op jit(solution)/shard_map/ppermute | solution.py:732
  7.2 16.7 %collective-permute-start.5 = (bf16[1040,128]{1,0:T(8,128)(2,1)S(1)}, bf16[1040,128]{1,0:T(8,128)(2,1)S(1)}, u32[]{:S(2)}, u32[]{:S(2)}) collective-permute-start(bf16[1040,128]{1,0:T(8,128)(2,1)S(1)} %get-tuple-element.39.refs_3_), channel_id=1, source_target_pairs={{4,24},{5,25},{6,26},{7,27}} | collective-permute-start | bytes 798728 | tf_op jit(solution)/shard_map/ppermute | solution.py:732
  11.7 9.2 %copy-start = (bf16[256,16,128]{2,1,0:T(8,128)(2,1)S(1)}, bf16[256,16,128]{2,1,0:T(8,128)(2,1)}, u32[]{:S(2)}) copy-start(bf16[256,16,128]{2,1,0:T(8,128)(2,1)} %param.10) | copy-start | bytes 3145732
  11.7 11.2 %collective-permute-start = (bf16[528,128]{1,0:T(8,128)(2,1)S(1)}, bf16[528,128]{1,0:T(8,128)(2,1)S(1)}, u32[]{:S(2)}, u32[]{:S(2)}) collective-permute-start(bf16[528,128]{1,0:T(8,128)(2,1)S(1)} %get-tuple-element.35), channel_id=1, source_target_pairs={{0,4},{4,0},{8,12},{12,8},{16,20},{20,16},{24,28},{28,24},{1,5},{5... | collective-permute-start | bytes 405512 | tf_op jit(solution)/shard_map/ppermute | solution.py:732
  16.7 6.1 %collective-permute-start.1 = (bf16[528,128]{1,0:T(8,128)(2,1)S(1)}, bf16[528,128]{1,0:T(8,128)(2,1)S(1)}, u32[]{:S(2)}, u32[]{:S(2)}) collective-permute-start(bf16[528,128]{1,0:T(8,128)(2,1)S(1)} %get-tuple-element.36), channel_id=1, source_target_pairs={{0,8},{4,12},{8,0},{12,4},{16,24},{20,28},{24,16},{28,20},{1,9},{5... | collective-permute-start | bytes 405512 | tf_op jit(solution)/shard_map/ppermute | solution.py:732
  16.7 6.9 %collective-permute-start.2 = (bf16[528,128]{1,0:T(8,128)(2,1)S(1)}, bf16[528,128]{1,0:T(8,128)(2,1)S(1)}, u32[]{:S(2)}, u32[]{:S(2)}) collective-permute-start(bf16[528,128]{1,0:T(8,128)(2,1)S(1)} %get-tuple-element.37), channel_id=1, source_target_pairs={{0,12},{4,8},{8,4},{12,0},{16,28},{20,24},{24,20},{28,16},{1,13},{... | collective-permute-start | bytes 405512 | tf_op jit(solution)/shard_map/ppermute | solution.py:732
  24.0 18.0 %collective-permute-start.11 = (bf16[1040,128]{1,0:T(8,128)(2,1)S(1)}, bf16[1040,128]{1,0:T(8,128)(2,1)S(1)}, u32[]{:S(2)}, u32[]{:S(2)}) collective-permute-start(bf16[1040,128]{1,0:T(8,128)(2,1)S(1)} %get-tuple-element.44.refs_4_), channel_id=1, source_target_pairs={{8,16},{12,20},{16,24},{20,28},{9,17},{13,21},{17,25},{21,29},{10,... | collective-permute-start | bytes 798728 | tf_op jit(solution)/shard_map/ppermute | solution.py:732
  24.9 17.1 %collective-permute-start.10 = (bf16[1040,128]{1,0:T(8,128)(2,1)S(1)}, bf16[1040,128]{1,0:T(8,128)(2,1)S(1)}, u32[]{:S(2)}, u32[]{:S(2)}) collective-permute-start(bf16[1040,128]{1,0:T(8,128)(2,1)S(1)} %get-tuple-element.44.refs_4_), channel_id=1, source_target_pairs={{0,4},{4,0},{8,12},{12,8},{16,20},{20,16},{24,28},{28,24},{1,5},{5... | collective-permute-start | bytes 798728 | tf_op jit(solution)/shard_map/ppermute | solution.py:732
  26.6 11.5 %collective-permute-start.4 = (bf16[528,128]{1,0:T(8,128)(2,1)S(1)}, bf16[528,128]{1,0:T(8,128)(2,1)S(1)}, u32[]{:S(2)}, u32[]{:S(2)}) collective-permute-start(bf16[528,128]{1,0:T(8,128)(2,1)S(1)} %group_map.1.refs_3_.refs_5_), channel_id=1, source_target_pairs={{0,16},{4,20},{8,24},{12,28},{16,0},{20,4},{24,8},{28,12},{1,17},{... | collective-permute-start | bytes 405512 | tf_op jit(solution)/shard_map/ppermute | solution.py:732
  38.4 7.3 %collective-permute-start.7 = (bf16[512,128]{1,0:T(8,128)(2,1)S(1)}, bf16[512,128]{1,0:T(8,128)(2,1)S(1)}, u32[]{:S(2)}, u32[]{:S(2)}) collective-permute-start(bf16[512,128]{1,0:T(8,128)(2,1)S(1)} %get-tuple-element.50), channel_id=1, source_target_pairs={{0,4},{4,0},{8,12},{12,8},{16,20},{20,16},{24,28},{28,24},{1,5},{5... | collective-permute-start | bytes 393224 | tf_op jit(solution)/shard_map/ppermute | solution.py:732
  39.5 6.4 %collective-permute-start.8 = (bf16[512,128]{1,0:T(8,128)(2,1)S(1)}, bf16[512,128]{1,0:T(8,128)(2,1)S(1)}, u32[]{:S(2)}, u32[]{:S(2)}) collective-permute-start(bf16[512,128]{1,0:T(8,128)(2,1)S(1)} %get-tuple-element.51), channel_id=1, source_target_pairs={{0,8},{4,12},{8,0},{12,4},{16,24},{20,28},{24,16},{28,20},{1,9},{5... | collective-permute-start | bytes 393224 | tf_op jit(solution)/shard_map/ppermute | solution.py:732
  42.0 5.9 %collective-permute-start.9 = (bf16[512,128]{1,0:T(8,128)(2,1)S(1)}, bf16[512,128]{1,0:T(8,128)(2,1)S(1)}, u32[]{:S(2)}, u32[]{:S(2)}) collective-permute-start(bf16[512,128]{1,0:T(8,128)(2,1)S(1)} %get-tuple-element.52), channel_id=1, source_target_pairs={{0,12},{4,8},{8,4},{12,0},{16,28},{20,24},{24,20},{28,16},{1,13},{... | collective-permute-start | bytes 393224 | tf_op jit(solution)/shard_map/ppermute | solution.py:732
  47.9 8.0 %collective-permute-start.15 = (bf16[1040,128]{1,0:T(8,128)(2,1)S(1)}, bf16[1040,128]{1,0:T(8,128)(2,1)S(1)}, u32[]{:S(2)}, u32[]{:S(2)}) collective-permute-start(bf16[1040,128]{1,0:T(8,128)(2,1)S(1)} %pass_on.1), channel_id=1, source_target_pairs={{0,4},{4,0},{8,12},{12,8},{16,20},{20,16},{24,28},{28,24},{1,5},{5... | collective-permute-start | bytes 798728 | tf_op jit(solution)/shard_map/ppermute | solution.py:732
  48.9 5.3 %copy-start.1 = (bf16[256,16,128]{2,1,0:T(8,128)(2,1)S(1)}, bf16[256,16,128]{2,1,0:T(8,128)(2,1)}, u32[]{:S(2)}) copy-start(bf16[256,16,128]{2,1,0:T(8,128)(2,1)} %param.13) | copy-start | bytes 3145732
  48.9 5.3 %copy-start.2 = (f32[16,128]{1,0:T(8,128)S(1)}, f32[16,128]{1,0:T(8,128)}, u32[]{:S(2)}) copy-start(f32[16,128]{1,0:T(8,128)} %refs_0_.1) | copy-start | bytes 24580
  50.5 3.1 %collective-permute-start.14 = (f32[8,256]{1,0:T(8,128)S(1)}, f32[8,256]{1,0:T(8,128)S(1)}, u32[]{:S(2)}, u32[]{:S(2)}) collective-permute-start(f32[8,256]{1,0:T(8,128)S(1)} %get-tuple-element.54.refs_3_.refs_7_), channel_id=1, source_target_pairs={{0,3},{1,2},{2,1},{3,0},{4,7},{5,6},{6,5},{7,4},{8,11},{9,10},{10,... | collective-permute-start | bytes 24584 | tf_op jit(solution)/shard_map/ppermute | solution.py:822
  50.5 3.7 %collective-permute-start.13 = (f32[8,256]{1,0:T(8,128)S(1)}, f32[8,256]{1,0:T(8,128)S(1)}, u32[]{:S(2)}, u32[]{:S(2)}) collective-permute-start(f32[8,256]{1,0:T(8,128)S(1)} %get-tuple-element.54.refs_3_.refs_7_), channel_id=1, source_target_pairs={{0,2},{1,3},{2,0},{3,1},{4,6},{5,7},{6,4},{7,5},{8,10},{9,11},{10,... | collective-permute-start | bytes 24584 | tf_op jit(solution)/shard_map/ppermute | solution.py:822
  52.1 2.2 %collective-permute-start.12 = (f32[8,256]{1,0:T(8,128)S(1)}, f32[8,256]{1,0:T(8,128)S(1)}, u32[]{:S(2)}, u32[]{:S(2)}) collective-permute-start(f32[8,256]{1,0:T(8,128)S(1)} %get-tuple-element.54.refs_3_.refs_7_), channel_id=1, source_target_pairs={{0,1},{1,0},{2,3},{3,2},{4,5},{5,4},{6,7},{7,6},{8,9},{9,8},{10,11... | collective-permute-start | bytes 24584 | tf_op jit(solution)/shard_map/ppermute | solution.py:822

commit v16 on v13

--- a/solution.py
+++ b/solution.py
@@ -633,7 +633,7 @@
                 out_ref[g, 0 : STATE_ROWS - 8, at[u]] = total[0 : STATE_ROWS - 8]
                 out_ref[g, STATE_ROWS - 8 : STATE_ROWS, at[u]] = jnp.broadcast_to(top, (8, CHUNK))
 
-        ahead = 2
+        ahead = 3
         for n in range(len(chains) + ahead):
             if n < len(chains):
                 begin(*chains[n])
@@ -664,7 +664,7 @@
     kv = [block for block, _ in kv]
     blocks = len(kv)
     rows = tokens * heads // kv_here
-    unroll = min(4, rows // CHUNK)
+    unroll = min(8, rows // CHUNK)
     wide_shape = sds((kv_here, rows, 2 * LANES), BF16)
     state_shape = sds((kv_here, STATE_ROWS, rows), F32)
     out_shape = sds((tokens * heads, LANES), BF16) if is_last else state_shape
@@ -746,6 +746,7 @@
             last = next(a for a in everyone if hop[a] == b + window)
             hop[b], hop[last] = b + window, hop[b]
     ahead = send(own_kv, forward)
+    beside = (send(own_kv, list(hop.items())), (window if window % 2 else blocks, 1))
 
     size = quarter_rows(heads)
     others = range(1, GROUP_BLOCKS)
@@ -780,20 +781,18 @@
         qh.append(got[1])
         return (got[0], *got[2:]) if relay else got[0]
 
-    done = first_attention([sent[0]])
-    lane = ahead
+    done, lane = first_attention([sent[0]]), ahead
     if parts > 1:
         done, lane = inner_of(0, [done], [ahead])
-    second = send(lane, [(b, b + 2) for b in range(2, blocks - 2)])
-    run, lane, own_copy = group_map(place, quarters, size, [done], [lane, own_kv])
+    second = send(lane, forward)
+    run, lane = group_map(place, quarters, size, [done, beside[0]], [lane])
     first_cross = send(lane, swap)
-    beside = (send(own_copy, list(hop.items())), (window if window % 2 else blocks, 1))
     stages = (blocks // GROUP_BLOCKS).bit_length() - 1
     before, done = None, run
     for stage in range(stages):
         came = send(run, [(b, b ^ (GROUP_BLOCKS << stage)) for b in everyone])
         if stage == stages - 1:
-            done = more_attention([(lane, (2, 2))], False, [done])
+            done = more_attention([beside, (lane, (2, 2))], False, [done])
             done = inner_of(parts - 1, [done])
         else:
             run, before = scan_step(place, stage + 2, run, came, before, size, [done])
@@ -802,7 +801,7 @@
     priors = [priors[0]] + [send(priors[j], [(b, b ^ j) for b in everyone]) for j in others]
     done = more_attention([(first_cross, (2, 3)), (second, (4, 4))], False, [prior_doc])
     lane = pass_on(second, [done, *priors])
-    rest = [beside, (send(lane, swap), (4, 5))]
+    rest = [(send(lane, swap), (4, 5))]
     for back in range(3, window // 2 + 1):
         lane = send(lane, forward)
         rest.append((lane, (2 * back, 2 * back)))

time: 59.5 us -> 59.2 us (level)
  waiting for transfers between devices: 8.41 us -> 14.7 us
  starting transfers between devices: 23.5 us -> 18.7 us
  Pallas kernels: 26.4 us -> 24.6 us
    ppermute x12, waiting for transfers between devices: 8.4 us -> 14.7 us  [send(): return lax.ppermute(x, 'seq', [(a, b % blocks) for a, b in pairs])]
    ppermute x12, starting transfers between devices: 21.6 us -> 16.8 us  [send(): return lax.ppermute(x, 'seq', [(a, b % blocks) for a, b in pairs])]
    pallas_call x13, Pallas kernels: 26.4 us -> 24.6 us  [call(): pl.pallas_call(run, out_shape=outs, in_specs=[SMEM] * len(scalars) + [HBM...]
  transfers between devices with their start and end apart: 15 -> 15, of which waited for: 5 -> 6; matrix products, arithmetic and copies ran while one was open for 0% -> 0% of each run, Pallas kernels for 38% -> 36%
where the time goes in v16:
time: 59.2 us; the launch traced here: 59 us
  Pallas kernels  24.6 us (42%)
  starting transfers between devices  18.7 us (32%)
  waiting for transfers between devices  14.7 us (25%)
  between operations  0.97 us (2%)
    pallas_call x13, Pallas kernels, call(): pl.pallas_call(run, out_shape=outs, in_specs=[SMEM] * len(scalars) + [HBM...  24.6 us
    ppermute x12, starting transfers between devices, send(): return lax.ppermute(x, 'seq', [(a, b % blocks) for a, b in pairs])  16.8 us
    ppermute x12, waiting for transfers between devices, send(): return lax.ppermute(x, 'seq', [(a, b % blocks) for a, b in pairs])  14.7 us
    ppermute x3, starting transfers between devices, body(): lax.ppermute(squares, 'tp', [(t, t ^ other) for t in range(tensor)])  1.88 us
  transfers between devices with their start and end apart: 15, of which 6 were waited for; matrix products, arithmetic and copies ran while one was open for 0% of the time, Pallas kernels for 36%

profile of v16, /device:TPU:0, one launch (start us, length us, event | category | flops | bytes accessed | tf_op | source)
XLA Modules:
  0.0 59.0 jit_solution(1682132266700526730)
XLA Ops:
  0.6 1.9 %fetch.1 = (bf16[1040,128]{1,0:T(8,128)(2,1)S(1)}, f32[16,128]{1,0:T(8,128)S(1)}, f32[256,128]{1,0:T(8,128)S(1)}, bf16[4096,128]{1,0:T(8,128)(2,1)S(1)}, bf16[4096,128]{1,0:T(8,128)(2,1)S(1)}) custom-call(s32[1]{0:T(128)} %bitcast.2.refs_0_, s32[2,128]{1,0:T(2,128)} %bitcast.23, f32[16,256]{1,0:T(8,128)} %bitcast.22, bf16[2048,128]{1,0:T(8,128)(2,1)} %bitcast.20, ...), custom_call_target="tpu_custom_call" | custom-call | bytes 3145728 | tf_op jit(solution)/shard_map/fetch/pallas_call | solution.py:68
  2.6 3.1 %collective-permute-start.3 = (bf16[1040,128]{1,0:T(8,128)(2,1)S(1)}, bf16[1040,128]{1,0:T(8,128)(2,1)S(1)}, u32[]{:S(2)}, u32[]{:S(2)}) collective-permute-start(bf16[1040,128]{1,0:T(8,128)(2,1)S(1)} %get-tuple-element.39.refs_3_), channel_id=1, source_target_pairs={{0,8},{4,12},{8,16},{12,20},{16,24},{20,28},{24,0},{28,4},{1,9},{5... | collective-permute-start | bytes 798728 | tf_op jit(solution)/shard_map/ppermute | solution.py:722
  5.7 1.5 %collective-permute-start.4 = (bf16[1040,128]{1,0:T(8,128)(2,1)S(1)}, bf16[1040,128]{1,0:T(8,128)(2,1)S(1)}, u32[]{:S(2)}, u32[]{:S(2)}) collective-permute-start(bf16[1040,128]{1,0:T(8,128)(2,1)S(1)} %get-tuple-element.39.refs_3_), channel_id=1, source_target_pairs={{0,4},{4,24},{8,12},{12,8},{16,20},{20,16},{24,28},{28,0},{1,5},{5... | collective-permute-start | bytes 798728 | tf_op jit(solution)/shard_map/ppermute | solution.py:722
  7.2 3.8 %block_state.1 = (bf16[528,128]{1,0:T(8,128)(2,1)S(1)}, bf16[528,128]{1,0:T(8,128)(2,1)S(1)}, bf16[528,128]{1,0:T(8,128)(2,1)S(1)}, bf16[528,128]{1,0:T(8,128)(2,1)S(1)}, bf16[4096,128]{1,0:T(8,128)(2,1)S(1)}) custom-call(s32[1]{0:T(128)} %bitcast.1.refs_0_, bf16[4096,128]{1,0:T(8,128)(2,1)} %bitcast.19, ...), custom_call_target="tpu_custom_call" | custom-call | flops 134217728 | bytes 5242880 | tf_op jit(solution)/shard_map/block_state/pallas_call | solution.py:68
  11.0 0.0 copy-start
  11.0 2.1 %collective-permute-start = (bf16[528,128]{1,0:T(8,128)(2,1)S(1)}, bf16[528,128]{1,0:T(8,128)(2,1)S(1)}, u32[]{:S(2)}, u32[]{:S(2)}) collective-permute-start(bf16[528,128]{1,0:T(8,128)(2,1)S(1)} %get-tuple-element.35), channel_id=1, source_target_pairs={{0,4},{4,0},{8,12},{12,8},{16,20},{20,16},{24,28},{28,24},{1,5},{5... | collective-permute-start | bytes 405512 | tf_op jit(solution)/shard_map/ppermute | solution.py:722
  13.1 0.0 collective-permute-start.1
  13.1 1.5 %collective-permute-start.2 = (bf16[528,128]{1,0:T(8,128)(2,1)S(1)}, bf16[528,128]{1,0:T(8,128)(2,1)S(1)}, u32[]{:S(2)}, u32[]{:S(2)}) collective-permute-start(bf16[528,128]{1,0:T(8,128)(2,1)S(1)} %get-tuple-element.37), channel_id=1, source_target_pairs={{0,12},{4,8},{8,4},{12,0},{16,28},{20,24},{24,20},{28,16},{1,13},{... | collective-permute-start | bytes 405512 | tf_op jit(solution)/shard_map/ppermute | solution.py:722
  14.6 1.9 %attend.4 = (bf16[2,2048,256]{2,1,0:T(8,128)(2,1)S(1)}, f32[2,144,2048]{2,1,0:T(8,128)S(1)}) custom-call(s32[1]{0:T(128)} %bitcast.1.refs_0_, f32[16,128]{1,0:T(8,128)S(1)} %get-tuple-element.30.refs_3_.refs_1_, bf16[4096,128]{1,0:T(8,128)(2,1)S(1)} %get-tuple-element.38.refs_2_, bf16[1040,128]{1,0:T(8,128)(2,1)S(1)} %get-tuple-element.39.refs_3_, ...), custom_call_target="tpu_custom_call" | custom-call | flops 1073741824 | bytes 8388608 | tf_op jit(solution)/shard_map/attend/pallas_call | solution.py:68
  16.5 0.0 collective-permute-done.3.refs_6_
  16.5 0.0 copy-done
  16.5 1.9 %inner_part.2 = (f32[2048,128]{1,0:T(8,128)S(1)}, bf16[2048,128]{1,0:T(8,128)(2,1)S(1)}, bf16[1040,128]{1,0:T(8,128)(2,1)S(1)}) custom-call(f32[256,128]{1,0:T(8,128)S(1)} %get-tuple-element.31.refs_2_.refs_0_.refs_3_, f32[16,128]{1,0:T(8,128)S(1)} %get-tuple-element.30.refs_3_.refs_1_, bf16[4096,128]{1,0:T(8,128)(2,1)S(1)} %bitcast.13, ...), custom_call_target="tpu_custom_call" | custom-call | flops 268435456 | bytes 6291456 | tf_op jit(solution)/shard_map/inner_part/pallas_call | solution.py:68
  18.5 1.7 %collective-permute-start.10 = (bf16[1040,128]{1,0:T(8,128)(2,1)S(1)}, bf16[1040,128]{1,0:T(8,128)(2,1)S(1)}, u32[]{:S(2)}, u32[]{:S(2)}) collective-permute-start(bf16[1040,128]{1,0:T(8,128)(2,1)S(1)} %get-tuple-element.42.refs_7_), channel_id=1, source_target_pairs={{0,8},{4,12},{8,16},{12,20},{16,24},{20,28},{24,0},{28,4},{1,9},{5... | collective-permute-start | bytes 798728 | tf_op jit(solution)/shard_map/ppermute | solution.py:722
  20.2 1.9 %collective-permute-done.refs_2_ = bf16[528,128]{1,0:T(8,128)(2,1)S(1)} collective-permute-done((bf16[528,128]{1,0:T(8,128)(2,1)S(1)}, bf16[528,128]{1,0:T(8,128)(2,1)S(1)}, u32[]{:S(2)}, u32[]{:S(2)}) %collective-permute-start) | collective-permute-done | bytes 135200 | tf_op jit(solution)/shard_map/ppermute | solution.py:722
  22.1 0.0 collective-permute-done.1.refs_3_
  22.1 5.5 %collective-permute-done.2.refs_4_ = bf16[528,128]{1,0:T(8,128)(2,1)S(1)} collective-permute-done((bf16[528,128]{1,0:T(8,128)(2,1)S(1)}, bf16[528,128]{1,0:T(8,128)(2,1)S(1)}, u32[]{:S(2)}, u32[]{:S(2)}) %collective-permute-start.2) | collective-permute-done | bytes 135200 | tf_op jit(solution)/shard_map/ppermute | solution.py:722
  27.6 0.0 collective-permute-done.4.refs_6_.refs_3_
  27.6 0.2 group_map.1
  27.8 0.1 collective-permute-start.9
  27.9 0.7 %collective-permute-start.5 = (bf16[528,128]{1,0:T(8,128)(2,1)S(1)}, bf16[528,128]{1,0:T(8,128)(2,1)S(1)}, u32[]{:S(2)}, u32[]{:S(2)}) collective-permute-start(bf16[528,128]{1,0:T(8,128)(2,1)S(1)} %get-tuple-element.43.refs_5_), channel_id=1, source_target_pairs={{0,16},{4,20},{8,24},{12,28},{16,0},{20,4},{24,8},{28,12},{1,17},{... | collective-permute-start | bytes 405512 | tf_op jit(solution)/shard_map/ppermute | solution.py:722
  28.6 3.3 %attend.5.refs_5_.refs_2_ = f32[2,144,2048]{2,1,0:T(8,128)S(1)} custom-call(s32[1]{0:T(128)} %bitcast.1.refs_0_, bf16[2,2048,256]{2,1,0:T(8,128)(2,1)S(1)} %get-tuple-element.44.refs_1_, f32[2,144,2048]{2,1,0:T(8,128)S(1)} %get-tuple-element.40.refs_5_.refs_2_, bf16[1040,128]{1,0:T(8,128)(2,1)S(1)} %collective-permute-done.4.refs_6_.refs_3_, ...), custom_call_target="tpu_custom_call" | custom-call | flops 2147483648 | bytes 8388608 | tf_op jit(solution)/shard_map/attend/pallas_call | solution.py:68
  31.9 1.9 %inner_part.3 = (f32[2048,128]{1,0:T(8,128)S(1)}, bf16[2048,128]{1,0:T(8,128)(2,1)S(1)}) custom-call(f32[256,128]{1,0:T(8,128)S(1)} %get-tuple-element.31.refs_2_.refs_0_.refs_3_, f32[16,128]{1,0:T(8,128)S(1)} %get-tuple-element.30.refs_3_.refs_1_, bf16[4096,128]{1,0:T(8,128)(2,1)S(1)} %bitcast.14, bf16[4096,128]{1,0:T(8,128)(2,1)S(1)} %get-tuple-element.32.refs_4_.refs_3_, ...), custom_call_target="tpu_custom_call" | custom-call | flops 268435456 | bytes 6291456 | tf_op jit(solution)/shard_map/inner_part/pallas_call | solution.py:68
  33.8 2.1 %collective-permute-done.5.refs_5_ = bf16[528,128]{1,0:T(8,128)(2,1)S(1)} collective-permute-done((bf16[528,128]{1,0:T(8,128)(2,1)S(1)}, bf16[528,128]{1,0:T(8,128)(2,1)S(1)}, u32[]{:S(2)}, u32[]{:S(2)}) %collective-permute-start.5) | collective-permute-done | bytes 135200 | tf_op jit(solution)/shard_map/ppermute | solution.py:722
  35.9 0.3 prior_states.1
  36.1 2.9 %collective-permute-start.6 = (bf16[512,128]{1,0:T(8,128)(2,1)S(1)}, bf16[512,128]{1,0:T(8,128)(2,1)S(1)}, u32[]{:S(2)}, u32[]{:S(2)}) collective-permute-start(bf16[512,128]{1,0:T(8,128)(2,1)S(1)} %get-tuple-element.51), channel_id=1, source_target_pairs={{0,4},{4,0},{8,12},{12,8},{16,20},{20,16},{24,28},{28,24},{1,5},{5... | collective-permute-start | bytes 393224 | tf_op jit(solution)/shard_map/ppermute | solution.py:722
  39.0 0.0 collective-permute-start.7
  39.0 1.5 %collective-permute-start.8 = (bf16[512,128]{1,0:T(8,128)(2,1)S(1)}, bf16[512,128]{1,0:T(8,128)(2,1)S(1)}, u32[]{:S(2)}, u32[]{:S(2)}) collective-permute-start(bf16[512,128]{1,0:T(8,128)(2,1)S(1)} %get-tuple-element.53), channel_id=1, source_target_pairs={{0,12},{4,8},{8,4},{12,0},{16,28},{20,24},{24,20},{28,16},{1,13},{... | collective-permute-start | bytes 393224 | tf_op jit(solution)/shard_map/ppermute | solution.py:722
  40.5 0.0 collective-permute-done.10.refs_4_.refs_5_
  40.5 0.0 collective-permute-done.9.refs_3_
  40.5 3.3 %attend.6.refs_12_.refs_0_.refs_2_ = f32[2,144,2048]{2,1,0:T(8,128)S(1)} custom-call(s32[1]{0:T(128)} %bitcast.1.refs_0_, bf16[2,2048,256]{2,1,0:T(8,128)(2,1)S(1)} %get-tuple-element.44.refs_1_, f32[2,144,2048]{2,1,0:T(8,128)S(1)} %attend.5.refs_5_.refs_2_, bf16[1040,128]{1,0:T(8,128)(2,1)S(1)} %collective-permute-done.9.refs_3_, ...), custom_call_target="tpu_custom_call" | custom-call | flops 2147483648 | bytes 8388608 | tf_op jit(solution)/shard_map/attend/pallas_call | solution.py:68
  43.8 0.0 collective-permute-done.6.refs_9_.refs_2_
  43.8 1.5 %collective-permute-done.7.refs_10_.refs_3_ = bf16[512,128]{1,0:T(8,128)(2,1)S(1)} collective-permute-done((bf16[512,128]{1,0:T(8,128)(2,1)S(1)}, bf16[512,128]{1,0:T(8,128)(2,1)S(1)}, u32[]{:S(2)}, u32[]{:S(2)}) %collective-permute-start.7) | collective-permute-done | bytes 131104 | tf_op jit(solution)/shard_map/ppermute | solution.py:722
  45.4 1.3 %collective-permute-done.8.refs_11_.refs_4_ = bf16[512,128]{1,0:T(8,128)(2,1)S(1)} collective-permute-done((bf16[512,128]{1,0:T(8,128)(2,1)S(1)}, bf16[512,128]{1,0:T(8,128)(2,1)S(1)}, u32[]{:S(2)}, u32[]{:S(2)}) %collective-permute-start.8) | collective-permute-done | bytes 131104 | tf_op jit(solution)/shard_map/ppermute | solution.py:722
  46.7 1.7 %collective-permute-start.14 = (bf16[1040,128]{1,0:T(8,128)(2,1)S(1)}, bf16[1040,128]{1,0:T(8,128)(2,1)S(1)}, u32[]{:S(2)}, u32[]{:S(2)}) collective-permute-start(bf16[1040,128]{1,0:T(8,128)(2,1)S(1)} %pass_on.1), channel_id=1, source_target_pairs={{0,4},{4,0},{8,12},{12,8},{16,20},{20,16},{24,28},{28,24},{1,5},{5... | collective-permute-start | bytes 798728 | tf_op jit(solution)/shard_map/ppermute | solution.py:722
  48.5 1.6 %mix.1 = (f32[4096,128]{1,0:T(8,128)S(1)}, f32[8,256]{1,0:T(8,128)S(1)}) custom-call(s32[1]{0:T(128)} %bitcast.1.refs_0_, f32[16,128]{1,0:T(8,128)S(1)} %get-tuple-element.30.refs_3_.refs_1_, f32[8,128]{1,0:T(8,128)S(1)} %get-tuple-element.47.refs_5_.refs_2_, f32[256,128]{1,0:T(8,128)S(1)} %get-tuple-element.31.refs_2_.refs_0_.refs_3_, ...), custom_call_target="tpu_custom_call" | custom-call | flops 134217728 | bytes 5242880 | tf_op jit(solution)/shard_map/mix/pallas_call | solution.py:68
  50.1 0.0 copy-start.1
  50.1 0.0 copy-start.2
  50.1 0.0 collective-permute-start.13
  50.1 1.6 %collective-permute-start.12 = (f32[8,256]{1,0:T(8,128)S(1)}, f32[8,256]{1,0:T(8,128)S(1)}, u32[]{:S(2)}, u32[]{:S(2)}) collective-permute-start(f32[8,256]{1,0:T(8,128)S(1)} %get-tuple-element.55.refs_4_.refs_3_), channel_id=1, source_target_pairs={{0,2},{1,3},{2,0},{3,1},{4,6},{5,7},{6,4},{7,5},{8,10},{9,11},{10,... | collective-permute-start | bytes 24584 | tf_op jit(solution)/shard_map/ppermute | solution.py:812
  51.7 0.3 collective-permute-start.11
  52.0 2.3 %collective-permute-done.14.refs_3_ = bf16[1040,128]{1,0:T(8,128)(2,1)S(1)} collective-permute-done((bf16[1040,128]{1,0:T(8,128)(2,1)S(1)}, bf16[1040,128]{1,0:T(8,128)(2,1)S(1)}, u32[]{:S(2)}, u32[]{:S(2)}) %collective-permute-start.14) | collective-permute-done | bytes 266272 | tf_op jit(solution)/shard_map/ppermute | solution.py:722
  54.3 2.8 %attend.7 = (bf16[4096,128]{1,0:T(8,128)(2,1)}, f32[8,128]{1,0:T(8,128)S(1)}) custom-call(s32[1]{0:T(128)} %bitcast.1.refs_0_, bf16[2,2048,256]{2,1,0:T(8,128)(2,1)S(1)} %get-tuple-element.44.refs_1_, f32[2,144,2048]{2,1,0:T(8,128)S(1)} %attend.6.refs_12_.refs_0_.refs_2_, bf16[1040,128]{1,0:T(8,128)(2,1)S(1)} %collective-permute-done.14.refs_3_, ...), custom_call_target="tpu_custom_call" | custom-call | flops 1073741824 | bytes 8388608 | tf_op jit(solution)/shard_map/attend/pallas_call | solution.py:68
  57.1 0.0 collective-permute-done.13.refs_6_
  57.1 0.0 collective-permute-done.12.refs_5_
  57.1 0.0 collective-permute-done.11.refs_4_
  57.2 0.0 copy-done.1
  57.2 0.0 copy-done.2
  57.2 1.6 %finish.1 = bf16[4096,128]{1,0:T(8,128)(2,1)} custom-call(f32[16,128]{1,0:T(8,128)S(1)} %copy-done.2, bf16[4096,128]{1,0:T(8,128)(2,1)S(1)} %bitcast.15, f32[4096,128]{1,0:T(8,128)S(1)} %get-tuple-element.54.refs_2_, f32[8,256]{1,0:T(8,128)S(1)} %get-tuple-element.55.refs_4_.refs_3_, f32[8,256]{1,0:T(8,128)S(1)} %collective-permute-done.11.refs_4_, ...), custom_call_target="tpu_custom_call" | custom-call | bytes 4194304 | tf_op jit(solution)/shard_map/finish/pallas_call | solution.py:68
  (1 shorter events, 0.0 us)
Async XLA Ops:
  2.6 13.9 %collective-permute-start.3 = (bf16[1040,128]{1,0:T(8,128)(2,1)S(1)}, bf16[1040,128]{1,0:T(8,128)(2,1)S(1)}, u32[]{:S(2)}, u32[]{:S(2)}) collective-permute-start(bf16[1040,128]{1,0:T(8,128)(2,1)S(1)} %get-tuple-element.39.refs_3_), channel_id=1, source_target_pairs={{0,8},{4,12},{8,16},{12,20},{16,24},{20,28},{24,0},{28,4},{1,9},{5... | collective-permute-start | bytes 798728 | tf_op jit(solution)/shard_map/ppermute | solution.py:722
  5.7 21.9 %collective-permute-start.4 = (bf16[1040,128]{1,0:T(8,128)(2,1)S(1)}, bf16[1040,128]{1,0:T(8,128)(2,1)S(1)}, u32[]{:S(2)}, u32[]{:S(2)}) collective-permute-start(bf16[1040,128]{1,0:T(8,128)(2,1)S(1)} %get-tuple-element.39.refs_3_), channel_id=1, source_target_pairs={{0,4},{4,24},{8,12},{12,8},{16,20},{20,16},{24,28},{28,0},{1,5},{5... | collective-permute-start | bytes 798728 | tf_op jit(solution)/shard_map/ppermute | solution.py:722
  11.0 5.6 %copy-start = (bf16[256,16,128]{2,1,0:T(8,128)(2,1)S(1)}, bf16[256,16,128]{2,1,0:T(8,128)(2,1)}, u32[]{:S(2)}) copy-start(bf16[256,16,128]{2,1,0:T(8,128)(2,1)} %param.10) | copy-start | bytes 3145732
  11.0 11.1 %collective-permute-start = (bf16[528,128]{1,0:T(8,128)(2,1)S(1)}, bf16[528,128]{1,0:T(8,128)(2,1)S(1)}, u32[]{:S(2)}, u32[]{:S(2)}) collective-permute-start(bf16[528,128]{1,0:T(8,128)(2,1)S(1)} %get-tuple-element.35), channel_id=1, source_target_pairs={{0,4},{4,0},{8,12},{12,8},{16,20},{20,16},{24,28},{28,24},{1,5},{5... | collective-permute-start | bytes 405512 | tf_op jit(solution)/shard_map/ppermute | solution.py:722
  13.1 9.0 %collective-permute-start.1 = (bf16[528,128]{1,0:T(8,128)(2,1)S(1)}, bf16[528,128]{1,0:T(8,128)(2,1)S(1)}, u32[]{:S(2)}, u32[]{:S(2)}) collective-permute-start(bf16[528,128]{1,0:T(8,128)(2,1)S(1)} %get-tuple-element.36), channel_id=1, source_target_pairs={{0,8},{4,12},{8,0},{12,4},{16,24},{20,28},{24,16},{28,20},{1,9},{5... | collective-permute-start | bytes 405512 | tf_op jit(solution)/shard_map/ppermute | solution.py:722
  13.1 14.5 %collective-permute-start.2 = (bf16[528,128]{1,0:T(8,128)(2,1)S(1)}, bf16[528,128]{1,0:T(8,128)(2,1)S(1)}, u32[]{:S(2)}, u32[]{:S(2)}) collective-permute-start(bf16[528,128]{1,0:T(8,128)(2,1)S(1)} %get-tuple-element.37), channel_id=1, source_target_pairs={{0,12},{4,8},{8,4},{12,0},{16,28},{20,24},{24,20},{28,16},{1,13},{... | collective-permute-start | bytes 405512 | tf_op jit(solution)/shard_map/ppermute | solution.py:722
  18.5 22.1 %collective-permute-start.10 = (bf16[1040,128]{1,0:T(8,128)(2,1)S(1)}, bf16[1040,128]{1,0:T(8,128)(2,1)S(1)}, u32[]{:S(2)}, u32[]{:S(2)}) collective-permute-start(bf16[1040,128]{1,0:T(8,128)(2,1)S(1)} %get-tuple-element.42.refs_7_), channel_id=1, source_target_pairs={{0,8},{4,12},{8,16},{12,20},{16,24},{20,28},{24,0},{28,4},{1,9},{5... | collective-permute-start | bytes 798728 | tf_op jit(solution)/shard_map/ppermute | solution.py:722
  27.8 12.7 %collective-permute-start.9 = (bf16[1040,128]{1,0:T(8,128)(2,1)S(1)}, bf16[1040,128]{1,0:T(8,128)(2,1)S(1)}, u32[]{:S(2)}, u32[]{:S(2)}) collective-permute-start(bf16[1040,128]{1,0:T(8,128)(2,1)S(1)} %get-tuple-element.45.refs_4_), channel_id=1, source_target_pairs={{0,4},{4,0},{8,12},{12,8},{16,20},{20,16},{24,28},{28,24},{1,5},{5... | collective-permute-start | bytes 798728 | tf_op jit(solution)/shard_map/ppermute | solution.py:722
  27.9 8.0 %collective-permute-start.5 = (bf16[528,128]{1,0:T(8,128)(2,1)S(1)}, bf16[528,128]{1,0:T(8,128)(2,1)S(1)}, u32[]{:S(2)}, u32[]{:S(2)}) collective-permute-start(bf16[528,128]{1,0:T(8,128)(2,1)S(1)} %get-tuple-element.43.refs_5_), channel_id=1, source_target_pairs={{0,16},{4,20},{8,24},{12,28},{16,0},{20,4},{24,8},{28,12},{1,17},{... | collective-permute-start | bytes 405512 | tf_op jit(solution)/shard_map/ppermute | solution.py:722
  36.1 7.7 %collective-permute-start.6 = (bf16[512,128]{1,0:T(8,128)(2,1)S(1)}, bf16[512,128]{1,0:T(8,128)(2,1)S(1)}, u32[]{:S(2)}, u32[]{:S(2)}) collective-permute-start(bf16[512,128]{1,0:T(8,128)(2,1)S(1)} %get-tuple-element.51), channel_id=1, source_target_pairs={{0,4},{4,0},{8,12},{12,8},{16,20},{20,16},{24,28},{28,24},{1,5},{5... | collective-permute-start | bytes 393224 | tf_op jit(solution)/shard_map/ppermute | solution.py:722
  39.0 6.4 %collective-permute-start.7 = (bf16[512,128]{1,0:T(8,128)(2,1)S(1)}, bf16[512,128]{1,0:T(8,128)(2,1)S(1)}, u32[]{:S(2)}, u32[]{:S(2)}) collective-permute-start(bf16[512,128]{1,0:T(8,128)(2,1)S(1)} %get-tuple-element.52), channel_id=1, source_target_pairs={{0,8},{4,12},{8,0},{12,4},{16,24},{20,28},{24,16},{28,20},{1,9},{5... | collective-permute-start | bytes 393224 | tf_op jit(solution)/shard_map/ppermute | solution.py:722
  39.0 7.7 %collective-permute-start.8 = (bf16[512,128]{1,0:T(8,128)(2,1)S(1)}, bf16[512,128]{1,0:T(8,128)(2,1)S(1)}, u32[]{:S(2)}, u32[]{:S(2)}) collective-permute-start(bf16[512,128]{1,0:T(8,128)(2,1)S(1)} %get-tuple-element.53), channel_id=1, source_target_pairs={{0,12},{4,8},{8,4},{12,0},{16,28},{20,24},{24,20},{28,16},{1,13},{... | collective-permute-start | bytes 393224 | tf_op jit(solution)/shard_map/ppermute | solution.py:722
  46.7 7.5 %collective-permute-start.14 = (bf16[1040,128]{1,0:T(8,128)(2,1)S(1)}, bf16[1040,128]{1,0:T(8,128)(2,1)S(1)}, u32[]{:S(2)}, u32[]{:S(2)}) collective-permute-start(bf16[1040,128]{1,0:T(8,128)(2,1)S(1)} %pass_on.1), channel_id=1, source_target_pairs={{0,4},{4,0},{8,12},{12,8},{16,20},{20,16},{24,28},{28,24},{1,5},{5... | collective-permute-start | bytes 798728 | tf_op jit(solution)/shard_map/ppermute | solution.py:722
  50.1 7.1 %copy-start.1 = (bf16[256,16,128]{2,1,0:T(8,128)(2,1)S(1)}, bf16[256,16,128]{2,1,0:T(8,128)(2,1)}, u32[]{:S(2)}) copy-start(bf16[256,16,128]{2,1,0:T(8,128)(2,1)} %param.13) | copy-start | bytes 3145732
  50.1 7.1 %copy-start.2 = (f32[16,128]{1,0:T(8,128)S(1)}, f32[16,128]{1,0:T(8,128)}, u32[]{:S(2)}) copy-start(f32[16,128]{1,0:T(8,128)} %refs_0_.1) | copy-start | bytes 24580
  50.1 7.1 %collective-permute-start.13 = (f32[8,256]{1,0:T(8,128)S(1)}, f32[8,256]{1,0:T(8,128)S(1)}, u32[]{:S(2)}, u32[]{:S(2)}) collective-permute-start(f32[8,256]{1,0:T(8,128)S(1)} %get-tuple-element.55.refs_4_.refs_3_), channel_id=1, source_target_pairs={{0,3},{1,2},{2,1},{3,0},{4,7},{5,6},{6,5},{7,4},{8,11},{9,10},{10,... | collective-permute-start | bytes 24584 | tf_op jit(solution)/shard_map/ppermute | solution.py:812
  50.1 7.0 %collective-permute-start.12 = (f32[8,256]{1,0:T(8,128)S(1)}, f32[8,256]{1,0:T(8,128)S(1)}, u32[]{:S(2)}, u32[]{:S(2)}) collective-permute-start(f32[8,256]{1,0:T(8,128)S(1)} %get-tuple-element.55.refs_4_.refs_3_), channel_id=1, source_target_pairs={{0,2},{1,3},{2,0},{3,1},{4,6},{5,7},{6,4},{7,5},{8,10},{9,11},{10,... | collective-permute-start | bytes 24584 | tf_op jit(solution)/shard_map/ppermute | solution.py:812
  51.7 5.5 %collective-permute-start.11 = (f32[8,256]{1,0:T(8,128)S(1)}, f32[8,256]{1,0:T(8,128)S(1)}, u32[]{:S(2)}, u32[]{:S(2)}) collective-permute-start(f32[8,256]{1,0:T(8,128)S(1)} %get-tuple-element.55.refs_4_.refs_3_), channel_id=1, source_target_pairs={{0,1},{1,0},{2,3},{3,2},{4,5},{5,4},{6,7},{7,6},{8,9},{9,8},{10,11... | collective-permute-start | bytes 24584 | tf_op jit(solution)/shard_map/ppermute | solution.py:812

commit v17 on v16

--- a/solution.py
+++ b/solution.py
@@ -96,8 +96,16 @@
     return rows >= cols
 
 
-def pass_on(x, after):
-    return call(lambda: None, "pass_on", [], [], (), after=after, relay=[x])[0]
+def pick_kernel(place_ref, even_ref, odd_ref, out_ref):
+    out_ref[...] = jnp.where(place_ref[0] % 2 == 0, even_ref[...], odd_ref[...])
+
+
+def pick(place, even, odd, after):
+    return call(pick_kernel, "pick", [place], [even, odd], sds(even.shape, BF16), after=after)
+
+
+def pass_on(arrays, after):
+    return call(lambda: None, "pass_on", [], [], (), after=after, relay=arrays)
 
 
 def fetch_kernel(tokens, heads, kv_here, start_ref, *refs):
@@ -740,13 +748,7 @@
     )
 
     forward = [(b, b + 2) for b in everyone]
-    hop = {b: b ^ 1 for b in everyone}
-    if window % 2:
-        for b in range(1, blocks - window, 2):
-            last = next(a for a in everyone if hop[a] == b + window)
-            hop[b], hop[last] = b + window, hop[b]
     ahead = send(own_kv, forward)
-    beside = (send(own_kv, list(hop.items())), (window if window % 2 else blocks, 1))
 
     size = quarter_rows(heads)
     others = range(1, GROUP_BLOCKS)
@@ -784,15 +786,16 @@
     done, lane = first_attention([sent[0]]), ahead
     if parts > 1:
         done, lane = inner_of(0, [done], [ahead])
-    second = send(lane, forward)
-    run, lane = group_map(place, quarters, size, [done, beside[0]], [lane])
+    second = send(lane, [(b, b + 2) for b in range(2, blocks - 2)])
+    run, lane, own_copy = group_map(place, quarters, size, [done], [lane, own_kv])
     first_cross = send(lane, swap)
+    beside = send(own_copy, swap)
     stages = (blocks // GROUP_BLOCKS).bit_length() - 1
     before, done = None, run
     for stage in range(stages):
         came = send(run, [(b, b ^ (GROUP_BLOCKS << stage)) for b in everyone])
         if stage == stages - 1:
-            done = more_attention([beside, (lane, (2, 2))], False, [done])
+            done = more_attention([(lane, (2, 2))], False, [done])
             done = inner_of(parts - 1, [done])
         else:
             run, before = scan_step(place, stage + 2, run, came, before, size, [done])
@@ -800,8 +803,11 @@
     *priors, prior_doc = prior_states(place, stages + 1, quarters, came, before, size, [done])
     priors = [priors[0]] + [send(priors[j], [(b, b ^ j) for b in everyone]) for j in others]
     done = more_attention([(first_cross, (2, 3)), (second, (4, 4))], False, [prior_doc])
-    lane = pass_on(second, [done, *priors])
-    rest = [(send(lane, swap), (4, 5))]
+    lane, own_copy = pass_on([second, own_kv], [done, *priors])
+    rest = [(send(lane, [(b, b ^ 1) for b in range(4, blocks)]), (4, 5))]
+    far = None
+    if window % 2:
+        far = send(own_copy, [(b, b + window) for b in range(1, blocks - window, 2)])
     for back in range(3, window // 2 + 1):
         lane = send(lane, forward)
         rest.append((lane, (2 * back, 2 * back)))
@@ -810,6 +816,8 @@
     sums = [squares]
     for other in range(1, tensor):
         sums.append(lax.ppermute(squares, "tp", [(t, t ^ other) for t in range(tensor)]))
+    slot = beside if far is None else pick(place, far, beside, [squares])
+    rest.insert(0, (slot, (blocks if far is None else window, 1)))
     done = squares
     while rest:
         got = more_attention(rest[:2], len(rest) <= 2, [done])

time: 59.2 us -> 57.9 us (0.978)
  the two profiles are of different devices: /device:TPU:0 before, /device:TPU:26 now
where the time goes in v17:
time: 57.9 us; the launch traced here: 57.7 us
  Pallas kernels  24.7 us (43%)
  starting transfers between devices  19.1 us (33%)
  waiting for transfers between devices  12.8 us (22%)
  between operations  1.04 us (2%)
    pallas_call x14, Pallas kernels, call(): pl.pallas_call(run, out_shape=outs, in_specs=[SMEM] * len(scalars) + [HBM...  24.7 us
    ppermute x13, starting transfers between devices, send(): return lax.ppermute(x, 'seq', [(a, b % blocks) for a, b in pairs])  17.2 us
    ppermute x13, waiting for transfers between devices, send(): return lax.ppermute(x, 'seq', [(a, b % blocks) for a, b in pairs])  12.8 us
    ppermute x3, starting transfers between devices, body(): lax.ppermute(squares, 'tp', [(t, t ^ other) for t in range(tensor)])  1.89 us
  transfers between devices with their start and end apart: 16, of which 5 were waited for; matrix products, arithmetic and copies ran while one was open for 0% of the time, Pallas kernels for 37%

profile of v17, /device:TPU:26, one launch (start us, length us, event | category | flops | bytes accessed | tf_op | source)
XLA Modules:
  0.0 57.7 jit_solution(6431373219747279643)
XLA Ops:
  0.6 1.9 %fetch.1 = (bf16[1040,128]{1,0:T(8,128)(2,1)S(1)}, f32[16,128]{1,0:T(8,128)S(1)}, f32[256,128]{1,0:T(8,128)S(1)}, bf16[4096,128]{1,0:T(8,128)(2,1)S(1)}, bf16[4096,128]{1,0:T(8,128)(2,1)S(1)}) custom-call(s32[1]{0:T(128)} %bitcast.2.refs_0_, s32[2,128]{1,0:T(2,128)} %bitcast.23, f32[16,256]{1,0:T(8,128)} %bitcast.22, bf16[2048,128]{1,0:T(8,128)(2,1)} %bitcast.20, ...), custom_call_target="tpu_custom_call" | custom-call | bytes 3145728 | tf_op jit(solution)/shard_map/fetch/pallas_call | solution.py:68
  2.6 0.3 collective-permute-start.3
  2.9 3.8 %block_state.1 = (bf16[528,128]{1,0:T(8,128)(2,1)S(1)}, bf16[528,128]{1,0:T(8,128)(2,1)S(1)}, bf16[528,128]{1,0:T(8,128)(2,1)S(1)}, bf16[528,128]{1,0:T(8,128)(2,1)S(1)}, bf16[4096,128]{1,0:T(8,128)(2,1)S(1)}) custom-call(s32[1]{0:T(128)} %bitcast.1.refs_0_, bf16[4096,128]{1,0:T(8,128)(2,1)} %bitcast.19, ...), custom_call_target="tpu_custom_call" | custom-call | flops 134217728 | bytes 5242880 | tf_op jit(solution)/shard_map/block_state/pallas_call | solution.py:68
  6.6 0.0 copy-start
  6.6 1.6 %collective-permute-start = (bf16[528,128]{1,0:T(8,128)(2,1)S(1)}, bf16[528,128]{1,0:T(8,128)(2,1)S(1)}, u32[]{:S(2)}, u32[]{:S(2)}) collective-permute-start(bf16[528,128]{1,0:T(8,128)(2,1)S(1)} %get-tuple-element.38), channel_id=1, source_target_pairs={{0,4},{4,0},{8,12},{12,8},{16,20},{20,16},{24,28},{28,24},{1,5},{5... | collective-permute-start | bytes 405512 | tf_op jit(solution)/shard_map/ppermute | solution.py:730
  8.2 1.8 %collective-permute-start.1 = (bf16[528,128]{1,0:T(8,128)(2,1)S(1)}, bf16[528,128]{1,0:T(8,128)(2,1)S(1)}, u32[]{:S(2)}, u32[]{:S(2)}) collective-permute-start(bf16[528,128]{1,0:T(8,128)(2,1)S(1)} %get-tuple-element.39), channel_id=1, source_target_pairs={{0,8},{4,12},{8,0},{12,4},{16,24},{20,28},{24,16},{28,20},{1,9},{5... | collective-permute-start | bytes 405512 | tf_op jit(solution)/shard_map/ppermute | solution.py:730
  10.0 0.2 collective-permute-start.2
  10.2 1.9 %attend.4 = (bf16[2,2048,256]{2,1,0:T(8,128)(2,1)S(1)}, f32[2,144,2048]{2,1,0:T(8,128)S(1)}) custom-call(s32[1]{0:T(128)} %bitcast.1.refs_0_, f32[16,128]{1,0:T(8,128)S(1)} %get-tuple-element.33.refs_3_.refs_1_, bf16[4096,128]{1,0:T(8,128)(2,1)S(1)} %get-tuple-element.41.refs_2_, bf16[1040,128]{1,0:T(8,128)(2,1)S(1)} %get-tuple-element.42.refs_3_.refs_7_.refs_6_, ...), custom_call_target="tpu_custom_call" | custom-call | flops 1073741824 | bytes 8388608 | tf_op jit(solution)/shard_map/attend/pallas_call | solution.py:68
  12.1 0.0 collective-permute-done.3.refs_6_
  12.1 1.9 %inner_part.2 = (f32[2048,128]{1,0:T(8,128)S(1)}, bf16[2048,128]{1,0:T(8,128)(2,1)S(1)}, bf16[1040,128]{1,0:T(8,128)(2,1)S(1)}) custom-call(f32[256,128]{1,0:T(8,128)S(1)} %get-tuple-element.34.refs_2_.refs_0_.refs_3_, f32[16,128]{1,0:T(8,128)S(1)} %get-tuple-element.33.refs_3_.refs_1_, bf16[4096,128]{1,0:T(8,128)(2,1)S(1)} %bitcast.13, ...), custom_call_target="tpu_custom_call" | custom-call | flops 268435456 | bytes 6291456 | tf_op jit(solution)/shard_map/inner_part/pallas_call | solution.py:68
  14.1 1.5 %collective-permute-start.9 = (bf16[1040,128]{1,0:T(8,128)(2,1)S(1)}, bf16[1040,128]{1,0:T(8,128)(2,1)S(1)}, u32[]{:S(2)}, u32[]{:S(2)}) collective-permute-start(bf16[1040,128]{1,0:T(8,128)(2,1)S(1)} %get-tuple-element.45.refs_6_), channel_id=1, source_target_pairs={{8,16},{12,20},{16,24},{20,28},{9,17},{13,21},{17,25},{21,29},{10,... | collective-permute-start | bytes 798728 | tf_op jit(solution)/shard_map/ppermute | solution.py:730
  15.5 0.0 collective-permute-done.refs_2_
  15.5 0.0 collective-permute-done.1.refs_3_
  15.6 2.0 %collective-permute-done.2.refs_4_ = bf16[528,128]{1,0:T(8,128)(2,1)S(1)} collective-permute-done((bf16[528,128]{1,0:T(8,128)(2,1)S(1)}, bf16[528,128]{1,0:T(8,128)(2,1)S(1)}, u32[]{:S(2)}, u32[]{:S(2)}) %collective-permute-start.2) | collective-permute-done | bytes 135200 | tf_op jit(solution)/shard_map/ppermute | solution.py:730
  17.5 0.2 group_map.1
  17.8 0.6 collective-permute-start.8
  18.3 2.9 %collective-permute-start.4 = (bf16[528,128]{1,0:T(8,128)(2,1)S(1)}, bf16[528,128]{1,0:T(8,128)(2,1)S(1)}, u32[]{:S(2)}, u32[]{:S(2)}) collective-permute-start(bf16[528,128]{1,0:T(8,128)(2,1)S(1)} %get-tuple-element.46.refs_4_), channel_id=1, source_target_pairs={{0,16},{4,20},{8,24},{12,28},{16,0},{20,4},{24,8},{28,12},{1,17},{... | collective-permute-start | bytes 405512 | tf_op jit(solution)/shard_map/ppermute | solution.py:730
  21.3 0.5 collective-permute-start.14
  21.8 1.9 %attend.5.refs_5_.refs_2_ = f32[2,144,2048]{2,1,0:T(8,128)S(1)} custom-call(s32[1]{0:T(128)} %bitcast.1.refs_0_, bf16[2,2048,256]{2,1,0:T(8,128)(2,1)S(1)} %get-tuple-element.47.refs_1_, f32[2,144,2048]{2,1,0:T(8,128)S(1)} %get-tuple-element.43.refs_5_.refs_2_, bf16[1040,128]{1,0:T(8,128)(2,1)S(1)} %get-tuple-element.48.refs_3_, ...), custom_call_target="tpu_custom_call" | custom-call | flops 1073741824 | bytes 8388608 | tf_op jit(solution)/shard_map/attend/pallas_call | solution.py:68
  23.7 1.9 %inner_part.3 = (f32[2048,128]{1,0:T(8,128)S(1)}, bf16[2048,128]{1,0:T(8,128)(2,1)S(1)}) custom-call(f32[256,128]{1,0:T(8,128)S(1)} %get-tuple-element.34.refs_2_.refs_0_.refs_3_, f32[16,128]{1,0:T(8,128)S(1)} %get-tuple-element.33.refs_3_.refs_1_, bf16[4096,128]{1,0:T(8,128)(2,1)S(1)} %bitcast.14, bf16[4096,128]{1,0:T(8,128)(2,1)S(1)} %get-tuple-element.35.refs_4_.refs_3_, ...), custom_call_target="tpu_custom_call" | custom-call | flops 268435456 | bytes 6291456 | tf_op jit(solution)/shard_map/inner_part/pallas_call | solution.py:68
  25.6 4.4 %collective-permute-done.4.refs_5_ = bf16[528,128]{1,0:T(8,128)(2,1)S(1)} collective-permute-done((bf16[528,128]{1,0:T(8,128)(2,1)S(1)}, bf16[528,128]{1,0:T(8,128)(2,1)S(1)}, u32[]{:S(2)}, u32[]{:S(2)}) %collective-permute-start.4) | collective-permute-done | bytes 135200 | tf_op jit(solution)/shard_map/ppermute | solution.py:730
  30.0 0.3 prior_states.1
  30.3 1.6 %collective-permute-start.5 = (bf16[512,128]{1,0:T(8,128)(2,1)S(1)}, bf16[512,128]{1,0:T(8,128)(2,1)S(1)}, u32[]{:S(2)}, u32[]{:S(2)}) collective-permute-start(bf16[512,128]{1,0:T(8,128)(2,1)S(1)} %get-tuple-element.54), channel_id=1, source_target_pairs={{0,4},{4,0},{8,12},{12,8},{16,20},{20,16},{24,28},{28,24},{1,5},{5... | collective-permute-start | bytes 393224 | tf_op jit(solution)/shard_map/ppermute | solution.py:730
  31.9 0.0 collective-permute-start.6
  31.9 0.0 collective-permute-done.9.refs_4_.refs_5_
  31.9 2.0 %collective-permute-start.7 = (bf16[512,128]{1,0:T(8,128)(2,1)S(1)}, bf16[512,128]{1,0:T(8,128)(2,1)S(1)}, u32[]{:S(2)}, u32[]{:S(2)}) collective-permute-start(bf16[512,128]{1,0:T(8,128)(2,1)S(1)} %get-tuple-element.56), channel_id=1, source_target_pairs={{0,12},{4,8},{8,4},{12,0},{16,28},{20,24},{24,20},{28,16},{1,13},{... | collective-permute-start | bytes 393224 | tf_op jit(solution)/shard_map/ppermute | solution.py:730
  33.8 0.0 collective-permute-done.8.refs_3_
  33.8 3.3 %attend.6.refs_12_.refs_0_.refs_2_ = f32[2,144,2048]{2,1,0:T(8,128)S(1)} custom-call(s32[1]{0:T(128)} %bitcast.1.refs_0_, bf16[2,2048,256]{2,1,0:T(8,128)(2,1)S(1)} %get-tuple-element.47.refs_1_, f32[2,144,2048]{2,1,0:T(8,128)S(1)} %attend.5.refs_5_.refs_2_, bf16[1040,128]{1,0:T(8,128)(2,1)S(1)} %collective-permute-done.8.refs_3_, ...), custom_call_target="tpu_custom_call" | custom-call | flops 2147483648 | bytes 8388608 | tf_op jit(solution)/shard_map/attend/pallas_call | solution.py:68
  37.2 0.0 collective-permute-done.5.refs_9_.refs_2_
  37.2 0.0 collective-permute-done.6.refs_10_.refs_3_
  37.2 1.0 %collective-permute-done.7.refs_11_.refs_4_ = bf16[512,128]{1,0:T(8,128)(2,1)S(1)} collective-permute-done((bf16[512,128]{1,0:T(8,128)(2,1)S(1)}, bf16[512,128]{1,0:T(8,128)(2,1)S(1)}, u32[]{:S(2)}, u32[]{:S(2)}) %collective-permute-start.7) | collective-permute-done | bytes 131104 | tf_op jit(solution)/shard_map/ppermute | solution.py:730
  38.2 1.3 %collective-permute-start.13 = (bf16[1040,128]{1,0:T(8,128)(2,1)S(1)}, bf16[1040,128]{1,0:T(8,128)(2,1)S(1)}, u32[]{:S(2)}, u32[]{:S(2)}) collective-permute-start(bf16[1040,128]{1,0:T(8,128)(2,1)S(1)} %get-tuple-element.59), channel_id=1, source_target_pairs={{4,24},{5,25},{6,26},{7,27}} | collective-permute-start | bytes 798728 | tf_op jit(solution)/shard_map/ppermute | solution.py:730
  39.5 3.0 %collective-permute-start.15 = (bf16[1040,128]{1,0:T(8,128)(2,1)S(1)}, bf16[1040,128]{1,0:T(8,128)(2,1)S(1)}, u32[]{:S(2)}, u32[]{:S(2)}) collective-permute-start(bf16[1040,128]{1,0:T(8,128)(2,1)S(1)} %get-tuple-element.61), channel_id=1, source_target_pairs={{16,20},{20,16},{24,28},{28,24},{17,21},{21,17},{25,29},{29,25},{1... | collective-permute-start | bytes 798728 | tf_op jit(solution)/shard_map/ppermute | solution.py:730
  42.6 1.6 %mix.1 = (f32[4096,128]{1,0:T(8,128)S(1)}, f32[8,256]{1,0:T(8,128)S(1)}) custom-call(s32[1]{0:T(128)} %bitcast.1.refs_0_, f32[16,128]{1,0:T(8,128)S(1)} %get-tuple-element.33.refs_3_.refs_1_, f32[8,128]{1,0:T(8,128)S(1)} %get-tuple-element.50.refs_5_.refs_2_, f32[256,128]{1,0:T(8,128)S(1)} %get-tuple-element.34.refs_2_.refs_0_.refs_3_, ...), custom_call_target="tpu_custom_call" | custom-call | flops 134217728 | bytes 5242880 | tf_op jit(solution)/shard_map/mix/pallas_call | solution.py:68
  44.1 0.0 collective-permute-start.12
  44.1 0.6 %collective-permute-start.11 = (f32[8,256]{1,0:T(8,128)S(1)}, f32[8,256]{1,0:T(8,128)S(1)}, u32[]{:S(2)}, u32[]{:S(2)}) collective-permute-start(f32[8,256]{1,0:T(8,128)S(1)} %get-tuple-element.58.refs_3_.refs_5_), channel_id=1, source_target_pairs={{0,2},{1,3},{2,0},{3,1},{4,6},{5,7},{6,4},{7,5},{8,10},{9,11},{10,... | collective-permute-start | bytes 24584 | tf_op jit(solution)/shard_map/ppermute | solution.py:818
  44.7 0.0 collective-permute-done.14.refs_2_
  44.7 1.3 %collective-permute-start.10 = (f32[8,256]{1,0:T(8,128)S(1)}, f32[8,256]{1,0:T(8,128)S(1)}, u32[]{:S(2)}, u32[]{:S(2)}) collective-permute-start(f32[8,256]{1,0:T(8,128)S(1)} %get-tuple-element.58.refs_3_.refs_5_), channel_id=1, source_target_pairs={{0,1},{1,0},{2,3},{3,2},{4,5},{5,4},{6,7},{7,6},{8,9},{9,8},{10,11... | collective-permute-start | bytes 24584 | tf_op jit(solution)/shard_map/ppermute | solution.py:818
  46.0 3.3 %collective-permute-done.13.refs_1_ = bf16[1040,128]{1,0:T(8,128)(2,1)S(1)} collective-permute-done((bf16[1040,128]{1,0:T(8,128)(2,1)S(1)}, bf16[1040,128]{1,0:T(8,128)(2,1)S(1)}, u32[]{:S(2)}, u32[]{:S(2)}) %collective-permute-start.13) | collective-permute-done | bytes 266272 | tf_op jit(solution)/shard_map/ppermute | solution.py:730
  49.3 0.1 pick.1.refs_3_
  49.4 0.0 copy-start.1
  49.4 0.0 copy-start.2
  49.4 2.1 %collective-permute-done.15.refs_4_ = bf16[1040,128]{1,0:T(8,128)(2,1)S(1)} collective-permute-done((bf16[1040,128]{1,0:T(8,128)(2,1)S(1)}, bf16[1040,128]{1,0:T(8,128)(2,1)S(1)}, u32[]{:S(2)}, u32[]{:S(2)}) %collective-permute-start.15) | collective-permute-done | bytes 266272 | tf_op jit(solution)/shard_map/ppermute | solution.py:730
  51.5 4.2 %attend.7 = (bf16[4096,128]{1,0:T(8,128)(2,1)}, f32[8,128]{1,0:T(8,128)S(1)}) custom-call(s32[1]{0:T(128)} %bitcast.1.refs_0_, bf16[2,2048,256]{2,1,0:T(8,128)(2,1)S(1)} %get-tuple-element.47.refs_1_, f32[2,144,2048]{2,1,0:T(8,128)S(1)} %attend.6.refs_12_.refs_0_.refs_2_, bf16[1040,128]{1,0:T(8,128)(2,1)S(1)} %pick.1.refs_3_, ...), custom_call_target="tpu_custom_call" | custom-call | flops 2147483648 | bytes 8388608 | tf_op jit(solution)/shard_map/attend/pallas_call | solution.py:68
  55.8 0.0 collective-permute-done.12.refs_6_
  55.8 0.0 collective-permute-done.11.refs_5_
  55.8 0.0 collective-permute-done.10.refs_4_
  55.8 1.6 %finish.1 = bf16[4096,128]{1,0:T(8,128)(2,1)} custom-call(f32[16,128]{1,0:T(8,128)S(1)} %copy-done.2, bf16[4096,128]{1,0:T(8,128)(2,1)S(1)} %bitcast.15, f32[4096,128]{1,0:T(8,128)S(1)} %get-tuple-element.57.refs_2_, f32[8,256]{1,0:T(8,128)S(1)} %get-tuple-element.58.refs_3_.refs_5_, f32[8,256]{1,0:T(8,128)S(1)} %collective-permute-done.10.refs_4_, ...), custom_call_target="tpu_custom_call" | custom-call | bytes 4194304 | tf_op jit(solution)/shard_map/finish/pallas_call | solution.py:68
  (4 shorter events, 0.0 us)
Async XLA Ops:
  2.6 9.5 %collective-permute-start.3 = (bf16[1040,128]{1,0:T(8,128)(2,1)S(1)}, bf16[1040,128]{1,0:T(8,128)(2,1)S(1)}, u32[]{:S(2)}, u32[]{:S(2)}) collective-permute-start(bf16[1040,128]{1,0:T(8,128)(2,1)S(1)} %get-tuple-element.42.refs_3_.refs_7_.refs_6_), channel_id=1, source_target_pairs={{0,8},{4,12},{8,16},{12,20},{16,24},{20,28},{24,0},{28,4},{1,9},{5... | collective-permute-start | bytes 798728 | tf_op jit(solution)/shard_map/ppermute | solution.py:730
  6.6 5.5 %copy-start = (bf16[256,16,128]{2,1,0:T(8,128)(2,1)S(1)}, bf16[256,16,128]{2,1,0:T(8,128)(2,1)}, u32[]{:S(2)}) copy-start(bf16[256,16,128]{2,1,0:T(8,128)(2,1)} %param.10) | copy-start | bytes 3145732
  6.6 8.9 %collective-permute-start = (bf16[528,128]{1,0:T(8,128)(2,1)S(1)}, bf16[528,128]{1,0:T(8,128)(2,1)S(1)}, u32[]{:S(2)}, u32[]{:S(2)}) collective-permute-start(bf16[528,128]{1,0:T(8,128)(2,1)S(1)} %get-tuple-element.38), channel_id=1, source_target_pairs={{0,4},{4,0},{8,12},{12,8},{16,20},{20,16},{24,28},{28,24},{1,5},{5... | collective-permute-start | bytes 405512 | tf_op jit(solution)/shard_map/ppermute | solution.py:730
  8.2 7.3 %collective-permute-start.1 = (bf16[528,128]{1,0:T(8,128)(2,1)S(1)}, bf16[528,128]{1,0:T(8,128)(2,1)S(1)}, u32[]{:S(2)}, u32[]{:S(2)}) collective-permute-start(bf16[528,128]{1,0:T(8,128)(2,1)S(1)} %get-tuple-element.39), channel_id=1, source_target_pairs={{0,8},{4,12},{8,0},{12,4},{16,24},{20,28},{24,16},{28,20},{1,9},{5... | collective-permute-start | bytes 405512 | tf_op jit(solution)/shard_map/ppermute | solution.py:730
  10.0 7.5 %collective-permute-start.2 = (bf16[528,128]{1,0:T(8,128)(2,1)S(1)}, bf16[528,128]{1,0:T(8,128)(2,1)S(1)}, u32[]{:S(2)}, u32[]{:S(2)}) collective-permute-start(bf16[528,128]{1,0:T(8,128)(2,1)S(1)} %get-tuple-element.40), channel_id=1, source_target_pairs={{0,12},{4,8},{8,4},{12,0},{16,28},{20,24},{24,20},{28,16},{1,13},{... | collective-permute-start | bytes 405512 | tf_op jit(solution)/shard_map/ppermute | solution.py:730
  14.1 17.8 %collective-permute-start.9 = (bf16[1040,128]{1,0:T(8,128)(2,1)S(1)}, bf16[1040,128]{1,0:T(8,128)(2,1)S(1)}, u32[]{:S(2)}, u32[]{:S(2)}) collective-permute-start(bf16[1040,128]{1,0:T(8,128)(2,1)S(1)} %get-tuple-element.45.refs_6_), channel_id=1, source_target_pairs={{8,16},{12,20},{16,24},{20,28},{9,17},{13,21},{17,25},{21,29},{10,... | collective-permute-start | bytes 798728 | tf_op jit(solution)/shard_map/ppermute | solution.py:730
  17.8 16.1 %collective-permute-start.8 = (bf16[1040,128]{1,0:T(8,128)(2,1)S(1)}, bf16[1040,128]{1,0:T(8,128)(2,1)S(1)}, u32[]{:S(2)}, u32[]{:S(2)}) collective-permute-start(bf16[1040,128]{1,0:T(8,128)(2,1)S(1)} %get-tuple-element.48.refs_3_), channel_id=1, source_target_pairs={{0,4},{4,0},{8,12},{12,8},{16,20},{20,16},{24,28},{28,24},{1,5},{5... | collective-permute-start | bytes 798728 | tf_op jit(solution)/shard_map/ppermute | solution.py:730
  18.3 11.7 %collective-permute-start.4 = (bf16[528,128]{1,0:T(8,128)(2,1)S(1)}, bf16[528,128]{1,0:T(8,128)(2,1)S(1)}, u32[]{:S(2)}, u32[]{:S(2)}) collective-permute-start(bf16[528,128]{1,0:T(8,128)(2,1)S(1)} %get-tuple-element.46.refs_4_), channel_id=1, source_target_pairs={{0,16},{4,20},{8,24},{12,28},{16,0},{20,4},{24,8},{28,12},{1,17},{... | collective-permute-start | bytes 405512 | tf_op jit(solution)/shard_map/ppermute | solution.py:730
  21.3 23.5 %collective-permute-start.14 = (bf16[1040,128]{1,0:T(8,128)(2,1)S(1)}, bf16[1040,128]{1,0:T(8,128)(2,1)S(1)}, u32[]{:S(2)}, u32[]{:S(2)}) collective-permute-start(bf16[1040,128]{1,0:T(8,128)(2,1)S(1)} %get-tuple-element.60), channel_id=1, source_target_pairs={{0,4},{4,0},{8,12},{12,8},{16,20},{20,16},{24,28},{28,24},{1,5},{5... | collective-permute-start | bytes 798728 | tf_op jit(solution)/shard_map/ppermute | solution.py:730
  30.3 6.9 %collective-permute-start.5 = (bf16[512,128]{1,0:T(8,128)(2,1)S(1)}, bf16[512,128]{1,0:T(8,128)(2,1)S(1)}, u32[]{:S(2)}, u32[]{:S(2)}) collective-permute-start(bf16[512,128]{1,0:T(8,128)(2,1)S(1)} %get-tuple-element.54), channel_id=1, source_target_pairs={{0,4},{4,0},{8,12},{12,8},{16,20},{20,16},{24,28},{28,24},{1,5},{5... | collective-permute-start | bytes 393224 | tf_op jit(solution)/shard_map/ppermute | solution.py:730
  31.9 5.3 %collective-permute-start.6 = (bf16[512,128]{1,0:T(8,128)(2,1)S(1)}, bf16[512,128]{1,0:T(8,128)(2,1)S(1)}, u32[]{:S(2)}, u32[]{:S(2)}) collective-permute-start(bf16[512,128]{1,0:T(8,128)(2,1)S(1)} %get-tuple-element.55), channel_id=1, source_target_pairs={{0,8},{4,12},{8,0},{12,4},{16,24},{20,28},{24,16},{28,20},{1,9},{5... | collective-permute-start | bytes 393224 | tf_op jit(solution)/shard_map/ppermute | solution.py:730
  31.9 6.3 %collective-permute-start.7 = (bf16[512,128]{1,0:T(8,128)(2,1)S(1)}, bf16[512,128]{1,0:T(8,128)(2,1)S(1)}, u32[]{:S(2)}, u32[]{:S(2)}) collective-permute-start(bf16[512,128]{1,0:T(8,128)(2,1)S(1)} %get-tuple-element.56), channel_id=1, source_target_pairs={{0,12},{4,8},{8,4},{12,0},{16,28},{20,24},{24,20},{28,16},{1,13},{... | collective-permute-start | bytes 393224 | tf_op jit(solution)/shard_map/ppermute | solution.py:730
  38.2 11.1 %collective-permute-start.13 = (bf16[1040,128]{1,0:T(8,128)(2,1)S(1)}, bf16[1040,128]{1,0:T(8,128)(2,1)S(1)}, u32[]{:S(2)}, u32[]{:S(2)}) collective-permute-start(bf16[1040,128]{1,0:T(8,128)(2,1)S(1)} %get-tuple-element.59), channel_id=1, source_target_pairs={{4,24},{5,25},{6,26},{7,27}} | collective-permute-start | bytes 798728 | tf_op jit(solution)/shard_map/ppermute | solution.py:730
  39.5 12.0 %collective-permute-start.15 = (bf16[1040,128]{1,0:T(8,128)(2,1)S(1)}, bf16[1040,128]{1,0:T(8,128)(2,1)S(1)}, u32[]{:S(2)}, u32[]{:S(2)}) collective-permute-start(bf16[1040,128]{1,0:T(8,128)(2,1)S(1)} %get-tuple-element.61), channel_id=1, source_target_pairs={{16,20},{20,16},{24,28},{28,24},{17,21},{21,17},{25,29},{29,25},{1... | collective-permute-start | bytes 798728 | tf_op jit(solution)/shard_map/ppermute | solution.py:730
  44.1 11.6 %collective-permute-start.12 = (f32[8,256]{1,0:T(8,128)S(1)}, f32[8,256]{1,0:T(8,128)S(1)}, u32[]{:S(2)}, u32[]{:S(2)}) collective-permute-start(f32[8,256]{1,0:T(8,128)S(1)} %get-tuple-element.58.refs_3_.refs_5_), channel_id=1, source_target_pairs={{0,3},{1,2},{2,1},{3,0},{4,7},{5,6},{6,5},{7,4},{8,11},{9,10},{10,... | collective-permute-start | bytes 24584 | tf_op jit(solution)/shard_map/ppermute | solution.py:818
  44.1 11.6 %collective-permute-start.11 = (f32[8,256]{1,0:T(8,128)S(1)}, f32[8,256]{1,0:T(8,128)S(1)}, u32[]{:S(2)}, u32[]{:S(2)}) collective-permute-start(f32[8,256]{1,0:T(8,128)S(1)} %get-tuple-element.58.refs_3_.refs_5_), channel_id=1, source_target_pairs={{0,2},{1,3},{2,0},{3,1},{4,6},{5,7},{6,4},{7,5},{8,10},{9,11},{10,... | collective-permute-start | bytes 24584 | tf_op jit(solution)/shard_map/ppermute | solution.py:818
  44.7 11.1 %collective-permute-start.10 = (f32[8,256]{1,0:T(8,128)S(1)}, f32[8,256]{1,0:T(8,128)S(1)}, u32[]{:S(2)}, u32[]{:S(2)}) collective-permute-start(f32[8,256]{1,0:T(8,128)S(1)} %get-tuple-element.58.refs_3_.refs_5_), channel_id=1, source_target_pairs={{0,1},{1,0},{2,3},{3,2},{4,5},{5,4},{6,7},{7,6},{8,9},{9,8},{10,11... | collective-permute-start | bytes 24584 | tf_op jit(solution)/shard_map/ppermute | solution.py:818
  49.4 6.4 %copy-start.1 = (bf16[256,16,128]{2,1,0:T(8,128)(2,1)S(1)}, bf16[256,16,128]{2,1,0:T(8,128)(2,1)}, u32[]{:S(2)}) copy-start(bf16[256,16,128]{2,1,0:T(8,128)(2,1)} %param.13) | copy-start | bytes 3145732
  49.4 6.4 %copy-start.2 = (f32[16,128]{1,0:T(8,128)S(1)}, f32[16,128]{1,0:T(8,128)}, u32[]{:S(2)}) copy-start(f32[16,128]{1,0:T(8,128)} %refs_0_.1) | copy-start | bytes 24580

commit v18 on v17

--- a/solution.py
+++ b/solution.py
@@ -803,8 +803,8 @@
     *priors, prior_doc = prior_states(place, stages + 1, quarters, came, before, size, [done])
     priors = [priors[0]] + [send(priors[j], [(b, b ^ j) for b in everyone]) for j in others]
     done = more_attention([(first_cross, (2, 3)), (second, (4, 4))], False, [prior_doc])
-    lane, own_copy = pass_on([second, own_kv], [done, *priors])
-    rest = [(send(lane, [(b, b ^ 1) for b in range(4, blocks)]), (4, 5))]
+    lane, own_copy = pass_on([second, own_kv], [done, *priors, beside])
+    rest = [(send(lane, [(b, b ^ 1 if b >= 4 else b) for b in everyone]), (4, 5))]
     far = None
     if window % 2:
         far = send(own_copy, [(b, b + window) for b in range(1, blocks - window, 2)])
@@ -816,13 +816,13 @@
     sums = [squares]
     for other in range(1, tensor):
         sums.append(lax.ppermute(squares, "tp", [(t, t ^ other) for t in range(tensor)]))
-    slot = beside if far is None else pick(place, far, beside, [squares])
-    rest.insert(0, (slot, (blocks if far is None else window, 1)))
     done = squares
     while rest:
-        got = more_attention(rest[:2], len(rest) <= 2, [done])
-        rest, done = rest[2:], got
-    soft_out, done = got
+        done = more_attention(rest[:2], False, [done])
+        rest = rest[2:]
+    slot = beside if far is None else pick(place, far, beside, [done])
+    slot = (slot, (blocks if far is None else window, 1))
+    soft_out, done = more_attention([slot], True, [done])
     lin_out = finish(norm_gain, flat(lin_gate), mixed, sums, tokens, heads, [done])
     shape = (tokens, heads, HEAD_DIM)
     return lin_out.reshape(shape), soft_out.reshape(shape)

time: 57.9 us -> 58 us (level)
  the two profiles are of different devices: /device:TPU:26 before, /device:TPU:5 now
where the time goes in v18:
time: 58 us; the launch traced here: 57.8 us
  Pallas kernels  25.1 us (43%)
  starting transfers between devices  23.5 us (41%)
  waiting for transfers between devices  8.15 us (14%)
  between operations  1.04 us (2%)
    pallas_call x15, Pallas kernels, call(): pl.pallas_call(run, out_shape=outs, in_specs=[SMEM] * len(scalars) + [HBM...  25.1 us
    ppermute x13, starting transfers between devices, send(): return lax.ppermute(x, 'seq', [(a, b % blocks) for a, b in pairs])  17 us
    ppermute x13, waiting for transfers between devices, send(): return lax.ppermute(x, 'seq', [(a, b % blocks) for a, b in pairs])  8.14 us
    ppermute x3, starting transfers between devices, body(): lax.ppermute(squares, 'tp', [(t, t ^ other) for t in range(tensor)])  6.5 us
  transfers between devices with their start and end apart: 16, of which 4 were waited for; matrix products, arithmetic and copies ran while one was open for 0% of the time, Pallas kernels for 37%

profile of v18, /device:TPU:5, one launch (start us, length us, event | category | flops | bytes accessed | tf_op | source)
XLA Modules:
  0.0 57.8 jit_solution(12355942453464232455)
XLA Ops:
  0.6 1.9 %fetch.1 = (bf16[1040,128]{1,0:T(8,128)(2,1)S(1)}, f32[16,128]{1,0:T(8,128)S(1)}, f32[256,128]{1,0:T(8,128)S(1)}, bf16[4096,128]{1,0:T(8,128)(2,1)S(1)}, bf16[4096,128]{1,0:T(8,128)(2,1)S(1)}) custom-call(s32[1]{0:T(128)} %bitcast.2.refs_0_, s32[2,128]{1,0:T(2,128)} %bitcast.23, f32[16,256]{1,0:T(8,128)} %bitcast.22, bf16[2048,128]{1,0:T(8,128)(2,1)} %bitcast.20, ...), custom_call_target="tpu_custom_call" | custom-call | bytes 3145728 | tf_op jit(solution)/shard_map/fetch/pallas_call | solution.py:68
  2.6 1.3 %collective-permute-start.3 = (bf16[1040,128]{1,0:T(8,128)(2,1)S(1)}, bf16[1040,128]{1,0:T(8,128)(2,1)S(1)}, u32[]{:S(2)}, u32[]{:S(2)}) collective-permute-start(bf16[1040,128]{1,0:T(8,128)(2,1)S(1)} %get-tuple-element.42.refs_3_.refs_7_), channel_id=1, source_target_pairs={{0,8},{4,12},{8,16},{12,20},{16,24},{20,28},{24,0},{28,4},{1,9},{5... | collective-permute-start | bytes 798728 | tf_op jit(solution)/shard_map/ppermute | solution.py:730
  3.9 3.8 %block_state.1 = (bf16[528,128]{1,0:T(8,128)(2,1)S(1)}, bf16[528,128]{1,0:T(8,128)(2,1)S(1)}, bf16[528,128]{1,0:T(8,128)(2,1)S(1)}, bf16[528,128]{1,0:T(8,128)(2,1)S(1)}, bf16[4096,128]{1,0:T(8,128)(2,1)S(1)}) custom-call(s32[1]{0:T(128)} %bitcast.1.refs_0_, bf16[4096,128]{1,0:T(8,128)(2,1)} %bitcast.19, ...), custom_call_target="tpu_custom_call" | custom-call | flops 134217728 | bytes 5242880 | tf_op jit(solution)/shard_map/block_state/pallas_call | solution.py:68
  7.7 0.0 copy-start
  7.7 0.3 collective-permute-start
  8.0 1.3 %collective-permute-start.1 = (bf16[528,128]{1,0:T(8,128)(2,1)S(1)}, bf16[528,128]{1,0:T(8,128)(2,1)S(1)}, u32[]{:S(2)}, u32[]{:S(2)}) collective-permute-start(bf16[528,128]{1,0:T(8,128)(2,1)S(1)} %get-tuple-element.39), channel_id=1, source_target_pairs={{0,8},{4,12},{8,0},{12,4},{16,24},{20,28},{24,16},{28,20},{1,9},{5... | collective-permute-start | bytes 405512 | tf_op jit(solution)/shard_map/ppermute | solution.py:730
  9.3 1.1 %collective-permute-start.2 = (bf16[528,128]{1,0:T(8,128)(2,1)S(1)}, bf16[528,128]{1,0:T(8,128)(2,1)S(1)}, u32[]{:S(2)}, u32[]{:S(2)}) collective-permute-start(bf16[528,128]{1,0:T(8,128)(2,1)S(1)} %get-tuple-element.40), channel_id=1, source_target_pairs={{0,12},{4,8},{8,4},{12,0},{16,28},{20,24},{24,20},{28,16},{1,13},{... | collective-permute-start | bytes 405512 | tf_op jit(solution)/shard_map/ppermute | solution.py:730
  10.4 1.9 %attend.5 = (bf16[2,2048,256]{2,1,0:T(8,128)(2,1)S(1)}, f32[2,144,2048]{2,1,0:T(8,128)S(1)}) custom-call(s32[1]{0:T(128)} %bitcast.1.refs_0_, f32[16,128]{1,0:T(8,128)S(1)} %get-tuple-element.33.refs_3_.refs_1_, bf16[4096,128]{1,0:T(8,128)(2,1)S(1)} %get-tuple-element.41.refs_2_, bf16[1040,128]{1,0:T(8,128)(2,1)S(1)} %get-tuple-element.42.refs_3_.refs_7_, ...), custom_call_target="tpu_custom_call" | custom-call | flops 1073741824 | bytes 8388608 | tf_op jit(solution)/shard_map/attend/pallas_call | solution.py:68
  12.3 0.0 collective-permute-done.3.refs_6_
  12.3 1.9 %inner_part.2 = (f32[2048,128]{1,0:T(8,128)S(1)}, bf16[2048,128]{1,0:T(8,128)(2,1)S(1)}, bf16[1040,128]{1,0:T(8,128)(2,1)S(1)}) custom-call(f32[256,128]{1,0:T(8,128)S(1)} %get-tuple-element.34.refs_2_.refs_0_.refs_3_, f32[16,128]{1,0:T(8,128)S(1)} %get-tuple-element.33.refs_3_.refs_1_, bf16[4096,128]{1,0:T(8,128)(2,1)S(1)} %bitcast.13, ...), custom_call_target="tpu_custom_call" | custom-call | flops 268435456 | bytes 6291456 | tf_op jit(solution)/shard_map/inner_part/pallas_call | solution.py:68
  14.2 0.9 %collective-permute-start.9 = (bf16[1040,128]{1,0:T(8,128)(2,1)S(1)}, bf16[1040,128]{1,0:T(8,128)(2,1)S(1)}, u32[]{:S(2)}, u32[]{:S(2)}) collective-permute-start(bf16[1040,128]{1,0:T(8,128)(2,1)S(1)} %get-tuple-element.45.refs_6_), channel_id=1, source_target_pairs={{8,16},{12,20},{16,24},{20,28},{9,17},{13,21},{17,25},{21,29},{10,... | collective-permute-start | bytes 798728 | tf_op jit(solution)/shard_map/ppermute | solution.py:730
  15.1 0.0 collective-permute-done.refs_2_
  15.1 0.6 %collective-permute-done.1.refs_3_ = bf16[528,128]{1,0:T(8,128)(2,1)S(1)} collective-permute-done((bf16[528,128]{1,0:T(8,128)(2,1)S(1)}, bf16[528,128]{1,0:T(8,128)(2,1)S(1)}, u32[]{:S(2)}, u32[]{:S(2)}) %collective-permute-start.1) | collective-permute-done | bytes 135200 | tf_op jit(solution)/shard_map/ppermute | solution.py:730
  15.7 2.4 %collective-permute-done.2.refs_4_ = bf16[528,128]{1,0:T(8,128)(2,1)S(1)} collective-permute-done((bf16[528,128]{1,0:T(8,128)(2,1)S(1)}, bf16[528,128]{1,0:T(8,128)(2,1)S(1)}, u32[]{:S(2)}, u32[]{:S(2)}) %collective-permute-start.2) | collective-permute-done | bytes 135200 | tf_op jit(solution)/shard_map/ppermute | solution.py:730
  18.1 0.2 group_map.1
  18.3 1.8 %collective-permute-start.8 = (bf16[1040,128]{1,0:T(8,128)(2,1)S(1)}, bf16[1040,128]{1,0:T(8,128)(2,1)S(1)}, u32[]{:S(2)}, u32[]{:S(2)}) collective-permute-start(bf16[1040,128]{1,0:T(8,128)(2,1)S(1)} %get-tuple-element.48.refs_3_), channel_id=1, source_target_pairs={{0,4},{4,0},{8,12},{12,8},{16,20},{20,16},{24,28},{28,24},{1,5},{5... | collective-permute-start | bytes 798728 | tf_op jit(solution)/shard_map/ppermute | solution.py:730
  20.1 0.0 collective-permute-start.4
  20.1 0.4 collective-permute-start.13
  20.5 1.9 %attend.6.refs_5_.refs_2_ = f32[2,144,2048]{2,1,0:T(8,128)S(1)} custom-call(s32[1]{0:T(128)} %bitcast.1.refs_0_, bf16[2,2048,256]{2,1,0:T(8,128)(2,1)S(1)} %get-tuple-element.47.refs_1_, f32[2,144,2048]{2,1,0:T(8,128)S(1)} %get-tuple-element.43.refs_5_.refs_2_, bf16[1040,128]{1,0:T(8,128)(2,1)S(1)} %get-tuple-element.48.refs_3_, ...), custom_call_target="tpu_custom_call" | custom-call | flops 1073741824 | bytes 8388608 | tf_op jit(solution)/shard_map/attend/pallas_call | solution.py:68
  22.4 1.9 %inner_part.3 = (f32[2048,128]{1,0:T(8,128)S(1)}, bf16[2048,128]{1,0:T(8,128)(2,1)S(1)}) custom-call(f32[256,128]{1,0:T(8,128)S(1)} %get-tuple-element.34.refs_2_.refs_0_.refs_3_, f32[16,128]{1,0:T(8,128)S(1)} %get-tuple-element.33.refs_3_.refs_1_, bf16[4096,128]{1,0:T(8,128)(2,1)S(1)} %bitcast.14, bf16[4096,128]{1,0:T(8,128)(2,1)S(1)} %get-tuple-element.35.refs_4_.refs_3_, ...), custom_call_target="tpu_custom_call" | custom-call | flops 268435456 | bytes 6291456 | tf_op jit(solution)/shard_map/inner_part/pallas_call | solution.py:68
  24.3 3.6 %collective-permute-done.4.refs_5_ = bf16[528,128]{1,0:T(8,128)(2,1)S(1)} collective-permute-done((bf16[528,128]{1,0:T(8,128)(2,1)S(1)}, bf16[528,128]{1,0:T(8,128)(2,1)S(1)}, u32[]{:S(2)}, u32[]{:S(2)}) %collective-permute-start.4) | collective-permute-done | bytes 135200 | tf_op jit(solution)/shard_map/ppermute | solution.py:730
  27.9 0.3 prior_states.1
  28.2 1.3 %collective-permute-start.5 = (bf16[512,128]{1,0:T(8,128)(2,1)S(1)}, bf16[512,128]{1,0:T(8,128)(2,1)S(1)}, u32[]{:S(2)}, u32[]{:S(2)}) collective-permute-start(bf16[512,128]{1,0:T(8,128)(2,1)S(1)} %get-tuple-element.54), channel_id=1, source_target_pairs={{0,4},{4,0},{8,12},{12,8},{16,20},{20,16},{24,28},{28,24},{1,5},{5... | collective-permute-start | bytes 393224 | tf_op jit(solution)/shard_map/ppermute | solution.py:730
  29.5 0.0 collective-permute-start.6
  29.5 0.0 collective-permute-done.9.refs_4_.refs_6_
  29.5 1.4 %collective-permute-start.7 = (bf16[512,128]{1,0:T(8,128)(2,1)S(1)}, bf16[512,128]{1,0:T(8,128)(2,1)S(1)}, u32[]{:S(2)}, u32[]{:S(2)}) collective-permute-start(bf16[512,128]{1,0:T(8,128)(2,1)S(1)} %get-tuple-element.56), channel_id=1, source_target_pairs={{0,12},{4,8},{8,4},{12,0},{16,28},{20,24},{24,20},{28,16},{1,13},{... | collective-permute-start | bytes 393224 | tf_op jit(solution)/shard_map/ppermute | solution.py:730
  30.9 0.0 collective-permute-done.8.refs_3_
  30.9 3.3 %attend.7.refs_12_.refs_0_.refs_2_ = f32[2,144,2048]{2,1,0:T(8,128)S(1)} custom-call(s32[1]{0:T(128)} %bitcast.1.refs_0_, bf16[2,2048,256]{2,1,0:T(8,128)(2,1)S(1)} %get-tuple-element.47.refs_1_, f32[2,144,2048]{2,1,0:T(8,128)S(1)} %attend.6.refs_5_.refs_2_, bf16[1040,128]{1,0:T(8,128)(2,1)S(1)} %collective-permute-done.8.refs_3_, ...), custom_call_target="tpu_custom_call" | custom-call | flops 2147483648 | bytes 8388608 | tf_op jit(solution)/shard_map/attend/pallas_call | solution.py:68
  34.2 1.6 %collective-permute-done.5.refs_9_.refs_2_ = bf16[512,128]{1,0:T(8,128)(2,1)S(1)} collective-permute-done((bf16[512,128]{1,0:T(8,128)(2,1)S(1)}, bf16[512,128]{1,0:T(8,128)(2,1)S(1)}, u32[]{:S(2)}, u32[]{:S(2)}) %collective-permute-start.5) | collective-permute-done | bytes 131104 | tf_op jit(solution)/shard_map/ppermute | solution.py:730
  35.8 0.0 collective-permute-done.6.refs_10_.refs_3_
  35.8 0.0 collective-permute-done.7.refs_11_.refs_4_
  35.8 0.0 collective-permute-done.13.refs_5_.refs_2_
  35.8 0.7 %collective-permute-start.14 = (bf16[1040,128]{1,0:T(8,128)(2,1)S(1)}, bf16[1040,128]{1,0:T(8,128)(2,1)S(1)}, u32[]{:S(2)}, u32[]{:S(2)}) collective-permute-start(bf16[1040,128]{1,0:T(8,128)(2,1)S(1)} %get-tuple-element.60), channel_id=1, source_target_pairs={{0,0},{4,4},{8,8},{12,12},{16,20},{20,16},{24,28},{28,24},{1,1},{5... | collective-permute-start | bytes 798728 | tf_op jit(solution)/shard_map/ppermute | solution.py:730
  36.5 6.5 %collective-permute-start.15 = (bf16[1040,128]{1,0:T(8,128)(2,1)S(1)}, bf16[1040,128]{1,0:T(8,128)(2,1)S(1)}, u32[]{:S(2)}, u32[]{:S(2)}) collective-permute-start(bf16[1040,128]{1,0:T(8,128)(2,1)S(1)} %get-tuple-element.61), channel_id=1, source_target_pairs={{4,24},{5,25},{6,26},{7,27}} | collective-permute-start | bytes 798728 | tf_op jit(solution)/shard_map/ppermute | solution.py:730
  43.0 1.6 %mix.1 = (f32[4096,128]{1,0:T(8,128)S(1)}, f32[8,256]{1,0:T(8,128)S(1)}) custom-call(s32[1]{0:T(128)} %bitcast.1.refs_0_, f32[16,128]{1,0:T(8,128)S(1)} %get-tuple-element.33.refs_3_.refs_1_, f32[8,128]{1,0:T(8,128)S(1)} %get-tuple-element.50.refs_5_.refs_2_, f32[256,128]{1,0:T(8,128)S(1)} %get-tuple-element.34.refs_2_.refs_0_.refs_3_, ...), custom_call_target="tpu_custom_call" | custom-call | flops 134217728 | bytes 5242880 | tf_op jit(solution)/shard_map/mix/pallas_call | solution.py:68
  44.6 6.1 %collective-permute-start.12 = (f32[8,256]{1,0:T(8,128)S(1)}, f32[8,256]{1,0:T(8,128)S(1)}, u32[]{:S(2)}, u32[]{:S(2)}) collective-permute-start(f32[8,256]{1,0:T(8,128)S(1)} %get-tuple-element.58.refs_4_.refs_3_), channel_id=1, source_target_pairs={{0,3},{1,2},{2,1},{3,0},{4,7},{5,6},{6,5},{7,4},{8,11},{9,10},{10,... | collective-permute-start | bytes 24584 | tf_op jit(solution)/shard_map/ppermute | solution.py:818
  50.7 0.2 collective-permute-start.11
  50.9 0.2 collective-permute-start.10
  51.1 0.0 collective-permute-done.14.refs_3_
  51.1 1.9 %attend.8.refs_3_.refs_2_.refs_4_ = f32[2,144,2048]{2,1,0:T(8,128)S(1)} custom-call(s32[1]{0:T(128)} %bitcast.1.refs_0_, bf16[2,2048,256]{2,1,0:T(8,128)(2,1)S(1)} %get-tuple-element.47.refs_1_, f32[2,144,2048]{2,1,0:T(8,128)S(1)} %attend.7.refs_12_.refs_0_.refs_2_, bf16[1040,128]{1,0:T(8,128)(2,1)S(1)} %collective-permute-done.14.refs_3_, ...), custom_call_target="tpu_custom_call" | custom-call | flops 1073741824 | bytes 8388608 | tf_op jit(solution)/shard_map/attend/pallas_call | solution.py:68
  53.0 0.0 collective-permute-done.15.refs_1_
  53.0 0.1 pick.1.refs_3_
  53.1 0.0 copy-start.1
  53.1 0.0 copy-start.2
  53.1 2.8 %attend.9 = (bf16[4096,128]{1,0:T(8,128)(2,1)}, f32[8,128]{1,0:T(8,128)S(1)}) custom-call(s32[1]{0:T(128)} %bitcast.1.refs_0_, bf16[2,2048,256]{2,1,0:T(8,128)(2,1)S(1)} %get-tuple-element.47.refs_1_, f32[2,144,2048]{2,1,0:T(8,128)S(1)} %attend.8.refs_3_.refs_2_.refs_4_, bf16[1040,128]{1,0:T(8,128)(2,1)S(1)} %pick.1.refs_3_, ...), custom_call_target="tpu_custom_call" | custom-call | flops 1073741824 | bytes 8388608 | tf_op jit(solution)/shard_map/attend/pallas_call | solution.py:68
  55.9 0.0 collective-permute-done.12.refs_6_
  55.9 0.0 collective-permute-done.11.refs_5_
  56.0 1.7 %finish.1 = bf16[4096,128]{1,0:T(8,128)(2,1)} custom-call(f32[16,128]{1,0:T(8,128)S(1)} %copy-done.2, bf16[4096,128]{1,0:T(8,128)(2,1)S(1)} %bitcast.15, f32[4096,128]{1,0:T(8,128)S(1)} %get-tuple-element.57.refs_2_, f32[8,256]{1,0:T(8,128)S(1)} %get-tuple-element.58.refs_4_.refs_3_, f32[8,256]{1,0:T(8,128)S(1)} %collective-permute-done.10.refs_4_, ...), custom_call_target="tpu_custom_call" | custom-call | bytes 4194304 | tf_op jit(solution)/shard_map/finish/pallas_call | solution.py:68
  (5 shorter events, 0.0 us)
Async XLA Ops:
  2.6 9.7 %collective-permute-start.3 = (bf16[1040,128]{1,0:T(8,128)(2,1)S(1)}, bf16[1040,128]{1,0:T(8,128)(2,1)S(1)}, u32[]{:S(2)}, u32[]{:S(2)}) collective-permute-start(bf16[1040,128]{1,0:T(8,128)(2,1)S(1)} %get-tuple-element.42.refs_3_.refs_7_), channel_id=1, source_target_pairs={{0,8},{4,12},{8,16},{12,20},{16,24},{20,28},{24,0},{28,4},{1,9},{5... | collective-permute-start | bytes 798728 | tf_op jit(solution)/shard_map/ppermute | solution.py:730
  7.7 4.6 %copy-start = (bf16[256,16,128]{2,1,0:T(8,128)(2,1)S(1)}, bf16[256,16,128]{2,1,0:T(8,128)(2,1)}, u32[]{:S(2)}) copy-start(bf16[256,16,128]{2,1,0:T(8,128)(2,1)} %param.10) | copy-start | bytes 3145732
  7.7 7.4 %collective-permute-start = (bf16[528,128]{1,0:T(8,128)(2,1)S(1)}, bf16[528,128]{1,0:T(8,128)(2,1)S(1)}, u32[]{:S(2)}, u32[]{:S(2)}) collective-permute-start(bf16[528,128]{1,0:T(8,128)(2,1)S(1)} %get-tuple-element.38), channel_id=1, source_target_pairs={{0,4},{4,0},{8,12},{12,8},{16,20},{20,16},{24,28},{28,24},{1,5},{5... | collective-permute-start | bytes 405512 | tf_op jit(solution)/shard_map/ppermute | solution.py:730
  8.0 7.7 %collective-permute-start.1 = (bf16[528,128]{1,0:T(8,128)(2,1)S(1)}, bf16[528,128]{1,0:T(8,128)(2,1)S(1)}, u32[]{:S(2)}, u32[]{:S(2)}) collective-permute-start(bf16[528,128]{1,0:T(8,128)(2,1)S(1)} %get-tuple-element.39), channel_id=1, source_target_pairs={{0,8},{4,12},{8,0},{12,4},{16,24},{20,28},{24,16},{28,20},{1,9},{5... | collective-permute-start | bytes 405512 | tf_op jit(solution)/shard_map/ppermute | solution.py:730
  9.3 8.8 %collective-permute-start.2 = (bf16[528,128]{1,0:T(8,128)(2,1)S(1)}, bf16[528,128]{1,0:T(8,128)(2,1)S(1)}, u32[]{:S(2)}, u32[]{:S(2)}) collective-permute-start(bf16[528,128]{1,0:T(8,128)(2,1)S(1)} %get-tuple-element.40), channel_id=1, source_target_pairs={{0,12},{4,8},{8,4},{12,0},{16,28},{20,24},{24,20},{28,16},{1,13},{... | collective-permute-start | bytes 405512 | tf_op jit(solution)/shard_map/ppermute | solution.py:730
  14.2 15.2 %collective-permute-start.9 = (bf16[1040,128]{1,0:T(8,128)(2,1)S(1)}, bf16[1040,128]{1,0:T(8,128)(2,1)S(1)}, u32[]{:S(2)}, u32[]{:S(2)}) collective-permute-start(bf16[1040,128]{1,0:T(8,128)(2,1)S(1)} %get-tuple-element.45.refs_6_), channel_id=1, source_target_pairs={{8,16},{12,20},{16,24},{20,28},{9,17},{13,21},{17,25},{21,29},{10,... | collective-permute-start | bytes 798728 | tf_op jit(solution)/shard_map/ppermute | solution.py:730
  18.3 12.6 %collective-permute-start.8 = (bf16[1040,128]{1,0:T(8,128)(2,1)S(1)}, bf16[1040,128]{1,0:T(8,128)(2,1)S(1)}, u32[]{:S(2)}, u32[]{:S(2)}) collective-permute-start(bf16[1040,128]{1,0:T(8,128)(2,1)S(1)} %get-tuple-element.48.refs_3_), channel_id=1, source_target_pairs={{0,4},{4,0},{8,12},{12,8},{16,20},{20,16},{24,28},{28,24},{1,5},{5... | collective-permute-start | bytes 798728 | tf_op jit(solution)/shard_map/ppermute | solution.py:730
  20.1 7.8 %collective-permute-start.4 = (bf16[528,128]{1,0:T(8,128)(2,1)S(1)}, bf16[528,128]{1,0:T(8,128)(2,1)S(1)}, u32[]{:S(2)}, u32[]{:S(2)}) collective-permute-start(bf16[528,128]{1,0:T(8,128)(2,1)S(1)} %get-tuple-element.46.refs_4_), channel_id=1, source_target_pairs={{0,16},{4,20},{8,24},{12,28},{16,0},{20,4},{24,8},{28,12},{1,17},{... | collective-permute-start | bytes 405512 | tf_op jit(solution)/shard_map/ppermute | solution.py:730
  20.1 15.7 %collective-permute-start.13 = (bf16[1040,128]{1,0:T(8,128)(2,1)S(1)}, bf16[1040,128]{1,0:T(8,128)(2,1)S(1)}, u32[]{:S(2)}, u32[]{:S(2)}) collective-permute-start(bf16[1040,128]{1,0:T(8,128)(2,1)S(1)} %get-tuple-element.59), channel_id=1, source_target_pairs={{0,4},{4,0},{8,12},{12,8},{16,20},{20,16},{24,28},{28,24},{1,5},{5... | collective-permute-start | bytes 798728 | tf_op jit(solution)/shard_map/ppermute | solution.py:730
  28.2 7.6 %collective-permute-start.5 = (bf16[512,128]{1,0:T(8,128)(2,1)S(1)}, bf16[512,128]{1,0:T(8,128)(2,1)S(1)}, u32[]{:S(2)}, u32[]{:S(2)}) collective-permute-start(bf16[512,128]{1,0:T(8,128)(2,1)S(1)} %get-tuple-element.54), channel_id=1, source_target_pairs={{0,4},{4,0},{8,12},{12,8},{16,20},{20,16},{24,28},{28,24},{1,5},{5... | collective-permute-start | bytes 393224 | tf_op jit(solution)/shard_map/ppermute | solution.py:730
  29.5 6.3 %collective-permute-start.6 = (bf16[512,128]{1,0:T(8,128)(2,1)S(1)}, bf16[512,128]{1,0:T(8,128)(2,1)S(1)}, u32[]{:S(2)}, u32[]{:S(2)}) collective-permute-start(bf16[512,128]{1,0:T(8,128)(2,1)S(1)} %get-tuple-element.55), channel_id=1, source_target_pairs={{0,8},{4,12},{8,0},{12,4},{16,24},{20,28},{24,16},{28,20},{1,9},{5... | collective-permute-start | bytes 393224 | tf_op jit(solution)/shard_map/ppermute | solution.py:730
  29.5 6.3 %collective-permute-start.7 = (bf16[512,128]{1,0:T(8,128)(2,1)S(1)}, bf16[512,128]{1,0:T(8,128)(2,1)S(1)}, u32[]{:S(2)}, u32[]{:S(2)}) collective-permute-start(bf16[512,128]{1,0:T(8,128)(2,1)S(1)} %get-tuple-element.56), channel_id=1, source_target_pairs={{0,12},{4,8},{8,4},{12,0},{16,28},{20,24},{24,20},{28,16},{1,13},{... | collective-permute-start | bytes 393224 | tf_op jit(solution)/shard_map/ppermute | solution.py:730
  35.8 15.3 %collective-permute-start.14 = (bf16[1040,128]{1,0:T(8,128)(2,1)S(1)}, bf16[1040,128]{1,0:T(8,128)(2,1)S(1)}, u32[]{:S(2)}, u32[]{:S(2)}) collective-permute-start(bf16[1040,128]{1,0:T(8,128)(2,1)S(1)} %get-tuple-element.60), channel_id=1, source_target_pairs={{0,0},{4,4},{8,8},{12,12},{16,20},{20,16},{24,28},{28,24},{1,1},{5... | collective-permute-start | bytes 798728 | tf_op jit(solution)/shard_map/ppermute | solution.py:730
  36.5 16.5 %collective-permute-start.15 = (bf16[1040,128]{1,0:T(8,128)(2,1)S(1)}, bf16[1040,128]{1,0:T(8,128)(2,1)S(1)}, u32[]{:S(2)}, u32[]{:S(2)}) collective-permute-start(bf16[1040,128]{1,0:T(8,128)(2,1)S(1)} %get-tuple-element.61), channel_id=1, source_target_pairs={{4,24},{5,25},{6,26},{7,27}} | collective-permute-start | bytes 798728 | tf_op jit(solution)/shard_map/ppermute | solution.py:730
  44.6 11.3 %collective-permute-start.12 = (f32[8,256]{1,0:T(8,128)S(1)}, f32[8,256]{1,0:T(8,128)S(1)}, u32[]{:S(2)}, u32[]{:S(2)}) collective-permute-start(f32[8,256]{1,0:T(8,128)S(1)} %get-tuple-element.58.refs_4_.refs_3_), channel_id=1, source_target_pairs={{0,3},{1,2},{2,1},{3,0},{4,7},{5,6},{6,5},{7,4},{8,11},{9,10},{10,... | collective-permute-start | bytes 24584 | tf_op jit(solution)/shard_map/ppermute | solution.py:818
  50.7 5.3 %collective-permute-start.11 = (f32[8,256]{1,0:T(8,128)S(1)}, f32[8,256]{1,0:T(8,128)S(1)}, u32[]{:S(2)}, u32[]{:S(2)}) collective-permute-start(f32[8,256]{1,0:T(8,128)S(1)} %get-tuple-element.58.refs_4_.refs_3_), channel_id=1, source_target_pairs={{0,2},{1,3},{2,0},{3,1},{4,6},{5,7},{6,4},{7,5},{8,10},{9,11},{10,... | collective-permute-start | bytes 24584 | tf_op jit(solution)/shard_map/ppermute | solution.py:818
  50.9 5.0 %collective-permute-start.10 = (f32[8,256]{1,0:T(8,128)S(1)}, f32[8,256]{1,0:T(8,128)S(1)}, u32[]{:S(2)}, u32[]{:S(2)}) collective-permute-start(f32[8,256]{1,0:T(8,128)S(1)} %get-tuple-element.58.refs_4_.refs_3_), channel_id=1, source_target_pairs={{0,1},{1,0},{2,3},{3,2},{4,5},{5,4},{6,7},{7,6},{8,9},{9,8},{10,11... | collective-permute-start | bytes 24584 | tf_op jit(solution)/shard_map/ppermute | solution.py:818
  53.1 2.9 %copy-start.1 = (bf16[256,16,128]{2,1,0:T(8,128)(2,1)S(1)}, bf16[256,16,128]{2,1,0:T(8,128)(2,1)}, u32[]{:S(2)}) copy-start(bf16[256,16,128]{2,1,0:T(8,128)(2,1)} %param.13) | copy-start | bytes 3145732
  53.1 2.8 %copy-start.2 = (f32[16,128]{1,0:T(8,128)S(1)}, f32[16,128]{1,0:T(8,128)}, u32[]{:S(2)}) copy-start(f32[16,128]{1,0:T(8,128)} %refs_0_.1) | copy-start | bytes 24580

commit v19 on v17

--- a/solution.py
+++ b/solution.py
@@ -787,9 +787,8 @@
     if parts > 1:
         done, lane = inner_of(0, [done], [ahead])
     second = send(lane, [(b, b + 2) for b in range(2, blocks - 2)])
-    run, lane, own_copy = group_map(place, quarters, size, [done], [lane, own_kv])
+    run, lane = group_map(place, quarters, size, [done], [lane])
     first_cross = send(lane, swap)
-    beside = send(own_copy, swap)
     stages = (blocks // GROUP_BLOCKS).bit_length() - 1
     before, done = None, run
     for stage in range(stages):
@@ -800,14 +799,14 @@
         else:
             run, before = scan_step(place, stage + 2, run, came, before, size, [done])
             done = run
+    assert window % 2 == 0 or window == 5
+    payload = pick(place, own_kv, second, [done])
+    slot = (send(payload, [(b, b + 1) for b in everyone]), (window if window % 2 else blocks, 1))
     *priors, prior_doc = prior_states(place, stages + 1, quarters, came, before, size, [done])
     priors = [priors[0]] + [send(priors[j], [(b, b ^ j) for b in everyone]) for j in others]
     done = more_attention([(first_cross, (2, 3)), (second, (4, 4))], False, [prior_doc])
-    lane, own_copy = pass_on([second, own_kv], [done, *priors])
-    rest = [(send(lane, [(b, b ^ 1) for b in range(4, blocks)]), (4, 5))]
-    far = None
-    if window % 2:
-        far = send(own_copy, [(b, b + window) for b in range(1, blocks - window, 2)])
+    (lane,) = pass_on([second], [done, *priors])
+    rest = [(send(lane, swap), (4, 5))]
     for back in range(3, window // 2 + 1):
         lane = send(lane, forward)
         rest.append((lane, (2 * back, 2 * back)))
@@ -816,12 +815,11 @@
     sums = [squares]
     for other in range(1, tensor):
         sums.append(lax.ppermute(squares, "tp", [(t, t ^ other) for t in range(tensor)]))
-    slot = beside if far is None else pick(place, far, beside, [squares])
-    rest.insert(0, (slot, (blocks if far is None else window, 1)))
+    rest.insert(0, slot)
     done = squares
     while rest:
-        got = more_attention(rest[:2], len(rest) <= 2, [done])
-        rest, done = rest[2:], got
+        got = more_attention(rest[:1], len(rest) == 1, [done])
+        rest, done = rest[1:], got
     soft_out, done = got
     lin_out = finish(norm_gain, flat(lin_gate), mixed, sums, tokens, heads, [done])
     shape = (tokens, heads, HEAD_DIM)

time: 57.9 us -> 56.4 us (0.974)
  the two profiles are of different devices: /device:TPU:26 before, /device:TPU:0 now
where the time goes in v19:
time: 56.4 us; the launch traced here: 56.2 us
  Pallas kernels  25.2 us (45%)
  starting transfers between devices  17 us (30%)
  waiting for transfers between devices  12.9 us (23%)
  between operations  1.01 us (2%)
    pallas_call x15, Pallas kernels, call(): pl.pallas_call(run, out_shape=outs, in_specs=[SMEM] * len(scalars) + [HBM...  25.2 us
    ppermute x12, starting transfers between devices, send(): return lax.ppermute(x, 'seq', [(a, b % blocks) for a, b in pairs])  15.1 us
    ppermute x12, waiting for transfers between devices, send(): return lax.ppermute(x, 'seq', [(a, b % blocks) for a, b in pairs])  12.9 us
    ppermute x3, starting transfers between devices, body(): lax.ppermute(squares, 'tp', [(t, t ^ other) for t in range(tensor)])  1.89 us
  transfers between devices with their start and end apart: 15, of which 5 were waited for; matrix products, arithmetic and copies ran while one was open for 0% of the time, Pallas kernels for 39%

profile of v19, /device:TPU:0, one launch (start us, length us, event | category | flops | bytes accessed | tf_op | source)
XLA Modules:
  0.0 56.2 jit_solution(14512095664236838168)
XLA Ops:
  0.6 1.9 %fetch.1 = (bf16[1040,128]{1,0:T(8,128)(2,1)S(1)}, f32[16,128]{1,0:T(8,128)S(1)}, f32[256,128]{1,0:T(8,128)S(1)}, bf16[4096,128]{1,0:T(8,128)(2,1)S(1)}, bf16[4096,128]{1,0:T(8,128)(2,1)S(1)}) custom-call(s32[1]{0:T(128)} %bitcast.2.refs_0_, s32[2,128]{1,0:T(2,128)} %bitcast.23, f32[16,256]{1,0:T(8,128)} %bitcast.22, bf16[2048,128]{1,0:T(8,128)(2,1)} %bitcast.20, ...), custom_call_target="tpu_custom_call" | custom-call | bytes 3145728 | tf_op jit(solution)/shard_map/fetch/pallas_call | solution.py:68
  2.6 3.1 %collective-permute-start.3 = (bf16[1040,128]{1,0:T(8,128)(2,1)S(1)}, bf16[1040,128]{1,0:T(8,128)(2,1)S(1)}, u32[]{:S(2)}, u32[]{:S(2)}) collective-permute-start(bf16[1040,128]{1,0:T(8,128)(2,1)S(1)} %get-tuple-element.39.refs_3_.refs_1_), channel_id=1, source_target_pairs={{0,8},{4,12},{8,16},{12,20},{16,24},{20,28},{24,0},{28,4},{1,9},{5... | collective-permute-start | bytes 798728 | tf_op jit(solution)/shard_map/ppermute | solution.py:730
  5.7 3.8 %block_state.1 = (bf16[528,128]{1,0:T(8,128)(2,1)S(1)}, bf16[528,128]{1,0:T(8,128)(2,1)S(1)}, bf16[528,128]{1,0:T(8,128)(2,1)S(1)}, bf16[528,128]{1,0:T(8,128)(2,1)S(1)}, bf16[4096,128]{1,0:T(8,128)(2,1)S(1)}) custom-call(s32[1]{0:T(128)} %bitcast.1.refs_0_, bf16[4096,128]{1,0:T(8,128)(2,1)} %bitcast.19, ...), custom_call_target="tpu_custom_call" | custom-call | flops 134217728 | bytes 5242880 | tf_op jit(solution)/shard_map/block_state/pallas_call | solution.py:68
  9.4 0.0 copy-start
  9.5 1.6 %collective-permute-start = (bf16[528,128]{1,0:T(8,128)(2,1)S(1)}, bf16[528,128]{1,0:T(8,128)(2,1)S(1)}, u32[]{:S(2)}, u32[]{:S(2)}) collective-permute-start(bf16[528,128]{1,0:T(8,128)(2,1)S(1)} %get-tuple-element.35), channel_id=1, source_target_pairs={{0,4},{4,0},{8,12},{12,8},{16,20},{20,16},{24,28},{28,24},{1,5},{5... | collective-permute-start | bytes 405512 | tf_op jit(solution)/shard_map/ppermute | solution.py:730
  11.1 1.6 %collective-permute-start.1 = (bf16[528,128]{1,0:T(8,128)(2,1)S(1)}, bf16[528,128]{1,0:T(8,128)(2,1)S(1)}, u32[]{:S(2)}, u32[]{:S(2)}) collective-permute-start(bf16[528,128]{1,0:T(8,128)(2,1)S(1)} %get-tuple-element.36), channel_id=1, source_target_pairs={{0,8},{4,12},{8,0},{12,4},{16,24},{20,28},{24,16},{28,20},{1,9},{5... | collective-permute-start | bytes 405512 | tf_op jit(solution)/shard_map/ppermute | solution.py:730
  12.6 0.4 collective-permute-start.2
  13.0 1.9 %attend.5 = (bf16[2,2048,256]{2,1,0:T(8,128)(2,1)S(1)}, f32[2,144,2048]{2,1,0:T(8,128)S(1)}) custom-call(s32[1]{0:T(128)} %bitcast.1.refs_0_, f32[16,128]{1,0:T(8,128)S(1)} %get-tuple-element.30.refs_3_.refs_1_, bf16[4096,128]{1,0:T(8,128)(2,1)S(1)} %get-tuple-element.38.refs_2_, bf16[1040,128]{1,0:T(8,128)(2,1)S(1)} %get-tuple-element.39.refs_3_.refs_1_, ...), custom_call_target="tpu_custom_call" | custom-call | flops 1073741824 | bytes 8388608 | tf_op jit(solution)/shard_map/attend/pallas_call | solution.py:68
  15.0 0.0 collective-permute-done.3.refs_6_
  15.0 0.0 copy-done
  15.0 1.9 %inner_part.2 = (f32[2048,128]{1,0:T(8,128)S(1)}, bf16[2048,128]{1,0:T(8,128)(2,1)S(1)}, bf16[1040,128]{1,0:T(8,128)(2,1)S(1)}) custom-call(f32[256,128]{1,0:T(8,128)S(1)} %get-tuple-element.31.refs_2_.refs_0_.refs_3_, f32[16,128]{1,0:T(8,128)S(1)} %get-tuple-element.30.refs_3_.refs_1_, bf16[4096,128]{1,0:T(8,128)(2,1)S(1)} %bitcast.13, ...), custom_call_target="tpu_custom_call" | custom-call | flops 268435456 | bytes 6291456 | tf_op jit(solution)/shard_map/inner_part/pallas_call | solution.py:68
  16.9 0.7 %collective-permute-start.9 = (bf16[1040,128]{1,0:T(8,128)(2,1)S(1)}, bf16[1040,128]{1,0:T(8,128)(2,1)S(1)}, u32[]{:S(2)}, u32[]{:S(2)}) collective-permute-start(bf16[1040,128]{1,0:T(8,128)(2,1)S(1)} %get-tuple-element.42.refs_6_), channel_id=1, source_target_pairs={{8,16},{12,20},{16,24},{20,28},{9,17},{13,21},{17,25},{21,29},{10,... | collective-permute-start | bytes 798728 | tf_op jit(solution)/shard_map/ppermute | solution.py:730
  17.6 0.0 collective-permute-done.refs_2_
  17.6 0.0 collective-permute-done.1.refs_3_
  17.6 3.2 %collective-permute-done.2.refs_4_ = bf16[528,128]{1,0:T(8,128)(2,1)S(1)} collective-permute-done((bf16[528,128]{1,0:T(8,128)(2,1)S(1)}, bf16[528,128]{1,0:T(8,128)(2,1)S(1)}, u32[]{:S(2)}, u32[]{:S(2)}) %collective-permute-start.2) | collective-permute-done | bytes 135200 | tf_op jit(solution)/shard_map/ppermute | solution.py:730
  20.8 0.2 group_map.1
  21.1 0.6 %collective-permute-start.8 = (bf16[1040,128]{1,0:T(8,128)(2,1)S(1)}, bf16[1040,128]{1,0:T(8,128)(2,1)S(1)}, u32[]{:S(2)}, u32[]{:S(2)}) collective-permute-start(bf16[1040,128]{1,0:T(8,128)(2,1)S(1)} %get-tuple-element.45.refs_3_), channel_id=1, source_target_pairs={{0,4},{4,0},{8,12},{12,8},{16,20},{20,16},{24,28},{28,24},{1,5},{5... | collective-permute-start | bytes 798728 | tf_op jit(solution)/shard_map/ppermute | solution.py:730
  21.6 1.8 %collective-permute-start.4 = (bf16[528,128]{1,0:T(8,128)(2,1)S(1)}, bf16[528,128]{1,0:T(8,128)(2,1)S(1)}, u32[]{:S(2)}, u32[]{:S(2)}) collective-permute-start(bf16[528,128]{1,0:T(8,128)(2,1)S(1)} %get-tuple-element.43.refs_4_), channel_id=1, source_target_pairs={{0,16},{4,20},{8,24},{12,28},{16,0},{20,4},{24,8},{28,12},{1,17},{... | collective-permute-start | bytes 405512 | tf_op jit(solution)/shard_map/ppermute | solution.py:730
  23.5 1.9 %attend.6.refs_5_.refs_2_ = f32[2,144,2048]{2,1,0:T(8,128)S(1)} custom-call(s32[1]{0:T(128)} %bitcast.1.refs_0_, bf16[2,2048,256]{2,1,0:T(8,128)(2,1)S(1)} %get-tuple-element.44.refs_1_, f32[2,144,2048]{2,1,0:T(8,128)S(1)} %get-tuple-element.40.refs_5_.refs_2_, bf16[1040,128]{1,0:T(8,128)(2,1)S(1)} %get-tuple-element.45.refs_3_, ...), custom_call_target="tpu_custom_call" | custom-call | flops 1073741824 | bytes 8388608 | tf_op jit(solution)/shard_map/attend/pallas_call | solution.py:68
  25.4 1.9 %inner_part.3 = (f32[2048,128]{1,0:T(8,128)S(1)}, bf16[2048,128]{1,0:T(8,128)(2,1)S(1)}) custom-call(f32[256,128]{1,0:T(8,128)S(1)} %get-tuple-element.31.refs_2_.refs_0_.refs_3_, f32[16,128]{1,0:T(8,128)S(1)} %get-tuple-element.30.refs_3_.refs_1_, bf16[4096,128]{1,0:T(8,128)(2,1)S(1)} %bitcast.14, bf16[4096,128]{1,0:T(8,128)(2,1)S(1)} %get-tuple-element.32.refs_4_.refs_3_, ...), custom_call_target="tpu_custom_call" | custom-call | flops 268435456 | bytes 6291456 | tf_op jit(solution)/shard_map/inner_part/pallas_call | solution.py:68
  27.3 3.2 %collective-permute-done.4.refs_5_ = bf16[528,128]{1,0:T(8,128)(2,1)S(1)} collective-permute-done((bf16[528,128]{1,0:T(8,128)(2,1)S(1)}, bf16[528,128]{1,0:T(8,128)(2,1)S(1)}, u32[]{:S(2)}, u32[]{:S(2)}) %collective-permute-start.4) | collective-permute-done | bytes 135200 | tf_op jit(solution)/shard_map/ppermute | solution.py:730
  30.5 0.3 prior_states.1
  30.8 0.8 %collective-permute-start.5 = (bf16[512,128]{1,0:T(8,128)(2,1)S(1)}, bf16[512,128]{1,0:T(8,128)(2,1)S(1)}, u32[]{:S(2)}, u32[]{:S(2)}) collective-permute-start(bf16[512,128]{1,0:T(8,128)(2,1)S(1)} %get-tuple-element.51), channel_id=1, source_target_pairs={{0,4},{4,0},{8,12},{12,8},{16,20},{20,16},{24,28},{28,24},{1,5},{5... | collective-permute-start | bytes 393224 | tf_op jit(solution)/shard_map/ppermute | solution.py:730
  31.6 2.6 %collective-permute-start.6 = (bf16[512,128]{1,0:T(8,128)(2,1)S(1)}, bf16[512,128]{1,0:T(8,128)(2,1)S(1)}, u32[]{:S(2)}, u32[]{:S(2)}) collective-permute-start(bf16[512,128]{1,0:T(8,128)(2,1)S(1)} %get-tuple-element.52), channel_id=1, source_target_pairs={{0,8},{4,12},{8,0},{12,4},{16,24},{20,28},{24,16},{28,20},{1,9},{5... | collective-permute-start | bytes 393224 | tf_op jit(solution)/shard_map/ppermute | solution.py:730
  34.1 0.2 collective-permute-start.7
  34.3 0.0 collective-permute-done.9.refs_4_.refs_2_.refs_5_
  34.3 0.1 pick.1
  34.4 1.5 %collective-permute-start.13 = (bf16[1040,128]{1,0:T(8,128)(2,1)S(1)}, bf16[1040,128]{1,0:T(8,128)(2,1)S(1)}, u32[]{:S(2)}, u32[]{:S(2)}) collective-permute-start(bf16[1040,128]{1,0:T(8,128)(2,1)S(1)} %pick.1), channel_id=1, source_target_pairs={{0,4},{4,8},{8,12},{12,16},{16,20},{20,24},{24,28},{28,0},{1,5},{5... | collective-permute-start | bytes 798728 | tf_op jit(solution)/shard_map/ppermute | solution.py:730
  35.9 0.0 collective-permute-done.8.refs_3_
  35.9 3.3 %attend.7.refs_12_.refs_2_.refs_0_ = f32[2,144,2048]{2,1,0:T(8,128)S(1)} custom-call(s32[1]{0:T(128)} %bitcast.1.refs_0_, bf16[2,2048,256]{2,1,0:T(8,128)(2,1)S(1)} %get-tuple-element.44.refs_1_, f32[2,144,2048]{2,1,0:T(8,128)S(1)} %attend.6.refs_5_.refs_2_, bf16[1040,128]{1,0:T(8,128)(2,1)S(1)} %collective-permute-done.8.refs_3_, ...), custom_call_target="tpu_custom_call" | custom-call | flops 2147483648 | bytes 8388608 | tf_op jit(solution)/shard_map/attend/pallas_call | solution.py:68
  39.2 0.0 collective-permute-done.5.refs_9_.refs_2_
  39.2 0.0 collective-permute-done.6.refs_10_.refs_3_
  39.3 1.7 %collective-permute-done.7.refs_11_.refs_4_ = bf16[512,128]{1,0:T(8,128)(2,1)S(1)} collective-permute-done((bf16[512,128]{1,0:T(8,128)(2,1)S(1)}, bf16[512,128]{1,0:T(8,128)(2,1)S(1)}, u32[]{:S(2)}, u32[]{:S(2)}) %collective-permute-start.7) | collective-permute-done | bytes 131104 | tf_op jit(solution)/shard_map/ppermute | solution.py:730
  41.0 0.4 collective-permute-start.14
  41.4 1.6 %mix.1 = (f32[4096,128]{1,0:T(8,128)S(1)}, f32[8,256]{1,0:T(8,128)S(1)}) custom-call(s32[1]{0:T(128)} %bitcast.1.refs_0_, f32[16,128]{1,0:T(8,128)S(1)} %get-tuple-element.30.refs_3_.refs_1_, f32[8,128]{1,0:T(8,128)S(1)} %get-tuple-element.47.refs_5_.refs_2_, f32[256,128]{1,0:T(8,128)S(1)} %get-tuple-element.31.refs_2_.refs_0_.refs_3_, ...), custom_call_target="tpu_custom_call" | custom-call | flops 134217728 | bytes 5242880 | tf_op jit(solution)/shard_map/mix/pallas_call | solution.py:68
  43.0 0.0 collective-permute-start.12
  43.0 1.6 %collective-permute-start.11 = (f32[8,256]{1,0:T(8,128)S(1)}, f32[8,256]{1,0:T(8,128)S(1)}, u32[]{:S(2)}, u32[]{:S(2)}) collective-permute-start(f32[8,256]{1,0:T(8,128)S(1)} %get-tuple-element.55.refs_4_.refs_3_), channel_id=1, source_target_pairs={{0,2},{1,3},{2,0},{3,1},{4,6},{5,7},{6,4},{7,5},{8,10},{9,11},{10,... | collective-permute-start | bytes 24584 | tf_op jit(solution)/shard_map/ppermute | solution.py:817
  44.5 0.3 collective-permute-start.10
  44.8 2.5 %collective-permute-done.13.refs_3_ = bf16[1040,128]{1,0:T(8,128)(2,1)S(1)} collective-permute-done((bf16[1040,128]{1,0:T(8,128)(2,1)S(1)}, bf16[1040,128]{1,0:T(8,128)(2,1)S(1)}, u32[]{:S(2)}, u32[]{:S(2)}) %collective-permute-start.13) | collective-permute-done | bytes 266272 | tf_op jit(solution)/shard_map/ppermute | solution.py:730
  47.4 1.9 %attend.8.refs_2_.refs_4_ = f32[2,144,2048]{2,1,0:T(8,128)S(1)} custom-call(s32[1]{0:T(128)} %bitcast.1.refs_0_, bf16[2,2048,256]{2,1,0:T(8,128)(2,1)S(1)} %get-tuple-element.44.refs_1_, f32[2,144,2048]{2,1,0:T(8,128)S(1)} %attend.7.refs_12_.refs_2_.refs_0_, bf16[1040,128]{1,0:T(8,128)(2,1)S(1)} %collective-permute-done.13.refs_3_, ...), custom_call_target="tpu_custom_call" | custom-call | flops 1073741824 | bytes 8388608 | tf_op jit(solution)/shard_map/attend/pallas_call | solution.py:68
  49.3 0.0 copy-start.1
  49.3 0.0 copy-start.2
  49.3 2.2 %collective-permute-done.14.refs_3_ = bf16[1040,128]{1,0:T(8,128)(2,1)S(1)} collective-permute-done((bf16[1040,128]{1,0:T(8,128)(2,1)S(1)}, bf16[1040,128]{1,0:T(8,128)(2,1)S(1)}, u32[]{:S(2)}, u32[]{:S(2)}) %collective-permute-start.14) | collective-permute-done | bytes 266272 | tf_op jit(solution)/shard_map/ppermute | solution.py:730
  51.5 2.8 %attend.9 = (bf16[4096,128]{1,0:T(8,128)(2,1)}, f32[8,128]{1,0:T(8,128)S(1)}) custom-call(s32[1]{0:T(128)} %bitcast.1.refs_0_, bf16[2,2048,256]{2,1,0:T(8,128)(2,1)S(1)} %get-tuple-element.44.refs_1_, f32[2,144,2048]{2,1,0:T(8,128)S(1)} %attend.8.refs_2_.refs_4_, bf16[1040,128]{1,0:T(8,128)(2,1)S(1)} %collective-permute-done.14.refs_3_, ...), custom_call_target="tpu_custom_call" | custom-call | flops 1073741824 | bytes 8388608 | tf_op jit(solution)/shard_map/attend/pallas_call | solution.py:68
  54.3 0.0 collective-permute-done.12.refs_6_
  54.4 0.0 collective-permute-done.11.refs_5_
  54.4 0.0 collective-permute-done.10.refs_4_
  54.4 1.7 %finish.1 = bf16[4096,128]{1,0:T(8,128)(2,1)} custom-call(f32[16,128]{1,0:T(8,128)S(1)} %copy-done.2, bf16[4096,128]{1,0:T(8,128)(2,1)S(1)} %bitcast.15, f32[4096,128]{1,0:T(8,128)S(1)} %get-tuple-element.54.refs_2_, f32[8,256]{1,0:T(8,128)S(1)} %get-tuple-element.55.refs_4_.refs_3_, f32[8,256]{1,0:T(8,128)S(1)} %collective-permute-done.10.refs_4_, ...), custom_call_target="tpu_custom_call" | custom-call | bytes 4194304 | tf_op jit(solution)/shard_map/finish/pallas_call | solution.py:68
  (3 shorter events, 0.0 us)
Async XLA Ops:
  2.6 12.4 %collective-permute-start.3 = (bf16[1040,128]{1,0:T(8,128)(2,1)S(1)}, bf16[1040,128]{1,0:T(8,128)(2,1)S(1)}, u32[]{:S(2)}, u32[]{:S(2)}) collective-permute-start(bf16[1040,128]{1,0:T(8,128)(2,1)S(1)} %get-tuple-element.39.refs_3_.refs_1_), channel_id=1, source_target_pairs={{0,8},{4,12},{8,16},{12,20},{16,24},{20,28},{24,0},{28,4},{1,9},{5... | collective-permute-start | bytes 798728 | tf_op jit(solution)/shard_map/ppermute | solution.py:730
  9.4 5.5 %copy-start = (bf16[256,16,128]{2,1,0:T(8,128)(2,1)S(1)}, bf16[256,16,128]{2,1,0:T(8,128)(2,1)}, u32[]{:S(2)}) copy-start(bf16[256,16,128]{2,1,0:T(8,128)(2,1)} %param.10) | copy-start | bytes 3145732
  9.5 8.1 %collective-permute-start = (bf16[528,128]{1,0:T(8,128)(2,1)S(1)}, bf16[528,128]{1,0:T(8,128)(2,1)S(1)}, u32[]{:S(2)}, u32[]{:S(2)}) collective-permute-start(bf16[528,128]{1,0:T(8,128)(2,1)S(1)} %get-tuple-element.35), channel_id=1, source_target_pairs={{0,4},{4,0},{8,12},{12,8},{16,20},{20,16},{24,28},{28,24},{1,5},{5... | collective-permute-start | bytes 405512 | tf_op jit(solution)/shard_map/ppermute | solution.py:730
  11.1 6.6 %collective-permute-start.1 = (bf16[528,128]{1,0:T(8,128)(2,1)S(1)}, bf16[528,128]{1,0:T(8,128)(2,1)S(1)}, u32[]{:S(2)}, u32[]{:S(2)}) collective-permute-start(bf16[528,128]{1,0:T(8,128)(2,1)S(1)} %get-tuple-element.36), channel_id=1, source_target_pairs={{0,8},{4,12},{8,0},{12,4},{16,24},{20,28},{24,16},{28,20},{1,9},{5... | collective-permute-start | bytes 405512 | tf_op jit(solution)/shard_map/ppermute | solution.py:730
  12.6 8.2 %collective-permute-start.2 = (bf16[528,128]{1,0:T(8,128)(2,1)S(1)}, bf16[528,128]{1,0:T(8,128)(2,1)S(1)}, u32[]{:S(2)}, u32[]{:S(2)}) collective-permute-start(bf16[528,128]{1,0:T(8,128)(2,1)S(1)} %get-tuple-element.37), channel_id=1, source_target_pairs={{0,12},{4,8},{8,4},{12,0},{16,28},{20,24},{24,20},{28,16},{1,13},{... | collective-permute-start | bytes 405512 | tf_op jit(solution)/shard_map/ppermute | solution.py:730
  16.9 17.4 %collective-permute-start.9 = (bf16[1040,128]{1,0:T(8,128)(2,1)S(1)}, bf16[1040,128]{1,0:T(8,128)(2,1)S(1)}, u32[]{:S(2)}, u32[]{:S(2)}) collective-permute-start(bf16[1040,128]{1,0:T(8,128)(2,1)S(1)} %get-tuple-element.42.refs_6_), channel_id=1, source_target_pairs={{8,16},{12,20},{16,24},{20,28},{9,17},{13,21},{17,25},{21,29},{10,... | collective-permute-start | bytes 798728 | tf_op jit(solution)/shard_map/ppermute | solution.py:730
  21.1 14.8 %collective-permute-start.8 = (bf16[1040,128]{1,0:T(8,128)(2,1)S(1)}, bf16[1040,128]{1,0:T(8,128)(2,1)S(1)}, u32[]{:S(2)}, u32[]{:S(2)}) collective-permute-start(bf16[1040,128]{1,0:T(8,128)(2,1)S(1)} %get-tuple-element.45.refs_3_), channel_id=1, source_target_pairs={{0,4},{4,0},{8,12},{12,8},{16,20},{20,16},{24,28},{28,24},{1,5},{5... | collective-permute-start | bytes 798728 | tf_op jit(solution)/shard_map/ppermute | solution.py:730
  21.6 8.9 %collective-permute-start.4 = (bf16[528,128]{1,0:T(8,128)(2,1)S(1)}, bf16[528,128]{1,0:T(8,128)(2,1)S(1)}, u32[]{:S(2)}, u32[]{:S(2)}) collective-permute-start(bf16[528,128]{1,0:T(8,128)(2,1)S(1)} %get-tuple-element.43.refs_4_), channel_id=1, source_target_pairs={{0,16},{4,20},{8,24},{12,28},{16,0},{20,4},{24,8},{28,12},{1,17},{... | collective-permute-start | bytes 405512 | tf_op jit(solution)/shard_map/ppermute | solution.py:730
  30.8 8.5 %collective-permute-start.5 = (bf16[512,128]{1,0:T(8,128)(2,1)S(1)}, bf16[512,128]{1,0:T(8,128)(2,1)S(1)}, u32[]{:S(2)}, u32[]{:S(2)}) collective-permute-start(bf16[512,128]{1,0:T(8,128)(2,1)S(1)} %get-tuple-element.51), channel_id=1, source_target_pairs={{0,4},{4,0},{8,12},{12,8},{16,20},{20,16},{24,28},{28,24},{1,5},{5... | collective-permute-start | bytes 393224 | tf_op jit(solution)/shard_map/ppermute | solution.py:730
  31.6 7.7 %collective-permute-start.6 = (bf16[512,128]{1,0:T(8,128)(2,1)S(1)}, bf16[512,128]{1,0:T(8,128)(2,1)S(1)}, u32[]{:S(2)}, u32[]{:S(2)}) collective-permute-start(bf16[512,128]{1,0:T(8,128)(2,1)S(1)} %get-tuple-element.52), channel_id=1, source_target_pairs={{0,8},{4,12},{8,0},{12,4},{16,24},{20,28},{24,16},{28,20},{1,9},{5... | collective-permute-start | bytes 393224 | tf_op jit(solution)/shard_map/ppermute | solution.py:730
  34.1 6.9 %collective-permute-start.7 = (bf16[512,128]{1,0:T(8,128)(2,1)S(1)}, bf16[512,128]{1,0:T(8,128)(2,1)S(1)}, u32[]{:S(2)}, u32[]{:S(2)}) collective-permute-start(bf16[512,128]{1,0:T(8,128)(2,1)S(1)} %get-tuple-element.53), channel_id=1, source_target_pairs={{0,12},{4,8},{8,4},{12,0},{16,28},{20,24},{24,20},{28,16},{1,13},{... | collective-permute-start | bytes 393224 | tf_op jit(solution)/shard_map/ppermute | solution.py:730
  34.4 12.9 %collective-permute-start.13 = (bf16[1040,128]{1,0:T(8,128)(2,1)S(1)}, bf16[1040,128]{1,0:T(8,128)(2,1)S(1)}, u32[]{:S(2)}, u32[]{:S(2)}) collective-permute-start(bf16[1040,128]{1,0:T(8,128)(2,1)S(1)} %pick.1), channel_id=1, source_target_pairs={{0,4},{4,8},{8,12},{12,16},{16,20},{20,24},{24,28},{28,0},{1,5},{5... | collective-permute-start | bytes 798728 | tf_op jit(solution)/shard_map/ppermute | solution.py:730
  41.0 10.5 %collective-permute-start.14 = (bf16[1040,128]{1,0:T(8,128)(2,1)S(1)}, bf16[1040,128]{1,0:T(8,128)(2,1)S(1)}, u32[]{:S(2)}, u32[]{:S(2)}) collective-permute-start(bf16[1040,128]{1,0:T(8,128)(2,1)S(1)} %pass_on.1), channel_id=1, source_target_pairs={{0,4},{4,0},{8,12},{12,8},{16,20},{20,16},{24,28},{28,24},{1,5},{5... | collective-permute-start | bytes 798728 | tf_op jit(solution)/shard_map/ppermute | solution.py:730
  43.0 11.4 %collective-permute-start.12 = (f32[8,256]{1,0:T(8,128)S(1)}, f32[8,256]{1,0:T(8,128)S(1)}, u32[]{:S(2)}, u32[]{:S(2)}) collective-permute-start(f32[8,256]{1,0:T(8,128)S(1)} %get-tuple-element.55.refs_4_.refs_3_), channel_id=1, source_target_pairs={{0,3},{1,2},{2,1},{3,0},{4,7},{5,6},{6,5},{7,4},{8,11},{9,10},{10,... | collective-permute-start | bytes 24584 | tf_op jit(solution)/shard_map/ppermute | solution.py:817
  43.0 11.4 %collective-permute-start.11 = (f32[8,256]{1,0:T(8,128)S(1)}, f32[8,256]{1,0:T(8,128)S(1)}, u32[]{:S(2)}, u32[]{:S(2)}) collective-permute-start(f32[8,256]{1,0:T(8,128)S(1)} %get-tuple-element.55.refs_4_.refs_3_), channel_id=1, source_target_pairs={{0,2},{1,3},{2,0},{3,1},{4,6},{5,7},{6,4},{7,5},{8,10},{9,11},{10,... | collective-permute-start | bytes 24584 | tf_op jit(solution)/shard_map/ppermute | solution.py:817
  44.5 9.9 %collective-permute-start.10 = (f32[8,256]{1,0:T(8,128)S(1)}, f32[8,256]{1,0:T(8,128)S(1)}, u32[]{:S(2)}, u32[]{:S(2)}) collective-permute-start(f32[8,256]{1,0:T(8,128)S(1)} %get-tuple-element.55.refs_4_.refs_3_), channel_id=1, source_target_pairs={{0,1},{1,0},{2,3},{3,2},{4,5},{5,4},{6,7},{7,6},{8,9},{9,8},{10,11... | collective-permute-start | bytes 24584 | tf_op jit(solution)/shard_map/ppermute | solution.py:817
  49.3 5.1 %copy-start.1 = (bf16[256,16,128]{2,1,0:T(8,128)(2,1)S(1)}, bf16[256,16,128]{2,1,0:T(8,128)(2,1)}, u32[]{:S(2)}) copy-start(bf16[256,16,128]{2,1,0:T(8,128)(2,1)} %param.13) | copy-start | bytes 3145732
  49.3 5.1 %copy-start.2 = (f32[16,128]{1,0:T(8,128)S(1)}, f32[16,128]{1,0:T(8,128)}, u32[]{:S(2)}) copy-start(f32[16,128]{1,0:T(8,128)} %refs_0_.1) | copy-start | bytes 24580

commit v20 on v19

--- a/solution.py
+++ b/solution.py
@@ -802,7 +802,7 @@
     assert window % 2 == 0 or window == 5
     payload = pick(place, own_kv, second, [done])
     slot = (send(payload, [(b, b + 1) for b in everyone]), (window if window % 2 else blocks, 1))
-    *priors, prior_doc = prior_states(place, stages + 1, quarters, came, before, size, [done])
+    *priors, prior_doc = prior_states(place, stages + 1, quarters, came, before, size, [payload])
     priors = [priors[0]] + [send(priors[j], [(b, b ^ j) for b in everyone]) for j in others]
     done = more_attention([(first_cross, (2, 3)), (second, (4, 4))], False, [prior_doc])
     (lane,) = pass_on([second], [done, *priors])

time: 56.4 us -> 54 us (0.957)
  waiting for transfers between devices: 12.9 us -> 9.66 us
  starting transfers between devices: 17 us -> 17.9 us
    ppermute x12, waiting for transfers between devices: 12.9 us -> 9.65 us  [send(): return lax.ppermute(x, 'seq', [(a, b % blocks) for a, b in pairs])]
    ppermute x12, starting transfers between devices: 15.1 us -> 16 us  [send(): return lax.ppermute(x, 'seq', [(a, b % blocks) for a, b in pairs])]
  transfers between devices with their start and end apart: 15 -> 15, of which waited for: 5 -> 5; matrix products, arithmetic and copies ran while one was open for 0% -> 0% of each run, Pallas kernels for 39% -> 40%
where the time goes in v20:
time: 54 us; the launch traced here: 53.8 us
  Pallas kernels  25.2 us (47%)
  starting transfers between devices  17.9 us (33%)
  waiting for transfers between devices  9.66 us (18%)
  between operations  1.01 us (2%)
    pallas_call x15, Pallas kernels, call(): pl.pallas_call(run, out_shape=outs, in_specs=[SMEM] * len(scalars) + [HBM...  25.2 us
    ppermute x12, starting transfers between devices, send(): return lax.ppermute(x, 'seq', [(a, b % blocks) for a, b in pairs])  16 us
    ppermute x12, waiting for transfers between devices, send(): return lax.ppermute(x, 'seq', [(a, b % blocks) for a, b in pairs])  9.65 us
    ppermute x3, starting transfers between devices, body(): lax.ppermute(squares, 'tp', [(t, t ^ other) for t in range(tensor)])  1.89 us
  transfers between devices with their start and end apart: 15, of which 5 were waited for; matrix products, arithmetic and copies ran while one was open for 0% of the time, Pallas kernels for 40%

profile of v20, /device:TPU:0, one launch (start us, length us, event | category | flops | bytes accessed | tf_op | source)
XLA Modules:
  0.0 53.8 jit_solution(3777637043358467177)
XLA Ops:
  0.6 1.9 %fetch.1 = (bf16[1040,128]{1,0:T(8,128)(2,1)S(1)}, f32[16,128]{1,0:T(8,128)S(1)}, f32[256,128]{1,0:T(8,128)S(1)}, bf16[4096,128]{1,0:T(8,128)(2,1)S(1)}, bf16[4096,128]{1,0:T(8,128)(2,1)S(1)}) custom-call(s32[1]{0:T(128)} %bitcast.2.refs_0_, s32[2,128]{1,0:T(2,128)} %bitcast.23, f32[16,256]{1,0:T(8,128)} %bitcast.22, bf16[2048,128]{1,0:T(8,128)(2,1)} %bitcast.20, ...), custom_call_target="tpu_custom_call" | custom-call | bytes 3145728 | tf_op jit(solution)/shard_map/fetch/pallas_call | solution.py:68
  2.6 3.1 %collective-permute-start.3 = (bf16[1040,128]{1,0:T(8,128)(2,1)S(1)}, bf16[1040,128]{1,0:T(8,128)(2,1)S(1)}, u32[]{:S(2)}, u32[]{:S(2)}) collective-permute-start(bf16[1040,128]{1,0:T(8,128)(2,1)S(1)} %get-tuple-element.39.refs_3_.refs_1_), channel_id=1, source_target_pairs={{0,8},{4,12},{8,16},{12,20},{16,24},{20,28},{24,0},{28,4},{1,9},{5... | collective-permute-start | bytes 798728 | tf_op jit(solution)/shard_map/ppermute | solution.py:730
  5.7 3.8 %block_state.1 = (bf16[528,128]{1,0:T(8,128)(2,1)S(1)}, bf16[528,128]{1,0:T(8,128)(2,1)S(1)}, bf16[528,128]{1,0:T(8,128)(2,1)S(1)}, bf16[528,128]{1,0:T(8,128)(2,1)S(1)}, bf16[4096,128]{1,0:T(8,128)(2,1)S(1)}) custom-call(s32[1]{0:T(128)} %bitcast.1.refs_0_, bf16[4096,128]{1,0:T(8,128)(2,1)} %bitcast.19, ...), custom_call_target="tpu_custom_call" | custom-call | flops 134217728 | bytes 5242880 | tf_op jit(solution)/shard_map/block_state/pallas_call | solution.py:68
  9.4 0.0 copy-start
  9.5 1.6 %collective-permute-start = (bf16[528,128]{1,0:T(8,128)(2,1)S(1)}, bf16[528,128]{1,0:T(8,128)(2,1)S(1)}, u32[]{:S(2)}, u32[]{:S(2)}) collective-permute-start(bf16[528,128]{1,0:T(8,128)(2,1)S(1)} %get-tuple-element.35), channel_id=1, source_target_pairs={{0,4},{4,0},{8,12},{12,8},{16,20},{20,16},{24,28},{28,24},{1,5},{5... | collective-permute-start | bytes 405512 | tf_op jit(solution)/shard_map/ppermute | solution.py:730
  11.1 1.6 %collective-permute-start.1 = (bf16[528,128]{1,0:T(8,128)(2,1)S(1)}, bf16[528,128]{1,0:T(8,128)(2,1)S(1)}, u32[]{:S(2)}, u32[]{:S(2)}) collective-permute-start(bf16[528,128]{1,0:T(8,128)(2,1)S(1)} %get-tuple-element.36), channel_id=1, source_target_pairs={{0,8},{4,12},{8,0},{12,4},{16,24},{20,28},{24,16},{28,20},{1,9},{5... | collective-permute-start | bytes 405512 | tf_op jit(solution)/shard_map/ppermute | solution.py:730
  12.6 0.4 collective-permute-start.2
  13.0 1.9 %attend.5 = (bf16[2,2048,256]{2,1,0:T(8,128)(2,1)S(1)}, f32[2,144,2048]{2,1,0:T(8,128)S(1)}) custom-call(s32[1]{0:T(128)} %bitcast.1.refs_0_, f32[16,128]{1,0:T(8,128)S(1)} %get-tuple-element.30.refs_3_.refs_1_, bf16[4096,128]{1,0:T(8,128)(2,1)S(1)} %get-tuple-element.38.refs_2_, bf16[1040,128]{1,0:T(8,128)(2,1)S(1)} %get-tuple-element.39.refs_3_.refs_1_, ...), custom_call_target="tpu_custom_call" | custom-call | flops 1073741824 | bytes 8388608 | tf_op jit(solution)/shard_map/attend/pallas_call | solution.py:68
  14.9 0.0 collective-permute-done.3.refs_6_
  15.0 0.0 copy-done
  15.0 1.9 %inner_part.2 = (f32[2048,128]{1,0:T(8,128)S(1)}, bf16[2048,128]{1,0:T(8,128)(2,1)S(1)}, bf16[1040,128]{1,0:T(8,128)(2,1)S(1)}) custom-call(f32[256,128]{1,0:T(8,128)S(1)} %get-tuple-element.31.refs_2_.refs_0_.refs_3_, f32[16,128]{1,0:T(8,128)S(1)} %get-tuple-element.30.refs_3_.refs_1_, bf16[4096,128]{1,0:T(8,128)(2,1)S(1)} %bitcast.13, ...), custom_call_target="tpu_custom_call" | custom-call | flops 268435456 | bytes 6291456 | tf_op jit(solution)/shard_map/inner_part/pallas_call | solution.py:68
  16.9 0.7 %collective-permute-start.5 = (bf16[1040,128]{1,0:T(8,128)(2,1)S(1)}, bf16[1040,128]{1,0:T(8,128)(2,1)S(1)}, u32[]{:S(2)}, u32[]{:S(2)}) collective-permute-start(bf16[1040,128]{1,0:T(8,128)(2,1)S(1)} %get-tuple-element.42.refs_6_), channel_id=1, source_target_pairs={{8,16},{12,20},{16,24},{20,28},{9,17},{13,21},{17,25},{21,29},{10,... | collective-permute-start | bytes 798728 | tf_op jit(solution)/shard_map/ppermute | solution.py:730
  17.6 0.0 collective-permute-done.refs_2_
  17.6 0.0 collective-permute-done.1.refs_3_
  17.6 3.2 %collective-permute-done.2.refs_4_ = bf16[528,128]{1,0:T(8,128)(2,1)S(1)} collective-permute-done((bf16[528,128]{1,0:T(8,128)(2,1)S(1)}, bf16[528,128]{1,0:T(8,128)(2,1)S(1)}, u32[]{:S(2)}, u32[]{:S(2)}) %collective-permute-start.2) | collective-permute-done | bytes 135200 | tf_op jit(solution)/shard_map/ppermute | solution.py:730
  20.8 0.2 group_map.1
  21.1 0.6 %collective-permute-start.9 = (bf16[1040,128]{1,0:T(8,128)(2,1)S(1)}, bf16[1040,128]{1,0:T(8,128)(2,1)S(1)}, u32[]{:S(2)}, u32[]{:S(2)}) collective-permute-start(bf16[1040,128]{1,0:T(8,128)(2,1)S(1)} %get-tuple-element.45.refs_3_), channel_id=1, source_target_pairs={{0,4},{4,0},{8,12},{12,8},{16,20},{20,16},{24,28},{28,24},{1,5},{5... | collective-permute-start | bytes 798728 | tf_op jit(solution)/shard_map/ppermute | solution.py:730
  21.6 1.8 %collective-permute-start.4 = (bf16[528,128]{1,0:T(8,128)(2,1)S(1)}, bf16[528,128]{1,0:T(8,128)(2,1)S(1)}, u32[]{:S(2)}, u32[]{:S(2)}) collective-permute-start(bf16[528,128]{1,0:T(8,128)(2,1)S(1)} %get-tuple-element.43.refs_4_), channel_id=1, source_target_pairs={{0,16},{4,20},{8,24},{12,28},{16,0},{20,4},{24,8},{28,12},{1,17},{... | collective-permute-start | bytes 405512 | tf_op jit(solution)/shard_map/ppermute | solution.py:730
  23.5 1.9 %attend.6.refs_5_.refs_2_ = f32[2,144,2048]{2,1,0:T(8,128)S(1)} custom-call(s32[1]{0:T(128)} %bitcast.1.refs_0_, bf16[2,2048,256]{2,1,0:T(8,128)(2,1)S(1)} %get-tuple-element.44.refs_1_, f32[2,144,2048]{2,1,0:T(8,128)S(1)} %get-tuple-element.40.refs_5_.refs_2_, bf16[1040,128]{1,0:T(8,128)(2,1)S(1)} %get-tuple-element.45.refs_3_, ...), custom_call_target="tpu_custom_call" | custom-call | flops 1073741824 | bytes 8388608 | tf_op jit(solution)/shard_map/attend/pallas_call | solution.py:68
  25.4 1.9 %inner_part.3 = (f32[2048,128]{1,0:T(8,128)S(1)}, bf16[2048,128]{1,0:T(8,128)(2,1)S(1)}) custom-call(f32[256,128]{1,0:T(8,128)S(1)} %get-tuple-element.31.refs_2_.refs_0_.refs_3_, f32[16,128]{1,0:T(8,128)S(1)} %get-tuple-element.30.refs_3_.refs_1_, bf16[4096,128]{1,0:T(8,128)(2,1)S(1)} %bitcast.14, bf16[4096,128]{1,0:T(8,128)(2,1)S(1)} %get-tuple-element.32.refs_4_.refs_3_, ...), custom_call_target="tpu_custom_call" | custom-call | flops 268435456 | bytes 6291456 | tf_op jit(solution)/shard_map/inner_part/pallas_call | solution.py:68
  27.3 0.0 collective-permute-done.5.refs_2_.refs_4_.refs_5_
  27.3 0.1 pick.1.refs_6_
  27.4 0.6 %collective-permute-start.13 = (bf16[1040,128]{1,0:T(8,128)(2,1)S(1)}, bf16[1040,128]{1,0:T(8,128)(2,1)S(1)}, u32[]{:S(2)}, u32[]{:S(2)}) collective-permute-start(bf16[1040,128]{1,0:T(8,128)(2,1)S(1)} %pick.1.refs_6_), channel_id=1, source_target_pairs={{0,4},{4,8},{8,12},{12,16},{16,20},{20,24},{24,28},{28,0},{1,5},{5... | collective-permute-start | bytes 798728 | tf_op jit(solution)/shard_map/ppermute | solution.py:730
  28.0 2.5 %collective-permute-done.4.refs_5_ = bf16[528,128]{1,0:T(8,128)(2,1)S(1)} collective-permute-done((bf16[528,128]{1,0:T(8,128)(2,1)S(1)}, bf16[528,128]{1,0:T(8,128)(2,1)S(1)}, u32[]{:S(2)}, u32[]{:S(2)}) %collective-permute-start.4) | collective-permute-done | bytes 135200 | tf_op jit(solution)/shard_map/ppermute | solution.py:730
  30.5 0.3 prior_states.1
  30.8 2.2 %collective-permute-start.6 = (bf16[512,128]{1,0:T(8,128)(2,1)S(1)}, bf16[512,128]{1,0:T(8,128)(2,1)S(1)}, u32[]{:S(2)}, u32[]{:S(2)}) collective-permute-start(bf16[512,128]{1,0:T(8,128)(2,1)S(1)} %get-tuple-element.51), channel_id=1, source_target_pairs={{0,4},{4,0},{8,12},{12,8},{16,20},{20,16},{24,28},{28,24},{1,5},{5... | collective-permute-start | bytes 393224 | tf_op jit(solution)/shard_map/ppermute | solution.py:730
  32.9 3.5 %collective-permute-start.7 = (bf16[512,128]{1,0:T(8,128)(2,1)S(1)}, bf16[512,128]{1,0:T(8,128)(2,1)S(1)}, u32[]{:S(2)}, u32[]{:S(2)}) collective-permute-start(bf16[512,128]{1,0:T(8,128)(2,1)S(1)} %get-tuple-element.52), channel_id=1, source_target_pairs={{0,8},{4,12},{8,0},{12,4},{16,24},{20,28},{24,16},{28,20},{1,9},{5... | collective-permute-start | bytes 393224 | tf_op jit(solution)/shard_map/ppermute | solution.py:730
  36.4 0.0 collective-permute-start.8
  36.4 0.0 collective-permute-done.9.refs_3_
  36.4 3.3 %attend.7.refs_12_.refs_2_.refs_0_ = f32[2,144,2048]{2,1,0:T(8,128)S(1)} custom-call(s32[1]{0:T(128)} %bitcast.1.refs_0_, bf16[2,2048,256]{2,1,0:T(8,128)(2,1)S(1)} %get-tuple-element.44.refs_1_, f32[2,144,2048]{2,1,0:T(8,128)S(1)} %attend.6.refs_5_.refs_2_, bf16[1040,128]{1,0:T(8,128)(2,1)S(1)} %collective-permute-done.9.refs_3_, ...), custom_call_target="tpu_custom_call" | custom-call | flops 2147483648 | bytes 8388608 | tf_op jit(solution)/shard_map/attend/pallas_call | solution.py:68
  39.8 0.8 %collective-permute-done.6.refs_9_.refs_2_ = bf16[512,128]{1,0:T(8,128)(2,1)S(1)} collective-permute-done((bf16[512,128]{1,0:T(8,128)(2,1)S(1)}, bf16[512,128]{1,0:T(8,128)(2,1)S(1)}, u32[]{:S(2)}, u32[]{:S(2)}) %collective-permute-start.6) | collective-permute-done | bytes 131104 | tf_op jit(solution)/shard_map/ppermute | solution.py:730
  40.6 0.0 collective-permute-done.7.refs_10_.refs_3_
  40.6 1.8 %collective-permute-done.8.refs_11_.refs_4_ = bf16[512,128]{1,0:T(8,128)(2,1)S(1)} collective-permute-done((bf16[512,128]{1,0:T(8,128)(2,1)S(1)}, bf16[512,128]{1,0:T(8,128)(2,1)S(1)}, u32[]{:S(2)}, u32[]{:S(2)}) %collective-permute-start.8) | collective-permute-done | bytes 131104 | tf_op jit(solution)/shard_map/ppermute | solution.py:730
  42.4 0.1 collective-permute-start.14
  42.5 1.6 %mix.1 = (f32[4096,128]{1,0:T(8,128)S(1)}, f32[8,256]{1,0:T(8,128)S(1)}) custom-call(s32[1]{0:T(128)} %bitcast.1.refs_0_, f32[16,128]{1,0:T(8,128)S(1)} %get-tuple-element.30.refs_3_.refs_1_, f32[8,128]{1,0:T(8,128)S(1)} %get-tuple-element.47.refs_5_.refs_2_, f32[256,128]{1,0:T(8,128)S(1)} %get-tuple-element.31.refs_2_.refs_0_.refs_3_, ...), custom_call_target="tpu_custom_call" | custom-call | flops 134217728 | bytes 5242880 | tf_op jit(solution)/shard_map/mix/pallas_call | solution.py:68
  44.1 0.0 collective-permute-start.12
  44.1 1.5 %collective-permute-start.11 = (f32[8,256]{1,0:T(8,128)S(1)}, f32[8,256]{1,0:T(8,128)S(1)}, u32[]{:S(2)}, u32[]{:S(2)}) collective-permute-start(f32[8,256]{1,0:T(8,128)S(1)} %get-tuple-element.55.refs_4_.refs_3_), channel_id=1, source_target_pairs={{0,2},{1,3},{2,0},{3,1},{4,6},{5,7},{6,4},{7,5},{8,10},{9,11},{10,... | collective-permute-start | bytes 24584 | tf_op jit(solution)/shard_map/ppermute | solution.py:817
  45.6 0.3 collective-permute-start.10
  46.0 0.0 collective-permute-done.13.refs_3_
  46.0 1.9 %attend.8.refs_2_.refs_4_ = f32[2,144,2048]{2,1,0:T(8,128)S(1)} custom-call(s32[1]{0:T(128)} %bitcast.1.refs_0_, bf16[2,2048,256]{2,1,0:T(8,128)(2,1)S(1)} %get-tuple-element.44.refs_1_, f32[2,144,2048]{2,1,0:T(8,128)S(1)} %attend.7.refs_12_.refs_2_.refs_0_, bf16[1040,128]{1,0:T(8,128)(2,1)S(1)} %collective-permute-done.13.refs_3_, ...), custom_call_target="tpu_custom_call" | custom-call | flops 1073741824 | bytes 8388608 | tf_op jit(solution)/shard_map/attend/pallas_call | solution.py:68
  47.9 0.0 copy-start.1
  47.9 0.0 copy-start.2
  47.9 1.3 %collective-permute-done.14.refs_3_ = bf16[1040,128]{1,0:T(8,128)(2,1)S(1)} collective-permute-done((bf16[1040,128]{1,0:T(8,128)(2,1)S(1)}, bf16[1040,128]{1,0:T(8,128)(2,1)S(1)}, u32[]{:S(2)}, u32[]{:S(2)}) %collective-permute-start.14) | collective-permute-done | bytes 266272 | tf_op jit(solution)/shard_map/ppermute | solution.py:730
  49.2 2.8 %attend.9 = (bf16[4096,128]{1,0:T(8,128)(2,1)}, f32[8,128]{1,0:T(8,128)S(1)}) custom-call(s32[1]{0:T(128)} %bitcast.1.refs_0_, bf16[2,2048,256]{2,1,0:T(8,128)(2,1)S(1)} %get-tuple-element.44.refs_1_, f32[2,144,2048]{2,1,0:T(8,128)S(1)} %attend.8.refs_2_.refs_4_, bf16[1040,128]{1,0:T(8,128)(2,1)S(1)} %collective-permute-done.14.refs_3_, ...), custom_call_target="tpu_custom_call" | custom-call | flops 1073741824 | bytes 8388608 | tf_op jit(solution)/shard_map/attend/pallas_call | solution.py:68
  52.0 0.0 collective-permute-done.12.refs_6_
  52.0 0.0 collective-permute-done.11.refs_5_
  52.0 0.0 collective-permute-done.10.refs_4_
  52.0 1.7 %finish.1 = bf16[4096,128]{1,0:T(8,128)(2,1)} custom-call(f32[16,128]{1,0:T(8,128)S(1)} %copy-done.2, bf16[4096,128]{1,0:T(8,128)(2,1)S(1)} %bitcast.15, f32[4096,128]{1,0:T(8,128)S(1)} %get-tuple-element.54.refs_2_, f32[8,256]{1,0:T(8,128)S(1)} %get-tuple-element.55.refs_4_.refs_3_, f32[8,256]{1,0:T(8,128)S(1)} %collective-permute-done.10.refs_4_, ...), custom_call_target="tpu_custom_call" | custom-call | bytes 4194304 | tf_op jit(solution)/shard_map/finish/pallas_call | solution.py:68
  (3 shorter events, 0.0 us)
Async XLA Ops:
  2.6 12.3 %collective-permute-start.3 = (bf16[1040,128]{1,0:T(8,128)(2,1)S(1)}, bf16[1040,128]{1,0:T(8,128)(2,1)S(1)}, u32[]{:S(2)}, u32[]{:S(2)}) collective-permute-start(bf16[1040,128]{1,0:T(8,128)(2,1)S(1)} %get-tuple-element.39.refs_3_.refs_1_), channel_id=1, source_target_pairs={{0,8},{4,12},{8,16},{12,20},{16,24},{20,28},{24,0},{28,4},{1,9},{5... | collective-permute-start | bytes 798728 | tf_op jit(solution)/shard_map/ppermute | solution.py:730
  9.4 5.5 %copy-start = (bf16[256,16,128]{2,1,0:T(8,128)(2,1)S(1)}, bf16[256,16,128]{2,1,0:T(8,128)(2,1)}, u32[]{:S(2)}) copy-start(bf16[256,16,128]{2,1,0:T(8,128)(2,1)} %param.10) | copy-start | bytes 3145732
  9.5 8.1 %collective-permute-start = (bf16[528,128]{1,0:T(8,128)(2,1)S(1)}, bf16[528,128]{1,0:T(8,128)(2,1)S(1)}, u32[]{:S(2)}, u32[]{:S(2)}) collective-permute-start(bf16[528,128]{1,0:T(8,128)(2,1)S(1)} %get-tuple-element.35), channel_id=1, source_target_pairs={{0,4},{4,0},{8,12},{12,8},{16,20},{20,16},{24,28},{28,24},{1,5},{5... | collective-permute-start | bytes 405512 | tf_op jit(solution)/shard_map/ppermute | solution.py:730
  11.1 6.5 %collective-permute-start.1 = (bf16[528,128]{1,0:T(8,128)(2,1)S(1)}, bf16[528,128]{1,0:T(8,128)(2,1)S(1)}, u32[]{:S(2)}, u32[]{:S(2)}) collective-permute-start(bf16[528,128]{1,0:T(8,128)(2,1)S(1)} %get-tuple-element.36), channel_id=1, source_target_pairs={{0,8},{4,12},{8,0},{12,4},{16,24},{20,28},{24,16},{28,20},{1,9},{5... | collective-permute-start | bytes 405512 | tf_op jit(solution)/shard_map/ppermute | solution.py:730
  12.6 8.2 %collective-permute-start.2 = (bf16[528,128]{1,0:T(8,128)(2,1)S(1)}, bf16[528,128]{1,0:T(8,128)(2,1)S(1)}, u32[]{:S(2)}, u32[]{:S(2)}) collective-permute-start(bf16[528,128]{1,0:T(8,128)(2,1)S(1)} %get-tuple-element.37), channel_id=1, source_target_pairs={{0,12},{4,8},{8,4},{12,0},{16,28},{20,24},{24,20},{28,16},{1,13},{... | collective-permute-start | bytes 405512 | tf_op jit(solution)/shard_map/ppermute | solution.py:730
  16.9 10.4 %collective-permute-start.5 = (bf16[1040,128]{1,0:T(8,128)(2,1)S(1)}, bf16[1040,128]{1,0:T(8,128)(2,1)S(1)}, u32[]{:S(2)}, u32[]{:S(2)}) collective-permute-start(bf16[1040,128]{1,0:T(8,128)(2,1)S(1)} %get-tuple-element.42.refs_6_), channel_id=1, source_target_pairs={{8,16},{12,20},{16,24},{20,28},{9,17},{13,21},{17,25},{21,29},{10,... | collective-permute-start | bytes 798728 | tf_op jit(solution)/shard_map/ppermute | solution.py:730
  21.1 15.4 %collective-permute-start.9 = (bf16[1040,128]{1,0:T(8,128)(2,1)S(1)}, bf16[1040,128]{1,0:T(8,128)(2,1)S(1)}, u32[]{:S(2)}, u32[]{:S(2)}) collective-permute-start(bf16[1040,128]{1,0:T(8,128)(2,1)S(1)} %get-tuple-element.45.refs_3_), channel_id=1, source_target_pairs={{0,4},{4,0},{8,12},{12,8},{16,20},{20,16},{24,28},{28,24},{1,5},{5... | collective-permute-start | bytes 798728 | tf_op jit(solution)/shard_map/ppermute | solution.py:730
  21.6 8.9 %collective-permute-start.4 = (bf16[528,128]{1,0:T(8,128)(2,1)S(1)}, bf16[528,128]{1,0:T(8,128)(2,1)S(1)}, u32[]{:S(2)}, u32[]{:S(2)}) collective-permute-start(bf16[528,128]{1,0:T(8,128)(2,1)S(1)} %get-tuple-element.43.refs_4_), channel_id=1, source_target_pairs={{0,16},{4,20},{8,24},{12,28},{16,0},{20,4},{24,8},{28,12},{1,17},{... | collective-permute-start | bytes 405512 | tf_op jit(solution)/shard_map/ppermute | solution.py:730
  27.4 18.6 %collective-permute-start.13 = (bf16[1040,128]{1,0:T(8,128)(2,1)S(1)}, bf16[1040,128]{1,0:T(8,128)(2,1)S(1)}, u32[]{:S(2)}, u32[]{:S(2)}) collective-permute-start(bf16[1040,128]{1,0:T(8,128)(2,1)S(1)} %pick.1.refs_6_), channel_id=1, source_target_pairs={{0,4},{4,8},{8,12},{12,16},{16,20},{20,24},{24,28},{28,0},{1,5},{5... | collective-permute-start | bytes 798728 | tf_op jit(solution)/shard_map/ppermute | solution.py:730
  30.8 9.8 %collective-permute-start.6 = (bf16[512,128]{1,0:T(8,128)(2,1)S(1)}, bf16[512,128]{1,0:T(8,128)(2,1)S(1)}, u32[]{:S(2)}, u32[]{:S(2)}) collective-permute-start(bf16[512,128]{1,0:T(8,128)(2,1)S(1)} %get-tuple-element.51), channel_id=1, source_target_pairs={{0,4},{4,0},{8,12},{12,8},{16,20},{20,16},{24,28},{28,24},{1,5},{5... | collective-permute-start | bytes 393224 | tf_op jit(solution)/shard_map/ppermute | solution.py:730
  32.9 7.6 %collective-permute-start.7 = (bf16[512,128]{1,0:T(8,128)(2,1)S(1)}, bf16[512,128]{1,0:T(8,128)(2,1)S(1)}, u32[]{:S(2)}, u32[]{:S(2)}) collective-permute-start(bf16[512,128]{1,0:T(8,128)(2,1)S(1)} %get-tuple-element.52), channel_id=1, source_target_pairs={{0,8},{4,12},{8,0},{12,4},{16,24},{20,28},{24,16},{28,20},{1,9},{5... | collective-permute-start | bytes 393224 | tf_op jit(solution)/shard_map/ppermute | solution.py:730
  36.4 5.9 %collective-permute-start.8 = (bf16[512,128]{1,0:T(8,128)(2,1)S(1)}, bf16[512,128]{1,0:T(8,128)(2,1)S(1)}, u32[]{:S(2)}, u32[]{:S(2)}) collective-permute-start(bf16[512,128]{1,0:T(8,128)(2,1)S(1)} %get-tuple-element.53), channel_id=1, source_target_pairs={{0,12},{4,8},{8,4},{12,0},{16,28},{20,24},{24,20},{28,16},{1,13},{... | collective-permute-start | bytes 393224 | tf_op jit(solution)/shard_map/ppermute | solution.py:730
  42.4 6.8 %collective-permute-start.14 = (bf16[1040,128]{1,0:T(8,128)(2,1)S(1)}, bf16[1040,128]{1,0:T(8,128)(2,1)S(1)}, u32[]{:S(2)}, u32[]{:S(2)}) collective-permute-start(bf16[1040,128]{1,0:T(8,128)(2,1)S(1)} %pass_on.1), channel_id=1, source_target_pairs={{0,4},{4,0},{8,12},{12,8},{16,20},{20,16},{24,28},{28,24},{1,5},{5... | collective-permute-start | bytes 798728 | tf_op jit(solution)/shard_map/ppermute | solution.py:730
  44.1 7.9 %collective-permute-start.12 = (f32[8,256]{1,0:T(8,128)S(1)}, f32[8,256]{1,0:T(8,128)S(1)}, u32[]{:S(2)}, u32[]{:S(2)}) collective-permute-start(f32[8,256]{1,0:T(8,128)S(1)} %get-tuple-element.55.refs_4_.refs_3_), channel_id=1, source_target_pairs={{0,3},{1,2},{2,1},{3,0},{4,7},{5,6},{6,5},{7,4},{8,11},{9,10},{10,... | collective-permute-start | bytes 24584 | tf_op jit(solution)/shard_map/ppermute | solution.py:817
  44.1 7.9 %collective-permute-start.11 = (f32[8,256]{1,0:T(8,128)S(1)}, f32[8,256]{1,0:T(8,128)S(1)}, u32[]{:S(2)}, u32[]{:S(2)}) collective-permute-start(f32[8,256]{1,0:T(8,128)S(1)} %get-tuple-element.55.refs_4_.refs_3_), channel_id=1, source_target_pairs={{0,2},{1,3},{2,0},{3,1},{4,6},{5,7},{6,4},{7,5},{8,10},{9,11},{10,... | collective-permute-start | bytes 24584 | tf_op jit(solution)/shard_map/ppermute | solution.py:817
  45.6 6.4 %collective-permute-start.10 = (f32[8,256]{1,0:T(8,128)S(1)}, f32[8,256]{1,0:T(8,128)S(1)}, u32[]{:S(2)}, u32[]{:S(2)}) collective-permute-start(f32[8,256]{1,0:T(8,128)S(1)} %get-tuple-element.55.refs_4_.refs_3_), channel_id=1, source_target_pairs={{0,1},{1,0},{2,3},{3,2},{4,5},{5,4},{6,7},{7,6},{8,9},{9,8},{10,11... | collective-permute-start | bytes 24584 | tf_op jit(solution)/shard_map/ppermute | solution.py:817
  47.9 4.1 %copy-start.1 = (bf16[256,16,128]{2,1,0:T(8,128)(2,1)S(1)}, bf16[256,16,128]{2,1,0:T(8,128)(2,1)}, u32[]{:S(2)}) copy-start(bf16[256,16,128]{2,1,0:T(8,128)(2,1)} %param.13) | copy-start | bytes 3145732
  47.9 4.1 %copy-start.2 = (f32[16,128]{1,0:T(8,128)S(1)}, f32[16,128]{1,0:T(8,128)}, u32[]{:S(2)}) copy-start(f32[16,128]{1,0:T(8,128)} %refs_0_.1) | copy-start | bytes 24580

commit v21 on v20

--- a/solution.py
+++ b/solution.py
@@ -759,11 +759,11 @@
 
     state = {}
 
-    def first_attention(after):
-        state["wide"], state["sum"] = attend(
-            place, (docs, query), None, [(own_kv, (0, 0))], False, tokens, heads, kv_here, after
+    def first_attention(after, relay):
+        state["wide"], state["sum"], copy = attend(
+            place, (docs, query), None, [(own_kv, (0, 0))], False, tokens, heads, kv_here, after, relay
         )
-        return state["sum"]
+        return state["sum"], copy
 
     def more_attention(kv, is_last, after, relay=()):
         out = attend(
@@ -783,9 +783,9 @@
         qh.append(got[1])
         return (got[0], *got[2:]) if relay else got[0]
 
-    done, lane = first_attention([sent[0]]), ahead
+    done, lane = first_attention([sent[0]], [ahead])
     if parts > 1:
-        done, lane = inner_of(0, [done], [ahead])
+        done = inner_of(0, [done])
     second = send(lane, [(b, b + 2) for b in range(2, blocks - 2)])
     run, lane = group_map(place, quarters, size, [done], [lane])
     first_cross = send(lane, swap)

time: 54 us -> 54.6 us (1.011)
  waiting for transfers between devices: 9.66 us -> 11.2 us
  starting transfers between devices: 17.9 us -> 17.1 us
    ppermute x12, waiting for transfers between devices: 9.65 us -> 11.2 us  [send(): return lax.ppermute(x, 'seq', [(a, b % blocks) for a, b in pairs])]
    ppermute x12, starting transfers between devices: 16 us -> 15.3 us  [send(): return lax.ppermute(x, 'seq', [(a, b % blocks) for a, b in pairs])]
  transfers between devices with their start and end apart: 15 -> 15, of which waited for: 5 -> 6; matrix products, arithmetic and copies ran while one was open for 0% -> 0% of each run, Pallas kernels for 40% -> 39%
where the time goes in v21:
time: 54.6 us; the launch traced here: 54.5 us
  Pallas kernels  25.1 us (46%)
  starting transfers between devices  17.1 us (31%)
  waiting for transfers between devices  11.2 us (21%)
  between operations  1.01 us (2%)
    pallas_call x15, Pallas kernels, call(): pl.pallas_call(run, out_shape=outs, in_specs=[SMEM] * len(scalars) + [HBM...  25.1 us
    ppermute x12, starting transfers between devices, send(): return lax.ppermute(x, 'seq', [(a, b % blocks) for a, b in pairs])  15.3 us
    ppermute x12, waiting for transfers between devices, send(): return lax.ppermute(x, 'seq', [(a, b % blocks) for a, b in pairs])  11.2 us
    ppermute x3, starting transfers between devices, body(): lax.ppermute(squares, 'tp', [(t, t ^ other) for t in range(tensor)])  1.89 us
  transfers between devices with their start and end apart: 15, of which 6 were waited for; matrix products, arithmetic and copies ran while one was open for 0% of the time, Pallas kernels for 39%

profile of v21, /device:TPU:0, one launch (start us, length us, event | category | flops | bytes accessed | tf_op | source)
XLA Modules:
  0.0 54.5 jit_solution(6557019233331412168)
XLA Ops:
  0.6 1.9 %fetch.1 = (bf16[1040,128]{1,0:T(8,128)(2,1)S(1)}, f32[16,128]{1,0:T(8,128)S(1)}, f32[256,128]{1,0:T(8,128)S(1)}, bf16[4096,128]{1,0:T(8,128)(2,1)S(1)}, bf16[4096,128]{1,0:T(8,128)(2,1)S(1)}) custom-call(s32[1]{0:T(128)} %bitcast.2.refs_0_, s32[2,128]{1,0:T(2,128)} %bitcast.23, f32[16,256]{1,0:T(8,128)} %bitcast.22, bf16[2048,128]{1,0:T(8,128)(2,1)} %bitcast.20, ...), custom_call_target="tpu_custom_call" | custom-call | bytes 3145728 | tf_op jit(solution)/shard_map/fetch/pallas_call | solution.py:68
  2.6 3.1 %collective-permute-start.3 = (bf16[1040,128]{1,0:T(8,128)(2,1)S(1)}, bf16[1040,128]{1,0:T(8,128)(2,1)S(1)}, u32[]{:S(2)}, u32[]{:S(2)}) collective-permute-start(bf16[1040,128]{1,0:T(8,128)(2,1)S(1)} %get-tuple-element.39.refs_3_.refs_1_), channel_id=1, source_target_pairs={{0,8},{4,12},{8,16},{12,20},{16,24},{20,28},{24,0},{28,4},{1,9},{5... | collective-permute-start | bytes 798728 | tf_op jit(solution)/shard_map/ppermute | solution.py:730
  5.7 3.8 %block_state.1 = (bf16[528,128]{1,0:T(8,128)(2,1)S(1)}, bf16[528,128]{1,0:T(8,128)(2,1)S(1)}, bf16[528,128]{1,0:T(8,128)(2,1)S(1)}, bf16[528,128]{1,0:T(8,128)(2,1)S(1)}, bf16[4096,128]{1,0:T(8,128)(2,1)S(1)}) custom-call(s32[1]{0:T(128)} %bitcast.1.refs_0_, bf16[4096,128]{1,0:T(8,128)(2,1)} %bitcast.19, ...), custom_call_target="tpu_custom_call" | custom-call | flops 134217728 | bytes 5242880 | tf_op jit(solution)/shard_map/block_state/pallas_call | solution.py:68
  9.4 0.0 copy-start
  9.5 1.6 %collective-permute-start = (bf16[528,128]{1,0:T(8,128)(2,1)S(1)}, bf16[528,128]{1,0:T(8,128)(2,1)S(1)}, u32[]{:S(2)}, u32[]{:S(2)}) collective-permute-start(bf16[528,128]{1,0:T(8,128)(2,1)S(1)} %get-tuple-element.35), channel_id=1, source_target_pairs={{0,4},{4,0},{8,12},{12,8},{16,20},{20,16},{24,28},{28,24},{1,5},{5... | collective-permute-start | bytes 405512 | tf_op jit(solution)/shard_map/ppermute | solution.py:730
  11.0 1.6 %collective-permute-start.1 = (bf16[528,128]{1,0:T(8,128)(2,1)S(1)}, bf16[528,128]{1,0:T(8,128)(2,1)S(1)}, u32[]{:S(2)}, u32[]{:S(2)}) collective-permute-start(bf16[528,128]{1,0:T(8,128)(2,1)S(1)} %get-tuple-element.36), channel_id=1, source_target_pairs={{0,8},{4,12},{8,0},{12,4},{16,24},{20,28},{24,16},{28,20},{1,9},{5... | collective-permute-start | bytes 405512 | tf_op jit(solution)/shard_map/ppermute | solution.py:730
  12.6 0.4 collective-permute-start.2
  13.0 1.2 %collective-permute-done.3.refs_5_ = bf16[1040,128]{1,0:T(8,128)(2,1)S(1)} collective-permute-done((bf16[1040,128]{1,0:T(8,128)(2,1)S(1)}, bf16[1040,128]{1,0:T(8,128)(2,1)S(1)}, u32[]{:S(2)}, u32[]{:S(2)}) %collective-permute-start.3) | collective-permute-done | bytes 266272 | tf_op jit(solution)/shard_map/ppermute | solution.py:730
  14.2 1.9 %attend.5 = (bf16[2,2048,256]{2,1,0:T(8,128)(2,1)S(1)}, f32[2,144,2048]{2,1,0:T(8,128)S(1)}, bf16[1040,128]{1,0:T(8,128)(2,1)S(1)}) custom-call(s32[1]{0:T(128)} %bitcast.1.refs_0_, f32[16,128]{1,0:T(8,128)S(1)} %get-tuple-element.30.refs_3_.refs_1_, bf16[4096,128]{1,0:T(8,128)(2,1)S(1)} %get-tuple-element.38.refs_2_, ...), custom_call_target="tpu_custom_call" | custom-call | flops 1073741824 | bytes 8388608 | tf_op jit(solution)/shard_map/attend/pallas_call | solution.py:68
  16.1 0.7 %collective-permute-start.5 = (bf16[1040,128]{1,0:T(8,128)(2,1)S(1)}, bf16[1040,128]{1,0:T(8,128)(2,1)S(1)}, u32[]{:S(2)}, u32[]{:S(2)}) collective-permute-start(bf16[1040,128]{1,0:T(8,128)(2,1)S(1)} %get-tuple-element.42.refs_6_), channel_id=1, source_target_pairs={{8,16},{12,20},{16,24},{20,28},{9,17},{13,21},{17,25},{21,29},{10,... | collective-permute-start | bytes 798728 | tf_op jit(solution)/shard_map/ppermute | solution.py:730
  16.7 0.0 copy-done
  16.8 1.9 %inner_part.2 = (f32[2048,128]{1,0:T(8,128)S(1)}, bf16[2048,128]{1,0:T(8,128)(2,1)S(1)}) custom-call(f32[256,128]{1,0:T(8,128)S(1)} %get-tuple-element.31.refs_2_.refs_0_.refs_3_, f32[16,128]{1,0:T(8,128)S(1)} %get-tuple-element.30.refs_3_.refs_1_, bf16[4096,128]{1,0:T(8,128)(2,1)S(1)} %bitcast.13, bf16[4096,128]{1,0:T(8,128)(2,1)S(1)} %get-tuple-element.32.refs_4_.refs_3_, ...), custom_call_target="tpu_custom_call" | custom-call | flops 268435456 | bytes 6291456 | tf_op jit(solution)/shard_map/inner_part/pallas_call | solution.py:68
  18.7 0.0 collective-permute-done.refs_2_
  18.7 0.0 collective-permute-done.1.refs_3_
  18.7 2.2 %collective-permute-done.2.refs_4_ = bf16[528,128]{1,0:T(8,128)(2,1)S(1)} collective-permute-done((bf16[528,128]{1,0:T(8,128)(2,1)S(1)}, bf16[528,128]{1,0:T(8,128)(2,1)S(1)}, u32[]{:S(2)}, u32[]{:S(2)}) %collective-permute-start.2) | collective-permute-done | bytes 135200 | tf_op jit(solution)/shard_map/ppermute | solution.py:730
  20.8 0.2 group_map.1
  21.1 0.6 %collective-permute-start.9 = (bf16[1040,128]{1,0:T(8,128)(2,1)S(1)}, bf16[1040,128]{1,0:T(8,128)(2,1)S(1)}, u32[]{:S(2)}, u32[]{:S(2)}) collective-permute-start(bf16[1040,128]{1,0:T(8,128)(2,1)S(1)} %get-tuple-element.45.refs_3_), channel_id=1, source_target_pairs={{0,4},{4,0},{8,12},{12,8},{16,20},{20,16},{24,28},{28,24},{1,5},{5... | collective-permute-start | bytes 798728 | tf_op jit(solution)/shard_map/ppermute | solution.py:730
  21.6 3.4 %collective-permute-start.4 = (bf16[528,128]{1,0:T(8,128)(2,1)S(1)}, bf16[528,128]{1,0:T(8,128)(2,1)S(1)}, u32[]{:S(2)}, u32[]{:S(2)}) collective-permute-start(bf16[528,128]{1,0:T(8,128)(2,1)S(1)} %get-tuple-element.43.refs_4_), channel_id=1, source_target_pairs={{0,16},{4,20},{8,24},{12,28},{16,0},{20,4},{24,8},{28,12},{1,17},{... | collective-permute-start | bytes 405512 | tf_op jit(solution)/shard_map/ppermute | solution.py:730
  25.1 1.9 %attend.6.refs_5_.refs_2_ = f32[2,144,2048]{2,1,0:T(8,128)S(1)} custom-call(s32[1]{0:T(128)} %bitcast.1.refs_0_, bf16[2,2048,256]{2,1,0:T(8,128)(2,1)S(1)} %get-tuple-element.44.refs_1_, f32[2,144,2048]{2,1,0:T(8,128)S(1)} %get-tuple-element.40.refs_5_.refs_2_, bf16[1040,128]{1,0:T(8,128)(2,1)S(1)} %get-tuple-element.45.refs_3_, ...), custom_call_target="tpu_custom_call" | custom-call | flops 1073741824 | bytes 8388608 | tf_op jit(solution)/shard_map/attend/pallas_call | solution.py:68
  27.0 1.9 %inner_part.3 = (f32[2048,128]{1,0:T(8,128)S(1)}, bf16[2048,128]{1,0:T(8,128)(2,1)S(1)}) custom-call(f32[256,128]{1,0:T(8,128)S(1)} %get-tuple-element.31.refs_2_.refs_0_.refs_3_, f32[16,128]{1,0:T(8,128)S(1)} %get-tuple-element.30.refs_3_.refs_1_, bf16[4096,128]{1,0:T(8,128)(2,1)S(1)} %bitcast.14, bf16[4096,128]{1,0:T(8,128)(2,1)S(1)} %get-tuple-element.32.refs_4_.refs_3_, ...), custom_call_target="tpu_custom_call" | custom-call | flops 268435456 | bytes 6291456 | tf_op jit(solution)/shard_map/inner_part/pallas_call | solution.py:68
  28.9 0.0 collective-permute-done.5.refs_2_.refs_4_.refs_5_
  28.9 0.1 pick.1.refs_6_
  29.0 0.3 collective-permute-start.13
  29.3 1.2 %collective-permute-done.4.refs_5_ = bf16[528,128]{1,0:T(8,128)(2,1)S(1)} collective-permute-done((bf16[528,128]{1,0:T(8,128)(2,1)S(1)}, bf16[528,128]{1,0:T(8,128)(2,1)S(1)}, u32[]{:S(2)}, u32[]{:S(2)}) %collective-permute-start.4) | collective-permute-done | bytes 135200 | tf_op jit(solution)/shard_map/ppermute | solution.py:730
  30.5 0.3 prior_states.1
  30.8 0.7 %collective-permute-start.6 = (bf16[512,128]{1,0:T(8,128)(2,1)S(1)}, bf16[512,128]{1,0:T(8,128)(2,1)S(1)}, u32[]{:S(2)}, u32[]{:S(2)}) collective-permute-start(bf16[512,128]{1,0:T(8,128)(2,1)S(1)} %get-tuple-element.51), channel_id=1, source_target_pairs={{0,4},{4,0},{8,12},{12,8},{16,20},{20,16},{24,28},{28,24},{1,5},{5... | collective-permute-start | bytes 393224 | tf_op jit(solution)/shard_map/ppermute | solution.py:730
  31.4 2.2 %collective-permute-start.7 = (bf16[512,128]{1,0:T(8,128)(2,1)S(1)}, bf16[512,128]{1,0:T(8,128)(2,1)S(1)}, u32[]{:S(2)}, u32[]{:S(2)}) collective-permute-start(bf16[512,128]{1,0:T(8,128)(2,1)S(1)} %get-tuple-element.52), channel_id=1, source_target_pairs={{0,8},{4,12},{8,0},{12,4},{16,24},{20,28},{24,16},{28,20},{1,9},{5... | collective-permute-start | bytes 393224 | tf_op jit(solution)/shard_map/ppermute | solution.py:730
  33.6 0.7 %collective-permute-start.8 = (bf16[512,128]{1,0:T(8,128)(2,1)S(1)}, bf16[512,128]{1,0:T(8,128)(2,1)S(1)}, u32[]{:S(2)}, u32[]{:S(2)}) collective-permute-start(bf16[512,128]{1,0:T(8,128)(2,1)S(1)} %get-tuple-element.53), channel_id=1, source_target_pairs={{0,12},{4,8},{8,4},{12,0},{16,28},{20,24},{24,20},{28,16},{1,13},{... | collective-permute-start | bytes 393224 | tf_op jit(solution)/shard_map/ppermute | solution.py:730
  34.3 0.0 collective-permute-done.9.refs_3_
  34.3 3.3 %attend.7.refs_12_.refs_2_.refs_0_ = f32[2,144,2048]{2,1,0:T(8,128)S(1)} custom-call(s32[1]{0:T(128)} %bitcast.1.refs_0_, bf16[2,2048,256]{2,1,0:T(8,128)(2,1)S(1)} %get-tuple-element.44.refs_1_, f32[2,144,2048]{2,1,0:T(8,128)S(1)} %attend.6.refs_5_.refs_2_, bf16[1040,128]{1,0:T(8,128)(2,1)S(1)} %collective-permute-done.9.refs_3_, ...), custom_call_target="tpu_custom_call" | custom-call | flops 2147483648 | bytes 8388608 | tf_op jit(solution)/shard_map/attend/pallas_call | solution.py:68
  37.6 3.8 %collective-permute-done.6.refs_9_.refs_2_ = bf16[512,128]{1,0:T(8,128)(2,1)S(1)} collective-permute-done((bf16[512,128]{1,0:T(8,128)(2,1)S(1)}, bf16[512,128]{1,0:T(8,128)(2,1)S(1)}, u32[]{:S(2)}, u32[]{:S(2)}) %collective-permute-start.6) | collective-permute-done | bytes 131104 | tf_op jit(solution)/shard_map/ppermute | solution.py:730
  41.4 0.0 collective-permute-done.7.refs_10_.refs_3_
  41.4 1.4 %collective-permute-done.8.refs_11_.refs_4_ = bf16[512,128]{1,0:T(8,128)(2,1)S(1)} collective-permute-done((bf16[512,128]{1,0:T(8,128)(2,1)S(1)}, bf16[512,128]{1,0:T(8,128)(2,1)S(1)}, u32[]{:S(2)}, u32[]{:S(2)}) %collective-permute-start.8) | collective-permute-done | bytes 131104 | tf_op jit(solution)/shard_map/ppermute | solution.py:730
  42.8 0.1 collective-permute-start.14
  42.9 1.6 %mix.1 = (f32[4096,128]{1,0:T(8,128)S(1)}, f32[8,256]{1,0:T(8,128)S(1)}) custom-call(s32[1]{0:T(128)} %bitcast.1.refs_0_, f32[16,128]{1,0:T(8,128)S(1)} %get-tuple-element.30.refs_3_.refs_1_, f32[8,128]{1,0:T(8,128)S(1)} %get-tuple-element.47.refs_5_.refs_2_, f32[256,128]{1,0:T(8,128)S(1)} %get-tuple-element.31.refs_2_.refs_0_.refs_3_, ...), custom_call_target="tpu_custom_call" | custom-call | flops 134217728 | bytes 5242880 | tf_op jit(solution)/shard_map/mix/pallas_call | solution.py:68
  44.5 0.0 collective-permute-start.12
  44.5 1.5 %collective-permute-start.11 = (f32[8,256]{1,0:T(8,128)S(1)}, f32[8,256]{1,0:T(8,128)S(1)}, u32[]{:S(2)}, u32[]{:S(2)}) collective-permute-start(f32[8,256]{1,0:T(8,128)S(1)} %get-tuple-element.55.refs_4_.refs_3_), channel_id=1, source_target_pairs={{0,2},{1,3},{2,0},{3,1},{4,6},{5,7},{6,4},{7,5},{8,10},{9,11},{10,... | collective-permute-start | bytes 24584 | tf_op jit(solution)/shard_map/ppermute | solution.py:817
  46.1 0.3 collective-permute-start.10
  46.4 0.0 collective-permute-done.13.refs_3_
  46.4 1.9 %attend.8.refs_2_.refs_4_ = f32[2,144,2048]{2,1,0:T(8,128)S(1)} custom-call(s32[1]{0:T(128)} %bitcast.1.refs_0_, bf16[2,2048,256]{2,1,0:T(8,128)(2,1)S(1)} %get-tuple-element.44.refs_1_, f32[2,144,2048]{2,1,0:T(8,128)S(1)} %attend.7.refs_12_.refs_2_.refs_0_, bf16[1040,128]{1,0:T(8,128)(2,1)S(1)} %collective-permute-done.13.refs_3_, ...), custom_call_target="tpu_custom_call" | custom-call | flops 1073741824 | bytes 8388608 | tf_op jit(solution)/shard_map/attend/pallas_call | solution.py:68
  48.3 0.0 copy-start.1
  48.3 0.0 copy-start.2
  48.3 1.4 %collective-permute-done.14.refs_3_ = bf16[1040,128]{1,0:T(8,128)(2,1)S(1)} collective-permute-done((bf16[1040,128]{1,0:T(8,128)(2,1)S(1)}, bf16[1040,128]{1,0:T(8,128)(2,1)S(1)}, u32[]{:S(2)}, u32[]{:S(2)}) %collective-permute-start.14) | collective-permute-done | bytes 266272 | tf_op jit(solution)/shard_map/ppermute | solution.py:730
  49.8 2.8 %attend.9 = (bf16[4096,128]{1,0:T(8,128)(2,1)}, f32[8,128]{1,0:T(8,128)S(1)}) custom-call(s32[1]{0:T(128)} %bitcast.1.refs_0_, bf16[2,2048,256]{2,1,0:T(8,128)(2,1)S(1)} %get-tuple-element.44.refs_1_, f32[2,144,2048]{2,1,0:T(8,128)S(1)} %attend.8.refs_2_.refs_4_, bf16[1040,128]{1,0:T(8,128)(2,1)S(1)} %collective-permute-done.14.refs_3_, ...), custom_call_target="tpu_custom_call" | custom-call | flops 1073741824 | bytes 8388608 | tf_op jit(solution)/shard_map/attend/pallas_call | solution.py:68
  52.6 0.0 collective-permute-done.12.refs_6_
  52.6 0.0 collective-permute-done.11.refs_5_
  52.6 0.0 collective-permute-done.10.refs_4_
  52.6 1.7 %finish.1 = bf16[4096,128]{1,0:T(8,128)(2,1)} custom-call(f32[16,128]{1,0:T(8,128)S(1)} %copy-done.2, bf16[4096,128]{1,0:T(8,128)(2,1)S(1)} %bitcast.15, f32[4096,128]{1,0:T(8,128)S(1)} %get-tuple-element.54.refs_2_, f32[8,256]{1,0:T(8,128)S(1)} %get-tuple-element.55.refs_4_.refs_3_, f32[8,256]{1,0:T(8,128)S(1)} %collective-permute-done.10.refs_4_, ...), custom_call_target="tpu_custom_call" | custom-call | bytes 4194304 | tf_op jit(solution)/shard_map/finish/pallas_call | solution.py:68
  (3 shorter events, 0.0 us)
Async XLA Ops:
  2.6 11.6 %collective-permute-start.3 = (bf16[1040,128]{1,0:T(8,128)(2,1)S(1)}, bf16[1040,128]{1,0:T(8,128)(2,1)S(1)}, u32[]{:S(2)}, u32[]{:S(2)}) collective-permute-start(bf16[1040,128]{1,0:T(8,128)(2,1)S(1)} %get-tuple-element.39.refs_3_.refs_1_), channel_id=1, source_target_pairs={{0,8},{4,12},{8,16},{12,20},{16,24},{20,28},{24,0},{28,4},{1,9},{5... | collective-permute-start | bytes 798728 | tf_op jit(solution)/shard_map/ppermute | solution.py:730
  9.4 7.3 %copy-start = (bf16[256,16,128]{2,1,0:T(8,128)(2,1)S(1)}, bf16[256,16,128]{2,1,0:T(8,128)(2,1)}, u32[]{:S(2)}) copy-start(bf16[256,16,128]{2,1,0:T(8,128)(2,1)} %param.10) | copy-start | bytes 3145732
  9.5 9.2 %collective-permute-start = (bf16[528,128]{1,0:T(8,128)(2,1)S(1)}, bf16[528,128]{1,0:T(8,128)(2,1)S(1)}, u32[]{:S(2)}, u32[]{:S(2)}) collective-permute-start(bf16[528,128]{1,0:T(8,128)(2,1)S(1)} %get-tuple-element.35), channel_id=1, source_target_pairs={{0,4},{4,0},{8,12},{12,8},{16,20},{20,16},{24,28},{28,24},{1,5},{5... | collective-permute-start | bytes 405512 | tf_op jit(solution)/shard_map/ppermute | solution.py:730
  11.0 7.6 %collective-permute-start.1 = (bf16[528,128]{1,0:T(8,128)(2,1)S(1)}, bf16[528,128]{1,0:T(8,128)(2,1)S(1)}, u32[]{:S(2)}, u32[]{:S(2)}) collective-permute-start(bf16[528,128]{1,0:T(8,128)(2,1)S(1)} %get-tuple-element.36), channel_id=1, source_target_pairs={{0,8},{4,12},{8,0},{12,4},{16,24},{20,28},{24,16},{28,20},{1,9},{5... | collective-permute-start | bytes 405512 | tf_op jit(solution)/shard_map/ppermute | solution.py:730
  12.6 8.2 %collective-permute-start.2 = (bf16[528,128]{1,0:T(8,128)(2,1)S(1)}, bf16[528,128]{1,0:T(8,128)(2,1)S(1)}, u32[]{:S(2)}, u32[]{:S(2)}) collective-permute-start(bf16[528,128]{1,0:T(8,128)(2,1)S(1)} %get-tuple-element.37), channel_id=1, source_target_pairs={{0,12},{4,8},{8,4},{12,0},{16,28},{20,24},{24,20},{28,16},{1,13},{... | collective-permute-start | bytes 405512 | tf_op jit(solution)/shard_map/ppermute | solution.py:730
  16.1 12.8 %collective-permute-start.5 = (bf16[1040,128]{1,0:T(8,128)(2,1)S(1)}, bf16[1040,128]{1,0:T(8,128)(2,1)S(1)}, u32[]{:S(2)}, u32[]{:S(2)}) collective-permute-start(bf16[1040,128]{1,0:T(8,128)(2,1)S(1)} %get-tuple-element.42.refs_6_), channel_id=1, source_target_pairs={{8,16},{12,20},{16,24},{20,28},{9,17},{13,21},{17,25},{21,29},{10,... | collective-permute-start | bytes 798728 | tf_op jit(solution)/shard_map/ppermute | solution.py:730
  21.1 13.3 %collective-permute-start.9 = (bf16[1040,128]{1,0:T(8,128)(2,1)S(1)}, bf16[1040,128]{1,0:T(8,128)(2,1)S(1)}, u32[]{:S(2)}, u32[]{:S(2)}) collective-permute-start(bf16[1040,128]{1,0:T(8,128)(2,1)S(1)} %get-tuple-element.45.refs_3_), channel_id=1, source_target_pairs={{0,4},{4,0},{8,12},{12,8},{16,20},{20,16},{24,28},{28,24},{1,5},{5... | collective-permute-start | bytes 798728 | tf_op jit(solution)/shard_map/ppermute | solution.py:730
  21.6 8.9 %collective-permute-start.4 = (bf16[528,128]{1,0:T(8,128)(2,1)S(1)}, bf16[528,128]{1,0:T(8,128)(2,1)S(1)}, u32[]{:S(2)}, u32[]{:S(2)}) collective-permute-start(bf16[528,128]{1,0:T(8,128)(2,1)S(1)} %get-tuple-element.43.refs_4_), channel_id=1, source_target_pairs={{0,16},{4,20},{8,24},{12,28},{16,0},{20,4},{24,8},{28,12},{1,17},{... | collective-permute-start | bytes 405512 | tf_op jit(solution)/shard_map/ppermute | solution.py:730
  29.0 17.4 %collective-permute-start.13 = (bf16[1040,128]{1,0:T(8,128)(2,1)S(1)}, bf16[1040,128]{1,0:T(8,128)(2,1)S(1)}, u32[]{:S(2)}, u32[]{:S(2)}) collective-permute-start(bf16[1040,128]{1,0:T(8,128)(2,1)S(1)} %pick.1.refs_6_), channel_id=1, source_target_pairs={{0,4},{4,8},{8,12},{12,16},{16,20},{20,24},{24,28},{28,0},{1,5},{5... | collective-permute-start | bytes 798728 | tf_op jit(solution)/shard_map/ppermute | solution.py:730
  30.8 10.6 %collective-permute-start.6 = (bf16[512,128]{1,0:T(8,128)(2,1)S(1)}, bf16[512,128]{1,0:T(8,128)(2,1)S(1)}, u32[]{:S(2)}, u32[]{:S(2)}) collective-permute-start(bf16[512,128]{1,0:T(8,128)(2,1)S(1)} %get-tuple-element.51), channel_id=1, source_target_pairs={{0,4},{4,0},{8,12},{12,8},{16,20},{20,16},{24,28},{28,24},{1,5},{5... | collective-permute-start | bytes 393224 | tf_op jit(solution)/shard_map/ppermute | solution.py:730
  31.4 10.0 %collective-permute-start.7 = (bf16[512,128]{1,0:T(8,128)(2,1)S(1)}, bf16[512,128]{1,0:T(8,128)(2,1)S(1)}, u32[]{:S(2)}, u32[]{:S(2)}) collective-permute-start(bf16[512,128]{1,0:T(8,128)(2,1)S(1)} %get-tuple-element.52), channel_id=1, source_target_pairs={{0,8},{4,12},{8,0},{12,4},{16,24},{20,28},{24,16},{28,20},{1,9},{5... | collective-permute-start | bytes 393224 | tf_op jit(solution)/shard_map/ppermute | solution.py:730
  33.6 9.2 %collective-permute-start.8 = (bf16[512,128]{1,0:T(8,128)(2,1)S(1)}, bf16[512,128]{1,0:T(8,128)(2,1)S(1)}, u32[]{:S(2)}, u32[]{:S(2)}) collective-permute-start(bf16[512,128]{1,0:T(8,128)(2,1)S(1)} %get-tuple-element.53), channel_id=1, source_target_pairs={{0,12},{4,8},{8,4},{12,0},{16,28},{20,24},{24,20},{28,16},{1,13},{... | collective-permute-start | bytes 393224 | tf_op jit(solution)/shard_map/ppermute | solution.py:730
  42.8 6.9 %collective-permute-start.14 = (bf16[1040,128]{1,0:T(8,128)(2,1)S(1)}, bf16[1040,128]{1,0:T(8,128)(2,1)S(1)}, u32[]{:S(2)}, u32[]{:S(2)}) collective-permute-start(bf16[1040,128]{1,0:T(8,128)(2,1)S(1)} %pass_on.1), channel_id=1, source_target_pairs={{0,4},{4,0},{8,12},{12,8},{16,20},{20,16},{24,28},{28,24},{1,5},{5... | collective-permute-start | bytes 798728 | tf_op jit(solution)/shard_map/ppermute | solution.py:730
  44.5 8.1 %collective-permute-start.12 = (f32[8,256]{1,0:T(8,128)S(1)}, f32[8,256]{1,0:T(8,128)S(1)}, u32[]{:S(2)}, u32[]{:S(2)}) collective-permute-start(f32[8,256]{1,0:T(8,128)S(1)} %get-tuple-element.55.refs_4_.refs_3_), channel_id=1, source_target_pairs={{0,3},{1,2},{2,1},{3,0},{4,7},{5,6},{6,5},{7,4},{8,11},{9,10},{10,... | collective-permute-start | bytes 24584 | tf_op jit(solution)/shard_map/ppermute | solution.py:817
  44.5 8.1 %collective-permute-start.11 = (f32[8,256]{1,0:T(8,128)S(1)}, f32[8,256]{1,0:T(8,128)S(1)}, u32[]{:S(2)}, u32[]{:S(2)}) collective-permute-start(f32[8,256]{1,0:T(8,128)S(1)} %get-tuple-element.55.refs_4_.refs_3_), channel_id=1, source_target_pairs={{0,2},{1,3},{2,0},{3,1},{4,6},{5,7},{6,4},{7,5},{8,10},{9,11},{10,... | collective-permute-start | bytes 24584 | tf_op jit(solution)/shard_map/ppermute | solution.py:817
  46.1 6.6 %collective-permute-start.10 = (f32[8,256]{1,0:T(8,128)S(1)}, f32[8,256]{1,0:T(8,128)S(1)}, u32[]{:S(2)}, u32[]{:S(2)}) collective-permute-start(f32[8,256]{1,0:T(8,128)S(1)} %get-tuple-element.55.refs_4_.refs_3_), channel_id=1, source_target_pairs={{0,1},{1,0},{2,3},{3,2},{4,5},{5,4},{6,7},{7,6},{8,9},{9,8},{10,11... | collective-permute-start | bytes 24584 | tf_op jit(solution)/shard_map/ppermute | solution.py:817
  48.3 4.3 %copy-start.1 = (bf16[256,16,128]{2,1,0:T(8,128)(2,1)S(1)}, bf16[256,16,128]{2,1,0:T(8,128)(2,1)}, u32[]{:S(2)}) copy-start(bf16[256,16,128]{2,1,0:T(8,128)(2,1)} %param.13) | copy-start | bytes 3145732
  48.3 4.3 %copy-start.2 = (f32[16,128]{1,0:T(8,128)S(1)}, f32[16,128]{1,0:T(8,128)}, u32[]{:S(2)}) copy-start(f32[16,128]{1,0:T(8,128)} %refs_0_.1) | copy-start | bytes 24580
